TPU v7x, 512 devices: a whole 4x4x16 slice. The times are simulated.
512 devices in a mesh: grp: 4 (over x_hi, core), row: 16 (over z), col: 8 (over x_lo, y).
Axes of the slice: x: 4 (x_hi: 2, x_lo: 2; x = x_hi * 2 + x_lo), y: 4, z: 16, core: 2. Of those that a mesh axis runs over, the one named last changes fastest.
Arguments:
- tokens_in: bfloat16 [1024, 6144], P('col', 'row'), may hold values from -6 to 6
- cotangent: bfloat16 [1024, 6144], P('col', 'grp'), may hold values from -6 to 6
- sample_rows: int32 [256], P('col'), may hold values from 0 to 1023, as said below
- act_inverse: bfloat16 [6144, 6144], P('grp', 'row'), as said below
- grad_inverse: bfloat16 [6144, 6144], P('grp', 'col'), as said below
Outputs:
- precond: float32 [6144, 6144], P(('grp', 'row'), 'col')
- act_cov: float32 [6144, 6144], P(('row', 'col'), 'grp')
- grad_cov: float32 [6144, 6144], P(('row', 'col'), 'grp')
Inputs may be any that keep to these rules, and one draw needn't show every extreme that they name: `sample_rows`: for each block c, entries c * 32 to (c + 1) * 32 - 1 are distinct token rows of that block, between c * 128 and (c + 1) * 128 - 1. `act_inverse`: Symmetric. `grad_inverse`: Symmetric.
All inputs are finite; a program needn't handle non-finite values.
Results may differ from a plain program's by a relative error of at most 0.03.
Values may be sent and summed in bfloat16 or wider, within the bound.
No kernel may reach another device: no remote copies, remote signals or barrier semaphores. Data moves between devices by JAX's collectives and lax.ppermute only.
A program may use at most 64 MiB of HBM per device.

v0:
```python
import jax
import jax.numpy as jnp
from jax import lax
from jax.sharding import PartitionSpec as P


def body(tokens_in, cotangent, sample_rows, act_inverse, grad_inverse):
    feat_row = tokens_in.shape[1]
    feat_grp = cotangent.shape[1]
    n_row = lax.axis_size("row")
    n_col = lax.axis_size("col")
    n_grp = lax.axis_size("grp")
    width = feat_row * n_row
    contract = (((0,), (0,)), ((), ()))
    term = lax.dot_general(tokens_in, cotangent, contract, preferred_element_type=jnp.float32)
    summed = lax.psum(term.astype(jnp.bfloat16), "col")
    part_right = jnp.dot(summed, grad_inverse, preferred_element_type=jnp.float32)
    right = lax.psum(part_right.astype(jnp.bfloat16), "grp")
    precond = lax.psum_scatter(
        jnp.dot(act_inverse, right, preferred_element_type=jnp.float32).astype(jnp.bfloat16),
        "row",
        scatter_dimension=0,
        tiled=True,
    ).astype(jnp.float32)
    col_index = lax.axis_index("col")
    grp_index = lax.axis_index("grp")
    offsets = sample_rows - col_index * tokens_in.shape[0]
    picked_x = jnp.take(tokens_in, offsets, axis=0)
    picked_g = jnp.take(cotangent, offsets, axis=0)
    samples = picked_x.shape[0]
    total = samples * n_col
    act_panel = lax.all_gather(picked_x[None], ("row", "col"), axis=0, tiled=True).reshape(
        n_row, total, feat_row
    )
    grad_panel = lax.all_gather(picked_g[None], ("grp", "col"), axis=0, tiled=True).reshape(
        n_grp, total, feat_grp
    )
    tile = width // (n_row * n_col)
    first = (lax.axis_index("row") * n_col + col_index) * tile
    act_left = lax.dynamic_slice(
        act_panel, (first // feat_row, 0, first % feat_row), (1, total, tile)
    )[0]
    per = feat_grp // feat_row
    act_span = lax.dynamic_slice_in_dim(act_panel, grp_index * per, per, 0)
    act_cov = jnp.einsum("sa,psf->apf", act_left, act_span, preferred_element_type=jnp.float32)
    act_cov = act_cov.reshape(tile, feat_grp) / total
    grad_left = lax.dynamic_slice(
        grad_panel, (first // feat_grp, 0, first % feat_grp), (1, total, tile)
    )[0]
    grad_span = lax.dynamic_index_in_dim(grad_panel, grp_index, 0, keepdims=False)
    grad_cov = (
        lax.dot_general(grad_left, grad_span, contract, preferred_element_type=jnp.float32) / total
    )
    return (precond, act_cov, grad_cov)


def solution(mesh):
    return jax.shard_map(
        body,
        mesh=mesh,
        in_specs=(P("col", "row"), P("col", "grp"), P("col"), P("grp", "row"), P("grp", "col")),
        out_specs=(P(("grp", "row"), "col"), P(("row", "col"), "grp"), P(("row", "col"), "grp")),
        check_vma=False,
    )
```

profile of v0, /device:TPU:4, one launch (start us, length us, event | category | flops | bytes accessed | tf_op | source)
XLA Modules:
  0.0 822.6 jit_solution(5387528244009619449)
XLA Ops:
  8.0 0.0 copy-start
  8.0 0.0 all-reduce.3.cloned.1.call-start
  8.1 2.7 convolution_convert_fusion.1
  10.8 0.0 all-reduce.3.cloned.1.call-update
  10.8 0.0 all-reduce.5.cloned.1.call-start
  10.8 0.0 copy-start.3
  10.9 0.0 copy-start.1
  10.9 0.0 copy-start.2
  10.9 98.2 %all-reduce.3.cloned.1.call-done = bf16[384,1536]{1,0:T(8,128)(2,1)} async-done(((bf16[384,1536]{1,0:T(8,128)(2,1)}), bf16[384,1536]{1,0:T(8,128)(2,1)}) %all-reduce.3.cloned.1.call-update) | async-done | bytes 1179664 | tf_op jit(solution)/shard_map/psum | solution.py:16
  109.1 3.2 convolution_convert_fusion.2
  112.2 0.0 all-reduce.5.cloned.1.call-update
  112.2 0.0 all-gather.5.cloned.1.call-start
  112.3 0.6 gather_fusion.1
  113.0 0.7 bitcast_select_fusion
  113.7 0.0 all-gather.5.cloned.1.call-update
  113.7 0.0 all-gather.3.cloned.1.call-start
  113.8 0.6 gather_fusion
  114.4 0.7 bitcast_select_fusion.1
  115.1 0.0 all-gather.3.cloned.1.call-update
  115.1 0.0 reduce-scatter.4.cloned.1.call-start
  115.2 53.3 %all-reduce.5.cloned.1.call-done = bf16[384,768]{1,0:T(8,128)(2,1)} async-done(((bf16[384,768]{1,0:T(8,128)(2,1)}), bf16[384,768]{1,0:T(8,128)(2,1)}) %all-reduce.5.cloned.1.call-update) | async-done | bytes 589840 | tf_op jit(solution)/shard_map/psum | solution.py:18
  168.5 4.4 fusion
  172.9 4.4 copy.14
  177.3 0.0 reduce-scatter.4.cloned.1.call-update
  177.3 32.2 %all-gather.5.cloned.1.call-done = bf16[32,32,1536]{2,1,0:T(8,128)(2,1)} async-done(((bf16[1,32,1536]{2,1,0:T(8,128)(2,1)}), bf16[32,32,1536]{2,1,0:T(8,128)(2,1)}) %all-gather.5.cloned.1.call-update) | async-done | bytes 3145744 | tf_op jit(solution)/shard_map/all_gather | solution.py:35
  209.6 2.3 convolution_multiply_fusion
  211.9 597.0 %all-gather.3.cloned.1.call-done = bf16[128,32,384]{2,1,0:T(8,128)(2,1)} async-done(((bf16[1,32,384]{2,1,0:T(8,128)(2,1)}), bf16[128,32,384]{2,1,0:T(8,128)(2,1)}) %all-gather.3.cloned.1.call-update) | async-done | bytes 3145744 | tf_op jit(solution)/shard_map/all_gather | solution.py:32
  808.8 1.2 dynamic-slice_bitcast_fusion
  810.0 1.2 copy.12
  811.2 2.3 convolution_multiply_fusion.1
  813.6 1.1 copy.15
  814.6 0.9 copy.13
  (7 shorter events, 0.0 us)
Async XLA Ops:
  8.0 101.1 %copy-start = (bf16[1536,768]{1,0:T(8,128)(2,1)S(1)}, bf16[1536,768]{1,0:T(8,128)(2,1)}, u32[]{:S(2)}) copy-start(bf16[1536,768]{1,0:T(8,128)(2,1)} %param.9) | copy-start | bytes 7077892
  8.0 101.0 %all-reduce.3.cloned.1.call-start = ((), (), s32[]{:S(2)}) async-start(), calls=%async_computation.1 | async-start | bytes 2359296 | tf_op jit(solution)/shard_map/psum | solution.py:16
  10.8 157.7 %all-reduce.5.cloned.1.call-start = ((), (), s32[]{:S(2)}) async-start(), calls=%async_computation.2 | async-start | bytes 1179648 | tf_op jit(solution)/shard_map/psum | solution.py:18
  10.8 101.5 %copy-start.3 = (s32[32]{0:T(128)S(1)}, s32[32]{0:T(128)}, u32[]{:S(2)}) copy-start(s32[32]{0:T(128)} %param.7) | copy-start | bytes 388
  10.9 101.5 %copy-start.1 = (bf16[128,1536]{1,0:T(8,128)(2,1)S(1)}, bf16[128,1536]{1,0:T(8,128)(2,1)}, u32[]{:S(2)}) copy-start(bf16[128,1536]{1,0:T(8,128)(2,1)} %param.6) | copy-start | bytes 1179652
  10.9 102.9 %copy-start.2 = (bf16[128,384]{1,0:T(8,128)(2,1)S(1)}, bf16[128,384]{1,0:T(8,128)(2,1)}, u32[]{:S(2)}) copy-start(bf16[128,384]{1,0:T(8,128)(2,1)} %param.5) | copy-start | bytes 294916
  112.2 97.3 %all-gather.5.cloned.1.call-start = ((), (), s32[]{:S(2)}) async-start(), calls=%async_computation.4 | async-start | bytes 3244032 | tf_op jit(solution)/shard_map/all_gather | solution.py:35
  113.7 695.1 %all-gather.3.cloned.1.call-start = ((), (), s32[]{:S(2)}) async-start(), calls=%async_computation.3 | async-start | bytes 3170304 | tf_op jit(solution)/shard_map/all_gather | solution.py:32
  115.1 698.4 %reduce-scatter.4.cloned.1.call-start = ((), (), s32[]{:S(2)}) async-start(), calls=%async_computation.5 | async-start | bytes 2506752
Sparse Core Ops, SparseCore 0:
  11.8 97.2 all-reduce.2
  112.4 56.0 all-reduce.4
  177.4 75.7 reduce-scatter.3
Sparse Core Ops, SparseCore 1:
  115.4 94.1 all-gather.4
  212.1 596.7 all-gather.2
where the time goes:
time: 823 us
  waiting for transfers between devices  781 us (95%)
  between operations  15.4 us (2%)
  matrix products  14.9 us (2%)
  local copies, waits for them, and re-layouts  9.99 us (1%)
    all_gather x1, waiting for transfers between devices, body(): lax.all_gather(picked_x[None], ('row', 'col'), axis=0, tiled=True)  597 us
    psum x1, waiting for transfers between devices, body(): summed = lax.psum(term.astype(jnp.bfloat16), 'col')  98.2 us
    psum x1, waiting for transfers between devices, body(): right = lax.psum(part_right.astype(jnp.bfloat16), 'grp')  53.3 us
    all_gather x1, waiting for transfers between devices, body(): lax.all_gather(picked_g[None], ('grp', 'col'), axis=0, tiled=True)  32.2 us
  transfers between devices with their start and end apart: 5, of which 4 were waited for; matrix products, arithmetic and copies ran while one was open for 2% of the time, Pallas kernels for 0%

commit v1 on v0

v1 whole, which is shorter than its diff:
```python
import jax
import jax.numpy as jnp
from jax import lax
from jax.sharding import PartitionSpec as P

BF = jnp.bfloat16
F32 = jnp.float32
LANES = 128


def body(tokens_in, cotangent, sample_rows, act_inverse, grad_inverse):
    n_row = lax.axis_size("row")
    n_col = lax.axis_size("col")
    n_grp = lax.axis_size("grp")
    grp = lax.axis_index("grp")
    row = lax.axis_index("row")
    col = lax.axis_index("col")
    tok, feat_row = tokens_in.shape
    feat_grp = cotangent.shape[1]
    samp = sample_rows.shape[0]
    total = samp * n_col
    quarter = samp // n_grp
    tile = feat_row // n_col
    out_rows = feat_grp // n_row

    half = tok // 2
    g_lo = lax.all_gather(cotangent[:half], "col", axis=0)
    g_hi = lax.all_gather(cotangent[half:], "col", axis=0)

    part = lax.dot_general(
        act_inverse, tokens_in, (((1,), (1,)), ((), ())), preferred_element_type=F32
    ).astype(BF)
    part = part.reshape(n_row, out_rows, tok)
    offsets = sample_rows - col * tok
    own = lax.dynamic_slice_in_dim(offsets, grp * quarter, quarter, 0)
    picked_x = jnp.take(tokens_in, own, axis=0)
    strips = feat_row // LANES
    x_send = picked_x.reshape(quarter, strips, LANES).transpose(1, 0, 2)
    x_send = x_send.reshape(1, strips * quarter, LANES)
    x_send = jnp.broadcast_to(x_send, (n_row, strips * quarter, LANES))
    first = lax.all_to_all(jnp.concatenate([part, x_send], axis=1), "row", 0, 0)
    left = jnp.sum(first[:, :out_rows].astype(F32), axis=0).astype(BF)
    x_all = first[:, out_rows:].reshape(n_grp, -1, LANES)
    x_rows = x_all.shape[1]

    picked_g = jnp.take(cotangent, offsets, axis=0)
    own_g = lax.dynamic_slice_in_dim(picked_g, (row % n_grp) * feat_row, feat_row, 1)
    side_g = own_g.reshape(samp, n_col, tile).transpose(1, 0, 2)
    side_x = picked_x.reshape(quarter, n_col, tile).transpose(1, 0, 2)
    side_x = jnp.pad(side_x, ((0, 0), (0, samp - quarter), (0, 0)))
    place = jnp.broadcast_to(offsets.astype(BF)[None, :, None], (n_col, samp, LANES - 2 * tile))
    side = jnp.concatenate([side_g, side_x, place], axis=2)

    both = (n_grp, n_col)
    send = jnp.concatenate(
        [
            jnp.broadcast_to(left, both + left.shape),
            jnp.broadcast_to(x_all[:, None], both + x_all.shape[1:]),
            jnp.broadcast_to(side[None], both + side.shape[1:]),
        ],
        axis=2,
    )
    send = send.reshape((n_grp * n_col,) + send.shape[2:])
    got = lax.all_to_all(send, ("grp", "col"), 0, 0)
    got = got.reshape(both + got.shape[1:])
    lefts = got[:, :, :out_rows]
    samples_x = got[:, :, out_rows : out_rows + x_rows]
    sides = got[:, :, out_rows + x_rows :]

    v_lo = jnp.einsum("ctf,fn->ctn", g_lo, grad_inverse, preferred_element_type=F32).astype(BF)
    v_hi = jnp.einsum("ctf,fn->ctn", g_hi, grad_inverse, preferred_element_type=F32).astype(BF)
    v_all = jnp.concatenate([v_lo, v_hi], axis=1)
    term = jnp.einsum("gcat,ctn->gan", lefts, v_all, preferred_element_type=F32).astype(BF)
    term = lax.all_to_all(term, "grp", 0, 0)
    precond = jnp.sum(term.astype(F32), axis=0)

    scale = 1.0 / total
    x_full = samples_x.reshape(n_grp, n_col, x_rows // quarter, quarter, LANES)
    x_left = sides[:, :, :quarter, tile : 2 * tile]
    act_cov = jnp.einsum("gcsa,gcwsf->awf", x_left, x_full, preferred_element_type=F32)
    act_cov = act_cov.reshape(tile, feat_grp) * scale

    mine = lax.dynamic_index_in_dim(sides, row // n_grp, 0, keepdims=False)
    hot = mine[:, :, 2 * tile : 2 * tile + 1] == jnp.arange(tok, dtype=F32).astype(BF)
    spread = jnp.einsum(
        "cst,csa->cta", hot.astype(BF), mine[:, :, :tile], preferred_element_type=F32
    ).astype(BF)
    grad_cov = jnp.einsum(
        "cta,ctf->af", spread[:, :half], g_lo, preferred_element_type=F32
    ) + jnp.einsum("cta,ctf->af", spread[:, half:], g_hi, preferred_element_type=F32)
    return (precond, act_cov, grad_cov * scale)


def solution(mesh):
    return jax.shard_map(
        body,
        mesh=mesh,
        in_specs=(P("col", "row"), P("col", "grp"), P("col"), P("grp", "row"), P("grp", "col")),
        out_specs=(P(("grp", "row"), "col"), P(("row", "col"), "grp"), P(("row", "col"), "grp")),
        check_vma=False,
    )
```

time: 823 us -> 151 us (0.18)
  the two profiles are of different devices: /device:TPU:4 before, /device:TPU:1 now
where the time goes in v1:
time: 151 us; the launch traced here: 150 us
  waiting for transfers between devices  71 us (47%)
  starting transfers between devices  37.4 us (25%)
  matrix products  17.7 us (12%)
  between operations  14.3 us (9%)
  local copies, waits for them, and re-layouts  5.94 us (4%)
  other arithmetic  4.14 us (3%)
    all_gather x1, waiting for transfers between devices, body(): g_hi = lax.all_gather(cotangent[half:], 'col', axis=0)  43.9 us
    all_to_all x1, waiting for transfers between devices, body(): first = lax.all_to_all(jnp.concatenate([part, x_send], axis=1), 'row', 0, 0)  19.6 us
    all_to_all x1, starting transfers between devices, body(): first = lax.all_to_all(jnp.concatenate([part, x_send], axis=1), 'row', 0, 0)  15.8 us
    all_to_all x1, starting transfers between devices, body(): got = lax.all_to_all(send, ('grp', 'col'), 0, 0)  14.6 us
    all_to_all x1, starting transfers between devices, body(): term = lax.all_to_all(term, 'grp', 0, 0)  7.01 us
    all_to_all x1, waiting for transfers between devices, body(): term = lax.all_to_all(term, 'grp', 0, 0)  6.69 us
    dot_general x1, matrix products, body(): jnp.einsum('ctf,fn->ctn', g_lo, grad_inverse, preferred_element_type=F32)  3.73 us
    dot_general x1, matrix products, body(): jnp.einsum('ctf,fn->ctn', g_hi, grad_inverse, preferred_element_type=F32)  3.67 us
  transfers between devices with their start and end apart: 5, of which 3 were waited for; matrix products, arithmetic and copies ran while one was open for 12% of the time, Pallas kernels for 0%

profile of v1, /device:TPU:1, one launch (start us, length us, event | category | flops | bytes accessed | tf_op | source)
XLA Modules:
  0.0 150.4 jit_solution(2436868978416465685)
XLA Ops:
  7.2 1.9 %fusion.34 = (bf16[64,1536]{1,0:T(8,128)(2,1)}, bf16[64,1536]{1,0:T(8,128)(2,1)}) fusion(bf16[128,1536]{1,0:T(8,128)(2,1)} %param.6), kind=kLoop, calls=%fused_computation.58 | loop fusion | bytes 786432 | tf_op jit(solution)/shard_map/slice | solution.py:27
  9.2 0.7 compare_and_fusion
  9.9 0.1 compare_and_fusion.1
  9.9 1.5 gather_fusion
  11.5 1.8 %convolution_convert_fusion = bf16[1536,128]{1,0:T(8,128)(2,1)S(1)} fusion(bf16[1536,384]{1,0:T(8,128)(2,1)} %param.8, bf16[128,384]{1,0:T(8,128)(2,1)} %param.5), kind=kOutput, calls=%fused_computation.2 | convolution fusion | flops 151191552 | bytes 1671168 | tf_op jit(solution)/shard_map/dot_general | solution.py:30
  13.3 0.8 pad_maximum_fusion.1
  14.1 15.8 %all-to-all-start = ((bf16[16,120,128]{2,1,0:T(8,128)(2,1)}), bf16[16,120,128]{2,1,0:T(8,128)(2,1)S(1)}, u32[]{:S(2)}, u32[]{:S(2)}) async-start(bf16[16,120,128]{2,1,0:T(8,128)(2,1)} %pad_maximum_fusion.1), calls=%async_computation | async-start | bytes 983040 | tf_op jit(solution)/shard_map/all_to_all | solution.py:41
  30.0 0.7 all-gather.7.cloned.1.call-update
  30.7 0.1 gather.15
  30.8 0.6 gather_fusion.1
  31.5 0.1 reshape.56
  31.6 0.1 select_bitcast_fusion
  31.7 0.1 broadcast_in_dim.71
  31.8 0.1 fusion.27
  31.9 19.6 %all-to-all-done = bf16[16,120,128]{2,1,0:T(8,128)(2,1)S(1)} async-done(((bf16[16,120,128]{2,1,0:T(8,128)(2,1)}), bf16[16,120,128]{2,1,0:T(8,128)(2,1)S(1)}, u32[]{:S(2)}, u32[]{:S(2)}) %all-to-all-start) | async-done | bytes 491552 | tf_op jit(solution)/shard_map/all_to_all | solution.py:41
  51.7 0.1 broadcast_in_dim.65
  51.8 0.1 broadcast_in_dim.63
  51.9 1.4 pad_maximum_fusion
  53.3 14.6 %all-to-all-start.1 = ((bf16[32,224,128]{2,1,0:T(8,128)(2,1)}), bf16[32,224,128]{2,1,0:T(8,128)(2,1)}, u32[]{:S(2)}, u32[]{:S(2)}) async-start(bf16[32,224,128]{2,1,0:T(8,128)(2,1)} %bitcast.69), calls=%async_computation.1 | async-start | bytes 3670016 | tf_op jit(solution)/shard_map/all_to_all | solution.py:64
  68.0 3.7 %fusion.11 = bf16[8,64,768]{2,1,0:T(8,128)(2,1)} fusion(bf16[8,64,1536]{2,1,0:T(8,128)(2,1)} %bitcast.70, bf16[1536,768]{1,0:T(8,128)(2,1)S(1)} %copy-done), kind=kOutput, calls=%fused_computation.19 | convolution fusion | flops 1208352768 | bytes 4718592 | tf_op jit(solution)/shard_map/ctf,fn->ctn/dot_general | solution.py:70
  71.7 43.9 %all-gather.7.cloned.1.call-done = bf16[512,1536]{1,0:T(8,128)(2,1)} async-done(((bf16[64,1536]{1,0:T(8,128)(2,1)}), bf16[512,1536]{1,0:T(8,128)(2,1)}) %all-gather.7.cloned.1.call-update) | async-done | bytes 1572880 | tf_op jit(solution)/shard_map/all_gather | solution.py:28
  115.6 3.7 %fusion.14 = bf16[8,64,768]{2,1,0:T(8,128)(2,1)} fusion(bf16[8,64,1536]{2,1,0:T(8,128)(2,1)} %bitcast.72, bf16[1536,768]{1,0:T(8,128)(2,1)S(1)} %copy-done), kind=kOutput, calls=%fused_computation.20 | convolution fusion | flops 1208352768 | bytes 4718592 | tf_op jit(solution)/shard_map/ctf,fn->ctn/dot_general | solution.py:71
  119.3 1.1 slice.58
  120.4 2.2 %fusion.4 = f32[48,1536]{1,0:T(8,128)} fusion(bf16[4,8,224,128]{3,2,1,0:T(8,128)(2,1)} %bitcast.8), kind=kOutput, calls=%fused_computation.10 | convolution fusion | flops 37822464 | bytes 1146880 | tf_op jit(solution)/shard_map/gcsa,gcwsf->awf/dot_general | solution.py:80
  122.6 0.2 slice_reduce_fusion.1
  122.8 2.8 %fusion.17 = bf16[4,96,768]{2,1,0:T(8,128)(2,1)} fusion(bf16[8,64,768]{2,1,0:T(8,128)(2,1)S(1)} %copy-done.4, bf16[8,64,768]{2,1,0:T(8,128)(2,1)S(1)} %copy-done.3, bf16[4,8,224,128]{3,2,1,0:T(8,128)(2,1)} %bitcast.8), kind=kOutput, calls=%fused_computation.21 | convolution fusion | flops 607420416 | bytes 2949120 | tf_op jit(solution)/shard_map/gcat,ctn->gan/dot_general | solution.py:73
  125.6 7.0 %all-to-all-start.2 = ((bf16[4,96,768]{2,1,0:T(8,128)(2,1)}), bf16[4,96,768]{2,1,0:T(8,128)(2,1)S(1)}, u32[]{:S(2)}, u32[]{:S(2)}) async-start(bf16[4,96,768]{2,1,0:T(8,128)(2,1)} %fusion.17), calls=%async_computation.2 | async-start | bytes 1179648 | tf_op jit(solution)/shard_map/all_to_all | solution.py:74
  132.6 0.3 convolution_convert_fusion.1
  132.9 2.0 %convolution_bitcast_fusion = f32[48,1536]{1,0:T(8,128)S(1)} fusion(bf16[8,64,1536]{2,1,0:T(8,128)(2,1)} %bitcast.73, bf16[8,128,48]{1,2,0:T(8,128)(2,1)S(1)} %convolution_convert_fusion.1), kind=kOutput, calls=%fused_computation.7 | convolution fusion | flops 75497472 | bytes 1966080 | tf_op jit(solution)/shard_map/cta,ctf->af/dot_general | solution.py:90
  135.0 1.1 fusion.6
  136.1 6.7 %all-to-all-done.2 = bf16[4,96,768]{2,1,0:T(8,128)(2,1)S(1)} async-done(((bf16[4,96,768]{2,1,0:T(8,128)(2,1)}), bf16[4,96,768]{2,1,0:T(8,128)(2,1)S(1)}, u32[]{:S(2)}, u32[]{:S(2)}) %all-to-all-start.2) | async-done | bytes 589856 | tf_op jit(solution)/shard_map/all_to_all | solution.py:74
  142.8 0.8 convert_reduce_fusion
  (27 shorter events, 0.5 us)
Async XLA Ops:
  7.2 60.8 %copy-start = (bf16[1536,768]{1,0:T(8,128)(2,1)S(1)}, bf16[1536,768]{1,0:T(8,128)(2,1)}, u32[]{:S(2)}) copy-start(bf16[1536,768]{1,0:T(8,128)(2,1)} %param.9) | copy-start | bytes 7077892
  7.2 60.8 %all-gather.5.cloned.1.call-start = ((), (), s32[]{:S(2)}) async-start(), calls=%async_computation.3 | async-start | bytes 1769472 | tf_op jit(solution)/shard_map/all_gather | solution.py:27
  11.5 19.3 %copy-start.1 = (bf16[128,1536]{1,0:T(8,128)(2,1)S(1)}, bf16[128,1536]{1,0:T(8,128)(2,1)}, u32[]{:S(2)}) copy-start(bf16[128,1536]{1,0:T(8,128)(2,1)} %param.6) | copy-start | bytes 1179652
  14.1 37.4 %all-to-all-start = ((bf16[16,120,128]{2,1,0:T(8,128)(2,1)}), bf16[16,120,128]{2,1,0:T(8,128)(2,1)S(1)}, u32[]{:S(2)}, u32[]{:S(2)}) async-start(bf16[16,120,128]{2,1,0:T(8,128)(2,1)} %pad_maximum_fusion.1), calls=%async_computation | async-start | bytes 983040 | tf_op jit(solution)/shard_map/all_to_all | solution.py:41
  29.9 85.7 %all-gather.7.cloned.1.call-start = ((), (), s32[]{:S(2)}) async-start(), calls=%async_computation.4 | async-start | bytes 1769472 | tf_op jit(solution)/shard_map/all_gather | solution.py:28
  53.3 66.0 %all-to-all-start.1 = ((bf16[32,224,128]{2,1,0:T(8,128)(2,1)}), bf16[32,224,128]{2,1,0:T(8,128)(2,1)}, u32[]{:S(2)}, u32[]{:S(2)}) async-start(bf16[32,224,128]{2,1,0:T(8,128)(2,1)} %bitcast.69), calls=%async_computation.1 | async-start | bytes 3670016 | tf_op jit(solution)/shard_map/all_to_all | solution.py:64
  119.3 3.5 %copy-start.3 = (bf16[8,64,768]{2,1,0:T(8,128)(2,1)S(1)}, bf16[8,64,768]{2,1,0:T(8,128)(2,1)}, u32[]{:S(2)}) copy-start(bf16[8,64,768]{2,1,0:T(8,128)(2,1)} %fusion.11) | copy-start | bytes 2359300
  119.3 3.6 %copy-start.4 = (bf16[8,64,768]{2,1,0:T(8,128)(2,1)S(1)}, bf16[8,64,768]{2,1,0:T(8,128)(2,1)}, u32[]{:S(2)}) copy-start(bf16[8,64,768]{2,1,0:T(8,128)(2,1)} %fusion.14) | copy-start | bytes 2359300
  125.6 17.2 %all-to-all-start.2 = ((bf16[4,96,768]{2,1,0:T(8,128)(2,1)}), bf16[4,96,768]{2,1,0:T(8,128)(2,1)S(1)}, u32[]{:S(2)}, u32[]{:S(2)}) async-start(bf16[4,96,768]{2,1,0:T(8,128)(2,1)} %fusion.17), calls=%async_computation.2 | async-start | bytes 1179648 | tf_op jit(solution)/shard_map/all_to_all | solution.py:74
  132.6 2.3 %copy-start.2 = (bf16[512,1536]{1,0:T(8,128)(2,1)S(1)}, bf16[512,1536]{1,0:T(8,128)(2,1)}, u32[]{:S(2)}) copy-start(bf16[512,1536]{1,0:T(8,128)(2,1)} %all-gather.5.cloned.1.call-done) | copy-start | bytes 4718596
Sparse Core Ops, SparseCore 0:
  10.7 48.5 all-gather.4
  62.0 53.5 all-gather.6

commit v2 on v1

--- a/solution.py
+++ b/solution.py
@@ -23,9 +23,9 @@
     tile = feat_row // n_col
     out_rows = feat_grp // n_row
 
-    half = tok // 2
-    g_lo = lax.all_gather(cotangent[:half], "col", axis=0)
-    g_hi = lax.all_gather(cotangent[half:], "col", axis=0)
+    g_all = lax.all_to_all(
+        jnp.broadcast_to(cotangent, (n_col,) + cotangent.shape), "col", 0, 0
+    )
 
     part = lax.dot_general(
         act_inverse, tokens_in, (((1,), (1,)), ((), ())), preferred_element_type=F32
@@ -44,7 +44,8 @@
     x_rows = x_all.shape[1]
 
     picked_g = jnp.take(cotangent, offsets, axis=0)
-    own_g = lax.dynamic_slice_in_dim(picked_g, (row % n_grp) * feat_row, feat_row, 1)
+    per = feat_grp // feat_row
+    own_g = lax.dynamic_slice_in_dim(picked_g, (row % per) * feat_row, feat_row, 1)
     side_g = own_g.reshape(samp, n_col, tile).transpose(1, 0, 2)
     side_x = picked_x.reshape(quarter, n_col, tile).transpose(1, 0, 2)
     side_x = jnp.pad(side_x, ((0, 0), (0, samp - quarter), (0, 0)))
@@ -67,9 +68,7 @@
     samples_x = got[:, :, out_rows : out_rows + x_rows]
     sides = got[:, :, out_rows + x_rows :]
 
-    v_lo = jnp.einsum("ctf,fn->ctn", g_lo, grad_inverse, preferred_element_type=F32).astype(BF)
-    v_hi = jnp.einsum("ctf,fn->ctn", g_hi, grad_inverse, preferred_element_type=F32).astype(BF)
-    v_all = jnp.concatenate([v_lo, v_hi], axis=1)
+    v_all = jnp.einsum("ctf,fn->ctn", g_all, grad_inverse, preferred_element_type=F32).astype(BF)
     term = jnp.einsum("gcat,ctn->gan", lefts, v_all, preferred_element_type=F32).astype(BF)
     term = lax.all_to_all(term, "grp", 0, 0)
     precond = jnp.sum(term.astype(F32), axis=0)
@@ -80,14 +79,12 @@
     act_cov = jnp.einsum("gcsa,gcwsf->awf", x_left, x_full, preferred_element_type=F32)
     act_cov = act_cov.reshape(tile, feat_grp) * scale
 
-    mine = lax.dynamic_index_in_dim(sides, row // n_grp, 0, keepdims=False)
+    mine = lax.dynamic_index_in_dim(sides, row // per, 0, keepdims=False)
     hot = mine[:, :, 2 * tile : 2 * tile + 1] == jnp.arange(tok, dtype=F32).astype(BF)
     spread = jnp.einsum(
         "cst,csa->cta", hot.astype(BF), mine[:, :, :tile], preferred_element_type=F32
     ).astype(BF)
-    grad_cov = jnp.einsum(
-        "cta,ctf->af", spread[:, :half], g_lo, preferred_element_type=F32
-    ) + jnp.einsum("cta,ctf->af", spread[:, half:], g_hi, preferred_element_type=F32)
+    grad_cov = jnp.einsum("cta,ctf->af", spread, g_all, preferred_element_type=F32)
     return (precond, act_cov, grad_cov * scale)
 
 

time: 151 us -> 149 us (0.987)
  blocking collectives: 0 us -> 39.6 us
  between operations: 14.3 us -> 0.84 us
  starting transfers between devices: 37.4 us -> 24.4 us
  waiting for transfers between devices: 71 us -> 61.1 us
  matrix products: 17.7 us -> 14 us
    all_gather x2 -> x0, waiting for transfers between devices: 43.9 us -> none  [the longest x1 43.9 us: body(): g_hi = lax.all_gather(cotangent[half:], 'col', axis=0)]
    all_to_all x0 -> x1, blocking collectives: none -> 39.6 us  [body(): got = lax.all_to_all(send, ('grp', 'col'), 0, 0)]
    all_to_all x1, waiting for transfers between devices: 0.01 us -> 34.2 us  [body(): lax.all_to_all(jnp.broadcast_to(cotangent, (n_col,) + cotangent.shape), '...]
    all_to_all x1, starting transfers between devices: 14.6 us -> 4.45 us  [body(): lax.all_to_all(jnp.broadcast_to(cotangent, (n_col,) + cotangent.shape), '...]
    dot_general x5 -> x1, matrix products: 10.9 us -> 3.44 us  [body(): jnp.einsum('cta,ctf->af', spread, g_all, preferred_element_type=F32)]
    dot_general x1, matrix products: 2.76 us -> 6.49 us  [body(): jnp.einsum('gcat,ctn->gan', lefts, v_all, preferred_element_type=F32)]
    all_to_all x1, starting transfers between devices: 7.01 us -> 4.18 us  [body(): term = lax.all_to_all(term, 'grp', 0, 0)]
    broadcast_in_dim x0 -> x1, local copies, waits for them, and re-layouts: none -> 1.95 us  [body(): jnp.broadcast_to(cotangent, (n_col,) + cotangent.shape)]
  transfers between devices with their start and end apart: 5 -> 3, of which waited for: 3 -> 3; matrix products, arithmetic and copies ran while one was open for 12% -> 5% of each run, Pallas kernels for 0% -> 0%
where the time goes in v2:
time: 149 us
  waiting for transfers between devices  61.1 us (41%)
  blocking collectives  39.6 us (27%)
  starting transfers between devices  24.4 us (16%)
  matrix products  14 us (9%)
  local copies, waits for them, and re-layouts  5.82 us (4%)
  other arithmetic  3.04 us (2%)
    all_to_all x1, blocking collectives, body(): got = lax.all_to_all(send, ('grp', 'col'), 0, 0)  39.6 us
    all_to_all x1, waiting for transfers between devices, body(): lax.all_to_all(jnp.broadcast_to(cotangent, (n_col,) + cotangent.shape), '...  34.2 us
    all_to_all x1, waiting for transfers between devices, body(): first = lax.all_to_all(jnp.concatenate([part, x_send], axis=1), 'row', 0, 0)  20.4 us
    all_to_all x1, starting transfers between devices, body(): first = lax.all_to_all(jnp.concatenate([part, x_send], axis=1), 'row', 0, 0)  15.8 us
    all_to_all x1, waiting for transfers between devices, body(): term = lax.all_to_all(term, 'grp', 0, 0)  6.55 us
    dot_general x1, matrix products, body(): jnp.einsum('gcat,ctn->gan', lefts, v_all, preferred_element_type=F32)  6.49 us
    all_to_all x1, starting transfers between devices, body(): lax.all_to_all(jnp.broadcast_to(cotangent, (n_col,) + cotangent.shape), '...  4.45 us
    all_to_all x1, starting transfers between devices, body(): term = lax.all_to_all(term, 'grp', 0, 0)  4.18 us
  transfers between devices with their start and end apart: 3, of which 3 were waited for; matrix products, arithmetic and copies ran while one was open for 5% of the time, Pallas kernels for 0%

profile of v2, /device:TPU:1, one launch (start us, length us, event | category | flops | bytes accessed | tf_op | source)
XLA Modules:
  0.0 148.8 jit_solution(13057539111422974886)
XLA Ops:
  0.6 0.0 copy-start
  0.7 0.8 compare_and_fusion
  1.5 0.1 compare_and_fusion.1
  1.6 1.5 gather_fusion
  3.0 1.8 %convolution_convert_fusion = bf16[1536,128]{1,0:T(8,128)(2,1)S(1)} fusion(bf16[1536,384]{1,0:T(8,128)(2,1)} %param.8, bf16[128,384]{1,0:T(8,128)(2,1)} %param.5), kind=kOutput, calls=%fused_computation.2 | convolution fusion | flops 151191552 | bytes 1671168 | tf_op jit(solution)/shard_map/dot_general | solution.py:30
  4.8 0.1 fusion.35
  4.9 0.8 pad_maximum_fusion.1
  5.7 15.8 %all-to-all-start = ((bf16[16,120,128]{2,1,0:T(8,128)(2,1)}), bf16[16,120,128]{2,1,0:T(8,128)(2,1)S(1)}, u32[]{:S(2)}, u32[]{:S(2)}) async-start(bf16[16,120,128]{2,1,0:T(8,128)(2,1)} %pad_maximum_fusion.1), calls=%async_computation | async-start | bytes 983040 | tf_op jit(solution)/shard_map/all_to_all | solution.py:41
  21.5 0.1 gather.15
  21.6 0.6 gather_fusion.1
  22.3 0.1 dynamic-slice_select_fusion
  22.4 0.1 reshape.56
  22.5 0.1 select_bitcast_fusion
  22.6 0.1 broadcast_in_dim.74
  22.7 0.1 fusion.27
  22.8 20.4 %all-to-all-done = bf16[16,120,128]{2,1,0:T(8,128)(2,1)S(1)} async-done(((bf16[16,120,128]{2,1,0:T(8,128)(2,1)}), bf16[16,120,128]{2,1,0:T(8,128)(2,1)S(1)}, u32[]{:S(2)}, u32[]{:S(2)}) %all-to-all-start) | async-done | bytes 491552 | tf_op jit(solution)/shard_map/all_to_all | solution.py:41
  43.2 0.1 slice_reduce_fusion
  43.3 0.1 broadcast_in_dim.68
  43.4 0.1 broadcast_in_dim.66
  43.5 0.1 pad_maximum_fusion
  43.7 39.6 %all_to_all.20 = bf16[32,224,128]{2,1,0:T(8,128)(2,1)} all-to-all(bf16[32,224,128]{2,1,0:T(8,128)(2,1)S(1)} %bitcast.61), channel_id=1, replica_groups=mesh['grp'=4,'row'=16,'col'=8] {'grp','col'}, dimensions={0} | all-to-all | bytes 3670016 | tf_op jit(solution)/shard_map/all_to_all | solution.py:65
  83.2 1.9 %broadcast_in_dim.76 = bf16[8,128,1536]{2,1,0:T(8,128)(2,1)} broadcast(bf16[128,1536]{1,0:T(8,128)(2,1)S(1)} %copy-done.1), dimensions={1,2} | broadcast | bytes 3538944 | tf_op jit(solution)/shard_map/broadcast_in_dim | solution.py:27
  85.2 4.5 %all-to-all-start.2 = ((bf16[8,128,1536]{2,1,0:T(8,128)(2,1)}), bf16[8,128,1536]{2,1,0:T(8,128)(2,1)}, u32[]{:S(2)}, u32[]{:S(2)}) async-start(bf16[8,128,1536]{2,1,0:T(8,128)(2,1)} %broadcast_in_dim.76), calls=%async_computation.2 | async-start | bytes 6291456 | tf_op jit(solution)/shard_map/all_to_all | solution.py:26
  89.7 1.0 slice.42
  90.7 2.2 %fusion.3 = f32[48,1536]{1,0:T(8,128)} fusion(bf16[4,8,224,128]{3,2,1,0:T(8,128)(2,1)} %bitcast.63), kind=kOutput, calls=%fused_computation.8 | convolution fusion | flops 37822464 | bytes 1146880 | tf_op jit(solution)/shard_map/gcsa,gcwsf->awf/dot_general | solution.py:79
  92.9 34.2 %all-to-all-done.2 = bf16[8,128,1536]{2,1,0:T(8,128)(2,1)} async-done(((bf16[8,128,1536]{2,1,0:T(8,128)(2,1)}), bf16[8,128,1536]{2,1,0:T(8,128)(2,1)}, u32[]{:S(2)}, u32[]{:S(2)}) %all-to-all-start.2) | async-done | bytes 3145760 | tf_op jit(solution)/shard_map/all_to_all | solution.py:26
  127.1 6.5 %fusion.12 = bf16[4,96,768]{2,1,0:T(8,128)(2,1)} fusion(bf16[8,128,1536]{2,1,0:T(8,128)(2,1)} %all-to-all-done.2, bf16[1536,768]{1,0:T(8,128)(2,1)S(1)} %copy-done, bf16[4,8,224,128]{3,2,1,0:T(8,128)(2,1)} %bitcast.64), kind=kOutput, calls=%fused_computation.14 | convolution fusion | flops 3020980224 | bytes 6881280 | tf_op jit(solution)/shard_map/gcat,ctn->gan/dot_general | solution.py:72
  133.6 4.2 %all-to-all-start.3 = ((bf16[4,96,768]{2,1,0:T(8,128)(2,1)}), bf16[4,96,768]{2,1,0:T(8,128)(2,1)S(1)}, u32[]{:S(2)}, u32[]{:S(2)}) async-start(bf16[4,96,768]{2,1,0:T(8,128)(2,1)} %fusion.12), calls=%async_computation.3 | async-start | bytes 1179648 | tf_op jit(solution)/shard_map/all_to_all | solution.py:73
  137.8 0.2 slice_reduce_fusion.1
  138.0 3.4 %fusion.2 = f32[48,1536]{1,0:T(8,128)} fusion(bf16[8,128,1536]{2,1,0:T(8,128)(2,1)} %all-to-all-done.2, bf16[8,32,128]{2,1,0:T(8,128)(2,1)S(1)} %dynamic-slice_bitcast_fusion, bf16[128]{0:T(256)(128)(2,1)S(1)} %iota_convert_fusion, bf16[8,32]{1,0:T(8,128)(2,1)S(1)} %slice_reduce_fusion.1), kind=kOutput, calls=%fused_computation.6 | convolution fusion | flops 154296320 | bytes 3506944 | tf_op jit(solution)/shard_map/cta,ctf->af/dot_general | solution.py:87
  141.4 6.6 %all-to-all-done.3 = bf16[4,96,768]{2,1,0:T(8,128)(2,1)S(1)} async-done(((bf16[4,96,768]{2,1,0:T(8,128)(2,1)}), bf16[4,96,768]{2,1,0:T(8,128)(2,1)S(1)}, u32[]{:S(2)}, u32[]{:S(2)}) %all-to-all-start.3) | async-done | bytes 589856 | tf_op jit(solution)/shard_map/all_to_all | solution.py:73
  148.0 0.8 convert_reduce_fusion
  (12 shorter events, 0.1 us)
Async XLA Ops:
  0.6 126.5 %copy-start = (bf16[1536,768]{1,0:T(8,128)(2,1)S(1)}, bf16[1536,768]{1,0:T(8,128)(2,1)}, u32[]{:S(2)}) copy-start(bf16[1536,768]{1,0:T(8,128)(2,1)} %param.9) | copy-start | bytes 7077892
  3.0 18.6 %copy-start.1 = (bf16[128,1536]{1,0:T(8,128)(2,1)S(1)}, bf16[128,1536]{1,0:T(8,128)(2,1)}, u32[]{:S(2)}) copy-start(bf16[128,1536]{1,0:T(8,128)(2,1)} %param.6) | copy-start | bytes 1179652
  5.7 37.4 %all-to-all-start = ((bf16[16,120,128]{2,1,0:T(8,128)(2,1)}), bf16[16,120,128]{2,1,0:T(8,128)(2,1)S(1)}, u32[]{:S(2)}, u32[]{:S(2)}) async-start(bf16[16,120,128]{2,1,0:T(8,128)(2,1)} %pad_maximum_fusion.1), calls=%async_computation | async-start | bytes 983040 | tf_op jit(solution)/shard_map/all_to_all | solution.py:41
  85.2 41.9 %all-to-all-start.2 = ((bf16[8,128,1536]{2,1,0:T(8,128)(2,1)}), bf16[8,128,1536]{2,1,0:T(8,128)(2,1)}, u32[]{:S(2)}, u32[]{:S(2)}) async-start(bf16[8,128,1536]{2,1,0:T(8,128)(2,1)} %broadcast_in_dim.76), calls=%async_computation.2 | async-start | bytes 6291456 | tf_op jit(solution)/shard_map/all_to_all | solution.py:26
  133.6 14.4 %all-to-all-start.3 = ((bf16[4,96,768]{2,1,0:T(8,128)(2,1)}), bf16[4,96,768]{2,1,0:T(8,128)(2,1)S(1)}, u32[]{:S(2)}, u32[]{:S(2)}) async-start(bf16[4,96,768]{2,1,0:T(8,128)(2,1)} %fusion.12), calls=%async_computation.3 | async-start | bytes 1179648 | tf_op jit(solution)/shard_map/all_to_all | solution.py:73

commit v3 on v2

--- a/solution.py
+++ b/solution.py
@@ -23,9 +23,6 @@
     tile = feat_row // n_col
     out_rows = feat_grp // n_row
 
-    g_all = lax.all_to_all(
-        jnp.broadcast_to(cotangent, (n_col,) + cotangent.shape), "col", 0, 0
-    )
 
     part = lax.dot_general(
         act_inverse, tokens_in, (((1,), (1,)), ((), ())), preferred_element_type=F32
@@ -38,7 +35,14 @@
     x_send = picked_x.reshape(quarter, strips, LANES).transpose(1, 0, 2)
     x_send = x_send.reshape(1, strips * quarter, LANES)
     x_send = jnp.broadcast_to(x_send, (n_row, strips * quarter, LANES))
-    first = lax.all_to_all(jnp.concatenate([part, x_send], axis=1), "row", 0, 0)
+    payload, own_cot = lax.optimization_barrier(
+        (jnp.concatenate([part, x_send], axis=1), cotangent)
+    )
+    first = lax.all_to_all(payload, "row", 0, 0)
+    blocks = [cotangent] + [
+        lax.ppermute(own_cot, "col", [(i, (i + k) % n_col) for i in range(n_col)])
+        for k in range(1, n_col)
+    ]
     left = jnp.sum(first[:, :out_rows].astype(F32), axis=0).astype(BF)
     x_all = first[:, out_rows:].reshape(n_grp, -1, LANES)
     x_rows = x_all.shape[1]
@@ -68,8 +72,13 @@
     samples_x = got[:, :, out_rows : out_rows + x_rows]
     sides = got[:, :, out_rows + x_rows :]
 
-    v_all = jnp.einsum("ctf,fn->ctn", g_all, grad_inverse, preferred_element_type=F32).astype(BF)
-    term = jnp.einsum("gcat,ctn->gan", lefts, v_all, preferred_element_type=F32).astype(BF)
+    term = jnp.zeros((n_grp, out_rows, grad_inverse.shape[1]), F32)
+    for k, block in enumerate(blocks):
+        source = (col - k) % n_col
+        v_blk = jnp.dot(block, grad_inverse, preferred_element_type=F32).astype(BF)
+        u_blk = lax.dynamic_index_in_dim(lefts, source, 1, keepdims=False)
+        term = term + jnp.einsum("gat,tn->gan", u_blk, v_blk, preferred_element_type=F32)
+    term = term.astype(BF)
     term = lax.all_to_all(term, "grp", 0, 0)
     precond = jnp.sum(term.astype(F32), axis=0)
 
@@ -84,7 +93,10 @@
     spread = jnp.einsum(
         "cst,csa->cta", hot.astype(BF), mine[:, :, :tile], preferred_element_type=F32
     ).astype(BF)
-    grad_cov = jnp.einsum("cta,ctf->af", spread, g_all, preferred_element_type=F32)
+    grad_cov = jnp.zeros((tile, feat_grp), F32)
+    for k, block in enumerate(blocks):
+        mask = lax.dynamic_index_in_dim(spread, (col - k) % n_col, 0, keepdims=False)
+        grad_cov = grad_cov + jnp.einsum("ta,tf->af", mask, block, preferred_element_type=F32)
     return (precond, act_cov, grad_cov * scale)
 
 

time: 149 us -> 177 us (1.19)
  starting transfers between devices: 24.4 us -> 75.1 us
  blocking collectives: 39.6 us -> 0 us
  matrix products: 14 us -> 39.2 us
  waiting for transfers between devices: 61.1 us -> 48.5 us
  local copies, waits for them, and re-layouts: 5.82 us -> 7.81 us
    all_to_all x1 -> x0, blocking collectives: 39.6 us -> none  [body(): got = lax.all_to_all(send, ('grp', 'col'), 0, 0)]
    ppermute x0 -> x7, starting transfers between devices: none -> 39 us  [body(): lax.ppermute(own_cot, 'col', [(i, (i + k) % n_col) for i in range(n_col)])]
    all_to_all x2, waiting for transfers between devices: 54.6 us -> 28.1 us  [the longest x1 20.4 us: body(): first = lax.all_to_all(payload, 'row', 0, 0)]
    dot_general x2 -> x17, matrix products: 9.93 us -> 35.4 us  [the longest x8 25.2 us: body(): jnp.einsum('gat,tn->gan', u_blk, v_blk, preferred_element_type=F32)]
    ppermute x0 -> x7, waiting for transfers between devices: none -> 19.3 us  [body(): lax.ppermute(own_cot, 'col', [(i, (i + k) % n_col) for i in range(n_col)])]
    all_to_all x2, starting transfers between devices: 20.2 us -> 30.3 us  [the longest x1 15.7 us: body(): first = lax.all_to_all(payload, 'row', 0, 0)]
    all_to_all x1, waiting for transfers between devices: 6.55 us -> 1.05 us  [body(): term = lax.all_to_all(term, 'grp', 0, 0)]
    reshape x0 -> x1, local copies, waits for them, and re-layouts: none -> 2.39 us  [body(): x_full = samples_x.reshape(n_grp, n_col, x_rows // quarter, quarter, LANES)]
  transfers between devices with their start and end apart: 3 -> 10, of which waited for: 3 -> 4; matrix products, arithmetic and copies ran while one was open for 5% -> 23% of each run, Pallas kernels for 0% -> 0%
where the time goes in v3:
time: 177 us; the launch traced here: 176 us
  starting transfers between devices  75.1 us (42%)
  waiting for transfers between devices  48.5 us (27%)
  matrix products  39.2 us (22%)
  local copies, waits for them, and re-layouts  7.81 us (4%)
  other arithmetic  4.29 us (2%)
    ppermute x7, starting transfers between devices, body(): lax.ppermute(own_cot, 'col', [(i, (i + k) % n_col) for i in range(n_col)])  39 us
    dot_general x8, matrix products, body(): jnp.einsum('gat,tn->gan', u_blk, v_blk, preferred_element_type=F32)  25.2 us
    all_to_all x1, waiting for transfers between devices, body(): first = lax.all_to_all(payload, 'row', 0, 0)  20.4 us
    ppermute x7, waiting for transfers between devices, body(): lax.ppermute(own_cot, 'col', [(i, (i + k) % n_col) for i in range(n_col)])  19.3 us
    all_to_all x1, starting transfers between devices, body(): first = lax.all_to_all(payload, 'row', 0, 0)  15.7 us
    all_to_all x1, starting transfers between devices, body(): got = lax.all_to_all(send, ('grp', 'col'), 0, 0)  14.6 us
    dot_general x8, matrix products, body(): jnp.einsum('ta,tf->af', mask, block, preferred_element_type=F32)  10 us
    all_to_all x1, waiting for transfers between devices, body(): got = lax.all_to_all(send, ('grp', 'col'), 0, 0)  7.78 us
  transfers between devices with their start and end apart: 10, of which 4 were waited for; matrix products, arithmetic and copies ran while one was open for 23% of the time, Pallas kernels for 0%

profile of v3, /device:TPU:1, one launch (start us, length us, event | category | flops | bytes accessed | tf_op | source)
XLA Modules:
  0.0 176.0 jit_solution(2080159198067351434)
XLA Ops:
  1.6 1.5 gather_fusion
  3.1 1.8 %convolution_convert_fusion = bf16[1536,128]{1,0:T(8,128)(2,1)S(1)} fusion(bf16[1536,384]{1,0:T(8,128)(2,1)} %param.8, bf16[128,384]{1,0:T(8,128)(2,1)} %param.5), kind=kOutput, calls=%fused_computation.2 | convolution fusion | flops 151191552 | bytes 1671168 | tf_op jit(solution)/shard_map/dot_general | solution.py:27
  5.8 15.7 %all-to-all-start = ((bf16[16,120,128]{2,1,0:T(8,128)(2,1)}), bf16[16,120,128]{2,1,0:T(8,128)(2,1)S(1)}, u32[]{:S(2)}, u32[]{:S(2)}) async-start(bf16[16,120,128]{2,1,0:T(8,128)(2,1)} %pad_maximum_fusion.1), calls=%async_computation | async-start | bytes 983040 | tf_op jit(solution)/shard_map/all_to_all | solution.py:41
  22.8 20.4 %all-to-all-done = bf16[16,120,128]{2,1,0:T(8,128)(2,1)S(1)} async-done(((bf16[16,120,128]{2,1,0:T(8,128)(2,1)}), bf16[16,120,128]{2,1,0:T(8,128)(2,1)S(1)}, u32[]{:S(2)}, u32[]{:S(2)}) %all-to-all-start) | async-done | bytes 491552 | tf_op jit(solution)/shard_map/all_to_all | solution.py:41
  43.5 1.4 pad_maximum_fusion
  44.9 14.6 %all-to-all-start.1 = ((bf16[32,224,128]{2,1,0:T(8,128)(2,1)}), bf16[32,224,128]{2,1,0:T(8,128)(2,1)}, u32[]{:S(2)}, u32[]{:S(2)}) async-start(bf16[32,224,128]{2,1,0:T(8,128)(2,1)} %bitcast.136), calls=%async_computation.1 | async-start | bytes 3670016 | tf_op jit(solution)/shard_map/all_to_all | solution.py:69
  59.5 5.4 %collective-permute-start.6 = (bf16[128,1536]{1,0:T(8,128)(2,1)S(1)}, bf16[128,1536]{1,0:T(8,128)(2,1)}, u32[]{:S(2)}, u32[]{:S(2)}) collective-permute-start(bf16[128,1536]{1,0:T(8,128)(2,1)S(1)} %copy-done.1), channel_id=1, source_target_pairs={{0,7},{1,0},{2,1},{3,2},{4,3},{5,4},{6,5},{7,6},{8,15},{9,8},{10,9... | collective-permute-start | bytes 1179656 | tf_op jit(solution)/shard_map/ppermute | solution.py:43
  64.9 2.5 %collective-permute-start.5 = (bf16[128,1536]{1,0:T(8,128)(2,1)S(1)}, bf16[128,1536]{1,0:T(8,128)(2,1)}, u32[]{:S(2)}, u32[]{:S(2)}) collective-permute-start(bf16[128,1536]{1,0:T(8,128)(2,1)S(1)} %copy-done.1), channel_id=1, source_target_pairs={{0,6},{1,7},{2,0},{3,1},{4,2},{5,3},{6,4},{7,5},{8,14},{9,15},{10,... | collective-permute-start | bytes 1179656 | tf_op jit(solution)/shard_map/ppermute | solution.py:43
  67.4 2.5 %collective-permute-start.4 = (bf16[128,1536]{1,0:T(8,128)(2,1)S(1)}, bf16[128,1536]{1,0:T(8,128)(2,1)}, u32[]{:S(2)}, u32[]{:S(2)}) collective-permute-start(bf16[128,1536]{1,0:T(8,128)(2,1)S(1)} %copy-done.1), channel_id=1, source_target_pairs={{0,5},{1,6},{2,7},{3,0},{4,1},{5,2},{6,3},{7,4},{8,13},{9,14},{10,... | collective-permute-start | bytes 1179656 | tf_op jit(solution)/shard_map/ppermute | solution.py:43
  69.9 3.7 %collective-permute-start.1 = (bf16[128,1536]{1,0:T(8,128)(2,1)S(1)}, bf16[128,1536]{1,0:T(8,128)(2,1)}, u32[]{:S(2)}, u32[]{:S(2)}) collective-permute-start(bf16[128,1536]{1,0:T(8,128)(2,1)S(1)} %copy-done.1), channel_id=1, source_target_pairs={{0,2},{1,3},{2,4},{3,5},{4,6},{5,7},{6,0},{7,1},{8,10},{9,11},{10,... | collective-permute-start | bytes 1179656 | tf_op jit(solution)/shard_map/ppermute | solution.py:43
  73.7 2.8 %collective-permute-start = (bf16[128,1536]{1,0:T(8,128)(2,1)S(1)}, bf16[128,1536]{1,0:T(8,128)(2,1)}, u32[]{:S(2)}, u32[]{:S(2)}) collective-permute-start(bf16[128,1536]{1,0:T(8,128)(2,1)S(1)} %copy-done.1), channel_id=1, source_target_pairs={{0,1},{1,2},{2,3},{3,4},{4,5},{5,6},{6,7},{7,0},{8,9},{9,10},{10,1... | collective-permute-start | bytes 1179656 | tf_op jit(solution)/shard_map/ppermute | solution.py:43
  76.6 7.8 %all-to-all-done.1 = bf16[32,224,128]{2,1,0:T(8,128)(2,1)} async-done(((bf16[32,224,128]{2,1,0:T(8,128)(2,1)}), bf16[32,224,128]{2,1,0:T(8,128)(2,1)}, u32[]{:S(2)}, u32[]{:S(2)}) %all-to-all-start.1) | async-done | bytes 1835040 | tf_op jit(solution)/shard_map/all_to_all | solution.py:69
  84.4 2.4 %slice_bitcast_fusion = (bf16[4,8,12,8,128]{4,3,2,1,0:T(8,128)(2,1)S(1)}, bf16[4,8,96,128]{3,2,1,0:T(8,128)(2,1)}) fusion(bf16[4,8,224,128]{3,2,1,0:T(8,128)(2,1)} %bitcast.8), kind=kLoop, calls=%fused_computation.41 | loop fusion | bytes 3145728 | tf_op jit(solution)/shard_map/reshape | solution.py:86
  86.8 2.7 %fusion.16 = f32[4,96,768]{2,1,0:T(8,128)} fusion(bf16[128,1536]{1,0:T(8,128)(2,1)S(1)} %copy-done.1, bf16[1536,768]{1,0:T(8,128)(2,1)S(1)} %copy-done, bf16[4,8,96,128]{3,2,1,0:T(8,128)(2,1)} %get-tuple-element.12, s32[]{:T(128)S(6)} %select_n.134), kind=kOutput, calls=%fused_computation.40 | convolution fusion | flops 377585664 | bytes 4030468 | tf_op jit(solution)/shard_map/gat,tn->gan/dot_general | solution.py:80
  89.5 19.3 %collective-permute-done = bf16[128,1536]{1,0:T(8,128)(2,1)} collective-permute-done((bf16[128,1536]{1,0:T(8,128)(2,1)S(1)}, bf16[128,1536]{1,0:T(8,128)(2,1)}, u32[]{:S(2)}, u32[]{:S(2)}) %collective-permute-start) | collective-permute-done | bytes 393248 | tf_op jit(solution)/shard_map/ppermute | solution.py:43
  108.7 18.5 %collective-permute-start.2 = (bf16[128,1536]{1,0:T(8,128)(2,1)S(1)}, bf16[128,1536]{1,0:T(8,128)(2,1)}, u32[]{:S(2)}, u32[]{:S(2)}) collective-permute-start(bf16[128,1536]{1,0:T(8,128)(2,1)S(1)} %copy-done.1), channel_id=1, source_target_pairs={{0,3},{1,4},{2,5},{3,6},{4,7},{5,0},{6,1},{7,2},{8,11},{9,12},{10,... | collective-permute-start | bytes 1179656 | tf_op jit(solution)/shard_map/ppermute | solution.py:43
  127.2 3.2 %convolution_add_fusion.8 = f32[4,96,768]{2,1,0:T(8,128)} fusion(f32[4,96,768]{2,1,0:T(8,128)} %fusion.16, bf16[128,1536]{1,0:T(8,128)(2,1)} %collective-permute-done, bf16[1536,768]{1,0:T(8,128)(2,1)S(1)} %copy-done, bf16[4,8,96,128]{3,2,1,0:T(8,128)(2,1)} %get-tuple-element.12, s32[]{:T(128)S(6)} %select_n.136), kind=kOutput, calls=%fused_computation.20 | convolution fusion | flops 377880576 | bytes 5210116 | tf_op jit(solution)/shard_map/gat,tn->gan/dot_general | solution.py:80
  130.5 1.7 slice.42
  132.1 3.6 %collective-permute-start.3 = (bf16[128,1536]{1,0:T(8,128)(2,1)S(1)}, bf16[128,1536]{1,0:T(8,128)(2,1)}, u32[]{:S(2)}, u32[]{:S(2)}) collective-permute-start(bf16[128,1536]{1,0:T(8,128)(2,1)S(1)} %copy-done.1), channel_id=1, source_target_pairs={{0,4},{1,5},{2,6},{3,7},{4,0},{5,1},{6,2},{7,3},{8,12},{9,13},{10,... | collective-permute-start | bytes 1179656 | tf_op jit(solution)/shard_map/ppermute | solution.py:43
  135.8 3.2 %convolution_add_fusion.7 = f32[4,96,768]{2,1,0:T(8,128)} fusion(f32[4,96,768]{2,1,0:T(8,128)} %convolution_add_fusion.8, bf16[128,1536]{1,0:T(8,128)(2,1)} %collective-permute-done.1, bf16[1536,768]{1,0:T(8,128)(2,1)S(1)} %copy-done, bf16[4,8,96,128]{3,2,1,0:T(8,128)(2,1)} %get-tuple-element.12, s32[]{:T(128)S(6)} %select_n.138), kind=kOutput, calls=%fused_computation.19 | convolution fusion | flops 377880576 | bytes 5210116 | tf_op jit(solution)/shard_map/gat,tn->gan/dot_general | solution.py:80
  139.0 3.2 %convolution_add_fusion.6 = f32[4,96,768]{2,1,0:T(8,128)} fusion(f32[4,96,768]{2,1,0:T(8,128)} %convolution_add_fusion.7, bf16[128,1536]{1,0:T(8,128)(2,1)} %collective-permute-done.2, bf16[1536,768]{1,0:T(8,128)(2,1)S(1)} %copy-done, bf16[4,8,96,128]{3,2,1,0:T(8,128)(2,1)} %get-tuple-element.12, s32[]{:T(128)S(6)} %select_n.140), kind=kOutput, calls=%fused_computation.18 | convolution fusion | flops 377880576 | bytes 5210116 | tf_op jit(solution)/shard_map/gat,tn->gan/dot_general | solution.py:80
  143.1 1.9 %fusion.6 = f32[48,1536]{1,0:T(8,128)} fusion(bf16[4,8,12,8,128]{4,3,2,1,0:T(8,128)(2,1)S(1)} %get-tuple-element.11, bf16[4,8,224,128]{3,2,1,0:T(8,128)(2,1)} %bitcast.8), kind=kOutput, calls=%fused_computation.12 | convolution fusion | flops 37822464 | bytes 1146880 | tf_op jit(solution)/shard_map/gcsa,gcwsf->awf/dot_general | solution.py:88
  145.2 3.2 %convolution_add_fusion.5 = f32[4,96,768]{2,1,0:T(8,128)} fusion(f32[4,96,768]{2,1,0:T(8,128)} %convolution_add_fusion.6, bf16[128,1536]{1,0:T(8,128)(2,1)} %collective-permute-done.3, bf16[1536,768]{1,0:T(8,128)(2,1)S(1)} %copy-done, bf16[4,8,96,128]{3,2,1,0:T(8,128)(2,1)} %get-tuple-element.12, s32[]{:T(128)S(6)} %select_n.142), kind=kOutput, calls=%fused_computation.17 | convolution fusion | flops 377880576 | bytes 5210116 | tf_op jit(solution)/shard_map/gat,tn->gan/dot_general | solution.py:80
  148.5 3.3 %convolution_add_fusion.4 = f32[4,96,768]{2,1,0:T(8,128)} fusion(f32[4,96,768]{2,1,0:T(8,128)} %convolution_add_fusion.5, bf16[128,1536]{1,0:T(8,128)(2,1)} %collective-permute-done.4, bf16[1536,768]{1,0:T(8,128)(2,1)S(1)} %copy-done, bf16[4,8,96,128]{3,2,1,0:T(8,128)(2,1)} %get-tuple-element.12, s32[]{:T(128)S(6)} %select_n.144), kind=kOutput, calls=%fused_computation.16 | convolution fusion | flops 377880576 | bytes 5210116 | tf_op jit(solution)/shard_map/gat,tn->gan/dot_general | solution.py:80
  153.0 3.2 %convolution_add_fusion.3 = f32[4,96,768]{2,1,0:T(8,128)} fusion(f32[4,96,768]{2,1,0:T(8,128)} %convolution_add_fusion.4, bf16[128,1536]{1,0:T(8,128)(2,1)} %collective-permute-done.5, bf16[1536,768]{1,0:T(8,128)(2,1)S(1)} %copy-done, bf16[4,8,96,128]{3,2,1,0:T(8,128)(2,1)} %get-tuple-element.12, s32[]{:T(128)S(6)} %select_n.146), kind=kOutput, calls=%fused_computation.15 | convolution fusion | flops 377880576 | bytes 5210116 | tf_op jit(solution)/shard_map/gat,tn->gan/dot_general | solution.py:80
  156.2 3.0 %fusion.7 = bf16[4,96,768]{2,1,0:T(8,128)(2,1)} fusion(f32[4,96,768]{2,1,0:T(8,128)} %convolution_add_fusion.3, bf16[128,1536]{1,0:T(8,128)(2,1)} %collective-permute-done.6, bf16[1536,768]{1,0:T(8,128)(2,1)S(1)} %copy-done, bf16[4,8,96,128]{3,2,1,0:T(8,128)(2,1)} %get-tuple-element.12, s32[]{:T(128)S(6)} %select_n.148), kind=kOutput, calls=%fused_computation.21 | convolution fusion | flops 378175488 | bytes 4620292 | tf_op jit(solution)/shard_map/gat,tn->gan/dot_general | solution.py:80
  159.2 5.8 %all-to-all-start.2 = ((bf16[4,96,768]{2,1,0:T(8,128)(2,1)}), bf16[4,96,768]{2,1,0:T(8,128)(2,1)S(1)}, u32[]{:S(2)}, u32[]{:S(2)}) async-start(bf16[4,96,768]{2,1,0:T(8,128)(2,1)} %fusion.7), calls=%async_computation.2 | async-start | bytes 1179648 | tf_op jit(solution)/shard_map/all_to_all | solution.py:82
  166.2 1.2 fusion.46
  168.6 1.2 fusion.50
  169.8 1.2 convolution_add_fusion.1
  171.0 1.2 fusion.52
  172.2 1.9 %fusion.5 = f32[48,1536]{1,0:T(8,128)} fusion(f32[48,1536]{1,0:T(8,128)S(1)} %fusion.44, f32[48,1536]{1,0:T(8,128)S(1)} %fusion.46, f32[48,1536]{1,0:T(8,128)S(1)} %fusion.48, f32[48,1536]{1,0:T(8,128)S(1)} %fusion.50, f32[48,1536]{1,0:T(8,128)S(1)} %fusion.52, f32[48,1536]{1,0:T(8,128)S(1)} %convolution_add_fusion.1, ...), kind=kOutput, calls=%fused_computation.10 | convolution fusion | flops 19390464 | bytes 2469892 | tf_op jit(solution)/shard_map/ta,tf->af/dot_general | solution.py:99
  (46 shorter events, 9.8 us)
Async XLA Ops:
  0.6 86.1 %copy-start = (bf16[1536,768]{1,0:T(8,128)(2,1)S(1)}, bf16[1536,768]{1,0:T(8,128)(2,1)}, u32[]{:S(2)}) copy-start(bf16[1536,768]{1,0:T(8,128)(2,1)} %param.9) | copy-start | bytes 7077892
  3.0 18.6 %copy-start.1 = (bf16[128,1536]{1,0:T(8,128)(2,1)S(1)}, bf16[128,1536]{1,0:T(8,128)(2,1)}, u32[]{:S(2)}) copy-start(bf16[128,1536]{1,0:T(8,128)(2,1)} %param.6) | copy-start | bytes 1179652
  5.8 37.4 %all-to-all-start = ((bf16[16,120,128]{2,1,0:T(8,128)(2,1)}), bf16[16,120,128]{2,1,0:T(8,128)(2,1)S(1)}, u32[]{:S(2)}, u32[]{:S(2)}) async-start(bf16[16,120,128]{2,1,0:T(8,128)(2,1)} %pad_maximum_fusion.1), calls=%async_computation | async-start | bytes 983040 | tf_op jit(solution)/shard_map/all_to_all | solution.py:41
  44.9 39.5 %all-to-all-start.1 = ((bf16[32,224,128]{2,1,0:T(8,128)(2,1)}), bf16[32,224,128]{2,1,0:T(8,128)(2,1)}, u32[]{:S(2)}, u32[]{:S(2)}) async-start(bf16[32,224,128]{2,1,0:T(8,128)(2,1)} %bitcast.136), calls=%async_computation.1 | async-start | bytes 3670016 | tf_op jit(solution)/shard_map/all_to_all | solution.py:69
  59.5 96.7 %collective-permute-start.6 = (bf16[128,1536]{1,0:T(8,128)(2,1)S(1)}, bf16[128,1536]{1,0:T(8,128)(2,1)}, u32[]{:S(2)}, u32[]{:S(2)}) collective-permute-start(bf16[128,1536]{1,0:T(8,128)(2,1)S(1)} %copy-done.1), channel_id=1, source_target_pairs={{0,7},{1,0},{2,1},{3,2},{4,3},{5,4},{6,5},{7,6},{8,15},{9,8},{10,9... | collective-permute-start | bytes 1179656 | tf_op jit(solution)/shard_map/ppermute | solution.py:43
  64.9 88.0 %collective-permute-start.5 = (bf16[128,1536]{1,0:T(8,128)(2,1)S(1)}, bf16[128,1536]{1,0:T(8,128)(2,1)}, u32[]{:S(2)}, u32[]{:S(2)}) collective-permute-start(bf16[128,1536]{1,0:T(8,128)(2,1)S(1)} %copy-done.1), channel_id=1, source_target_pairs={{0,6},{1,7},{2,0},{3,1},{4,2},{5,3},{6,4},{7,5},{8,14},{9,15},{10,... | collective-permute-start | bytes 1179656 | tf_op jit(solution)/shard_map/ppermute | solution.py:43
  67.4 81.1 %collective-permute-start.4 = (bf16[128,1536]{1,0:T(8,128)(2,1)S(1)}, bf16[128,1536]{1,0:T(8,128)(2,1)}, u32[]{:S(2)}, u32[]{:S(2)}) collective-permute-start(bf16[128,1536]{1,0:T(8,128)(2,1)S(1)} %copy-done.1), channel_id=1, source_target_pairs={{0,5},{1,6},{2,7},{3,0},{4,1},{5,2},{6,3},{7,4},{8,13},{9,14},{10,... | collective-permute-start | bytes 1179656 | tf_op jit(solution)/shard_map/ppermute | solution.py:43
  69.9 62.2 %collective-permute-start.1 = (bf16[128,1536]{1,0:T(8,128)(2,1)S(1)}, bf16[128,1536]{1,0:T(8,128)(2,1)}, u32[]{:S(2)}, u32[]{:S(2)}) collective-permute-start(bf16[128,1536]{1,0:T(8,128)(2,1)S(1)} %copy-done.1), channel_id=1, source_target_pairs={{0,2},{1,3},{2,4},{3,5},{4,6},{5,7},{6,0},{7,1},{8,10},{9,11},{10,... | collective-permute-start | bytes 1179656 | tf_op jit(solution)/shard_map/ppermute | solution.py:43
  73.7 35.1 %collective-permute-start = (bf16[128,1536]{1,0:T(8,128)(2,1)S(1)}, bf16[128,1536]{1,0:T(8,128)(2,1)}, u32[]{:S(2)}, u32[]{:S(2)}) collective-permute-start(bf16[128,1536]{1,0:T(8,128)(2,1)S(1)} %copy-done.1), channel_id=1, source_target_pairs={{0,1},{1,2},{2,3},{3,4},{4,5},{5,6},{6,7},{7,0},{8,9},{9,10},{10,1... | collective-permute-start | bytes 1179656 | tf_op jit(solution)/shard_map/ppermute | solution.py:43
  108.7 30.3 %collective-permute-start.2 = (bf16[128,1536]{1,0:T(8,128)(2,1)S(1)}, bf16[128,1536]{1,0:T(8,128)(2,1)}, u32[]{:S(2)}, u32[]{:S(2)}) collective-permute-start(bf16[128,1536]{1,0:T(8,128)(2,1)S(1)} %copy-done.1), channel_id=1, source_target_pairs={{0,3},{1,4},{2,5},{3,6},{4,7},{5,0},{6,1},{7,2},{8,11},{9,12},{10,... | collective-permute-start | bytes 1179656 | tf_op jit(solution)/shard_map/ppermute | solution.py:43
  132.1 13.1 %collective-permute-start.3 = (bf16[128,1536]{1,0:T(8,128)(2,1)S(1)}, bf16[128,1536]{1,0:T(8,128)(2,1)}, u32[]{:S(2)}, u32[]{:S(2)}) collective-permute-start(bf16[128,1536]{1,0:T(8,128)(2,1)S(1)} %copy-done.1), channel_id=1, source_target_pairs={{0,4},{1,5},{2,6},{3,7},{4,0},{5,1},{6,2},{7,3},{8,12},{9,13},{10,... | collective-permute-start | bytes 1179656 | tf_op jit(solution)/shard_map/ppermute | solution.py:43
  143.1 1.9 %copy-start.3 = (bf16[8,32,128]{2,1,0:T(8,128)(2,1)}, bf16[8,32,128]{2,1,0:T(8,128)(2,1)S(1)}, u32[]{:S(2)}) copy-start(bf16[8,32,128]{2,1,0:T(8,128)(2,1)S(1)} %dynamic-slice_bitcast_fusion) | copy-start | bytes 196612
  148.5 3.3 %copy-start.4 = (bf16[8,32,128]{2,1,0:T(8,128)(2,1)S(1)}, bf16[8,32,128]{2,1,0:T(8,128)(2,1)}, u32[]{:S(2)}) copy-start(bf16[8,32,128]{2,1,0:T(8,128)(2,1)} %copy-done.3) | copy-start | bytes 196612
  159.2 10.6 %copy-start.2 = (f32[48,1536]{1,0:T(8,128)S(1)}, f32[48,1536]{1,0:T(8,128)}, u32[]{:S(2)}) copy-start(f32[48,1536]{1,0:T(8,128)} %fusion.56) | copy-start | bytes 884740
  159.2 16.0 %all-to-all-start.2 = ((bf16[4,96,768]{2,1,0:T(8,128)(2,1)}), bf16[4,96,768]{2,1,0:T(8,128)(2,1)S(1)}, u32[]{:S(2)}, u32[]{:S(2)}) async-start(bf16[4,96,768]{2,1,0:T(8,128)(2,1)} %fusion.7), calls=%async_computation.2 | async-start | bytes 1179648 | tf_op jit(solution)/shard_map/all_to_all | solution.py:82

commit v4 on v3

--- a/solution.py
+++ b/solution.py
@@ -1,11 +1,53 @@
 import jax
 import jax.numpy as jnp
 from jax import lax
+from jax.experimental import pallas as pl
+from jax.experimental.pallas import tpu as pltpu
 from jax.sharding import PartitionSpec as P
 
 BF = jnp.bfloat16
 F32 = jnp.float32
 LANES = 128
+
+
+def final_kernel(col_ref, u_ref, *refs):
+    v_refs, out_ref = refs[:-1], refs[-1]
+    n_col = len(v_refs)
+    groups, unused, rows, tok = u_ref.shape
+    col = col_ref[0]
+    total = None
+    for k in range(0, n_col, 2):
+        sides = []
+        for j in (k, k + 1):
+            source = lax.rem(col - j + n_col, n_col)
+            sides.append(u_ref[:, source].reshape(groups * rows, tok))
+        u_pair = jnp.concatenate(sides, axis=1)
+        v_pair = jnp.concatenate([v_refs[k][...], v_refs[k + 1][...]], axis=0)
+        term = jnp.dot(u_pair, v_pair, preferred_element_type=F32)
+        total = term if total is None else total + term
+    out_ref[...] = total.reshape(out_ref.shape).astype(out_ref.dtype)
+
+
+def final_product(col, got, v_blocks, out_rows):
+    n_grp, n_col, unused, tok = got.shape
+    width = v_blocks[0].shape[1]
+    return pl.pallas_call(
+        final_kernel,
+        out_shape=jax.ShapeDtypeStruct((n_grp, out_rows, width), BF),
+        grid=(1,),
+        in_specs=[
+            pl.BlockSpec(memory_space=pltpu.SMEM),
+            pl.BlockSpec((n_grp, n_col, out_rows, tok), lambda i: (0, 0, 0, 0)),
+        ]
+        + [pl.BlockSpec((tok, width), lambda i: (0, 0))] * n_col,
+        out_specs=pl.BlockSpec((n_grp, out_rows, width), lambda i: (0, 0, 0)),
+        compiler_params=pltpu.CompilerParams(vmem_limit_bytes=32 * 1024 * 1024),
+        cost_estimate=pl.CostEstimate(
+            flops=2 * n_grp * out_rows * n_col * tok * width,
+            bytes_accessed=4 * 1024 * 1024,
+            transcendentals=0,
+        ),
+    )(jnp.reshape(col, (1,)).astype(jnp.int32), got, *v_blocks)
 
 
 def body(tokens_in, cotangent, sample_rows, act_inverse, grad_inverse):
@@ -39,10 +81,13 @@
         (jnp.concatenate([part, x_send], axis=1), cotangent)
     )
     first = lax.all_to_all(payload, "row", 0, 0)
-    blocks = [cotangent] + [
-        lax.ppermute(own_cot, "col", [(i, (i + k) % n_col) for i in range(n_col)])
-        for k in range(1, n_col)
-    ]
+    def shifted(block, k):
+        return lax.ppermute(block, "col", [(i, (i + k) % n_col) for i in range(n_col)])
+
+    early = {k: shifted(own_cot, k) for k in (1, 3, 4, 5)}
+    first, own_cot, early = lax.optimization_barrier((first, own_cot, early))
+    late = {k: shifted(own_cot, k) for k in (2, 6, 7)}
+    blocks = [own_cot] + [early[k] if k in early else late[k] for k in range(1, n_col)]
     left = jnp.sum(first[:, :out_rows].astype(F32), axis=0).astype(BF)
     x_all = first[:, out_rows:].reshape(n_grp, -1, LANES)
     x_rows = x_all.shape[1]
@@ -68,17 +113,13 @@
     send = send.reshape((n_grp * n_col,) + send.shape[2:])
     got = lax.all_to_all(send, ("grp", "col"), 0, 0)
     got = got.reshape(both + got.shape[1:])
-    lefts = got[:, :, :out_rows]
     samples_x = got[:, :, out_rows : out_rows + x_rows]
     sides = got[:, :, out_rows + x_rows :]
 
-    term = jnp.zeros((n_grp, out_rows, grad_inverse.shape[1]), F32)
-    for k, block in enumerate(blocks):
-        source = (col - k) % n_col
-        v_blk = jnp.dot(block, grad_inverse, preferred_element_type=F32).astype(BF)
-        u_blk = lax.dynamic_index_in_dim(lefts, source, 1, keepdims=False)
-        term = term + jnp.einsum("gat,tn->gan", u_blk, v_blk, preferred_element_type=F32)
-    term = term.astype(BF)
+    v_blocks = [
+        jnp.dot(block, grad_inverse, preferred_element_type=F32).astype(BF) for block in blocks
+    ]
+    term = final_product(col, got, v_blocks, out_rows)
     term = lax.all_to_all(term, "grp", 0, 0)
     precond = jnp.sum(term.astype(F32), axis=0)
 

time: 177 us -> 146 us (0.82)
  waiting for transfers between devices: 48.5 us -> 37 us
  matrix products: 39.2 us -> 28.9 us
  starting transfers between devices: 75.1 us -> 65 us
  Pallas kernels: 0 us -> 2.74 us
  local copies, waits for them, and re-layouts: 7.81 us -> 5.11 us
    all_to_all x1, waiting for transfers between devices: 20.4 us -> 0.01 us  [body(): first = lax.all_to_all(payload, 'row', 0, 0)]
    ppermute x7, waiting for transfers between devices: 19.3 us -> 32.7 us  [shifted(): lax.ppermute(block, 'col', [(i, (i + k) % n_col) for i in range(n_col)])]
    dot_general x8, matrix products: 25.2 us -> 12.2 us  [body(): jnp.dot(block, grad_inverse, preferred_element_type=F32).astype(BF)]
    ppermute x7, starting transfers between devices: 39 us -> 31.2 us  [shifted(): lax.ppermute(block, 'col', [(i, (i + k) % n_col) for i in range(n_col)])]
    all_to_all x1, waiting for transfers between devices: 7.78 us -> 0.01 us  [body(): got = lax.all_to_all(send, ('grp', 'col'), 0, 0)]
    all_to_all x1, starting transfers between devices: 14.6 us -> 7.36 us  [body(): got = lax.all_to_all(send, ('grp', 'col'), 0, 0)]
    all_to_all x1, starting transfers between devices: 5.82 us -> 10.7 us  [body(): term = lax.all_to_all(term, 'grp', 0, 0)]
    all_to_all x1, waiting for transfers between devices: 1.05 us -> 4.37 us  [body(): term = lax.all_to_all(term, 'grp', 0, 0)]
  transfers between devices with their start and end apart: 10 -> 10, of which waited for: 4 -> 5; matrix products, arithmetic and copies ran while one was open for 23% -> 15% of each run, Pallas kernels for 0% -> 0%
where the time goes in v4:
time: 146 us; the launch traced here: 144 us
  starting transfers between devices  65 us (45%)
  waiting for transfers between devices  37 us (25%)
  matrix products  28.9 us (20%)
  local copies, waits for them, and re-layouts  5.11 us (4%)
  other arithmetic  4.28 us (3%)
  Pallas kernels  2.74 us (2%)
    ppermute x7, waiting for transfers between devices, shifted(): lax.ppermute(block, 'col', [(i, (i + k) % n_col) for i in range(n_col)])  32.7 us
    ppermute x7, starting transfers between devices, shifted(): lax.ppermute(block, 'col', [(i, (i + k) % n_col) for i in range(n_col)])  31.2 us
    all_to_all x1, starting transfers between devices, body(): first = lax.all_to_all(payload, 'row', 0, 0)  15.7 us
    dot_general x8, matrix products, body(): jnp.einsum('ta,tf->af', mask, block, preferred_element_type=F32)  12.4 us
    dot_general x8, matrix products, body(): jnp.dot(block, grad_inverse, preferred_element_type=F32).astype(BF)  12.2 us
    all_to_all x1, starting transfers between devices, body(): term = lax.all_to_all(term, 'grp', 0, 0)  10.7 us
    all_to_all x1, starting transfers between devices, body(): got = lax.all_to_all(send, ('grp', 'col'), 0, 0)  7.36 us
    all_to_all x1, waiting for transfers between devices, body(): term = lax.all_to_all(term, 'grp', 0, 0)  4.37 us
  transfers between devices with their start and end apart: 10, of which 5 were waited for; matrix products, arithmetic and copies ran while one was open for 15% of the time, Pallas kernels for 0%

profile of v4, /device:TPU:1, one launch (start us, length us, event | category | flops | bytes accessed | tf_op | source)
XLA Modules:
  0.0 144.3 jit_solution(8354425108074269120)
XLA Ops:
  1.6 1.5 %gather_fusion = bf16[8,384]{1,0:T(8,128)(2,1)S(1)} fusion(bf16[128,384]{1,0:T(8,128)(2,1)} %param.5, s32[1024]{0:T(1024)S(1)} %pad_clamp_fusion.1), kind=kCustom, calls=%fused_computation | custom fusion | bytes 12320 | tf_op jit(solution)/shard_map/jit(_take)/gather | solution.py:75
  3.0 1.7 %convolution_convert_fusion = bf16[1536,128]{1,0:T(8,128)(2,1)S(1)} fusion(bf16[1536,384]{1,0:T(8,128)(2,1)} %param.8, bf16[128,384]{1,0:T(8,128)(2,1)} %param.5), kind=kOutput, calls=%fused_computation.2 | convolution fusion | flops 151191552 | bytes 1671168 | tf_op jit(solution)/shard_map/dot_general | solution.py:69
  5.7 15.7 %all-to-all-start = ((bf16[16,120,128]{2,1,0:T(8,128)(2,1)}), bf16[16,120,128]{2,1,0:T(8,128)(2,1)S(1)}, u32[]{:S(2)}, u32[]{:S(2)}) async-start(bf16[16,120,128]{2,1,0:T(8,128)(2,1)} %pad_maximum_fusion.1), calls=%async_computation | async-start | bytes 983040 | tf_op jit(solution)/shard_map/all_to_all | solution.py:83
  21.5 3.2 %collective-permute-start = (bf16[128,1536]{1,0:T(8,128)(2,1)}, bf16[128,1536]{1,0:T(8,128)(2,1)S(1)}, u32[]{:S(2)}, u32[]{:S(2)}) collective-permute-start(bf16[128,1536]{1,0:T(8,128)(2,1)} %param.6), channel_id=1, source_target_pairs={{0,1},{1,2},{2,3},{3,4},{4,5},{5,6},{6,7},{7,0},{8,9},{9,10},{10,1... | collective-permute-start | bytes 1179656 | tf_op jit(solution)/shard_map/ppermute | solution.py:85
  24.7 4.2 %collective-permute-start.1 = (bf16[128,1536]{1,0:T(8,128)(2,1)}, bf16[128,1536]{1,0:T(8,128)(2,1)}, u32[]{:S(2)}, u32[]{:S(2)}) collective-permute-start(bf16[128,1536]{1,0:T(8,128)(2,1)} %param.6), channel_id=1, source_target_pairs={{0,3},{1,4},{2,5},{3,6},{4,7},{5,0},{6,1},{7,2},{8,11},{9,12},{10,... | collective-permute-start | bytes 1179656 | tf_op jit(solution)/shard_map/ppermute | solution.py:85
  28.9 2.3 %collective-permute-start.2 = (bf16[128,1536]{1,0:T(8,128)(2,1)}, bf16[128,1536]{1,0:T(8,128)(2,1)}, u32[]{:S(2)}, u32[]{:S(2)}) collective-permute-start(bf16[128,1536]{1,0:T(8,128)(2,1)} %param.6), channel_id=1, source_target_pairs={{0,4},{1,5},{2,6},{3,7},{4,0},{5,1},{6,2},{7,3},{8,12},{9,13},{10,... | collective-permute-start | bytes 1179656 | tf_op jit(solution)/shard_map/ppermute | solution.py:85
  31.2 2.8 %collective-permute-start.3 = (bf16[128,1536]{1,0:T(8,128)(2,1)}, bf16[128,1536]{1,0:T(8,128)(2,1)}, u32[]{:S(2)}, u32[]{:S(2)}) collective-permute-start(bf16[128,1536]{1,0:T(8,128)(2,1)} %param.6), channel_id=1, source_target_pairs={{0,5},{1,6},{2,7},{3,0},{4,1},{5,2},{6,3},{7,4},{8,13},{9,14},{10,... | collective-permute-start | bytes 1179656 | tf_op jit(solution)/shard_map/ppermute | solution.py:85
  34.3 1.8 %gather_fusion.1 = bf16[32,1536]{1,0:T(8,128)(2,1)S(1)} fusion(bf16[128,1536]{1,0:T(8,128)(2,1)} %param.6, s32[1024]{0:T(1024)S(1)} %pad_clamp_fusion), kind=kCustom, calls=%fused_computation.1 | custom fusion | bytes 196736 | tf_op jit(solution)/shard_map/jit(_take)/gather | solution.py:95
  37.2 3.0 %collective-permute-done.2 = bf16[128,1536]{1,0:T(8,128)(2,1)} collective-permute-done((bf16[128,1536]{1,0:T(8,128)(2,1)}, bf16[128,1536]{1,0:T(8,128)(2,1)}, u32[]{:S(2)}, u32[]{:S(2)}) %collective-permute-start.2) | collective-permute-done | bytes 393248 | tf_op jit(solution)/shard_map/ppermute | solution.py:85
  40.2 6.7 %collective-permute-done.3 = bf16[128,1536]{1,0:T(8,128)(2,1)} collective-permute-done((bf16[128,1536]{1,0:T(8,128)(2,1)}, bf16[128,1536]{1,0:T(8,128)(2,1)}, u32[]{:S(2)}, u32[]{:S(2)}) %collective-permute-start.3) | collective-permute-done | bytes 393248 | tf_op jit(solution)/shard_map/ppermute | solution.py:85
  47.0 10.8 %collective-permute-start.4 = (bf16[128,1536]{1,0:T(8,128)(2,1)}, bf16[128,1536]{1,0:T(8,128)(2,1)}, u32[]{:S(2)}, u32[]{:S(2)}) collective-permute-start(bf16[128,1536]{1,0:T(8,128)(2,1)} %param.6), channel_id=1, source_target_pairs={{0,2},{1,3},{2,4},{3,5},{4,6},{5,7},{6,0},{7,1},{8,10},{9,11},{10,... | collective-permute-start | bytes 1179656 | tf_op jit(solution)/shard_map/ppermute | solution.py:85
  57.8 2.9 %collective-permute-start.5 = (bf16[128,1536]{1,0:T(8,128)(2,1)}, bf16[128,1536]{1,0:T(8,128)(2,1)}, u32[]{:S(2)}, u32[]{:S(2)}) collective-permute-start(bf16[128,1536]{1,0:T(8,128)(2,1)} %param.6), channel_id=1, source_target_pairs={{0,6},{1,7},{2,0},{3,1},{4,2},{5,3},{6,4},{7,5},{8,14},{9,15},{10,... | collective-permute-start | bytes 1179656 | tf_op jit(solution)/shard_map/ppermute | solution.py:85
  60.7 5.0 %collective-permute-start.6 = (bf16[128,1536]{1,0:T(8,128)(2,1)}, bf16[128,1536]{1,0:T(8,128)(2,1)}, u32[]{:S(2)}, u32[]{:S(2)}) collective-permute-start(bf16[128,1536]{1,0:T(8,128)(2,1)} %param.6), channel_id=1, source_target_pairs={{0,7},{1,0},{2,1},{3,2},{4,3},{5,4},{6,5},{7,6},{8,15},{9,8},{10,9... | collective-permute-start | bytes 1179656 | tf_op jit(solution)/shard_map/ppermute | solution.py:85
  65.9 1.4 pad_maximum_fusion
  67.3 7.4 %all-to-all-start.1 = ((bf16[32,224,128]{2,1,0:T(8,128)(2,1)}), bf16[32,224,128]{2,1,0:T(8,128)(2,1)}, u32[]{:S(2)}, u32[]{:S(2)}) async-start(bf16[32,224,128]{2,1,0:T(8,128)(2,1)} %bitcast.83), calls=%async_computation.1 | async-start | bytes 3670016 | tf_op jit(solution)/shard_map/all_to_all | solution.py:114
  74.7 1.5 %convolution_convert_fusion.8.refs_0_ = bf16[128,768]{1,0:T(8,128)(2,1)S(1)} fusion(bf16[128,1536]{1,0:T(8,128)(2,1)} %param.6, bf16[1536,768]{1,0:T(8,128)(2,1)S(1)} %copy-done), kind=kOutput, calls=%fused_computation.22 | convolution fusion | flops 302088192 | bytes 2949120 | tf_op jit(solution)/shard_map/dot_general | solution.py:120
  76.2 1.5 %convolution_convert_fusion.3.refs_5_ = bf16[128,768]{1,0:T(8,128)(2,1)S(1)} fusion(bf16[128,1536]{1,0:T(8,128)(2,1)} %collective-permute-done.3, bf16[1536,768]{1,0:T(8,128)(2,1)S(1)} %copy-done), kind=kOutput, calls=%fused_computation.17 | convolution fusion | flops 302088192 | bytes 2949120 | tf_op jit(solution)/shard_map/dot_general | solution.py:120
  77.7 1.5 %convolution_convert_fusion.4.refs_4_ = bf16[128,768]{1,0:T(8,128)(2,1)S(1)} fusion(bf16[128,1536]{1,0:T(8,128)(2,1)} %collective-permute-done.2, bf16[1536,768]{1,0:T(8,128)(2,1)S(1)} %copy-done), kind=kOutput, calls=%fused_computation.18 | convolution fusion | flops 302088192 | bytes 2949120 | tf_op jit(solution)/shard_map/dot_general | solution.py:120
  79.2 1.5 %convolution_convert_fusion.5.refs_3_ = bf16[128,768]{1,0:T(8,128)(2,1)S(1)} fusion(bf16[128,1536]{1,0:T(8,128)(2,1)} %collective-permute-done.1, bf16[1536,768]{1,0:T(8,128)(2,1)S(1)} %copy-done), kind=kOutput, calls=%fused_computation.19 | convolution fusion | flops 302088192 | bytes 2949120 | tf_op jit(solution)/shard_map/dot_general | solution.py:120
  81.2 22.4 %collective-permute-done.6 = bf16[128,1536]{1,0:T(8,128)(2,1)} collective-permute-done((bf16[128,1536]{1,0:T(8,128)(2,1)}, bf16[128,1536]{1,0:T(8,128)(2,1)}, u32[]{:S(2)}, u32[]{:S(2)}) %collective-permute-start.6) | collective-permute-done | bytes 393248 | tf_op jit(solution)/shard_map/ppermute | solution.py:85
  103.6 1.5 %convolution_convert_fusion.1.refs_7_ = bf16[128,768]{1,0:T(8,128)(2,1)S(1)} fusion(bf16[128,1536]{1,0:T(8,128)(2,1)} %collective-permute-done.6, bf16[1536,768]{1,0:T(8,128)(2,1)S(1)} %copy-done), kind=kOutput, calls=%fused_computation.15 | convolution fusion | flops 302088192 | bytes 2949120 | tf_op jit(solution)/shard_map/dot_general | solution.py:120
  105.1 2.2 %convolution_convert_fusion.2.refs_6_ = bf16[128,768]{1,0:T(8,128)(2,1)} fusion(bf16[128,1536]{1,0:T(8,128)(2,1)} %collective-permute-done.5, bf16[1536,768]{1,0:T(8,128)(2,1)S(1)} %copy-done), kind=kOutput, calls=%fused_computation.16 | convolution fusion | flops 302088192 | bytes 2949120 | tf_op jit(solution)/shard_map/dot_general | solution.py:120
  107.3 2.2 %convolution_convert_fusion.6.refs_2_ = bf16[128,768]{1,0:T(8,128)(2,1)} fusion(bf16[128,1536]{1,0:T(8,128)(2,1)} %collective-permute-done.4, bf16[1536,768]{1,0:T(8,128)(2,1)S(1)} %copy-done), kind=kOutput, calls=%fused_computation.20 | convolution fusion | flops 302088192 | bytes 2949120 | tf_op jit(solution)/shard_map/dot_general | solution.py:120
  110.5 2.2 %fusion.7 = f32[48,1536]{1,0:T(8,128)} fusion(bf16[4,8,224,128]{3,2,1,0:T(8,128)(2,1)} %bitcast.9.u_ref), kind=kOutput, calls=%fused_computation.12 | convolution fusion | flops 37822464 | bytes 1146880 | tf_op jit(solution)/shard_map/gcsa,gcwsf->awf/dot_general | solution.py:129
  114.2 1.9 %fusion.27 = f32[48,1536]{1,0:T(8,128)} fusion(bf16[128,1536]{1,0:T(8,128)(2,1)} %collective-permute-done.1, bf16[8,128,48]{1,2,0:T(8,128)(2,1)S(1)} %convolution_convert_fusion.9, s32[]{:T(128)S(6)} %select_n.117), kind=kOutput, calls=%fused_computation.52 | convolution fusion | flops 18874368 | bytes 700420 | tf_op jit(solution)/shard_map/ta,tf->af/dot_general | solution.py:140
  116.1 1.9 %fusion.25 = f32[48,1536]{1,0:T(8,128)} fusion(bf16[128,1536]{1,0:T(8,128)(2,1)} %collective-permute-done.2, bf16[8,128,48]{1,2,0:T(8,128)(2,1)S(1)} %convolution_convert_fusion.9, s32[]{:T(128)S(6)} %select_n.119), kind=kOutput, calls=%fused_computation.50 | convolution fusion | flops 18874368 | bytes 700420 | tf_op jit(solution)/shard_map/ta,tf->af/dot_general | solution.py:140
  118.0 1.9 %fusion.23 = f32[48,1536]{1,0:T(8,128)} fusion(bf16[128,1536]{1,0:T(8,128)(2,1)} %collective-permute-done.3, bf16[8,128,48]{1,2,0:T(8,128)(2,1)S(1)} %convolution_convert_fusion.9, s32[]{:T(128)S(6)} %select_n.121), kind=kOutput, calls=%fused_computation.48 | convolution fusion | flops 18874368 | bytes 700420 | tf_op jit(solution)/shard_map/ta,tf->af/dot_general | solution.py:140
  119.9 2.7 %shard_map.76 = bf16[4,96,768]{2,1,0:T(8,128)(2,1)} custom-call(s32[1]{0:T(128)} %bitcast.col_ref, bf16[4,8,224,128]{3,2,1,0:T(8,128)(2,1)} %bitcast.9.u_ref, bf16[128,768]{1,0:T(8,128)(2,1)S(1)} %convolution_convert_fusion.8.refs_0_, bf16[128,768]{1,0:T(8,128)(2,1)S(1)} %convolution_convert_fusion.7.refs_1_, bf16[128,768]{1,0:T(8,128)(2,1)S(1)} %copy-done.2, ...), custom_call_target="tpu_custom_call" | custom-call | flops 603979776 | bytes 4194304 | tf_op jit(solution)/shard_map/pallas_call | solution.py:34
  122.6 10.7 %all-to-all-start.2 = ((bf16[4,96,768]{2,1,0:T(8,128)(2,1)}), bf16[4,96,768]{2,1,0:T(8,128)(2,1)S(1)}, u32[]{:S(2)}, u32[]{:S(2)}) async-start(bf16[4,96,768]{2,1,0:T(8,128)(2,1)} %shard_map.76), calls=%async_computation.2 | async-start | bytes 1179648 | tf_op jit(solution)/shard_map/all_to_all | solution.py:123
  134.6 1.2 fusion.21
  137.0 2.2 %fusion.6 = f32[48,1536]{1,0:T(8,128)} fusion(f32[48,1536]{1,0:T(8,128)S(1)} %fusion.19, f32[48,1536]{1,0:T(8,128)S(1)} %fusion.21, f32[48,1536]{1,0:T(8,128)} %fusion.23, f32[48,1536]{1,0:T(8,128)} %fusion.25, f32[48,1536]{1,0:T(8,128)S(1)} %copy-done.7, f32[48,1536]{1,0:T(8,128)S(1)} %fusion.29, f32[48,1536]{1,0:T(8,128)S(1)} %copy-done.6, ...), kind=kOutput, calls=%fused_computation.10 | convolution fusion | flops 19464192 | bytes 2764804 | tf_op jit(solution)/shard_map/ta,tf->af/dot_general | solution.py:140
  139.2 4.4 %all-to-all-done.2 = bf16[4,96,768]{2,1,0:T(8,128)(2,1)S(1)} async-done(((bf16[4,96,768]{2,1,0:T(8,128)(2,1)}), bf16[4,96,768]{2,1,0:T(8,128)(2,1)S(1)}, u32[]{:S(2)}, u32[]{:S(2)}) %all-to-all-start.2) | async-done | bytes 589856 | tf_op jit(solution)/shard_map/all_to_all | solution.py:123
  (54 shorter events, 9.4 us)
Async XLA Ops:
  0.6 74.0 %copy-start = (bf16[1536,768]{1,0:T(8,128)(2,1)S(1)}, bf16[1536,768]{1,0:T(8,128)(2,1)}, u32[]{:S(2)}) copy-start(bf16[1536,768]{1,0:T(8,128)(2,1)} %param.9) | copy-start | bytes 7077892
  5.7 41.2 %all-to-all-start = ((bf16[16,120,128]{2,1,0:T(8,128)(2,1)}), bf16[16,120,128]{2,1,0:T(8,128)(2,1)S(1)}, u32[]{:S(2)}, u32[]{:S(2)}) async-start(bf16[16,120,128]{2,1,0:T(8,128)(2,1)} %pad_maximum_fusion.1), calls=%async_computation | async-start | bytes 983040 | tf_op jit(solution)/shard_map/all_to_all | solution.py:83
  21.5 15.2 %collective-permute-start = (bf16[128,1536]{1,0:T(8,128)(2,1)}, bf16[128,1536]{1,0:T(8,128)(2,1)S(1)}, u32[]{:S(2)}, u32[]{:S(2)}) collective-permute-start(bf16[128,1536]{1,0:T(8,128)(2,1)} %param.6), channel_id=1, source_target_pairs={{0,1},{1,2},{2,3},{3,4},{4,5},{5,6},{6,7},{7,0},{8,9},{9,10},{10,1... | collective-permute-start | bytes 1179656 | tf_op jit(solution)/shard_map/ppermute | solution.py:85
  24.7 12.5 %collective-permute-start.1 = (bf16[128,1536]{1,0:T(8,128)(2,1)}, bf16[128,1536]{1,0:T(8,128)(2,1)}, u32[]{:S(2)}, u32[]{:S(2)}) collective-permute-start(bf16[128,1536]{1,0:T(8,128)(2,1)} %param.6), channel_id=1, source_target_pairs={{0,3},{1,4},{2,5},{3,6},{4,7},{5,0},{6,1},{7,2},{8,11},{9,12},{10,... | collective-permute-start | bytes 1179656 | tf_op jit(solution)/shard_map/ppermute | solution.py:85
  28.9 11.3 %collective-permute-start.2 = (bf16[128,1536]{1,0:T(8,128)(2,1)}, bf16[128,1536]{1,0:T(8,128)(2,1)}, u32[]{:S(2)}, u32[]{:S(2)}) collective-permute-start(bf16[128,1536]{1,0:T(8,128)(2,1)} %param.6), channel_id=1, source_target_pairs={{0,4},{1,5},{2,6},{3,7},{4,0},{5,1},{6,2},{7,3},{8,12},{9,13},{10,... | collective-permute-start | bytes 1179656 | tf_op jit(solution)/shard_map/ppermute | solution.py:85
  31.2 15.7 %collective-permute-start.3 = (bf16[128,1536]{1,0:T(8,128)(2,1)}, bf16[128,1536]{1,0:T(8,128)(2,1)}, u32[]{:S(2)}, u32[]{:S(2)}) collective-permute-start(bf16[128,1536]{1,0:T(8,128)(2,1)} %param.6), channel_id=1, source_target_pairs={{0,5},{1,6},{2,7},{3,0},{4,1},{5,2},{6,3},{7,4},{8,13},{9,14},{10,... | collective-permute-start | bytes 1179656 | tf_op jit(solution)/shard_map/ppermute | solution.py:85
  36.7 30.6 %copy-start.3 = (bf16[128,1536]{1,0:T(8,128)(2,1)}, bf16[128,1536]{1,0:T(8,128)(2,1)S(1)}, u32[]{:S(2)}) copy-start(bf16[128,1536]{1,0:T(8,128)(2,1)S(1)} %collective-permute-done) | copy-start | bytes 1179652
  47.0 60.3 %collective-permute-start.4 = (bf16[128,1536]{1,0:T(8,128)(2,1)}, bf16[128,1536]{1,0:T(8,128)(2,1)}, u32[]{:S(2)}, u32[]{:S(2)}) collective-permute-start(bf16[128,1536]{1,0:T(8,128)(2,1)} %param.6), channel_id=1, source_target_pairs={{0,2},{1,3},{2,4},{3,5},{4,6},{5,7},{6,0},{7,1},{8,10},{9,11},{10,... | collective-permute-start | bytes 1179656 | tf_op jit(solution)/shard_map/ppermute | solution.py:85
  57.8 47.3 %collective-permute-start.5 = (bf16[128,1536]{1,0:T(8,128)(2,1)}, bf16[128,1536]{1,0:T(8,128)(2,1)}, u32[]{:S(2)}, u32[]{:S(2)}) collective-permute-start(bf16[128,1536]{1,0:T(8,128)(2,1)} %param.6), channel_id=1, source_target_pairs={{0,6},{1,7},{2,0},{3,1},{4,2},{5,3},{6,4},{7,5},{8,14},{9,15},{10,... | collective-permute-start | bytes 1179656 | tf_op jit(solution)/shard_map/ppermute | solution.py:85
  60.7 42.9 %collective-permute-start.6 = (bf16[128,1536]{1,0:T(8,128)(2,1)}, bf16[128,1536]{1,0:T(8,128)(2,1)}, u32[]{:S(2)}, u32[]{:S(2)}) collective-permute-start(bf16[128,1536]{1,0:T(8,128)(2,1)} %param.6), channel_id=1, source_target_pairs={{0,7},{1,0},{2,1},{3,2},{4,3},{5,4},{6,5},{7,6},{8,15},{9,8},{10,9... | collective-permute-start | bytes 1179656 | tf_op jit(solution)/shard_map/ppermute | solution.py:85
  67.3 42.1 %all-to-all-start.1 = ((bf16[32,224,128]{2,1,0:T(8,128)(2,1)}), bf16[32,224,128]{2,1,0:T(8,128)(2,1)}, u32[]{:S(2)}, u32[]{:S(2)}) async-start(bf16[32,224,128]{2,1,0:T(8,128)(2,1)} %bitcast.83), calls=%async_computation.1 | async-start | bytes 3670016 | tf_op jit(solution)/shard_map/all_to_all | solution.py:114
  77.6 3.0 %copy-start.4 = (bf16[128,1536]{1,0:T(8,128)(2,1)S(1)}, bf16[128,1536]{1,0:T(8,128)(2,1)}, u32[]{:S(2)}) copy-start(bf16[128,1536]{1,0:T(8,128)(2,1)} %copy-done.3) | copy-start | bytes 1179652
  109.4 3.8 %copy-start.5 = (bf16[128,1536]{1,0:T(8,128)(2,1)S(1)}, bf16[128,1536]{1,0:T(8,128)(2,1)}, u32[]{:S(2)}) copy-start(bf16[128,1536]{1,0:T(8,128)(2,1)} %copy-done.3) | copy-start | bytes 1179652
  109.4 10.5 %copy-start.1 = (bf16[128,768]{1,0:T(8,128)(2,1)S(1)}, bf16[128,768]{1,0:T(8,128)(2,1)}, u32[]{:S(2)}) copy-start(bf16[128,768]{1,0:T(8,128)(2,1)} %convolution_convert_fusion.2.refs_6_) | copy-start | bytes 589828
  109.4 10.5 %copy-start.2 = (bf16[128,768]{1,0:T(8,128)(2,1)S(1)}, bf16[128,768]{1,0:T(8,128)(2,1)}, u32[]{:S(2)}) copy-start(bf16[128,768]{1,0:T(8,128)(2,1)} %convolution_convert_fusion.6.refs_2_) | copy-start | bytes 589828
  113.2 4.7 %copy-start.8 = (bf16[8,128,48]{1,2,0:T(8,128)(2,1)}, bf16[8,128,48]{1,2,0:T(8,128)(2,1)S(1)}, u32[]{:S(2)}) copy-start(bf16[8,128,48]{1,2,0:T(8,128)(2,1)S(1)} %convolution_convert_fusion.9) | copy-start | bytes 294916
  122.6 14.3 %copy-start.6 = (f32[48,1536]{1,0:T(8,128)S(1)}, f32[48,1536]{1,0:T(8,128)}, u32[]{:S(2)}) copy-start(f32[48,1536]{1,0:T(8,128)} %fusion.31) | copy-start | bytes 884740
  122.6 14.3 %copy-start.7 = (f32[48,1536]{1,0:T(8,128)S(1)}, f32[48,1536]{1,0:T(8,128)}, u32[]{:S(2)}) copy-start(f32[48,1536]{1,0:T(8,128)} %fusion.27) | copy-start | bytes 884740
  122.6 20.9 %all-to-all-start.2 = ((bf16[4,96,768]{2,1,0:T(8,128)(2,1)}), bf16[4,96,768]{2,1,0:T(8,128)(2,1)S(1)}, u32[]{:S(2)}, u32[]{:S(2)}) async-start(bf16[4,96,768]{2,1,0:T(8,128)(2,1)} %shard_map.76), calls=%async_computation.2 | async-start | bytes 1179648 | tf_op jit(solution)/shard_map/all_to_all | solution.py:123

commit v5 on v2

v5 whole, which is shorter than its diff:
```python
import functools

import jax
import jax.numpy as jnp
from jax import lax
from jax.experimental import pallas as pl
from jax.experimental.pallas import tpu as pltpu
from jax.sharding import PartitionSpec as P

BF = jnp.bfloat16
F32 = jnp.float32
LANES = 128
FIRST = (((0,), (0,)), ((), ()))
LAST = (((1,), (1,)), ((), ()))
SMEM = pl.BlockSpec(memory_space=pltpu.SMEM)
VMEM = pl.BlockSpec(memory_space=pltpu.VMEM)


def call(kernel, inputs, outs, flops, scratch=()):
    moved = sum(x.size * x.dtype.itemsize for x in list(inputs) + list(outs))
    return pl.pallas_call(
        kernel,
        out_shape=outs,
        in_specs=[SMEM if x.dtype == jnp.int32 else VMEM for x in inputs],
        out_specs=[VMEM] * len(outs),
        scratch_shapes=list(scratch),
        compiler_params=pltpu.CompilerParams(vmem_limit_bytes=40 * 1024 * 1024),
        cost_estimate=pl.CostEstimate(flops=flops, bytes_accessed=moved, transcendentals=0),
    )(*inputs)


def rows_hot(targets, tok):
    shape = (len(targets), tok)
    sub = lax.broadcasted_iota(jnp.int32, shape, 0)
    lane = lax.broadcasted_iota(jnp.int32, shape, 1)
    want = jnp.zeros(shape, jnp.int32)
    for i, target in enumerate(targets):
        want = jnp.where(sub == i, target, want)
    return jnp.where(want == lane, 1.0, 0.0).astype(BF)


def first_kernel(at, picks, x_ref, a_ref, out_ref):
    n_row, unused, tok = out_ref.shape
    part = lax.dot_general(a_ref[...], x_ref[...], LAST, preferred_element_type=F32)
    out_rows = part.shape[0] // n_row
    out_ref[:, :out_rows, :] = part.astype(BF).reshape(n_row, out_rows, tok)
    quarter = picks.shape[0]
    hot = rows_hot([picks[i] for i in range(quarter)], tok)
    chosen = jnp.dot(hot, x_ref[...], preferred_element_type=F32)
    strips = [chosen[:, k : k + LANES] for k in range(0, chosen.shape[1], LANES)]
    block = jnp.concatenate(strips, axis=0).astype(BF)
    out_ref[:, out_rows:, :] = jnp.broadcast_to(block[None], (n_row,) + block.shape)


def pick_kernel(at, picks, g_ref, out_ref):
    tok = g_ref.shape[0]
    samp = picks.shape[0]
    ours = [32 * (i // 8) + 8 * at[1] + i % 8 for i in range(out_ref.shape[0] - samp)]
    hot = rows_hot(ours + [picks[i] for i in range(samp)], tok)
    out_ref[...] = jnp.dot(hot, g_ref[...], preferred_element_type=F32).astype(BF)


def side_kernel(at, picks, x_ref, gy_ref, out_ref):
    n_col, samp, unused = out_ref.shape
    tok, feat = x_ref.shape
    tile = feat // n_col
    quarter = picks.shape[0]
    hot = rows_hot([picks[i] for i in range(quarter)], tok)
    chosen = jnp.dot(hot, x_ref[...], preferred_element_type=F32)
    begin = pl.multiple_of(at[2] * feat, LANES)
    own = gy_ref[gy_ref.shape[0] - samp :, pl.ds(begin, feat)].astype(F32)
    chosen = jnp.concatenate([chosen, jnp.zeros((samp - quarter, feat), F32)], axis=0)
    empty = jnp.zeros((samp, LANES - 2 * tile), F32)
    for c in range(n_col):
        span = slice(c * tile, (c + 1) * tile)
        out_ref[c] = jnp.concatenate([own[:, span], chosen[:, span], empty], axis=1).astype(BF)


def right_kernel(at, b_ref, *refs):
    n_grp = 4
    blocks, outs, held = refs[: -n_grp - 1], refs[-n_grp - 1 : -1], refs[-1]
    each = blocks[0].shape[0] // 2
    rows = jnp.concatenate([block[:each, :] for block in blocks], axis=0)
    term = jnp.dot(rows, b_ref[...], preferred_element_type=F32)
    size = each // n_grp
    held[...] = term.reshape(held.shape)
    for x in range(n_grp):
        piece = held[:, at[0] ^ x]
        outs[x][...] = piece.reshape(len(blocks) * size, -1).astype(BF)


def second_kernel(got_ref, side_ref, out_ref):
    n_grp, n_col, unused, unused = out_ref.shape
    n_row, depth, tok = got_ref.shape
    strip = depth - (depth // 32) * 32
    out_rows = depth - strip
    total = got_ref[0, :out_rows, :].astype(F32)
    for r in range(1, n_row):
        total = total + got_ref[r, :out_rows, :].astype(F32)
    total = jnp.concatenate([total, jnp.zeros((LANES - out_rows, tok), F32)], axis=0)
    turned = jnp.transpose(total).astype(BF)
    size = tok // n_grp
    per = n_row // n_grp
    x_rows = per * strip
    for g in range(n_grp):
        u_block = turned[g * size : (g + 1) * size]
        x_block = got_ref[g * per : (g + 1) * per, out_rows:, :].astype(F32)
        x_block = x_block.reshape(x_rows, tok).astype(BF)
        for c in range(n_col):
            out_ref[g, c, :size, :] = u_block
            out_ref[g, c, size : size + x_rows, :] = x_block
            out_ref[g, c, size + x_rows :, :] = side_ref[c]


def final_kernel(at, got_ref, *refs):
    v_refs, out_ref, held = refs[:-2], refs[-2], refs[-1]
    n_col, spread, size, width = held.shape
    n_grp, out_rows, unused = out_ref.shape
    for j in range(spread):
        plane = lax.rem(at[1] - j + spread, spread)
        block = v_refs[j][...].astype(F32)
        for k in range(n_col):
            source = lax.rem(at[3] - k + n_col, n_col)
            held[source, plane] = block[k * size : (k + 1) * size]
    tokens = n_col * spread * size
    right = held[...].reshape(tokens, width).astype(BF)
    for g in range(n_grp):
        left = got_ref[g, :, : spread * size, :].reshape(tokens, LANES)
        term = lax.dot_general(left, right, FIRST, preferred_element_type=F32)
        out_ref[g] = term[:out_rows].astype(BF)


def factor_kernel(at, got_ref, *refs):
    blocks, act_ref, grad_ref = refs[:-2], refs[-2], refs[-1]
    n_grp, n_col, depth, unused = got_ref.shape
    tile, width = act_ref.shape
    samp = blocks[0].shape[0] // 2
    quarter = samp // n_grp
    total = samp * n_col
    scale = 1.0 / total
    side = depth - samp
    begin = side - quarter * (width // LANES)
    left = got_ref[:, :, side : side + 16, :].astype(F32)[:, :, :quarter, :]
    left = left.reshape(total, LANES).astype(BF)
    span = got_ref[:, :, begin:side, :].astype(F32)
    for t in range(width // LANES):
        strip = span[:, :, t * quarter : (t + 1) * quarter, :].reshape(total, LANES).astype(BF)
        term = lax.dot_general(left, strip, FIRST, preferred_element_type=F32)
        act_ref[:, t * LANES : (t + 1) * LANES] = term[tile : 2 * tile] * scale
    lefts, rights = [], []
    for k, block in enumerate(blocks):
        source = lax.rem(at[3] - k + n_col, n_col)
        lefts.append(got_ref[at[4], source, side:, :])
        rights.append(block[samp:, :])
    left = jnp.concatenate(lefts, axis=0)
    right = jnp.concatenate(rights, axis=0)
    grad_ref[...] = lax.dot_general(left, right, FIRST, preferred_element_type=F32)[:tile] * scale


def body(tokens_in, cotangent, sample_rows, act_inverse, grad_inverse):
    n_row = lax.axis_size("row")
    n_col = lax.axis_size("col")
    n_grp = lax.axis_size("grp")
    grp = lax.axis_index("grp")
    row = lax.axis_index("row")
    col = lax.axis_index("col")
    tok, feat_row = tokens_in.shape
    feat_grp = cotangent.shape[1]
    width = grad_inverse.shape[1]
    samp = sample_rows.shape[0]
    quarter = samp // n_grp
    tile = feat_row // n_col
    out_rows = feat_grp // n_row
    per = feat_grp // feat_row
    strip = quarter * feat_row // LANES
    spread = 4
    size = tok // n_grp // spread
    shape = jax.ShapeDtypeStruct

    at = jnp.stack([grp, row % spread, row % per, col, row // per]).astype(jnp.int32)
    offsets = sample_rows - col * tok
    own = lax.dynamic_slice_in_dim(offsets, grp * quarter, quarter, 0)

    payload = call(
        first_kernel,
        (at, own, tokens_in, act_inverse),
        [shape((n_row, out_rows + strip, tok), BF)],
        2 * feat_grp * feat_row * tok,
    )[0]
    payload, cot = lax.optimization_barrier((payload, cotangent))
    first = lax.all_to_all(payload, "row", 0, 0)

    picked = call(
        pick_kernel,
        (at, offsets, cot),
        [shape((n_grp * size + samp, feat_grp), BF)],
        2 * 64 * tok * feat_grp,
    )[0]
    blocks = [picked] + [
        lax.ppermute(picked, "col", [(i, (i + k) % n_col) for i in range(n_col)])
        for k in range(1, n_col)
    ]
    side = call(
        side_kernel,
        (at, own, tokens_in, picked),
        [shape((n_col, samp, LANES), BF)],
        2 * samp * tok * feat_row,
    )[0]
    first, blocks = lax.optimization_barrier((first, blocks))

    send = call(
        second_kernel,
        (first, side),
        [shape((n_grp, n_col, size * spread + strip * n_row // n_grp + samp, LANES), BF)],
        1000000,
    )[0]
    parts = call(
        right_kernel,
        (at, grad_inverse, *blocks),
        [shape((n_col * size, width), BF)] * n_grp,
        2 * n_col * n_grp * size * feat_grp * width,
        [pltpu.VMEM((n_col, n_grp, size, width), F32)],
    )
    send, parts = lax.optimization_barrier((send, parts))
    got = lax.all_to_all(send.reshape((n_grp * n_col,) + send.shape[2:]), ("grp", "col"), 0, 0)
    got = got.reshape(send.shape)
    total = parts[0].astype(F32)
    for x in range(1, n_grp):
        moved = lax.ppermute(parts[x], "grp", [(i, i ^ x) for i in range(n_grp)])
        total = total + moved.astype(F32)
    right = total.astype(BF)
    rights = [right] + [
        lax.ppermute(
            right, "row", [(i, i - i % spread + (i + j) % spread) for i in range(n_row)]
        )
        for j in range(1, spread)
    ]

    term = call(
        final_kernel,
        (at, got, *rights),
        [shape((n_grp, out_rows, width), BF)],
        2 * n_grp * LANES * n_col * spread * size * width,
        [pltpu.VMEM((n_col, spread, size, width), F32)],
    )[0]
    term, got, blocks = lax.optimization_barrier((term, got, blocks))
    term = lax.all_to_all(term, "grp", 0, 0)
    precond = jnp.sum(term.astype(F32), axis=0)
    act_cov, grad_cov = call(
        factor_kernel,
        (at, got, *blocks),
        [shape((tile, feat_grp), F32)] * 2,
        4 * LANES * samp * n_col * feat_grp,
    )
    return (precond, act_cov, grad_cov)


def solution(mesh):
    return jax.shard_map(
        body,
        mesh=mesh,
        in_specs=(P("col", "row"), P("col", "grp"), P("col"), P("grp", "row"), P("grp", "col")),
        out_specs=(P(("grp", "row"), "col"), P(("row", "col"), "grp"), P(("row", "col"), "grp")),
        check_vma=False,
    )
```

time: 149 us -> 123 us (0.83)
  starting transfers between devices: 24.4 us -> 69.2 us
  blocking collectives: 39.6 us -> 0 us
  waiting for transfers between devices: 61.1 us -> 36 us
  matrix products: 14 us -> 0 us
  Pallas kernels: 0 us -> 9.49 us
  local copies, waits for them, and re-layouts: 5.82 us -> 3.99 us
    all_to_all x2, waiting for transfers between devices: 54.6 us -> 0.01 us  [the longest x1 0.01 us: body(): first = lax.all_to_all(payload, 'row', 0, 0)]
    ppermute x0 -> x13, starting transfers between devices: none -> 41.4 us  [the longest x7 22.6 us: body(): lax.ppermute(picked, 'col', [(i, (i + k) % n_col) for i in range(n_col)])]
    all_to_all x1 -> x0, blocking collectives: 39.6 us -> none  [body(): got = lax.all_to_all(send, ('grp', 'col'), 0, 0)]
    ppermute x0 -> x13, waiting for transfers between devices: none -> 27.4 us  [the longest x3 12.8 us: body(): moved = lax.ppermute(parts[x], 'grp', [(i, i ^ x) for i in range(n_grp)])]
    dot_general x4 -> x0, matrix products: 14 us -> none  [the longest x1 6.49 us: body(): jnp.einsum('gcat,ctn->gan', lefts, v_all, preferred_element_type=F32)]
    pallas_call x0 -> x7, Pallas kernels: none -> 9.49 us  [call(): pl.pallas_call(kernel, out_shape=outs, in_specs=[SMEM if x.dtype == jnp.i...]
    unnamed x4 -> x10, local copies, waits for them, and re-layouts: 0.01 us -> 3.83 us
    broadcast_in_dim x6 -> x0, local copies, waits for them, and re-layouts: 2.32 us -> none  [the longest x1 1.95 us: body(): jnp.broadcast_to(cotangent, (n_col,) + cotangent.shape)]
  transfers between devices with their start and end apart: 3 -> 16, of which waited for: 3 -> 8; matrix products, arithmetic and copies ran while one was open for 5% -> 0% of each run, Pallas kernels for 0% -> 3%
where the time goes in v5:
time: 123 us; the launch traced here: 122 us
  starting transfers between devices  69.2 us (56%)
  waiting for transfers between devices  36 us (29%)
  Pallas kernels  9.49 us (8%)
  local copies, waits for them, and re-layouts  3.99 us (3%)
  other arithmetic  2.6 us (2%)
    ppermute x7, starting transfers between devices, body(): lax.ppermute(picked, 'col', [(i, (i + k) % n_col) for i in range(n_col)])  22.6 us
    all_to_all x1, starting transfers between devices, body(): first = lax.all_to_all(payload, 'row', 0, 0)  15.7 us
    ppermute x3, waiting for transfers between devices, body(): moved = lax.ppermute(parts[x], 'grp', [(i, i ^ x) for i in range(n_grp)])  12.8 us
    ppermute x7, waiting for transfers between devices, body(): lax.ppermute(picked, 'col', [(i, (i + k) % n_col) for i in range(n_col)])  9.54 us
    pallas_call x7, Pallas kernels, call(): pl.pallas_call(kernel, out_shape=outs, in_specs=[SMEM if x.dtype == jnp.i...  9.49 us
    ppermute x3, starting transfers between devices, body(): moved = lax.ppermute(parts[x], 'grp', [(i, i ^ x) for i in range(n_grp)])  9.37 us
    ppermute x3, starting transfers between devices, body(): lax.ppermute(right, 'row', [(i, i - i % spread + (i + j) % spread) for i...  9.36 us
    all_to_all x1, waiting for transfers between devices, body(): term = lax.all_to_all(term, 'grp', 0, 0)  8.56 us
  transfers between devices with their start and end apart: 16, of which 8 were waited for; matrix products, arithmetic and copies ran while one was open for 0% of the time, Pallas kernels for 3%

profile of v5, /device:TPU:1, one launch (start us, length us, event | category | flops | bytes accessed | tf_op | source)
XLA Modules:
  0.0 122.1 jit_solution(15900605212220754771)
XLA Ops:
  1.5 1.3 %copy-done.1 = bf16[1536,384]{1,0:T(8,128)(2,1)S(1)} copy-done((bf16[1536,384]{1,0:T(8,128)(2,1)S(1)}, bf16[1536,384]{1,0:T(8,128)(2,1)}, u32[]{:S(2)}) %copy-start.1) | copy-done | bytes 1179672
  3.6 1.8 %shard_map.76 = bf16[16,120,128]{2,1,0:T(8,128)(2,1)} custom-call(s32[5]{0:T(128)S(1)} %stack.20.at, s32[8]{0:T(128)S(1)} %dynamic_slice.3.picks, bf16[128,384]{1,0:T(8,128)(2,1)S(1)} %copy-done.3, bf16[1536,384]{1,0:T(8,128)(2,1)S(1)} %copy-done.1), custom_call_target="tpu_custom_call" | custom-call | flops 150994944 | bytes 1769524 | tf_op jit(solution)/shard_map/pallas_call | solution.py:21
  5.5 15.7 %all-to-all-start = ((bf16[16,120,128]{2,1,0:T(8,128)(2,1)}), bf16[16,120,128]{2,1,0:T(8,128)(2,1)S(1)}, u32[]{:S(2)}, u32[]{:S(2)}) async-start(bf16[16,120,128]{2,1,0:T(8,128)(2,1)} %shard_map.76), calls=%async_computation | async-start | bytes 983040 | tf_op jit(solution)/shard_map/all_to_all | solution.py:191
  22.0 5.6 %collective-permute-start.6 = (bf16[64,1536]{1,0:T(8,128)(2,1)S(1)}, bf16[64,1536]{1,0:T(8,128)(2,1)S(1)}, u32[]{:S(2)}, u32[]{:S(2)}) collective-permute-start(bf16[64,1536]{1,0:T(8,128)(2,1)S(1)} %shard_map.77.gy_ref.refs_0_), channel_id=1, source_target_pairs={{0,7},{1,0},{2,1},{3,2},{4,3},{5,4},{6,5},{7,6},{8,15},{9,8},{10,9... | collective-permute-start | bytes 589832 | tf_op jit(solution)/shard_map/ppermute | solution.py:200
  27.6 2.3 %collective-permute-start.5 = (bf16[64,1536]{1,0:T(8,128)(2,1)S(1)}, bf16[64,1536]{1,0:T(8,128)(2,1)S(1)}, u32[]{:S(2)}, u32[]{:S(2)}) collective-permute-start(bf16[64,1536]{1,0:T(8,128)(2,1)S(1)} %shard_map.77.gy_ref.refs_0_), channel_id=1, source_target_pairs={{0,6},{1,7},{2,0},{3,1},{4,2},{5,3},{6,4},{7,5},{8,14},{9,15},{10,... | collective-permute-start | bytes 589832 | tf_op jit(solution)/shard_map/ppermute | solution.py:200
  29.8 2.6 %collective-permute-start.4 = (bf16[64,1536]{1,0:T(8,128)(2,1)S(1)}, bf16[64,1536]{1,0:T(8,128)(2,1)S(1)}, u32[]{:S(2)}, u32[]{:S(2)}) collective-permute-start(bf16[64,1536]{1,0:T(8,128)(2,1)S(1)} %shard_map.77.gy_ref.refs_0_), channel_id=1, source_target_pairs={{0,5},{1,6},{2,7},{3,0},{4,1},{5,2},{6,3},{7,4},{8,13},{9,14},{10,... | collective-permute-start | bytes 589832 | tf_op jit(solution)/shard_map/ppermute | solution.py:200
  32.4 3.1 %collective-permute-start.3 = (bf16[64,1536]{1,0:T(8,128)(2,1)S(1)}, bf16[64,1536]{1,0:T(8,128)(2,1)S(1)}, u32[]{:S(2)}, u32[]{:S(2)}) collective-permute-start(bf16[64,1536]{1,0:T(8,128)(2,1)S(1)} %shard_map.77.gy_ref.refs_0_), channel_id=1, source_target_pairs={{0,4},{1,5},{2,6},{3,7},{4,0},{5,1},{6,2},{7,3},{8,12},{9,13},{10,... | collective-permute-start | bytes 589832 | tf_op jit(solution)/shard_map/ppermute | solution.py:200
  35.5 3.0 %collective-permute-start.2 = (bf16[64,1536]{1,0:T(8,128)(2,1)S(1)}, bf16[64,1536]{1,0:T(8,128)(2,1)S(1)}, u32[]{:S(2)}, u32[]{:S(2)}) collective-permute-start(bf16[64,1536]{1,0:T(8,128)(2,1)S(1)} %shard_map.77.gy_ref.refs_0_), channel_id=1, source_target_pairs={{0,3},{1,4},{2,5},{3,6},{4,7},{5,0},{6,1},{7,2},{8,11},{9,12},{10,... | collective-permute-start | bytes 589832 | tf_op jit(solution)/shard_map/ppermute | solution.py:200
  38.5 4.2 %collective-permute-start.1 = (bf16[64,1536]{1,0:T(8,128)(2,1)S(1)}, bf16[64,1536]{1,0:T(8,128)(2,1)S(1)}, u32[]{:S(2)}, u32[]{:S(2)}) collective-permute-start(bf16[64,1536]{1,0:T(8,128)(2,1)S(1)} %shard_map.77.gy_ref.refs_0_), channel_id=1, source_target_pairs={{0,2},{1,3},{2,4},{3,5},{4,6},{5,7},{6,0},{7,1},{8,10},{9,11},{10,... | collective-permute-start | bytes 589832 | tf_op jit(solution)/shard_map/ppermute | solution.py:200
  42.7 1.9 %collective-permute-start = (bf16[64,1536]{1,0:T(8,128)(2,1)S(1)}, bf16[64,1536]{1,0:T(8,128)(2,1)S(1)}, u32[]{:S(2)}, u32[]{:S(2)}) collective-permute-start(bf16[64,1536]{1,0:T(8,128)(2,1)S(1)} %shard_map.77.gy_ref.refs_0_), channel_id=1, source_target_pairs={{0,1},{1,2},{2,3},{3,4},{4,5},{5,6},{6,7},{7,0},{8,9},{9,10},{10,1... | collective-permute-start | bytes 589832 | tf_op jit(solution)/shard_map/ppermute | solution.py:200
  45.5 3.8 %collective-permute-done.2.refs_3_ = bf16[64,1536]{1,0:T(8,128)(2,1)S(1)} collective-permute-done((bf16[64,1536]{1,0:T(8,128)(2,1)S(1)}, bf16[64,1536]{1,0:T(8,128)(2,1)S(1)}, u32[]{:S(2)}, u32[]{:S(2)}) %collective-permute-start.2) | collective-permute-done | bytes 196640 | tf_op jit(solution)/shard_map/ppermute | solution.py:200
  49.3 2.0 %collective-permute-done.1.refs_2_ = bf16[64,1536]{1,0:T(8,128)(2,1)S(1)} collective-permute-done((bf16[64,1536]{1,0:T(8,128)(2,1)S(1)}, bf16[64,1536]{1,0:T(8,128)(2,1)S(1)}, u32[]{:S(2)}, u32[]{:S(2)}) %collective-permute-start.1) | collective-permute-done | bytes 196640 | tf_op jit(solution)/shard_map/ppermute | solution.py:200
  51.3 3.7 %collective-permute-done.refs_1_ = bf16[64,1536]{1,0:T(8,128)(2,1)S(1)} collective-permute-done((bf16[64,1536]{1,0:T(8,128)(2,1)S(1)}, bf16[64,1536]{1,0:T(8,128)(2,1)S(1)}, u32[]{:S(2)}, u32[]{:S(2)}) %collective-permute-start) | collective-permute-done | bytes 196640 | tf_op jit(solution)/shard_map/ppermute | solution.py:200
  55.0 1.3 %shard_map.79 = bf16[4,8,160,128]{3,2,1,0:T(8,128)(2,1)} custom-call(bf16[16,120,128]{2,1,0:T(8,128)(2,1)S(1)} %all-to-all-done.got_ref, bf16[8,32,128]{2,1,0:T(8,128)(2,1)S(1)} %shard_map.78.side_ref), custom_call_target="tpu_custom_call" | custom-call | flops 1000000 | bytes 1867776 | tf_op jit(solution)/shard_map/pallas_call | solution.py:21
  56.3 1.7 %copy-done = bf16[1536,768]{1,0:T(8,128)(2,1)S(1)} copy-done((bf16[1536,768]{1,0:T(8,128)(2,1)S(1)}, bf16[1536,768]{1,0:T(8,128)(2,1)}, u32[]{:S(2)}) %copy-start) | copy-done | bytes 2359320
  57.9 1.4 %shard_map.80 = (bf16[64,768]{1,0:T(8,128)(2,1)S(1)}, bf16[64,768]{1,0:T(8,128)(2,1)S(1)}, bf16[64,768]{1,0:T(8,128)(2,1)S(1)}, bf16[64,768]{1,0:T(8,128)(2,1)S(1)}) custom-call(s32[5]{0:T(128)S(1)} %stack.20.at, bf16[1536,768]{1,0:T(8,128)(2,1)S(1)} %copy-done, bf16[64,1536]{1,0:T(8,128)(2,1)S(1)} %shard_map.77.gy_ref.refs_0_, ...), custom_call_target="tpu_custom_call" | custom-call | flops 603979776 | bytes 4325396 | tf_op jit(solution)/shard_map/pallas_call | solution.py:21
  59.3 6.6 %all-to-all-start.1 = ((bf16[32,160,128]{2,1,0:T(8,128)(2,1)}), bf16[32,160,128]{2,1,0:T(8,128)(2,1)S(1)}, u32[]{:S(2)}, u32[]{:S(2)}) async-start(bf16[32,160,128]{2,1,0:T(8,128)(2,1)} %bitcast.4), calls=%async_computation.1 | async-start | bytes 2621440 | tf_op jit(solution)/shard_map/all_to_all | solution.py:225
  65.9 2.1 %collective-permute-start.7 = (bf16[64,768]{1,0:T(8,128)(2,1)S(1)}, bf16[64,768]{1,0:T(8,128)(2,1)S(1)}, u32[]{:S(2)}, u32[]{:S(2)}) collective-permute-start(bf16[64,768]{1,0:T(8,128)(2,1)S(1)} %get-tuple-element.52), channel_id=1, source_target_pairs={{0,128},{128,0},{256,384},{384,256},{1,129},{129,1},{257,385},{385... | collective-permute-start | bytes 294920 | tf_op jit(solution)/shard_map/ppermute | solution.py:229
  68.1 4.9 %collective-permute-start.8 = (bf16[64,768]{1,0:T(8,128)(2,1)S(1)}, bf16[64,768]{1,0:T(8,128)(2,1)S(1)}, u32[]{:S(2)}, u32[]{:S(2)}) collective-permute-start(bf16[64,768]{1,0:T(8,128)(2,1)S(1)} %get-tuple-element.53), channel_id=1, source_target_pairs={{0,256},{128,384},{256,0},{384,128},{1,257},{129,385},{257,1},{385... | collective-permute-start | bytes 294920 | tf_op jit(solution)/shard_map/ppermute | solution.py:229
  73.0 2.3 %collective-permute-start.9 = (bf16[64,768]{1,0:T(8,128)(2,1)S(1)}, bf16[64,768]{1,0:T(8,128)(2,1)S(1)}, u32[]{:S(2)}, u32[]{:S(2)}) collective-permute-start(bf16[64,768]{1,0:T(8,128)(2,1)S(1)} %get-tuple-element.54), channel_id=1, source_target_pairs={{0,384},{128,256},{256,128},{384,0},{1,385},{129,257},{257,129},{3... | collective-permute-start | bytes 294920 | tf_op jit(solution)/shard_map/ppermute | solution.py:229
  75.3 10.5 %collective-permute-done.8 = bf16[64,768]{1,0:T(8,128)(2,1)S(1)} collective-permute-done((bf16[64,768]{1,0:T(8,128)(2,1)S(1)}, bf16[64,768]{1,0:T(8,128)(2,1)S(1)}, u32[]{:S(2)}, u32[]{:S(2)}) %collective-permute-start.8) | collective-permute-done | bytes 98336 | tf_op jit(solution)/shard_map/ppermute | solution.py:229
  85.9 2.3 %collective-permute-done.9 = bf16[64,768]{1,0:T(8,128)(2,1)S(1)} collective-permute-done((bf16[64,768]{1,0:T(8,128)(2,1)S(1)}, bf16[64,768]{1,0:T(8,128)(2,1)S(1)}, u32[]{:S(2)}, u32[]{:S(2)}) %collective-permute-start.9) | collective-permute-done | bytes 98336 | tf_op jit(solution)/shard_map/ppermute | solution.py:229
  88.2 5.0 %collective-permute-start.12 = (bf16[64,768]{1,0:T(8,128)(2,1)S(1)}, bf16[64,768]{1,0:T(8,128)(2,1)S(1)}, u32[]{:S(2)}, u32[]{:S(2)}) collective-permute-start(bf16[64,768]{1,0:T(8,128)(2,1)S(1)} %add_convert_fusion.refs_0_), channel_id=1, source_target_pairs={{0,24},{8,0},{16,8},{24,16},{32,56},{40,32},{48,40},{56,48},{64,88... | collective-permute-start | bytes 294920 | tf_op jit(solution)/shard_map/ppermute | solution.py:233
  93.2 1.9 %collective-permute-start.11 = (bf16[64,768]{1,0:T(8,128)(2,1)S(1)}, bf16[64,768]{1,0:T(8,128)(2,1)S(1)}, u32[]{:S(2)}, u32[]{:S(2)}) collective-permute-start(bf16[64,768]{1,0:T(8,128)(2,1)S(1)} %add_convert_fusion.refs_0_), channel_id=1, source_target_pairs={{0,16},{8,24},{16,0},{24,8},{32,48},{40,56},{48,32},{56,40},{64,80... | collective-permute-start | bytes 294920 | tf_op jit(solution)/shard_map/ppermute | solution.py:233
  95.1 2.5 %collective-permute-start.10 = (bf16[64,768]{1,0:T(8,128)(2,1)S(1)}, bf16[64,768]{1,0:T(8,128)(2,1)S(1)}, u32[]{:S(2)}, u32[]{:S(2)}) collective-permute-start(bf16[64,768]{1,0:T(8,128)(2,1)S(1)} %add_convert_fusion.refs_0_), channel_id=1, source_target_pairs={{0,8},{8,16},{16,24},{24,0},{32,40},{40,48},{48,56},{56,32},{64,72... | collective-permute-start | bytes 294920 | tf_op jit(solution)/shard_map/ppermute | solution.py:233
  97.6 2.7 %collective-permute-done.11.refs_2_ = bf16[64,768]{1,0:T(8,128)(2,1)S(1)} collective-permute-done((bf16[64,768]{1,0:T(8,128)(2,1)S(1)}, bf16[64,768]{1,0:T(8,128)(2,1)S(1)}, u32[]{:S(2)}, u32[]{:S(2)}) %collective-permute-start.11) | collective-permute-done | bytes 98336 | tf_op jit(solution)/shard_map/ppermute | solution.py:233
  100.2 2.4 %collective-permute-done.10.refs_1_ = bf16[64,768]{1,0:T(8,128)(2,1)S(1)} collective-permute-done((bf16[64,768]{1,0:T(8,128)(2,1)S(1)}, bf16[64,768]{1,0:T(8,128)(2,1)S(1)}, u32[]{:S(2)}, u32[]{:S(2)}) %collective-permute-start.10) | collective-permute-done | bytes 98336 | tf_op jit(solution)/shard_map/ppermute | solution.py:233
  102.6 1.8 %shard_map.81 = bf16[4,96,768]{2,1,0:T(8,128)(2,1)} custom-call(s32[5]{0:T(128)S(1)} %stack.20.at, bf16[4,8,160,128]{3,2,1,0:T(8,128)(2,1)S(1)} %bitcast.6, bf16[64,768]{1,0:T(8,128)(2,1)S(1)} %add_convert_fusion.refs_0_, bf16[64,768]{1,0:T(8,128)(2,1)S(1)} %collective-permute-done.10.refs_1_, bf16[64,768]{1,0:T(8,128)(2,1)S(1)} %collective-permute-done.11.refs_2_, ...), custom_call_target="tpu_custom_call" | custom-call | flops 201326592 | bytes 2293780 | tf_op jit(solution)/shard_map/pallas_call | solution.py:21
  104.5 5.5 %all-to-all-start.2 = ((bf16[4,96,768]{2,1,0:T(8,128)(2,1)}), bf16[4,96,768]{2,1,0:T(8,128)(2,1)}, u32[]{:S(2)}, u32[]{:S(2)}) async-start(bf16[4,96,768]{2,1,0:T(8,128)(2,1)} %shard_map.81), calls=%async_computation.2 | async-start | bytes 1179648 | tf_op jit(solution)/shard_map/all_to_all | solution.py:247
  109.9 1.7 %shard_map.82 = (f32[48,1536]{1,0:T(8,128)}, f32[48,1536]{1,0:T(8,128)}) custom-call(s32[5]{0:T(128)S(1)} %stack.20.at, bf16[4,8,160,128]{3,2,1,0:T(8,128)(2,1)S(1)} %bitcast.7, bf16[64,1536]{1,0:T(8,128)(2,1)S(1)} %shard_map.77.gy_ref.refs_0_, bf16[64,1536]{1,0:T(8,128)(2,1)S(1)} %collective-permute-done.refs_1_, ...), custom_call_target="tpu_custom_call" | custom-call | flops 201326592 | bytes 3473428 | tf_op jit(solution)/shard_map/pallas_call | solution.py:21
  111.7 8.6 %all-to-all-done.2 = bf16[4,96,768]{2,1,0:T(8,128)(2,1)} async-done(((bf16[4,96,768]{2,1,0:T(8,128)(2,1)}), bf16[4,96,768]{2,1,0:T(8,128)(2,1)}, u32[]{:S(2)}, u32[]{:S(2)}) %all-to-all-start.2) | async-done | bytes 589856 | tf_op jit(solution)/shard_map/all_to_all | solution.py:247
  120.2 1.9 %convert_reduce_fusion = f32[96,768]{1,0:T(8,128)} fusion(bf16[4,96,768]{2,1,0:T(8,128)(2,1)} %all-to-all-done.2), kind=kLoop, calls=%fused_computation | loop fusion | flops 516096 | bytes 884736 | tf_op jit(solution)/shard_map/reduce_sum | solution.py:248
  (22 shorter events, 3.3 us)
Async XLA Ops:
  1.5 1.3 %copy-start.1 = (bf16[1536,384]{1,0:T(8,128)(2,1)S(1)}, bf16[1536,384]{1,0:T(8,128)(2,1)}, u32[]{:S(2)}) copy-start(bf16[1536,384]{1,0:T(8,128)(2,1)} %a_ref.1) | copy-start | bytes 3538948
  2.8 0.9 copy-start.3
  3.6 17.6 %copy-start.2 = (bf16[128,1536]{1,0:T(8,128)(2,1)S(1)}, bf16[128,1536]{1,0:T(8,128)(2,1)}, u32[]{:S(2)}) copy-start(bf16[128,1536]{1,0:T(8,128)(2,1)} %g_ref) | copy-start | bytes 1179652
  3.6 41.0 %copy-start.4 = (bf16[128,384]{1,0:T(8,128)(2,1)S(1)}, bf16[128,384]{1,0:T(8,128)(2,1)}, u32[]{:S(2)}) copy-start(bf16[128,384]{1,0:T(8,128)(2,1)} %x_ref.3) | copy-start | bytes 294916
  5.5 49.5 %all-to-all-start = ((bf16[16,120,128]{2,1,0:T(8,128)(2,1)}), bf16[16,120,128]{2,1,0:T(8,128)(2,1)S(1)}, u32[]{:S(2)}, u32[]{:S(2)}) async-start(bf16[16,120,128]{2,1,0:T(8,128)(2,1)} %shard_map.76), calls=%async_computation | async-start | bytes 983040 | tf_op jit(solution)/shard_map/all_to_all | solution.py:191
  22.0 16.5 %collective-permute-start.6 = (bf16[64,1536]{1,0:T(8,128)(2,1)S(1)}, bf16[64,1536]{1,0:T(8,128)(2,1)S(1)}, u32[]{:S(2)}, u32[]{:S(2)}) collective-permute-start(bf16[64,1536]{1,0:T(8,128)(2,1)S(1)} %shard_map.77.gy_ref.refs_0_), channel_id=1, source_target_pairs={{0,7},{1,0},{2,1},{3,2},{4,3},{5,4},{6,5},{7,6},{8,15},{9,8},{10,9... | collective-permute-start | bytes 589832 | tf_op jit(solution)/shard_map/ppermute | solution.py:200
  27.6 15.2 %collective-permute-start.5 = (bf16[64,1536]{1,0:T(8,128)(2,1)S(1)}, bf16[64,1536]{1,0:T(8,128)(2,1)S(1)}, u32[]{:S(2)}, u32[]{:S(2)}) collective-permute-start(bf16[64,1536]{1,0:T(8,128)(2,1)S(1)} %shard_map.77.gy_ref.refs_0_), channel_id=1, source_target_pairs={{0,6},{1,7},{2,0},{3,1},{4,2},{5,3},{6,4},{7,5},{8,14},{9,15},{10,... | collective-permute-start | bytes 589832 | tf_op jit(solution)/shard_map/ppermute | solution.py:200
  29.8 15.6 %collective-permute-start.4 = (bf16[64,1536]{1,0:T(8,128)(2,1)S(1)}, bf16[64,1536]{1,0:T(8,128)(2,1)S(1)}, u32[]{:S(2)}, u32[]{:S(2)}) collective-permute-start(bf16[64,1536]{1,0:T(8,128)(2,1)S(1)} %shard_map.77.gy_ref.refs_0_), channel_id=1, source_target_pairs={{0,5},{1,6},{2,7},{3,0},{4,1},{5,2},{6,3},{7,4},{8,13},{9,14},{10,... | collective-permute-start | bytes 589832 | tf_op jit(solution)/shard_map/ppermute | solution.py:200
  32.4 13.1 %collective-permute-start.3 = (bf16[64,1536]{1,0:T(8,128)(2,1)S(1)}, bf16[64,1536]{1,0:T(8,128)(2,1)S(1)}, u32[]{:S(2)}, u32[]{:S(2)}) collective-permute-start(bf16[64,1536]{1,0:T(8,128)(2,1)S(1)} %shard_map.77.gy_ref.refs_0_), channel_id=1, source_target_pairs={{0,4},{1,5},{2,6},{3,7},{4,0},{5,1},{6,2},{7,3},{8,12},{9,13},{10,... | collective-permute-start | bytes 589832 | tf_op jit(solution)/shard_map/ppermute | solution.py:200
  35.5 13.8 %collective-permute-start.2 = (bf16[64,1536]{1,0:T(8,128)(2,1)S(1)}, bf16[64,1536]{1,0:T(8,128)(2,1)S(1)}, u32[]{:S(2)}, u32[]{:S(2)}) collective-permute-start(bf16[64,1536]{1,0:T(8,128)(2,1)S(1)} %shard_map.77.gy_ref.refs_0_), channel_id=1, source_target_pairs={{0,3},{1,4},{2,5},{3,6},{4,7},{5,0},{6,1},{7,2},{8,11},{9,12},{10,... | collective-permute-start | bytes 589832 | tf_op jit(solution)/shard_map/ppermute | solution.py:200
  38.5 12.8 %collective-permute-start.1 = (bf16[64,1536]{1,0:T(8,128)(2,1)S(1)}, bf16[64,1536]{1,0:T(8,128)(2,1)S(1)}, u32[]{:S(2)}, u32[]{:S(2)}) collective-permute-start(bf16[64,1536]{1,0:T(8,128)(2,1)S(1)} %shard_map.77.gy_ref.refs_0_), channel_id=1, source_target_pairs={{0,2},{1,3},{2,4},{3,5},{4,6},{5,7},{6,0},{7,1},{8,10},{9,11},{10,... | collective-permute-start | bytes 589832 | tf_op jit(solution)/shard_map/ppermute | solution.py:200
  42.7 12.3 %collective-permute-start = (bf16[64,1536]{1,0:T(8,128)(2,1)S(1)}, bf16[64,1536]{1,0:T(8,128)(2,1)S(1)}, u32[]{:S(2)}, u32[]{:S(2)}) collective-permute-start(bf16[64,1536]{1,0:T(8,128)(2,1)S(1)} %shard_map.77.gy_ref.refs_0_), channel_id=1, source_target_pairs={{0,1},{1,2},{2,3},{3,4},{4,5},{5,6},{6,7},{7,0},{8,9},{9,10},{10,1... | collective-permute-start | bytes 589832 | tf_op jit(solution)/shard_map/ppermute | solution.py:200
  56.3 1.7 %copy-start = (bf16[1536,768]{1,0:T(8,128)(2,1)S(1)}, bf16[1536,768]{1,0:T(8,128)(2,1)}, u32[]{:S(2)}) copy-start(bf16[1536,768]{1,0:T(8,128)(2,1)} %b_ref.1) | copy-start | bytes 7077892
  59.3 43.3 %all-to-all-start.1 = ((bf16[32,160,128]{2,1,0:T(8,128)(2,1)}), bf16[32,160,128]{2,1,0:T(8,128)(2,1)S(1)}, u32[]{:S(2)}, u32[]{:S(2)}) async-start(bf16[32,160,128]{2,1,0:T(8,128)(2,1)} %bitcast.4), calls=%async_computation.1 | async-start | bytes 2621440 | tf_op jit(solution)/shard_map/all_to_all | solution.py:225
  65.9 9.4 %collective-permute-start.7 = (bf16[64,768]{1,0:T(8,128)(2,1)S(1)}, bf16[64,768]{1,0:T(8,128)(2,1)S(1)}, u32[]{:S(2)}, u32[]{:S(2)}) collective-permute-start(bf16[64,768]{1,0:T(8,128)(2,1)S(1)} %get-tuple-element.52), channel_id=1, source_target_pairs={{0,128},{128,0},{256,384},{384,256},{1,129},{129,1},{257,385},{385... | collective-permute-start | bytes 294920 | tf_op jit(solution)/shard_map/ppermute | solution.py:229
  68.1 17.8 %collective-permute-start.8 = (bf16[64,768]{1,0:T(8,128)(2,1)S(1)}, bf16[64,768]{1,0:T(8,128)(2,1)S(1)}, u32[]{:S(2)}, u32[]{:S(2)}) collective-permute-start(bf16[64,768]{1,0:T(8,128)(2,1)S(1)} %get-tuple-element.53), channel_id=1, source_target_pairs={{0,256},{128,384},{256,0},{384,128},{1,257},{129,385},{257,1},{385... | collective-permute-start | bytes 294920 | tf_op jit(solution)/shard_map/ppermute | solution.py:229
  73.0 15.1 %collective-permute-start.9 = (bf16[64,768]{1,0:T(8,128)(2,1)S(1)}, bf16[64,768]{1,0:T(8,128)(2,1)S(1)}, u32[]{:S(2)}, u32[]{:S(2)}) collective-permute-start(bf16[64,768]{1,0:T(8,128)(2,1)S(1)} %get-tuple-element.54), channel_id=1, source_target_pairs={{0,384},{128,256},{256,128},{384,0},{1,385},{129,257},{257,129},{3... | collective-permute-start | bytes 294920 | tf_op jit(solution)/shard_map/ppermute | solution.py:229
  88.2 9.4 %collective-permute-start.12 = (bf16[64,768]{1,0:T(8,128)(2,1)S(1)}, bf16[64,768]{1,0:T(8,128)(2,1)S(1)}, u32[]{:S(2)}, u32[]{:S(2)}) collective-permute-start(bf16[64,768]{1,0:T(8,128)(2,1)S(1)} %add_convert_fusion.refs_0_), channel_id=1, source_target_pairs={{0,24},{8,0},{16,8},{24,16},{32,56},{40,32},{48,40},{56,48},{64,88... | collective-permute-start | bytes 294920 | tf_op jit(solution)/shard_map/ppermute | solution.py:233
  93.2 7.1 %collective-permute-start.11 = (bf16[64,768]{1,0:T(8,128)(2,1)S(1)}, bf16[64,768]{1,0:T(8,128)(2,1)S(1)}, u32[]{:S(2)}, u32[]{:S(2)}) collective-permute-start(bf16[64,768]{1,0:T(8,128)(2,1)S(1)} %add_convert_fusion.refs_0_), channel_id=1, source_target_pairs={{0,16},{8,24},{16,0},{24,8},{32,48},{40,56},{48,32},{56,40},{64,80... | collective-permute-start | bytes 294920 | tf_op jit(solution)/shard_map/ppermute | solution.py:233
  95.1 7.5 %collective-permute-start.10 = (bf16[64,768]{1,0:T(8,128)(2,1)S(1)}, bf16[64,768]{1,0:T(8,128)(2,1)S(1)}, u32[]{:S(2)}, u32[]{:S(2)}) collective-permute-start(bf16[64,768]{1,0:T(8,128)(2,1)S(1)} %add_convert_fusion.refs_0_), channel_id=1, source_target_pairs={{0,8},{8,16},{16,24},{24,0},{32,40},{40,48},{48,56},{56,32},{64,72... | collective-permute-start | bytes 294920 | tf_op jit(solution)/shard_map/ppermute | solution.py:233
  104.5 15.8 %all-to-all-start.2 = ((bf16[4,96,768]{2,1,0:T(8,128)(2,1)}), bf16[4,96,768]{2,1,0:T(8,128)(2,1)}, u32[]{:S(2)}, u32[]{:S(2)}) async-start(bf16[4,96,768]{2,1,0:T(8,128)(2,1)} %shard_map.81), calls=%async_computation.2 | async-start | bytes 1179648 | tf_op jit(solution)/shard_map/all_to_all | solution.py:247

commit v6 on v5

--- a/solution.py
+++ b/solution.py
@@ -27,6 +27,10 @@
         compiler_params=pltpu.CompilerParams(vmem_limit_bytes=40 * 1024 * 1024),
         cost_estimate=pl.CostEstimate(flops=flops, bytes_accessed=moved, transcendentals=0),
     )(*inputs)
+
+
+def source_of(col, k):
+    return 4 * ((col // 4) ^ (k % 2)) + lax.rem(col % 4 - k // 2 + 4, 4)
 
 
 def rows_hot(targets, tok):
@@ -77,16 +81,16 @@
 
 
 def right_kernel(at, b_ref, *refs):
-    n_grp = 4
-    blocks, outs, held = refs[: -n_grp - 1], refs[-n_grp - 1 : -1], refs[-1]
-    each = blocks[0].shape[0] // 2
-    rows = jnp.concatenate([block[:each, :] for block in blocks], axis=0)
+    blocks, keep_ref, give_ref, held = refs[:-3], refs[-3], refs[-2], refs[-1]
+    n_blk, n_grp, size, width = held.shape
+    rows = jnp.concatenate([block[...] for block in blocks], axis=0)
     term = jnp.dot(rows, b_ref[...], preferred_element_type=F32)
-    size = each // n_grp
     held[...] = term.reshape(held.shape)
+    half = n_blk * size
     for x in range(n_grp):
-        piece = held[:, at[0] ^ x]
-        outs[x][...] = piece.reshape(len(blocks) * size, -1).astype(BF)
+        piece = held[:, at[0] ^ x].reshape(half, width).astype(BF)
+        out = give_ref if x % 2 else keep_ref
+        out[(x // 2) * half : (x // 2 + 1) * half, :] = piece
 
 
 def second_kernel(got_ref, side_ref, out_ref):
@@ -120,8 +124,7 @@
         plane = lax.rem(at[1] - j + spread, spread)
         block = v_refs[j][...].astype(F32)
         for k in range(n_col):
-            source = lax.rem(at[3] - k + n_col, n_col)
-            held[source, plane] = block[k * size : (k + 1) * size]
+            held[source_of(at[3], k), plane] = block[k * size : (k + 1) * size]
     tokens = n_col * spread * size
     right = held[...].reshape(tokens, width).astype(BF)
     for g in range(n_grp):
@@ -148,10 +151,10 @@
         term = lax.dot_general(left, strip, FIRST, preferred_element_type=F32)
         act_ref[:, t * LANES : (t + 1) * LANES] = term[tile : 2 * tile] * scale
     lefts, rights = [], []
-    for k, block in enumerate(blocks):
-        source = lax.rem(at[3] - k + n_col, n_col)
-        lefts.append(got_ref[at[4], source, side:, :])
-        rights.append(block[samp:, :])
+    for k in range(n_col):
+        lefts.append(got_ref[at[4], source_of(at[3], k), side:, :])
+    for block in blocks:
+        rights.append(block[...])
     left = jnp.concatenate(lefts, axis=0)
     right = jnp.concatenate(rights, axis=0)
     grad_ref[...] = lax.dot_general(left, right, FIRST, preferred_element_type=F32)[:tile] * scale
@@ -187,48 +190,53 @@
         [shape((n_row, out_rows + strip, tok), BF)],
         2 * feat_grp * feat_row * tok,
     )[0]
-    payload, cot = lax.optimization_barrier((payload, cotangent))
     first = lax.all_to_all(payload, "row", 0, 0)
+
+    def along_y(block, k):
+        return lax.ppermute(
+            block, "col", [(i, i - i % 4 + (i + k) % 4) for i in range(n_col)]
+        )
 
     picked = call(
         pick_kernel,
-        (at, offsets, cot),
+        (at, offsets, cotangent),
         [shape((n_grp * size + samp, feat_grp), BF)],
         2 * 64 * tok * feat_grp,
     )[0]
-    blocks = [picked] + [
-        lax.ppermute(picked, "col", [(i, (i + k) % n_col) for i in range(n_col)])
-        for k in range(1, n_col)
-    ]
+    beside = lax.ppermute(picked, "col", [(i, (i + 4) % n_col) for i in range(n_col)])
+    cut = n_grp * size
+    pair = jnp.concatenate([picked[:cut], beside[:cut]], axis=0)
+    pairs = [pair] + [along_y(pair, k) for k in range(1, 4)]
+    keep, give = call(
+        right_kernel,
+        (at, grad_inverse, *pairs),
+        [shape((2 * n_col * size, width), BF)] * 2,
+        2 * n_col * n_grp * size * feat_grp * width,
+        [pltpu.VMEM((n_col, n_grp, size, width), F32)],
+    )
+    taken = lax.ppermute(give, "grp", [(i, i ^ 1) for i in range(n_grp)])
+    halves = keep.astype(F32) + taken.astype(F32)
+    half = n_col * size
+    taken = lax.ppermute(halves[half:].astype(BF), "grp", [(i, i ^ 2) for i in range(n_grp)])
+    right = (halves[:half] + taken.astype(F32)).astype(BF)
+
+    keep, picked_y, beside_y = lax.optimization_barrier((keep, picked[cut:], beside[cut:]))
+    samples = jnp.concatenate([picked_y, beside_y], axis=0)
+    samples = [samples] + [along_y(samples, k) for k in range(1, 4)]
     side = call(
         side_kernel,
         (at, own, tokens_in, picked),
         [shape((n_col, samp, LANES), BF)],
         2 * samp * tok * feat_row,
     )[0]
-    first, blocks = lax.optimization_barrier((first, blocks))
-
     send = call(
         second_kernel,
         (first, side),
         [shape((n_grp, n_col, size * spread + strip * n_row // n_grp + samp, LANES), BF)],
         1000000,
     )[0]
-    parts = call(
-        right_kernel,
-        (at, grad_inverse, *blocks),
-        [shape((n_col * size, width), BF)] * n_grp,
-        2 * n_col * n_grp * size * feat_grp * width,
-        [pltpu.VMEM((n_col, n_grp, size, width), F32)],
-    )
-    send, parts = lax.optimization_barrier((send, parts))
     got = lax.all_to_all(send.reshape((n_grp * n_col,) + send.shape[2:]), ("grp", "col"), 0, 0)
     got = got.reshape(send.shape)
-    total = parts[0].astype(F32)
-    for x in range(1, n_grp):
-        moved = lax.ppermute(parts[x], "grp", [(i, i ^ x) for i in range(n_grp)])
-        total = total + moved.astype(F32)
-    right = total.astype(BF)
     rights = [right] + [
         lax.ppermute(
             right, "row", [(i, i - i % spread + (i + j) % spread) for i in range(n_row)]
@@ -243,12 +251,12 @@
         2 * n_grp * LANES * n_col * spread * size * width,
         [pltpu.VMEM((n_col, spread, size, width), F32)],
     )[0]
-    term, got, blocks = lax.optimization_barrier((term, got, blocks))
+    term, got, samples = lax.optimization_barrier((term, got, samples))
     term = lax.all_to_all(term, "grp", 0, 0)
     precond = jnp.sum(term.astype(F32), axis=0)
     act_cov, grad_cov = call(
         factor_kernel,
-        (at, got, *blocks),
+        (at, got, *samples),
         [shape((tile, feat_grp), F32)] * 2,
         4 * LANES * samp * n_col * feat_grp,
     )

time: 123 us -> 123 us (level)
  starting transfers between devices: 69.2 us -> 72.7 us
  local copies, waits for them, and re-layouts: 3.99 us -> 2.4 us
    ppermute x3, waiting for transfers between devices: 5.05 us -> 2.98 us  [body(): lax.ppermute(right, 'row', [(i, i - i % spread + (i + j) % spread) for i...]
    ppermute x10 -> x9, starting transfers between devices: 32 us -> 33.8 us  [the longest x6 21.3 us: along_y(): lax.ppermute(block, 'col', [(i, i - i % 4 + (i + k) % 4) for i in range(n...]
    unnamed x10 -> x11, local copies, waits for them, and re-layouts: 3.83 us -> 2.18 us
    ppermute x10 -> x9, waiting for transfers between devices: 22.4 us -> 23.6 us  [the longest x1 15 us: body(): lax.ppermute(halves[half:].astype(BF), 'grp', [(i, i ^ 2) for i in range(...]
  transfers between devices with their start and end apart: 16 -> 15, of which waited for: 8 -> 7; matrix products, arithmetic and copies ran while one was open for 0% -> 0% of each run, Pallas kernels for 3% -> 6%
where the time goes in v6:
time: 123 us; the launch traced here: 122 us
  starting transfers between devices  72.7 us (59%)
  waiting for transfers between devices  35 us (28%)
  Pallas kernels  9.49 us (8%)
  local copies, waits for them, and re-layouts  2.4 us (2%)
  other arithmetic  1.52 us (1%)
    ppermute x6, starting transfers between devices, along_y(): lax.ppermute(block, 'col', [(i, i - i % 4 + (i + k) % 4) for i in range(n...  21.3 us
    all_to_all x1, starting transfers between devices, body(): first = lax.all_to_all(payload, 'row', 0, 0)  15.9 us
    ppermute x1, waiting for transfers between devices, body(): lax.ppermute(halves[half:].astype(BF), 'grp', [(i, i ^ 2) for i in range(...  15 us
    ppermute x3, starting transfers between devices, body(): lax.ppermute(right, 'row', [(i, i - i % spread + (i + j) % spread) for i...  10.3 us
    pallas_call x7, Pallas kernels, call(): pl.pallas_call(kernel, out_shape=outs, in_specs=[SMEM if x.dtype == jnp.i...  9.49 us
    all_to_all x1, waiting for transfers between devices, body(): term = lax.all_to_all(term, 'grp', 0, 0)  8.45 us
    all_to_all x1, starting transfers between devices, body(): lax.all_to_all(send.reshape((n_grp * n_col,) + send.shape[2:]), ('grp', '...  6.58 us
    all_to_all x1, starting transfers between devices, body(): term = lax.all_to_all(term, 'grp', 0, 0)  6.14 us
  transfers between devices with their start and end apart: 15, of which 7 were waited for; matrix products, arithmetic and copies ran while one was open for 0% of the time, Pallas kernels for 6%

profile of v6, /device:TPU:1, one launch (start us, length us, event | category | flops | bytes accessed | tf_op | source)
XLA Modules:
  0.0 122.1 jit_solution(12760800850630485427)
XLA Ops:
  0.7 0.7 broadcast_subtract_fusion.picks
  1.5 1.3 %copy-done.1 = bf16[1536,384]{1,0:T(8,128)(2,1)S(1)} copy-done((bf16[1536,384]{1,0:T(8,128)(2,1)S(1)}, bf16[1536,384]{1,0:T(8,128)(2,1)}, u32[]{:S(2)}) %copy-start.1) | copy-done | bytes 1179672
  2.8 0.9 copy-done.3
  3.6 1.8 %shard_map.76 = bf16[16,120,128]{2,1,0:T(8,128)(2,1)} custom-call(s32[5]{0:T(128)S(1)} %stack.20.at, s32[8]{0:T(128)S(1)} %dynamic_slice.3.picks, bf16[128,384]{1,0:T(8,128)(2,1)S(1)} %copy-done.3, bf16[1536,384]{1,0:T(8,128)(2,1)S(1)} %copy-done.1), custom_call_target="tpu_custom_call" | custom-call | flops 150994944 | bytes 1769524 | tf_op jit(solution)/shard_map/pallas_call | solution.py:21
  5.5 15.9 %all-to-all-start = ((bf16[16,120,128]{2,1,0:T(8,128)(2,1)}), bf16[16,120,128]{2,1,0:T(8,128)(2,1)S(1)}, u32[]{:S(2)}, u32[]{:S(2)}) async-start(bf16[16,120,128]{2,1,0:T(8,128)(2,1)} %shard_map.76), calls=%async_computation | async-start | bytes 983040 | tf_op jit(solution)/shard_map/all_to_all | solution.py:193
  21.4 0.7 shard_map.77.gy_ref
  22.1 3.1 %collective-permute-start = (bf16[64,1536]{1,0:T(8,128)(2,1)S(1)}, bf16[64,1536]{1,0:T(8,128)(2,1)S(1)}, u32[]{:S(2)}, u32[]{:S(2)}) collective-permute-start(bf16[64,1536]{1,0:T(8,128)(2,1)S(1)} %shard_map.77.gy_ref), channel_id=1, source_target_pairs={{0,4},{1,5},{2,6},{3,7},{4,0},{5,1},{6,2},{7,3},{8,12},{9,13},{10,... | collective-permute-start | bytes 589832 | tf_op jit(solution)/shard_map/ppermute | solution.py:206
  25.3 4.2 %collective-permute-done = bf16[64,1536]{1,0:T(8,128)(2,1)S(1)} collective-permute-done((bf16[64,1536]{1,0:T(8,128)(2,1)S(1)}, bf16[64,1536]{1,0:T(8,128)(2,1)S(1)}, u32[]{:S(2)}, u32[]{:S(2)}) %collective-permute-start) | collective-permute-done | bytes 196640 | tf_op jit(solution)/shard_map/ppermute | solution.py:206
  29.5 3.4 %collective-permute-start.1 = (bf16[64,1536]{1,0:T(8,128)(2,1)S(1)}, bf16[64,1536]{1,0:T(8,128)(2,1)S(1)}, u32[]{:S(2)}, u32[]{:S(2)}) collective-permute-start(bf16[64,1536]{1,0:T(8,128)(2,1)S(1)} %pad_maximum_fusion.refs_0_), channel_id=1, source_target_pairs={{0,1},{1,2},{2,3},{3,0},{4,5},{5,6},{6,7},{7,4},{8,9},{9,10},{10,1... | collective-permute-start | bytes 589832 | tf_op jit(solution)/shard_map/ppermute | solution.py:196
  32.9 4.5 %collective-permute-start.2 = (bf16[64,1536]{1,0:T(8,128)(2,1)S(1)}, bf16[64,1536]{1,0:T(8,128)(2,1)S(1)}, u32[]{:S(2)}, u32[]{:S(2)}) collective-permute-start(bf16[64,1536]{1,0:T(8,128)(2,1)S(1)} %pad_maximum_fusion.refs_0_), channel_id=1, source_target_pairs={{0,2},{1,3},{2,0},{3,1},{4,6},{5,7},{6,4},{7,5},{8,10},{9,11},{10,... | collective-permute-start | bytes 589832 | tf_op jit(solution)/shard_map/ppermute | solution.py:196
  37.4 3.0 %collective-permute-start.3 = (bf16[64,1536]{1,0:T(8,128)(2,1)S(1)}, bf16[64,1536]{1,0:T(8,128)(2,1)S(1)}, u32[]{:S(2)}, u32[]{:S(2)}) collective-permute-start(bf16[64,1536]{1,0:T(8,128)(2,1)S(1)} %pad_maximum_fusion.refs_0_), channel_id=1, source_target_pairs={{0,3},{1,0},{2,1},{3,2},{4,7},{5,4},{6,5},{7,6},{8,11},{9,8},{10,9... | collective-permute-start | bytes 589832 | tf_op jit(solution)/shard_map/ppermute | solution.py:196
  40.4 2.7 %collective-permute-done.2.refs_2_ = bf16[64,1536]{1,0:T(8,128)(2,1)S(1)} collective-permute-done((bf16[64,1536]{1,0:T(8,128)(2,1)S(1)}, bf16[64,1536]{1,0:T(8,128)(2,1)S(1)}, u32[]{:S(2)}, u32[]{:S(2)}) %collective-permute-start.2) | collective-permute-done | bytes 196640 | tf_op jit(solution)/shard_map/ppermute | solution.py:196
  43.1 1.6 %collective-permute-done.3.refs_3_ = bf16[64,1536]{1,0:T(8,128)(2,1)S(1)} collective-permute-done((bf16[64,1536]{1,0:T(8,128)(2,1)S(1)}, bf16[64,1536]{1,0:T(8,128)(2,1)S(1)}, u32[]{:S(2)}, u32[]{:S(2)}) %collective-permute-start.3) | collective-permute-done | bytes 196640 | tf_op jit(solution)/shard_map/ppermute | solution.py:196
  44.8 1.4 %shard_map.80 = (bf16[128,768]{1,0:T(8,128)(2,1)S(1)}, bf16[128,768]{1,0:T(8,128)(2,1)S(1)}) custom-call(s32[5]{0:T(128)S(1)} %stack.20.at, bf16[1536,768]{1,0:T(8,128)(2,1)S(1)} %copy-done, bf16[64,1536]{1,0:T(8,128)(2,1)S(1)} %pad_maximum_fusion.refs_0_, bf16[64,1536]{1,0:T(8,128)(2,1)S(1)} %collective-permute-done.1.refs_1_, ...), custom_call_target="tpu_custom_call" | custom-call | flops 603979776 | bytes 3538964 | tf_op jit(solution)/shard_map/pallas_call | solution.py:21
  46.1 4.5 %collective-permute-start.4 = (bf16[128,768]{1,0:T(8,128)(2,1)S(1)}, bf16[128,768]{1,0:T(8,128)(2,1)S(1)}, u32[]{:S(2)}, u32[]{:S(2)}) collective-permute-start(bf16[128,768]{1,0:T(8,128)(2,1)S(1)} %get-tuple-element.16), channel_id=1, source_target_pairs={{0,128},{128,0},{256,384},{384,256},{1,129},{129,1},{257,385},{385... | collective-permute-start | bytes 589832 | tf_op jit(solution)/shard_map/ppermute | solution.py:217
  50.7 0.8 shard_map.78.side_ref
  51.4 1.3 %shard_map.79 = bf16[4,8,160,128]{3,2,1,0:T(8,128)(2,1)} custom-call(bf16[16,120,128]{2,1,0:T(8,128)(2,1)S(1)} %all-to-all-done.got_ref, bf16[8,32,128]{2,1,0:T(8,128)(2,1)S(1)} %shard_map.78.side_ref), custom_call_target="tpu_custom_call" | custom-call | flops 1000000 | bytes 1867776 | tf_op jit(solution)/shard_map/pallas_call | solution.py:21
  52.7 6.6 %all-to-all-start.1 = ((bf16[32,160,128]{2,1,0:T(8,128)(2,1)}), bf16[32,160,128]{2,1,0:T(8,128)(2,1)S(1)}, u32[]{:S(2)}, u32[]{:S(2)}) async-start(bf16[32,160,128]{2,1,0:T(8,128)(2,1)} %bitcast.4), calls=%async_computation.1 | async-start | bytes 2621440 | tf_op jit(solution)/shard_map/all_to_all | solution.py:238
  59.4 4.8 %collective-permute-start.5 = (bf16[64,768]{1,0:T(8,128)(2,1)S(1)}, bf16[64,768]{1,0:T(8,128)(2,1)S(1)}, u32[]{:S(2)}, u32[]{:S(2)}) collective-permute-start(bf16[64,768]{1,0:T(8,128)(2,1)S(1)} %slice.35), channel_id=1, source_target_pairs={{0,256},{128,384},{256,0},{384,128},{1,257},{129,385},{257,1},{385... | collective-permute-start | bytes 294920 | tf_op jit(solution)/shard_map/ppermute | solution.py:220
  64.2 15.0 %collective-permute-done.5 = bf16[64,768]{1,0:T(8,128)(2,1)S(1)} collective-permute-done((bf16[64,768]{1,0:T(8,128)(2,1)S(1)}, bf16[64,768]{1,0:T(8,128)(2,1)S(1)}, u32[]{:S(2)}, u32[]{:S(2)}) %collective-permute-start.5) | collective-permute-done | bytes 98336 | tf_op jit(solution)/shard_map/ppermute | solution.py:220
  79.3 3.3 %collective-permute-start.6 = (bf16[64,768]{1,0:T(8,128)(2,1)S(1)}, bf16[64,768]{1,0:T(8,128)(2,1)S(1)}, u32[]{:S(2)}, u32[]{:S(2)}) collective-permute-start(bf16[64,768]{1,0:T(8,128)(2,1)S(1)} %fusion.refs_0_), channel_id=1, source_target_pairs={{0,8},{8,16},{16,24},{24,0},{32,40},{40,48},{48,56},{56,32},{64,72... | collective-permute-start | bytes 294920 | tf_op jit(solution)/shard_map/ppermute | solution.py:241
  82.5 3.1 %collective-permute-start.9 = (bf16[64,1536]{1,0:T(8,128)(2,1)S(1)}, bf16[64,1536]{1,0:T(8,128)(2,1)S(1)}, u32[]{:S(2)}, u32[]{:S(2)}) collective-permute-start(bf16[64,1536]{1,0:T(8,128)(2,1)S(1)} %constant_dynamic-update-slice_fusion.refs_0_), channel_id=1, source_target_pairs={{0,1},{1,2},{2,3},{3,0},{4,5},{5,6},{6,7},{7,4},{8,9},{9,10},{10,1... | collective-permute-start | bytes 589832 | tf_op jit(solution)/shard_map/ppermute | solution.py:196
  85.6 4.3 %collective-permute-start.10 = (bf16[64,1536]{1,0:T(8,128)(2,1)S(1)}, bf16[64,1536]{1,0:T(8,128)(2,1)S(1)}, u32[]{:S(2)}, u32[]{:S(2)}) collective-permute-start(bf16[64,1536]{1,0:T(8,128)(2,1)S(1)} %constant_dynamic-update-slice_fusion.refs_0_), channel_id=1, source_target_pairs={{0,2},{1,3},{2,0},{3,1},{4,6},{5,7},{6,4},{7,5},{8,10},{9,11},{10,... | collective-permute-start | bytes 589832 | tf_op jit(solution)/shard_map/ppermute | solution.py:196
  90.0 3.1 %collective-permute-start.11 = (bf16[64,1536]{1,0:T(8,128)(2,1)S(1)}, bf16[64,1536]{1,0:T(8,128)(2,1)S(1)}, u32[]{:S(2)}, u32[]{:S(2)}) collective-permute-start(bf16[64,1536]{1,0:T(8,128)(2,1)S(1)} %constant_dynamic-update-slice_fusion.refs_0_), channel_id=1, source_target_pairs={{0,3},{1,0},{2,1},{3,2},{4,7},{5,4},{6,5},{7,6},{8,11},{9,8},{10,9... | collective-permute-start | bytes 589832 | tf_op jit(solution)/shard_map/ppermute | solution.py:196
  93.0 4.0 %collective-permute-start.7 = (bf16[64,768]{1,0:T(8,128)(2,1)S(1)}, bf16[64,768]{1,0:T(8,128)(2,1)S(1)}, u32[]{:S(2)}, u32[]{:S(2)}) collective-permute-start(bf16[64,768]{1,0:T(8,128)(2,1)S(1)} %fusion.refs_0_), channel_id=1, source_target_pairs={{0,16},{8,24},{16,0},{24,8},{32,48},{40,56},{48,32},{56,40},{64,80... | collective-permute-start | bytes 294920 | tf_op jit(solution)/shard_map/ppermute | solution.py:241
  97.1 3.1 %collective-permute-start.8 = (bf16[64,768]{1,0:T(8,128)(2,1)S(1)}, bf16[64,768]{1,0:T(8,128)(2,1)S(1)}, u32[]{:S(2)}, u32[]{:S(2)}) collective-permute-start(bf16[64,768]{1,0:T(8,128)(2,1)S(1)} %fusion.refs_0_), channel_id=1, source_target_pairs={{0,24},{8,0},{16,8},{24,16},{32,56},{40,32},{48,40},{56,48},{64,88... | collective-permute-start | bytes 294920 | tf_op jit(solution)/shard_map/ppermute | solution.py:241
  100.4 2.8 %collective-permute-done.8.refs_3_ = bf16[64,768]{1,0:T(8,128)(2,1)S(1)} collective-permute-done((bf16[64,768]{1,0:T(8,128)(2,1)S(1)}, bf16[64,768]{1,0:T(8,128)(2,1)S(1)}, u32[]{:S(2)}, u32[]{:S(2)}) %collective-permute-start.8) | collective-permute-done | bytes 98336 | tf_op jit(solution)/shard_map/ppermute | solution.py:241
  103.1 1.8 %shard_map.81 = bf16[4,96,768]{2,1,0:T(8,128)(2,1)} custom-call(s32[5]{0:T(128)S(1)} %stack.20.at, bf16[4,8,160,128]{3,2,1,0:T(8,128)(2,1)S(1)} %bitcast.6, bf16[64,768]{1,0:T(8,128)(2,1)S(1)} %fusion.refs_0_, bf16[64,768]{1,0:T(8,128)(2,1)S(1)} %collective-permute-done.6.refs_1_, bf16[64,768]{1,0:T(8,128)(2,1)S(1)} %collective-permute-done.7.refs_2_, ...), custom_call_target="tpu_custom_call" | custom-call | flops 201326592 | bytes 2293780 | tf_op jit(solution)/shard_map/pallas_call | solution.py:21
  105.0 6.1 %all-to-all-start.2 = ((bf16[4,96,768]{2,1,0:T(8,128)(2,1)}), bf16[4,96,768]{2,1,0:T(8,128)(2,1)S(1)}, u32[]{:S(2)}, u32[]{:S(2)}) async-start(bf16[4,96,768]{2,1,0:T(8,128)(2,1)} %shard_map.81), calls=%async_computation.2 | async-start | bytes 1179648 | tf_op jit(solution)/shard_map/all_to_all | solution.py:255
  111.1 1.7 %shard_map.82 = (f32[48,1536]{1,0:T(8,128)}, f32[48,1536]{1,0:T(8,128)}) custom-call(s32[5]{0:T(128)S(1)} %stack.20.at, bf16[4,8,160,128]{3,2,1,0:T(8,128)(2,1)S(1)} %bitcast.7, bf16[64,1536]{1,0:T(8,128)(2,1)S(1)} %constant_dynamic-update-slice_fusion.refs_0_, bf16[64,1536]{1,0:T(8,128)(2,1)S(1)} %collective-permute-done.9.refs_1_, ...), custom_call_target="tpu_custom_call" | custom-call | flops 201326592 | bytes 2686996 | tf_op jit(solution)/shard_map/pallas_call | solution.py:21
  112.9 8.5 %all-to-all-done.2 = bf16[4,96,768]{2,1,0:T(8,128)(2,1)S(1)} async-done(((bf16[4,96,768]{2,1,0:T(8,128)(2,1)}), bf16[4,96,768]{2,1,0:T(8,128)(2,1)S(1)}, u32[]{:S(2)}, u32[]{:S(2)}) %all-to-all-start.2) | async-done | bytes 589856 | tf_op jit(solution)/shard_map/all_to_all | solution.py:255
  121.3 0.8 convert_reduce_fusion
  (27 shorter events, 0.5 us)
Async XLA Ops:
  1.5 1.3 %copy-start.1 = (bf16[1536,384]{1,0:T(8,128)(2,1)S(1)}, bf16[1536,384]{1,0:T(8,128)(2,1)}, u32[]{:S(2)}) copy-start(bf16[1536,384]{1,0:T(8,128)(2,1)} %a_ref.1) | copy-start | bytes 3538948
  2.8 0.9 copy-start.3
  3.6 17.7 %copy-start.2 = (bf16[128,1536]{1,0:T(8,128)(2,1)S(1)}, bf16[128,1536]{1,0:T(8,128)(2,1)}, u32[]{:S(2)}) copy-start(bf16[128,1536]{1,0:T(8,128)(2,1)} %g_ref.1) | copy-start | bytes 1179652
  5.5 39.3 %copy-start = (bf16[1536,768]{1,0:T(8,128)(2,1)S(1)}, bf16[1536,768]{1,0:T(8,128)(2,1)}, u32[]{:S(2)}) copy-start(bf16[1536,768]{1,0:T(8,128)(2,1)} %b_ref.1) | copy-start | bytes 7077892
  5.5 46.0 %all-to-all-start = ((bf16[16,120,128]{2,1,0:T(8,128)(2,1)}), bf16[16,120,128]{2,1,0:T(8,128)(2,1)S(1)}, u32[]{:S(2)}, u32[]{:S(2)}) async-start(bf16[16,120,128]{2,1,0:T(8,128)(2,1)} %shard_map.76), calls=%async_computation | async-start | bytes 983040 | tf_op jit(solution)/shard_map/all_to_all | solution.py:193
  22.1 7.3 %collective-permute-start = (bf16[64,1536]{1,0:T(8,128)(2,1)S(1)}, bf16[64,1536]{1,0:T(8,128)(2,1)S(1)}, u32[]{:S(2)}, u32[]{:S(2)}) collective-permute-start(bf16[64,1536]{1,0:T(8,128)(2,1)S(1)} %shard_map.77.gy_ref), channel_id=1, source_target_pairs={{0,4},{1,5},{2,6},{3,7},{4,0},{5,1},{6,2},{7,3},{8,12},{9,13},{10,... | collective-permute-start | bytes 589832 | tf_op jit(solution)/shard_map/ppermute | solution.py:206
  29.5 21.2 %copy-start.4 = (bf16[128,384]{1,0:T(8,128)(2,1)S(1)}, bf16[128,384]{1,0:T(8,128)(2,1)}, u32[]{:S(2)}) copy-start(bf16[128,384]{1,0:T(8,128)(2,1)} %x_ref.3) | copy-start | bytes 294916
  29.5 10.9 %collective-permute-start.1 = (bf16[64,1536]{1,0:T(8,128)(2,1)S(1)}, bf16[64,1536]{1,0:T(8,128)(2,1)S(1)}, u32[]{:S(2)}, u32[]{:S(2)}) collective-permute-start(bf16[64,1536]{1,0:T(8,128)(2,1)S(1)} %pad_maximum_fusion.refs_0_), channel_id=1, source_target_pairs={{0,1},{1,2},{2,3},{3,0},{4,5},{5,6},{6,7},{7,4},{8,9},{9,10},{10,1... | collective-permute-start | bytes 589832 | tf_op jit(solution)/shard_map/ppermute | solution.py:196
  32.9 10.3 %collective-permute-start.2 = (bf16[64,1536]{1,0:T(8,128)(2,1)S(1)}, bf16[64,1536]{1,0:T(8,128)(2,1)S(1)}, u32[]{:S(2)}, u32[]{:S(2)}) collective-permute-start(bf16[64,1536]{1,0:T(8,128)(2,1)S(1)} %pad_maximum_fusion.refs_0_), channel_id=1, source_target_pairs={{0,2},{1,3},{2,0},{3,1},{4,6},{5,7},{6,4},{7,5},{8,10},{9,11},{10,... | collective-permute-start | bytes 589832 | tf_op jit(solution)/shard_map/ppermute | solution.py:196
  37.4 7.4 %collective-permute-start.3 = (bf16[64,1536]{1,0:T(8,128)(2,1)S(1)}, bf16[64,1536]{1,0:T(8,128)(2,1)S(1)}, u32[]{:S(2)}, u32[]{:S(2)}) collective-permute-start(bf16[64,1536]{1,0:T(8,128)(2,1)S(1)} %pad_maximum_fusion.refs_0_), channel_id=1, source_target_pairs={{0,3},{1,0},{2,1},{3,2},{4,7},{5,4},{6,5},{7,6},{8,11},{9,8},{10,9... | collective-permute-start | bytes 589832 | tf_op jit(solution)/shard_map/ppermute | solution.py:196
  46.1 13.2 %collective-permute-start.4 = (bf16[128,768]{1,0:T(8,128)(2,1)S(1)}, bf16[128,768]{1,0:T(8,128)(2,1)S(1)}, u32[]{:S(2)}, u32[]{:S(2)}) collective-permute-start(bf16[128,768]{1,0:T(8,128)(2,1)S(1)} %get-tuple-element.16), channel_id=1, source_target_pairs={{0,128},{128,0},{256,384},{384,256},{1,129},{129,1},{257,385},{385... | collective-permute-start | bytes 589832 | tf_op jit(solution)/shard_map/ppermute | solution.py:217
  52.7 50.4 %all-to-all-start.1 = ((bf16[32,160,128]{2,1,0:T(8,128)(2,1)}), bf16[32,160,128]{2,1,0:T(8,128)(2,1)S(1)}, u32[]{:S(2)}, u32[]{:S(2)}) async-start(bf16[32,160,128]{2,1,0:T(8,128)(2,1)} %bitcast.4), calls=%async_computation.1 | async-start | bytes 2621440 | tf_op jit(solution)/shard_map/all_to_all | solution.py:238
  59.4 19.9 %collective-permute-start.5 = (bf16[64,768]{1,0:T(8,128)(2,1)S(1)}, bf16[64,768]{1,0:T(8,128)(2,1)S(1)}, u32[]{:S(2)}, u32[]{:S(2)}) collective-permute-start(bf16[64,768]{1,0:T(8,128)(2,1)S(1)} %slice.35), channel_id=1, source_target_pairs={{0,256},{128,384},{256,0},{384,128},{1,257},{129,385},{257,1},{385... | collective-permute-start | bytes 294920 | tf_op jit(solution)/shard_map/ppermute | solution.py:220
  79.3 17.8 %collective-permute-start.6 = (bf16[64,768]{1,0:T(8,128)(2,1)S(1)}, bf16[64,768]{1,0:T(8,128)(2,1)S(1)}, u32[]{:S(2)}, u32[]{:S(2)}) collective-permute-start(bf16[64,768]{1,0:T(8,128)(2,1)S(1)} %fusion.refs_0_), channel_id=1, source_target_pairs={{0,8},{8,16},{16,24},{24,0},{32,40},{40,48},{48,56},{56,32},{64,72... | collective-permute-start | bytes 294920 | tf_op jit(solution)/shard_map/ppermute | solution.py:241
  82.5 22.4 %collective-permute-start.9 = (bf16[64,1536]{1,0:T(8,128)(2,1)S(1)}, bf16[64,1536]{1,0:T(8,128)(2,1)S(1)}, u32[]{:S(2)}, u32[]{:S(2)}) collective-permute-start(bf16[64,1536]{1,0:T(8,128)(2,1)S(1)} %constant_dynamic-update-slice_fusion.refs_0_), channel_id=1, source_target_pairs={{0,1},{1,2},{2,3},{3,0},{4,5},{5,6},{6,7},{7,4},{8,9},{9,10},{10,1... | collective-permute-start | bytes 589832 | tf_op jit(solution)/shard_map/ppermute | solution.py:196
  85.6 19.4 %collective-permute-start.10 = (bf16[64,1536]{1,0:T(8,128)(2,1)S(1)}, bf16[64,1536]{1,0:T(8,128)(2,1)S(1)}, u32[]{:S(2)}, u32[]{:S(2)}) collective-permute-start(bf16[64,1536]{1,0:T(8,128)(2,1)S(1)} %constant_dynamic-update-slice_fusion.refs_0_), channel_id=1, source_target_pairs={{0,2},{1,3},{2,0},{3,1},{4,6},{5,7},{6,4},{7,5},{8,10},{9,11},{10,... | collective-permute-start | bytes 589832 | tf_op jit(solution)/shard_map/ppermute | solution.py:196
  90.0 15.0 %collective-permute-start.11 = (bf16[64,1536]{1,0:T(8,128)(2,1)S(1)}, bf16[64,1536]{1,0:T(8,128)(2,1)S(1)}, u32[]{:S(2)}, u32[]{:S(2)}) collective-permute-start(bf16[64,1536]{1,0:T(8,128)(2,1)S(1)} %constant_dynamic-update-slice_fusion.refs_0_), channel_id=1, source_target_pairs={{0,3},{1,0},{2,1},{3,2},{4,7},{5,4},{6,5},{7,6},{8,11},{9,8},{10,9... | collective-permute-start | bytes 589832 | tf_op jit(solution)/shard_map/ppermute | solution.py:196
  93.0 7.3 %collective-permute-start.7 = (bf16[64,768]{1,0:T(8,128)(2,1)S(1)}, bf16[64,768]{1,0:T(8,128)(2,1)S(1)}, u32[]{:S(2)}, u32[]{:S(2)}) collective-permute-start(bf16[64,768]{1,0:T(8,128)(2,1)S(1)} %fusion.refs_0_), channel_id=1, source_target_pairs={{0,16},{8,24},{16,0},{24,8},{32,48},{40,56},{48,32},{56,40},{64,80... | collective-permute-start | bytes 294920 | tf_op jit(solution)/shard_map/ppermute | solution.py:241
  97.1 6.1 %collective-permute-start.8 = (bf16[64,768]{1,0:T(8,128)(2,1)S(1)}, bf16[64,768]{1,0:T(8,128)(2,1)S(1)}, u32[]{:S(2)}, u32[]{:S(2)}) collective-permute-start(bf16[64,768]{1,0:T(8,128)(2,1)S(1)} %fusion.refs_0_), channel_id=1, source_target_pairs={{0,24},{8,0},{16,8},{24,16},{32,56},{40,32},{48,40},{56,48},{64,88... | collective-permute-start | bytes 294920 | tf_op jit(solution)/shard_map/ppermute | solution.py:241
  105.0 16.3 %all-to-all-start.2 = ((bf16[4,96,768]{2,1,0:T(8,128)(2,1)}), bf16[4,96,768]{2,1,0:T(8,128)(2,1)S(1)}, u32[]{:S(2)}, u32[]{:S(2)}) async-start(bf16[4,96,768]{2,1,0:T(8,128)(2,1)} %shard_map.81), calls=%async_computation.2 | async-start | bytes 1179648 | tf_op jit(solution)/shard_map/all_to_all | solution.py:255

commit v7 on v6

--- a/solution.py
+++ b/solution.py
@@ -59,7 +59,7 @@
 def pick_kernel(at, picks, g_ref, out_ref):
     tok = g_ref.shape[0]
     samp = picks.shape[0]
-    ours = [32 * (i // 8) + 8 * at[1] + i % 8 for i in range(out_ref.shape[0] - samp)]
+    ours = [64 * (i // 16) + 16 * at[1] + i % 16 for i in range(out_ref.shape[0] - samp)]
     hot = rows_hot(ours + [picks[i] for i in range(samp)], tok)
     out_ref[...] = jnp.dot(hot, g_ref[...], preferred_element_type=F32).astype(BF)
 
@@ -82,15 +82,13 @@
 
 def right_kernel(at, b_ref, *refs):
     blocks, keep_ref, give_ref, held = refs[:-3], refs[-3], refs[-2], refs[-1]
-    n_blk, n_grp, size, width = held.shape
+    n_blk, unused, size, width = held.shape
     rows = jnp.concatenate([block[...] for block in blocks], axis=0)
     term = jnp.dot(rows, b_ref[...], preferred_element_type=F32)
     held[...] = term.reshape(held.shape)
-    half = n_blk * size
-    for x in range(n_grp):
-        piece = held[:, at[0] ^ x].reshape(half, width).astype(BF)
-        out = give_ref if x % 2 else keep_ref
-        out[(x // 2) * half : (x // 2 + 1) * half, :] = piece
+    core = at[0] % 2
+    keep_ref[...] = held[:, core].reshape(n_blk * size, width).astype(BF)
+    give_ref[...] = held[:, 1 - core].reshape(n_blk * size, width).astype(BF)
 
 
 def second_kernel(got_ref, side_ref, out_ref):
@@ -103,11 +101,11 @@
         total = total + got_ref[r, :out_rows, :].astype(F32)
     total = jnp.concatenate([total, jnp.zeros((LANES - out_rows, tok), F32)], axis=0)
     turned = jnp.transpose(total).astype(BF)
-    size = tok // n_grp
+    size = tok // 2
     per = n_row // n_grp
     x_rows = per * strip
     for g in range(n_grp):
-        u_block = turned[g * size : (g + 1) * size]
+        u_block = turned[(g % 2) * size : (g % 2 + 1) * size]
         x_block = got_ref[g * per : (g + 1) * per, out_rows:, :].astype(F32)
         x_block = x_block.reshape(x_rows, tok).astype(BF)
         for c in range(n_col):
@@ -177,7 +175,7 @@
     per = feat_grp // feat_row
     strip = quarter * feat_row // LANES
     spread = 4
-    size = tok // n_grp // spread
+    size = tok // 2 // spread
     shape = jax.ShapeDtypeStruct
 
     at = jnp.stack([grp, row % spread, row % per, col, row // per]).astype(jnp.int32)
@@ -200,27 +198,29 @@
     picked = call(
         pick_kernel,
         (at, offsets, cotangent),
-        [shape((n_grp * size + samp, feat_grp), BF)],
+        [shape((2 * size + samp, feat_grp), BF)],
         2 * 64 * tok * feat_grp,
     )[0]
     beside = lax.ppermute(picked, "col", [(i, (i + 4) % n_col) for i in range(n_col)])
-    cut = n_grp * size
+    cut = 2 * size
     pair = jnp.concatenate([picked[:cut], beside[:cut]], axis=0)
     pairs = [pair] + [along_y(pair, k) for k in range(1, 4)]
     keep, give = call(
         right_kernel,
         (at, grad_inverse, *pairs),
-        [shape((2 * n_col * size, width), BF)] * 2,
-        2 * n_col * n_grp * size * feat_grp * width,
-        [pltpu.VMEM((n_col, n_grp, size, width), F32)],
+        [shape((n_col * size, width), BF)] * 2,
+        4 * n_col * size * feat_grp * width,
+        [pltpu.VMEM((n_col, 2, size, width), F32)],
     )
     taken = lax.ppermute(give, "grp", [(i, i ^ 1) for i in range(n_grp)])
-    halves = keep.astype(F32) + taken.astype(F32)
-    half = n_col * size
-    taken = lax.ppermute(halves[half:].astype(BF), "grp", [(i, i ^ 2) for i in range(n_grp)])
-    right = (halves[:half] + taken.astype(F32)).astype(BF)
-
-    keep, picked_y, beside_y = lax.optimization_barrier((keep, picked[cut:], beside[cut:]))
+    right = (keep.astype(F32) + taken.astype(F32)).astype(BF)
+    rights = [right] + [
+        lax.ppermute(
+            right, "row", [(i, i - i % spread + (i + j) % spread) for i in range(n_row)]
+        )
+        for j in range(1, spread)
+    ]
+    rights, picked_y, beside_y = lax.optimization_barrier((rights, picked[cut:], beside[cut:]))
     samples = jnp.concatenate([picked_y, beside_y], axis=0)
     samples = [samples] + [along_y(samples, k) for k in range(1, 4)]
     side = call(
@@ -237,12 +237,6 @@
     )[0]
     got = lax.all_to_all(send.reshape((n_grp * n_col,) + send.shape[2:]), ("grp", "col"), 0, 0)
     got = got.reshape(send.shape)
-    rights = [right] + [
-        lax.ppermute(
-            right, "row", [(i, i - i % spread + (i + j) % spread) for i in range(n_row)]
-        )
-        for j in range(1, spread)
-    ]
 
     term = call(
         final_kernel,

time: 123 us -> 151 us (1.23)
  the two profiles are of different devices: /device:TPU:1 before, /device:TPU:32 now
where the time goes in v7:
time: 151 us; the launch traced here: 150 us
  waiting for transfers between devices  68.8 us (46%)
  starting transfers between devices  63.8 us (42%)
  Pallas kernels  9.95 us (7%)
  local copies, waits for them, and re-layouts  4.04 us (3%)
  other arithmetic  2.61 us (2%)
    ppermute x6, waiting for transfers between devices, along_y(): lax.ppermute(block, 'col', [(i, i - i % 4 + (i + k) % 4) for i in range(n...  23.2 us
    ppermute x6, starting transfers between devices, along_y(): lax.ppermute(block, 'col', [(i, i - i % 4 + (i + k) % 4) for i in range(n...  21.1 us
    all_to_all x1, waiting for transfers between devices, body(): first = lax.all_to_all(payload, 'row', 0, 0)  18.1 us
    all_to_all x1, starting transfers between devices, body(): first = lax.all_to_all(payload, 'row', 0, 0)  15.2 us
    ppermute x3, waiting for transfers between devices, body(): lax.ppermute(right, 'row', [(i, i - i % spread + (i + j) % spread) for i...  13 us
    ppermute x3, starting transfers between devices, body(): lax.ppermute(right, 'row', [(i, i - i % spread + (i + j) % spread) for i...  10.3 us
    pallas_call x7, Pallas kernels, call(): pl.pallas_call(kernel, out_shape=outs, in_specs=[SMEM if x.dtype == jnp.i...  9.95 us
    all_to_all x1, waiting for transfers between devices, body(): term = lax.all_to_all(term, 'grp', 0, 0)  9.41 us
  transfers between devices with their start and end apart: 14, of which 11 were waited for; matrix products, arithmetic and copies ran while one was open for 0% of the time, Pallas kernels for 5%

profile of v7, /device:TPU:32, one launch (start us, length us, event | category | flops | bytes accessed | tf_op | source)
XLA Modules:
  0.0 150.0 jit_solution(17752541768643253198)
XLA Ops:
  1.5 1.3 copy-done.1
  3.6 1.8 %shard_map.76 = bf16[16,120,128]{2,1,0:T(8,128)(2,1)} custom-call(s32[5]{0:T(128)S(1)} %stack.20.at, s32[8]{0:T(128)S(1)} %dynamic_slice.3.picks, bf16[128,384]{1,0:T(8,128)(2,1)S(1)} %copy-done.3, bf16[1536,384]{1,0:T(8,128)(2,1)S(1)} %copy-done.1), custom_call_target="tpu_custom_call" | custom-call | flops 150994944 | bytes 1769524 | tf_op jit(solution)/shard_map/pallas_call | solution.py:21
  5.5 15.2 %all-to-all-start = ((bf16[16,120,128]{2,1,0:T(8,128)(2,1)}), bf16[16,120,128]{2,1,0:T(8,128)(2,1)S(1)}, u32[]{:S(2)}, u32[]{:S(2)}) async-start(bf16[16,120,128]{2,1,0:T(8,128)(2,1)} %shard_map.76), calls=%async_computation | async-start | bytes 983040 | tf_op jit(solution)/shard_map/all_to_all | solution.py:191
  21.4 3.4 %collective-permute-start = (bf16[64,1536]{1,0:T(8,128)(2,1)S(1)}, bf16[64,1536]{1,0:T(8,128)(2,1)S(1)}, u32[]{:S(2)}, u32[]{:S(2)}) collective-permute-start(bf16[64,1536]{1,0:T(8,128)(2,1)S(1)} %shard_map.77.gy_ref), channel_id=1, source_target_pairs={{0,4},{1,5},{2,6},{3,7},{4,0},{5,1},{6,2},{7,3},{8,12},{9,13},{10,... | collective-permute-start | bytes 589832 | tf_op jit(solution)/shard_map/ppermute | solution.py:204
  25.6 3.8 %collective-permute-done = bf16[64,1536]{1,0:T(8,128)(2,1)S(1)} collective-permute-done((bf16[64,1536]{1,0:T(8,128)(2,1)S(1)}, bf16[64,1536]{1,0:T(8,128)(2,1)S(1)}, u32[]{:S(2)}, u32[]{:S(2)}) %collective-permute-start) | collective-permute-done | bytes 196640 | tf_op jit(solution)/shard_map/ppermute | solution.py:204
  29.4 18.1 %all-to-all-done.got_ref = bf16[16,120,128]{2,1,0:T(8,128)(2,1)S(1)} async-done(((bf16[16,120,128]{2,1,0:T(8,128)(2,1)}), bf16[16,120,128]{2,1,0:T(8,128)(2,1)S(1)}, u32[]{:S(2)}, u32[]{:S(2)}) %all-to-all-start) | async-done | bytes 491552 | tf_op jit(solution)/shard_map/all_to_all | solution.py:191
  47.5 1.4 shard_map.79
  48.9 7.3 %all-to-all-start.1 = ((bf16[32,192,128]{2,1,0:T(8,128)(2,1)}), bf16[32,192,128]{2,1,0:T(8,128)(2,1)S(1)}, u32[]{:S(2)}, u32[]{:S(2)}) async-start(bf16[32,192,128]{2,1,0:T(8,128)(2,1)} %bitcast.4), calls=%async_computation.1 | async-start | bytes 3145728 | tf_op jit(solution)/shard_map/all_to_all | solution.py:238
  56.3 3.7 %collective-permute-start.1 = (bf16[64,1536]{1,0:T(8,128)(2,1)S(1)}, bf16[64,1536]{1,0:T(8,128)(2,1)S(1)}, u32[]{:S(2)}, u32[]{:S(2)}) collective-permute-start(bf16[64,1536]{1,0:T(8,128)(2,1)S(1)} %pad_maximum_fusion.refs_0_), channel_id=1, source_target_pairs={{0,1},{1,2},{2,3},{3,0},{4,5},{5,6},{6,7},{7,4},{8,9},{9,10},{10,1... | collective-permute-start | bytes 589832 | tf_op jit(solution)/shard_map/ppermute | solution.py:194
  60.0 4.6 %collective-permute-start.2 = (bf16[64,1536]{1,0:T(8,128)(2,1)S(1)}, bf16[64,1536]{1,0:T(8,128)(2,1)S(1)}, u32[]{:S(2)}, u32[]{:S(2)}) collective-permute-start(bf16[64,1536]{1,0:T(8,128)(2,1)S(1)} %pad_maximum_fusion.refs_0_), channel_id=1, source_target_pairs={{0,2},{1,3},{2,0},{3,1},{4,6},{5,7},{6,4},{7,5},{8,10},{9,11},{10,... | collective-permute-start | bytes 589832 | tf_op jit(solution)/shard_map/ppermute | solution.py:194
  64.5 3.4 %collective-permute-start.3 = (bf16[64,1536]{1,0:T(8,128)(2,1)S(1)}, bf16[64,1536]{1,0:T(8,128)(2,1)S(1)}, u32[]{:S(2)}, u32[]{:S(2)}) collective-permute-start(bf16[64,1536]{1,0:T(8,128)(2,1)S(1)} %pad_maximum_fusion.refs_0_), channel_id=1, source_target_pairs={{0,3},{1,0},{2,1},{3,2},{4,7},{5,4},{6,5},{7,6},{8,11},{9,8},{10,9... | collective-permute-start | bytes 589832 | tf_op jit(solution)/shard_map/ppermute | solution.py:194
  67.9 13.6 %collective-permute-done.1.refs_1_ = bf16[64,1536]{1,0:T(8,128)(2,1)S(1)} collective-permute-done((bf16[64,1536]{1,0:T(8,128)(2,1)S(1)}, bf16[64,1536]{1,0:T(8,128)(2,1)S(1)}, u32[]{:S(2)}, u32[]{:S(2)}) %collective-permute-start.1) | collective-permute-done | bytes 196640 | tf_op jit(solution)/shard_map/ppermute | solution.py:194
  81.6 4.3 %collective-permute-done.2.refs_2_ = bf16[64,1536]{1,0:T(8,128)(2,1)S(1)} collective-permute-done((bf16[64,1536]{1,0:T(8,128)(2,1)S(1)}, bf16[64,1536]{1,0:T(8,128)(2,1)S(1)}, u32[]{:S(2)}, u32[]{:S(2)}) %collective-permute-start.2) | collective-permute-done | bytes 196640 | tf_op jit(solution)/shard_map/ppermute | solution.py:194
  86.0 1.7 %copy-done = bf16[1536,768]{1,0:T(8,128)(2,1)S(1)} copy-done((bf16[1536,768]{1,0:T(8,128)(2,1)S(1)}, bf16[1536,768]{1,0:T(8,128)(2,1)}, u32[]{:S(2)}) %copy-start) | copy-done | bytes 2359320
  87.7 1.4 shard_map.80
  89.1 1.9 %collective-permute-start.4 = (bf16[128,768]{1,0:T(8,128)(2,1)S(1)}, bf16[128,768]{1,0:T(8,128)(2,1)S(1)}, u32[]{:S(2)}, u32[]{:S(2)}) collective-permute-start(bf16[128,768]{1,0:T(8,128)(2,1)S(1)} %get-tuple-element.20), channel_id=1, source_target_pairs={{0,128},{128,0},{256,384},{384,256},{1,129},{129,1},{257,385},{385... | collective-permute-start | bytes 589832 | tf_op jit(solution)/shard_map/ppermute | solution.py:215
  91.0 1.4 collective-permute-done.4
  92.5 2.5 %collective-permute-start.5 = (bf16[128,768]{1,0:T(8,128)(2,1)S(1)}, bf16[128,768]{1,0:T(8,128)(2,1)S(1)}, u32[]{:S(2)}, u32[]{:S(2)}) collective-permute-start(bf16[128,768]{1,0:T(8,128)(2,1)S(1)} %add_convert_fusion.refs_0_), channel_id=1, source_target_pairs={{0,8},{8,16},{16,24},{24,0},{32,40},{40,48},{48,56},{56,32},{64,72... | collective-permute-start | bytes 589832 | tf_op jit(solution)/shard_map/ppermute | solution.py:218
  95.0 5.1 %collective-permute-start.6 = (bf16[128,768]{1,0:T(8,128)(2,1)S(1)}, bf16[128,768]{1,0:T(8,128)(2,1)S(1)}, u32[]{:S(2)}, u32[]{:S(2)}) collective-permute-start(bf16[128,768]{1,0:T(8,128)(2,1)S(1)} %add_convert_fusion.refs_0_), channel_id=1, source_target_pairs={{0,16},{8,24},{16,0},{24,8},{32,48},{40,56},{48,32},{56,40},{64,80... | collective-permute-start | bytes 589832 | tf_op jit(solution)/shard_map/ppermute | solution.py:218
  100.1 2.7 %collective-permute-start.7 = (bf16[128,768]{1,0:T(8,128)(2,1)S(1)}, bf16[128,768]{1,0:T(8,128)(2,1)S(1)}, u32[]{:S(2)}, u32[]{:S(2)}) collective-permute-start(bf16[128,768]{1,0:T(8,128)(2,1)S(1)} %add_convert_fusion.refs_0_), channel_id=1, source_target_pairs={{0,24},{8,0},{16,8},{24,16},{32,56},{40,32},{48,40},{56,48},{64,88... | collective-permute-start | bytes 589832 | tf_op jit(solution)/shard_map/ppermute | solution.py:218
  102.8 9.9 %collective-permute-done.6.refs_2_ = bf16[128,768]{1,0:T(8,128)(2,1)S(1)} collective-permute-done((bf16[128,768]{1,0:T(8,128)(2,1)S(1)}, bf16[128,768]{1,0:T(8,128)(2,1)S(1)}, u32[]{:S(2)}, u32[]{:S(2)}) %collective-permute-start.6) | collective-permute-done | bytes 196640 | tf_op jit(solution)/shard_map/ppermute | solution.py:218
  112.7 3.1 %collective-permute-done.7.refs_3_ = bf16[128,768]{1,0:T(8,128)(2,1)S(1)} collective-permute-done((bf16[128,768]{1,0:T(8,128)(2,1)S(1)}, bf16[128,768]{1,0:T(8,128)(2,1)S(1)}, u32[]{:S(2)}, u32[]{:S(2)}) %collective-permute-start.7) | collective-permute-done | bytes 196640 | tf_op jit(solution)/shard_map/ppermute | solution.py:218
  115.8 1.9 %collective-permute-start.8 = (bf16[64,1536]{1,0:T(8,128)(2,1)S(1)}, bf16[64,1536]{1,0:T(8,128)(2,1)S(1)}, u32[]{:S(2)}, u32[]{:S(2)}) collective-permute-start(bf16[64,1536]{1,0:T(8,128)(2,1)S(1)} %constant_dynamic-update-slice_fusion.refs_0_), channel_id=1, source_target_pairs={{0,1},{1,2},{2,3},{3,0},{4,5},{5,6},{6,7},{7,4},{8,9},{9,10},{10,1... | collective-permute-start | bytes 589832 | tf_op jit(solution)/shard_map/ppermute | solution.py:194
  117.7 5.0 %collective-permute-start.9 = (bf16[64,1536]{1,0:T(8,128)(2,1)S(1)}, bf16[64,1536]{1,0:T(8,128)(2,1)S(1)}, u32[]{:S(2)}, u32[]{:S(2)}) collective-permute-start(bf16[64,1536]{1,0:T(8,128)(2,1)S(1)} %constant_dynamic-update-slice_fusion.refs_0_), channel_id=1, source_target_pairs={{0,2},{1,3},{2,0},{3,1},{4,6},{5,7},{6,4},{7,5},{8,10},{9,11},{10,... | collective-permute-start | bytes 589832 | tf_op jit(solution)/shard_map/ppermute | solution.py:194
  122.7 2.5 %collective-permute-start.10 = (bf16[64,1536]{1,0:T(8,128)(2,1)S(1)}, bf16[64,1536]{1,0:T(8,128)(2,1)S(1)}, u32[]{:S(2)}, u32[]{:S(2)}) collective-permute-start(bf16[64,1536]{1,0:T(8,128)(2,1)S(1)} %constant_dynamic-update-slice_fusion.refs_0_), channel_id=1, source_target_pairs={{0,3},{1,0},{2,1},{3,2},{4,7},{5,4},{6,5},{7,6},{8,11},{9,8},{10,9... | collective-permute-start | bytes 589832 | tf_op jit(solution)/shard_map/ppermute | solution.py:194
  125.3 2.1 %shard_map.81 = bf16[4,96,768]{2,1,0:T(8,128)(2,1)} custom-call(s32[5]{0:T(128)S(1)} %stack.20.at, bf16[4,8,192,128]{3,2,1,0:T(8,128)(2,1)S(1)} %bitcast.6, bf16[128,768]{1,0:T(8,128)(2,1)S(1)} %add_convert_fusion.refs_0_, bf16[128,768]{1,0:T(8,128)(2,1)S(1)} %collective-permute-done.5.refs_1_, bf16[128,768]{1,0:T(8,128)(2,1)S(1)} %collective-permute-done.6.refs_2_, ...), custom_call_target="tpu_custom_call" | custom-call | flops 402653184 | bytes 2949140 | tf_op jit(solution)/shard_map/pallas_call | solution.py:21
  127.4 2.6 %collective-permute-done.8.refs_1_ = bf16[64,1536]{1,0:T(8,128)(2,1)S(1)} collective-permute-done((bf16[64,1536]{1,0:T(8,128)(2,1)S(1)}, bf16[64,1536]{1,0:T(8,128)(2,1)S(1)}, u32[]{:S(2)}, u32[]{:S(2)}) %collective-permute-start.8) | collective-permute-done | bytes 196640 | tf_op jit(solution)/shard_map/ppermute | solution.py:194
  129.9 2.5 %collective-permute-done.10.refs_3_ = bf16[64,1536]{1,0:T(8,128)(2,1)S(1)} collective-permute-done((bf16[64,1536]{1,0:T(8,128)(2,1)S(1)}, bf16[64,1536]{1,0:T(8,128)(2,1)S(1)}, u32[]{:S(2)}, u32[]{:S(2)}) %collective-permute-start.10) | collective-permute-done | bytes 196640 | tf_op jit(solution)/shard_map/ppermute | solution.py:194
  132.4 4.6 %all-to-all-start.2 = ((bf16[4,96,768]{2,1,0:T(8,128)(2,1)}), bf16[4,96,768]{2,1,0:T(8,128)(2,1)}, u32[]{:S(2)}, u32[]{:S(2)}) async-start(bf16[4,96,768]{2,1,0:T(8,128)(2,1)} %shard_map.81), calls=%async_computation.2 | async-start | bytes 1179648 | tf_op jit(solution)/shard_map/all_to_all | solution.py:249
  137.0 1.8 %shard_map.82 = (f32[48,1536]{1,0:T(8,128)}, f32[48,1536]{1,0:T(8,128)}) custom-call(s32[5]{0:T(128)S(1)} %stack.20.at, bf16[4,8,192,128]{3,2,1,0:T(8,128)(2,1)S(1)} %bitcast.7, bf16[64,1536]{1,0:T(8,128)(2,1)S(1)} %constant_dynamic-update-slice_fusion.refs_0_, bf16[64,1536]{1,0:T(8,128)(2,1)S(1)} %collective-permute-done.8.refs_1_, ...), custom_call_target="tpu_custom_call" | custom-call | flops 201326592 | bytes 2949140 | tf_op jit(solution)/shard_map/pallas_call | solution.py:21
  138.7 9.4 %all-to-all-done.2 = bf16[4,96,768]{2,1,0:T(8,128)(2,1)} async-done(((bf16[4,96,768]{2,1,0:T(8,128)(2,1)}), bf16[4,96,768]{2,1,0:T(8,128)(2,1)}, u32[]{:S(2)}, u32[]{:S(2)}) %all-to-all-start.2) | async-done | bytes 589856 | tf_op jit(solution)/shard_map/all_to_all | solution.py:249
  148.2 1.9 %convert_reduce_fusion = f32[96,768]{1,0:T(8,128)} fusion(bf16[4,96,768]{2,1,0:T(8,128)(2,1)} %all-to-all-done.2), kind=kLoop, calls=%fused_computation | loop fusion | flops 516096 | bytes 884736 | tf_op jit(solution)/shard_map/reduce_sum | solution.py:250
  (23 shorter events, 3.5 us)
Async XLA Ops:
  1.5 1.3 copy-start.1
  2.8 0.9 copy-start.3
  3.6 17.0 %copy-start.2 = (bf16[128,1536]{1,0:T(8,128)(2,1)S(1)}, bf16[128,1536]{1,0:T(8,128)(2,1)}, u32[]{:S(2)}) copy-start(bf16[128,1536]{1,0:T(8,128)(2,1)} %g_ref.1) | copy-start | bytes 1179652
  3.6 21.2 %copy-start.4 = (bf16[128,384]{1,0:T(8,128)(2,1)S(1)}, bf16[128,384]{1,0:T(8,128)(2,1)}, u32[]{:S(2)}) copy-start(bf16[128,384]{1,0:T(8,128)(2,1)} %x_ref.3) | copy-start | bytes 294916
  5.5 42.0 %all-to-all-start = ((bf16[16,120,128]{2,1,0:T(8,128)(2,1)}), bf16[16,120,128]{2,1,0:T(8,128)(2,1)S(1)}, u32[]{:S(2)}, u32[]{:S(2)}) async-start(bf16[16,120,128]{2,1,0:T(8,128)(2,1)} %shard_map.76), calls=%async_computation | async-start | bytes 983040 | tf_op jit(solution)/shard_map/all_to_all | solution.py:191
  21.4 8.0 %collective-permute-start = (bf16[64,1536]{1,0:T(8,128)(2,1)S(1)}, bf16[64,1536]{1,0:T(8,128)(2,1)S(1)}, u32[]{:S(2)}, u32[]{:S(2)}) collective-permute-start(bf16[64,1536]{1,0:T(8,128)(2,1)S(1)} %shard_map.77.gy_ref), channel_id=1, source_target_pairs={{0,4},{1,5},{2,6},{3,7},{4,0},{5,1},{6,2},{7,3},{8,12},{9,13},{10,... | collective-permute-start | bytes 589832 | tf_op jit(solution)/shard_map/ppermute | solution.py:204
  48.9 76.4 %all-to-all-start.1 = ((bf16[32,192,128]{2,1,0:T(8,128)(2,1)}), bf16[32,192,128]{2,1,0:T(8,128)(2,1)S(1)}, u32[]{:S(2)}, u32[]{:S(2)}) async-start(bf16[32,192,128]{2,1,0:T(8,128)(2,1)} %bitcast.4), calls=%async_computation.1 | async-start | bytes 3145728 | tf_op jit(solution)/shard_map/all_to_all | solution.py:238
  56.3 25.3 %collective-permute-start.1 = (bf16[64,1536]{1,0:T(8,128)(2,1)S(1)}, bf16[64,1536]{1,0:T(8,128)(2,1)S(1)}, u32[]{:S(2)}, u32[]{:S(2)}) collective-permute-start(bf16[64,1536]{1,0:T(8,128)(2,1)S(1)} %pad_maximum_fusion.refs_0_), channel_id=1, source_target_pairs={{0,1},{1,2},{2,3},{3,0},{4,5},{5,6},{6,7},{7,4},{8,9},{9,10},{10,1... | collective-permute-start | bytes 589832 | tf_op jit(solution)/shard_map/ppermute | solution.py:194
  60.0 25.9 %collective-permute-start.2 = (bf16[64,1536]{1,0:T(8,128)(2,1)S(1)}, bf16[64,1536]{1,0:T(8,128)(2,1)S(1)}, u32[]{:S(2)}, u32[]{:S(2)}) collective-permute-start(bf16[64,1536]{1,0:T(8,128)(2,1)S(1)} %pad_maximum_fusion.refs_0_), channel_id=1, source_target_pairs={{0,2},{1,3},{2,0},{3,1},{4,6},{5,7},{6,4},{7,5},{8,10},{9,11},{10,... | collective-permute-start | bytes 589832 | tf_op jit(solution)/shard_map/ppermute | solution.py:194
  64.5 21.5 %collective-permute-start.3 = (bf16[64,1536]{1,0:T(8,128)(2,1)S(1)}, bf16[64,1536]{1,0:T(8,128)(2,1)S(1)}, u32[]{:S(2)}, u32[]{:S(2)}) collective-permute-start(bf16[64,1536]{1,0:T(8,128)(2,1)S(1)} %pad_maximum_fusion.refs_0_), channel_id=1, source_target_pairs={{0,3},{1,0},{2,1},{3,2},{4,7},{5,4},{6,5},{7,6},{8,11},{9,8},{10,9... | collective-permute-start | bytes 589832 | tf_op jit(solution)/shard_map/ppermute | solution.py:194
  86.0 1.7 %copy-start = (bf16[1536,768]{1,0:T(8,128)(2,1)S(1)}, bf16[1536,768]{1,0:T(8,128)(2,1)}, u32[]{:S(2)}) copy-start(bf16[1536,768]{1,0:T(8,128)(2,1)} %b_ref.1) | copy-start | bytes 7077892
  89.1 3.3 %collective-permute-start.4 = (bf16[128,768]{1,0:T(8,128)(2,1)S(1)}, bf16[128,768]{1,0:T(8,128)(2,1)S(1)}, u32[]{:S(2)}, u32[]{:S(2)}) collective-permute-start(bf16[128,768]{1,0:T(8,128)(2,1)S(1)} %get-tuple-element.20), channel_id=1, source_target_pairs={{0,128},{128,0},{256,384},{384,256},{1,129},{129,1},{257,385},{385... | collective-permute-start | bytes 589832 | tf_op jit(solution)/shard_map/ppermute | solution.py:215
  92.5 10.3 %collective-permute-start.5 = (bf16[128,768]{1,0:T(8,128)(2,1)S(1)}, bf16[128,768]{1,0:T(8,128)(2,1)S(1)}, u32[]{:S(2)}, u32[]{:S(2)}) collective-permute-start(bf16[128,768]{1,0:T(8,128)(2,1)S(1)} %add_convert_fusion.refs_0_), channel_id=1, source_target_pairs={{0,8},{8,16},{16,24},{24,0},{32,40},{40,48},{48,56},{56,32},{64,72... | collective-permute-start | bytes 589832 | tf_op jit(solution)/shard_map/ppermute | solution.py:218
  95.0 17.7 %collective-permute-start.6 = (bf16[128,768]{1,0:T(8,128)(2,1)S(1)}, bf16[128,768]{1,0:T(8,128)(2,1)S(1)}, u32[]{:S(2)}, u32[]{:S(2)}) collective-permute-start(bf16[128,768]{1,0:T(8,128)(2,1)S(1)} %add_convert_fusion.refs_0_), channel_id=1, source_target_pairs={{0,16},{8,24},{16,0},{24,8},{32,48},{40,56},{48,32},{56,40},{64,80... | collective-permute-start | bytes 589832 | tf_op jit(solution)/shard_map/ppermute | solution.py:218
  100.1 15.7 %collective-permute-start.7 = (bf16[128,768]{1,0:T(8,128)(2,1)S(1)}, bf16[128,768]{1,0:T(8,128)(2,1)S(1)}, u32[]{:S(2)}, u32[]{:S(2)}) collective-permute-start(bf16[128,768]{1,0:T(8,128)(2,1)S(1)} %add_convert_fusion.refs_0_), channel_id=1, source_target_pairs={{0,24},{8,0},{16,8},{24,16},{32,56},{40,32},{48,40},{56,48},{64,88... | collective-permute-start | bytes 589832 | tf_op jit(solution)/shard_map/ppermute | solution.py:218
  115.8 14.1 %collective-permute-start.8 = (bf16[64,1536]{1,0:T(8,128)(2,1)S(1)}, bf16[64,1536]{1,0:T(8,128)(2,1)S(1)}, u32[]{:S(2)}, u32[]{:S(2)}) collective-permute-start(bf16[64,1536]{1,0:T(8,128)(2,1)S(1)} %constant_dynamic-update-slice_fusion.refs_0_), channel_id=1, source_target_pairs={{0,1},{1,2},{2,3},{3,0},{4,5},{5,6},{6,7},{7,4},{8,9},{9,10},{10,1... | collective-permute-start | bytes 589832 | tf_op jit(solution)/shard_map/ppermute | solution.py:194
  117.7 12.2 %collective-permute-start.9 = (bf16[64,1536]{1,0:T(8,128)(2,1)S(1)}, bf16[64,1536]{1,0:T(8,128)(2,1)S(1)}, u32[]{:S(2)}, u32[]{:S(2)}) collective-permute-start(bf16[64,1536]{1,0:T(8,128)(2,1)S(1)} %constant_dynamic-update-slice_fusion.refs_0_), channel_id=1, source_target_pairs={{0,2},{1,3},{2,0},{3,1},{4,6},{5,7},{6,4},{7,5},{8,10},{9,11},{10,... | collective-permute-start | bytes 589832 | tf_op jit(solution)/shard_map/ppermute | solution.py:194
  122.7 9.7 %collective-permute-start.10 = (bf16[64,1536]{1,0:T(8,128)(2,1)S(1)}, bf16[64,1536]{1,0:T(8,128)(2,1)S(1)}, u32[]{:S(2)}, u32[]{:S(2)}) collective-permute-start(bf16[64,1536]{1,0:T(8,128)(2,1)S(1)} %constant_dynamic-update-slice_fusion.refs_0_), channel_id=1, source_target_pairs={{0,3},{1,0},{2,1},{3,2},{4,7},{5,4},{6,5},{7,6},{8,11},{9,8},{10,9... | collective-permute-start | bytes 589832 | tf_op jit(solution)/shard_map/ppermute | solution.py:194
  132.4 15.7 %all-to-all-start.2 = ((bf16[4,96,768]{2,1,0:T(8,128)(2,1)}), bf16[4,96,768]{2,1,0:T(8,128)(2,1)}, u32[]{:S(2)}, u32[]{:S(2)}) async-start(bf16[4,96,768]{2,1,0:T(8,128)(2,1)} %shard_map.81), calls=%async_computation.2 | async-start | bytes 1179648 | tf_op jit(solution)/shard_map/all_to_all | solution.py:249

commit v8 on v7

--- a/solution.py
+++ b/solution.py
@@ -212,6 +212,7 @@
         4 * n_col * size * feat_grp * width,
         [pltpu.VMEM((n_col, 2, size, width), F32)],
     )
+    first, unused = lax.optimization_barrier((first, give))
     taken = lax.ppermute(give, "grp", [(i, i ^ 1) for i in range(n_grp)])
     right = (keep.astype(F32) + taken.astype(F32)).astype(BF)
     rights = [right] + [
@@ -245,7 +246,7 @@
         2 * n_grp * LANES * n_col * spread * size * width,
         [pltpu.VMEM((n_col, spread, size, width), F32)],
     )[0]
-    term, got, samples = lax.optimization_barrier((term, got, samples))
+    got, unused = lax.optimization_barrier((got, term))
     term = lax.all_to_all(term, "grp", 0, 0)
     precond = jnp.sum(term.astype(F32), axis=0)
     act_cov, grad_cov = call(

time: 151 us -> 111 us (0.74)
  the two profiles are of different devices: /device:TPU:32 before, /device:TPU:47 now
where the time goes in v8:
time: 111 us
  starting transfers between devices  63 us (57%)
  waiting for transfers between devices  32.9 us (30%)
  Pallas kernels  9.94 us (9%)
  local copies, waits for them, and re-layouts  2.38 us (2%)
  other arithmetic  1.51 us (1%)
    ppermute x6, starting transfers between devices, along_y(): lax.ppermute(block, 'col', [(i, i - i % 4 + (i + k) % 4) for i in range(n...  19.4 us
    all_to_all x1, starting transfers between devices, body(): first = lax.all_to_all(payload, 'row', 0, 0)  14.8 us
    ppermute x3, waiting for transfers between devices, body(): lax.ppermute(right, 'row', [(i, i - i % spread + (i + j) % spread) for i...  13.7 us
    ppermute x6, waiting for transfers between devices, along_y(): lax.ppermute(block, 'col', [(i, i - i % 4 + (i + k) % 4) for i in range(n...  13.5 us
    pallas_call x7, Pallas kernels, call(): pl.pallas_call(kernel, out_shape=outs, in_specs=[SMEM if x.dtype == jnp.i...  9.94 us
    all_to_all x1, starting transfers between devices, body(): lax.all_to_all(send.reshape((n_grp * n_col,) + send.shape[2:]), ('grp', '...  9.71 us
    ppermute x3, starting transfers between devices, body(): lax.ppermute(right, 'row', [(i, i - i % spread + (i + j) % spread) for i...  9.43 us
    all_to_all x1, starting transfers between devices, body(): term = lax.all_to_all(term, 'grp', 0, 0)  5 us
  transfers between devices with their start and end apart: 14, of which 8 were waited for; matrix products, arithmetic and copies ran while one was open for 0% of the time, Pallas kernels for 4%

profile of v8, /device:TPU:47, one launch (start us, length us, event | category | flops | bytes accessed | tf_op | source)
XLA Modules:
  0.0 110.6 jit_solution(6706069282184898406)
XLA Ops:
  1.5 1.3 %copy-done.1 = bf16[1536,384]{1,0:T(8,128)(2,1)S(1)} copy-done((bf16[1536,384]{1,0:T(8,128)(2,1)S(1)}, bf16[1536,384]{1,0:T(8,128)(2,1)}, u32[]{:S(2)}) %copy-start.1) | copy-done | bytes 1179672
  2.8 0.9 copy-done.3
  3.6 1.8 %shard_map.76 = bf16[16,120,128]{2,1,0:T(8,128)(2,1)} custom-call(s32[5]{0:T(128)S(1)} %stack.20.at, s32[8]{0:T(128)S(1)} %dynamic_slice.3.picks, bf16[128,384]{1,0:T(8,128)(2,1)S(1)} %copy-done.3, bf16[1536,384]{1,0:T(8,128)(2,1)S(1)} %copy-done.1), custom_call_target="tpu_custom_call" | custom-call | flops 150994944 | bytes 1769524 | tf_op jit(solution)/shard_map/pallas_call | solution.py:21
  5.5 14.8 %all-to-all-start = ((bf16[16,120,128]{2,1,0:T(8,128)(2,1)}), bf16[16,120,128]{2,1,0:T(8,128)(2,1)S(1)}, u32[]{:S(2)}, u32[]{:S(2)}) async-start(bf16[16,120,128]{2,1,0:T(8,128)(2,1)} %shard_map.76), calls=%async_computation | async-start | bytes 983040 | tf_op jit(solution)/shard_map/all_to_all | solution.py:191
  20.3 0.7 shard_map.77.gy_ref
  21.0 2.5 %collective-permute-start = (bf16[64,1536]{1,0:T(8,128)(2,1)S(1)}, bf16[64,1536]{1,0:T(8,128)(2,1)S(1)}, u32[]{:S(2)}, u32[]{:S(2)}) collective-permute-start(bf16[64,1536]{1,0:T(8,128)(2,1)S(1)} %shard_map.77.gy_ref), channel_id=1, source_target_pairs={{0,4},{1,5},{2,6},{3,7},{4,0},{5,1},{6,2},{7,3},{8,12},{9,13},{10,... | collective-permute-start | bytes 589832 | tf_op jit(solution)/shard_map/ppermute | solution.py:204
  23.5 4.6 %collective-permute-done = bf16[64,1536]{1,0:T(8,128)(2,1)S(1)} collective-permute-done((bf16[64,1536]{1,0:T(8,128)(2,1)S(1)}, bf16[64,1536]{1,0:T(8,128)(2,1)S(1)}, u32[]{:S(2)}, u32[]{:S(2)}) %collective-permute-start) | collective-permute-done | bytes 196640 | tf_op jit(solution)/shard_map/ppermute | solution.py:204
  28.1 3.2 %collective-permute-start.1 = (bf16[64,1536]{1,0:T(8,128)(2,1)S(1)}, bf16[64,1536]{1,0:T(8,128)(2,1)S(1)}, u32[]{:S(2)}, u32[]{:S(2)}) collective-permute-start(bf16[64,1536]{1,0:T(8,128)(2,1)S(1)} %pad_maximum_fusion.refs_0_), channel_id=1, source_target_pairs={{0,1},{1,2},{2,3},{3,0},{4,5},{5,6},{6,7},{7,4},{8,9},{9,10},{10,1... | collective-permute-start | bytes 589832 | tf_op jit(solution)/shard_map/ppermute | solution.py:194
  31.3 2.6 %collective-permute-start.2 = (bf16[64,1536]{1,0:T(8,128)(2,1)S(1)}, bf16[64,1536]{1,0:T(8,128)(2,1)S(1)}, u32[]{:S(2)}, u32[]{:S(2)}) collective-permute-start(bf16[64,1536]{1,0:T(8,128)(2,1)S(1)} %pad_maximum_fusion.refs_0_), channel_id=1, source_target_pairs={{0,2},{1,3},{2,0},{3,1},{4,6},{5,7},{6,4},{7,5},{8,10},{9,11},{10,... | collective-permute-start | bytes 589832 | tf_op jit(solution)/shard_map/ppermute | solution.py:194
  34.0 4.0 %collective-permute-start.3 = (bf16[64,1536]{1,0:T(8,128)(2,1)S(1)}, bf16[64,1536]{1,0:T(8,128)(2,1)S(1)}, u32[]{:S(2)}, u32[]{:S(2)}) collective-permute-start(bf16[64,1536]{1,0:T(8,128)(2,1)S(1)} %pad_maximum_fusion.refs_0_), channel_id=1, source_target_pairs={{0,3},{1,0},{2,1},{3,2},{4,7},{5,4},{6,5},{7,6},{8,11},{9,8},{10,9... | collective-permute-start | bytes 589832 | tf_op jit(solution)/shard_map/ppermute | solution.py:194
  37.9 0.8 shard_map.79.side_ref
  38.7 0.8 collective-permute-done.2.refs_2_
  39.5 4.8 %collective-permute-done.3.refs_3_ = bf16[64,1536]{1,0:T(8,128)(2,1)S(1)} collective-permute-done((bf16[64,1536]{1,0:T(8,128)(2,1)S(1)}, bf16[64,1536]{1,0:T(8,128)(2,1)S(1)}, u32[]{:S(2)}, u32[]{:S(2)}) %collective-permute-start.3) | collective-permute-done | bytes 196640 | tf_op jit(solution)/shard_map/ppermute | solution.py:194
  44.3 1.4 %shard_map.78 = (bf16[128,768]{1,0:T(8,128)(2,1)S(1)}, bf16[128,768]{1,0:T(8,128)(2,1)S(1)}) custom-call(s32[5]{0:T(128)S(1)} %stack.20.at, bf16[1536,768]{1,0:T(8,128)(2,1)S(1)} %copy-done, bf16[64,1536]{1,0:T(8,128)(2,1)S(1)} %pad_maximum_fusion.refs_0_, bf16[64,1536]{1,0:T(8,128)(2,1)S(1)} %collective-permute-done.1.refs_1_, ...), custom_call_target="tpu_custom_call" | custom-call | flops 603979776 | bytes 3538964 | tf_op jit(solution)/shard_map/pallas_call | solution.py:21
  45.7 1.4 %shard_map.80 = bf16[4,8,192,128]{3,2,1,0:T(8,128)(2,1)} custom-call(bf16[16,120,128]{2,1,0:T(8,128)(2,1)S(1)} %all-to-all-done.got_ref, bf16[8,32,128]{2,1,0:T(8,128)(2,1)S(1)} %shard_map.79.side_ref), custom_call_target="tpu_custom_call" | custom-call | flops 1000000 | bytes 2129920 | tf_op jit(solution)/shard_map/pallas_call | solution.py:21
  47.1 9.7 %all-to-all-start.1 = ((bf16[32,192,128]{2,1,0:T(8,128)(2,1)}), bf16[32,192,128]{2,1,0:T(8,128)(2,1)S(1)}, u32[]{:S(2)}, u32[]{:S(2)}) async-start(bf16[32,192,128]{2,1,0:T(8,128)(2,1)} %bitcast.4), calls=%async_computation.1 | async-start | bytes 3145728 | tf_op jit(solution)/shard_map/all_to_all | solution.py:239
  56.8 2.2 %collective-permute-start.4 = (bf16[128,768]{1,0:T(8,128)(2,1)S(1)}, bf16[128,768]{1,0:T(8,128)(2,1)S(1)}, u32[]{:S(2)}, u32[]{:S(2)}) collective-permute-start(bf16[128,768]{1,0:T(8,128)(2,1)S(1)} %get-tuple-element.15), channel_id=1, source_target_pairs={{0,128},{128,0},{256,384},{384,256},{1,129},{129,1},{257,385},{385... | collective-permute-start | bytes 589832 | tf_op jit(solution)/shard_map/ppermute | solution.py:216
  59.1 1.1 collective-permute-done.4
  60.2 2.3 %collective-permute-start.5 = (bf16[128,768]{1,0:T(8,128)(2,1)S(1)}, bf16[128,768]{1,0:T(8,128)(2,1)S(1)}, u32[]{:S(2)}, u32[]{:S(2)}) collective-permute-start(bf16[128,768]{1,0:T(8,128)(2,1)S(1)} %add_convert_fusion.refs_0_), channel_id=1, source_target_pairs={{0,8},{8,16},{16,24},{24,0},{32,40},{40,48},{48,56},{56,32},{64,72... | collective-permute-start | bytes 589832 | tf_op jit(solution)/shard_map/ppermute | solution.py:219
  62.5 4.8 %collective-permute-start.6 = (bf16[128,768]{1,0:T(8,128)(2,1)S(1)}, bf16[128,768]{1,0:T(8,128)(2,1)S(1)}, u32[]{:S(2)}, u32[]{:S(2)}) collective-permute-start(bf16[128,768]{1,0:T(8,128)(2,1)S(1)} %add_convert_fusion.refs_0_), channel_id=1, source_target_pairs={{0,16},{8,24},{16,0},{24,8},{32,48},{40,56},{48,32},{56,40},{64,80... | collective-permute-start | bytes 589832 | tf_op jit(solution)/shard_map/ppermute | solution.py:219
  67.3 2.4 %collective-permute-start.7 = (bf16[128,768]{1,0:T(8,128)(2,1)S(1)}, bf16[128,768]{1,0:T(8,128)(2,1)S(1)}, u32[]{:S(2)}, u32[]{:S(2)}) collective-permute-start(bf16[128,768]{1,0:T(8,128)(2,1)S(1)} %add_convert_fusion.refs_0_), channel_id=1, source_target_pairs={{0,24},{8,0},{16,8},{24,16},{32,56},{40,32},{48,40},{56,48},{64,88... | collective-permute-start | bytes 589832 | tf_op jit(solution)/shard_map/ppermute | solution.py:219
  69.7 10.4 %collective-permute-done.6.refs_2_ = bf16[128,768]{1,0:T(8,128)(2,1)S(1)} collective-permute-done((bf16[128,768]{1,0:T(8,128)(2,1)S(1)}, bf16[128,768]{1,0:T(8,128)(2,1)S(1)}, u32[]{:S(2)}, u32[]{:S(2)}) %collective-permute-start.6) | collective-permute-done | bytes 196640 | tf_op jit(solution)/shard_map/ppermute | solution.py:219
  80.1 3.3 %collective-permute-done.7.refs_3_ = bf16[128,768]{1,0:T(8,128)(2,1)S(1)} collective-permute-done((bf16[128,768]{1,0:T(8,128)(2,1)S(1)}, bf16[128,768]{1,0:T(8,128)(2,1)S(1)}, u32[]{:S(2)}, u32[]{:S(2)}) %collective-permute-start.7) | collective-permute-done | bytes 196640 | tf_op jit(solution)/shard_map/ppermute | solution.py:219
  83.4 2.1 %shard_map.81 = bf16[4,96,768]{2,1,0:T(8,128)(2,1)} custom-call(s32[5]{0:T(128)S(1)} %stack.20.at, bf16[4,8,192,128]{3,2,1,0:T(8,128)(2,1)S(1)} %bitcast.6, bf16[128,768]{1,0:T(8,128)(2,1)S(1)} %add_convert_fusion.refs_0_, bf16[128,768]{1,0:T(8,128)(2,1)S(1)} %collective-permute-done.5.refs_1_, bf16[128,768]{1,0:T(8,128)(2,1)S(1)} %collective-permute-done.6.refs_2_, ...), custom_call_target="tpu_custom_call" | custom-call | flops 402653184 | bytes 2949140 | tf_op jit(solution)/shard_map/pallas_call | solution.py:21
  85.5 5.0 %all-to-all-start.2 = ((bf16[4,96,768]{2,1,0:T(8,128)(2,1)}), bf16[4,96,768]{2,1,0:T(8,128)(2,1)S(1)}, u32[]{:S(2)}, u32[]{:S(2)}) async-start(bf16[4,96,768]{2,1,0:T(8,128)(2,1)} %shard_map.81), calls=%async_computation.2 | async-start | bytes 1179648 | tf_op jit(solution)/shard_map/all_to_all | solution.py:250
  90.5 3.1 %collective-permute-start.8 = (bf16[64,1536]{1,0:T(8,128)(2,1)S(1)}, bf16[64,1536]{1,0:T(8,128)(2,1)S(1)}, u32[]{:S(2)}, u32[]{:S(2)}) collective-permute-start(bf16[64,1536]{1,0:T(8,128)(2,1)S(1)} %constant_dynamic-update-slice_fusion.refs_0_), channel_id=1, source_target_pairs={{0,1},{1,2},{2,3},{3,0},{4,5},{5,6},{6,7},{7,4},{8,9},{9,10},{10,1... | collective-permute-start | bytes 589832 | tf_op jit(solution)/shard_map/ppermute | solution.py:194
  93.6 2.8 %collective-permute-start.9 = (bf16[64,1536]{1,0:T(8,128)(2,1)S(1)}, bf16[64,1536]{1,0:T(8,128)(2,1)S(1)}, u32[]{:S(2)}, u32[]{:S(2)}) collective-permute-start(bf16[64,1536]{1,0:T(8,128)(2,1)S(1)} %constant_dynamic-update-slice_fusion.refs_0_), channel_id=1, source_target_pairs={{0,2},{1,3},{2,0},{3,1},{4,6},{5,7},{6,4},{7,5},{8,10},{9,11},{10,... | collective-permute-start | bytes 589832 | tf_op jit(solution)/shard_map/ppermute | solution.py:194
  96.4 3.7 %collective-permute-start.10 = (bf16[64,1536]{1,0:T(8,128)(2,1)S(1)}, bf16[64,1536]{1,0:T(8,128)(2,1)S(1)}, u32[]{:S(2)}, u32[]{:S(2)}) collective-permute-start(bf16[64,1536]{1,0:T(8,128)(2,1)S(1)} %constant_dynamic-update-slice_fusion.refs_0_), channel_id=1, source_target_pairs={{0,3},{1,0},{2,1},{3,2},{4,7},{5,4},{6,5},{7,6},{8,11},{9,8},{10,9... | collective-permute-start | bytes 589832 | tf_op jit(solution)/shard_map/ppermute | solution.py:194
  100.1 2.7 %collective-permute-done.9.refs_2_ = bf16[64,1536]{1,0:T(8,128)(2,1)S(1)} collective-permute-done((bf16[64,1536]{1,0:T(8,128)(2,1)S(1)}, bf16[64,1536]{1,0:T(8,128)(2,1)S(1)}, u32[]{:S(2)}, u32[]{:S(2)}) %collective-permute-start.9) | collective-permute-done | bytes 196640 | tf_op jit(solution)/shard_map/ppermute | solution.py:194
  102.8 5.2 %collective-permute-done.10.refs_3_ = bf16[64,1536]{1,0:T(8,128)(2,1)S(1)} collective-permute-done((bf16[64,1536]{1,0:T(8,128)(2,1)S(1)}, bf16[64,1536]{1,0:T(8,128)(2,1)S(1)}, u32[]{:S(2)}, u32[]{:S(2)}) %collective-permute-start.10) | collective-permute-done | bytes 196640 | tf_op jit(solution)/shard_map/ppermute | solution.py:194
  108.0 1.7 %shard_map.82 = (f32[48,1536]{1,0:T(8,128)}, f32[48,1536]{1,0:T(8,128)}) custom-call(s32[5]{0:T(128)S(1)} %stack.20.at, bf16[4,8,192,128]{3,2,1,0:T(8,128)(2,1)S(1)} %bitcast.7, bf16[64,1536]{1,0:T(8,128)(2,1)S(1)} %constant_dynamic-update-slice_fusion.refs_0_, bf16[64,1536]{1,0:T(8,128)(2,1)S(1)} %collective-permute-done.8.refs_1_, ...), custom_call_target="tpu_custom_call" | custom-call | flops 201326592 | bytes 2949140 | tf_op jit(solution)/shard_map/pallas_call | solution.py:21
  109.8 0.8 convert_reduce_fusion
  (23 shorter events, 1.0 us)
Async XLA Ops:
  1.5 1.3 %copy-start.1 = (bf16[1536,384]{1,0:T(8,128)(2,1)S(1)}, bf16[1536,384]{1,0:T(8,128)(2,1)}, u32[]{:S(2)}) copy-start(bf16[1536,384]{1,0:T(8,128)(2,1)} %a_ref.1) | copy-start | bytes 3538948
  2.8 0.9 copy-start.3
  3.6 16.6 %copy-start.2 = (bf16[128,1536]{1,0:T(8,128)(2,1)S(1)}, bf16[128,1536]{1,0:T(8,128)(2,1)}, u32[]{:S(2)}) copy-start(bf16[128,1536]{1,0:T(8,128)(2,1)} %g_ref.1) | copy-start | bytes 1179652
  5.5 32.5 %copy-start.4 = (bf16[128,384]{1,0:T(8,128)(2,1)S(1)}, bf16[128,384]{1,0:T(8,128)(2,1)}, u32[]{:S(2)}) copy-start(bf16[128,384]{1,0:T(8,128)(2,1)} %x_ref.3) | copy-start | bytes 294916
  5.5 38.8 %copy-start = (bf16[1536,768]{1,0:T(8,128)(2,1)S(1)}, bf16[1536,768]{1,0:T(8,128)(2,1)}, u32[]{:S(2)}) copy-start(bf16[1536,768]{1,0:T(8,128)(2,1)} %b_ref.1) | copy-start | bytes 7077892
  5.5 40.2 %all-to-all-start = ((bf16[16,120,128]{2,1,0:T(8,128)(2,1)}), bf16[16,120,128]{2,1,0:T(8,128)(2,1)S(1)}, u32[]{:S(2)}, u32[]{:S(2)}) async-start(bf16[16,120,128]{2,1,0:T(8,128)(2,1)} %shard_map.76), calls=%async_computation | async-start | bytes 983040 | tf_op jit(solution)/shard_map/all_to_all | solution.py:191
  21.0 7.1 %collective-permute-start = (bf16[64,1536]{1,0:T(8,128)(2,1)S(1)}, bf16[64,1536]{1,0:T(8,128)(2,1)S(1)}, u32[]{:S(2)}, u32[]{:S(2)}) collective-permute-start(bf16[64,1536]{1,0:T(8,128)(2,1)S(1)} %shard_map.77.gy_ref), channel_id=1, source_target_pairs={{0,4},{1,5},{2,6},{3,7},{4,0},{5,1},{6,2},{7,3},{8,12},{9,13},{10,... | collective-permute-start | bytes 589832 | tf_op jit(solution)/shard_map/ppermute | solution.py:204
  28.1 10.6 %collective-permute-start.1 = (bf16[64,1536]{1,0:T(8,128)(2,1)S(1)}, bf16[64,1536]{1,0:T(8,128)(2,1)S(1)}, u32[]{:S(2)}, u32[]{:S(2)}) collective-permute-start(bf16[64,1536]{1,0:T(8,128)(2,1)S(1)} %pad_maximum_fusion.refs_0_), channel_id=1, source_target_pairs={{0,1},{1,2},{2,3},{3,0},{4,5},{5,6},{6,7},{7,4},{8,9},{9,10},{10,1... | collective-permute-start | bytes 589832 | tf_op jit(solution)/shard_map/ppermute | solution.py:194
  31.3 8.2 %collective-permute-start.2 = (bf16[64,1536]{1,0:T(8,128)(2,1)S(1)}, bf16[64,1536]{1,0:T(8,128)(2,1)S(1)}, u32[]{:S(2)}, u32[]{:S(2)}) collective-permute-start(bf16[64,1536]{1,0:T(8,128)(2,1)S(1)} %pad_maximum_fusion.refs_0_), channel_id=1, source_target_pairs={{0,2},{1,3},{2,0},{3,1},{4,6},{5,7},{6,4},{7,5},{8,10},{9,11},{10,... | collective-permute-start | bytes 589832 | tf_op jit(solution)/shard_map/ppermute | solution.py:194
  34.0 10.3 %collective-permute-start.3 = (bf16[64,1536]{1,0:T(8,128)(2,1)S(1)}, bf16[64,1536]{1,0:T(8,128)(2,1)S(1)}, u32[]{:S(2)}, u32[]{:S(2)}) collective-permute-start(bf16[64,1536]{1,0:T(8,128)(2,1)S(1)} %pad_maximum_fusion.refs_0_), channel_id=1, source_target_pairs={{0,3},{1,0},{2,1},{3,2},{4,7},{5,4},{6,5},{7,6},{8,11},{9,8},{10,9... | collective-permute-start | bytes 589832 | tf_op jit(solution)/shard_map/ppermute | solution.py:194
  47.1 36.3 %all-to-all-start.1 = ((bf16[32,192,128]{2,1,0:T(8,128)(2,1)}), bf16[32,192,128]{2,1,0:T(8,128)(2,1)S(1)}, u32[]{:S(2)}, u32[]{:S(2)}) async-start(bf16[32,192,128]{2,1,0:T(8,128)(2,1)} %bitcast.4), calls=%async_computation.1 | async-start | bytes 3145728 | tf_op jit(solution)/shard_map/all_to_all | solution.py:239
  56.8 3.3 %collective-permute-start.4 = (bf16[128,768]{1,0:T(8,128)(2,1)S(1)}, bf16[128,768]{1,0:T(8,128)(2,1)S(1)}, u32[]{:S(2)}, u32[]{:S(2)}) collective-permute-start(bf16[128,768]{1,0:T(8,128)(2,1)S(1)} %get-tuple-element.15), channel_id=1, source_target_pairs={{0,128},{128,0},{256,384},{384,256},{1,129},{129,1},{257,385},{385... | collective-permute-start | bytes 589832 | tf_op jit(solution)/shard_map/ppermute | solution.py:216
  60.2 9.5 %collective-permute-start.5 = (bf16[128,768]{1,0:T(8,128)(2,1)S(1)}, bf16[128,768]{1,0:T(8,128)(2,1)S(1)}, u32[]{:S(2)}, u32[]{:S(2)}) collective-permute-start(bf16[128,768]{1,0:T(8,128)(2,1)S(1)} %add_convert_fusion.refs_0_), channel_id=1, source_target_pairs={{0,8},{8,16},{16,24},{24,0},{32,40},{40,48},{48,56},{56,32},{64,72... | collective-permute-start | bytes 589832 | tf_op jit(solution)/shard_map/ppermute | solution.py:219
  62.5 17.6 %collective-permute-start.6 = (bf16[128,768]{1,0:T(8,128)(2,1)S(1)}, bf16[128,768]{1,0:T(8,128)(2,1)S(1)}, u32[]{:S(2)}, u32[]{:S(2)}) collective-permute-start(bf16[128,768]{1,0:T(8,128)(2,1)S(1)} %add_convert_fusion.refs_0_), channel_id=1, source_target_pairs={{0,16},{8,24},{16,0},{24,8},{32,48},{40,56},{48,32},{56,40},{64,80... | collective-permute-start | bytes 589832 | tf_op jit(solution)/shard_map/ppermute | solution.py:219
  67.3 16.1 %collective-permute-start.7 = (bf16[128,768]{1,0:T(8,128)(2,1)S(1)}, bf16[128,768]{1,0:T(8,128)(2,1)S(1)}, u32[]{:S(2)}, u32[]{:S(2)}) collective-permute-start(bf16[128,768]{1,0:T(8,128)(2,1)S(1)} %add_convert_fusion.refs_0_), channel_id=1, source_target_pairs={{0,24},{8,0},{16,8},{24,16},{32,56},{40,32},{48,40},{56,48},{64,88... | collective-permute-start | bytes 589832 | tf_op jit(solution)/shard_map/ppermute | solution.py:219
  85.5 24.3 %all-to-all-start.2 = ((bf16[4,96,768]{2,1,0:T(8,128)(2,1)}), bf16[4,96,768]{2,1,0:T(8,128)(2,1)S(1)}, u32[]{:S(2)}, u32[]{:S(2)}) async-start(bf16[4,96,768]{2,1,0:T(8,128)(2,1)} %shard_map.81), calls=%async_computation.2 | async-start | bytes 1179648 | tf_op jit(solution)/shard_map/all_to_all | solution.py:250
  90.5 9.6 %collective-permute-start.8 = (bf16[64,1536]{1,0:T(8,128)(2,1)S(1)}, bf16[64,1536]{1,0:T(8,128)(2,1)S(1)}, u32[]{:S(2)}, u32[]{:S(2)}) collective-permute-start(bf16[64,1536]{1,0:T(8,128)(2,1)S(1)} %constant_dynamic-update-slice_fusion.refs_0_), channel_id=1, source_target_pairs={{0,1},{1,2},{2,3},{3,0},{4,5},{5,6},{6,7},{7,4},{8,9},{9,10},{10,1... | collective-permute-start | bytes 589832 | tf_op jit(solution)/shard_map/ppermute | solution.py:194
  93.6 9.2 %collective-permute-start.9 = (bf16[64,1536]{1,0:T(8,128)(2,1)S(1)}, bf16[64,1536]{1,0:T(8,128)(2,1)S(1)}, u32[]{:S(2)}, u32[]{:S(2)}) collective-permute-start(bf16[64,1536]{1,0:T(8,128)(2,1)S(1)} %constant_dynamic-update-slice_fusion.refs_0_), channel_id=1, source_target_pairs={{0,2},{1,3},{2,0},{3,1},{4,6},{5,7},{6,4},{7,5},{8,10},{9,11},{10,... | collective-permute-start | bytes 589832 | tf_op jit(solution)/shard_map/ppermute | solution.py:194
  96.4 11.6 %collective-permute-start.10 = (bf16[64,1536]{1,0:T(8,128)(2,1)S(1)}, bf16[64,1536]{1,0:T(8,128)(2,1)S(1)}, u32[]{:S(2)}, u32[]{:S(2)}) collective-permute-start(bf16[64,1536]{1,0:T(8,128)(2,1)S(1)} %constant_dynamic-update-slice_fusion.refs_0_), channel_id=1, source_target_pairs={{0,3},{1,0},{2,1},{3,2},{4,7},{5,4},{6,5},{7,6},{8,11},{9,8},{10,9... | collective-permute-start | bytes 589832 | tf_op jit(solution)/shard_map/ppermute | solution.py:194

commit v9 on v8

v9 whole, which is shorter than its diff:
```python
import functools

import jax
import jax.numpy as jnp
from jax import lax
from jax.experimental import pallas as pl
from jax.experimental.pallas import tpu as pltpu
from jax.sharding import PartitionSpec as P

BF = jnp.bfloat16
F32 = jnp.float32
LANES = 128
FIRST = (((0,), (0,)), ((), ()))
LAST = (((1,), (1,)), ((), ()))
SMEM = pl.BlockSpec(memory_space=pltpu.SMEM)
VMEM = pl.BlockSpec(memory_space=pltpu.VMEM)
SHIFTS = (0, 2, 1, -1)


def call(kernel, inputs, outs, flops, scratch=(), place=VMEM):
    moved = sum(x.size * x.dtype.itemsize for x in list(inputs) + list(outs))
    return pl.pallas_call(
        kernel,
        out_shape=outs,
        in_specs=[SMEM if x.dtype == jnp.int32 else place for x in inputs],
        out_specs=[VMEM] * len(outs),
        scratch_shapes=list(scratch),
        compiler_params=pltpu.CompilerParams(vmem_limit_bytes=40 * 1024 * 1024),
        cost_estimate=pl.CostEstimate(flops=flops, bytes_accessed=moved, transcendentals=0),
    )(*inputs)


def source_of(k):
    col = lax.axis_index("col")
    return 4 * ((col // 4) ^ (k % 2)) + lax.rem(col % 4 - k // 2 + 4, 4)


def own_picks(picks, count, tok):
    begin = lax.axis_index("grp") * count
    first = lax.axis_index("col") * tok
    return [picks[begin + i] - first for i in range(count)]


def rows_hot(targets, tok):
    shape = (len(targets), tok)
    sub = lax.broadcasted_iota(jnp.int32, shape, 0)
    lane = lax.broadcasted_iota(jnp.int32, shape, 1)
    want = jnp.zeros(shape, jnp.int32)
    for i, target in enumerate(targets):
        want = jnp.where(sub == i, target, want)
    return jnp.where(want == lane, 1.0, 0.0).astype(BF)


def first_kernel(picks, x_hbm, a_hbm, out_ref, x_ref, a_ref, sems):
    n_row, depth, tok = out_ref.shape
    parts = sems.shape[0] - 1
    step = a_ref.shape[0] // parts
    copies = [pltpu.make_async_copy(x_hbm, x_ref, sems.at[parts])]
    for p in range(parts):
        span = pl.ds(p * step, step)
        copies.append(pltpu.make_async_copy(a_hbm.at[span], a_ref.at[span], sems.at[p]))
    for copy in copies:
        copy.start()
    out_rows = a_ref.shape[0] // n_row
    quarter = picks.shape[0] // 4
    hot = rows_hot(own_picks(picks, quarter, tok), tok)
    copies[0].wait()
    chosen = jnp.dot(hot, x_ref[...], preferred_element_type=F32)
    strips = [chosen[:, k : k + LANES] for k in range(0, chosen.shape[1], LANES)]
    block = jnp.concatenate(strips, axis=0).astype(BF)
    out_ref[:, out_rows:, :] = jnp.broadcast_to(block[None], (n_row,) + block.shape)
    each = step // out_rows
    for p in range(parts):
        copies[p + 1].wait()
        rows = a_ref[p * step : (p + 1) * step, :]
        part = lax.dot_general(rows, x_ref[...], LAST, preferred_element_type=F32)
        out_ref[p * each : (p + 1) * each, :out_rows, :] = part.astype(BF).reshape(
            each, out_rows, tok
        )


def pick_kernel(picks, g_ref, out_ref):
    tok = g_ref.shape[0]
    samp = picks.shape[0]
    plane = lax.axis_index("row") % 4
    first = lax.axis_index("col") * tok
    count = out_ref.shape[0] - samp
    ours = [64 * (i // 16) + 16 * plane + i % 16 for i in range(count)]
    hot = rows_hot(ours + [picks[i] - first for i in range(samp)], tok)
    out_ref[...] = jnp.dot(hot, g_ref[...], preferred_element_type=F32).astype(BF)


def side_kernel(picks, x_ref, gy_ref, out_ref):
    n_col, depth, unused = out_ref.shape
    tok, feat = x_ref.shape
    samp = picks.shape[0]
    tile = feat // n_col
    quarter = samp // 4
    hot = rows_hot(own_picks(picks, quarter, tok), tok)
    chosen = jnp.dot(hot, x_ref[...], preferred_element_type=F32)
    begin = pl.multiple_of((lax.axis_index("row") % 4) * feat, LANES)
    own = gy_ref[gy_ref.shape[0] - samp :, pl.ds(begin, feat)].astype(F32)
    empty = jnp.zeros((samp - 3 * quarter, 16), F32)
    for c in range(n_col):
        at = c * tile
        top = own[:, at : at + 32]
        cuts = [chosen[:, at + k : at + k + 16] for k in range(0, tile, 16)]
        low = jnp.concatenate(
            [own[:, at + 32 : at + tile], jnp.concatenate(cuts + [empty], axis=0)], axis=1
        )
        block = jnp.concatenate([top, low], axis=0)
        block = jnp.concatenate([jnp.zeros((depth, LANES - 32), F32), block], axis=1)
        out_ref[c] = block.astype(BF)


def right_kernel(b_ref, *refs):
    blocks, keep_ref, give_ref, held = refs[:-3], refs[-3], refs[-2], refs[-1]
    n_blk, unused, size, width = held.shape
    rows = jnp.concatenate([block[...] for block in blocks], axis=0)
    term = jnp.dot(rows, b_ref[...], preferred_element_type=F32)
    held[...] = term.reshape(held.shape)
    core = lax.axis_index("grp") % 2
    keep_ref[...] = held[:, core].reshape(n_blk * size, width).astype(BF)
    give_ref[...] = held[:, 1 - core].reshape(n_blk * size, width).astype(BF)


def second_kernel(got_ref, side_ref, out_ref):
    n_grp, n_col, unused, unused = out_ref.shape
    n_row, depth, tok = got_ref.shape
    strip = depth - (depth // 32) * 32
    out_rows = depth - strip
    total = got_ref[0, :out_rows, :].astype(F32)
    for r in range(1, n_row):
        total = total + got_ref[r, :out_rows, :].astype(F32)
    total = jnp.concatenate([total, jnp.zeros((LANES - out_rows, tok), F32)], axis=0)
    turned = jnp.transpose(total).astype(BF)
    size = tok // 2
    per = n_row // n_grp
    x_rows = per * strip
    for g in range(n_grp):
        u_block = turned[(g % 2) * size : (g % 2 + 1) * size]
        x_block = got_ref[g * per : (g + 1) * per, out_rows:, :].astype(F32)
        x_block = x_block.reshape(x_rows, tok).astype(BF)
        for c in range(n_col):
            out_ref[g, c, :size, :] = u_block + side_ref[c]
            out_ref[g, c, size:, :] = x_block


def final_kernel(got_ref, *refs):
    v_refs, out_ref, held = refs[:-2], refs[-2], refs[-1]
    n_col, spread, size, width = held.shape
    n_grp, out_rows, unused = out_ref.shape
    row = lax.axis_index("row")
    for j, shift in enumerate(SHIFTS):
        plane = lax.rem(row - shift + spread, spread)
        block = v_refs[j][...].astype(F32)
        for k in range(n_col):
            held[source_of(k), plane] = block[k * size : (k + 1) * size]
    tokens = n_col * spread * size
    right = held[...].reshape(tokens, width).astype(BF)
    for g in range(n_grp):
        left = got_ref[g, :, : spread * size, :].reshape(tokens, LANES)
        term = lax.dot_general(left, right, FIRST, preferred_element_type=F32)
        out_ref[g] = term[:out_rows].astype(BF)


def factor_kernel(got_ref, *refs):
    blocks, act_ref, grad_ref = refs[:-2], refs[-2], refs[-1]
    n_grp, n_col, depth, unused = got_ref.shape
    tile, width = act_ref.shape
    samp = blocks[0].shape[0] // 2
    quarter = samp // n_grp
    total = samp * n_col
    scale = 1.0 / total
    begin = depth - quarter * (width // LANES)
    span = got_ref[:, :, begin:, :].astype(F32)
    strips = []
    for t in range(width // LANES):
        strip = span[:, :, t * quarter : (t + 1) * quarter, :].reshape(total, LANES)
        strips.append(strip.astype(BF))
    right = jnp.concatenate(strips, axis=1)
    lefts = got_ref[:, :, samp : 2 * samp, :].astype(F32)
    for k in range(tile // 16):
        left = lefts[:, :, k * quarter : (k + 1) * quarter, :].reshape(total, LANES).astype(BF)
        term = lax.dot_general(left, right, FIRST, preferred_element_type=F32)
        act_ref[16 * k : 16 * (k + 1), :] = term[LANES - 16 :] * scale
    owner = lax.axis_index("row") // 4
    sides = [got_ref[owner, source_of(k), : 2 * samp, :] for k in range(n_col)]
    right = jnp.concatenate([block[...] for block in blocks], axis=0)
    left = jnp.concatenate([side[:samp] for side in sides], axis=0)
    term = lax.dot_general(left, right, FIRST, preferred_element_type=F32)
    grad_ref[:32, :] = term[LANES - 32 :] * scale
    left = jnp.concatenate([side[samp:] for side in sides], axis=0)
    term = lax.dot_general(left, right, FIRST, preferred_element_type=F32)
    grad_ref[32:, :] = term[LANES - 32 : LANES - 16] * scale


def body(tokens_in, cotangent, sample_rows, act_inverse, grad_inverse):
    n_row = lax.axis_size("row")
    n_col = lax.axis_size("col")
    n_grp = lax.axis_size("grp")
    tok, feat_row = tokens_in.shape
    feat_grp = cotangent.shape[1]
    width = grad_inverse.shape[1]
    samp = sample_rows.shape[0]
    quarter = samp // n_grp
    tile = feat_row // n_col
    out_rows = feat_grp // n_row
    strip = quarter * feat_row // LANES
    spread = 4
    size = tok // 2 // spread
    shape = jax.ShapeDtypeStruct

    payload = call(
        first_kernel,
        (sample_rows, tokens_in, act_inverse),
        [shape((n_row, out_rows + strip, tok), BF)],
        2 * feat_grp * feat_row * tok,
        [
            pltpu.VMEM(tokens_in.shape, BF),
            pltpu.VMEM(act_inverse.shape, BF),
            pltpu.SemaphoreType.DMA((5,)),
        ],
        pl.BlockSpec(memory_space=pl.ANY),
    )[0]
    first = lax.all_to_all(payload, "row", 0, 0)

    def along_y(block, k):
        return lax.ppermute(
            block, "col", [(i, i - i % 4 + (i + k) % 4) for i in range(n_col)]
        )

    picked = call(
        pick_kernel,
        (sample_rows, cotangent),
        [shape((2 * size + samp, feat_grp), BF)],
        2 * 64 * tok * feat_grp,
    )[0]
    beside = lax.ppermute(picked, "col", [(i, (i + 4) % n_col) for i in range(n_col)])
    cut = 2 * size
    pair = jnp.concatenate([picked[:cut], beside[:cut]], axis=0)
    pairs = [pair] + [along_y(pair, k) for k in range(1, 4)]
    keep, give = call(
        right_kernel,
        (grad_inverse, *pairs),
        [shape((n_col * size, width), BF)] * 2,
        4 * n_col * size * feat_grp * width,
        [pltpu.VMEM((n_col, 2, size, width), F32)],
    )
    first, unused = lax.optimization_barrier((first, give))
    taken = lax.ppermute(give, "grp", [(i, i ^ 1) for i in range(n_grp)])
    right = (keep.astype(F32) + taken.astype(F32)).astype(BF)
    rights = [right] + [
        lax.ppermute(right, "row", [(i, (i + j) % n_row) for i in range(n_row)])
        for j in SHIFTS[1:]
    ]
    unused, picked_y, beside_y = lax.optimization_barrier(
        (rights[2], picked[cut:], beside[cut:])
    )
    samples = jnp.concatenate([picked_y, beside_y], axis=0)
    samples = [samples] + [along_y(samples, k) for k in range(1, 4)]
    side = call(
        side_kernel,
        (sample_rows, tokens_in, picked),
        [shape((n_col, 2 * samp, LANES), BF)],
        2 * samp * tok * feat_row,
    )[0]
    send = call(
        second_kernel,
        (first, side),
        [shape((n_grp, n_col, size * spread + strip * n_row // n_grp, LANES), BF)],
        1000000,
    )[0]
    got = lax.all_to_all(send.reshape((n_grp * n_col,) + send.shape[2:]), ("grp", "col"), 0, 0)
    got = got.reshape(send.shape)

    term = call(
        final_kernel,
        (got, *rights),
        [shape((n_grp, out_rows, width), BF)],
        2 * n_grp * LANES * n_col * spread * size * width,
        [pltpu.VMEM((n_col, spread, size, width), F32)],
    )[0]
    got, unused = lax.optimization_barrier((got, term))
    term = lax.all_to_all(term, "grp", 0, 0)
    precond = jnp.sum(term.astype(F32), axis=0)
    act_cov, grad_cov = call(
        factor_kernel,
        (got, *samples),
        [shape((tile, feat_grp), F32)] * 2,
        4 * LANES * samp * n_col * feat_grp,
    )
    return (precond, act_cov, grad_cov)


def solution(mesh):
    return jax.shard_map(
        body,
        mesh=mesh,
        in_specs=(P("col", "row"), P("col", "grp"), P("col"), P("grp", "row"), P("grp", "col")),
        out_specs=(P(("grp", "row"), "col"), P(("row", "col"), "grp"), P(("row", "col"), "grp")),
        check_vma=False,
    )
```

time: 111 us -> 110 us (level)
  the two profiles are of different devices: /device:TPU:47 before, /device:TPU:1 now
where the time goes in v9:
time: 110 us; the launch traced here: 109 us
  starting transfers between devices  68.6 us (62%)
  waiting for transfers between devices  24.4 us (22%)
  Pallas kernels  9.81 us (9%)
  local copies, waits for them, and re-layouts  4.19 us (4%)
    ppermute x6, starting transfers between devices, along_y(): lax.ppermute(block, 'col', [(i, i - i % 4 + (i + k) % 4) for i in range(n...  21.2 us
    all_to_all x1, starting transfers between devices, body(): first = lax.all_to_all(payload, 'row', 0, 0)  15.9 us
    all_to_all x1, starting transfers between devices, body(): lax.all_to_all(send.reshape((n_grp * n_col,) + send.shape[2:]), ('grp', '...  11.5 us
    ppermute x3, waiting for transfers between devices, body(): lax.ppermute(right, 'row', [(i, (i + j) % n_row) for i in range(n_row)])  10.5 us
    pallas_call x7, Pallas kernels, call(): pl.pallas_call(kernel, out_shape=outs, in_specs=[SMEM if x.dtype == jnp.i...  9.81 us
    ppermute x3, starting transfers between devices, body(): lax.ppermute(right, 'row', [(i, (i + j) % n_row) for i in range(n_row)])  9.34 us
    ppermute x6, waiting for transfers between devices, along_y(): lax.ppermute(block, 'col', [(i, i - i % 4 + (i + k) % 4) for i in range(n...  9.11 us
    all_to_all x1, starting transfers between devices, body(): term = lax.all_to_all(term, 'grp', 0, 0)  5.5 us
  transfers between devices with their start and end apart: 14, of which 8 were waited for; matrix products, arithmetic and copies ran while one was open for 1% of the time, Pallas kernels for 4%

profile of v9, /device:TPU:1, one launch (start us, length us, event | category | flops | bytes accessed | tf_op | source)
XLA Modules:
  0.0 108.8 jit_solution(10929703702119951686)
XLA Ops:
  0.6 1.3 %copy-done.1 = bf16[1536,384]{1,0:T(8,128)(2,1)S(1)} copy-done((bf16[1536,384]{1,0:T(8,128)(2,1)S(1)}, bf16[1536,384]{1,0:T(8,128)(2,1)}, u32[]{:S(2)}) %copy-start.1) | copy-done | bytes 1179672
  1.9 0.9 copy-done.3
  3.5 3.0 %shard_map.76 = bf16[16,120,128]{2,1,0:T(8,128)(2,1)} custom-call(s32[32]{0:T(128)S(1)} %copy-done.5, bf16[128,384]{1,0:T(8,128)(2,1)S(1)} %copy-done.3, bf16[1536,384]{1,0:T(8,128)(2,1)S(1)} %copy-done.1), custom_call_target="tpu_custom_call" | custom-call | flops 150994944 | bytes 1769600 | tf_op jit(solution)/shard_map/pallas_call | solution.py:22
  6.4 15.9 %all-to-all-start = ((bf16[16,120,128]{2,1,0:T(8,128)(2,1)}), bf16[16,120,128]{2,1,0:T(8,128)(2,1)S(1)}, u32[]{:S(2)}, u32[]{:S(2)}) async-start(bf16[16,120,128]{2,1,0:T(8,128)(2,1)} %shard_map.76), calls=%async_computation | async-start | bytes 983040 | tf_op jit(solution)/shard_map/all_to_all | solution.py:226
  22.4 0.7 shard_map.77.gy_ref
  23.1 3.1 %collective-permute-start = (bf16[64,1536]{1,0:T(8,128)(2,1)S(1)}, bf16[64,1536]{1,0:T(8,128)(2,1)S(1)}, u32[]{:S(2)}, u32[]{:S(2)}) collective-permute-start(bf16[64,1536]{1,0:T(8,128)(2,1)S(1)} %shard_map.77.gy_ref), channel_id=1, source_target_pairs={{0,4},{1,5},{2,6},{3,7},{4,0},{5,1},{6,2},{7,3},{8,12},{9,13},{10,... | collective-permute-start | bytes 589832 | tf_op jit(solution)/shard_map/ppermute | solution.py:239
  26.9 3.6 %collective-permute-done = bf16[64,1536]{1,0:T(8,128)(2,1)S(1)} collective-permute-done((bf16[64,1536]{1,0:T(8,128)(2,1)S(1)}, bf16[64,1536]{1,0:T(8,128)(2,1)S(1)}, u32[]{:S(2)}, u32[]{:S(2)}) %collective-permute-start) | collective-permute-done | bytes 196640 | tf_op jit(solution)/shard_map/ppermute | solution.py:239
  30.5 3.2 %collective-permute-start.1 = (bf16[64,1536]{1,0:T(8,128)(2,1)S(1)}, bf16[64,1536]{1,0:T(8,128)(2,1)S(1)}, u32[]{:S(2)}, u32[]{:S(2)}) collective-permute-start(bf16[64,1536]{1,0:T(8,128)(2,1)S(1)} %pad_maximum_fusion.refs_0_), channel_id=1, source_target_pairs={{0,1},{1,2},{2,3},{3,0},{4,5},{5,6},{6,7},{7,4},{8,9},{9,10},{10,1... | collective-permute-start | bytes 589832 | tf_op jit(solution)/shard_map/ppermute | solution.py:229
  33.7 4.5 %collective-permute-start.2 = (bf16[64,1536]{1,0:T(8,128)(2,1)S(1)}, bf16[64,1536]{1,0:T(8,128)(2,1)S(1)}, u32[]{:S(2)}, u32[]{:S(2)}) collective-permute-start(bf16[64,1536]{1,0:T(8,128)(2,1)S(1)} %pad_maximum_fusion.refs_0_), channel_id=1, source_target_pairs={{0,2},{1,3},{2,0},{3,1},{4,6},{5,7},{6,4},{7,5},{8,10},{9,11},{10,... | collective-permute-start | bytes 589832 | tf_op jit(solution)/shard_map/ppermute | solution.py:229
  38.2 3.0 %collective-permute-start.3 = (bf16[64,1536]{1,0:T(8,128)(2,1)S(1)}, bf16[64,1536]{1,0:T(8,128)(2,1)S(1)}, u32[]{:S(2)}, u32[]{:S(2)}) collective-permute-start(bf16[64,1536]{1,0:T(8,128)(2,1)S(1)} %pad_maximum_fusion.refs_0_), channel_id=1, source_target_pairs={{0,3},{1,0},{2,1},{3,2},{4,7},{5,4},{6,5},{7,6},{8,11},{9,8},{10,9... | collective-permute-start | bytes 589832 | tf_op jit(solution)/shard_map/ppermute | solution.py:229
  41.2 1.0 shard_map.79.side_ref
  42.2 1.8 %collective-permute-done.2.refs_2_ = bf16[64,1536]{1,0:T(8,128)(2,1)S(1)} collective-permute-done((bf16[64,1536]{1,0:T(8,128)(2,1)S(1)}, bf16[64,1536]{1,0:T(8,128)(2,1)S(1)}, u32[]{:S(2)}, u32[]{:S(2)}) %collective-permute-start.2) | collective-permute-done | bytes 196640 | tf_op jit(solution)/shard_map/ppermute | solution.py:229
  44.0 1.7 %collective-permute-done.3.refs_3_ = bf16[64,1536]{1,0:T(8,128)(2,1)S(1)} collective-permute-done((bf16[64,1536]{1,0:T(8,128)(2,1)S(1)}, bf16[64,1536]{1,0:T(8,128)(2,1)S(1)}, u32[]{:S(2)}, u32[]{:S(2)}) %collective-permute-start.3) | collective-permute-done | bytes 196640 | tf_op jit(solution)/shard_map/ppermute | solution.py:229
  45.6 0.9 shard_map.78
  47.2 1.3 %shard_map.80 = bf16[4,8,160,128]{3,2,1,0:T(8,128)(2,1)} custom-call(bf16[16,120,128]{2,1,0:T(8,128)(2,1)S(1)} %all-to-all-done.got_ref, bf16[8,64,128]{2,1,0:T(8,128)(2,1)S(1)} %shard_map.79.side_ref), custom_call_target="tpu_custom_call" | custom-call | flops 1000000 | bytes 1933312 | tf_op jit(solution)/shard_map/pallas_call | solution.py:22
  48.5 11.5 %all-to-all-start.1 = ((bf16[32,160,128]{2,1,0:T(8,128)(2,1)}), bf16[32,160,128]{2,1,0:T(8,128)(2,1)S(1)}, u32[]{:S(2)}, u32[]{:S(2)}) async-start(bf16[32,160,128]{2,1,0:T(8,128)(2,1)} %bitcast), calls=%async_computation.1 | async-start | bytes 2621440 | tf_op jit(solution)/shard_map/all_to_all | solution.py:274
  60.0 2.1 %collective-permute-start.4 = (bf16[128,768]{1,0:T(8,128)(2,1)S(1)}, bf16[128,768]{1,0:T(8,128)(2,1)S(1)}, u32[]{:S(2)}, u32[]{:S(2)}) collective-permute-start(bf16[128,768]{1,0:T(8,128)(2,1)S(1)} %copy-done.8), channel_id=1, source_target_pairs={{0,128},{128,0},{256,384},{384,256},{1,129},{129,1},{257,385},{385... | collective-permute-start | bytes 589832 | tf_op jit(solution)/shard_map/ppermute | solution.py:251
  62.1 1.2 %collective-permute-done.4 = bf16[128,768]{1,0:T(8,128)(2,1)S(1)} collective-permute-done((bf16[128,768]{1,0:T(8,128)(2,1)S(1)}, bf16[128,768]{1,0:T(8,128)(2,1)S(1)}, u32[]{:S(2)}, u32[]{:S(2)}) %collective-permute-start.4) | collective-permute-done | bytes 196640 | tf_op jit(solution)/shard_map/ppermute | solution.py:251
  63.4 2.3 %collective-permute-start.6 = (bf16[128,768]{1,0:T(8,128)(2,1)S(1)}, bf16[128,768]{1,0:T(8,128)(2,1)S(1)}, u32[]{:S(2)}, u32[]{:S(2)}) collective-permute-start(bf16[128,768]{1,0:T(8,128)(2,1)S(1)} %add_convert_fusion.refs_0_), channel_id=1, source_target_pairs={{0,8},{8,16},{16,24},{24,32},{32,40},{40,48},{48,56},{56,64},{64,7... | collective-permute-start | bytes 589832 | tf_op jit(solution)/shard_map/ppermute | solution.py:254
  65.6 4.1 %collective-permute-start.5 = (bf16[128,768]{1,0:T(8,128)(2,1)S(1)}, bf16[128,768]{1,0:T(8,128)(2,1)S(1)}, u32[]{:S(2)}, u32[]{:S(2)}) collective-permute-start(bf16[128,768]{1,0:T(8,128)(2,1)S(1)} %add_convert_fusion.refs_0_), channel_id=1, source_target_pairs={{0,16},{8,24},{16,32},{24,40},{32,48},{40,56},{48,64},{56,72},{64,... | collective-permute-start | bytes 589832 | tf_op jit(solution)/shard_map/ppermute | solution.py:254
  69.8 3.0 %collective-permute-start.7 = (bf16[128,768]{1,0:T(8,128)(2,1)S(1)}, bf16[128,768]{1,0:T(8,128)(2,1)S(1)}, u32[]{:S(2)}, u32[]{:S(2)}) collective-permute-start(bf16[128,768]{1,0:T(8,128)(2,1)S(1)} %add_convert_fusion.refs_0_), channel_id=1, source_target_pairs={{0,120},{8,0},{16,8},{24,16},{32,24},{40,32},{48,40},{56,48},{64,5... | collective-permute-start | bytes 589832 | tf_op jit(solution)/shard_map/ppermute | solution.py:254
  72.7 1.3 %collective-permute-done.6.refs_2_ = bf16[128,768]{1,0:T(8,128)(2,1)S(1)} collective-permute-done((bf16[128,768]{1,0:T(8,128)(2,1)S(1)}, bf16[128,768]{1,0:T(8,128)(2,1)S(1)}, u32[]{:S(2)}, u32[]{:S(2)}) %collective-permute-start.6) | collective-permute-done | bytes 196640 | tf_op jit(solution)/shard_map/ppermute | solution.py:254
  74.0 9.3 %collective-permute-done.5.refs_1_ = bf16[128,768]{1,0:T(8,128)(2,1)S(1)} collective-permute-done((bf16[128,768]{1,0:T(8,128)(2,1)S(1)}, bf16[128,768]{1,0:T(8,128)(2,1)S(1)}, u32[]{:S(2)}, u32[]{:S(2)}) %collective-permute-start.5) | collective-permute-done | bytes 196640 | tf_op jit(solution)/shard_map/ppermute | solution.py:254
  83.3 1.6 %shard_map.81 = bf16[4,96,768]{2,1,0:T(8,128)(2,1)} custom-call(bf16[4,8,160,128]{3,2,1,0:T(8,128)(2,1)S(1)} %bitcast.2, bf16[128,768]{1,0:T(8,128)(2,1)S(1)} %add_convert_fusion.refs_0_, bf16[128,768]{1,0:T(8,128)(2,1)S(1)} %collective-permute-done.5.refs_1_, bf16[128,768]{1,0:T(8,128)(2,1)S(1)} %collective-permute-done.6.refs_2_, ...), custom_call_target="tpu_custom_call" | custom-call | flops 402653184 | bytes 2686976 | tf_op jit(solution)/shard_map/pallas_call | solution.py:22
  84.8 5.5 %all-to-all-start.2 = ((bf16[4,96,768]{2,1,0:T(8,128)(2,1)}), bf16[4,96,768]{2,1,0:T(8,128)(2,1)S(1)}, u32[]{:S(2)}, u32[]{:S(2)}) async-start(bf16[4,96,768]{2,1,0:T(8,128)(2,1)} %shard_map.81), calls=%async_computation.2 | async-start | bytes 1179648 | tf_op jit(solution)/shard_map/all_to_all | solution.py:285
  90.3 3.1 %collective-permute-start.8 = (bf16[64,1536]{1,0:T(8,128)(2,1)S(1)}, bf16[64,1536]{1,0:T(8,128)(2,1)S(1)}, u32[]{:S(2)}, u32[]{:S(2)}) collective-permute-start(bf16[64,1536]{1,0:T(8,128)(2,1)S(1)} %constant_dynamic-update-slice_fusion.refs_0_), channel_id=1, source_target_pairs={{0,1},{1,2},{2,3},{3,0},{4,5},{5,6},{6,7},{7,4},{8,9},{9,10},{10,1... | collective-permute-start | bytes 589832 | tf_op jit(solution)/shard_map/ppermute | solution.py:229
  93.4 4.3 %collective-permute-start.9 = (bf16[64,1536]{1,0:T(8,128)(2,1)S(1)}, bf16[64,1536]{1,0:T(8,128)(2,1)S(1)}, u32[]{:S(2)}, u32[]{:S(2)}) collective-permute-start(bf16[64,1536]{1,0:T(8,128)(2,1)S(1)} %constant_dynamic-update-slice_fusion.refs_0_), channel_id=1, source_target_pairs={{0,2},{1,3},{2,0},{3,1},{4,6},{5,7},{6,4},{7,5},{8,10},{9,11},{10,... | collective-permute-start | bytes 589832 | tf_op jit(solution)/shard_map/ppermute | solution.py:229
  97.8 3.1 %collective-permute-start.10 = (bf16[64,1536]{1,0:T(8,128)(2,1)S(1)}, bf16[64,1536]{1,0:T(8,128)(2,1)S(1)}, u32[]{:S(2)}, u32[]{:S(2)}) collective-permute-start(bf16[64,1536]{1,0:T(8,128)(2,1)S(1)} %constant_dynamic-update-slice_fusion.refs_0_), channel_id=1, source_target_pairs={{0,3},{1,0},{2,1},{3,2},{4,7},{5,4},{6,5},{7,6},{8,11},{9,8},{10,9... | collective-permute-start | bytes 589832 | tf_op jit(solution)/shard_map/ppermute | solution.py:229
  100.9 4.2 %collective-permute-done.9.refs_2_ = bf16[64,1536]{1,0:T(8,128)(2,1)S(1)} collective-permute-done((bf16[64,1536]{1,0:T(8,128)(2,1)S(1)}, bf16[64,1536]{1,0:T(8,128)(2,1)S(1)}, u32[]{:S(2)}, u32[]{:S(2)}) %collective-permute-start.9) | collective-permute-done | bytes 196640 | tf_op jit(solution)/shard_map/ppermute | solution.py:229
  105.1 1.5 %collective-permute-done.10.refs_3_ = bf16[64,1536]{1,0:T(8,128)(2,1)S(1)} collective-permute-done((bf16[64,1536]{1,0:T(8,128)(2,1)S(1)}, bf16[64,1536]{1,0:T(8,128)(2,1)S(1)}, u32[]{:S(2)}, u32[]{:S(2)}) %collective-permute-start.10) | collective-permute-done | bytes 196640 | tf_op jit(solution)/shard_map/ppermute | solution.py:229
  106.6 1.4 %shard_map.82 = (f32[48,1536]{1,0:T(8,128)}, f32[48,1536]{1,0:T(8,128)}) custom-call(bf16[4,8,160,128]{3,2,1,0:T(8,128)(2,1)S(1)} %bitcast.3, bf16[64,1536]{1,0:T(8,128)(2,1)S(1)} %constant_dynamic-update-slice_fusion.refs_0_, bf16[64,1536]{1,0:T(8,128)(2,1)S(1)} %collective-permute-done.8.refs_1_, bf16[64,1536]{1,0:T(8,128)(2,1)S(1)} %collective-permute-done.9.refs_2_, ...), custom_call_target="tpu_custom_call" | custom-call | flops 201326592 | bytes 2686976 | tf_op jit(solution)/shard_map/pallas_call | solution.py:22
  108.0 0.8 convert_reduce_fusion
  (30 shorter events, 2.1 us)
Async XLA Ops:
  0.6 1.3 %copy-start.1 = (bf16[1536,384]{1,0:T(8,128)(2,1)S(1)}, bf16[1536,384]{1,0:T(8,128)(2,1)}, u32[]{:S(2)}) copy-start(bf16[1536,384]{1,0:T(8,128)(2,1)} %a_hbm.1) | copy-start | bytes 3538948
  1.9 0.9 copy-start.3
  2.8 0.7 copy-start.5
  3.5 18.9 %copy-start.2 = (bf16[128,1536]{1,0:T(8,128)(2,1)S(1)}, bf16[128,1536]{1,0:T(8,128)(2,1)}, u32[]{:S(2)}) copy-start(bf16[128,1536]{1,0:T(8,128)(2,1)} %g_ref.1) | copy-start | bytes 1179652
  3.5 18.9 %copy-start.6 = (s32[32]{0:T(128)S(1)}, s32[32]{0:T(128)}, u32[]{:S(2)}) copy-start(s32[32]{0:T(128)} %picks.5) | copy-start | bytes 388
  6.4 34.8 %copy-start.4 = (bf16[128,384]{1,0:T(8,128)(2,1)S(1)}, bf16[128,384]{1,0:T(8,128)(2,1)}, u32[]{:S(2)}) copy-start(bf16[128,384]{1,0:T(8,128)(2,1)} %x_ref.1) | copy-start | bytes 294916
  6.4 39.2 %copy-start = (bf16[1536,768]{1,0:T(8,128)(2,1)S(1)}, bf16[1536,768]{1,0:T(8,128)(2,1)}, u32[]{:S(2)}) copy-start(bf16[1536,768]{1,0:T(8,128)(2,1)} %b_ref.1) | copy-start | bytes 7077892
  6.4 40.8 %all-to-all-start = ((bf16[16,120,128]{2,1,0:T(8,128)(2,1)}), bf16[16,120,128]{2,1,0:T(8,128)(2,1)S(1)}, u32[]{:S(2)}, u32[]{:S(2)}) async-start(bf16[16,120,128]{2,1,0:T(8,128)(2,1)} %shard_map.76), calls=%async_computation | async-start | bytes 983040 | tf_op jit(solution)/shard_map/all_to_all | solution.py:226
  23.1 7.3 %collective-permute-start = (bf16[64,1536]{1,0:T(8,128)(2,1)S(1)}, bf16[64,1536]{1,0:T(8,128)(2,1)S(1)}, u32[]{:S(2)}, u32[]{:S(2)}) collective-permute-start(bf16[64,1536]{1,0:T(8,128)(2,1)S(1)} %shard_map.77.gy_ref), channel_id=1, source_target_pairs={{0,4},{1,5},{2,6},{3,7},{4,0},{5,1},{6,2},{7,3},{8,12},{9,13},{10,... | collective-permute-start | bytes 589832 | tf_op jit(solution)/shard_map/ppermute | solution.py:239
  30.5 11.7 %collective-permute-start.1 = (bf16[64,1536]{1,0:T(8,128)(2,1)S(1)}, bf16[64,1536]{1,0:T(8,128)(2,1)S(1)}, u32[]{:S(2)}, u32[]{:S(2)}) collective-permute-start(bf16[64,1536]{1,0:T(8,128)(2,1)S(1)} %pad_maximum_fusion.refs_0_), channel_id=1, source_target_pairs={{0,1},{1,2},{2,3},{3,0},{4,5},{5,6},{6,7},{7,4},{8,9},{9,10},{10,1... | collective-permute-start | bytes 589832 | tf_op jit(solution)/shard_map/ppermute | solution.py:229
  33.7 10.3 %collective-permute-start.2 = (bf16[64,1536]{1,0:T(8,128)(2,1)S(1)}, bf16[64,1536]{1,0:T(8,128)(2,1)S(1)}, u32[]{:S(2)}, u32[]{:S(2)}) collective-permute-start(bf16[64,1536]{1,0:T(8,128)(2,1)S(1)} %pad_maximum_fusion.refs_0_), channel_id=1, source_target_pairs={{0,2},{1,3},{2,0},{3,1},{4,6},{5,7},{6,4},{7,5},{8,10},{9,11},{10,... | collective-permute-start | bytes 589832 | tf_op jit(solution)/shard_map/ppermute | solution.py:229
  38.2 7.4 %collective-permute-start.3 = (bf16[64,1536]{1,0:T(8,128)(2,1)S(1)}, bf16[64,1536]{1,0:T(8,128)(2,1)S(1)}, u32[]{:S(2)}, u32[]{:S(2)}) collective-permute-start(bf16[64,1536]{1,0:T(8,128)(2,1)S(1)} %pad_maximum_fusion.refs_0_), channel_id=1, source_target_pairs={{0,3},{1,0},{2,1},{3,2},{4,7},{5,4},{6,5},{7,6},{8,11},{9,8},{10,9... | collective-permute-start | bytes 589832 | tf_op jit(solution)/shard_map/ppermute | solution.py:229
  46.5 0.7 copy-start.7
  48.5 11.5 %copy-start.8 = (bf16[128,768]{1,0:T(8,128)(2,1)S(1)}, bf16[128,768]{1,0:T(8,128)(2,1)}, u32[]{:S(2)}) copy-start(bf16[128,768]{1,0:T(8,128)(2,1)} %copy-done.7) | copy-start | bytes 589828
  48.5 25.5 %copy-start.9 = (bf16[32,1536]{1,0:T(8,128)(2,1)S(1)}, bf16[32,1536]{1,0:T(8,128)(2,1)}, u32[]{:S(2)}) copy-start(bf16[32,1536]{1,0:T(8,128)(2,1)} %get-tuple-element.15) | copy-start | bytes 294916
  48.5 34.8 %all-to-all-start.1 = ((bf16[32,160,128]{2,1,0:T(8,128)(2,1)}), bf16[32,160,128]{2,1,0:T(8,128)(2,1)S(1)}, u32[]{:S(2)}, u32[]{:S(2)}) async-start(bf16[32,160,128]{2,1,0:T(8,128)(2,1)} %bitcast), calls=%async_computation.1 | async-start | bytes 2621440 | tf_op jit(solution)/shard_map/all_to_all | solution.py:274
  60.0 3.3 %collective-permute-start.4 = (bf16[128,768]{1,0:T(8,128)(2,1)S(1)}, bf16[128,768]{1,0:T(8,128)(2,1)S(1)}, u32[]{:S(2)}, u32[]{:S(2)}) collective-permute-start(bf16[128,768]{1,0:T(8,128)(2,1)S(1)} %copy-done.8), channel_id=1, source_target_pairs={{0,128},{128,0},{256,384},{384,256},{1,129},{129,1},{257,385},{385... | collective-permute-start | bytes 589832 | tf_op jit(solution)/shard_map/ppermute | solution.py:251
  63.4 10.6 %collective-permute-start.6 = (bf16[128,768]{1,0:T(8,128)(2,1)S(1)}, bf16[128,768]{1,0:T(8,128)(2,1)S(1)}, u32[]{:S(2)}, u32[]{:S(2)}) collective-permute-start(bf16[128,768]{1,0:T(8,128)(2,1)S(1)} %add_convert_fusion.refs_0_), channel_id=1, source_target_pairs={{0,8},{8,16},{16,24},{24,32},{32,40},{40,48},{48,56},{56,64},{64,7... | collective-permute-start | bytes 589832 | tf_op jit(solution)/shard_map/ppermute | solution.py:254
  65.6 17.6 %collective-permute-start.5 = (bf16[128,768]{1,0:T(8,128)(2,1)S(1)}, bf16[128,768]{1,0:T(8,128)(2,1)S(1)}, u32[]{:S(2)}, u32[]{:S(2)}) collective-permute-start(bf16[128,768]{1,0:T(8,128)(2,1)S(1)} %add_convert_fusion.refs_0_), channel_id=1, source_target_pairs={{0,16},{8,24},{16,32},{24,40},{32,48},{40,56},{48,64},{56,72},{64,... | collective-permute-start | bytes 589832 | tf_op jit(solution)/shard_map/ppermute | solution.py:254
  69.8 13.5 %collective-permute-start.7 = (bf16[128,768]{1,0:T(8,128)(2,1)S(1)}, bf16[128,768]{1,0:T(8,128)(2,1)S(1)}, u32[]{:S(2)}, u32[]{:S(2)}) collective-permute-start(bf16[128,768]{1,0:T(8,128)(2,1)S(1)} %add_convert_fusion.refs_0_), channel_id=1, source_target_pairs={{0,120},{8,0},{16,8},{24,16},{32,24},{40,32},{48,40},{56,48},{64,5... | collective-permute-start | bytes 589832 | tf_op jit(solution)/shard_map/ppermute | solution.py:254
  84.8 23.2 %all-to-all-start.2 = ((bf16[4,96,768]{2,1,0:T(8,128)(2,1)}), bf16[4,96,768]{2,1,0:T(8,128)(2,1)S(1)}, u32[]{:S(2)}, u32[]{:S(2)}) async-start(bf16[4,96,768]{2,1,0:T(8,128)(2,1)} %shard_map.81), calls=%async_computation.2 | async-start | bytes 1179648 | tf_op jit(solution)/shard_map/all_to_all | solution.py:285
  90.3 10.5 %collective-permute-start.8 = (bf16[64,1536]{1,0:T(8,128)(2,1)S(1)}, bf16[64,1536]{1,0:T(8,128)(2,1)S(1)}, u32[]{:S(2)}, u32[]{:S(2)}) collective-permute-start(bf16[64,1536]{1,0:T(8,128)(2,1)S(1)} %constant_dynamic-update-slice_fusion.refs_0_), channel_id=1, source_target_pairs={{0,1},{1,2},{2,3},{3,0},{4,5},{5,6},{6,7},{7,4},{8,9},{9,10},{10,1... | collective-permute-start | bytes 589832 | tf_op jit(solution)/shard_map/ppermute | solution.py:229
  93.4 11.7 %collective-permute-start.9 = (bf16[64,1536]{1,0:T(8,128)(2,1)S(1)}, bf16[64,1536]{1,0:T(8,128)(2,1)S(1)}, u32[]{:S(2)}, u32[]{:S(2)}) collective-permute-start(bf16[64,1536]{1,0:T(8,128)(2,1)S(1)} %constant_dynamic-update-slice_fusion.refs_0_), channel_id=1, source_target_pairs={{0,2},{1,3},{2,0},{3,1},{4,6},{5,7},{6,4},{7,5},{8,10},{9,11},{10,... | collective-permute-start | bytes 589832 | tf_op jit(solution)/shard_map/ppermute | solution.py:229
  97.8 8.8 %collective-permute-start.10 = (bf16[64,1536]{1,0:T(8,128)(2,1)S(1)}, bf16[64,1536]{1,0:T(8,128)(2,1)S(1)}, u32[]{:S(2)}, u32[]{:S(2)}) collective-permute-start(bf16[64,1536]{1,0:T(8,128)(2,1)S(1)} %constant_dynamic-update-slice_fusion.refs_0_), channel_id=1, source_target_pairs={{0,3},{1,0},{2,1},{3,2},{4,7},{5,4},{6,5},{7,6},{8,11},{9,8},{10,9... | collective-permute-start | bytes 589832 | tf_op jit(solution)/shard_map/ppermute | solution.py:229

commit v10 on v9

v10 whole, which is shorter than its diff:
```python
import functools

import jax
import jax.numpy as jnp
from jax import lax
from jax.experimental import pallas as pl
from jax.experimental.pallas import tpu as pltpu
from jax.sharding import PartitionSpec as P

BF = jnp.bfloat16
F32 = jnp.float32
LANES = 128
FIRST = (((0,), (0,)), ((), ()))
LAST = (((1,), (1,)), ((), ()))
SMEM = pl.BlockSpec(memory_space=pltpu.SMEM)
VMEM = pl.BlockSpec(memory_space=pltpu.VMEM)
SHIFTS = (0, 2, 1, -1)


def call(kernel, inputs, outs, flops, scratch=(), place=VMEM, limit=40):
    moved = sum(x.size * x.dtype.itemsize for x in list(inputs) + list(outs))
    return pl.pallas_call(
        kernel,
        out_shape=outs,
        in_specs=[SMEM if x.dtype == jnp.int32 else place for x in inputs],
        out_specs=[VMEM] * len(outs),
        scratch_shapes=list(scratch),
        compiler_params=pltpu.CompilerParams(vmem_limit_bytes=limit * 1024 * 1024),
        cost_estimate=pl.CostEstimate(flops=flops, bytes_accessed=moved, transcendentals=0),
    )(*inputs)


def source_of(k):
    col = lax.axis_index("col")
    return 4 * ((col // 4) ^ (k % 2)) + lax.rem(col % 4 - k // 2 + 4, 4)


def own_picks(picks, count, tok):
    begin = lax.axis_index("grp") * count
    first = lax.axis_index("col") * tok
    return [picks[begin + i] - first for i in range(count)]


def rows_hot(targets, tok):
    shape = (len(targets), tok)
    sub = lax.broadcasted_iota(jnp.int32, shape, 0)
    lane = lax.broadcasted_iota(jnp.int32, shape, 1)
    want = jnp.zeros(shape, jnp.int32)
    for i, target in enumerate(targets):
        want = jnp.where(sub == i, target, want)
    return jnp.where(want == lane, 1.0, 0.0).astype(BF)


def first_kernel(picks, x_hbm, a_hbm, out_ref, x_ref, a_ref, sems):
    n_row, depth, tok = out_ref.shape
    parts = sems.shape[0] - 1
    step = a_ref.shape[0] // parts
    copies = [pltpu.make_async_copy(x_hbm, x_ref, sems.at[parts])]
    for p in range(parts):
        span = pl.ds(p * step, step)
        copies.append(pltpu.make_async_copy(a_hbm.at[span], a_ref.at[span], sems.at[p]))
    for copy in copies:
        copy.start()
    out_rows = a_ref.shape[0] // n_row
    quarter = picks.shape[0] // 4
    hot = rows_hot(own_picks(picks, quarter, tok), tok)
    copies[0].wait()
    chosen = jnp.dot(hot, x_ref[...], preferred_element_type=F32)
    strips = [chosen[:, k : k + LANES] for k in range(0, chosen.shape[1], LANES)]
    block = jnp.concatenate(strips, axis=0).astype(BF)
    out_ref[:, out_rows:, :] = jnp.broadcast_to(block[None], (n_row,) + block.shape)
    each = step // out_rows
    for p in range(parts):
        copies[p + 1].wait()
        rows = a_ref[p * step : (p + 1) * step, :]
        part = lax.dot_general(rows, x_ref[...], LAST, preferred_element_type=F32)
        out_ref[p * each : (p + 1) * each, :out_rows, :] = part.astype(BF).reshape(
            each, out_rows, tok
        )


def pick_kernel(picks, g_ref, out_ref):
    tok = g_ref.shape[0]
    samp = picks.shape[0]
    plane = lax.axis_index("row") % 4
    first = lax.axis_index("col") * tok
    count = out_ref.shape[0] - samp
    ours = [64 * (i // 16) + 16 * plane + i % 16 for i in range(count)]
    hot = rows_hot(ours + [picks[i] - first for i in range(samp)], tok)
    out_ref[...] = jnp.dot(hot, g_ref[...], preferred_element_type=F32).astype(BF)


def right_kernel(b_ref, gy_ref, *refs):
    blocks, keep_ref, give_ref, held = refs[:-3], refs[-3], refs[-2], refs[-1]
    n_blk, unused, size, width = held.shape
    rows = jnp.concatenate([block[...] for block in blocks], axis=0)
    term = jnp.dot(rows, b_ref[...], preferred_element_type=F32)
    held[...] = term.reshape(held.shape)
    core = lax.axis_index("grp") % 2
    cut = n_blk * size
    keep_ref[:cut, :] = held[:, core].reshape(cut, width)
    give_ref[:cut, :] = held[:, 1 - core].reshape(cut, width).astype(BF)
    feat = width // 2
    samp = 2 * (give_ref.shape[0] - cut)
    begin = pl.multiple_of((lax.axis_index("row") % 4) * feat, LANES)
    own = gy_ref[gy_ref.shape[0] - samp :, pl.ds(begin, feat)]
    own = jnp.concatenate([own[: samp // 2], own[samp // 2 :]], axis=1)
    keep_ref[cut:, :] = own.astype(F32)
    give_ref[cut:, :] = own


def gather_kernel(got_ref, u_ref, x_ref):
    n_grp, x_rows, unused = x_ref.shape
    n_row, depth, tok = got_ref.shape
    out_rows = u_ref.shape[0]
    total = got_ref[0, :out_rows, :].astype(F32)
    for r in range(1, n_row):
        total = total + got_ref[r, :out_rows, :].astype(F32)
    u_ref[...] = total.astype(BF)
    per = n_row // n_grp
    for g in range(n_grp):
        block = got_ref[g * per : (g + 1) * per, out_rows:, :].astype(F32)
        x_ref[g] = block.reshape(x_rows, tok).astype(BF)


def second_kernel(picks, u_ref, x_ref, y_ref, tokens_ref, out_ref):
    n_col, depth, unused = out_ref.shape
    out_rows, tok = u_ref.shape
    feat = tokens_ref.shape[1]
    samp = picks.shape[0]
    tile = feat // n_col
    begin = lax.axis_index("col") * tok
    hot = rows_hot([picks[i] - begin for i in range(samp)], tok)
    chosen = jnp.dot(hot, tokens_ref[...], preferred_element_type=F32)
    own = y_ref[...].astype(F32)
    own = jnp.concatenate([own[:, :feat], own[:, feat:]], axis=0)
    empty = jnp.zeros((samp, LANES - 2 * tile), F32)
    u_block = u_ref[...]
    x_block = x_ref[...].reshape(x_ref.shape[0] * x_ref.shape[1], LANES)
    for c in range(n_col):
        span = slice(c * tile, (c + 1) * tile)
        out_ref[c, :out_rows, :] = u_block
        out_ref[c, out_rows : depth - samp, :] = x_block
        side = jnp.concatenate([own[:, span], chosen[:, span], empty], axis=1)
        out_ref[c, depth - samp :, :] = side.astype(BF)


def final_kernel(got_ref, pair_ref, *refs):
    v_refs, out_ref, held = refs[:-2], refs[-2], refs[-1]
    n_col, unused, spread, size, width = held.shape
    out_rows = out_ref.shape[0]
    row = lax.axis_index("row")
    core = lax.axis_index("grp") % 2
    cut = n_col * size
    for j, shift in enumerate(SHIFTS):
        plane = lax.rem(row - shift + spread, spread)
        for k in range(n_col):
            span = slice(k * size, (k + 1) * size)
            held[source_of(k), core, plane] = v_refs[j][span, :]
            span = slice(j * cut + k * size, j * cut + (k + 1) * size)
            held[source_of(k), 1 - core, plane] = pair_ref[span, :]
    tokens = 2 * spread * size
    total = None
    for c in range(0, n_col, 2):
        left = jnp.concatenate([got_ref[c, :out_rows, :], got_ref[c + 1, :out_rows, :]], axis=1)
        right = held[c : c + 2].reshape(2 * tokens, width)
        term = jnp.dot(left, right, preferred_element_type=F32)
        total = term if total is None else total + term
    out_ref[...] = total


def factor_kernel(got_ref, *refs):
    blocks, act_ref, grad_ref = refs[:-2], refs[-2], refs[-1]
    n_col, depth, unused = got_ref.shape
    tile, width = act_ref.shape
    samp = blocks[0].shape[0] // 2
    quarter = samp // 4
    total = samp * n_col
    scale = 1.0 / total
    count = 4 * quarter * (width // LANES)
    span = got_ref[:, depth - samp - count : depth - samp, :].astype(F32)
    span = span.reshape(n_col, 4, count // 4, LANES)
    strips = []
    for t in range(width // LANES):
        strip = span[:, :, t * quarter : (t + 1) * quarter, :].reshape(total, LANES)
        strips.append(strip.astype(BF))
    right = jnp.concatenate(strips, axis=1)
    left = got_ref[:, depth - samp :, :].reshape(total, LANES)
    term = lax.dot_general(left, right, FIRST, preferred_element_type=F32)
    act_ref[...] = term[tile : 2 * tile] * scale
    sides = [got_ref[source_of(k), depth - samp :, :] for k in range(n_col)]
    left = jnp.concatenate(sides, axis=0)
    right = jnp.concatenate([block[...] for block in blocks], axis=0)
    term = lax.dot_general(left, right, FIRST, preferred_element_type=F32)
    grad_ref[...] = term[:tile] * scale


def body(tokens_in, cotangent, sample_rows, act_inverse, grad_inverse):
    n_row = lax.axis_size("row")
    n_col = lax.axis_size("col")
    n_grp = lax.axis_size("grp")
    tok, feat_row = tokens_in.shape
    feat_grp = cotangent.shape[1]
    width = grad_inverse.shape[1]
    samp = sample_rows.shape[0]
    quarter = samp // n_grp
    tile = feat_row // n_col
    out_rows = feat_grp // n_row
    strip = quarter * feat_row // LANES
    spread = 4
    size = tok // 2 // spread
    shape = jax.ShapeDtypeStruct

    picked = call(
        pick_kernel,
        (sample_rows, cotangent),
        [shape((2 * size + samp, feat_grp), BF)],
        2 * 64 * tok * feat_grp,
    )[0]
    beside = lax.ppermute(picked, "col", [(i, (i + 4) % n_col) for i in range(n_col)])
    picked, x_in = lax.optimization_barrier((picked, tokens_in))
    payload = call(
        first_kernel,
        (sample_rows, x_in, act_inverse),
        [shape((n_row, out_rows + strip, tok), BF)],
        2 * feat_grp * feat_row * tok,
        [
            pltpu.VMEM(tokens_in.shape, BF),
            pltpu.VMEM(act_inverse.shape, BF),
            pltpu.SemaphoreType.DMA((5,)),
        ],
        pl.BlockSpec(memory_space=pl.ANY),
        limit=56,
    )[0]
    first = lax.all_to_all(payload, "row", 0, 0)

    def along_y(block, k):
        return lax.ppermute(
            block, "col", [(i, i - i % 4 + (i + k) % 4) for i in range(n_col)]
        )

    cut = 2 * size
    pair = jnp.concatenate([picked[:cut], beside[:cut]], axis=0)
    pairs = [pair] + [along_y(pair, k) for k in range(1, 4)]
    half = n_col * size
    extra = samp // 2
    keep, give = call(
        right_kernel,
        (grad_inverse, picked, *pairs),
        [shape((half + extra, width), F32), shape((half + extra, width), BF)],
        4 * n_col * size * feat_grp * width,
        [pltpu.VMEM((n_col, 2, size, width), F32)],
    )
    first, unused = lax.optimization_barrier((first, give))

    owner = lax.axis_index("row") // 4
    grp = lax.axis_index("grp")
    taken = lax.ppermute(give, "grp", [(i, i ^ 1) for i in range(n_grp)]).astype(F32)
    own_y = jnp.where(grp % 2 == owner % 2, keep[half:], taken[half:])
    keep = jnp.concatenate([keep[:half] + taken[:half], own_y], axis=0)
    taken = lax.ppermute(keep.astype(BF), "grp", [(i, i ^ 2) for i in range(n_grp)]).astype(F32)
    own_y = jnp.where(grp // 2 == owner // 2, keep[half:], taken[half:]).astype(BF)
    right = (keep[:half] + taken[:half]).astype(BF)
    rights = [right] + [
        lax.ppermute(right, "row", [(i, (i + j) % n_row) for i in range(n_row)])
        for j in SHIFTS[1:]
    ]
    other = lax.ppermute(
        jnp.concatenate(rights, axis=0), "grp", [(i, i ^ 1) for i in range(n_grp)]
    )

    unused, picked_y, beside_y = lax.optimization_barrier((keep, picked[cut:], beside[cut:]))
    samples = jnp.concatenate([picked_y, beside_y], axis=0)
    samples = [samples] + [along_y(samples, k) for k in range(1, 4)]

    u_own, x_send = call(
        gather_kernel,
        (first,),
        [shape((out_rows, tok), BF), shape((n_grp, strip * n_row // n_grp, LANES), BF)],
        1000000,
    )
    x_got = lax.all_to_all(x_send, "grp", 0, 0)
    send = call(
        second_kernel,
        (sample_rows, u_own, x_got, own_y, tokens_in),
        [shape((n_col, out_rows + strip * n_row + samp, LANES), BF)],
        2 * samp * tok * feat_row,
    )[0]
    got = lax.all_to_all(send, "col", 0, 0)

    precond = call(
        final_kernel,
        (got, other, *rights),
        [shape((out_rows, width), F32)],
        2 * out_rows * n_col * tok * width,
        [pltpu.VMEM((n_col, 2, spread, size, width), BF)],
    )[0]
    act_cov, grad_cov = call(
        factor_kernel,
        (got, *samples),
        [shape((tile, feat_grp), F32)] * 2,
        4 * LANES * samp * n_col * feat_grp,
    )
    return (precond, act_cov, grad_cov)


def solution(mesh):
    return jax.shard_map(
        body,
        mesh=mesh,
        in_specs=(P("col", "row"), P("col", "grp"), P("col"), P("grp", "row"), P("grp", "col")),
        out_specs=(P(("grp", "row"), "col"), P(("row", "col"), "grp"), P(("row", "col"), "grp")),
        check_vma=False,
    )
```

time: 110 us -> 112 us (1.018)
  starting transfers between devices: 68.6 us -> 72.1 us
  local copies, waits for them, and re-layouts: 4.19 us -> 3 us
    ppermute x3, waiting for transfers between devices: 10.5 us -> 0.01 us  [body(): lax.ppermute(right, 'row', [(i, (i + j) % n_row) for i in range(n_row)])]
    ppermute x1 -> x3, starting transfers between devices: 2.14 us -> 11.6 us  [the longest x1 4.37 us: body(): lax.ppermute(give, 'grp', [(i, i ^ 1) for i in range(n_grp)]).astype(F32)]
    all_to_all x2, starting transfers between devices: 17 us -> 10.1 us  [the longest x1 6.04 us: body(): x_got = lax.all_to_all(x_send, 'grp', 0, 0)]
    all_to_all x2, waiting for transfers between devices: 0.01 us -> 5.98 us  [the longest x1 5.14 us: body(): x_got = lax.all_to_all(x_send, 'grp', 0, 0)]
    ppermute x1 -> x3, waiting for transfers between devices: 1.19 us -> 6.88 us  [the longest x1 5.64 us: body(): lax.ppermute(keep.astype(BF), 'grp', [(i, i ^ 2) for i in range(n_grp)])]
    ppermute x1, waiting for transfers between devices: 3.57 us -> 0.01 us  [body(): lax.ppermute(picked, 'col', [(i, (i + 4) % n_col) for i in range(n_col)])]
    unnamed x21 -> x15, local copies, waits for them, and re-layouts: 3.52 us -> 1.68 us
    ppermute x6, waiting for transfers between devices: 9.11 us -> 10.6 us  [along_y(): lax.ppermute(block, 'col', [(i, i - i % 4 + (i + k) % 4) for i in range(n...]
  transfers between devices with their start and end apart: 14 -> 16, of which waited for: 8 -> 8; matrix products, arithmetic and copies ran while one was open for 1% -> 1% of each run, Pallas kernels for 4% -> 8%
where the time goes in v10:
time: 112 us; the launch traced here: 110 us
  starting transfers between devices  72.1 us (64%)
  waiting for transfers between devices  23.4 us (21%)
  Pallas kernels  10.7 us (10%)
  local copies, waits for them, and re-layouts  3 us (3%)
    ppermute x6, starting transfers between devices, along_y(): lax.ppermute(block, 'col', [(i, i - i % 4 + (i + k) % 4) for i in range(n...  21.7 us
    all_to_all x1, starting transfers between devices, body(): first = lax.all_to_all(payload, 'row', 0, 0)  14.9 us
    pallas_call x7, Pallas kernels, call(): pl.pallas_call(kernel, out_shape=outs, in_specs=[SMEM if x.dtype == jnp.i...  10.7 us
    ppermute x6, waiting for transfers between devices, along_y(): lax.ppermute(block, 'col', [(i, i - i % 4 + (i + k) % 4) for i in range(n...  10.6 us
    ppermute x3, starting transfers between devices, body(): lax.ppermute(right, 'row', [(i, (i + j) % n_row) for i in range(n_row)])  9.63 us
    all_to_all x1, starting transfers between devices, body(): x_got = lax.all_to_all(x_send, 'grp', 0, 0)  6.04 us
    ppermute x1, waiting for transfers between devices, body(): lax.ppermute(keep.astype(BF), 'grp', [(i, i ^ 2) for i in range(n_grp)])  5.64 us
    all_to_all x1, waiting for transfers between devices, body(): x_got = lax.all_to_all(x_send, 'grp', 0, 0)  5.14 us
  transfers between devices with their start and end apart: 16, of which 8 were waited for; matrix products, arithmetic and copies ran while one was open for 1% of the time, Pallas kernels for 8%

profile of v10, /device:TPU:1, one launch (start us, length us, event | category | flops | bytes accessed | tf_op | source)
XLA Modules:
  0.0 110.5 jit_solution(1433974529193479638)
XLA Ops:
  0.6 1.0 copy-done.1
  2.3 0.7 shard_map.76.gy_ref
  3.0 4.1 %collective-permute-start = (bf16[64,1536]{1,0:T(8,128)(2,1)S(1)}, bf16[64,1536]{1,0:T(8,128)(2,1)S(1)}, u32[]{:S(2)}, u32[]{:S(2)}) collective-permute-start(bf16[64,1536]{1,0:T(8,128)(2,1)S(1)} %shard_map.76.gy_ref), channel_id=1, source_target_pairs={{0,4},{1,5},{2,6},{3,7},{4,0},{5,1},{6,2},{7,3},{8,12},{9,13},{10,... | collective-permute-start | bytes 589832 | tf_op jit(solution)/shard_map/ppermute | solution.py:220
  7.1 3.6 %shard_map.77 = bf16[16,120,128]{2,1,0:T(8,128)(2,1)} custom-call(s32[32]{0:T(128)} %picks.5, bf16[128,384]{1,0:T(8,128)(2,1)} %tokens_ref.1, bf16[1536,384]{1,0:T(8,128)(2,1)} %a_hbm.1), custom_call_target="tpu_custom_call" | custom-call | flops 150994944 | bytes 1769600 | tf_op jit(solution)/shard_map/pallas_call | solution.py:22
  10.7 14.9 %all-to-all-start = ((bf16[16,120,128]{2,1,0:T(8,128)(2,1)}), bf16[16,120,128]{2,1,0:T(8,128)(2,1)S(1)}, u32[]{:S(2)}, u32[]{:S(2)}) async-start(bf16[16,120,128]{2,1,0:T(8,128)(2,1)} %shard_map.77), calls=%async_computation | async-start | bytes 983040 | tf_op jit(solution)/shard_map/all_to_all | solution.py:235
  27.0 3.2 %collective-permute-start.1 = (bf16[64,1536]{1,0:T(8,128)(2,1)S(1)}, bf16[64,1536]{1,0:T(8,128)(2,1)S(1)}, u32[]{:S(2)}, u32[]{:S(2)}) collective-permute-start(bf16[64,1536]{1,0:T(8,128)(2,1)S(1)} %pad_maximum_fusion.2.refs_0_), channel_id=1, source_target_pairs={{0,1},{1,2},{2,3},{3,0},{4,5},{5,6},{6,7},{7,4},{8,9},{9,10},{10,1... | collective-permute-start | bytes 589832 | tf_op jit(solution)/shard_map/ppermute | solution.py:238
  30.2 4.5 %collective-permute-start.2 = (bf16[64,1536]{1,0:T(8,128)(2,1)S(1)}, bf16[64,1536]{1,0:T(8,128)(2,1)S(1)}, u32[]{:S(2)}, u32[]{:S(2)}) collective-permute-start(bf16[64,1536]{1,0:T(8,128)(2,1)S(1)} %pad_maximum_fusion.2.refs_0_), channel_id=1, source_target_pairs={{0,2},{1,3},{2,0},{3,1},{4,6},{5,7},{6,4},{7,5},{8,10},{9,11},{10,... | collective-permute-start | bytes 589832 | tf_op jit(solution)/shard_map/ppermute | solution.py:238
  34.7 3.0 %collective-permute-start.3 = (bf16[64,1536]{1,0:T(8,128)(2,1)S(1)}, bf16[64,1536]{1,0:T(8,128)(2,1)S(1)}, u32[]{:S(2)}, u32[]{:S(2)}) collective-permute-start(bf16[64,1536]{1,0:T(8,128)(2,1)S(1)} %pad_maximum_fusion.2.refs_0_), channel_id=1, source_target_pairs={{0,3},{1,0},{2,1},{3,2},{4,7},{5,4},{6,5},{7,6},{8,11},{9,8},{10,9... | collective-permute-start | bytes 589832 | tf_op jit(solution)/shard_map/ppermute | solution.py:238
  37.7 3.0 %collective-permute-done.2.refs_2_ = bf16[64,1536]{1,0:T(8,128)(2,1)S(1)} collective-permute-done((bf16[64,1536]{1,0:T(8,128)(2,1)S(1)}, bf16[64,1536]{1,0:T(8,128)(2,1)S(1)}, u32[]{:S(2)}, u32[]{:S(2)}) %collective-permute-start.2) | collective-permute-done | bytes 196640 | tf_op jit(solution)/shard_map/ppermute | solution.py:238
  40.7 1.0 collective-permute-done.3.refs_3_
  41.7 1.6 %shard_map.78 = (f32[144,768]{1,0:T(8,128)S(1)}, bf16[144,768]{1,0:T(8,128)(2,1)}) custom-call(bf16[1536,768]{1,0:T(8,128)(2,1)S(1)} %copy-done, bf16[64,1536]{1,0:T(8,128)(2,1)S(1)} %shard_map.76.gy_ref, bf16[64,1536]{1,0:T(8,128)(2,1)S(1)} %pad_maximum_fusion.2.refs_0_, bf16[64,1536]{1,0:T(8,128)(2,1)S(1)} %collective-permute-done.1.refs_1_, ...), custom_call_target="tpu_custom_call" | custom-call | flops 603979776 | bytes 4005888 | tf_op jit(solution)/shard_map/pallas_call | solution.py:22
  43.3 4.4 %collective-permute-start.4 = (bf16[144,768]{1,0:T(8,128)(2,1)}, bf16[144,768]{1,0:T(8,128)(2,1)S(1)}, u32[]{:S(2)}, u32[]{:S(2)}) collective-permute-start(bf16[144,768]{1,0:T(8,128)(2,1)} %get-tuple-element.16), channel_id=1, source_target_pairs={{0,128},{128,0},{256,384},{384,256},{1,129},{129,1},{257,385},{385... | collective-permute-start | bytes 663560 | tf_op jit(solution)/shard_map/ppermute | solution.py:258
  47.7 1.2 %collective-permute-done.4 = bf16[144,768]{1,0:T(8,128)(2,1)S(1)} collective-permute-done((bf16[144,768]{1,0:T(8,128)(2,1)}, bf16[144,768]{1,0:T(8,128)(2,1)S(1)}, u32[]{:S(2)}, u32[]{:S(2)}) %collective-permute-start.4) | collective-permute-done | bytes 221216 | tf_op jit(solution)/shard_map/ppermute | solution.py:258
  49.1 4.4 %collective-permute-start.5 = (bf16[144,768]{1,0:T(8,128)(2,1)S(1)}, bf16[144,768]{1,0:T(8,128)(2,1)S(1)}, u32[]{:S(2)}, u32[]{:S(2)}) collective-permute-start(bf16[144,768]{1,0:T(8,128)(2,1)S(1)} %fusion.2), channel_id=1, source_target_pairs={{0,256},{128,384},{256,0},{384,128},{1,257},{129,385},{257,1},{385... | collective-permute-start | bytes 663560 | tf_op jit(solution)/shard_map/ppermute | solution.py:261
  53.5 5.6 %collective-permute-done.5 = bf16[144,768]{1,0:T(8,128)(2,1)S(1)} collective-permute-done((bf16[144,768]{1,0:T(8,128)(2,1)S(1)}, bf16[144,768]{1,0:T(8,128)(2,1)S(1)}, u32[]{:S(2)}, u32[]{:S(2)}) %collective-permute-start.5) | collective-permute-done | bytes 221216 | tf_op jit(solution)/shard_map/ppermute | solution.py:261
  59.3 4.7 %collective-permute-start.8 = (bf16[128,768]{1,0:T(8,128)(2,1)S(1)}, bf16[128,768]{1,0:T(8,128)(2,1)S(1)}, u32[]{:S(2)}, u32[]{:S(2)}) collective-permute-start(bf16[128,768]{1,0:T(8,128)(2,1)S(1)} %fusion.refs_0_), channel_id=1, source_target_pairs={{0,120},{8,0},{16,8},{24,16},{32,24},{40,32},{48,40},{56,48},{64,5... | collective-permute-start | bytes 589832 | tf_op jit(solution)/shard_map/ppermute | solution.py:265
  63.9 1.9 %collective-permute-start.7 = (bf16[128,768]{1,0:T(8,128)(2,1)S(1)}, bf16[128,768]{1,0:T(8,128)(2,1)S(1)}, u32[]{:S(2)}, u32[]{:S(2)}) collective-permute-start(bf16[128,768]{1,0:T(8,128)(2,1)S(1)} %fusion.refs_0_), channel_id=1, source_target_pairs={{0,8},{8,16},{16,24},{24,32},{32,40},{40,48},{48,56},{56,64},{64,7... | collective-permute-start | bytes 589832 | tf_op jit(solution)/shard_map/ppermute | solution.py:265
  65.9 3.0 %collective-permute-start.6 = (bf16[128,768]{1,0:T(8,128)(2,1)S(1)}, bf16[128,768]{1,0:T(8,128)(2,1)S(1)}, u32[]{:S(2)}, u32[]{:S(2)}) collective-permute-start(bf16[128,768]{1,0:T(8,128)(2,1)S(1)} %fusion.refs_0_), channel_id=1, source_target_pairs={{0,16},{8,24},{16,32},{24,40},{32,48},{40,56},{48,64},{56,72},{64,... | collective-permute-start | bytes 589832 | tf_op jit(solution)/shard_map/ppermute | solution.py:265
  68.9 0.7 shard_map.79
  69.6 6.0 %all-to-all-start.1 = ((bf16[4,96,128]{2,1,0:T(8,128)(2,1)}), bf16[4,96,128]{2,1,0:T(8,128)(2,1)S(1)}, u32[]{:S(2)}, u32[]{:S(2)}) async-start(bf16[4,96,128]{2,1,0:T(8,128)(2,1)} %get-tuple-element.19), calls=%async_computation.1 | async-start | bytes 196608 | tf_op jit(solution)/shard_map/all_to_all | solution.py:282
  75.6 5.1 %all-to-all-done.1.x_ref = bf16[4,96,128]{2,1,0:T(8,128)(2,1)S(1)} async-done(((bf16[4,96,128]{2,1,0:T(8,128)(2,1)}), bf16[4,96,128]{2,1,0:T(8,128)(2,1)S(1)}, u32[]{:S(2)}, u32[]{:S(2)}) %all-to-all-start.1) | async-done | bytes 98336 | tf_op jit(solution)/shard_map/all_to_all | solution.py:282
  80.8 1.8 %shard_map.80 = bf16[8,512,128]{2,1,0:T(8,128)(2,1)} custom-call(s32[32]{0:T(128)S(1)} %copy-done.4, bf16[96,128]{1,0:T(8,128)(2,1)S(1)} %get-tuple-element.18.u_ref, bf16[4,96,128]{2,1,0:T(8,128)(2,1)S(1)} %all-to-all-done.1.x_ref, bf16[16,768]{1,0:T(8,128)(2,1)S(1)} %fusion.1.y_ref, bf16[128,384]{1,0:T(8,128)(2,1)S(1)} %copy-done.2), custom_call_target="tpu_custom_call" | custom-call | flops 3145728 | bytes 1294464 | tf_op jit(solution)/shard_map/pallas_call | solution.py:22
  82.6 4.1 %all-to-all-start.2 = ((bf16[8,512,128]{2,1,0:T(8,128)(2,1)}), bf16[8,512,128]{2,1,0:T(8,128)(2,1)S(1)}, u32[]{:S(2)}, u32[]{:S(2)}) async-start(bf16[8,512,128]{2,1,0:T(8,128)(2,1)} %shard_map.80), calls=%async_computation.2 | async-start | bytes 2097152 | tf_op jit(solution)/shard_map/all_to_all | solution.py:289
  86.7 2.8 %collective-permute-start.9 = (bf16[512,768]{1,0:T(8,128)(2,1)S(1)}, bf16[512,768]{1,0:T(8,128)(2,1)S(1)}, u32[]{:S(2)}, u32[]{:S(2)}) collective-permute-start(bf16[512,768]{1,0:T(8,128)(2,1)S(1)} %pad_maximum_fusion), channel_id=1, source_target_pairs={{0,128},{128,0},{256,384},{384,256},{1,129},{129,1},{257,385},{385... | collective-permute-start | bytes 2359304 | tf_op jit(solution)/shard_map/ppermute | solution.py:268
  89.6 3.6 %collective-permute-start.10 = (bf16[64,1536]{1,0:T(8,128)(2,1)S(1)}, bf16[64,1536]{1,0:T(8,128)(2,1)S(1)}, u32[]{:S(2)}, u32[]{:S(2)}) collective-permute-start(bf16[64,1536]{1,0:T(8,128)(2,1)S(1)} %constant_dynamic-update-slice_fusion.refs_0_), channel_id=1, source_target_pairs={{0,1},{1,2},{2,3},{3,0},{4,5},{5,6},{6,7},{7,4},{8,9},{9,10},{10,1... | collective-permute-start | bytes 589832 | tf_op jit(solution)/shard_map/ppermute | solution.py:238
  93.3 4.3 %collective-permute-start.11 = (bf16[64,1536]{1,0:T(8,128)(2,1)S(1)}, bf16[64,1536]{1,0:T(8,128)(2,1)S(1)}, u32[]{:S(2)}, u32[]{:S(2)}) collective-permute-start(bf16[64,1536]{1,0:T(8,128)(2,1)S(1)} %constant_dynamic-update-slice_fusion.refs_0_), channel_id=1, source_target_pairs={{0,2},{1,3},{2,0},{3,1},{4,6},{5,7},{6,4},{7,5},{8,10},{9,11},{10,... | collective-permute-start | bytes 589832 | tf_op jit(solution)/shard_map/ppermute | solution.py:238
  97.6 3.1 %collective-permute-start.12 = (bf16[64,1536]{1,0:T(8,128)(2,1)S(1)}, bf16[64,1536]{1,0:T(8,128)(2,1)S(1)}, u32[]{:S(2)}, u32[]{:S(2)}) collective-permute-start(bf16[64,1536]{1,0:T(8,128)(2,1)S(1)} %constant_dynamic-update-slice_fusion.refs_0_), channel_id=1, source_target_pairs={{0,3},{1,0},{2,1},{3,2},{4,7},{5,4},{6,5},{7,6},{8,11},{9,8},{10,9... | collective-permute-start | bytes 589832 | tf_op jit(solution)/shard_map/ppermute | solution.py:238
  100.7 0.8 all-to-all-done.2.got_ref
  101.5 1.2 %shard_map.81 = f32[96,768]{1,0:T(8,128)} custom-call(bf16[8,512,128]{2,1,0:T(8,128)(2,1)S(1)} %all-to-all-done.2.got_ref, bf16[512,768]{1,0:T(8,128)(2,1)S(1)} %collective-permute-done.9.pair_ref, bf16[128,768]{1,0:T(8,128)(2,1)S(1)} %fusion.refs_0_, bf16[128,768]{1,0:T(8,128)(2,1)S(1)} %collective-permute-done.6.refs_1_, ...), custom_call_target="tpu_custom_call" | custom-call | flops 150994944 | bytes 2916352 | tf_op jit(solution)/shard_map/pallas_call | solution.py:22
  102.8 3.6 %collective-permute-done.10.refs_1_ = bf16[64,1536]{1,0:T(8,128)(2,1)S(1)} collective-permute-done((bf16[64,1536]{1,0:T(8,128)(2,1)S(1)}, bf16[64,1536]{1,0:T(8,128)(2,1)S(1)}, u32[]{:S(2)}, u32[]{:S(2)}) %collective-permute-start.10) | collective-permute-done | bytes 196640 | tf_op jit(solution)/shard_map/ppermute | solution.py:238
  106.4 3.0 %collective-permute-done.11.refs_2_ = bf16[64,1536]{1,0:T(8,128)(2,1)S(1)} collective-permute-done((bf16[64,1536]{1,0:T(8,128)(2,1)S(1)}, bf16[64,1536]{1,0:T(8,128)(2,1)S(1)}, u32[]{:S(2)}, u32[]{:S(2)}) %collective-permute-start.11) | collective-permute-done | bytes 196640 | tf_op jit(solution)/shard_map/ppermute | solution.py:238
  109.3 1.1 %shard_map.82 = (f32[48,1536]{1,0:T(8,128)}, f32[48,1536]{1,0:T(8,128)}) custom-call(bf16[8,512,128]{2,1,0:T(8,128)(2,1)S(1)} %all-to-all-done.2.got_ref, bf16[64,1536]{1,0:T(8,128)(2,1)S(1)} %constant_dynamic-update-slice_fusion.refs_0_, bf16[64,1536]{1,0:T(8,128)(2,1)S(1)} %collective-permute-done.10.refs_1_, ...), custom_call_target="tpu_custom_call" | custom-call | flops 201326592 | bytes 2424832 | tf_op jit(solution)/shard_map/pallas_call | solution.py:22
  (34 shorter events, 2.3 us)
Async XLA Ops:
  0.6 1.0 copy-start.1
  1.6 0.7 copy-start.3
  3.0 38.7 %copy-start = (bf16[1536,768]{1,0:T(8,128)(2,1)S(1)}, bf16[1536,768]{1,0:T(8,128)(2,1)}, u32[]{:S(2)}) copy-start(bf16[1536,768]{1,0:T(8,128)(2,1)} %b_ref.1) | copy-start | bytes 7077892
  3.0 23.3 %collective-permute-start = (bf16[64,1536]{1,0:T(8,128)(2,1)S(1)}, bf16[64,1536]{1,0:T(8,128)(2,1)S(1)}, u32[]{:S(2)}, u32[]{:S(2)}) collective-permute-start(bf16[64,1536]{1,0:T(8,128)(2,1)S(1)} %shard_map.76.gy_ref), channel_id=1, source_target_pairs={{0,4},{1,5},{2,6},{3,7},{4,0},{5,1},{6,2},{7,3},{8,12},{9,13},{10,... | collective-permute-start | bytes 589832 | tf_op jit(solution)/shard_map/ppermute | solution.py:220
  10.7 58.2 %all-to-all-start = ((bf16[16,120,128]{2,1,0:T(8,128)(2,1)}), bf16[16,120,128]{2,1,0:T(8,128)(2,1)S(1)}, u32[]{:S(2)}, u32[]{:S(2)}) async-start(bf16[16,120,128]{2,1,0:T(8,128)(2,1)} %shard_map.77), calls=%async_computation | async-start | bytes 983040 | tf_op jit(solution)/shard_map/all_to_all | solution.py:235
  27.0 10.7 %collective-permute-start.1 = (bf16[64,1536]{1,0:T(8,128)(2,1)S(1)}, bf16[64,1536]{1,0:T(8,128)(2,1)S(1)}, u32[]{:S(2)}, u32[]{:S(2)}) collective-permute-start(bf16[64,1536]{1,0:T(8,128)(2,1)S(1)} %pad_maximum_fusion.2.refs_0_), channel_id=1, source_target_pairs={{0,1},{1,2},{2,3},{3,0},{4,5},{5,6},{6,7},{7,4},{8,9},{9,10},{10,1... | collective-permute-start | bytes 589832 | tf_op jit(solution)/shard_map/ppermute | solution.py:238
  30.2 10.5 %collective-permute-start.2 = (bf16[64,1536]{1,0:T(8,128)(2,1)S(1)}, bf16[64,1536]{1,0:T(8,128)(2,1)S(1)}, u32[]{:S(2)}, u32[]{:S(2)}) collective-permute-start(bf16[64,1536]{1,0:T(8,128)(2,1)S(1)} %pad_maximum_fusion.2.refs_0_), channel_id=1, source_target_pairs={{0,2},{1,3},{2,0},{3,1},{4,6},{5,7},{6,4},{7,5},{8,10},{9,11},{10,... | collective-permute-start | bytes 589832 | tf_op jit(solution)/shard_map/ppermute | solution.py:238
  34.7 7.0 %collective-permute-start.3 = (bf16[64,1536]{1,0:T(8,128)(2,1)S(1)}, bf16[64,1536]{1,0:T(8,128)(2,1)S(1)}, u32[]{:S(2)}, u32[]{:S(2)}) collective-permute-start(bf16[64,1536]{1,0:T(8,128)(2,1)S(1)} %pad_maximum_fusion.2.refs_0_), channel_id=1, source_target_pairs={{0,3},{1,0},{2,1},{3,2},{4,7},{5,4},{6,5},{7,6},{8,11},{9,8},{10,9... | collective-permute-start | bytes 589832 | tf_op jit(solution)/shard_map/ppermute | solution.py:238
  43.3 5.7 %collective-permute-start.4 = (bf16[144,768]{1,0:T(8,128)(2,1)}, bf16[144,768]{1,0:T(8,128)(2,1)S(1)}, u32[]{:S(2)}, u32[]{:S(2)}) collective-permute-start(bf16[144,768]{1,0:T(8,128)(2,1)} %get-tuple-element.16), channel_id=1, source_target_pairs={{0,128},{128,0},{256,384},{384,256},{1,129},{129,1},{257,385},{385... | collective-permute-start | bytes 663560 | tf_op jit(solution)/shard_map/ppermute | solution.py:258
  49.1 31.7 %copy-start.2 = (bf16[128,384]{1,0:T(8,128)(2,1)S(1)}, bf16[128,384]{1,0:T(8,128)(2,1)}, u32[]{:S(2)}) copy-start(bf16[128,384]{1,0:T(8,128)(2,1)} %tokens_ref.1) | copy-start | bytes 294916
  49.1 31.7 %copy-start.4 = (s32[32]{0:T(128)S(1)}, s32[32]{0:T(128)}, u32[]{:S(2)}) copy-start(s32[32]{0:T(128)} %picks.5) | copy-start | bytes 388
  49.1 10.0 %collective-permute-start.5 = (bf16[144,768]{1,0:T(8,128)(2,1)S(1)}, bf16[144,768]{1,0:T(8,128)(2,1)S(1)}, u32[]{:S(2)}, u32[]{:S(2)}) collective-permute-start(bf16[144,768]{1,0:T(8,128)(2,1)S(1)} %fusion.2), channel_id=1, source_target_pairs={{0,256},{128,384},{256,0},{384,128},{1,257},{129,385},{257,1},{385... | collective-permute-start | bytes 663560 | tf_op jit(solution)/shard_map/ppermute | solution.py:261
  59.3 27.4 %collective-permute-start.8 = (bf16[128,768]{1,0:T(8,128)(2,1)S(1)}, bf16[128,768]{1,0:T(8,128)(2,1)S(1)}, u32[]{:S(2)}, u32[]{:S(2)}) collective-permute-start(bf16[128,768]{1,0:T(8,128)(2,1)S(1)} %fusion.refs_0_), channel_id=1, source_target_pairs={{0,120},{8,0},{16,8},{24,16},{32,24},{40,32},{48,40},{56,48},{64,5... | collective-permute-start | bytes 589832 | tf_op jit(solution)/shard_map/ppermute | solution.py:265
  63.9 22.7 %collective-permute-start.7 = (bf16[128,768]{1,0:T(8,128)(2,1)S(1)}, bf16[128,768]{1,0:T(8,128)(2,1)S(1)}, u32[]{:S(2)}, u32[]{:S(2)}) collective-permute-start(bf16[128,768]{1,0:T(8,128)(2,1)S(1)} %fusion.refs_0_), channel_id=1, source_target_pairs={{0,8},{8,16},{16,24},{24,32},{32,40},{40,48},{48,56},{56,64},{64,7... | collective-permute-start | bytes 589832 | tf_op jit(solution)/shard_map/ppermute | solution.py:265
  65.9 20.8 %collective-permute-start.6 = (bf16[128,768]{1,0:T(8,128)(2,1)S(1)}, bf16[128,768]{1,0:T(8,128)(2,1)S(1)}, u32[]{:S(2)}, u32[]{:S(2)}) collective-permute-start(bf16[128,768]{1,0:T(8,128)(2,1)S(1)} %fusion.refs_0_), channel_id=1, source_target_pairs={{0,16},{8,24},{16,32},{24,40},{32,48},{40,56},{48,64},{56,72},{64,... | collective-permute-start | bytes 589832 | tf_op jit(solution)/shard_map/ppermute | solution.py:265
  69.6 11.2 %all-to-all-start.1 = ((bf16[4,96,128]{2,1,0:T(8,128)(2,1)}), bf16[4,96,128]{2,1,0:T(8,128)(2,1)S(1)}, u32[]{:S(2)}, u32[]{:S(2)}) async-start(bf16[4,96,128]{2,1,0:T(8,128)(2,1)} %get-tuple-element.19), calls=%async_computation.1 | async-start | bytes 196608 | tf_op jit(solution)/shard_map/all_to_all | solution.py:282
  82.6 7.0 %copy-start.5 = (bf16[32,1536]{1,0:T(8,128)(2,1)S(1)}, bf16[32,1536]{1,0:T(8,128)(2,1)}, u32[]{:S(2)}) copy-start(bf16[32,1536]{1,0:T(8,128)(2,1)} %get-tuple-element.21) | copy-start | bytes 294916
  82.6 7.0 %copy-start.6 = (bf16[32,1536]{1,0:T(8,128)(2,1)S(1)}, bf16[32,1536]{1,0:T(8,128)(2,1)}, u32[]{:S(2)}) copy-start(bf16[32,1536]{1,0:T(8,128)(2,1)} %get-tuple-element.22) | copy-start | bytes 294916
  82.6 19.0 %all-to-all-start.2 = ((bf16[8,512,128]{2,1,0:T(8,128)(2,1)}), bf16[8,512,128]{2,1,0:T(8,128)(2,1)S(1)}, u32[]{:S(2)}, u32[]{:S(2)}) async-start(bf16[8,512,128]{2,1,0:T(8,128)(2,1)} %shard_map.80), calls=%async_computation.2 | async-start | bytes 2097152 | tf_op jit(solution)/shard_map/all_to_all | solution.py:289
  86.7 14.0 %collective-permute-start.9 = (bf16[512,768]{1,0:T(8,128)(2,1)S(1)}, bf16[512,768]{1,0:T(8,128)(2,1)S(1)}, u32[]{:S(2)}, u32[]{:S(2)}) collective-permute-start(bf16[512,768]{1,0:T(8,128)(2,1)S(1)} %pad_maximum_fusion), channel_id=1, source_target_pairs={{0,128},{128,0},{256,384},{384,256},{1,129},{129,1},{257,385},{385... | collective-permute-start | bytes 2359304 | tf_op jit(solution)/shard_map/ppermute | solution.py:268
  89.6 16.7 %collective-permute-start.10 = (bf16[64,1536]{1,0:T(8,128)(2,1)S(1)}, bf16[64,1536]{1,0:T(8,128)(2,1)S(1)}, u32[]{:S(2)}, u32[]{:S(2)}) collective-permute-start(bf16[64,1536]{1,0:T(8,128)(2,1)S(1)} %constant_dynamic-update-slice_fusion.refs_0_), channel_id=1, source_target_pairs={{0,1},{1,2},{2,3},{3,0},{4,5},{5,6},{6,7},{7,4},{8,9},{9,10},{10,1... | collective-permute-start | bytes 589832 | tf_op jit(solution)/shard_map/ppermute | solution.py:238
  93.3 16.1 %collective-permute-start.11 = (bf16[64,1536]{1,0:T(8,128)(2,1)S(1)}, bf16[64,1536]{1,0:T(8,128)(2,1)S(1)}, u32[]{:S(2)}, u32[]{:S(2)}) collective-permute-start(bf16[64,1536]{1,0:T(8,128)(2,1)S(1)} %constant_dynamic-update-slice_fusion.refs_0_), channel_id=1, source_target_pairs={{0,2},{1,3},{2,0},{3,1},{4,6},{5,7},{6,4},{7,5},{8,10},{9,11},{10,... | collective-permute-start | bytes 589832 | tf_op jit(solution)/shard_map/ppermute | solution.py:238
  97.6 11.8 %collective-permute-start.12 = (bf16[64,1536]{1,0:T(8,128)(2,1)S(1)}, bf16[64,1536]{1,0:T(8,128)(2,1)S(1)}, u32[]{:S(2)}, u32[]{:S(2)}) collective-permute-start(bf16[64,1536]{1,0:T(8,128)(2,1)S(1)} %constant_dynamic-update-slice_fusion.refs_0_), channel_id=1, source_target_pairs={{0,3},{1,0},{2,1},{3,2},{4,7},{5,4},{6,5},{7,6},{8,11},{9,8},{10,9... | collective-permute-start | bytes 589832 | tf_op jit(solution)/shard_map/ppermute | solution.py:238

commit v11 on v10

--- a/solution.py
+++ b/solution.py
@@ -93,7 +93,9 @@
 def right_kernel(b_ref, gy_ref, *refs):
     blocks, keep_ref, give_ref, held = refs[:-3], refs[-3], refs[-2], refs[-1]
     n_blk, unused, size, width = held.shape
-    rows = jnp.concatenate([block[...] for block in blocks], axis=0)
+    step = gy_ref.shape[0]
+    spans = [slice(at, at + 2 * size) for at in (0, step)]
+    rows = jnp.concatenate([block[span, :] for block in blocks for span in spans], axis=0)
     term = jnp.dot(rows, b_ref[...], preferred_element_type=F32)
     held[...] = term.reshape(held.shape)
     core = lax.axis_index("grp") % 2
@@ -118,9 +120,14 @@
         total = total + got_ref[r, :out_rows, :].astype(F32)
     u_ref[...] = total.astype(BF)
     per = n_row // n_grp
+    feats = out_rows
+    half = tok // 2
+    other = jnp.where(lax.axis_index("grp") % 2 == 0, total[:, half:], total[:, :half])
+    other = jnp.concatenate([other[: out_rows // 2], other[out_rows // 2 :]], axis=1).astype(BF)
     for g in range(n_grp):
         block = got_ref[g * per : (g + 1) * per, out_rows:, :].astype(F32)
-        x_ref[g] = block.reshape(x_rows, tok).astype(BF)
+        x_ref[g, :feats, :] = block.reshape(feats, tok).astype(BF)
+        x_ref[g, feats:, :] = other
 
 
 def second_kernel(picks, u_ref, x_ref, y_ref, tokens_ref, out_ref):
@@ -135,8 +142,14 @@
     own = y_ref[...].astype(F32)
     own = jnp.concatenate([own[:, :feat], own[:, feat:]], axis=0)
     empty = jnp.zeros((samp, LANES - 2 * tile), F32)
-    u_block = u_ref[...]
-    x_block = x_ref[...].reshape(x_ref.shape[0] * x_ref.shape[1], LANES)
+    half = tok // 2
+    grp = lax.axis_index("grp")
+    u_own = u_ref[...].astype(F32)
+    u_own = jnp.where(grp % 2 == 0, u_own[:, :half], u_own[:, half:])
+    u_pair = x_ref[grp ^ 1, out_rows:, :].astype(F32)
+    u_pair = jnp.concatenate([u_pair[:, :half], u_pair[:, half:]], axis=0)
+    u_block = jnp.concatenate([u_own, u_pair], axis=1).astype(BF)
+    x_block = x_ref[:, :out_rows, :].reshape(x_ref.shape[0] * out_rows, LANES)
     for c in range(n_col):
         span = slice(c * tile, (c + 1) * tile)
         out_ref[c, :out_rows, :] = u_block
@@ -145,35 +158,34 @@
         out_ref[c, depth - samp :, :] = side.astype(BF)
 
 
-def final_kernel(got_ref, pair_ref, *refs):
-    v_refs, out_ref, held = refs[:-2], refs[-2], refs[-1]
-    n_col, unused, spread, size, width = held.shape
-    out_rows = out_ref.shape[0]
+def final_kernel(got_ref, *refs):
+    v_refs, own_ref, pair_ref, held = refs[:-3], refs[-3], refs[-2], refs[-1]
+    n_col, spread, size, width = held.shape
+    out_rows = own_ref.shape[0]
     row = lax.axis_index("row")
-    core = lax.axis_index("grp") % 2
-    cut = n_col * size
     for j, shift in enumerate(SHIFTS):
         plane = lax.rem(row - shift + spread, spread)
         for k in range(n_col):
-            span = slice(k * size, (k + 1) * size)
-            held[source_of(k), core, plane] = v_refs[j][span, :]
-            span = slice(j * cut + k * size, j * cut + (k + 1) * size)
-            held[source_of(k), 1 - core, plane] = pair_ref[span, :]
-    tokens = 2 * spread * size
+            held[source_of(k), plane] = v_refs[j][k * size : (k + 1) * size, :]
+    half = spread * size
     total = None
-    for c in range(0, n_col, 2):
-        left = jnp.concatenate([got_ref[c, :out_rows, :], got_ref[c + 1, :out_rows, :]], axis=1)
-        right = held[c : c + 2].reshape(2 * tokens, width)
+    for c in range(0, n_col, 4):
+        blocks = [got_ref[c + i, :out_rows, :] for i in range(4)]
+        own = jnp.concatenate([block[:, :half] for block in blocks], axis=1)
+        pair = jnp.concatenate([block[:, half:] for block in blocks], axis=1)
+        left = jnp.concatenate([own, pair], axis=0)
+        right = held[c : c + 4].reshape(4 * half, width)
         term = jnp.dot(left, right, preferred_element_type=F32)
         total = term if total is None else total + term
-    out_ref[...] = total
+    own_ref[...] = total[:out_rows]
+    pair_ref[...] = total[out_rows:].astype(BF)
 
 
 def factor_kernel(got_ref, *refs):
     blocks, act_ref, grad_ref = refs[:-2], refs[-2], refs[-1]
     n_col, depth, unused = got_ref.shape
     tile, width = act_ref.shape
-    samp = blocks[0].shape[0] // 2
+    samp = blocks[0].shape[0] // 4
     quarter = samp // 4
     total = samp * n_col
     scale = 1.0 / total
@@ -190,7 +202,8 @@
     act_ref[...] = term[tile : 2 * tile] * scale
     sides = [got_ref[source_of(k), depth - samp :, :] for k in range(n_col)]
     left = jnp.concatenate(sides, axis=0)
-    right = jnp.concatenate([block[...] for block in blocks], axis=0)
+    spans = [slice(at, at + samp) for at in (samp, 3 * samp)]
+    right = jnp.concatenate([block[span, :] for block in blocks for span in spans], axis=0)
     term = lax.dot_general(left, right, FIRST, preferred_element_type=F32)
     grad_ref[...] = term[:tile] * scale
 
@@ -216,6 +229,7 @@
         (sample_rows, cotangent),
         [shape((2 * size + samp, feat_grp), BF)],
         2 * 64 * tok * feat_grp,
+        limit=56,
     )[0]
     beside = lax.ppermute(picked, "col", [(i, (i + 4) % n_col) for i in range(n_col)])
     picked, x_in = lax.optimization_barrier((picked, tokens_in))
@@ -239,8 +253,7 @@
             block, "col", [(i, i - i % 4 + (i + k) % 4) for i in range(n_col)]
         )
 
-    cut = 2 * size
-    pair = jnp.concatenate([picked[:cut], beside[:cut]], axis=0)
+    pair = jnp.concatenate([picked, beside], axis=0)
     pairs = [pair] + [along_y(pair, k) for k in range(1, 4)]
     half = n_col * size
     extra = samp // 2
@@ -261,24 +274,17 @@
     taken = lax.ppermute(keep.astype(BF), "grp", [(i, i ^ 2) for i in range(n_grp)]).astype(F32)
     own_y = jnp.where(grp // 2 == owner // 2, keep[half:], taken[half:]).astype(BF)
     right = (keep[:half] + taken[:half]).astype(BF)
+    u_own, x_send = call(
+        gather_kernel,
+        (first,),
+        [shape((out_rows, tok), BF), shape((n_grp, out_rows + out_rows // 2, LANES), BF)],
+        1000000,
+    )
+    right, unused = lax.optimization_barrier((right, x_send))
     rights = [right] + [
         lax.ppermute(right, "row", [(i, (i + j) % n_row) for i in range(n_row)])
         for j in SHIFTS[1:]
     ]
-    other = lax.ppermute(
-        jnp.concatenate(rights, axis=0), "grp", [(i, i ^ 1) for i in range(n_grp)]
-    )
-
-    unused, picked_y, beside_y = lax.optimization_barrier((keep, picked[cut:], beside[cut:]))
-    samples = jnp.concatenate([picked_y, beside_y], axis=0)
-    samples = [samples] + [along_y(samples, k) for k in range(1, 4)]
-
-    u_own, x_send = call(
-        gather_kernel,
-        (first,),
-        [shape((out_rows, tok), BF), shape((n_grp, strip * n_row // n_grp, LANES), BF)],
-        1000000,
-    )
     x_got = lax.all_to_all(x_send, "grp", 0, 0)
     send = call(
         second_kernel,
@@ -288,16 +294,19 @@
     )[0]
     got = lax.all_to_all(send, "col", 0, 0)
 
-    precond = call(
+    term, send = call(
         final_kernel,
-        (got, other, *rights),
-        [shape((out_rows, width), F32)],
+        (got, *rights),
+        [shape((out_rows, width), F32), shape((out_rows, width), BF)],
         2 * out_rows * n_col * tok * width,
-        [pltpu.VMEM((n_col, 2, spread, size, width), BF)],
-    )[0]
+        [pltpu.VMEM((n_col, spread, size, width), BF)],
+    )
+    got, unused = lax.optimization_barrier((got, send))
+    taken = lax.ppermute(send, "grp", [(i, i ^ 1) for i in range(n_grp)])
+    precond = term + taken.astype(F32)
     act_cov, grad_cov = call(
         factor_kernel,
-        (got, *samples),
+        (got, *pairs),
         [shape((tile, feat_grp), F32)] * 2,
         4 * LANES * samp * n_col * feat_grp,
     )

time: 112 us -> 118 us (1.054)
  waiting for transfers between devices: 23.4 us -> 39.9 us
  starting transfers between devices: 72.1 us -> 57.2 us
  other arithmetic: 0.27 us -> 2.99 us
  local copies, waits for them, and re-layouts: 3 us -> 4.92 us
    ppermute x6 -> x3, starting transfers between devices: 21.7 us -> 9.5 us  [along_y(): lax.ppermute(block, 'col', [(i, i - i % 4 + (i + k) % 4) for i in range(n...]
    ppermute x3, waiting for transfers between devices: 0.01 us -> 9.9 us  [body(): lax.ppermute(right, 'row', [(i, (i + j) % n_row) for i in range(n_row)])]
    ppermute x6 -> x3, waiting for transfers between devices: 10.6 us -> 18 us  [along_y(): lax.ppermute(block, 'col', [(i, i - i % 4 + (i + k) % 4) for i in range(n...]
    unnamed x15 -> x21, local copies, waits for them, and re-layouts: 1.68 us -> 4.91 us
    ppermute x1, starting transfers between devices: 4.37 us -> 2.54 us  [body(): lax.ppermute(give, 'grp', [(i, i ^ 1) for i in range(n_grp)]).astype(F32)]
    slice x2 -> x0, local copies, waits for them, and re-layouts: 1.31 us -> none  [the longest x1 0.65 us: body(): picked[cut:]]
  transfers between devices with their start and end apart: 16 -> 13, of which waited for: 8 -> 8; matrix products, arithmetic and copies ran while one was open for 1% -> 2% of each run, Pallas kernels for 8% -> 5%
where the time goes in v11:
time: 118 us; the launch traced here: 116 us
  starting transfers between devices  57.2 us (48%)
  waiting for transfers between devices  39.9 us (34%)
  Pallas kernels  10.5 us (9%)
  local copies, waits for them, and re-layouts  4.92 us (4%)
  other arithmetic  2.99 us (3%)
    ppermute x3, waiting for transfers between devices, along_y(): lax.ppermute(block, 'col', [(i, i - i % 4 + (i + k) % 4) for i in range(n...  18 us
    all_to_all x1, starting transfers between devices, body(): first = lax.all_to_all(payload, 'row', 0, 0)  14.9 us
    pallas_call x7, Pallas kernels, call(): pl.pallas_call(kernel, out_shape=outs, in_specs=[SMEM if x.dtype == jnp.i...  10.5 us
    ppermute x3, waiting for transfers between devices, body(): lax.ppermute(right, 'row', [(i, (i + j) % n_row) for i in range(n_row)])  9.9 us
    ppermute x3, starting transfers between devices, along_y(): lax.ppermute(block, 'col', [(i, i - i % 4 + (i + k) % 4) for i in range(n...  9.5 us
    ppermute x3, starting transfers between devices, body(): lax.ppermute(right, 'row', [(i, (i + j) % n_row) for i in range(n_row)])  9.45 us
    ppermute x1, waiting for transfers between devices, body(): lax.ppermute(keep.astype(BF), 'grp', [(i, i ^ 2) for i in range(n_grp)])  5.75 us
    all_to_all x1, waiting for transfers between devices, body(): x_got = lax.all_to_all(x_send, 'grp', 0, 0)  5.22 us
  transfers between devices with their start and end apart: 13, of which 8 were waited for; matrix products, arithmetic and copies ran while one was open for 2% of the time, Pallas kernels for 5%

profile of v11, /device:TPU:1, one launch (start us, length us, event | category | flops | bytes accessed | tf_op | source)
XLA Modules:
  0.0 116.5 jit_solution(5179605076915255092)
XLA Ops:
  0.6 1.9 %shard_map.76.gy_ref = bf16[64,1536]{1,0:T(8,128)(2,1)} custom-call(s32[32]{0:T(128)} %picks.5, bf16[128,1536]{1,0:T(8,128)(2,1)} %g_ref.1), custom_call_target="tpu_custom_call" | custom-call | flops 25165824 | bytes 589952 | tf_op jit(solution)/shard_map/pallas_call | solution.py:22
  2.5 4.1 %collective-permute-start = (bf16[64,1536]{1,0:T(8,128)(2,1)}, bf16[64,1536]{1,0:T(8,128)(2,1)S(1)}, u32[]{:S(2)}, u32[]{:S(2)}) collective-permute-start(bf16[64,1536]{1,0:T(8,128)(2,1)} %shard_map.76.gy_ref), channel_id=1, source_target_pairs={{0,4},{1,5},{2,6},{3,7},{4,0},{5,1},{6,2},{7,3},{8,12},{9,13},{10,... | collective-permute-start | bytes 589832 | tf_op jit(solution)/shard_map/ppermute | solution.py:234
  6.6 3.6 %shard_map.77 = bf16[16,120,128]{2,1,0:T(8,128)(2,1)} custom-call(s32[32]{0:T(128)} %picks.5, bf16[128,384]{1,0:T(8,128)(2,1)} %tokens_ref.1, bf16[1536,384]{1,0:T(8,128)(2,1)} %a_hbm.1), custom_call_target="tpu_custom_call" | custom-call | flops 150994944 | bytes 1769600 | tf_op jit(solution)/shard_map/pallas_call | solution.py:22
  10.2 14.9 %all-to-all-start = ((bf16[16,120,128]{2,1,0:T(8,128)(2,1)}), bf16[16,120,128]{2,1,0:T(8,128)(2,1)S(1)}, u32[]{:S(2)}, u32[]{:S(2)}) async-start(bf16[16,120,128]{2,1,0:T(8,128)(2,1)} %shard_map.77), calls=%async_computation | async-start | bytes 983040 | tf_op jit(solution)/shard_map/all_to_all | solution.py:249
  25.2 4.6 %collective-permute-start.3 = (bf16[128,1536]{1,0:T(8,128)(2,1)S(1)}, bf16[128,1536]{1,0:T(8,128)(2,1)S(1)}, u32[]{:S(2)}, u32[]{:S(2)}) collective-permute-start(bf16[128,1536]{1,0:T(8,128)(2,1)S(1)} %constant_dynamic-update-slice_fusion.refs_0_), channel_id=1, source_target_pairs={{0,3},{1,0},{2,1},{3,2},{4,7},{5,4},{6,5},{7,6},{8,11},{9,8},{10,9... | collective-permute-start | bytes 1179656 | tf_op jit(solution)/shard_map/ppermute | solution.py:252
  29.9 2.3 %collective-permute-start.2 = (bf16[128,1536]{1,0:T(8,128)(2,1)S(1)}, bf16[128,1536]{1,0:T(8,128)(2,1)S(1)}, u32[]{:S(2)}, u32[]{:S(2)}) collective-permute-start(bf16[128,1536]{1,0:T(8,128)(2,1)S(1)} %constant_dynamic-update-slice_fusion.refs_0_), channel_id=1, source_target_pairs={{0,2},{1,3},{2,0},{3,1},{4,6},{5,7},{6,4},{7,5},{8,10},{9,11},{10,... | collective-permute-start | bytes 1179656 | tf_op jit(solution)/shard_map/ppermute | solution.py:252
  32.1 2.6 %collective-permute-start.1 = (bf16[128,1536]{1,0:T(8,128)(2,1)S(1)}, bf16[128,1536]{1,0:T(8,128)(2,1)S(1)}, u32[]{:S(2)}, u32[]{:S(2)}) collective-permute-start(bf16[128,1536]{1,0:T(8,128)(2,1)S(1)} %constant_dynamic-update-slice_fusion.refs_0_), channel_id=1, source_target_pairs={{0,1},{1,2},{2,3},{3,0},{4,5},{5,6},{6,7},{7,4},{8,9},{9,10},{10,1... | collective-permute-start | bytes 1179656 | tf_op jit(solution)/shard_map/ppermute | solution.py:252
  34.7 3.3 %collective-permute-done.3.refs_3_ = bf16[128,1536]{1,0:T(8,128)(2,1)S(1)} collective-permute-done((bf16[128,1536]{1,0:T(8,128)(2,1)S(1)}, bf16[128,1536]{1,0:T(8,128)(2,1)S(1)}, u32[]{:S(2)}, u32[]{:S(2)}) %collective-permute-start.3) | collective-permute-done | bytes 393248 | tf_op jit(solution)/shard_map/ppermute | solution.py:252
  38.0 4.3 %collective-permute-done.2.refs_2_ = bf16[128,1536]{1,0:T(8,128)(2,1)S(1)} collective-permute-done((bf16[128,1536]{1,0:T(8,128)(2,1)S(1)}, bf16[128,1536]{1,0:T(8,128)(2,1)S(1)}, u32[]{:S(2)}, u32[]{:S(2)}) %collective-permute-start.2) | collective-permute-done | bytes 393248 | tf_op jit(solution)/shard_map/ppermute | solution.py:252
  42.4 10.3 %collective-permute-done.1.refs_1_ = bf16[128,1536]{1,0:T(8,128)(2,1)S(1)} collective-permute-done((bf16[128,1536]{1,0:T(8,128)(2,1)S(1)}, bf16[128,1536]{1,0:T(8,128)(2,1)S(1)}, u32[]{:S(2)}, u32[]{:S(2)}) %collective-permute-start.1) | collective-permute-done | bytes 393248 | tf_op jit(solution)/shard_map/ppermute | solution.py:252
  52.7 1.7 %copy-done = bf16[1536,768]{1,0:T(8,128)(2,1)S(1)} copy-done((bf16[1536,768]{1,0:T(8,128)(2,1)S(1)}, bf16[1536,768]{1,0:T(8,128)(2,1)}, u32[]{:S(2)}) %copy-start) | copy-done | bytes 2359320
  54.4 0.9 shard_map.78
  55.3 2.5 %collective-permute-start.4 = (bf16[144,768]{1,0:T(8,128)(2,1)S(1)}, bf16[144,768]{1,0:T(8,128)(2,1)S(1)}, u32[]{:S(2)}, u32[]{:S(2)}) collective-permute-start(bf16[144,768]{1,0:T(8,128)(2,1)S(1)} %get-tuple-element.18), channel_id=1, source_target_pairs={{0,128},{128,0},{256,384},{384,256},{1,129},{129,1},{257,385},{385... | collective-permute-start | bytes 663560 | tf_op jit(solution)/shard_map/ppermute | solution.py:271
  57.9 1.0 collective-permute-done.4
  59.1 4.3 %collective-permute-start.5 = (bf16[144,768]{1,0:T(8,128)(2,1)S(1)}, bf16[144,768]{1,0:T(8,128)(2,1)}, u32[]{:S(2)}, u32[]{:S(2)}) collective-permute-start(bf16[144,768]{1,0:T(8,128)(2,1)S(1)} %pad_maximum_fusion), channel_id=1, source_target_pairs={{0,256},{128,384},{256,0},{384,128},{1,257},{129,385},{257,1},{385... | collective-permute-start | bytes 663560 | tf_op jit(solution)/shard_map/ppermute | solution.py:274
  63.4 5.8 %collective-permute-done.5 = bf16[144,768]{1,0:T(8,128)(2,1)} collective-permute-done((bf16[144,768]{1,0:T(8,128)(2,1)S(1)}, bf16[144,768]{1,0:T(8,128)(2,1)}, u32[]{:S(2)}, u32[]{:S(2)}) %collective-permute-start.5) | collective-permute-done | bytes 221216 | tf_op jit(solution)/shard_map/ppermute | solution.py:274
  69.2 1.0 convert_element_type.17
  70.2 0.8 shard_map.79
  71.0 5.2 %all-to-all-start.1 = ((bf16[4,144,128]{2,1,0:T(8,128)(2,1)}), bf16[4,144,128]{2,1,0:T(8,128)(2,1)S(1)}, u32[]{:S(2)}, u32[]{:S(2)}) async-start(bf16[4,144,128]{2,1,0:T(8,128)(2,1)} %get-tuple-element.21), calls=%async_computation.1 | async-start | bytes 294912 | tf_op jit(solution)/shard_map/all_to_all | solution.py:288
  76.2 5.2 %all-to-all-done.1.x_ref = bf16[4,144,128]{2,1,0:T(8,128)(2,1)S(1)} async-done(((bf16[4,144,128]{2,1,0:T(8,128)(2,1)}), bf16[4,144,128]{2,1,0:T(8,128)(2,1)S(1)}, u32[]{:S(2)}, u32[]{:S(2)}) %all-to-all-start.1) | async-done | bytes 147488 | tf_op jit(solution)/shard_map/all_to_all | solution.py:288
  81.5 1.8 %shard_map.80 = bf16[8,512,128]{2,1,0:T(8,128)(2,1)} custom-call(s32[32]{0:T(128)S(1)} %copy-done.7, bf16[96,128]{1,0:T(8,128)(2,1)S(1)} %get-tuple-element.20.u_ref, bf16[4,144,128]{2,1,0:T(8,128)(2,1)S(1)} %all-to-all-done.1.x_ref, bf16[16,768]{1,0:T(8,128)(2,1)S(1)} %fusion.2.y_ref, bf16[128,384]{1,0:T(8,128)(2,1)S(1)} %copy-done.4), custom_call_target="tpu_custom_call" | custom-call | flops 3145728 | bytes 1343616 | tf_op jit(solution)/shard_map/pallas_call | solution.py:22
  83.3 3.6 %all-to-all-start.2 = ((bf16[8,512,128]{2,1,0:T(8,128)(2,1)}), bf16[8,512,128]{2,1,0:T(8,128)(2,1)S(1)}, u32[]{:S(2)}, u32[]{:S(2)}) async-start(bf16[8,512,128]{2,1,0:T(8,128)(2,1)} %shard_map.80), calls=%async_computation.2 | async-start | bytes 2097152 | tf_op jit(solution)/shard_map/all_to_all | solution.py:295
  86.8 1.2 %fusion.refs_0_ = bf16[128,768]{1,0:T(8,128)(2,1)S(1)} fusion(f32[144,768]{1,0:T(8,128)} %copy-done.9, f32[144,768]{1,0:T(8,128)} %copy-done.8, f32[144,768]{1,0:T(8,128)S(1)} %get-tuple-element.22), kind=kLoop, calls=%fused_computation.1 | loop fusion | flops 294912 | bytes 1376256 | tf_op jit(solution)/shard_map/convert_element_type | solution.py:276
  88.0 4.5 %collective-permute-start.8 = (bf16[128,768]{1,0:T(8,128)(2,1)S(1)}, bf16[128,768]{1,0:T(8,128)(2,1)S(1)}, u32[]{:S(2)}, u32[]{:S(2)}) collective-permute-start(bf16[128,768]{1,0:T(8,128)(2,1)S(1)} %fusion.refs_0_), channel_id=1, source_target_pairs={{0,120},{8,0},{16,8},{24,16},{32,24},{40,32},{48,40},{56,48},{64,5... | collective-permute-start | bytes 589832 | tf_op jit(solution)/shard_map/ppermute | solution.py:285
  92.5 1.9 %collective-permute-start.7 = (bf16[128,768]{1,0:T(8,128)(2,1)S(1)}, bf16[128,768]{1,0:T(8,128)(2,1)S(1)}, u32[]{:S(2)}, u32[]{:S(2)}) collective-permute-start(bf16[128,768]{1,0:T(8,128)(2,1)S(1)} %fusion.refs_0_), channel_id=1, source_target_pairs={{0,8},{8,16},{16,24},{24,32},{32,40},{40,48},{48,56},{56,64},{64,7... | collective-permute-start | bytes 589832 | tf_op jit(solution)/shard_map/ppermute | solution.py:285
  94.4 3.0 %collective-permute-start.6 = (bf16[128,768]{1,0:T(8,128)(2,1)S(1)}, bf16[128,768]{1,0:T(8,128)(2,1)S(1)}, u32[]{:S(2)}, u32[]{:S(2)}) collective-permute-start(bf16[128,768]{1,0:T(8,128)(2,1)S(1)} %fusion.refs_0_), channel_id=1, source_target_pairs={{0,16},{8,24},{16,32},{24,40},{32,48},{40,56},{48,64},{56,72},{64,... | collective-permute-start | bytes 589832 | tf_op jit(solution)/shard_map/ppermute | solution.py:285
  98.2 2.5 %collective-permute-done.7.refs_2_ = bf16[128,768]{1,0:T(8,128)(2,1)S(1)} collective-permute-done((bf16[128,768]{1,0:T(8,128)(2,1)S(1)}, bf16[128,768]{1,0:T(8,128)(2,1)S(1)}, u32[]{:S(2)}, u32[]{:S(2)}) %collective-permute-start.7) | collective-permute-done | bytes 196640 | tf_op jit(solution)/shard_map/ppermute | solution.py:285
  100.6 7.4 %collective-permute-done.6.refs_1_ = bf16[128,768]{1,0:T(8,128)(2,1)S(1)} collective-permute-done((bf16[128,768]{1,0:T(8,128)(2,1)S(1)}, bf16[128,768]{1,0:T(8,128)(2,1)S(1)}, u32[]{:S(2)}, u32[]{:S(2)}) %collective-permute-start.6) | collective-permute-done | bytes 196640 | tf_op jit(solution)/shard_map/ppermute | solution.py:285
  108.7 0.9 copy-done.3
  109.7 0.9 copy-done.6
  111.0 3.6 %collective-permute-start.9 = (bf16[96,768]{1,0:T(8,128)(2,1)S(1)}, bf16[96,768]{1,0:T(8,128)(2,1)S(1)}, u32[]{:S(2)}, u32[]{:S(2)}) collective-permute-start(bf16[96,768]{1,0:T(8,128)(2,1)S(1)} %get-tuple-element.25), channel_id=1, source_target_pairs={{0,128},{128,0},{256,384},{384,256},{1,129},{129,1},{257,385},{385... | collective-permute-start | bytes 442376 | tf_op jit(solution)/shard_map/ppermute | solution.py:305
  114.6 1.1 shard_map.82
  (31 shorter events, 2.7 us)
Async XLA Ops:
  2.5 22.6 %copy-start.1 = (bf16[64,1536]{1,0:T(8,128)(2,1)S(1)}, bf16[64,1536]{1,0:T(8,128)(2,1)}, u32[]{:S(2)}) copy-start(bf16[64,1536]{1,0:T(8,128)(2,1)} %shard_map.76.gy_ref) | copy-start | bytes 589828
  2.5 22.6 %collective-permute-start = (bf16[64,1536]{1,0:T(8,128)(2,1)}, bf16[64,1536]{1,0:T(8,128)(2,1)S(1)}, u32[]{:S(2)}, u32[]{:S(2)}) collective-permute-start(bf16[64,1536]{1,0:T(8,128)(2,1)} %shard_map.76.gy_ref), channel_id=1, source_target_pairs={{0,4},{1,5},{2,6},{3,7},{4,0},{5,1},{6,2},{7,3},{8,12},{9,13},{10,... | collective-permute-start | bytes 589832 | tf_op jit(solution)/shard_map/ppermute | solution.py:234
  10.2 60.0 %all-to-all-start = ((bf16[16,120,128]{2,1,0:T(8,128)(2,1)}), bf16[16,120,128]{2,1,0:T(8,128)(2,1)S(1)}, u32[]{:S(2)}, u32[]{:S(2)}) async-start(bf16[16,120,128]{2,1,0:T(8,128)(2,1)} %shard_map.77), calls=%async_computation | async-start | bytes 983040 | tf_op jit(solution)/shard_map/all_to_all | solution.py:249
  25.2 12.8 %collective-permute-start.3 = (bf16[128,1536]{1,0:T(8,128)(2,1)S(1)}, bf16[128,1536]{1,0:T(8,128)(2,1)S(1)}, u32[]{:S(2)}, u32[]{:S(2)}) collective-permute-start(bf16[128,1536]{1,0:T(8,128)(2,1)S(1)} %constant_dynamic-update-slice_fusion.refs_0_), channel_id=1, source_target_pairs={{0,3},{1,0},{2,1},{3,2},{4,7},{5,4},{6,5},{7,6},{8,11},{9,8},{10,9... | collective-permute-start | bytes 1179656 | tf_op jit(solution)/shard_map/ppermute | solution.py:252
  29.9 12.5 %collective-permute-start.2 = (bf16[128,1536]{1,0:T(8,128)(2,1)S(1)}, bf16[128,1536]{1,0:T(8,128)(2,1)S(1)}, u32[]{:S(2)}, u32[]{:S(2)}) collective-permute-start(bf16[128,1536]{1,0:T(8,128)(2,1)S(1)} %constant_dynamic-update-slice_fusion.refs_0_), channel_id=1, source_target_pairs={{0,2},{1,3},{2,0},{3,1},{4,6},{5,7},{6,4},{7,5},{8,10},{9,11},{10,... | collective-permute-start | bytes 1179656 | tf_op jit(solution)/shard_map/ppermute | solution.py:252
  32.1 20.6 %collective-permute-start.1 = (bf16[128,1536]{1,0:T(8,128)(2,1)S(1)}, bf16[128,1536]{1,0:T(8,128)(2,1)S(1)}, u32[]{:S(2)}, u32[]{:S(2)}) collective-permute-start(bf16[128,1536]{1,0:T(8,128)(2,1)S(1)} %constant_dynamic-update-slice_fusion.refs_0_), channel_id=1, source_target_pairs={{0,1},{1,2},{2,3},{3,0},{4,5},{5,6},{6,7},{7,4},{8,9},{9,10},{10,1... | collective-permute-start | bytes 1179656 | tf_op jit(solution)/shard_map/ppermute | solution.py:252
  52.7 1.7 %copy-start = (bf16[1536,768]{1,0:T(8,128)(2,1)S(1)}, bf16[1536,768]{1,0:T(8,128)(2,1)}, u32[]{:S(2)}) copy-start(bf16[1536,768]{1,0:T(8,128)(2,1)} %b_ref.1) | copy-start | bytes 7077892
  55.3 26.2 %copy-start.4 = (bf16[128,384]{1,0:T(8,128)(2,1)S(1)}, bf16[128,384]{1,0:T(8,128)(2,1)}, u32[]{:S(2)}) copy-start(bf16[128,384]{1,0:T(8,128)(2,1)} %tokens_ref.1) | copy-start | bytes 294916
  55.3 26.2 %copy-start.7 = (s32[32]{0:T(128)S(1)}, s32[32]{0:T(128)}, u32[]{:S(2)}) copy-start(s32[32]{0:T(128)} %picks.5) | copy-start | bytes 388
  55.3 3.6 %collective-permute-start.4 = (bf16[144,768]{1,0:T(8,128)(2,1)S(1)}, bf16[144,768]{1,0:T(8,128)(2,1)S(1)}, u32[]{:S(2)}, u32[]{:S(2)}) collective-permute-start(bf16[144,768]{1,0:T(8,128)(2,1)S(1)} %get-tuple-element.18), channel_id=1, source_target_pairs={{0,128},{128,0},{256,384},{384,256},{1,129},{129,1},{257,385},{385... | collective-permute-start | bytes 663560 | tf_op jit(solution)/shard_map/ppermute | solution.py:271
  59.0 24.3 %copy-start.8 = (f32[144,768]{1,0:T(8,128)}, f32[144,768]{1,0:T(8,128)S(1)}, u32[]{:S(2)}) copy-start(f32[144,768]{1,0:T(8,128)S(1)} %convert_element_type.16) | copy-start | bytes 1327108
  59.1 10.1 %collective-permute-start.5 = (bf16[144,768]{1,0:T(8,128)(2,1)S(1)}, bf16[144,768]{1,0:T(8,128)(2,1)}, u32[]{:S(2)}, u32[]{:S(2)}) collective-permute-start(bf16[144,768]{1,0:T(8,128)(2,1)S(1)} %pad_maximum_fusion), channel_id=1, source_target_pairs={{0,256},{128,384},{256,0},{384,128},{1,257},{129,385},{257,1},{385... | collective-permute-start | bytes 663560 | tf_op jit(solution)/shard_map/ppermute | solution.py:274
  70.2 13.1 %copy-start.9 = (f32[144,768]{1,0:T(8,128)}, f32[144,768]{1,0:T(8,128)S(1)}, u32[]{:S(2)}) copy-start(f32[144,768]{1,0:T(8,128)S(1)} %convert_element_type.17) | copy-start | bytes 1327108
  71.0 10.4 %all-to-all-start.1 = ((bf16[4,144,128]{2,1,0:T(8,128)(2,1)}), bf16[4,144,128]{2,1,0:T(8,128)(2,1)S(1)}, u32[]{:S(2)}, u32[]{:S(2)}) async-start(bf16[4,144,128]{2,1,0:T(8,128)(2,1)} %get-tuple-element.21), calls=%async_computation.1 | async-start | bytes 294912 | tf_op jit(solution)/shard_map/all_to_all | solution.py:288
  83.3 25.5 %all-to-all-start.2 = ((bf16[8,512,128]{2,1,0:T(8,128)(2,1)}), bf16[8,512,128]{2,1,0:T(8,128)(2,1)S(1)}, u32[]{:S(2)}, u32[]{:S(2)}) async-start(bf16[8,512,128]{2,1,0:T(8,128)(2,1)} %shard_map.80), calls=%async_computation.2 | async-start | bytes 2097152 | tf_op jit(solution)/shard_map/all_to_all | solution.py:295
  88.0 10.2 %collective-permute-start.8 = (bf16[128,768]{1,0:T(8,128)(2,1)S(1)}, bf16[128,768]{1,0:T(8,128)(2,1)S(1)}, u32[]{:S(2)}, u32[]{:S(2)}) collective-permute-start(bf16[128,768]{1,0:T(8,128)(2,1)S(1)} %fusion.refs_0_), channel_id=1, source_target_pairs={{0,120},{8,0},{16,8},{24,16},{32,24},{40,32},{48,40},{56,48},{64,5... | collective-permute-start | bytes 589832 | tf_op jit(solution)/shard_map/ppermute | solution.py:285
  92.5 8.1 %collective-permute-start.7 = (bf16[128,768]{1,0:T(8,128)(2,1)S(1)}, bf16[128,768]{1,0:T(8,128)(2,1)S(1)}, u32[]{:S(2)}, u32[]{:S(2)}) collective-permute-start(bf16[128,768]{1,0:T(8,128)(2,1)S(1)} %fusion.refs_0_), channel_id=1, source_target_pairs={{0,8},{8,16},{16,24},{24,32},{32,40},{40,48},{48,56},{56,64},{64,7... | collective-permute-start | bytes 589832 | tf_op jit(solution)/shard_map/ppermute | solution.py:285
  94.4 13.6 %collective-permute-start.6 = (bf16[128,768]{1,0:T(8,128)(2,1)S(1)}, bf16[128,768]{1,0:T(8,128)(2,1)S(1)}, u32[]{:S(2)}, u32[]{:S(2)}) collective-permute-start(bf16[128,768]{1,0:T(8,128)(2,1)S(1)} %fusion.refs_0_), channel_id=1, source_target_pairs={{0,16},{8,24},{16,32},{24,40},{32,48},{40,56},{48,64},{56,72},{64,... | collective-permute-start | bytes 589832 | tf_op jit(solution)/shard_map/ppermute | solution.py:285
  97.5 0.7 copy-start.2
  108.1 0.7 copy-start.5
  108.7 0.9 copy-start.3
  109.7 0.9 copy-start.6
  111.0 4.7 %collective-permute-start.9 = (bf16[96,768]{1,0:T(8,128)(2,1)S(1)}, bf16[96,768]{1,0:T(8,128)(2,1)S(1)}, u32[]{:S(2)}, u32[]{:S(2)}) collective-permute-start(bf16[96,768]{1,0:T(8,128)(2,1)S(1)} %get-tuple-element.25), channel_id=1, source_target_pairs={{0,128},{128,0},{256,384},{384,256},{1,129},{129,1},{257,385},{385... | collective-permute-start | bytes 442376 | tf_op jit(solution)/shard_map/ppermute | solution.py:305

commit v12 on v11

--- a/solution.py
+++ b/solution.py
@@ -17,7 +17,7 @@
 SHIFTS = (0, 2, 1, -1)
 
 
-def call(kernel, inputs, outs, flops, scratch=(), place=VMEM, limit=40):
+def call(kernel, inputs, outs, flops, scratch=(), place=VMEM, limit=16):
     moved = sum(x.size * x.dtype.itemsize for x in list(inputs) + list(outs))
     return pl.pallas_call(
         kernel,
@@ -264,28 +264,24 @@
         4 * n_col * size * feat_grp * width,
         [pltpu.VMEM((n_col, 2, size, width), F32)],
     )
-    first, unused = lax.optimization_barrier((first, give))
-
     owner = lax.axis_index("row") // 4
     grp = lax.axis_index("grp")
-    taken = lax.ppermute(give, "grp", [(i, i ^ 1) for i in range(n_grp)]).astype(F32)
+    first, unused = lax.optimization_barrier((first, give))
+    u_own, x_send = call(
+        gather_kernel,
+        (first,),
+        [shape((out_rows, tok), BF), shape((n_grp, out_rows + out_rows // 2, LANES), BF)],
+        1000000,
+    )
+    x_got = lax.all_to_all(x_send, "grp", 0, 0)
+    taken = lax.ppermute(give, "grp", [(i, i ^ 1) for i in range(n_grp)])
+    taken, unused = lax.optimization_barrier((taken, x_send))
+    taken = taken.astype(F32)
     own_y = jnp.where(grp % 2 == owner % 2, keep[half:], taken[half:])
     keep = jnp.concatenate([keep[:half] + taken[:half], own_y], axis=0)
     taken = lax.ppermute(keep.astype(BF), "grp", [(i, i ^ 2) for i in range(n_grp)]).astype(F32)
     own_y = jnp.where(grp // 2 == owner // 2, keep[half:], taken[half:]).astype(BF)
     right = (keep[:half] + taken[:half]).astype(BF)
-    u_own, x_send = call(
-        gather_kernel,
-        (first,),
-        [shape((out_rows, tok), BF), shape((n_grp, out_rows + out_rows // 2, LANES), BF)],
-        1000000,
-    )
-    right, unused = lax.optimization_barrier((right, x_send))
-    rights = [right] + [
-        lax.ppermute(right, "row", [(i, (i + j) % n_row) for i in range(n_row)])
-        for j in SHIFTS[1:]
-    ]
-    x_got = lax.all_to_all(x_send, "grp", 0, 0)
     send = call(
         second_kernel,
         (sample_rows, u_own, x_got, own_y, tokens_in),
@@ -293,7 +289,11 @@
         2 * samp * tok * feat_row,
     )[0]
     got = lax.all_to_all(send, "col", 0, 0)
-
+    right, unused = lax.optimization_barrier((right, send))
+    rights = [right] + [
+        lax.ppermute(right, "row", [(i, (i + j) % n_row) for i in range(n_row)])
+        for j in SHIFTS[1:]
+    ]
     term, send = call(
         final_kernel,
         (got, *rights),

time: 118 us -> 112 us (0.949)
  local copies, waits for them, and re-layouts: 4.92 us -> 1.71 us
  waiting for transfers between devices: 39.9 us -> 36.7 us
  other arithmetic: 2.99 us -> 4.56 us
  starting transfers between devices: 57.2 us -> 55.8 us
    ppermute x1, waiting for transfers between devices: 5.75 us -> 1.38 us  [body(): lax.ppermute(keep.astype(BF), 'grp', [(i, i ^ 2) for i in range(n_grp)])]
    ppermute x1, waiting for transfers between devices: 0.01 us -> 4.2 us  [body(): lax.ppermute(picked, 'col', [(i, (i + 4) % n_col) for i in range(n_col)])]
    unnamed x21 -> x11, local copies, waits for them, and re-layouts: 4.91 us -> 1.7 us
    all_to_all x1, waiting for transfers between devices: 5.22 us -> 2.23 us  [body(): x_got = lax.all_to_all(x_send, 'grp', 0, 0)]
    all_to_all x1, starting transfers between devices: 5.18 us -> 3.97 us  [body(): x_got = lax.all_to_all(x_send, 'grp', 0, 0)]
  transfers between devices with their start and end apart: 13 -> 13, of which waited for: 8 -> 9; matrix products, arithmetic and copies ran while one was open for 2% -> 3% of each run, Pallas kernels for 5% -> 3%
where the time goes in v12:
time: 112 us; the launch traced here: 110 us
  starting transfers between devices  55.8 us (50%)
  waiting for transfers between devices  36.7 us (33%)
  Pallas kernels  10.7 us (10%)
  other arithmetic  4.56 us (4%)
  local copies, waits for them, and re-layouts  1.71 us (2%)
    ppermute x3, waiting for transfers between devices, along_y(): lax.ppermute(block, 'col', [(i, i - i % 4 + (i + k) % 4) for i in range(n...  18 us
    all_to_all x1, starting transfers between devices, body(): first = lax.all_to_all(payload, 'row', 0, 0)  15.8 us
    pallas_call x7, Pallas kernels, call(): pl.pallas_call(kernel, out_shape=outs, in_specs=[SMEM if x.dtype == jnp.i...  10.7 us
    ppermute x3, waiting for transfers between devices, body(): lax.ppermute(right, 'row', [(i, (i + j) % n_row) for i in range(n_row)])  10.6 us
    ppermute x3, starting transfers between devices, along_y(): lax.ppermute(block, 'col', [(i, i - i % 4 + (i + k) % 4) for i in range(n...  9.5 us
    ppermute x3, starting transfers between devices, body(): lax.ppermute(right, 'row', [(i, (i + j) % n_row) for i in range(n_row)])  9.16 us
    ppermute x1, starting transfers between devices, body(): lax.ppermute(keep.astype(BF), 'grp', [(i, i ^ 2) for i in range(n_grp)])  4.65 us
    ppermute x1, waiting for transfers between devices, body(): lax.ppermute(picked, 'col', [(i, (i + 4) % n_col) for i in range(n_col)])  4.2 us
  transfers between devices with their start and end apart: 13, of which 9 were waited for; matrix products, arithmetic and copies ran while one was open for 3% of the time, Pallas kernels for 3%

profile of v12, /device:TPU:1, one launch (start us, length us, event | category | flops | bytes accessed | tf_op | source)
XLA Modules:
  0.0 110.4 jit_solution(15438138076645781551)
XLA Ops:
  0.6 1.9 %shard_map.76.gy_ref = bf16[64,1536]{1,0:T(8,128)(2,1)} custom-call(s32[32]{0:T(128)} %picks.5, bf16[128,1536]{1,0:T(8,128)(2,1)} %g_ref.1), custom_call_target="tpu_custom_call" | custom-call | flops 25165824 | bytes 589952 | tf_op jit(solution)/shard_map/pallas_call | solution.py:22
  2.5 3.7 %shard_map.77 = bf16[16,120,128]{2,1,0:T(8,128)(2,1)} custom-call(s32[32]{0:T(128)} %picks.5, bf16[128,384]{1,0:T(8,128)(2,1)} %tokens_ref.1, bf16[1536,384]{1,0:T(8,128)(2,1)} %a_hbm.1), custom_call_target="tpu_custom_call" | custom-call | flops 150994944 | bytes 1769600 | tf_op jit(solution)/shard_map/pallas_call | solution.py:22
  6.3 15.8 %all-to-all-start = ((bf16[16,120,128]{2,1,0:T(8,128)(2,1)}), bf16[16,120,128]{2,1,0:T(8,128)(2,1)S(1)}, u32[]{:S(2)}, u32[]{:S(2)}) async-start(bf16[16,120,128]{2,1,0:T(8,128)(2,1)} %shard_map.77), calls=%async_computation | async-start | bytes 983040 | tf_op jit(solution)/shard_map/all_to_all | solution.py:249
  22.0 3.1 %collective-permute-start = (bf16[64,1536]{1,0:T(8,128)(2,1)S(1)}, bf16[64,1536]{1,0:T(8,128)(2,1)S(1)}, u32[]{:S(2)}, u32[]{:S(2)}) collective-permute-start(bf16[64,1536]{1,0:T(8,128)(2,1)S(1)} %copy-done.1), channel_id=1, source_target_pairs={{0,4},{1,5},{2,6},{3,7},{4,0},{5,1},{6,2},{7,3},{8,12},{9,13},{10,... | collective-permute-start | bytes 589832 | tf_op jit(solution)/shard_map/ppermute | solution.py:234
  25.2 4.2 %collective-permute-done = bf16[64,1536]{1,0:T(8,128)(2,1)S(1)} collective-permute-done((bf16[64,1536]{1,0:T(8,128)(2,1)S(1)}, bf16[64,1536]{1,0:T(8,128)(2,1)S(1)}, u32[]{:S(2)}, u32[]{:S(2)}) %collective-permute-start) | collective-permute-done | bytes 196640 | tf_op jit(solution)/shard_map/ppermute | solution.py:234
  29.4 4.6 %collective-permute-start.3 = (bf16[128,1536]{1,0:T(8,128)(2,1)S(1)}, bf16[128,1536]{1,0:T(8,128)(2,1)S(1)}, u32[]{:S(2)}, u32[]{:S(2)}) collective-permute-start(bf16[128,1536]{1,0:T(8,128)(2,1)S(1)} %constant_dynamic-update-slice_fusion.refs_0_), channel_id=1, source_target_pairs={{0,3},{1,0},{2,1},{3,2},{4,7},{5,4},{6,5},{7,6},{8,11},{9,8},{10,9... | collective-permute-start | bytes 1179656 | tf_op jit(solution)/shard_map/ppermute | solution.py:252
  34.0 2.2 %collective-permute-start.2 = (bf16[128,1536]{1,0:T(8,128)(2,1)S(1)}, bf16[128,1536]{1,0:T(8,128)(2,1)S(1)}, u32[]{:S(2)}, u32[]{:S(2)}) collective-permute-start(bf16[128,1536]{1,0:T(8,128)(2,1)S(1)} %constant_dynamic-update-slice_fusion.refs_0_), channel_id=1, source_target_pairs={{0,2},{1,3},{2,0},{3,1},{4,6},{5,7},{6,4},{7,5},{8,10},{9,11},{10,... | collective-permute-start | bytes 1179656 | tf_op jit(solution)/shard_map/ppermute | solution.py:252
  36.3 2.6 %collective-permute-start.1 = (bf16[128,1536]{1,0:T(8,128)(2,1)S(1)}, bf16[128,1536]{1,0:T(8,128)(2,1)S(1)}, u32[]{:S(2)}, u32[]{:S(2)}) collective-permute-start(bf16[128,1536]{1,0:T(8,128)(2,1)S(1)} %constant_dynamic-update-slice_fusion.refs_0_), channel_id=1, source_target_pairs={{0,1},{1,2},{2,3},{3,0},{4,5},{5,6},{6,7},{7,4},{8,9},{9,10},{10,1... | collective-permute-start | bytes 1179656 | tf_op jit(solution)/shard_map/ppermute | solution.py:252
  38.9 2.7 %collective-permute-done.3.refs_3_ = bf16[128,1536]{1,0:T(8,128)(2,1)S(1)} collective-permute-done((bf16[128,1536]{1,0:T(8,128)(2,1)S(1)}, bf16[128,1536]{1,0:T(8,128)(2,1)S(1)}, u32[]{:S(2)}, u32[]{:S(2)}) %collective-permute-start.3) | collective-permute-done | bytes 393248 | tf_op jit(solution)/shard_map/ppermute | solution.py:252
  41.6 4.3 %collective-permute-done.2.refs_2_ = bf16[128,1536]{1,0:T(8,128)(2,1)S(1)} collective-permute-done((bf16[128,1536]{1,0:T(8,128)(2,1)S(1)}, bf16[128,1536]{1,0:T(8,128)(2,1)S(1)}, u32[]{:S(2)}, u32[]{:S(2)}) %collective-permute-start.2) | collective-permute-done | bytes 393248 | tf_op jit(solution)/shard_map/ppermute | solution.py:252
  46.0 11.0 %collective-permute-done.1.refs_1_ = bf16[128,1536]{1,0:T(8,128)(2,1)S(1)} collective-permute-done((bf16[128,1536]{1,0:T(8,128)(2,1)S(1)}, bf16[128,1536]{1,0:T(8,128)(2,1)S(1)}, u32[]{:S(2)}, u32[]{:S(2)}) %collective-permute-start.1) | collective-permute-done | bytes 393248 | tf_op jit(solution)/shard_map/ppermute | solution.py:252
  56.9 1.7 %copy-done = bf16[1536,768]{1,0:T(8,128)(2,1)S(1)} copy-done((bf16[1536,768]{1,0:T(8,128)(2,1)S(1)}, bf16[1536,768]{1,0:T(8,128)(2,1)}, u32[]{:S(2)}) %copy-start) | copy-done | bytes 2359320
  58.6 0.9 shard_map.78
  59.5 2.5 %collective-permute-start.4 = (bf16[144,768]{1,0:T(8,128)(2,1)S(1)}, bf16[144,768]{1,0:T(8,128)(2,1)}, u32[]{:S(2)}, u32[]{:S(2)}) collective-permute-start(bf16[144,768]{1,0:T(8,128)(2,1)S(1)} %get-tuple-element.19), channel_id=1, source_target_pairs={{0,128},{128,0},{256,384},{384,256},{1,129},{129,1},{257,385},{385... | collective-permute-start | bytes 663560 | tf_op jit(solution)/shard_map/ppermute | solution.py:277
  62.1 0.8 shard_map.79
  63.2 1.0 convert_element_type.16
  64.3 4.6 %collective-permute-start.5 = (bf16[144,768]{1,0:T(8,128)(2,1)S(1)}, bf16[144,768]{1,0:T(8,128)(2,1)S(1)}, u32[]{:S(2)}, u32[]{:S(2)}) collective-permute-start(bf16[144,768]{1,0:T(8,128)(2,1)S(1)} %pad_maximum_fusion), channel_id=1, source_target_pairs={{0,256},{128,384},{256,0},{384,128},{1,257},{129,385},{257,1},{385... | collective-permute-start | bytes 663560 | tf_op jit(solution)/shard_map/ppermute | solution.py:282
  69.0 4.0 %all-to-all-start.1 = ((bf16[4,144,128]{2,1,0:T(8,128)(2,1)}), bf16[4,144,128]{2,1,0:T(8,128)(2,1)S(1)}, u32[]{:S(2)}, u32[]{:S(2)}) async-start(bf16[4,144,128]{2,1,0:T(8,128)(2,1)} %get-tuple-element.22), calls=%async_computation.1 | async-start | bytes 294912 | tf_op jit(solution)/shard_map/all_to_all | solution.py:276
  73.0 1.4 %collective-permute-done.5 = bf16[144,768]{1,0:T(8,128)(2,1)S(1)} collective-permute-done((bf16[144,768]{1,0:T(8,128)(2,1)S(1)}, bf16[144,768]{1,0:T(8,128)(2,1)S(1)}, u32[]{:S(2)}, u32[]{:S(2)}) %collective-permute-start.5) | collective-permute-done | bytes 221216 | tf_op jit(solution)/shard_map/ppermute | solution.py:282
  74.3 0.8 convert_element_type.17
  75.2 0.8 fusion.2.y_ref
  76.0 2.2 %all-to-all-done.1.x_ref = bf16[4,144,128]{2,1,0:T(8,128)(2,1)S(1)} async-done(((bf16[4,144,128]{2,1,0:T(8,128)(2,1)}), bf16[4,144,128]{2,1,0:T(8,128)(2,1)S(1)}, u32[]{:S(2)}, u32[]{:S(2)}) %all-to-all-start.1) | async-done | bytes 147488 | tf_op jit(solution)/shard_map/all_to_all | solution.py:276
  78.2 1.8 %shard_map.80 = bf16[8,512,128]{2,1,0:T(8,128)(2,1)} custom-call(s32[32]{0:T(128)S(1)} %copy-done.3, bf16[96,128]{1,0:T(8,128)(2,1)S(1)} %get-tuple-element.21.u_ref, bf16[4,144,128]{2,1,0:T(8,128)(2,1)S(1)} %all-to-all-done.1.x_ref, bf16[16,768]{1,0:T(8,128)(2,1)S(1)} %fusion.2.y_ref, bf16[128,384]{1,0:T(8,128)(2,1)S(1)} %copy-done.2), custom_call_target="tpu_custom_call" | custom-call | flops 3145728 | bytes 1343616 | tf_op jit(solution)/shard_map/pallas_call | solution.py:22
  80.0 3.6 %all-to-all-start.2 = ((bf16[8,512,128]{2,1,0:T(8,128)(2,1)}), bf16[8,512,128]{2,1,0:T(8,128)(2,1)S(1)}, u32[]{:S(2)}, u32[]{:S(2)}) async-start(bf16[8,512,128]{2,1,0:T(8,128)(2,1)} %shard_map.80), calls=%async_computation.2 | async-start | bytes 2097152 | tf_op jit(solution)/shard_map/all_to_all | solution.py:291
  83.6 1.2 %fusion.refs_0_ = bf16[128,768]{1,0:T(8,128)(2,1)S(1)} fusion(f32[144,768]{1,0:T(8,128)} %convert_element_type.17, f32[144,768]{1,0:T(8,128)} %copy-done.4, f32[144,768]{1,0:T(8,128)S(1)} %get-tuple-element.23), kind=kLoop, calls=%fused_computation.1 | loop fusion | flops 294912 | bytes 1376256 | tf_op jit(solution)/shard_map/convert_element_type | solution.py:284
  84.8 4.2 %collective-permute-start.8 = (bf16[128,768]{1,0:T(8,128)(2,1)S(1)}, bf16[128,768]{1,0:T(8,128)(2,1)S(1)}, u32[]{:S(2)}, u32[]{:S(2)}) collective-permute-start(bf16[128,768]{1,0:T(8,128)(2,1)S(1)} %fusion.refs_0_), channel_id=1, source_target_pairs={{0,120},{8,0},{16,8},{24,16},{32,24},{40,32},{48,40},{56,48},{64,5... | collective-permute-start | bytes 589832 | tf_op jit(solution)/shard_map/ppermute | solution.py:294
  89.0 1.9 %collective-permute-start.7 = (bf16[128,768]{1,0:T(8,128)(2,1)S(1)}, bf16[128,768]{1,0:T(8,128)(2,1)S(1)}, u32[]{:S(2)}, u32[]{:S(2)}) collective-permute-start(bf16[128,768]{1,0:T(8,128)(2,1)S(1)} %fusion.refs_0_), channel_id=1, source_target_pairs={{0,8},{8,16},{16,24},{24,32},{32,40},{40,48},{48,56},{56,64},{64,7... | collective-permute-start | bytes 589832 | tf_op jit(solution)/shard_map/ppermute | solution.py:294
  90.9 3.0 %collective-permute-start.6 = (bf16[128,768]{1,0:T(8,128)(2,1)S(1)}, bf16[128,768]{1,0:T(8,128)(2,1)S(1)}, u32[]{:S(2)}, u32[]{:S(2)}) collective-permute-start(bf16[128,768]{1,0:T(8,128)(2,1)S(1)} %fusion.refs_0_), channel_id=1, source_target_pairs={{0,16},{8,24},{16,32},{24,40},{32,48},{40,56},{48,64},{56,72},{64,... | collective-permute-start | bytes 589832 | tf_op jit(solution)/shard_map/ppermute | solution.py:294
  93.9 3.1 %collective-permute-done.7.refs_2_ = bf16[128,768]{1,0:T(8,128)(2,1)S(1)} collective-permute-done((bf16[128,768]{1,0:T(8,128)(2,1)S(1)}, bf16[128,768]{1,0:T(8,128)(2,1)S(1)}, u32[]{:S(2)}, u32[]{:S(2)}) %collective-permute-start.7) | collective-permute-done | bytes 196640 | tf_op jit(solution)/shard_map/ppermute | solution.py:294
  97.1 7.4 %collective-permute-done.6.refs_1_ = bf16[128,768]{1,0:T(8,128)(2,1)S(1)} collective-permute-done((bf16[128,768]{1,0:T(8,128)(2,1)S(1)}, bf16[128,768]{1,0:T(8,128)(2,1)S(1)}, u32[]{:S(2)}, u32[]{:S(2)}) %collective-permute-start.6) | collective-permute-done | bytes 196640 | tf_op jit(solution)/shard_map/ppermute | solution.py:294
  105.0 3.6 %collective-permute-start.9 = (bf16[96,768]{1,0:T(8,128)(2,1)S(1)}, bf16[96,768]{1,0:T(8,128)(2,1)S(1)}, u32[]{:S(2)}, u32[]{:S(2)}) collective-permute-start(bf16[96,768]{1,0:T(8,128)(2,1)S(1)} %get-tuple-element.27), channel_id=1, source_target_pairs={{0,128},{128,0},{256,384},{384,256},{1,129},{129,1},{257,385},{385... | collective-permute-start | bytes 442376 | tf_op jit(solution)/shard_map/ppermute | solution.py:305
  108.5 1.1 %shard_map.82 = (f32[48,1536]{1,0:T(8,128)}, f32[48,1536]{1,0:T(8,128)}) custom-call(bf16[8,512,128]{2,1,0:T(8,128)(2,1)S(1)} %all-to-all-done.2.got_ref, bf16[128,1536]{1,0:T(8,128)(2,1)S(1)} %constant_dynamic-update-slice_fusion.refs_0_, bf16[128,1536]{1,0:T(8,128)(2,1)S(1)} %collective-permute-done.1.refs_1_, ...), custom_call_target="tpu_custom_call" | custom-call | flops 201326592 | bytes 3211264 | tf_op jit(solution)/shard_map/pallas_call | solution.py:22
  (21 shorter events, 1.6 us)
Async XLA Ops:
  2.5 19.5 %copy-start.1 = (bf16[64,1536]{1,0:T(8,128)(2,1)S(1)}, bf16[64,1536]{1,0:T(8,128)(2,1)}, u32[]{:S(2)}) copy-start(bf16[64,1536]{1,0:T(8,128)(2,1)} %shard_map.76.gy_ref) | copy-start | bytes 589828
  6.3 55.8 %all-to-all-start = ((bf16[16,120,128]{2,1,0:T(8,128)(2,1)}), bf16[16,120,128]{2,1,0:T(8,128)(2,1)S(1)}, u32[]{:S(2)}, u32[]{:S(2)}) async-start(bf16[16,120,128]{2,1,0:T(8,128)(2,1)} %shard_map.77), calls=%async_computation | async-start | bytes 983040 | tf_op jit(solution)/shard_map/all_to_all | solution.py:249
  22.0 7.3 %collective-permute-start = (bf16[64,1536]{1,0:T(8,128)(2,1)S(1)}, bf16[64,1536]{1,0:T(8,128)(2,1)S(1)}, u32[]{:S(2)}, u32[]{:S(2)}) collective-permute-start(bf16[64,1536]{1,0:T(8,128)(2,1)S(1)} %copy-done.1), channel_id=1, source_target_pairs={{0,4},{1,5},{2,6},{3,7},{4,0},{5,1},{6,2},{7,3},{8,12},{9,13},{10,... | collective-permute-start | bytes 589832 | tf_op jit(solution)/shard_map/ppermute | solution.py:234
  29.4 12.2 %collective-permute-start.3 = (bf16[128,1536]{1,0:T(8,128)(2,1)S(1)}, bf16[128,1536]{1,0:T(8,128)(2,1)S(1)}, u32[]{:S(2)}, u32[]{:S(2)}) collective-permute-start(bf16[128,1536]{1,0:T(8,128)(2,1)S(1)} %constant_dynamic-update-slice_fusion.refs_0_), channel_id=1, source_target_pairs={{0,3},{1,0},{2,1},{3,2},{4,7},{5,4},{6,5},{7,6},{8,11},{9,8},{10,9... | collective-permute-start | bytes 1179656 | tf_op jit(solution)/shard_map/ppermute | solution.py:252
  34.0 11.9 %collective-permute-start.2 = (bf16[128,1536]{1,0:T(8,128)(2,1)S(1)}, bf16[128,1536]{1,0:T(8,128)(2,1)S(1)}, u32[]{:S(2)}, u32[]{:S(2)}) collective-permute-start(bf16[128,1536]{1,0:T(8,128)(2,1)S(1)} %constant_dynamic-update-slice_fusion.refs_0_), channel_id=1, source_target_pairs={{0,2},{1,3},{2,0},{3,1},{4,6},{5,7},{6,4},{7,5},{8,10},{9,11},{10,... | collective-permute-start | bytes 1179656 | tf_op jit(solution)/shard_map/ppermute | solution.py:252
  36.3 20.6 %collective-permute-start.1 = (bf16[128,1536]{1,0:T(8,128)(2,1)S(1)}, bf16[128,1536]{1,0:T(8,128)(2,1)S(1)}, u32[]{:S(2)}, u32[]{:S(2)}) collective-permute-start(bf16[128,1536]{1,0:T(8,128)(2,1)S(1)} %constant_dynamic-update-slice_fusion.refs_0_), channel_id=1, source_target_pairs={{0,1},{1,2},{2,3},{3,0},{4,5},{5,6},{6,7},{7,4},{8,9},{9,10},{10,1... | collective-permute-start | bytes 1179656 | tf_op jit(solution)/shard_map/ppermute | solution.py:252
  56.9 1.7 %copy-start = (bf16[1536,768]{1,0:T(8,128)(2,1)S(1)}, bf16[1536,768]{1,0:T(8,128)(2,1)}, u32[]{:S(2)}) copy-start(bf16[1536,768]{1,0:T(8,128)(2,1)} %b_ref.1) | copy-start | bytes 7077892
  59.5 18.7 %copy-start.2 = (bf16[128,384]{1,0:T(8,128)(2,1)S(1)}, bf16[128,384]{1,0:T(8,128)(2,1)}, u32[]{:S(2)}) copy-start(bf16[128,384]{1,0:T(8,128)(2,1)} %tokens_ref.1) | copy-start | bytes 294916
  59.5 18.7 %copy-start.3 = (s32[32]{0:T(128)S(1)}, s32[32]{0:T(128)}, u32[]{:S(2)}) copy-start(s32[32]{0:T(128)} %picks.5) | copy-start | bytes 388
  59.5 3.7 %collective-permute-start.4 = (bf16[144,768]{1,0:T(8,128)(2,1)S(1)}, bf16[144,768]{1,0:T(8,128)(2,1)}, u32[]{:S(2)}, u32[]{:S(2)}) collective-permute-start(bf16[144,768]{1,0:T(8,128)(2,1)S(1)} %get-tuple-element.19), channel_id=1, source_target_pairs={{0,128},{128,0},{256,384},{384,256},{1,129},{129,1},{257,385},{385... | collective-permute-start | bytes 663560 | tf_op jit(solution)/shard_map/ppermute | solution.py:277
  64.2 15.8 %copy-start.4 = (f32[144,768]{1,0:T(8,128)}, f32[144,768]{1,0:T(8,128)S(1)}, u32[]{:S(2)}) copy-start(f32[144,768]{1,0:T(8,128)S(1)} %convert_element_type.16) | copy-start | bytes 1327108
  64.3 10.0 %collective-permute-start.5 = (bf16[144,768]{1,0:T(8,128)(2,1)S(1)}, bf16[144,768]{1,0:T(8,128)(2,1)S(1)}, u32[]{:S(2)}, u32[]{:S(2)}) collective-permute-start(bf16[144,768]{1,0:T(8,128)(2,1)S(1)} %pad_maximum_fusion), channel_id=1, source_target_pairs={{0,256},{128,384},{256,0},{384,128},{1,257},{129,385},{257,1},{385... | collective-permute-start | bytes 663560 | tf_op jit(solution)/shard_map/ppermute | solution.py:282
  69.0 9.2 %all-to-all-start.1 = ((bf16[4,144,128]{2,1,0:T(8,128)(2,1)}), bf16[4,144,128]{2,1,0:T(8,128)(2,1)S(1)}, u32[]{:S(2)}, u32[]{:S(2)}) async-start(bf16[4,144,128]{2,1,0:T(8,128)(2,1)} %get-tuple-element.22), calls=%async_computation.1 | async-start | bytes 294912 | tf_op jit(solution)/shard_map/all_to_all | solution.py:276
  80.0 24.5 %all-to-all-start.2 = ((bf16[8,512,128]{2,1,0:T(8,128)(2,1)}), bf16[8,512,128]{2,1,0:T(8,128)(2,1)S(1)}, u32[]{:S(2)}, u32[]{:S(2)}) async-start(bf16[8,512,128]{2,1,0:T(8,128)(2,1)} %shard_map.80), calls=%async_computation.2 | async-start | bytes 2097152 | tf_op jit(solution)/shard_map/all_to_all | solution.py:291
  84.8 9.2 %collective-permute-start.8 = (bf16[128,768]{1,0:T(8,128)(2,1)S(1)}, bf16[128,768]{1,0:T(8,128)(2,1)S(1)}, u32[]{:S(2)}, u32[]{:S(2)}) collective-permute-start(bf16[128,768]{1,0:T(8,128)(2,1)S(1)} %fusion.refs_0_), channel_id=1, source_target_pairs={{0,120},{8,0},{16,8},{24,16},{32,24},{40,32},{48,40},{56,48},{64,5... | collective-permute-start | bytes 589832 | tf_op jit(solution)/shard_map/ppermute | solution.py:294
  89.0 8.1 %collective-permute-start.7 = (bf16[128,768]{1,0:T(8,128)(2,1)S(1)}, bf16[128,768]{1,0:T(8,128)(2,1)S(1)}, u32[]{:S(2)}, u32[]{:S(2)}) collective-permute-start(bf16[128,768]{1,0:T(8,128)(2,1)S(1)} %fusion.refs_0_), channel_id=1, source_target_pairs={{0,8},{8,16},{16,24},{24,32},{32,40},{40,48},{48,56},{56,64},{64,7... | collective-permute-start | bytes 589832 | tf_op jit(solution)/shard_map/ppermute | solution.py:294
  90.9 13.7 %collective-permute-start.6 = (bf16[128,768]{1,0:T(8,128)(2,1)S(1)}, bf16[128,768]{1,0:T(8,128)(2,1)S(1)}, u32[]{:S(2)}, u32[]{:S(2)}) collective-permute-start(bf16[128,768]{1,0:T(8,128)(2,1)S(1)} %fusion.refs_0_), channel_id=1, source_target_pairs={{0,16},{8,24},{16,32},{24,40},{32,48},{40,56},{48,64},{56,72},{64,... | collective-permute-start | bytes 589832 | tf_op jit(solution)/shard_map/ppermute | solution.py:294
  105.0 4.7 %collective-permute-start.9 = (bf16[96,768]{1,0:T(8,128)(2,1)S(1)}, bf16[96,768]{1,0:T(8,128)(2,1)S(1)}, u32[]{:S(2)}, u32[]{:S(2)}) collective-permute-start(bf16[96,768]{1,0:T(8,128)(2,1)S(1)} %get-tuple-element.27), channel_id=1, source_target_pairs={{0,128},{128,0},{256,384},{384,256},{1,129},{129,1},{257,385},{385... | collective-permute-start | bytes 442376 | tf_op jit(solution)/shard_map/ppermute | solution.py:305

commit v13 on v10

--- a/solution.py
+++ b/solution.py
@@ -17,7 +17,7 @@
 SHIFTS = (0, 2, 1, -1)
 
 
-def call(kernel, inputs, outs, flops, scratch=(), place=VMEM, limit=40):
+def call(kernel, inputs, outs, flops, scratch=(), place=VMEM, limit=16):
     moved = sum(x.size * x.dtype.itemsize for x in list(inputs) + list(outs))
     return pl.pallas_call(
         kernel,
@@ -51,8 +51,25 @@
     return jnp.where(want == lane, 1.0, 0.0).astype(BF)
 
 
-def first_kernel(picks, x_hbm, a_hbm, out_ref, x_ref, a_ref, sems):
-    n_row, depth, tok = out_ref.shape
+def pick_kernel(picks, g_ref, x_ref, rows_ref, samples_ref, block_ref):
+    tok = g_ref.shape[0]
+    samp = picks.shape[0]
+    plane = lax.axis_index("row") % 4
+    first = lax.axis_index("col") * tok
+    count = rows_ref.shape[0]
+    ours = [64 * (i // 16) + 16 * plane + i % 16 for i in range(count)]
+    hot = rows_hot(ours + [picks[i] - first for i in range(samp)], tok)
+    chosen = jnp.dot(hot, g_ref[...], preferred_element_type=F32).astype(BF)
+    rows_ref[...] = chosen[:count]
+    samples_ref[...] = chosen[count:]
+    hot = rows_hot(own_picks(picks, samp // 4, tok), tok)
+    chosen = jnp.dot(hot, x_ref[...], preferred_element_type=F32)
+    strips = [chosen[:, k : k + LANES] for k in range(0, chosen.shape[1], LANES)]
+    block_ref[...] = jnp.concatenate(strips, axis=0).astype(BF)
+
+
+def first_kernel(x_hbm, a_hbm, out_ref, x_ref, a_ref, sems):
+    n_row, out_rows, tok = out_ref.shape
     parts = sems.shape[0] - 1
     step = a_ref.shape[0] // parts
     copies = [pltpu.make_async_copy(x_hbm, x_ref, sems.at[parts])]
@@ -61,39 +78,18 @@
         copies.append(pltpu.make_async_copy(a_hbm.at[span], a_ref.at[span], sems.at[p]))
     for copy in copies:
         copy.start()
-    out_rows = a_ref.shape[0] // n_row
-    quarter = picks.shape[0] // 4
-    hot = rows_hot(own_picks(picks, quarter, tok), tok)
     copies[0].wait()
-    chosen = jnp.dot(hot, x_ref[...], preferred_element_type=F32)
-    strips = [chosen[:, k : k + LANES] for k in range(0, chosen.shape[1], LANES)]
-    block = jnp.concatenate(strips, axis=0).astype(BF)
-    out_ref[:, out_rows:, :] = jnp.broadcast_to(block[None], (n_row,) + block.shape)
     each = step // out_rows
     for p in range(parts):
         copies[p + 1].wait()
         rows = a_ref[p * step : (p + 1) * step, :]
         part = lax.dot_general(rows, x_ref[...], LAST, preferred_element_type=F32)
-        out_ref[p * each : (p + 1) * each, :out_rows, :] = part.astype(BF).reshape(
-            each, out_rows, tok
-        )
-
-
-def pick_kernel(picks, g_ref, out_ref):
-    tok = g_ref.shape[0]
-    samp = picks.shape[0]
-    plane = lax.axis_index("row") % 4
-    first = lax.axis_index("col") * tok
-    count = out_ref.shape[0] - samp
-    ours = [64 * (i // 16) + 16 * plane + i % 16 for i in range(count)]
-    hot = rows_hot(ours + [picks[i] - first for i in range(samp)], tok)
-    out_ref[...] = jnp.dot(hot, g_ref[...], preferred_element_type=F32).astype(BF)
-
-
-def right_kernel(b_ref, gy_ref, *refs):
-    blocks, keep_ref, give_ref, held = refs[:-3], refs[-3], refs[-2], refs[-1]
+        out_ref[p * each : (p + 1) * each] = part.astype(BF).reshape(each, out_rows, tok)
+
+
+def right_kernel(b_ref, y_ref, g_ref, keep_ref, give_ref, held):
     n_blk, unused, size, width = held.shape
-    rows = jnp.concatenate([block[...] for block in blocks], axis=0)
+    rows = g_ref[...].reshape(n_blk * 2 * size, g_ref.shape[2])
     term = jnp.dot(rows, b_ref[...], preferred_element_type=F32)
     held[...] = term.reshape(held.shape)
     core = lax.axis_index("grp") % 2
@@ -101,42 +97,33 @@
     keep_ref[:cut, :] = held[:, core].reshape(cut, width)
     give_ref[:cut, :] = held[:, 1 - core].reshape(cut, width).astype(BF)
     feat = width // 2
-    samp = 2 * (give_ref.shape[0] - cut)
+    samp = y_ref.shape[0]
     begin = pl.multiple_of((lax.axis_index("row") % 4) * feat, LANES)
-    own = gy_ref[gy_ref.shape[0] - samp :, pl.ds(begin, feat)]
+    own = y_ref[:, pl.ds(begin, feat)]
     own = jnp.concatenate([own[: samp // 2], own[samp // 2 :]], axis=1)
     keep_ref[cut:, :] = own.astype(F32)
     give_ref[cut:, :] = own
 
 
-def gather_kernel(got_ref, u_ref, x_ref):
-    n_grp, x_rows, unused = x_ref.shape
-    n_row, depth, tok = got_ref.shape
-    out_rows = u_ref.shape[0]
+def second_kernel(picks, got_ref, y_ref, tokens_ref, out_ref):
+    n_col, depth, unused = out_ref.shape
+    n_row, rows, tok = got_ref.shape
+    feat = tokens_ref.shape[1]
+    samp = picks.shape[0]
+    tile = feat // n_col
+    out_rows = rows - samp // 4 * feat // LANES
     total = got_ref[0, :out_rows, :].astype(F32)
     for r in range(1, n_row):
         total = total + got_ref[r, :out_rows, :].astype(F32)
-    u_ref[...] = total.astype(BF)
-    per = n_row // n_grp
-    for g in range(n_grp):
-        block = got_ref[g * per : (g + 1) * per, out_rows:, :].astype(F32)
-        x_ref[g] = block.reshape(x_rows, tok).astype(BF)
-
-
-def second_kernel(picks, u_ref, x_ref, y_ref, tokens_ref, out_ref):
-    n_col, depth, unused = out_ref.shape
-    out_rows, tok = u_ref.shape
-    feat = tokens_ref.shape[1]
-    samp = picks.shape[0]
-    tile = feat // n_col
+    u_block = total.astype(BF)
+    x_block = got_ref[:, out_rows:, :].astype(F32)
+    x_block = x_block.reshape(depth - samp - out_rows, LANES).astype(BF)
     begin = lax.axis_index("col") * tok
     hot = rows_hot([picks[i] - begin for i in range(samp)], tok)
     chosen = jnp.dot(hot, tokens_ref[...], preferred_element_type=F32)
     own = y_ref[...].astype(F32)
     own = jnp.concatenate([own[:, :feat], own[:, feat:]], axis=0)
     empty = jnp.zeros((samp, LANES - 2 * tile), F32)
-    u_block = u_ref[...]
-    x_block = x_ref[...].reshape(x_ref.shape[0] * x_ref.shape[1], LANES)
     for c in range(n_col):
         span = slice(c * tile, (c + 1) * tile)
         out_ref[c, :out_rows, :] = u_block
@@ -156,9 +143,9 @@
         plane = lax.rem(row - shift + spread, spread)
         for k in range(n_col):
             span = slice(k * size, (k + 1) * size)
-            held[source_of(k), core, plane] = v_refs[j][span, :]
+            held[k, core, plane] = v_refs[j][span, :]
             span = slice(j * cut + k * size, j * cut + (k + 1) * size)
-            held[source_of(k), 1 - core, plane] = pair_ref[span, :]
+            held[k, 1 - core, plane] = pair_ref[span, :]
     tokens = 2 * spread * size
     total = None
     for c in range(0, n_col, 2):
@@ -179,10 +166,12 @@
     scale = 1.0 / total
     count = 4 * quarter * (width // LANES)
     span = got_ref[:, depth - samp - count : depth - samp, :].astype(F32)
-    span = span.reshape(n_col, 4, count // 4, LANES)
+    per = width // LANES // 4
+    span = span.reshape(n_col, 4, 4, per * quarter, LANES)
     strips = []
     for t in range(width // LANES):
-        strip = span[:, :, t * quarter : (t + 1) * quarter, :].reshape(total, LANES)
+        at = t % per * quarter
+        strip = span[:, t // per, :, at : at + quarter, :].reshape(total, LANES)
         strips.append(strip.astype(BF))
     right = jnp.concatenate(strips, axis=1)
     left = got_ref[:, depth - samp :, :].reshape(total, LANES)
@@ -211,18 +200,24 @@
     size = tok // 2 // spread
     shape = jax.ShapeDtypeStruct
 
-    picked = call(
+    rows, samples, block = call(
         pick_kernel,
-        (sample_rows, cotangent),
-        [shape((2 * size + samp, feat_grp), BF)],
+        (sample_rows, cotangent, tokens_in),
+        [
+            shape((2 * size, feat_grp), BF),
+            shape((samp, feat_grp), BF),
+            shape((strip, LANES), BF),
+        ],
         2 * 64 * tok * feat_grp,
-    )[0]
-    beside = lax.ppermute(picked, "col", [(i, (i + 4) % n_col) for i in range(n_col)])
-    picked, x_in = lax.optimization_barrier((picked, tokens_in))
-    payload = call(
+        limit=56,
+    )
+    rows = lax.all_to_all(jnp.broadcast_to(rows, (n_col,) + rows.shape), "col", 0, 0)
+    turn = [(g * n_row + r, n_grp * r + g) for g in range(n_grp) for r in range(n_row)]
+    block = lax.ppermute(block, ("grp", "row"), turn)
+    parts = call(
         first_kernel,
-        (sample_rows, x_in, act_inverse),
-        [shape((n_row, out_rows + strip, tok), BF)],
+        (tokens_in, act_inverse),
+        [shape((n_row, out_rows, tok), BF)],
         2 * feat_grp * feat_row * tok,
         [
             pltpu.VMEM(tokens_in.shape, BF),
@@ -232,27 +227,19 @@
         pl.BlockSpec(memory_space=pl.ANY),
         limit=56,
     )[0]
+    payload = jnp.concatenate(
+        [parts, jnp.broadcast_to(block, (n_row,) + block.shape)], axis=1
+    )
     first = lax.all_to_all(payload, "row", 0, 0)
 
-    def along_y(block, k):
-        return lax.ppermute(
-            block, "col", [(i, i - i % 4 + (i + k) % 4) for i in range(n_col)]
-        )
-
-    cut = 2 * size
-    pair = jnp.concatenate([picked[:cut], beside[:cut]], axis=0)
-    pairs = [pair] + [along_y(pair, k) for k in range(1, 4)]
     half = n_col * size
-    extra = samp // 2
     keep, give = call(
         right_kernel,
-        (grad_inverse, picked, *pairs),
-        [shape((half + extra, width), F32), shape((half + extra, width), BF)],
+        (grad_inverse, samples, rows),
+        [shape((half + samp // 2, width), F32), shape((half + samp // 2, width), BF)],
         4 * n_col * size * feat_grp * width,
         [pltpu.VMEM((n_col, 2, size, width), F32)],
     )
-    first, unused = lax.optimization_barrier((first, give))
-
     owner = lax.axis_index("row") // 4
     grp = lax.axis_index("grp")
     taken = lax.ppermute(give, "grp", [(i, i ^ 1) for i in range(n_grp)]).astype(F32)
@@ -269,24 +256,21 @@
         jnp.concatenate(rights, axis=0), "grp", [(i, i ^ 1) for i in range(n_grp)]
     )
 
-    unused, picked_y, beside_y = lax.optimization_barrier((keep, picked[cut:], beside[cut:]))
-    samples = jnp.concatenate([picked_y, beside_y], axis=0)
-    samples = [samples] + [along_y(samples, k) for k in range(1, 4)]
-
-    u_own, x_send = call(
-        gather_kernel,
-        (first,),
-        [shape((out_rows, tok), BF), shape((n_grp, strip * n_row // n_grp, LANES), BF)],
-        1000000,
-    )
-    x_got = lax.all_to_all(x_send, "grp", 0, 0)
     send = call(
         second_kernel,
-        (sample_rows, u_own, x_got, own_y, tokens_in),
+        (sample_rows, first, own_y, tokens_in),
         [shape((n_col, out_rows + strip * n_row + samp, LANES), BF)],
         2 * samp * tok * feat_row,
     )[0]
     got = lax.all_to_all(send, "col", 0, 0)
+
+    unused, samples = lax.optimization_barrier((send, samples))
+    beside = lax.ppermute(samples, "col", [(i, (i + 4) % n_col) for i in range(n_col)])
+    samples = jnp.concatenate([samples, beside], axis=0)
+    pairs = [samples] + [
+        lax.ppermute(samples, "col", [(i, i - i % 4 + (i + k) % 4) for i in range(n_col)])
+        for k in range(1, 4)
+    ]
 
     precond = call(
         final_kernel,
@@ -297,7 +281,7 @@
     )[0]
     act_cov, grad_cov = call(
         factor_kernel,
-        (got, *samples),
+        (got, *pairs),
         [shape((tile, feat_grp), F32)] * 2,
         4 * LANES * samp * n_col * feat_grp,
     )

time: 112 us -> 114 us (1.018)
  the two profiles are of different devices: /device:TPU:1 before, /device:TPU:32 now
where the time goes in v13:
time: 114 us; the launch traced here: 113 us
  starting transfers between devices  70.5 us (62%)
  waiting for transfers between devices  24.2 us (21%)
  Pallas kernels  10.3 us (9%)
  other arithmetic  3.96 us (3%)
  local copies, waits for them, and re-layouts  2.68 us (2%)
    all_to_all x1, starting transfers between devices, body(): first = lax.all_to_all(payload, 'row', 0, 0)  20.3 us
    ppermute x3, starting transfers between devices, body(): lax.ppermute(right, 'row', [(i, (i + j) % n_row) for i in range(n_row)])  11.3 us
    pallas_call x6, Pallas kernels, call(): pl.pallas_call(kernel, out_shape=outs, in_specs=[SMEM if x.dtype == jnp.i...  10.3 us
    ppermute x3, starting transfers between devices, body(): lax.ppermute(samples, 'col', [(i, i - i % 4 + (i + k) % 4) for i in range...  10.1 us
    ppermute x1, waiting for transfers between devices, body(): lax.ppermute(keep.astype(BF), 'grp', [(i, i ^ 2) for i in range(n_grp)])  8.9 us
    ppermute x1, starting transfers between devices, body(): block = lax.ppermute(block, ('grp', 'row'), turn)  7.88 us
    ppermute x1, waiting for transfers between devices, body(): lax.ppermute(samples, 'col', [(i, (i + 4) % n_col) for i in range(n_col)])  5.86 us
    all_to_all x1, starting transfers between devices, body(): got = lax.all_to_all(send, 'col', 0, 0)  5.69 us
  transfers between devices with their start and end apart: 14, of which 7 were waited for; matrix products, arithmetic and copies ran while one was open for 4% of the time, Pallas kernels for 7%

profile of v13, /device:TPU:32, one launch (start us, length us, event | category | flops | bytes accessed | tf_op | source)
XLA Modules:
  0.0 112.7 jit_solution(9998722903065602190)
XLA Ops:
  0.6 1.9 %shard_map.77 = (bf16[32,1536]{1,0:T(8,128)(2,1)}, bf16[32,1536]{1,0:T(8,128)(2,1)}, bf16[24,128]{1,0:T(8,128)(2,1)}) custom-call(s32[32]{0:T(128)} %picks.3, bf16[128,1536]{1,0:T(8,128)(2,1)} %g_ref.1, bf16[128,384]{1,0:T(8,128)(2,1)} %tokens_ref.1), custom_call_target="tpu_custom_call" | custom-call | flops 25165824 | bytes 694400 | tf_op jit(solution)/shard_map/pallas_call | solution.py:22
  2.5 1.9 %broadcast_in_dim.7 = bf16[8,32,1536]{2,1,0:T(8,128)(2,1)} broadcast(bf16[32,1536]{1,0:T(8,128)(2,1)} %get-tuple-element.13), dimensions={1,2} | broadcast | bytes 884736 | tf_op jit(solution)/shard_map/broadcast_in_dim | solution.py:214
  4.4 5.4 %all-to-all-start.1 = ((bf16[8,32,1536]{2,1,0:T(8,128)(2,1)}), bf16[8,32,1536]{2,1,0:T(8,128)(2,1)S(1)}, u32[]{:S(2)}, u32[]{:S(2)}) async-start(bf16[8,32,1536]{2,1,0:T(8,128)(2,1)} %broadcast_in_dim.7), calls=%async_computation.1 | async-start | bytes 1572864 | tf_op jit(solution)/shard_map/all_to_all | solution.py:214
  9.8 7.9 %collective-permute-start = (bf16[24,128]{1,0:T(8,128)(2,1)S(1)}, bf16[24,128]{1,0:T(8,128)(2,1)S(1)}, u32[]{:S(2)}, u32[]{:S(2)}) collective-permute-start(bf16[24,128]{1,0:T(8,128)(2,1)S(1)} %copy-done.6), channel_id=1, source_target_pairs={{0,0},{8,32},{16,64},{24,96},{32,128},{40,160},{48,192},{56,224},{... | collective-permute-start | bytes 18440 | tf_op jit(solution)/shard_map/ppermute | solution.py:216
  17.7 2.9 %shard_map.76 = bf16[16,96,128]{2,1,0:T(8,128)(2,1)} custom-call(bf16[128,384]{1,0:T(8,128)(2,1)} %tokens_ref.1, bf16[1536,384]{1,0:T(8,128)(2,1)} %a_hbm.1), custom_call_target="tpu_custom_call" | custom-call | flops 150994944 | bytes 1671168 | tf_op jit(solution)/shard_map/pallas_call | solution.py:22
  20.6 1.8 %pad_maximum_fusion.1 = bf16[16,120,128]{2,1,0:T(8,128)(2,1)} fusion(bf16[16,24,128]{2,1,0:T(8,128)(2,1)S(1)} %broadcast_in_dim.6, bf16[16,96,128]{2,1,0:T(8,128)(2,1)} %shard_map.76), kind=kLoop, calls=%fused_computation.1 | loop fusion | flops 983040 | bytes 983040 | tf_op jit(solution)/shard_map/concatenate | solution.py:230
  22.5 20.3 %all-to-all-start = ((bf16[16,120,128]{2,1,0:T(8,128)(2,1)}), bf16[16,120,128]{2,1,0:T(8,128)(2,1)}, u32[]{:S(2)}, u32[]{:S(2)}) async-start(bf16[16,120,128]{2,1,0:T(8,128)(2,1)} %pad_maximum_fusion.1), calls=%async_computation | async-start | bytes 983040 | tf_op jit(solution)/shard_map/all_to_all | solution.py:233
  42.8 0.9 shard_map.78
  43.7 0.8 copy-done.1
  44.4 2.0 %collective-permute-start.1 = (bf16[144,768]{1,0:T(8,128)(2,1)S(1)}, bf16[144,768]{1,0:T(8,128)(2,1)S(1)}, u32[]{:S(2)}, u32[]{:S(2)}) collective-permute-start(bf16[144,768]{1,0:T(8,128)(2,1)S(1)} %get-tuple-element.15), channel_id=1, source_target_pairs={{0,128},{128,0},{256,384},{384,256},{1,129},{129,1},{257,385},{385... | collective-permute-start | bytes 663560 | tf_op jit(solution)/shard_map/ppermute | solution.py:245
  46.5 1.4 %collective-permute-done.1 = bf16[144,768]{1,0:T(8,128)(2,1)S(1)} collective-permute-done((bf16[144,768]{1,0:T(8,128)(2,1)S(1)}, bf16[144,768]{1,0:T(8,128)(2,1)S(1)}, u32[]{:S(2)}, u32[]{:S(2)}) %collective-permute-start.1) | collective-permute-done | bytes 221216 | tf_op jit(solution)/shard_map/ppermute | solution.py:245
  48.0 0.8 fusion.3
  48.8 1.1 fusion.1
  49.9 1.9 %collective-permute-start.2 = (bf16[144,768]{1,0:T(8,128)(2,1)S(1)}, bf16[144,768]{1,0:T(8,128)(2,1)S(1)}, u32[]{:S(2)}, u32[]{:S(2)}) collective-permute-start(bf16[144,768]{1,0:T(8,128)(2,1)S(1)} %pad_maximum_fusion.2), channel_id=1, source_target_pairs={{0,256},{128,384},{256,0},{384,128},{1,257},{129,385},{257,1},{385... | collective-permute-start | bytes 663560 | tf_op jit(solution)/shard_map/ppermute | solution.py:248
  51.9 8.9 %collective-permute-done.2 = bf16[144,768]{1,0:T(8,128)(2,1)S(1)} collective-permute-done((bf16[144,768]{1,0:T(8,128)(2,1)S(1)}, bf16[144,768]{1,0:T(8,128)(2,1)S(1)}, u32[]{:S(2)}, u32[]{:S(2)}) %collective-permute-start.2) | collective-permute-done | bytes 221216 | tf_op jit(solution)/shard_map/ppermute | solution.py:248
  60.9 2.1 %collective-permute-start.5 = (bf16[128,768]{1,0:T(8,128)(2,1)S(1)}, bf16[128,768]{1,0:T(8,128)(2,1)S(1)}, u32[]{:S(2)}, u32[]{:S(2)}) collective-permute-start(bf16[128,768]{1,0:T(8,128)(2,1)S(1)} %fusion.refs_0_), channel_id=1, source_target_pairs={{0,120},{8,0},{16,8},{24,16},{32,24},{40,32},{48,40},{56,48},{64,5... | collective-permute-start | bytes 589832 | tf_op jit(solution)/shard_map/ppermute | solution.py:252
  63.0 3.8 %collective-permute-start.4 = (bf16[128,768]{1,0:T(8,128)(2,1)S(1)}, bf16[128,768]{1,0:T(8,128)(2,1)S(1)}, u32[]{:S(2)}, u32[]{:S(2)}) collective-permute-start(bf16[128,768]{1,0:T(8,128)(2,1)S(1)} %fusion.refs_0_), channel_id=1, source_target_pairs={{0,8},{8,16},{16,24},{24,32},{32,40},{40,48},{48,56},{56,64},{64,7... | collective-permute-start | bytes 589832 | tf_op jit(solution)/shard_map/ppermute | solution.py:252
  66.8 5.5 %collective-permute-start.3 = (bf16[128,768]{1,0:T(8,128)(2,1)S(1)}, bf16[128,768]{1,0:T(8,128)(2,1)S(1)}, u32[]{:S(2)}, u32[]{:S(2)}) collective-permute-start(bf16[128,768]{1,0:T(8,128)(2,1)S(1)} %fusion.refs_0_), channel_id=1, source_target_pairs={{0,16},{8,24},{16,32},{24,40},{32,48},{40,56},{48,64},{56,72},{64,... | collective-permute-start | bytes 589832 | tf_op jit(solution)/shard_map/ppermute | solution.py:252
  72.3 2.4 %shard_map.79 = bf16[8,512,128]{2,1,0:T(8,128)(2,1)} custom-call(s32[32]{0:T(128)S(1)} %copy-done.5, bf16[16,120,128]{2,1,0:T(8,128)(2,1)} %all-to-all-done.got_ref, bf16[16,768]{1,0:T(8,128)(2,1)S(1)} %fusion.2.y_ref, bf16[128,384]{1,0:T(8,128)(2,1)S(1)} %copy-done.3), custom_call_target="tpu_custom_call" | custom-call | flops 3145728 | bytes 1663104 | tf_op jit(solution)/shard_map/pallas_call | solution.py:22
  74.7 5.7 %all-to-all-start.2 = ((bf16[8,512,128]{2,1,0:T(8,128)(2,1)}), bf16[8,512,128]{2,1,0:T(8,128)(2,1)S(1)}, u32[]{:S(2)}, u32[]{:S(2)}) async-start(bf16[8,512,128]{2,1,0:T(8,128)(2,1)} %shard_map.79), calls=%async_computation.2 | async-start | bytes 2097152 | tf_op jit(solution)/shard_map/all_to_all | solution.py:265
  80.4 2.6 %collective-permute-done.3.refs_1_ = bf16[128,768]{1,0:T(8,128)(2,1)S(1)} collective-permute-done((bf16[128,768]{1,0:T(8,128)(2,1)S(1)}, bf16[128,768]{1,0:T(8,128)(2,1)S(1)}, u32[]{:S(2)}, u32[]{:S(2)}) %collective-permute-start.3) | collective-permute-done | bytes 196640 | tf_op jit(solution)/shard_map/ppermute | solution.py:252
  83.0 1.9 %collective-permute-start.6 = (bf16[512,768]{1,0:T(8,128)(2,1)S(1)}, bf16[512,768]{1,0:T(8,128)(2,1)S(1)}, u32[]{:S(2)}, u32[]{:S(2)}) collective-permute-start(bf16[512,768]{1,0:T(8,128)(2,1)S(1)} %pad_maximum_fusion), channel_id=1, source_target_pairs={{0,128},{128,0},{256,384},{384,256},{1,129},{129,1},{257,385},{385... | collective-permute-start | bytes 2359304 | tf_op jit(solution)/shard_map/ppermute | solution.py:255
  85.0 3.9 %collective-permute-start.7 = (bf16[32,1536]{1,0:T(8,128)(2,1)S(1)}, bf16[32,1536]{1,0:T(8,128)(2,1)S(1)}, u32[]{:S(2)}, u32[]{:S(2)}) collective-permute-start(bf16[32,1536]{1,0:T(8,128)(2,1)S(1)} %copy-done.4), channel_id=1, source_target_pairs={{0,4},{1,5},{2,6},{3,7},{4,0},{5,1},{6,2},{7,3},{8,12},{9,13},{10,... | collective-permute-start | bytes 294920 | tf_op jit(solution)/shard_map/ppermute | solution.py:268
  88.9 5.9 %collective-permute-done.7 = bf16[32,1536]{1,0:T(8,128)(2,1)S(1)} collective-permute-done((bf16[32,1536]{1,0:T(8,128)(2,1)S(1)}, bf16[32,1536]{1,0:T(8,128)(2,1)S(1)}, u32[]{:S(2)}, u32[]{:S(2)}) %collective-permute-start.7) | collective-permute-done | bytes 98336 | tf_op jit(solution)/shard_map/ppermute | solution.py:268
  94.8 4.5 %collective-permute-start.10 = (bf16[64,1536]{1,0:T(8,128)(2,1)S(1)}, bf16[64,1536]{1,0:T(8,128)(2,1)S(1)}, u32[]{:S(2)}, u32[]{:S(2)}) collective-permute-start(bf16[64,1536]{1,0:T(8,128)(2,1)S(1)} %constant_dynamic-update-slice_fusion.refs_0_), channel_id=1, source_target_pairs={{0,3},{1,0},{2,1},{3,2},{4,7},{5,4},{6,5},{7,6},{8,11},{9,8},{10,9... | collective-permute-start | bytes 589832 | tf_op jit(solution)/shard_map/ppermute | solution.py:271
  99.3 2.8 %collective-permute-start.9 = (bf16[64,1536]{1,0:T(8,128)(2,1)S(1)}, bf16[64,1536]{1,0:T(8,128)(2,1)S(1)}, u32[]{:S(2)}, u32[]{:S(2)}) collective-permute-start(bf16[64,1536]{1,0:T(8,128)(2,1)S(1)} %constant_dynamic-update-slice_fusion.refs_0_), channel_id=1, source_target_pairs={{0,2},{1,3},{2,0},{3,1},{4,6},{5,7},{6,4},{7,5},{8,10},{9,11},{10,... | collective-permute-start | bytes 589832 | tf_op jit(solution)/shard_map/ppermute | solution.py:271
  102.1 2.8 %collective-permute-start.8 = (bf16[64,1536]{1,0:T(8,128)(2,1)S(1)}, bf16[64,1536]{1,0:T(8,128)(2,1)S(1)}, u32[]{:S(2)}, u32[]{:S(2)}) collective-permute-start(bf16[64,1536]{1,0:T(8,128)(2,1)S(1)} %constant_dynamic-update-slice_fusion.refs_0_), channel_id=1, source_target_pairs={{0,1},{1,2},{2,3},{3,0},{4,5},{5,6},{6,7},{7,4},{8,9},{9,10},{10,1... | collective-permute-start | bytes 589832 | tf_op jit(solution)/shard_map/ppermute | solution.py:271
  104.9 1.2 %shard_map.80 = f32[96,768]{1,0:T(8,128)} custom-call(bf16[8,512,128]{2,1,0:T(8,128)(2,1)S(1)} %all-to-all-done.2.got_ref, bf16[512,768]{1,0:T(8,128)(2,1)S(1)} %collective-permute-done.6.pair_ref, bf16[128,768]{1,0:T(8,128)(2,1)S(1)} %fusion.refs_0_, bf16[128,768]{1,0:T(8,128)(2,1)S(1)} %collective-permute-done.3.refs_1_, ...), custom_call_target="tpu_custom_call" | custom-call | flops 150994944 | bytes 2916352 | tf_op jit(solution)/shard_map/pallas_call | solution.py:22
  106.2 0.5 collective-permute-done.10.refs_3_
  106.7 2.8 %collective-permute-done.9.refs_2_ = bf16[64,1536]{1,0:T(8,128)(2,1)S(1)} collective-permute-done((bf16[64,1536]{1,0:T(8,128)(2,1)S(1)}, bf16[64,1536]{1,0:T(8,128)(2,1)S(1)}, u32[]{:S(2)}, u32[]{:S(2)}) %collective-permute-start.9) | collective-permute-done | bytes 196640 | tf_op jit(solution)/shard_map/ppermute | solution.py:271
  109.5 2.1 %collective-permute-done.8.refs_1_ = bf16[64,1536]{1,0:T(8,128)(2,1)S(1)} collective-permute-done((bf16[64,1536]{1,0:T(8,128)(2,1)S(1)}, bf16[64,1536]{1,0:T(8,128)(2,1)S(1)}, u32[]{:S(2)}, u32[]{:S(2)}) %collective-permute-start.8) | collective-permute-done | bytes 196640 | tf_op jit(solution)/shard_map/ppermute | solution.py:271
  111.6 1.1 shard_map.81
  (29 shorter events, 0.3 us)
Async XLA Ops:
  2.5 7.3 %copy-start.6 = (bf16[24,128]{1,0:T(8,128)(2,1)S(1)}, bf16[24,128]{1,0:T(8,128)(2,1)}, u32[]{:S(2)}) copy-start(bf16[24,128]{1,0:T(8,128)(2,1)} %get-tuple-element.11) | copy-start | bytes 18436
  4.4 18.1 %all-to-all-start.1 = ((bf16[8,32,1536]{2,1,0:T(8,128)(2,1)}), bf16[8,32,1536]{2,1,0:T(8,128)(2,1)S(1)}, u32[]{:S(2)}, u32[]{:S(2)}) async-start(bf16[8,32,1536]{2,1,0:T(8,128)(2,1)} %broadcast_in_dim.7), calls=%async_computation.1 | async-start | bytes 1572864 | tf_op jit(solution)/shard_map/all_to_all | solution.py:214
  9.8 33.0 %copy-start = (bf16[1536,768]{1,0:T(8,128)(2,1)S(1)}, bf16[1536,768]{1,0:T(8,128)(2,1)}, u32[]{:S(2)}) copy-start(bf16[1536,768]{1,0:T(8,128)(2,1)} %b_ref.1) | copy-start | bytes 7077892
  9.8 33.0 %copy-start.4 = (bf16[32,1536]{1,0:T(8,128)(2,1)S(1)}, bf16[32,1536]{1,0:T(8,128)(2,1)}, u32[]{:S(2)}) copy-start(bf16[32,1536]{1,0:T(8,128)(2,1)} %get-tuple-element.16.y_ref) | copy-start | bytes 294916
  9.8 10.8 %collective-permute-start = (bf16[24,128]{1,0:T(8,128)(2,1)S(1)}, bf16[24,128]{1,0:T(8,128)(2,1)S(1)}, u32[]{:S(2)}, u32[]{:S(2)}) collective-permute-start(bf16[24,128]{1,0:T(8,128)(2,1)S(1)} %copy-done.6), channel_id=1, source_target_pairs={{0,0},{8,32},{16,64},{24,96},{32,128},{40,160},{48,192},{56,224},{... | collective-permute-start | bytes 18440 | tf_op jit(solution)/shard_map/ppermute | solution.py:216
  22.5 49.8 %all-to-all-start = ((bf16[16,120,128]{2,1,0:T(8,128)(2,1)}), bf16[16,120,128]{2,1,0:T(8,128)(2,1)}, u32[]{:S(2)}, u32[]{:S(2)}) async-start(bf16[16,120,128]{2,1,0:T(8,128)(2,1)} %pad_maximum_fusion.1), calls=%async_computation | async-start | bytes 983040 | tf_op jit(solution)/shard_map/all_to_all | solution.py:233
  43.7 0.8 copy-start.1
  44.4 16.4 %copy-start.2 = (f32[144,768]{1,0:T(8,128)S(1)}, f32[144,768]{1,0:T(8,128)}, u32[]{:S(2)}) copy-start(f32[144,768]{1,0:T(8,128)} %copy-done.1) | copy-start | bytes 1327108
  44.4 3.5 %collective-permute-start.1 = (bf16[144,768]{1,0:T(8,128)(2,1)S(1)}, bf16[144,768]{1,0:T(8,128)(2,1)S(1)}, u32[]{:S(2)}, u32[]{:S(2)}) collective-permute-start(bf16[144,768]{1,0:T(8,128)(2,1)S(1)} %get-tuple-element.15), channel_id=1, source_target_pairs={{0,128},{128,0},{256,384},{384,256},{1,129},{129,1},{257,385},{385... | collective-permute-start | bytes 663560 | tf_op jit(solution)/shard_map/ppermute | solution.py:245
  48.8 23.5 %copy-start.3 = (bf16[128,384]{1,0:T(8,128)(2,1)S(1)}, bf16[128,384]{1,0:T(8,128)(2,1)}, u32[]{:S(2)}) copy-start(bf16[128,384]{1,0:T(8,128)(2,1)} %tokens_ref.1) | copy-start | bytes 294916
  48.8 23.5 %copy-start.5 = (s32[32]{0:T(128)S(1)}, s32[32]{0:T(128)}, u32[]{:S(2)}) copy-start(s32[32]{0:T(128)} %picks.3) | copy-start | bytes 388
  49.9 10.9 %collective-permute-start.2 = (bf16[144,768]{1,0:T(8,128)(2,1)S(1)}, bf16[144,768]{1,0:T(8,128)(2,1)S(1)}, u32[]{:S(2)}, u32[]{:S(2)}) collective-permute-start(bf16[144,768]{1,0:T(8,128)(2,1)S(1)} %pad_maximum_fusion.2), channel_id=1, source_target_pairs={{0,256},{128,384},{256,0},{384,128},{1,257},{129,385},{257,1},{385... | collective-permute-start | bytes 663560 | tf_op jit(solution)/shard_map/ppermute | solution.py:248
  60.9 19.4 %collective-permute-start.5 = (bf16[128,768]{1,0:T(8,128)(2,1)S(1)}, bf16[128,768]{1,0:T(8,128)(2,1)S(1)}, u32[]{:S(2)}, u32[]{:S(2)}) collective-permute-start(bf16[128,768]{1,0:T(8,128)(2,1)S(1)} %fusion.refs_0_), channel_id=1, source_target_pairs={{0,120},{8,0},{16,8},{24,16},{32,24},{40,32},{48,40},{56,48},{64,5... | collective-permute-start | bytes 589832 | tf_op jit(solution)/shard_map/ppermute | solution.py:252
  63.0 17.4 %collective-permute-start.4 = (bf16[128,768]{1,0:T(8,128)(2,1)S(1)}, bf16[128,768]{1,0:T(8,128)(2,1)S(1)}, u32[]{:S(2)}, u32[]{:S(2)}) collective-permute-start(bf16[128,768]{1,0:T(8,128)(2,1)S(1)} %fusion.refs_0_), channel_id=1, source_target_pairs={{0,8},{8,16},{16,24},{24,32},{32,40},{40,48},{48,56},{56,64},{64,7... | collective-permute-start | bytes 589832 | tf_op jit(solution)/shard_map/ppermute | solution.py:252
  66.8 16.2 %collective-permute-start.3 = (bf16[128,768]{1,0:T(8,128)(2,1)S(1)}, bf16[128,768]{1,0:T(8,128)(2,1)S(1)}, u32[]{:S(2)}, u32[]{:S(2)}) collective-permute-start(bf16[128,768]{1,0:T(8,128)(2,1)S(1)} %fusion.refs_0_), channel_id=1, source_target_pairs={{0,16},{8,24},{16,32},{24,40},{32,48},{40,56},{48,64},{56,72},{64,... | collective-permute-start | bytes 589832 | tf_op jit(solution)/shard_map/ppermute | solution.py:252
  74.7 30.3 %all-to-all-start.2 = ((bf16[8,512,128]{2,1,0:T(8,128)(2,1)}), bf16[8,512,128]{2,1,0:T(8,128)(2,1)S(1)}, u32[]{:S(2)}, u32[]{:S(2)}) async-start(bf16[8,512,128]{2,1,0:T(8,128)(2,1)} %shard_map.79), calls=%async_computation.2 | async-start | bytes 2097152 | tf_op jit(solution)/shard_map/all_to_all | solution.py:265
  83.0 21.9 %collective-permute-start.6 = (bf16[512,768]{1,0:T(8,128)(2,1)S(1)}, bf16[512,768]{1,0:T(8,128)(2,1)S(1)}, u32[]{:S(2)}, u32[]{:S(2)}) collective-permute-start(bf16[512,768]{1,0:T(8,128)(2,1)S(1)} %pad_maximum_fusion), channel_id=1, source_target_pairs={{0,128},{128,0},{256,384},{384,256},{1,129},{129,1},{257,385},{385... | collective-permute-start | bytes 2359304 | tf_op jit(solution)/shard_map/ppermute | solution.py:255
  85.0 9.8 %collective-permute-start.7 = (bf16[32,1536]{1,0:T(8,128)(2,1)S(1)}, bf16[32,1536]{1,0:T(8,128)(2,1)S(1)}, u32[]{:S(2)}, u32[]{:S(2)}) collective-permute-start(bf16[32,1536]{1,0:T(8,128)(2,1)S(1)} %copy-done.4), channel_id=1, source_target_pairs={{0,4},{1,5},{2,6},{3,7},{4,0},{5,1},{6,2},{7,3},{8,12},{9,13},{10,... | collective-permute-start | bytes 294920 | tf_op jit(solution)/shard_map/ppermute | solution.py:268
  94.8 11.9 %collective-permute-start.10 = (bf16[64,1536]{1,0:T(8,128)(2,1)S(1)}, bf16[64,1536]{1,0:T(8,128)(2,1)S(1)}, u32[]{:S(2)}, u32[]{:S(2)}) collective-permute-start(bf16[64,1536]{1,0:T(8,128)(2,1)S(1)} %constant_dynamic-update-slice_fusion.refs_0_), channel_id=1, source_target_pairs={{0,3},{1,0},{2,1},{3,2},{4,7},{5,4},{6,5},{7,6},{8,11},{9,8},{10,9... | collective-permute-start | bytes 589832 | tf_op jit(solution)/shard_map/ppermute | solution.py:271
  99.3 10.2 %collective-permute-start.9 = (bf16[64,1536]{1,0:T(8,128)(2,1)S(1)}, bf16[64,1536]{1,0:T(8,128)(2,1)S(1)}, u32[]{:S(2)}, u32[]{:S(2)}) collective-permute-start(bf16[64,1536]{1,0:T(8,128)(2,1)S(1)} %constant_dynamic-update-slice_fusion.refs_0_), channel_id=1, source_target_pairs={{0,2},{1,3},{2,0},{3,1},{4,6},{5,7},{6,4},{7,5},{8,10},{9,11},{10,... | collective-permute-start | bytes 589832 | tf_op jit(solution)/shard_map/ppermute | solution.py:271
  102.1 9.5 %collective-permute-start.8 = (bf16[64,1536]{1,0:T(8,128)(2,1)S(1)}, bf16[64,1536]{1,0:T(8,128)(2,1)S(1)}, u32[]{:S(2)}, u32[]{:S(2)}) collective-permute-start(bf16[64,1536]{1,0:T(8,128)(2,1)S(1)} %constant_dynamic-update-slice_fusion.refs_0_), channel_id=1, source_target_pairs={{0,1},{1,2},{2,3},{3,0},{4,5},{5,6},{6,7},{7,4},{8,9},{9,10},{10,1... | collective-permute-start | bytes 589832 | tf_op jit(solution)/shard_map/ppermute | solution.py:271

commit v14 on v9

--- a/solution.py
+++ b/solution.py
@@ -14,10 +14,10 @@
 LAST = (((1,), (1,)), ((), ()))
 SMEM = pl.BlockSpec(memory_space=pltpu.SMEM)
 VMEM = pl.BlockSpec(memory_space=pltpu.VMEM)
-SHIFTS = (0, 2, 1, -1)
-
-
-def call(kernel, inputs, outs, flops, scratch=(), place=VMEM):
+PLANES = 2
+
+
+def call(kernel, inputs, outs, flops, scratch=(), place=VMEM, limit=16):
     moved = sum(x.size * x.dtype.itemsize for x in list(inputs) + list(outs))
     return pl.pallas_call(
         kernel,
@@ -25,7 +25,7 @@
         in_specs=[SMEM if x.dtype == jnp.int32 else place for x in inputs],
         out_specs=[VMEM] * len(outs),
         scratch_shapes=list(scratch),
-        compiler_params=pltpu.CompilerParams(vmem_limit_bytes=40 * 1024 * 1024),
+        compiler_params=pltpu.CompilerParams(vmem_limit_bytes=limit * 1024 * 1024),
         cost_estimate=pl.CostEstimate(flops=flops, bytes_accessed=moved, transcendentals=0),
     )(*inputs)
 
@@ -82,10 +82,11 @@
 def pick_kernel(picks, g_ref, out_ref):
     tok = g_ref.shape[0]
     samp = picks.shape[0]
-    plane = lax.axis_index("row") % 4
+    plane = lax.axis_index("row") % PLANES
     first = lax.axis_index("col") * tok
     count = out_ref.shape[0] - samp
-    ours = [64 * (i // 16) + 16 * plane + i % 16 for i in range(count)]
+    size = count // 2
+    ours = [tok // 2 * (i // size) + size * plane + i % size for i in range(count)]
     hot = rows_hot(ours + [picks[i] - first for i in range(samp)], tok)
     out_ref[...] = jnp.dot(hot, g_ref[...], preferred_element_type=F32).astype(BF)
 
@@ -151,13 +152,12 @@
     n_col, spread, size, width = held.shape
     n_grp, out_rows, unused = out_ref.shape
     row = lax.axis_index("row")
-    for j, shift in enumerate(SHIFTS):
-        plane = lax.rem(row - shift + spread, spread)
-        block = v_refs[j][...].astype(F32)
+    for j in range(spread):
         for k in range(n_col):
-            held[source_of(k), plane] = block[k * size : (k + 1) * size]
+            span = slice(k * size, (k + 1) * size)
+            held[source_of(k), lax.rem(row + j, spread)] = v_refs[j][span, :]
     tokens = n_col * spread * size
-    right = held[...].reshape(tokens, width).astype(BF)
+    right = held[...].reshape(tokens, width)
     for g in range(n_grp):
         left = got_ref[g, :, : spread * size, :].reshape(tokens, LANES)
         term = lax.dot_general(left, right, FIRST, preferred_element_type=F32)
@@ -207,7 +207,7 @@
     tile = feat_row // n_col
     out_rows = feat_grp // n_row
     strip = quarter * feat_row // LANES
-    spread = 4
+    spread = PLANES
     size = tok // 2 // spread
     shape = jax.ShapeDtypeStruct
 
@@ -222,6 +222,7 @@
             pltpu.SemaphoreType.DMA((5,)),
         ],
         pl.BlockSpec(memory_space=pl.ANY),
+        limit=56,
     )[0]
     first = lax.all_to_all(payload, "row", 0, 0)
 
@@ -247,16 +248,11 @@
         4 * n_col * size * feat_grp * width,
         [pltpu.VMEM((n_col, 2, size, width), F32)],
     )
-    first, unused = lax.optimization_barrier((first, give))
+    first, unused = lax.optimization_barrier((first, (pairs[1], pairs[3])))
     taken = lax.ppermute(give, "grp", [(i, i ^ 1) for i in range(n_grp)])
     right = (keep.astype(F32) + taken.astype(F32)).astype(BF)
-    rights = [right] + [
-        lax.ppermute(right, "row", [(i, (i + j) % n_row) for i in range(n_row)])
-        for j in SHIFTS[1:]
-    ]
-    unused, picked_y, beside_y = lax.optimization_barrier(
-        (rights[2], picked[cut:], beside[cut:])
-    )
+    rights = [right, lax.ppermute(right, "row", [(i, i ^ 1) for i in range(n_row)])]
+    unused, picked_y, beside_y = lax.optimization_barrier((taken, picked[cut:], beside[cut:]))
     samples = jnp.concatenate([picked_y, beside_y], axis=0)
     samples = [samples] + [along_y(samples, k) for k in range(1, 4)]
     side = call(
@@ -274,12 +270,13 @@
     got = lax.all_to_all(send.reshape((n_grp * n_col,) + send.shape[2:]), ("grp", "col"), 0, 0)
     got = got.reshape(send.shape)
 
+    rights, samples = lax.optimization_barrier((rights, samples))
     term = call(
         final_kernel,
         (got, *rights),
         [shape((n_grp, out_rows, width), BF)],
         2 * n_grp * LANES * n_col * spread * size * width,
-        [pltpu.VMEM((n_col, spread, size, width), F32)],
+        [pltpu.VMEM((n_col, spread, size, width), BF)],
     )[0]
     got, unused = lax.optimization_barrier((got, term))
     term = lax.all_to_all(term, "grp", 0, 0)

time: 110 us -> 113 us (1.027)
  waiting for transfers between devices: 24.4 us -> 41 us
  starting transfers between devices: 68.6 us -> 56.4 us
  local copies, waits for them, and re-layouts: 4.19 us -> 1.75 us
  Pallas kernels: 9.81 us -> 11.2 us
    ppermute x6, waiting for transfers between devices: 9.11 us -> 25.9 us  [along_y(): lax.ppermute(block, 'col', [(i, i - i % 4 + (i + k) % 4) for i in range(n...]
    ppermute x3 -> x1, waiting for transfers between devices: 10.5 us -> 0.01 us  [body(): lax.ppermute(right, 'row', [(i, i ^ 1) for i in range(n_row)])]
    all_to_all x1, waiting for transfers between devices: 0.01 us -> 8.76 us  [body(): term = lax.all_to_all(term, 'grp', 0, 0)]
    ppermute x3 -> x1, starting transfers between devices: 9.34 us -> 2.98 us  [body(): lax.ppermute(right, 'row', [(i, i ^ 1) for i in range(n_row)])]
    all_to_all x1, starting transfers between devices: 11.5 us -> 6.6 us  [body(): lax.all_to_all(send.reshape((n_grp * n_col,) + send.shape[2:]), ('grp', '...]
    ppermute x1, waiting for transfers between devices: 3.57 us -> 6.31 us  [body(): lax.ppermute(picked, 'col', [(i, (i + 4) % n_col) for i in range(n_col)])]
    unnamed x21 -> x11, local copies, waits for them, and re-layouts: 3.52 us -> 1.69 us
    ppermute x1, starting transfers between devices: 2.14 us -> 3.67 us  [body(): taken = lax.ppermute(give, 'grp', [(i, i ^ 1) for i in range(n_grp)])]
  transfers between devices with their start and end apart: 14 -> 12, of which waited for: 8 -> 7; matrix products, arithmetic and copies ran while one was open for 1% -> 0% of each run, Pallas kernels for 4% -> 5%
where the time goes in v14:
time: 113 us; the launch traced here: 112 us
  starting transfers between devices  56.4 us (50%)
  waiting for transfers between devices  41 us (36%)
  Pallas kernels  11.2 us (10%)
  local copies, waits for them, and re-layouts  1.75 us (2%)
    ppermute x6, waiting for transfers between devices, along_y(): lax.ppermute(block, 'col', [(i, i - i % 4 + (i + k) % 4) for i in range(n...  25.9 us
    ppermute x6, starting transfers between devices, along_y(): lax.ppermute(block, 'col', [(i, i - i % 4 + (i + k) % 4) for i in range(n...  19.7 us
    all_to_all x1, starting transfers between devices, body(): first = lax.all_to_all(payload, 'row', 0, 0)  15.8 us
    pallas_call x7, Pallas kernels, call(): pl.pallas_call(kernel, out_shape=outs, in_specs=[SMEM if x.dtype == jnp.i...  11.2 us
    all_to_all x1, waiting for transfers between devices, body(): term = lax.all_to_all(term, 'grp', 0, 0)  8.76 us
    all_to_all x1, starting transfers between devices, body(): lax.all_to_all(send.reshape((n_grp * n_col,) + send.shape[2:]), ('grp', '...  6.6 us
    ppermute x1, waiting for transfers between devices, body(): lax.ppermute(picked, 'col', [(i, (i + 4) % n_col) for i in range(n_col)])  6.31 us
    all_to_all x1, starting transfers between devices, body(): term = lax.all_to_all(term, 'grp', 0, 0)  4.55 us
  transfers between devices with their start and end apart: 12, of which 7 were waited for; matrix products, arithmetic and copies ran while one was open for 0% of the time, Pallas kernels for 5%

profile of v14, /device:TPU:1, one launch (start us, length us, event | category | flops | bytes accessed | tf_op | source)
XLA Modules:
  0.0 112.1 jit_solution(11010328854457037088)
XLA Ops:
  0.7 3.7 %shard_map.76 = bf16[16,120,128]{2,1,0:T(8,128)(2,1)} custom-call(s32[32]{0:T(128)} %picks.5, bf16[128,384]{1,0:T(8,128)(2,1)} %x_ref.1, bf16[1536,384]{1,0:T(8,128)(2,1)} %a_hbm.1), custom_call_target="tpu_custom_call" | custom-call | flops 150994944 | bytes 1769600 | tf_op jit(solution)/shard_map/pallas_call | solution.py:22
  4.4 15.8 %all-to-all-start = ((bf16[16,120,128]{2,1,0:T(8,128)(2,1)}), bf16[16,120,128]{2,1,0:T(8,128)(2,1)S(1)}, u32[]{:S(2)}, u32[]{:S(2)}) async-start(bf16[16,120,128]{2,1,0:T(8,128)(2,1)} %shard_map.76), calls=%async_computation | async-start | bytes 983040 | tf_op jit(solution)/shard_map/all_to_all | solution.py:227
  20.2 0.8 shard_map.77.gy_ref
  20.9 3.1 %collective-permute-start = (bf16[96,1536]{1,0:T(8,128)(2,1)S(1)}, bf16[96,1536]{1,0:T(8,128)(2,1)S(1)}, u32[]{:S(2)}, u32[]{:S(2)}) collective-permute-start(bf16[96,1536]{1,0:T(8,128)(2,1)S(1)} %shard_map.77.gy_ref), channel_id=1, source_target_pairs={{0,4},{1,5},{2,6},{3,7},{4,0},{5,1},{6,2},{7,3},{8,12},{9,13},{10,... | collective-permute-start | bytes 884744 | tf_op jit(solution)/shard_map/ppermute | solution.py:240
  24.1 6.3 %collective-permute-done = bf16[96,1536]{1,0:T(8,128)(2,1)S(1)} collective-permute-done((bf16[96,1536]{1,0:T(8,128)(2,1)S(1)}, bf16[96,1536]{1,0:T(8,128)(2,1)S(1)}, u32[]{:S(2)}, u32[]{:S(2)}) %collective-permute-start) | collective-permute-done | bytes 294944 | tf_op jit(solution)/shard_map/ppermute | solution.py:240
  30.5 0.0 copy-start.1
  30.5 4.9 %collective-permute-start.3 = (bf16[128,1536]{1,0:T(8,128)(2,1)S(1)}, bf16[128,1536]{1,0:T(8,128)(2,1)S(1)}, u32[]{:S(2)}, u32[]{:S(2)}) collective-permute-start(bf16[128,1536]{1,0:T(8,128)(2,1)S(1)} %pad_maximum_fusion.refs_0_), channel_id=1, source_target_pairs={{0,2},{1,3},{2,0},{3,1},{4,6},{5,7},{6,4},{7,5},{8,10},{9,11},{10,... | collective-permute-start | bytes 1179656 | tf_op jit(solution)/shard_map/ppermute | solution.py:230
  35.4 2.7 %collective-permute-start.2 = (bf16[128,1536]{1,0:T(8,128)(2,1)S(1)}, bf16[128,1536]{1,0:T(8,128)(2,1)S(1)}, u32[]{:S(2)}, u32[]{:S(2)}) collective-permute-start(bf16[128,1536]{1,0:T(8,128)(2,1)S(1)} %pad_maximum_fusion.refs_0_), channel_id=1, source_target_pairs={{0,3},{1,0},{2,1},{3,2},{4,7},{5,4},{6,5},{7,6},{8,11},{9,8},{10,9... | collective-permute-start | bytes 1179656 | tf_op jit(solution)/shard_map/ppermute | solution.py:230
  38.1 2.6 %collective-permute-start.1 = (bf16[128,1536]{1,0:T(8,128)(2,1)S(1)}, bf16[128,1536]{1,0:T(8,128)(2,1)S(1)}, u32[]{:S(2)}, u32[]{:S(2)}) collective-permute-start(bf16[128,1536]{1,0:T(8,128)(2,1)S(1)} %pad_maximum_fusion.refs_0_), channel_id=1, source_target_pairs={{0,1},{1,2},{2,3},{3,0},{4,5},{5,6},{6,7},{7,4},{8,9},{9,10},{10,1... | collective-permute-start | bytes 1179656 | tf_op jit(solution)/shard_map/ppermute | solution.py:230
  40.7 2.0 %collective-permute-done.3.refs_2_ = bf16[128,1536]{1,0:T(8,128)(2,1)S(1)} collective-permute-done((bf16[128,1536]{1,0:T(8,128)(2,1)S(1)}, bf16[128,1536]{1,0:T(8,128)(2,1)S(1)}, u32[]{:S(2)}, u32[]{:S(2)}) %collective-permute-start.3) | collective-permute-done | bytes 393248 | tf_op jit(solution)/shard_map/ppermute | solution.py:230
  42.7 10.0 %collective-permute-done.2.refs_3_ = bf16[128,1536]{1,0:T(8,128)(2,1)S(1)} collective-permute-done((bf16[128,1536]{1,0:T(8,128)(2,1)S(1)}, bf16[128,1536]{1,0:T(8,128)(2,1)S(1)}, u32[]{:S(2)}, u32[]{:S(2)}) %collective-permute-start.2) | collective-permute-done | bytes 393248 | tf_op jit(solution)/shard_map/ppermute | solution.py:230
  52.8 0.0 collective-permute-done.1.refs_1_
  52.8 1.7 %copy-done.3 = bf16[1536,768]{1,0:T(8,128)(2,1)S(1)} copy-done((bf16[1536,768]{1,0:T(8,128)(2,1)S(1)}, bf16[1536,768]{1,0:T(8,128)(2,1)}, u32[]{:S(2)}) %copy-start.3) | copy-done | bytes 2359320
  54.4 1.6 %shard_map.80 = (bf16[256,768]{1,0:T(8,128)(2,1)S(1)}, bf16[256,768]{1,0:T(8,128)(2,1)S(1)}) custom-call(bf16[1536,768]{1,0:T(8,128)(2,1)S(1)} %copy-done.3, bf16[128,1536]{1,0:T(8,128)(2,1)S(1)} %pad_maximum_fusion.refs_0_, bf16[128,1536]{1,0:T(8,128)(2,1)S(1)} %collective-permute-done.1.refs_1_, bf16[128,1536]{1,0:T(8,128)(2,1)S(1)} %collective-permute-done.3.refs_2_, ...), custom_call_target="tpu_custom_call" | custom-call | flops 1207959552 | bytes 4718592 | tf_op jit(solution)/shard_map/pallas_call | solution.py:22
  56.0 3.7 %collective-permute-start.4 = (bf16[256,768]{1,0:T(8,128)(2,1)S(1)}, bf16[256,768]{1,0:T(8,128)(2,1)S(1)}, u32[]{:S(2)}, u32[]{:S(2)}) collective-permute-start(bf16[256,768]{1,0:T(8,128)(2,1)S(1)} %get-tuple-element.19), channel_id=1, source_target_pairs={{0,128},{128,0},{256,384},{384,256},{1,129},{129,1},{257,385},{385... | collective-permute-start | bytes 1179656 | tf_op jit(solution)/shard_map/ppermute | solution.py:252
  59.7 1.0 shard_map.78.side_ref
  60.7 1.3 %shard_map.79 = bf16[4,8,160,128]{3,2,1,0:T(8,128)(2,1)} custom-call(bf16[16,120,128]{2,1,0:T(8,128)(2,1)S(1)} %all-to-all-done.got_ref, bf16[8,64,128]{2,1,0:T(8,128)(2,1)S(1)} %shard_map.78.side_ref), custom_call_target="tpu_custom_call" | custom-call | flops 1000000 | bytes 1933312 | tf_op jit(solution)/shard_map/pallas_call | solution.py:22
  62.0 6.6 %all-to-all-start.1 = ((bf16[32,160,128]{2,1,0:T(8,128)(2,1)}), bf16[32,160,128]{2,1,0:T(8,128)(2,1)S(1)}, u32[]{:S(2)}, u32[]{:S(2)}) async-start(bf16[32,160,128]{2,1,0:T(8,128)(2,1)} %bitcast), calls=%async_computation.1 | async-start | bytes 2621440 | tf_op jit(solution)/shard_map/all_to_all | solution.py:270
  68.6 0.0 slice-start
  68.7 0.1 add_convert_fusion.refs_0_
  68.8 3.0 %collective-permute-start.5 = (bf16[256,768]{1,0:T(8,128)(2,1)S(1)}, bf16[256,768]{1,0:T(8,128)(2,1)S(1)}, u32[]{:S(2)}, u32[]{:S(2)}) collective-permute-start(bf16[256,768]{1,0:T(8,128)(2,1)S(1)} %add_convert_fusion.refs_0_), channel_id=1, source_target_pairs={{0,8},{8,0},{16,24},{24,16},{32,40},{40,32},{48,56},{56,48},{64,72... | collective-permute-start | bytes 1179656 | tf_op jit(solution)/shard_map/ppermute | solution.py:254
  71.8 4.5 %collective-permute-start.8 = (bf16[64,1536]{1,0:T(8,128)(2,1)S(1)}, bf16[64,1536]{1,0:T(8,128)(2,1)S(1)}, u32[]{:S(2)}, u32[]{:S(2)}) collective-permute-start(bf16[64,1536]{1,0:T(8,128)(2,1)S(1)} %constant_dynamic-update-slice_fusion.refs_0_), channel_id=1, source_target_pairs={{0,3},{1,0},{2,1},{3,2},{4,7},{5,4},{6,5},{7,6},{8,11},{9,8},{10,9... | collective-permute-start | bytes 589832 | tf_op jit(solution)/shard_map/ppermute | solution.py:230
  76.3 2.5 %collective-permute-start.7 = (bf16[64,1536]{1,0:T(8,128)(2,1)S(1)}, bf16[64,1536]{1,0:T(8,128)(2,1)S(1)}, u32[]{:S(2)}, u32[]{:S(2)}) collective-permute-start(bf16[64,1536]{1,0:T(8,128)(2,1)S(1)} %constant_dynamic-update-slice_fusion.refs_0_), channel_id=1, source_target_pairs={{0,2},{1,3},{2,0},{3,1},{4,6},{5,7},{6,4},{7,5},{8,10},{9,11},{10,... | collective-permute-start | bytes 589832 | tf_op jit(solution)/shard_map/ppermute | solution.py:230
  78.8 2.5 %collective-permute-start.6 = (bf16[64,1536]{1,0:T(8,128)(2,1)S(1)}, bf16[64,1536]{1,0:T(8,128)(2,1)S(1)}, u32[]{:S(2)}, u32[]{:S(2)}) collective-permute-start(bf16[64,1536]{1,0:T(8,128)(2,1)S(1)} %constant_dynamic-update-slice_fusion.refs_0_), channel_id=1, source_target_pairs={{0,1},{1,2},{2,3},{3,0},{4,5},{5,6},{6,7},{7,4},{8,9},{9,10},{10,1... | collective-permute-start | bytes 589832 | tf_op jit(solution)/shard_map/ppermute | solution.py:230
  81.3 8.1 %collective-permute-done.8.refs_3_ = bf16[64,1536]{1,0:T(8,128)(2,1)S(1)} collective-permute-done((bf16[64,1536]{1,0:T(8,128)(2,1)S(1)}, bf16[64,1536]{1,0:T(8,128)(2,1)S(1)}, u32[]{:S(2)}, u32[]{:S(2)}) %collective-permute-start.8) | collective-permute-done | bytes 196640 | tf_op jit(solution)/shard_map/ppermute | solution.py:230
  89.4 2.1 %collective-permute-done.7.refs_2_ = bf16[64,1536]{1,0:T(8,128)(2,1)S(1)} collective-permute-done((bf16[64,1536]{1,0:T(8,128)(2,1)S(1)}, bf16[64,1536]{1,0:T(8,128)(2,1)S(1)}, u32[]{:S(2)}, u32[]{:S(2)}) %collective-permute-start.7) | collective-permute-done | bytes 196640 | tf_op jit(solution)/shard_map/ppermute | solution.py:230
  91.5 3.6 %collective-permute-done.6.refs_1_ = bf16[64,1536]{1,0:T(8,128)(2,1)S(1)} collective-permute-done((bf16[64,1536]{1,0:T(8,128)(2,1)S(1)}, bf16[64,1536]{1,0:T(8,128)(2,1)S(1)}, u32[]{:S(2)}, u32[]{:S(2)}) %collective-permute-start.6) | collective-permute-done | bytes 196640 | tf_op jit(solution)/shard_map/ppermute | solution.py:230
  95.1 1.5 %shard_map.81 = bf16[4,96,768]{2,1,0:T(8,128)(2,1)} custom-call(bf16[4,8,160,128]{3,2,1,0:T(8,128)(2,1)S(1)} %bitcast.2, bf16[256,768]{1,0:T(8,128)(2,1)S(1)} %add_convert_fusion.refs_0_, bf16[256,768]{1,0:T(8,128)(2,1)S(1)} %collective-permute-done.5.refs_1_), custom_call_target="tpu_custom_call" | custom-call | flops 402653184 | bytes 2686976 | tf_op jit(solution)/shard_map/pallas_call | solution.py:22
  96.6 4.6 %all-to-all-start.2 = ((bf16[4,96,768]{2,1,0:T(8,128)(2,1)}), bf16[4,96,768]{2,1,0:T(8,128)(2,1)S(1)}, u32[]{:S(2)}, u32[]{:S(2)}) async-start(bf16[4,96,768]{2,1,0:T(8,128)(2,1)} %shard_map.81), calls=%async_computation.2 | async-start | bytes 1179648 | tf_op jit(solution)/shard_map/all_to_all | solution.py:282
  101.2 1.4 %shard_map.82 = (f32[48,1536]{1,0:T(8,128)}, f32[48,1536]{1,0:T(8,128)}) custom-call(bf16[4,8,160,128]{3,2,1,0:T(8,128)(2,1)S(1)} %bitcast.3, bf16[64,1536]{1,0:T(8,128)(2,1)S(1)} %constant_dynamic-update-slice_fusion.refs_0_, bf16[64,1536]{1,0:T(8,128)(2,1)S(1)} %collective-permute-done.6.refs_1_, bf16[64,1536]{1,0:T(8,128)(2,1)S(1)} %collective-permute-done.7.refs_2_, ...), custom_call_target="tpu_custom_call" | custom-call | flops 201326592 | bytes 2686976 | tf_op jit(solution)/shard_map/pallas_call | solution.py:22
  102.6 8.8 %all-to-all-done.2 = bf16[4,96,768]{2,1,0:T(8,128)(2,1)S(1)} async-done(((bf16[4,96,768]{2,1,0:T(8,128)(2,1)}), bf16[4,96,768]{2,1,0:T(8,128)(2,1)S(1)}, u32[]{:S(2)}, u32[]{:S(2)}) %all-to-all-start.2) | async-done | bytes 589856 | tf_op jit(solution)/shard_map/all_to_all | solution.py:282
  111.3 0.8 convert_reduce_fusion
  (19 shorter events, 0.1 us)
Async XLA Ops:
  0.6 19.5 %copy-start.2 = (s32[32]{0:T(128)S(1)}, s32[32]{0:T(128)}, u32[]{:S(2)}) copy-start(s32[32]{0:T(128)} %picks.5) | copy-start | bytes 388
  0.6 19.5 %copy-start = (bf16[128,1536]{1,0:T(8,128)(2,1)S(1)}, bf16[128,1536]{1,0:T(8,128)(2,1)}, u32[]{:S(2)}) copy-start(bf16[128,1536]{1,0:T(8,128)(2,1)} %g_ref.1) | copy-start | bytes 1179652
  4.4 56.3 %all-to-all-start = ((bf16[16,120,128]{2,1,0:T(8,128)(2,1)}), bf16[16,120,128]{2,1,0:T(8,128)(2,1)S(1)}, u32[]{:S(2)}, u32[]{:S(2)}) async-start(bf16[16,120,128]{2,1,0:T(8,128)(2,1)} %shard_map.76), calls=%async_computation | async-start | bytes 983040 | tf_op jit(solution)/shard_map/all_to_all | solution.py:227
  20.9 9.5 %collective-permute-start = (bf16[96,1536]{1,0:T(8,128)(2,1)S(1)}, bf16[96,1536]{1,0:T(8,128)(2,1)S(1)}, u32[]{:S(2)}, u32[]{:S(2)}) collective-permute-start(bf16[96,1536]{1,0:T(8,128)(2,1)S(1)} %shard_map.77.gy_ref), channel_id=1, source_target_pairs={{0,4},{1,5},{2,6},{3,7},{4,0},{5,1},{6,2},{7,3},{8,12},{9,13},{10,... | collective-permute-start | bytes 884744 | tf_op jit(solution)/shard_map/ppermute | solution.py:240
  30.4 38.2 %copy-start.4 = (bf16[96,1536]{1,0:T(8,128)(2,1)}, bf16[96,1536]{1,0:T(8,128)(2,1)S(1)}, u32[]{:S(2)}) copy-start(bf16[96,1536]{1,0:T(8,128)(2,1)S(1)} %collective-permute-done) | copy-start | bytes 884740
  30.5 29.3 %copy-start.1 = (bf16[128,384]{1,0:T(8,128)(2,1)S(1)}, bf16[128,384]{1,0:T(8,128)(2,1)}, u32[]{:S(2)}) copy-start(bf16[128,384]{1,0:T(8,128)(2,1)} %x_ref.1) | copy-start | bytes 294916
  30.5 12.3 %collective-permute-start.3 = (bf16[128,1536]{1,0:T(8,128)(2,1)S(1)}, bf16[128,1536]{1,0:T(8,128)(2,1)S(1)}, u32[]{:S(2)}, u32[]{:S(2)}) collective-permute-start(bf16[128,1536]{1,0:T(8,128)(2,1)S(1)} %pad_maximum_fusion.refs_0_), channel_id=1, source_target_pairs={{0,2},{1,3},{2,0},{3,1},{4,6},{5,7},{6,4},{7,5},{8,10},{9,11},{10,... | collective-permute-start | bytes 1179656 | tf_op jit(solution)/shard_map/ppermute | solution.py:230
  35.4 17.4 %collective-permute-start.2 = (bf16[128,1536]{1,0:T(8,128)(2,1)S(1)}, bf16[128,1536]{1,0:T(8,128)(2,1)S(1)}, u32[]{:S(2)}, u32[]{:S(2)}) collective-permute-start(bf16[128,1536]{1,0:T(8,128)(2,1)S(1)} %pad_maximum_fusion.refs_0_), channel_id=1, source_target_pairs={{0,3},{1,0},{2,1},{3,2},{4,7},{5,4},{6,5},{7,6},{8,11},{9,8},{10,9... | collective-permute-start | bytes 1179656 | tf_op jit(solution)/shard_map/ppermute | solution.py:230
  38.1 14.7 %collective-permute-start.1 = (bf16[128,1536]{1,0:T(8,128)(2,1)S(1)}, bf16[128,1536]{1,0:T(8,128)(2,1)S(1)}, u32[]{:S(2)}, u32[]{:S(2)}) collective-permute-start(bf16[128,1536]{1,0:T(8,128)(2,1)S(1)} %pad_maximum_fusion.refs_0_), channel_id=1, source_target_pairs={{0,1},{1,2},{2,3},{3,0},{4,5},{5,6},{6,7},{7,4},{8,9},{9,10},{10,1... | collective-permute-start | bytes 1179656 | tf_op jit(solution)/shard_map/ppermute | solution.py:230
  52.8 1.7 %copy-start.3 = (bf16[1536,768]{1,0:T(8,128)(2,1)S(1)}, bf16[1536,768]{1,0:T(8,128)(2,1)}, u32[]{:S(2)}) copy-start(bf16[1536,768]{1,0:T(8,128)(2,1)} %b_ref.1) | copy-start | bytes 7077892
  56.0 12.6 %collective-permute-start.4 = (bf16[256,768]{1,0:T(8,128)(2,1)S(1)}, bf16[256,768]{1,0:T(8,128)(2,1)S(1)}, u32[]{:S(2)}, u32[]{:S(2)}) collective-permute-start(bf16[256,768]{1,0:T(8,128)(2,1)S(1)} %get-tuple-element.19), channel_id=1, source_target_pairs={{0,128},{128,0},{256,384},{384,256},{1,129},{129,1},{257,385},{385... | collective-permute-start | bytes 1179656 | tf_op jit(solution)/shard_map/ppermute | solution.py:252
  62.0 33.1 %all-to-all-start.1 = ((bf16[32,160,128]{2,1,0:T(8,128)(2,1)}), bf16[32,160,128]{2,1,0:T(8,128)(2,1)S(1)}, u32[]{:S(2)}, u32[]{:S(2)}) async-start(bf16[32,160,128]{2,1,0:T(8,128)(2,1)} %bitcast), calls=%async_computation.1 | async-start | bytes 2621440 | tf_op jit(solution)/shard_map/all_to_all | solution.py:270
  68.6 3.1 %slice-start = ((bf16[96,1536]{1,0:T(8,128)(2,1)}), bf16[32,1536]{1,0:T(8,128)(2,1)S(1)}, s32[]{:S(2)}) async-start(bf16[96,1536]{1,0:T(8,128)(2,1)} %copy-done.4), calls=%async_computation.3 | async-start | bytes 196608 | tf_op jit(solution)/shard_map/slice | solution.py:255
  68.8 26.4 %collective-permute-start.5 = (bf16[256,768]{1,0:T(8,128)(2,1)S(1)}, bf16[256,768]{1,0:T(8,128)(2,1)S(1)}, u32[]{:S(2)}, u32[]{:S(2)}) collective-permute-start(bf16[256,768]{1,0:T(8,128)(2,1)S(1)} %add_convert_fusion.refs_0_), channel_id=1, source_target_pairs={{0,8},{8,0},{16,24},{24,16},{32,40},{40,32},{48,56},{56,48},{64,72... | collective-permute-start | bytes 1179656 | tf_op jit(solution)/shard_map/ppermute | solution.py:254
  71.8 17.6 %collective-permute-start.8 = (bf16[64,1536]{1,0:T(8,128)(2,1)S(1)}, bf16[64,1536]{1,0:T(8,128)(2,1)S(1)}, u32[]{:S(2)}, u32[]{:S(2)}) collective-permute-start(bf16[64,1536]{1,0:T(8,128)(2,1)S(1)} %constant_dynamic-update-slice_fusion.refs_0_), channel_id=1, source_target_pairs={{0,3},{1,0},{2,1},{3,2},{4,7},{5,4},{6,5},{7,6},{8,11},{9,8},{10,9... | collective-permute-start | bytes 589832 | tf_op jit(solution)/shard_map/ppermute | solution.py:230
  76.3 15.2 %collective-permute-start.7 = (bf16[64,1536]{1,0:T(8,128)(2,1)S(1)}, bf16[64,1536]{1,0:T(8,128)(2,1)S(1)}, u32[]{:S(2)}, u32[]{:S(2)}) collective-permute-start(bf16[64,1536]{1,0:T(8,128)(2,1)S(1)} %constant_dynamic-update-slice_fusion.refs_0_), channel_id=1, source_target_pairs={{0,2},{1,3},{2,0},{3,1},{4,6},{5,7},{6,4},{7,5},{8,10},{9,11},{10,... | collective-permute-start | bytes 589832 | tf_op jit(solution)/shard_map/ppermute | solution.py:230
  78.8 16.3 %collective-permute-start.6 = (bf16[64,1536]{1,0:T(8,128)(2,1)S(1)}, bf16[64,1536]{1,0:T(8,128)(2,1)S(1)}, u32[]{:S(2)}, u32[]{:S(2)}) collective-permute-start(bf16[64,1536]{1,0:T(8,128)(2,1)S(1)} %constant_dynamic-update-slice_fusion.refs_0_), channel_id=1, source_target_pairs={{0,1},{1,2},{2,3},{3,0},{4,5},{5,6},{6,7},{7,4},{8,9},{9,10},{10,1... | collective-permute-start | bytes 589832 | tf_op jit(solution)/shard_map/ppermute | solution.py:230
  96.6 14.7 %all-to-all-start.2 = ((bf16[4,96,768]{2,1,0:T(8,128)(2,1)}), bf16[4,96,768]{2,1,0:T(8,128)(2,1)S(1)}, u32[]{:S(2)}, u32[]{:S(2)}) async-start(bf16[4,96,768]{2,1,0:T(8,128)(2,1)} %shard_map.81), calls=%async_computation.2 | async-start | bytes 1179648 | tf_op jit(solution)/shard_map/all_to_all | solution.py:282

commit v15 on v14

--- a/solution.py
+++ b/solution.py
@@ -14,15 +14,17 @@
 LAST = (((1,), (1,)), ((), ()))
 SMEM = pl.BlockSpec(memory_space=pltpu.SMEM)
 VMEM = pl.BlockSpec(memory_space=pltpu.VMEM)
-PLANES = 2
-
-
-def call(kernel, inputs, outs, flops, scratch=(), place=VMEM, limit=16):
+PLANES = 4
+SHIFTS = (0, 2, 1, -1)
+
+
+def call(kernel, inputs, outs, flops, scratch=(), places=None, limit=16):
+    places = places or [SMEM if x.dtype == jnp.int32 else VMEM for x in inputs]
     moved = sum(x.size * x.dtype.itemsize for x in list(inputs) + list(outs))
     return pl.pallas_call(
         kernel,
         out_shape=outs,
-        in_specs=[SMEM if x.dtype == jnp.int32 else place for x in inputs],
+        in_specs=places,
         out_specs=[VMEM] * len(outs),
         scratch_shapes=list(scratch),
         compiler_params=pltpu.CompilerParams(vmem_limit_bytes=limit * 1024 * 1024),
@@ -114,11 +116,32 @@
         out_ref[c] = block.astype(BF)
 
 
-def right_kernel(b_ref, *refs):
-    blocks, keep_ref, give_ref, held = refs[:-3], refs[-3], refs[-2], refs[-1]
+def rows_of(block, begin, count):
+    step = block.shape[0] // 2
+    begin = begin if step > count else 0
+    return [block[at : at + count, :] for at in (begin, step + begin)]
+
+
+def right_kernel(b_hbm, *refs):
+    blocks, keep_ref, give_ref, held, b_ref, sems = refs[:-5], *refs[-5:]
     n_blk, unused, size, width = held.shape
-    rows = jnp.concatenate([block[...] for block in blocks], axis=0)
-    term = jnp.dot(rows, b_ref[...], preferred_element_type=F32)
+    parts = sems.shape[0]
+    step = b_ref.shape[0] // parts
+    spans = [pl.ds(p * step, step) for p in range(parts)]
+    copies = [
+        pltpu.make_async_copy(b_hbm.at[span], b_ref.at[span], sems.at[p])
+        for p, span in enumerate(spans)
+    ]
+    for copy in copies:
+        copy.start()
+    rows = [piece for block in blocks for piece in rows_of(block, 0, 2 * size)]
+    rows = jnp.concatenate(rows, axis=0)
+    term = None
+    for p in range(parts):
+        copies[p].wait()
+        left = rows[:, p * step : (p + 1) * step]
+        part = jnp.dot(left, b_ref[spans[p], :], preferred_element_type=F32)
+        term = part if term is None else term + part
     held[...] = term.reshape(held.shape)
     core = lax.axis_index("grp") % 2
     keep_ref[...] = held[:, core].reshape(n_blk * size, width).astype(BF)
@@ -152,10 +175,10 @@
     n_col, spread, size, width = held.shape
     n_grp, out_rows, unused = out_ref.shape
     row = lax.axis_index("row")
-    for j in range(spread):
+    for j, shift in enumerate(SHIFTS):
+        plane = lax.rem(row - shift + spread, spread)
         for k in range(n_col):
-            span = slice(k * size, (k + 1) * size)
-            held[source_of(k), lax.rem(row + j, spread)] = v_refs[j][span, :]
+            held[source_of(k), plane] = v_refs[j][k * size : (k + 1) * size, :]
     tokens = n_col * spread * size
     right = held[...].reshape(tokens, width)
     for g in range(n_grp):
@@ -168,7 +191,7 @@
     blocks, act_ref, grad_ref = refs[:-2], refs[-2], refs[-1]
     n_grp, n_col, depth, unused = got_ref.shape
     tile, width = act_ref.shape
-    samp = blocks[0].shape[0] // 2
+    samp = blocks[0].shape[0] // 4
     quarter = samp // n_grp
     total = samp * n_col
     scale = 1.0 / total
@@ -186,7 +209,8 @@
         act_ref[16 * k : 16 * (k + 1), :] = term[LANES - 16 :] * scale
     owner = lax.axis_index("row") // 4
     sides = [got_ref[owner, source_of(k), : 2 * samp, :] for k in range(n_col)]
-    right = jnp.concatenate([block[...] for block in blocks], axis=0)
+    rights = [piece for block in blocks for piece in rows_of(block, samp, samp)]
+    right = jnp.concatenate(rights, axis=0)
     left = jnp.concatenate([side[:samp] for side in sides], axis=0)
     term = lax.dot_general(left, right, FIRST, preferred_element_type=F32)
     grad_ref[:32, :] = term[LANES - 32 :] * scale
@@ -221,7 +245,7 @@
             pltpu.VMEM(act_inverse.shape, BF),
             pltpu.SemaphoreType.DMA((5,)),
         ],
-        pl.BlockSpec(memory_space=pl.ANY),
+        [SMEM] + [pl.BlockSpec(memory_space=pl.ANY)] * 2,
         limit=56,
     )[0]
     first = lax.all_to_all(payload, "row", 0, 0)
@@ -239,22 +263,29 @@
     )[0]
     beside = lax.ppermute(picked, "col", [(i, (i + 4) % n_col) for i in range(n_col)])
     cut = 2 * size
-    pair = jnp.concatenate([picked[:cut], beside[:cut]], axis=0)
-    pairs = [pair] + [along_y(pair, k) for k in range(1, 4)]
+    pair = jnp.concatenate([picked, beside], axis=0)
+    rows = jnp.concatenate([picked[:cut], beside[:cut]], axis=0)
+    near = {k: along_y(pair, k) for k in (1, 3)}
+    pairs = [pair, near[1], along_y(rows, 2), near[3]]
     keep, give = call(
         right_kernel,
         (grad_inverse, *pairs),
         [shape((n_col * size, width), BF)] * 2,
         4 * n_col * size * feat_grp * width,
-        [pltpu.VMEM((n_col, 2, size, width), F32)],
+        [
+            pltpu.VMEM((n_col, 2, size, width), F32),
+            pltpu.VMEM(grad_inverse.shape, BF),
+            pltpu.SemaphoreType.DMA((4,)),
+        ],
+        places=[pl.BlockSpec(memory_space=pl.ANY)] + [VMEM] * 4,
     )
-    first, unused = lax.optimization_barrier((first, (pairs[1], pairs[3])))
+    first, unused = lax.optimization_barrier((first, give))
     taken = lax.ppermute(give, "grp", [(i, i ^ 1) for i in range(n_grp)])
     right = (keep.astype(F32) + taken.astype(F32)).astype(BF)
-    rights = [right, lax.ppermute(right, "row", [(i, i ^ 1) for i in range(n_row)])]
-    unused, picked_y, beside_y = lax.optimization_barrier((taken, picked[cut:], beside[cut:]))
-    samples = jnp.concatenate([picked_y, beside_y], axis=0)
-    samples = [samples] + [along_y(samples, k) for k in range(1, 4)]
+    rights = [right] + [
+        lax.ppermute(right, "row", [(i, (i + j) % n_row) for i in range(n_row)])
+        for j in SHIFTS[1:]
+    ]
     side = call(
         side_kernel,
         (sample_rows, tokens_in, picked),
@@ -270,7 +301,6 @@
     got = lax.all_to_all(send.reshape((n_grp * n_col,) + send.shape[2:]), ("grp", "col"), 0, 0)
     got = got.reshape(send.shape)
 
-    rights, samples = lax.optimization_barrier((rights, samples))
     term = call(
         final_kernel,
         (got, *rights),
@@ -278,12 +308,13 @@
         2 * n_grp * LANES * n_col * spread * size * width,
         [pltpu.VMEM((n_col, spread, size, width), BF)],
     )[0]
-    got, unused = lax.optimization_barrier((got, term))
+    got, picked, beside, unused = lax.optimization_barrier((got, picked, beside, term))
     term = lax.all_to_all(term, "grp", 0, 0)
+    far = along_y(jnp.concatenate([picked[cut:], beside[cut:]], axis=0), 2)
     precond = jnp.sum(term.astype(F32), axis=0)
     act_cov, grad_cov = call(
         factor_kernel,
-        (got, *samples),
+        (got, pair, near[1], far, near[3]),
         [shape((tile, feat_grp), F32)] * 2,
         4 * LANES * samp * n_col * feat_grp,
     )

time: 113 us -> 101 us (0.89)
  waiting for transfers between devices: 41 us -> 25.5 us
  starting transfers between devices: 56.4 us -> 61.8 us
  local copies, waits for them, and re-layouts: 1.75 us -> 0.05 us
    ppermute x6 -> x4, waiting for transfers between devices: 25.9 us -> 11.5 us  [along_y(): lax.ppermute(block, 'col', [(i, i - i % 4 + (i + k) % 4) for i in range(n...]
    all_to_all x1, waiting for transfers between devices: 8.76 us -> 0.01 us  [body(): term = lax.all_to_all(term, 'grp', 0, 0)]
    ppermute x1 -> x3, waiting for transfers between devices: 0.01 us -> 8.64 us  [body(): lax.ppermute(right, 'row', [(i, (i + j) % n_row) for i in range(n_row)])]
    ppermute x1 -> x3, starting transfers between devices: 2.98 us -> 10.4 us  [body(): lax.ppermute(right, 'row', [(i, (i + j) % n_row) for i in range(n_row)])]
    ppermute x6 -> x4, starting transfers between devices: 19.7 us -> 14.7 us  [along_y(): lax.ppermute(block, 'col', [(i, i - i % 4 + (i + k) % 4) for i in range(n...]
    all_to_all x1, starting transfers between devices: 6.6 us -> 10.4 us  [body(): lax.all_to_all(send.reshape((n_grp * n_col,) + send.shape[2:]), ('grp', '...]
    ppermute x1, waiting for transfers between devices: 6.31 us -> 4.21 us  [body(): lax.ppermute(picked, 'col', [(i, (i + 4) % n_col) for i in range(n_col)])]
    unnamed x11 -> x10, local copies, waits for them, and re-layouts: 1.69 us -> 0.02 us
  transfers between devices with their start and end apart: 12 -> 12, of which waited for: 7 -> 6; matrix products, arithmetic and copies ran while one was open for 0% -> 0% of each run, Pallas kernels for 5% -> 5%
where the time goes in v15:
time: 101 us
  starting transfers between devices  61.8 us (61%)
  waiting for transfers between devices  25.5 us (25%)
  Pallas kernels  11.5 us (11%)
    all_to_all x1, starting transfers between devices, body(): first = lax.all_to_all(payload, 'row', 0, 0)  15.9 us
    ppermute x4, starting transfers between devices, along_y(): lax.ppermute(block, 'col', [(i, i - i % 4 + (i + k) % 4) for i in range(n...  14.7 us
    pallas_call x7, Pallas kernels, call(): pl.pallas_call(kernel, out_shape=outs, in_specs=places, out_specs=[VMEM]...  11.5 us
    ppermute x4, waiting for transfers between devices, along_y(): lax.ppermute(block, 'col', [(i, i - i % 4 + (i + k) % 4) for i in range(n...  11.5 us
    ppermute x3, starting transfers between devices, body(): lax.ppermute(right, 'row', [(i, (i + j) % n_row) for i in range(n_row)])  10.4 us
    all_to_all x1, starting transfers between devices, body(): lax.all_to_all(send.reshape((n_grp * n_col,) + send.shape[2:]), ('grp', '...  10.4 us
    ppermute x3, waiting for transfers between devices, body(): lax.ppermute(right, 'row', [(i, (i + j) % n_row) for i in range(n_row)])  8.64 us
    all_to_all x1, starting transfers between devices, body(): term = lax.all_to_all(term, 'grp', 0, 0)  5.19 us
  transfers between devices with their start and end apart: 12, of which 6 were waited for; matrix products, arithmetic and copies ran while one was open for 0% of the time, Pallas kernels for 5%

profile of v15, /device:TPU:1, one launch (start us, length us, event | category | flops | bytes accessed | tf_op | source)
XLA Modules:
  0.0 100.6 jit_solution(1918290572806573064)
XLA Ops:
  0.7 3.7 %shard_map.76 = bf16[16,120,128]{2,1,0:T(8,128)(2,1)} custom-call(s32[32]{0:T(128)} %picks.5, bf16[128,384]{1,0:T(8,128)(2,1)} %x_ref.1, bf16[1536,384]{1,0:T(8,128)(2,1)} %a_hbm.1), custom_call_target="tpu_custom_call" | custom-call | flops 150994944 | bytes 1769600 | tf_op jit(solution)/shard_map/pallas_call | solution.py:24
  4.4 0.0 copy-start.2
  4.4 15.9 %all-to-all-start = ((bf16[16,120,128]{2,1,0:T(8,128)(2,1)}), bf16[16,120,128]{2,1,0:T(8,128)(2,1)S(1)}, u32[]{:S(2)}, u32[]{:S(2)}) async-start(bf16[16,120,128]{2,1,0:T(8,128)(2,1)} %shard_map.76), calls=%async_computation | async-start | bytes 983040 | tf_op jit(solution)/shard_map/all_to_all | solution.py:251
  20.3 0.0 copy-start
  20.3 0.7 shard_map.77.gy_ref
  21.1 3.1 %collective-permute-start = (bf16[64,1536]{1,0:T(8,128)(2,1)S(1)}, bf16[64,1536]{1,0:T(8,128)(2,1)S(1)}, u32[]{:S(2)}, u32[]{:S(2)}) collective-permute-start(bf16[64,1536]{1,0:T(8,128)(2,1)S(1)} %shard_map.77.gy_ref), channel_id=1, source_target_pairs={{0,4},{1,5},{2,6},{3,7},{4,0},{5,1},{6,2},{7,3},{8,12},{9,13},{10,... | collective-permute-start | bytes 589832 | tf_op jit(solution)/shard_map/ppermute | solution.py:264
  24.2 4.2 %collective-permute-done = bf16[64,1536]{1,0:T(8,128)(2,1)S(1)} collective-permute-done((bf16[64,1536]{1,0:T(8,128)(2,1)S(1)}, bf16[64,1536]{1,0:T(8,128)(2,1)S(1)}, u32[]{:S(2)}, u32[]{:S(2)}) %collective-permute-start) | collective-permute-done | bytes 196640 | tf_op jit(solution)/shard_map/ppermute | solution.py:264
  28.4 3.2 %collective-permute-start.1 = (bf16[128,1536]{1,0:T(8,128)(2,1)S(1)}, bf16[128,1536]{1,0:T(8,128)(2,1)S(1)}, u32[]{:S(2)}, u32[]{:S(2)}) collective-permute-start(bf16[128,1536]{1,0:T(8,128)(2,1)S(1)} %pad_maximum_fusion.refs_0_), channel_id=1, source_target_pairs={{0,1},{1,2},{2,3},{3,0},{4,5},{5,6},{6,7},{7,4},{8,9},{9,10},{10,1... | collective-permute-start | bytes 1179656 | tf_op jit(solution)/shard_map/ppermute | solution.py:254
  31.7 3.4 %collective-permute-start.3 = (bf16[128,1536]{1,0:T(8,128)(2,1)S(1)}, bf16[128,1536]{1,0:T(8,128)(2,1)S(1)}, u32[]{:S(2)}, u32[]{:S(2)}) collective-permute-start(bf16[128,1536]{1,0:T(8,128)(2,1)S(1)} %pad_maximum_fusion.refs_0_), channel_id=1, source_target_pairs={{0,3},{1,0},{2,1},{3,2},{4,7},{5,4},{6,5},{7,6},{8,11},{9,8},{10,9... | collective-permute-start | bytes 1179656 | tf_op jit(solution)/shard_map/ppermute | solution.py:254
  35.1 3.5 %collective-permute-start.2 = (bf16[64,1536]{1,0:T(8,128)(2,1)S(1)}, bf16[64,1536]{1,0:T(8,128)(2,1)S(1)}, u32[]{:S(2)}, u32[]{:S(2)}) collective-permute-start(bf16[64,1536]{1,0:T(8,128)(2,1)S(1)} %pad_maximum_fusion.1), channel_id=1, source_target_pairs={{0,2},{1,3},{2,0},{3,1},{4,6},{5,7},{6,4},{7,5},{8,10},{9,11},{10,... | collective-permute-start | bytes 589832 | tf_op jit(solution)/shard_map/ppermute | solution.py:254
  38.6 1.0 shard_map.79.side_ref
  39.6 6.1 %collective-permute-done.2.refs_2_ = bf16[64,1536]{1,0:T(8,128)(2,1)S(1)} collective-permute-done((bf16[64,1536]{1,0:T(8,128)(2,1)S(1)}, bf16[64,1536]{1,0:T(8,128)(2,1)S(1)}, u32[]{:S(2)}, u32[]{:S(2)}) %collective-permute-start.2) | collective-permute-done | bytes 196640 | tf_op jit(solution)/shard_map/ppermute | solution.py:254
  45.7 0.0 collective-permute-done.1.refs_1_
  45.7 0.0 collective-permute-done.3.refs_3_
  45.7 1.9 %shard_map.78 = (bf16[128,768]{1,0:T(8,128)(2,1)S(1)}, bf16[128,768]{1,0:T(8,128)(2,1)S(1)}) custom-call(bf16[1536,768]{1,0:T(8,128)(2,1)S(1)} %copy-done, bf16[128,1536]{1,0:T(8,128)(2,1)S(1)} %pad_maximum_fusion.refs_0_, bf16[128,1536]{1,0:T(8,128)(2,1)S(1)} %collective-permute-done.1.refs_1_, bf16[64,1536]{1,0:T(8,128)(2,1)S(1)} %collective-permute-done.2.refs_2_, ...), custom_call_target="tpu_custom_call" | custom-call | flops 603979776 | bytes 4128768 | tf_op jit(solution)/shard_map/pallas_call | solution.py:24
  47.7 0.0 all-to-all-done.got_ref
  47.7 1.3 %shard_map.80 = bf16[4,8,160,128]{3,2,1,0:T(8,128)(2,1)} custom-call(bf16[16,120,128]{2,1,0:T(8,128)(2,1)S(1)} %all-to-all-done.got_ref, bf16[8,64,128]{2,1,0:T(8,128)(2,1)S(1)} %shard_map.79.side_ref), custom_call_target="tpu_custom_call" | custom-call | flops 1000000 | bytes 1933312 | tf_op jit(solution)/shard_map/pallas_call | solution.py:24
  49.0 10.4 %all-to-all-start.1 = ((bf16[32,160,128]{2,1,0:T(8,128)(2,1)}), bf16[32,160,128]{2,1,0:T(8,128)(2,1)S(1)}, u32[]{:S(2)}, u32[]{:S(2)}) async-start(bf16[32,160,128]{2,1,0:T(8,128)(2,1)} %bitcast), calls=%async_computation.1 | async-start | bytes 2621440 | tf_op jit(solution)/shard_map/all_to_all | solution.py:301
  59.4 2.1 %collective-permute-start.4 = (bf16[128,768]{1,0:T(8,128)(2,1)S(1)}, bf16[128,768]{1,0:T(8,128)(2,1)S(1)}, u32[]{:S(2)}, u32[]{:S(2)}) collective-permute-start(bf16[128,768]{1,0:T(8,128)(2,1)S(1)} %get-tuple-element.11), channel_id=1, source_target_pairs={{0,128},{128,0},{256,384},{384,256},{1,129},{129,1},{257,385},{385... | collective-permute-start | bytes 589832 | tf_op jit(solution)/shard_map/ppermute | solution.py:283
  61.5 1.2 %collective-permute-done.4 = bf16[128,768]{1,0:T(8,128)(2,1)S(1)} collective-permute-done((bf16[128,768]{1,0:T(8,128)(2,1)S(1)}, bf16[128,768]{1,0:T(8,128)(2,1)S(1)}, u32[]{:S(2)}, u32[]{:S(2)}) %collective-permute-start.4) | collective-permute-done | bytes 196640 | tf_op jit(solution)/shard_map/ppermute | solution.py:283
  62.7 3.9 %collective-permute-start.5 = (bf16[128,768]{1,0:T(8,128)(2,1)S(1)}, bf16[128,768]{1,0:T(8,128)(2,1)S(1)}, u32[]{:S(2)}, u32[]{:S(2)}) collective-permute-start(bf16[128,768]{1,0:T(8,128)(2,1)S(1)} %add_convert_fusion.refs_0_), channel_id=1, source_target_pairs={{0,16},{8,24},{16,32},{24,40},{32,48},{40,56},{48,64},{56,72},{64,... | collective-permute-start | bytes 589832 | tf_op jit(solution)/shard_map/ppermute | solution.py:286
  66.6 3.1 %collective-permute-start.6 = (bf16[128,768]{1,0:T(8,128)(2,1)S(1)}, bf16[128,768]{1,0:T(8,128)(2,1)S(1)}, u32[]{:S(2)}, u32[]{:S(2)}) collective-permute-start(bf16[128,768]{1,0:T(8,128)(2,1)S(1)} %add_convert_fusion.refs_0_), channel_id=1, source_target_pairs={{0,8},{8,16},{16,24},{24,32},{32,40},{40,48},{48,56},{56,64},{64,7... | collective-permute-start | bytes 589832 | tf_op jit(solution)/shard_map/ppermute | solution.py:286
  69.7 3.4 %collective-permute-start.7 = (bf16[128,768]{1,0:T(8,128)(2,1)S(1)}, bf16[128,768]{1,0:T(8,128)(2,1)S(1)}, u32[]{:S(2)}, u32[]{:S(2)}) collective-permute-start(bf16[128,768]{1,0:T(8,128)(2,1)S(1)} %add_convert_fusion.refs_0_), channel_id=1, source_target_pairs={{0,120},{8,0},{16,8},{24,16},{32,24},{40,32},{48,40},{56,48},{64,5... | collective-permute-start | bytes 589832 | tf_op jit(solution)/shard_map/ppermute | solution.py:286
  73.1 1.9 %collective-permute-done.5.refs_1_ = bf16[128,768]{1,0:T(8,128)(2,1)S(1)} collective-permute-done((bf16[128,768]{1,0:T(8,128)(2,1)S(1)}, bf16[128,768]{1,0:T(8,128)(2,1)S(1)}, u32[]{:S(2)}, u32[]{:S(2)}) %collective-permute-start.5) | collective-permute-done | bytes 196640 | tf_op jit(solution)/shard_map/ppermute | solution.py:286
  75.0 6.7 %collective-permute-done.6.refs_2_ = bf16[128,768]{1,0:T(8,128)(2,1)S(1)} collective-permute-done((bf16[128,768]{1,0:T(8,128)(2,1)S(1)}, bf16[128,768]{1,0:T(8,128)(2,1)S(1)}, u32[]{:S(2)}, u32[]{:S(2)}) %collective-permute-start.6) | collective-permute-done | bytes 196640 | tf_op jit(solution)/shard_map/ppermute | solution.py:286
  81.8 0.0 all-to-all-done.1
  81.8 1.5 %shard_map.81 = bf16[4,96,768]{2,1,0:T(8,128)(2,1)} custom-call(bf16[4,8,160,128]{3,2,1,0:T(8,128)(2,1)S(1)} %bitcast.2, bf16[128,768]{1,0:T(8,128)(2,1)S(1)} %add_convert_fusion.refs_0_, bf16[128,768]{1,0:T(8,128)(2,1)S(1)} %collective-permute-done.5.refs_1_, bf16[128,768]{1,0:T(8,128)(2,1)S(1)} %collective-permute-done.6.refs_2_, ...), custom_call_target="tpu_custom_call" | custom-call | flops 402653184 | bytes 2686976 | tf_op jit(solution)/shard_map/pallas_call | solution.py:24
  83.3 5.2 %all-to-all-start.2 = ((bf16[4,96,768]{2,1,0:T(8,128)(2,1)}), bf16[4,96,768]{2,1,0:T(8,128)(2,1)S(1)}, u32[]{:S(2)}, u32[]{:S(2)}) async-start(bf16[4,96,768]{2,1,0:T(8,128)(2,1)} %shard_map.81), calls=%async_computation.2 | async-start | bytes 1179648 | tf_op jit(solution)/shard_map/all_to_all | solution.py:312
  88.5 4.6 %collective-permute-start.8 = (bf16[64,1536]{1,0:T(8,128)(2,1)S(1)}, bf16[64,1536]{1,0:T(8,128)(2,1)S(1)}, u32[]{:S(2)}, u32[]{:S(2)}) collective-permute-start(bf16[64,1536]{1,0:T(8,128)(2,1)S(1)} %pad_maximum_fusion.2), channel_id=1, source_target_pairs={{0,2},{1,3},{2,0},{3,1},{4,6},{5,7},{6,4},{7,5},{8,10},{9,11},{10,... | collective-permute-start | bytes 589832 | tf_op jit(solution)/shard_map/ppermute | solution.py:254
  93.1 5.3 %collective-permute-done.8.refs_2_ = bf16[64,1536]{1,0:T(8,128)(2,1)S(1)} collective-permute-done((bf16[64,1536]{1,0:T(8,128)(2,1)S(1)}, bf16[64,1536]{1,0:T(8,128)(2,1)S(1)}, u32[]{:S(2)}, u32[]{:S(2)}) %collective-permute-start.8) | collective-permute-done | bytes 196640 | tf_op jit(solution)/shard_map/ppermute | solution.py:254
  98.4 1.4 %shard_map.82 = (f32[48,1536]{1,0:T(8,128)}, f32[48,1536]{1,0:T(8,128)}) custom-call(bf16[4,8,160,128]{3,2,1,0:T(8,128)(2,1)S(1)} %bitcast.3, bf16[128,1536]{1,0:T(8,128)(2,1)S(1)} %pad_maximum_fusion.refs_0_, bf16[128,1536]{1,0:T(8,128)(2,1)S(1)} %collective-permute-done.1.refs_1_, bf16[64,1536]{1,0:T(8,128)(2,1)S(1)} %collective-permute-done.8.refs_2_, ...), custom_call_target="tpu_custom_call" | custom-call | flops 201326592 | bytes 3276800 | tf_op jit(solution)/shard_map/pallas_call | solution.py:24
  99.9 0.8 convert_reduce_fusion
  (19 shorter events, 0.2 us)
Async XLA Ops:
  0.6 19.7 %copy-start.3 = (s32[32]{0:T(128)S(1)}, s32[32]{0:T(128)}, u32[]{:S(2)}) copy-start(s32[32]{0:T(128)} %picks.5) | copy-start | bytes 388
  0.6 19.7 %copy-start.1 = (bf16[128,1536]{1,0:T(8,128)(2,1)S(1)}, bf16[128,1536]{1,0:T(8,128)(2,1)}, u32[]{:S(2)}) copy-start(bf16[128,1536]{1,0:T(8,128)(2,1)} %g_ref.1) | copy-start | bytes 1179652
  4.4 34.2 %copy-start.2 = (bf16[128,384]{1,0:T(8,128)(2,1)S(1)}, bf16[128,384]{1,0:T(8,128)(2,1)}, u32[]{:S(2)}) copy-start(bf16[128,384]{1,0:T(8,128)(2,1)} %x_ref.1) | copy-start | bytes 294916
  4.4 43.3 %all-to-all-start = ((bf16[16,120,128]{2,1,0:T(8,128)(2,1)}), bf16[16,120,128]{2,1,0:T(8,128)(2,1)S(1)}, u32[]{:S(2)}, u32[]{:S(2)}) async-start(bf16[16,120,128]{2,1,0:T(8,128)(2,1)} %shard_map.76), calls=%async_computation | async-start | bytes 983040 | tf_op jit(solution)/shard_map/all_to_all | solution.py:251
  20.3 25.4 %copy-start = (bf16[1536,768]{1,0:T(8,128)(2,1)S(1)}, bf16[1536,768]{1,0:T(8,128)(2,1)}, u32[]{:S(2)}) copy-start(bf16[1536,768]{1,0:T(8,128)(2,1)} %b_hbm.1) | copy-start | bytes 7077892
  21.1 7.3 %collective-permute-start = (bf16[64,1536]{1,0:T(8,128)(2,1)S(1)}, bf16[64,1536]{1,0:T(8,128)(2,1)S(1)}, u32[]{:S(2)}, u32[]{:S(2)}) collective-permute-start(bf16[64,1536]{1,0:T(8,128)(2,1)S(1)} %shard_map.77.gy_ref), channel_id=1, source_target_pairs={{0,4},{1,5},{2,6},{3,7},{4,0},{5,1},{6,2},{7,3},{8,12},{9,13},{10,... | collective-permute-start | bytes 589832 | tf_op jit(solution)/shard_map/ppermute | solution.py:264
  28.4 6.6 %copy-start.4 = (bf16[64,1536]{1,0:T(8,128)(2,1)}, bf16[64,1536]{1,0:T(8,128)(2,1)S(1)}, u32[]{:S(2)}) copy-start(bf16[64,1536]{1,0:T(8,128)(2,1)S(1)} %collective-permute-done) | copy-start | bytes 589828
  28.4 17.3 %collective-permute-start.1 = (bf16[128,1536]{1,0:T(8,128)(2,1)S(1)}, bf16[128,1536]{1,0:T(8,128)(2,1)S(1)}, u32[]{:S(2)}, u32[]{:S(2)}) collective-permute-start(bf16[128,1536]{1,0:T(8,128)(2,1)S(1)} %pad_maximum_fusion.refs_0_), channel_id=1, source_target_pairs={{0,1},{1,2},{2,3},{3,0},{4,5},{5,6},{6,7},{7,4},{8,9},{9,10},{10,1... | collective-permute-start | bytes 1179656 | tf_op jit(solution)/shard_map/ppermute | solution.py:254
  31.7 14.1 %collective-permute-start.3 = (bf16[128,1536]{1,0:T(8,128)(2,1)S(1)}, bf16[128,1536]{1,0:T(8,128)(2,1)S(1)}, u32[]{:S(2)}, u32[]{:S(2)}) collective-permute-start(bf16[128,1536]{1,0:T(8,128)(2,1)S(1)} %pad_maximum_fusion.refs_0_), channel_id=1, source_target_pairs={{0,3},{1,0},{2,1},{3,2},{4,7},{5,4},{6,5},{7,6},{8,11},{9,8},{10,9... | collective-permute-start | bytes 1179656 | tf_op jit(solution)/shard_map/ppermute | solution.py:254
  35.1 10.7 %collective-permute-start.2 = (bf16[64,1536]{1,0:T(8,128)(2,1)S(1)}, bf16[64,1536]{1,0:T(8,128)(2,1)S(1)}, u32[]{:S(2)}, u32[]{:S(2)}) collective-permute-start(bf16[64,1536]{1,0:T(8,128)(2,1)S(1)} %pad_maximum_fusion.1), channel_id=1, source_target_pairs={{0,2},{1,3},{2,0},{3,1},{4,6},{5,7},{6,4},{7,5},{8,10},{9,11},{10,... | collective-permute-start | bytes 589832 | tf_op jit(solution)/shard_map/ppermute | solution.py:254
  49.0 32.8 %all-to-all-start.1 = ((bf16[32,160,128]{2,1,0:T(8,128)(2,1)}), bf16[32,160,128]{2,1,0:T(8,128)(2,1)S(1)}, u32[]{:S(2)}, u32[]{:S(2)}) async-start(bf16[32,160,128]{2,1,0:T(8,128)(2,1)} %bitcast), calls=%async_computation.1 | async-start | bytes 2621440 | tf_op jit(solution)/shard_map/all_to_all | solution.py:301
  59.4 3.3 %collective-permute-start.4 = (bf16[128,768]{1,0:T(8,128)(2,1)S(1)}, bf16[128,768]{1,0:T(8,128)(2,1)S(1)}, u32[]{:S(2)}, u32[]{:S(2)}) collective-permute-start(bf16[128,768]{1,0:T(8,128)(2,1)S(1)} %get-tuple-element.11), channel_id=1, source_target_pairs={{0,128},{128,0},{256,384},{384,256},{1,129},{129,1},{257,385},{385... | collective-permute-start | bytes 589832 | tf_op jit(solution)/shard_map/ppermute | solution.py:283
  62.7 12.3 %collective-permute-start.5 = (bf16[128,768]{1,0:T(8,128)(2,1)S(1)}, bf16[128,768]{1,0:T(8,128)(2,1)S(1)}, u32[]{:S(2)}, u32[]{:S(2)}) collective-permute-start(bf16[128,768]{1,0:T(8,128)(2,1)S(1)} %add_convert_fusion.refs_0_), channel_id=1, source_target_pairs={{0,16},{8,24},{16,32},{24,40},{32,48},{40,56},{48,64},{56,72},{64,... | collective-permute-start | bytes 589832 | tf_op jit(solution)/shard_map/ppermute | solution.py:286
  66.6 15.1 %collective-permute-start.6 = (bf16[128,768]{1,0:T(8,128)(2,1)S(1)}, bf16[128,768]{1,0:T(8,128)(2,1)S(1)}, u32[]{:S(2)}, u32[]{:S(2)}) collective-permute-start(bf16[128,768]{1,0:T(8,128)(2,1)S(1)} %add_convert_fusion.refs_0_), channel_id=1, source_target_pairs={{0,8},{8,16},{16,24},{24,32},{32,40},{40,48},{48,56},{56,64},{64,7... | collective-permute-start | bytes 589832 | tf_op jit(solution)/shard_map/ppermute | solution.py:286
  69.7 12.0 %collective-permute-start.7 = (bf16[128,768]{1,0:T(8,128)(2,1)S(1)}, bf16[128,768]{1,0:T(8,128)(2,1)S(1)}, u32[]{:S(2)}, u32[]{:S(2)}) collective-permute-start(bf16[128,768]{1,0:T(8,128)(2,1)S(1)} %add_convert_fusion.refs_0_), channel_id=1, source_target_pairs={{0,120},{8,0},{16,8},{24,16},{32,24},{40,32},{48,40},{56,48},{64,5... | collective-permute-start | bytes 589832 | tf_op jit(solution)/shard_map/ppermute | solution.py:286
  83.3 5.2 %slice-start = ((bf16[64,1536]{1,0:T(8,128)(2,1)}), bf16[32,1536]{1,0:T(8,128)(2,1)S(1)}, s32[]{:S(2)}) async-start(bf16[64,1536]{1,0:T(8,128)(2,1)} %copy-done.4), calls=%async_computation.3 | async-start | bytes 196608 | tf_op jit(solution)/shard_map/slice | solution.py:313
  83.3 16.6 %all-to-all-start.2 = ((bf16[4,96,768]{2,1,0:T(8,128)(2,1)}), bf16[4,96,768]{2,1,0:T(8,128)(2,1)S(1)}, u32[]{:S(2)}, u32[]{:S(2)}) async-start(bf16[4,96,768]{2,1,0:T(8,128)(2,1)} %shard_map.81), calls=%async_computation.2 | async-start | bytes 1179648 | tf_op jit(solution)/shard_map/all_to_all | solution.py:312
  88.5 9.9 %collective-permute-start.8 = (bf16[64,1536]{1,0:T(8,128)(2,1)S(1)}, bf16[64,1536]{1,0:T(8,128)(2,1)S(1)}, u32[]{:S(2)}, u32[]{:S(2)}) collective-permute-start(bf16[64,1536]{1,0:T(8,128)(2,1)S(1)} %pad_maximum_fusion.2), channel_id=1, source_target_pairs={{0,2},{1,3},{2,0},{3,1},{4,6},{5,7},{6,4},{7,5},{8,10},{9,11},{10,... | collective-permute-start | bytes 589832 | tf_op jit(solution)/shard_map/ppermute | solution.py:254

commit v16 on v15

--- a/solution.py
+++ b/solution.py
@@ -171,9 +171,8 @@
 
 
 def final_kernel(got_ref, *refs):
-    v_refs, out_ref, held = refs[:-2], refs[-2], refs[-1]
+    v_refs, own_ref, pair_ref, held = refs[:-3], refs[-3], refs[-2], refs[-1]
     n_col, spread, size, width = held.shape
-    n_grp, out_rows, unused = out_ref.shape
     row = lax.axis_index("row")
     for j, shift in enumerate(SHIFTS):
         plane = lax.rem(row - shift + spread, spread)
@@ -181,10 +180,11 @@
             held[source_of(k), plane] = v_refs[j][k * size : (k + 1) * size, :]
     tokens = n_col * spread * size
     right = held[...].reshape(tokens, width)
-    for g in range(n_grp):
-        left = got_ref[g, :, : spread * size, :].reshape(tokens, LANES)
+    grp = lax.axis_index("grp")
+    for source, ref in ((grp, own_ref), (grp ^ 1, pair_ref)):
+        left = got_ref[source, :, : spread * size, :].reshape(tokens, LANES)
         term = lax.dot_general(left, right, FIRST, preferred_element_type=F32)
-        out_ref[g] = term[:out_rows].astype(BF)
+        ref[...] = term[: ref.shape[0]].astype(ref.dtype)
 
 
 def factor_kernel(got_ref, *refs):
@@ -279,13 +279,18 @@
         ],
         places=[pl.BlockSpec(memory_space=pl.ANY)] + [VMEM] * 4,
     )
-    first, unused = lax.optimization_barrier((first, give))
     taken = lax.ppermute(give, "grp", [(i, i ^ 1) for i in range(n_grp)])
-    right = (keep.astype(F32) + taken.astype(F32)).astype(BF)
+    some = keep.astype(F32) + taken.astype(F32)
+    give = some.astype(BF)
+    first, give = lax.optimization_barrier((first, give))
+    taken = lax.ppermute(give, "grp", [(i, i ^ 2) for i in range(n_grp)])
+    right = (some + taken.astype(F32)).astype(BF)
     rights = [right] + [
         lax.ppermute(right, "row", [(i, (i + j) % n_row) for i in range(n_row)])
         for j in SHIFTS[1:]
     ]
+    unused, picked_y, beside_y = lax.optimization_barrier((right, picked[cut:], beside[cut:]))
+    far = along_y(jnp.concatenate([picked_y, beside_y], axis=0), 2)
     side = call(
         side_kernel,
         (sample_rows, tokens_in, picked),
@@ -301,17 +306,17 @@
     got = lax.all_to_all(send.reshape((n_grp * n_col,) + send.shape[2:]), ("grp", "col"), 0, 0)
     got = got.reshape(send.shape)
 
-    term = call(
+    rights, far = lax.optimization_barrier((rights, far))
+    term, give = call(
         final_kernel,
         (got, *rights),
-        [shape((n_grp, out_rows, width), BF)],
-        2 * n_grp * LANES * n_col * spread * size * width,
+        [shape((out_rows, width), F32), shape((out_rows, width), BF)],
+        4 * LANES * n_col * spread * size * width,
         [pltpu.VMEM((n_col, spread, size, width), BF)],
-    )[0]
-    got, picked, beside, unused = lax.optimization_barrier((got, picked, beside, term))
-    term = lax.all_to_all(term, "grp", 0, 0)
-    far = along_y(jnp.concatenate([picked[cut:], beside[cut:]], axis=0), 2)
-    precond = jnp.sum(term.astype(F32), axis=0)
+    )
+    taken = lax.ppermute(give, "grp", [(i, i ^ 1) for i in range(n_grp)])
+    precond = term + taken.astype(F32)
+    got, unused = lax.optimization_barrier((got, give))
     act_cov, grad_cov = call(
         factor_kernel,
         (got, pair, near[1], far, near[3]),

time: 101 us -> 111 us (1.099)
  waiting for transfers between devices: 25.5 us -> 32.3 us
  starting transfers between devices: 61.8 us -> 65.8 us
    ppermute x0 -> x1, waiting for transfers between devices: none -> 17.2 us  [body(): taken = lax.ppermute(give, 'grp', [(i, i ^ 2) for i in range(n_grp)])]
    ppermute x1 -> x2, starting transfers between devices: 2.14 us -> 8.99 us  [body(): taken = lax.ppermute(give, 'grp', [(i, i ^ 1) for i in range(n_grp)])]
    all_to_all x1 -> x0, starting transfers between devices: 5.19 us -> none  [body(): term = lax.all_to_all(term, 'grp', 0, 0)]
    ppermute x3, waiting for transfers between devices: 8.64 us -> 3.76 us  [body(): lax.ppermute(right, 'row', [(i, (i + j) % n_row) for i in range(n_row)])]
    ppermute x0 -> x1, starting transfers between devices: none -> 4.82 us  [body(): taken = lax.ppermute(give, 'grp', [(i, i ^ 2) for i in range(n_grp)])]
    ppermute x4, waiting for transfers between devices: 11.5 us -> 6.98 us  [along_y(): lax.ppermute(block, 'col', [(i, i - i % 4 + (i + k) % 4) for i in range(n...]
    all_to_all x1, starting transfers between devices: 10.4 us -> 7.94 us  [body(): lax.all_to_all(send.reshape((n_grp * n_col,) + send.shape[2:]), ('grp', '...]
    ppermute x1 -> x2, waiting for transfers between devices: 1.19 us -> 0.07 us  [body(): taken = lax.ppermute(give, 'grp', [(i, i ^ 1) for i in range(n_grp)])]
  transfers between devices with their start and end apart: 12 -> 13, of which waited for: 6 -> 5; matrix products, arithmetic and copies ran while one was open for 0% -> 0% of each run, Pallas kernels for 5% -> 5%
where the time goes in v16:
time: 111 us; the launch traced here: 110 us
  starting transfers between devices  65.8 us (59%)
  waiting for transfers between devices  32.3 us (29%)
  Pallas kernels  10.5 us (9%)
    ppermute x1, waiting for transfers between devices, body(): taken = lax.ppermute(give, 'grp', [(i, i ^ 2) for i in range(n_grp)])  17.2 us
    all_to_all x1, starting transfers between devices, body(): first = lax.all_to_all(payload, 'row', 0, 0)  15.8 us
    ppermute x4, starting transfers between devices, along_y(): lax.ppermute(block, 'col', [(i, i - i % 4 + (i + k) % 4) for i in range(n...  14.8 us
    pallas_call x7, Pallas kernels, call(): pl.pallas_call(kernel, out_shape=outs, in_specs=places, out_specs=[VMEM]...  10.5 us
    ppermute x3, starting transfers between devices, body(): lax.ppermute(right, 'row', [(i, (i + j) % n_row) for i in range(n_row)])  10.4 us
    ppermute x2, starting transfers between devices, body(): taken = lax.ppermute(give, 'grp', [(i, i ^ 1) for i in range(n_grp)])  8.99 us
    all_to_all x1, starting transfers between devices, body(): lax.all_to_all(send.reshape((n_grp * n_col,) + send.shape[2:]), ('grp', '...  7.94 us
    ppermute x4, waiting for transfers between devices, along_y(): lax.ppermute(block, 'col', [(i, i - i % 4 + (i + k) % 4) for i in range(n...  6.98 us
  transfers between devices with their start and end apart: 13, of which 5 were waited for; matrix products, arithmetic and copies ran while one was open for 0% of the time, Pallas kernels for 5%

profile of v16, /device:TPU:1, one launch (start us, length us, event | category | flops | bytes accessed | tf_op | source)
XLA Modules:
  0.0 110.5 jit_solution(12452614827274027273)
XLA Ops:
  0.7 3.7 %shard_map.76 = bf16[16,120,128]{2,1,0:T(8,128)(2,1)} custom-call(s32[32]{0:T(128)} %picks.5, bf16[128,384]{1,0:T(8,128)(2,1)} %x_ref.1, bf16[1536,384]{1,0:T(8,128)(2,1)} %a_hbm.1), custom_call_target="tpu_custom_call" | custom-call | flops 150994944 | bytes 1769600 | tf_op jit(solution)/shard_map/pallas_call | solution.py:24
  4.4 15.8 %all-to-all-start = ((bf16[16,120,128]{2,1,0:T(8,128)(2,1)}), bf16[16,120,128]{2,1,0:T(8,128)(2,1)S(1)}, u32[]{:S(2)}, u32[]{:S(2)}) async-start(bf16[16,120,128]{2,1,0:T(8,128)(2,1)} %shard_map.76), calls=%async_computation | async-start | bytes 983040 | tf_op jit(solution)/shard_map/all_to_all | solution.py:251
  20.2 0.0 copy-start
  20.2 0.7 shard_map.77.gy_ref
  20.9 3.1 %collective-permute-start = (bf16[64,1536]{1,0:T(8,128)(2,1)S(1)}, bf16[64,1536]{1,0:T(8,128)(2,1)S(1)}, u32[]{:S(2)}, u32[]{:S(2)}) collective-permute-start(bf16[64,1536]{1,0:T(8,128)(2,1)S(1)} %shard_map.77.gy_ref), channel_id=1, source_target_pairs={{0,4},{1,5},{2,6},{3,7},{4,0},{5,1},{6,2},{7,3},{8,12},{9,13},{10,... | collective-permute-start | bytes 589832 | tf_op jit(solution)/shard_map/ppermute | solution.py:264
  24.1 4.2 %collective-permute-done = bf16[64,1536]{1,0:T(8,128)(2,1)S(1)} collective-permute-done((bf16[64,1536]{1,0:T(8,128)(2,1)S(1)}, bf16[64,1536]{1,0:T(8,128)(2,1)S(1)}, u32[]{:S(2)}, u32[]{:S(2)}) %collective-permute-start) | collective-permute-done | bytes 196640 | tf_op jit(solution)/shard_map/ppermute | solution.py:264
  28.3 3.2 %collective-permute-start.1 = (bf16[128,1536]{1,0:T(8,128)(2,1)S(1)}, bf16[128,1536]{1,0:T(8,128)(2,1)S(1)}, u32[]{:S(2)}, u32[]{:S(2)}) collective-permute-start(bf16[128,1536]{1,0:T(8,128)(2,1)S(1)} %pad_maximum_fusion.refs_0_), channel_id=1, source_target_pairs={{0,1},{1,2},{2,3},{3,0},{4,5},{5,6},{6,7},{7,4},{8,9},{9,10},{10,1... | collective-permute-start | bytes 1179656 | tf_op jit(solution)/shard_map/ppermute | solution.py:254
  31.5 3.3 %collective-permute-start.3 = (bf16[128,1536]{1,0:T(8,128)(2,1)S(1)}, bf16[128,1536]{1,0:T(8,128)(2,1)S(1)}, u32[]{:S(2)}, u32[]{:S(2)}) collective-permute-start(bf16[128,1536]{1,0:T(8,128)(2,1)S(1)} %pad_maximum_fusion.refs_0_), channel_id=1, source_target_pairs={{0,3},{1,0},{2,1},{3,2},{4,7},{5,4},{6,5},{7,6},{8,11},{9,8},{10,9... | collective-permute-start | bytes 1179656 | tf_op jit(solution)/shard_map/ppermute | solution.py:254
  34.9 0.0 copy-start.2
  34.9 3.7 %collective-permute-start.2 = (bf16[64,1536]{1,0:T(8,128)(2,1)S(1)}, bf16[64,1536]{1,0:T(8,128)(2,1)S(1)}, u32[]{:S(2)}, u32[]{:S(2)}) collective-permute-start(bf16[64,1536]{1,0:T(8,128)(2,1)S(1)} %pad_maximum_fusion.1), channel_id=1, source_target_pairs={{0,2},{1,3},{2,0},{3,1},{4,6},{5,7},{6,4},{7,5},{8,10},{9,11},{10,... | collective-permute-start | bytes 589832 | tf_op jit(solution)/shard_map/ppermute | solution.py:254
  38.6 7.0 %collective-permute-done.2.refs_2_ = bf16[64,1536]{1,0:T(8,128)(2,1)S(1)} collective-permute-done((bf16[64,1536]{1,0:T(8,128)(2,1)S(1)}, bf16[64,1536]{1,0:T(8,128)(2,1)S(1)}, u32[]{:S(2)}, u32[]{:S(2)}) %collective-permute-start.2) | collective-permute-done | bytes 196640 | tf_op jit(solution)/shard_map/ppermute | solution.py:254
  45.6 0.0 collective-permute-done.1.refs_1_
  45.6 0.0 collective-permute-done.3.refs_3_
  45.6 1.9 %shard_map.78 = (bf16[128,768]{1,0:T(8,128)(2,1)S(1)}, bf16[128,768]{1,0:T(8,128)(2,1)S(1)}) custom-call(bf16[1536,768]{1,0:T(8,128)(2,1)S(1)} %copy-done, bf16[128,1536]{1,0:T(8,128)(2,1)S(1)} %pad_maximum_fusion.refs_0_, bf16[128,1536]{1,0:T(8,128)(2,1)S(1)} %collective-permute-done.1.refs_1_, bf16[64,1536]{1,0:T(8,128)(2,1)S(1)} %collective-permute-done.2.refs_2_, ...), custom_call_target="tpu_custom_call" | custom-call | flops 603979776 | bytes 4128768 | tf_op jit(solution)/shard_map/pallas_call | solution.py:24
  47.5 4.7 %collective-permute-start.4 = (bf16[128,768]{1,0:T(8,128)(2,1)S(1)}, bf16[128,768]{1,0:T(8,128)(2,1)S(1)}, u32[]{:S(2)}, u32[]{:S(2)}) collective-permute-start(bf16[128,768]{1,0:T(8,128)(2,1)S(1)} %get-tuple-element.20), channel_id=1, source_target_pairs={{0,128},{128,0},{256,384},{384,256},{1,129},{129,1},{257,385},{385... | collective-permute-start | bytes 589832 | tf_op jit(solution)/shard_map/ppermute | solution.py:282
  52.2 1.0 shard_map.79.side_ref
  53.2 0.1 collective-permute-done.4
  53.4 1.3 %shard_map.80 = bf16[4,8,160,128]{3,2,1,0:T(8,128)(2,1)} custom-call(bf16[16,120,128]{2,1,0:T(8,128)(2,1)S(1)} %all-to-all-done.got_ref, bf16[8,64,128]{2,1,0:T(8,128)(2,1)S(1)} %shard_map.79.side_ref), custom_call_target="tpu_custom_call" | custom-call | flops 1000000 | bytes 1933312 | tf_op jit(solution)/shard_map/pallas_call | solution.py:24
  54.6 7.9 %all-to-all-start.1 = ((bf16[32,160,128]{2,1,0:T(8,128)(2,1)}), bf16[32,160,128]{2,1,0:T(8,128)(2,1)S(1)}, u32[]{:S(2)}, u32[]{:S(2)}) async-start(bf16[32,160,128]{2,1,0:T(8,128)(2,1)} %bitcast), calls=%async_computation.1 | async-start | bytes 2621440 | tf_op jit(solution)/shard_map/all_to_all | solution.py:306
  62.6 4.8 %collective-permute-start.5 = (bf16[128,768]{1,0:T(8,128)(2,1)S(1)}, bf16[128,768]{1,0:T(8,128)(2,1)S(1)}, u32[]{:S(2)}, u32[]{:S(2)}) collective-permute-start(bf16[128,768]{1,0:T(8,128)(2,1)S(1)} %fusion), channel_id=1, source_target_pairs={{0,256},{128,384},{256,0},{384,128},{1,257},{129,385},{257,1},{385... | collective-permute-start | bytes 589832 | tf_op jit(solution)/shard_map/ppermute | solution.py:286
  67.4 17.2 %collective-permute-done.5 = bf16[128,768]{1,0:T(8,128)(2,1)S(1)} collective-permute-done((bf16[128,768]{1,0:T(8,128)(2,1)S(1)}, bf16[128,768]{1,0:T(8,128)(2,1)S(1)}, u32[]{:S(2)}, u32[]{:S(2)}) %collective-permute-start.5) | collective-permute-done | bytes 196640 | tf_op jit(solution)/shard_map/ppermute | solution.py:286
  84.6 0.1 add_convert_fusion.refs_0_
  84.7 3.9 %collective-permute-start.6 = (bf16[128,768]{1,0:T(8,128)(2,1)S(1)}, bf16[128,768]{1,0:T(8,128)(2,1)S(1)}, u32[]{:S(2)}, u32[]{:S(2)}) collective-permute-start(bf16[128,768]{1,0:T(8,128)(2,1)S(1)} %add_convert_fusion.refs_0_), channel_id=1, source_target_pairs={{0,16},{8,24},{16,32},{24,40},{32,48},{40,56},{48,64},{56,72},{64,... | collective-permute-start | bytes 589832 | tf_op jit(solution)/shard_map/ppermute | solution.py:289
  88.6 3.1 %collective-permute-start.7 = (bf16[128,768]{1,0:T(8,128)(2,1)S(1)}, bf16[128,768]{1,0:T(8,128)(2,1)S(1)}, u32[]{:S(2)}, u32[]{:S(2)}) collective-permute-start(bf16[128,768]{1,0:T(8,128)(2,1)S(1)} %add_convert_fusion.refs_0_), channel_id=1, source_target_pairs={{0,8},{8,16},{16,24},{24,32},{32,40},{40,48},{48,56},{56,64},{64,7... | collective-permute-start | bytes 589832 | tf_op jit(solution)/shard_map/ppermute | solution.py:289
  91.7 3.4 %collective-permute-start.8 = (bf16[128,768]{1,0:T(8,128)(2,1)S(1)}, bf16[128,768]{1,0:T(8,128)(2,1)S(1)}, u32[]{:S(2)}, u32[]{:S(2)}) collective-permute-start(bf16[128,768]{1,0:T(8,128)(2,1)S(1)} %add_convert_fusion.refs_0_), channel_id=1, source_target_pairs={{0,120},{8,0},{16,8},{24,16},{32,24},{40,32},{48,40},{56,48},{64,5... | collective-permute-start | bytes 589832 | tf_op jit(solution)/shard_map/ppermute | solution.py:289
  95.1 4.6 %collective-permute-start.9 = (bf16[64,1536]{1,0:T(8,128)(2,1)S(1)}, bf16[64,1536]{1,0:T(8,128)(2,1)S(1)}, u32[]{:S(2)}, u32[]{:S(2)}) collective-permute-start(bf16[64,1536]{1,0:T(8,128)(2,1)S(1)} %pad_maximum_fusion.2), channel_id=1, source_target_pairs={{0,2},{1,3},{2,0},{3,1},{4,6},{5,7},{6,4},{7,5},{8,10},{9,11},{10,... | collective-permute-start | bytes 589832 | tf_op jit(solution)/shard_map/ppermute | solution.py:254
  99.7 0.0 collective-permute-done.6.refs_1_
  99.8 3.8 %collective-permute-done.7.refs_2_ = bf16[128,768]{1,0:T(8,128)(2,1)S(1)} collective-permute-done((bf16[128,768]{1,0:T(8,128)(2,1)S(1)}, bf16[128,768]{1,0:T(8,128)(2,1)S(1)}, u32[]{:S(2)}, u32[]{:S(2)}) %collective-permute-start.7) | collective-permute-done | bytes 196640 | tf_op jit(solution)/shard_map/ppermute | solution.py:289
  103.5 0.5 shard_map.81
  104.0 4.3 %collective-permute-start.10 = (bf16[96,768]{1,0:T(8,128)(2,1)S(1)}, bf16[96,768]{1,0:T(8,128)(2,1)S(1)}, u32[]{:S(2)}, u32[]{:S(2)}) collective-permute-start(bf16[96,768]{1,0:T(8,128)(2,1)S(1)} %get-tuple-element.30), channel_id=1, source_target_pairs={{0,128},{128,0},{256,384},{384,256},{1,129},{129,1},{257,385},{385... | collective-permute-start | bytes 442376 | tf_op jit(solution)/shard_map/ppermute | solution.py:317
  108.3 1.4 %shard_map.82 = (f32[48,1536]{1,0:T(8,128)}, f32[48,1536]{1,0:T(8,128)}) custom-call(bf16[4,8,160,128]{3,2,1,0:T(8,128)(2,1)S(1)} %bitcast.3, bf16[128,1536]{1,0:T(8,128)(2,1)S(1)} %pad_maximum_fusion.refs_0_, bf16[128,1536]{1,0:T(8,128)(2,1)S(1)} %collective-permute-done.1.refs_1_, bf16[64,1536]{1,0:T(8,128)(2,1)S(1)} %collective-permute-done.9.refs_2_, ...), custom_call_target="tpu_custom_call" | custom-call | flops 201326592 | bytes 3276800 | tf_op jit(solution)/shard_map/pallas_call | solution.py:24
  109.7 0.7 convert_add_fusion.1
  (17 shorter events, 0.2 us)
Async XLA Ops:
  0.6 19.5 %copy-start.3 = (s32[32]{0:T(128)S(1)}, s32[32]{0:T(128)}, u32[]{:S(2)}) copy-start(s32[32]{0:T(128)} %picks.5) | copy-start | bytes 388
  0.6 19.5 %copy-start.1 = (bf16[128,1536]{1,0:T(8,128)(2,1)S(1)}, bf16[128,1536]{1,0:T(8,128)(2,1)}, u32[]{:S(2)}) copy-start(bf16[128,1536]{1,0:T(8,128)(2,1)} %g_ref.1) | copy-start | bytes 1179652
  4.4 49.0 %all-to-all-start = ((bf16[16,120,128]{2,1,0:T(8,128)(2,1)}), bf16[16,120,128]{2,1,0:T(8,128)(2,1)S(1)}, u32[]{:S(2)}, u32[]{:S(2)}) async-start(bf16[16,120,128]{2,1,0:T(8,128)(2,1)} %shard_map.76), calls=%async_computation | async-start | bytes 983040 | tf_op jit(solution)/shard_map/all_to_all | solution.py:251
  20.2 25.4 %copy-start = (bf16[1536,768]{1,0:T(8,128)(2,1)S(1)}, bf16[1536,768]{1,0:T(8,128)(2,1)}, u32[]{:S(2)}) copy-start(bf16[1536,768]{1,0:T(8,128)(2,1)} %b_hbm.1) | copy-start | bytes 7077892
  20.9 7.3 %collective-permute-start = (bf16[64,1536]{1,0:T(8,128)(2,1)S(1)}, bf16[64,1536]{1,0:T(8,128)(2,1)S(1)}, u32[]{:S(2)}, u32[]{:S(2)}) collective-permute-start(bf16[64,1536]{1,0:T(8,128)(2,1)S(1)} %shard_map.77.gy_ref), channel_id=1, source_target_pairs={{0,4},{1,5},{2,6},{3,7},{4,0},{5,1},{6,2},{7,3},{8,12},{9,13},{10,... | collective-permute-start | bytes 589832 | tf_op jit(solution)/shard_map/ppermute | solution.py:264
  28.3 17.3 %collective-permute-start.1 = (bf16[128,1536]{1,0:T(8,128)(2,1)S(1)}, bf16[128,1536]{1,0:T(8,128)(2,1)S(1)}, u32[]{:S(2)}, u32[]{:S(2)}) collective-permute-start(bf16[128,1536]{1,0:T(8,128)(2,1)S(1)} %pad_maximum_fusion.refs_0_), channel_id=1, source_target_pairs={{0,1},{1,2},{2,3},{3,0},{4,5},{5,6},{6,7},{7,4},{8,9},{9,10},{10,1... | collective-permute-start | bytes 1179656 | tf_op jit(solution)/shard_map/ppermute | solution.py:254
  31.5 14.1 %collective-permute-start.3 = (bf16[128,1536]{1,0:T(8,128)(2,1)S(1)}, bf16[128,1536]{1,0:T(8,128)(2,1)S(1)}, u32[]{:S(2)}, u32[]{:S(2)}) collective-permute-start(bf16[128,1536]{1,0:T(8,128)(2,1)S(1)} %pad_maximum_fusion.refs_0_), channel_id=1, source_target_pairs={{0,3},{1,0},{2,1},{3,2},{4,7},{5,4},{6,5},{7,6},{8,11},{9,8},{10,9... | collective-permute-start | bytes 1179656 | tf_op jit(solution)/shard_map/ppermute | solution.py:254
  34.9 17.3 %copy-start.2 = (bf16[128,384]{1,0:T(8,128)(2,1)S(1)}, bf16[128,384]{1,0:T(8,128)(2,1)}, u32[]{:S(2)}) copy-start(bf16[128,384]{1,0:T(8,128)(2,1)} %x_ref.1) | copy-start | bytes 294916
  34.9 10.7 %collective-permute-start.2 = (bf16[64,1536]{1,0:T(8,128)(2,1)S(1)}, bf16[64,1536]{1,0:T(8,128)(2,1)S(1)}, u32[]{:S(2)}, u32[]{:S(2)}) collective-permute-start(bf16[64,1536]{1,0:T(8,128)(2,1)S(1)} %pad_maximum_fusion.1), channel_id=1, source_target_pairs={{0,2},{1,3},{2,0},{3,1},{4,6},{5,7},{6,4},{7,5},{8,10},{9,11},{10,... | collective-permute-start | bytes 589832 | tf_op jit(solution)/shard_map/ppermute | solution.py:254
  47.5 5.8 %collective-permute-start.4 = (bf16[128,768]{1,0:T(8,128)(2,1)S(1)}, bf16[128,768]{1,0:T(8,128)(2,1)S(1)}, u32[]{:S(2)}, u32[]{:S(2)}) collective-permute-start(bf16[128,768]{1,0:T(8,128)(2,1)S(1)} %get-tuple-element.20), channel_id=1, source_target_pairs={{0,128},{128,0},{256,384},{384,256},{1,129},{129,1},{257,385},{385... | collective-permute-start | bytes 589832 | tf_op jit(solution)/shard_map/ppermute | solution.py:282
  54.6 48.9 %all-to-all-start.1 = ((bf16[32,160,128]{2,1,0:T(8,128)(2,1)}), bf16[32,160,128]{2,1,0:T(8,128)(2,1)S(1)}, u32[]{:S(2)}, u32[]{:S(2)}) async-start(bf16[32,160,128]{2,1,0:T(8,128)(2,1)} %bitcast), calls=%async_computation.1 | async-start | bytes 2621440 | tf_op jit(solution)/shard_map/all_to_all | solution.py:306
  62.6 22.1 %collective-permute-start.5 = (bf16[128,768]{1,0:T(8,128)(2,1)S(1)}, bf16[128,768]{1,0:T(8,128)(2,1)S(1)}, u32[]{:S(2)}, u32[]{:S(2)}) collective-permute-start(bf16[128,768]{1,0:T(8,128)(2,1)S(1)} %fusion), channel_id=1, source_target_pairs={{0,256},{128,384},{256,0},{384,128},{1,257},{129,385},{257,1},{385... | collective-permute-start | bytes 589832 | tf_op jit(solution)/shard_map/ppermute | solution.py:286
  84.7 15.0 %collective-permute-start.6 = (bf16[128,768]{1,0:T(8,128)(2,1)S(1)}, bf16[128,768]{1,0:T(8,128)(2,1)S(1)}, u32[]{:S(2)}, u32[]{:S(2)}) collective-permute-start(bf16[128,768]{1,0:T(8,128)(2,1)S(1)} %add_convert_fusion.refs_0_), channel_id=1, source_target_pairs={{0,16},{8,24},{16,32},{24,40},{32,48},{40,56},{48,64},{56,72},{64,... | collective-permute-start | bytes 589832 | tf_op jit(solution)/shard_map/ppermute | solution.py:289
  88.6 14.9 %collective-permute-start.7 = (bf16[128,768]{1,0:T(8,128)(2,1)S(1)}, bf16[128,768]{1,0:T(8,128)(2,1)S(1)}, u32[]{:S(2)}, u32[]{:S(2)}) collective-permute-start(bf16[128,768]{1,0:T(8,128)(2,1)S(1)} %add_convert_fusion.refs_0_), channel_id=1, source_target_pairs={{0,8},{8,16},{16,24},{24,32},{32,40},{40,48},{48,56},{56,64},{64,7... | collective-permute-start | bytes 589832 | tf_op jit(solution)/shard_map/ppermute | solution.py:289
  91.7 11.8 %collective-permute-start.8 = (bf16[128,768]{1,0:T(8,128)(2,1)S(1)}, bf16[128,768]{1,0:T(8,128)(2,1)S(1)}, u32[]{:S(2)}, u32[]{:S(2)}) collective-permute-start(bf16[128,768]{1,0:T(8,128)(2,1)S(1)} %add_convert_fusion.refs_0_), channel_id=1, source_target_pairs={{0,120},{8,0},{16,8},{24,16},{32,24},{40,32},{48,40},{56,48},{64,5... | collective-permute-start | bytes 589832 | tf_op jit(solution)/shard_map/ppermute | solution.py:289
  95.1 8.4 %collective-permute-start.9 = (bf16[64,1536]{1,0:T(8,128)(2,1)S(1)}, bf16[64,1536]{1,0:T(8,128)(2,1)S(1)}, u32[]{:S(2)}, u32[]{:S(2)}) collective-permute-start(bf16[64,1536]{1,0:T(8,128)(2,1)S(1)} %pad_maximum_fusion.2), channel_id=1, source_target_pairs={{0,2},{1,3},{2,0},{3,1},{4,6},{5,7},{6,4},{7,5},{8,10},{9,11},{10,... | collective-permute-start | bytes 589832 | tf_op jit(solution)/shard_map/ppermute | solution.py:254
  104.0 5.7 %collective-permute-start.10 = (bf16[96,768]{1,0:T(8,128)(2,1)S(1)}, bf16[96,768]{1,0:T(8,128)(2,1)S(1)}, u32[]{:S(2)}, u32[]{:S(2)}) collective-permute-start(bf16[96,768]{1,0:T(8,128)(2,1)S(1)} %get-tuple-element.30), channel_id=1, source_target_pairs={{0,128},{128,0},{256,384},{384,256},{1,129},{129,1},{257,385},{385... | collective-permute-start | bytes 442376 | tf_op jit(solution)/shard_map/ppermute | solution.py:317

commit v17 on v16

--- a/solution.py
+++ b/solution.py
@@ -122,26 +122,12 @@
     return [block[at : at + count, :] for at in (begin, step + begin)]
 
 
-def right_kernel(b_hbm, *refs):
-    blocks, keep_ref, give_ref, held, b_ref, sems = refs[:-5], *refs[-5:]
+def right_kernel(b_ref, *refs):
+    blocks, keep_ref, give_ref, held = refs[:-3], refs[-3], refs[-2], refs[-1]
     n_blk, unused, size, width = held.shape
-    parts = sems.shape[0]
-    step = b_ref.shape[0] // parts
-    spans = [pl.ds(p * step, step) for p in range(parts)]
-    copies = [
-        pltpu.make_async_copy(b_hbm.at[span], b_ref.at[span], sems.at[p])
-        for p, span in enumerate(spans)
-    ]
-    for copy in copies:
-        copy.start()
     rows = [piece for block in blocks for piece in rows_of(block, 0, 2 * size)]
     rows = jnp.concatenate(rows, axis=0)
-    term = None
-    for p in range(parts):
-        copies[p].wait()
-        left = rows[:, p * step : (p + 1) * step]
-        part = jnp.dot(left, b_ref[spans[p], :], preferred_element_type=F32)
-        term = part if term is None else term + part
+    term = jnp.dot(rows, b_ref[...], preferred_element_type=F32)
     held[...] = term.reshape(held.shape)
     core = lax.axis_index("grp") % 2
     keep_ref[...] = held[:, core].reshape(n_blk * size, width).astype(BF)
@@ -272,12 +258,7 @@
         (grad_inverse, *pairs),
         [shape((n_col * size, width), BF)] * 2,
         4 * n_col * size * feat_grp * width,
-        [
-            pltpu.VMEM((n_col, 2, size, width), F32),
-            pltpu.VMEM(grad_inverse.shape, BF),
-            pltpu.SemaphoreType.DMA((4,)),
-        ],
-        places=[pl.BlockSpec(memory_space=pl.ANY)] + [VMEM] * 4,
+        [pltpu.VMEM((n_col, 2, size, width), F32)],
     )
     taken = lax.ppermute(give, "grp", [(i, i ^ 1) for i in range(n_grp)])
     some = keep.astype(F32) + taken.astype(F32)
@@ -285,12 +266,6 @@
     first, give = lax.optimization_barrier((first, give))
     taken = lax.ppermute(give, "grp", [(i, i ^ 2) for i in range(n_grp)])
     right = (some + taken.astype(F32)).astype(BF)
-    rights = [right] + [
-        lax.ppermute(right, "row", [(i, (i + j) % n_row) for i in range(n_row)])
-        for j in SHIFTS[1:]
-    ]
-    unused, picked_y, beside_y = lax.optimization_barrier((right, picked[cut:], beside[cut:]))
-    far = along_y(jnp.concatenate([picked_y, beside_y], axis=0), 2)
     side = call(
         side_kernel,
         (sample_rows, tokens_in, picked),
@@ -303,8 +278,15 @@
         [shape((n_grp, n_col, size * spread + strip * n_row // n_grp, LANES), BF)],
         1000000,
     )[0]
+    send, right = lax.optimization_barrier((send, right))
     got = lax.all_to_all(send.reshape((n_grp * n_col,) + send.shape[2:]), ("grp", "col"), 0, 0)
     got = got.reshape(send.shape)
+    rights = [right] + [
+        lax.ppermute(right, "row", [(i, (i + j) % n_row) for i in range(n_row)])
+        for j in SHIFTS[1:]
+    ]
+    unused, picked_y, beside_y = lax.optimization_barrier((right, picked[cut:], beside[cut:]))
+    far = along_y(jnp.concatenate([picked_y, beside_y], axis=0), 2)
 
     rights, far = lax.optimization_barrier((rights, far))
     term, give = call(

time: 111 us -> 104 us (0.937)
  the two profiles are of different devices: /device:TPU:1 before, /device:TPU:33 now
where the time goes in v17:
time: 104 us; the launch traced here: 103 us
  starting transfers between devices  62.4 us (60%)
  waiting for transfers between devices  26 us (25%)
  Pallas kernels  9.34 us (9%)
  local copies, waits for them, and re-layouts  3.35 us (3%)
    ppermute x4, waiting for transfers between devices, along_y(): lax.ppermute(block, 'col', [(i, i - i % 4 + (i + k) % 4) for i in range(n...  16.6 us
    ppermute x4, starting transfers between devices, along_y(): lax.ppermute(block, 'col', [(i, i - i % 4 + (i + k) % 4) for i in range(n...  15 us
    all_to_all x1, starting transfers between devices, body(): first = lax.all_to_all(payload, 'row', 0, 0)  14.7 us
    ppermute x3, starting transfers between devices, body(): lax.ppermute(right, 'row', [(i, (i + j) % n_row) for i in range(n_row)])  10.5 us
    ppermute x2, starting transfers between devices, body(): taken = lax.ppermute(give, 'grp', [(i, i ^ 1) for i in range(n_grp)])  9.38 us
    pallas_call x7, Pallas kernels, call(): pl.pallas_call(kernel, out_shape=outs, in_specs=places, out_specs=[VMEM]...  9.34 us
    ppermute x3, waiting for transfers between devices, body(): lax.ppermute(right, 'row', [(i, (i + j) % n_row) for i in range(n_row)])  5.45 us
    all_to_all x1, starting transfers between devices, body(): lax.all_to_all(send.reshape((n_grp * n_col,) + send.shape[2:]), ('grp', '...  5.4 us
  transfers between devices with their start and end apart: 13, of which 5 were waited for; matrix products, arithmetic and copies ran while one was open for 0% of the time, Pallas kernels for 8%

profile of v17, /device:TPU:33, one launch (start us, length us, event | category | flops | bytes accessed | tf_op | source)
XLA Modules:
  0.0 103.0 jit_solution(2264665300513587192)
XLA Ops:
  0.6 1.0 copy-done.1
  1.6 0.7 copy-done.3
  2.3 0.7 shard_map.77.gy_ref
  3.0 3.1 %collective-permute-start = (bf16[64,1536]{1,0:T(8,128)(2,1)S(1)}, bf16[64,1536]{1,0:T(8,128)(2,1)S(1)}, u32[]{:S(2)}, u32[]{:S(2)}) collective-permute-start(bf16[64,1536]{1,0:T(8,128)(2,1)S(1)} %shard_map.77.gy_ref), channel_id=1, source_target_pairs={{0,4},{1,5},{2,6},{3,7},{4,0},{5,1},{6,2},{7,3},{8,12},{9,13},{10,... | collective-permute-start | bytes 589832 | tf_op jit(solution)/shard_map/ppermute | solution.py:250
  6.2 3.6 %shard_map.76 = bf16[16,120,128]{2,1,0:T(8,128)(2,1)} custom-call(s32[32]{0:T(128)} %picks.5, bf16[128,384]{1,0:T(8,128)(2,1)} %x_ref.1, bf16[1536,384]{1,0:T(8,128)(2,1)} %a_hbm.1), custom_call_target="tpu_custom_call" | custom-call | flops 150994944 | bytes 1769600 | tf_op jit(solution)/shard_map/pallas_call | solution.py:24
  9.8 14.7 %all-to-all-start = ((bf16[16,120,128]{2,1,0:T(8,128)(2,1)}), bf16[16,120,128]{2,1,0:T(8,128)(2,1)S(1)}, u32[]{:S(2)}, u32[]{:S(2)}) async-start(bf16[16,120,128]{2,1,0:T(8,128)(2,1)} %shard_map.76), calls=%async_computation | async-start | bytes 983040 | tf_op jit(solution)/shard_map/all_to_all | solution.py:237
  24.5 4.6 %collective-permute-start.3 = (bf16[128,1536]{1,0:T(8,128)(2,1)S(1)}, bf16[128,1536]{1,0:T(8,128)(2,1)S(1)}, u32[]{:S(2)}, u32[]{:S(2)}) collective-permute-start(bf16[128,1536]{1,0:T(8,128)(2,1)S(1)} %pad_maximum_fusion.refs_0_), channel_id=1, source_target_pairs={{0,3},{1,0},{2,1},{3,2},{4,7},{5,4},{6,5},{7,6},{8,11},{9,8},{10,9... | collective-permute-start | bytes 1179656 | tf_op jit(solution)/shard_map/ppermute | solution.py:240
  29.1 1.9 %collective-permute-start.1 = (bf16[128,1536]{1,0:T(8,128)(2,1)S(1)}, bf16[128,1536]{1,0:T(8,128)(2,1)S(1)}, u32[]{:S(2)}, u32[]{:S(2)}) collective-permute-start(bf16[128,1536]{1,0:T(8,128)(2,1)S(1)} %pad_maximum_fusion.refs_0_), channel_id=1, source_target_pairs={{0,1},{1,2},{2,3},{3,0},{4,5},{5,6},{6,7},{7,4},{8,9},{9,10},{10,1... | collective-permute-start | bytes 1179656 | tf_op jit(solution)/shard_map/ppermute | solution.py:240
  31.1 0.0 copy-start.2
  31.1 0.0 copy-start.4
  31.1 3.7 %collective-permute-start.2 = (bf16[64,1536]{1,0:T(8,128)(2,1)S(1)}, bf16[64,1536]{1,0:T(8,128)(2,1)S(1)}, u32[]{:S(2)}, u32[]{:S(2)}) collective-permute-start(bf16[64,1536]{1,0:T(8,128)(2,1)S(1)} %pad_maximum_fusion.1), channel_id=1, source_target_pairs={{0,2},{1,3},{2,0},{3,1},{4,6},{5,7},{6,4},{7,5},{8,10},{9,11},{10,... | collective-permute-start | bytes 589832 | tf_op jit(solution)/shard_map/ppermute | solution.py:240
  34.8 9.4 %collective-permute-done.2.refs_2_ = bf16[64,1536]{1,0:T(8,128)(2,1)S(1)} collective-permute-done((bf16[64,1536]{1,0:T(8,128)(2,1)S(1)}, bf16[64,1536]{1,0:T(8,128)(2,1)S(1)}, u32[]{:S(2)}, u32[]{:S(2)}) %collective-permute-start.2) | collective-permute-done | bytes 196640 | tf_op jit(solution)/shard_map/ppermute | solution.py:240
  44.3 1.7 %copy-done = bf16[1536,768]{1,0:T(8,128)(2,1)S(1)} copy-done((bf16[1536,768]{1,0:T(8,128)(2,1)S(1)}, bf16[1536,768]{1,0:T(8,128)(2,1)}, u32[]{:S(2)}) %copy-start) | copy-done | bytes 2359320
  45.9 0.9 shard_map.78
  46.8 5.6 %collective-permute-start.4 = (bf16[128,768]{1,0:T(8,128)(2,1)S(1)}, bf16[128,768]{1,0:T(8,128)(2,1)S(1)}, u32[]{:S(2)}, u32[]{:S(2)}) collective-permute-start(bf16[128,768]{1,0:T(8,128)(2,1)S(1)} %get-tuple-element.22), channel_id=1, source_target_pairs={{0,128},{128,0},{256,384},{384,256},{1,129},{129,1},{257,385},{385... | collective-permute-start | bytes 589832 | tf_op jit(solution)/shard_map/ppermute | solution.py:263
  52.5 1.0 %collective-permute-done.4 = bf16[128,768]{1,0:T(8,128)(2,1)S(1)} collective-permute-done((bf16[128,768]{1,0:T(8,128)(2,1)S(1)}, bf16[128,768]{1,0:T(8,128)(2,1)S(1)}, u32[]{:S(2)}, u32[]{:S(2)}) %collective-permute-start.4) | collective-permute-done | bytes 196640 | tf_op jit(solution)/shard_map/ppermute | solution.py:263
  53.6 4.4 %collective-permute-start.5 = (bf16[128,768]{1,0:T(8,128)(2,1)S(1)}, bf16[128,768]{1,0:T(8,128)(2,1)S(1)}, u32[]{:S(2)}, u32[]{:S(2)}) collective-permute-start(bf16[128,768]{1,0:T(8,128)(2,1)S(1)} %fusion), channel_id=1, source_target_pairs={{0,256},{128,384},{256,0},{384,128},{1,257},{129,385},{257,1},{385... | collective-permute-start | bytes 589832 | tf_op jit(solution)/shard_map/ppermute | solution.py:267
  57.9 1.0 shard_map.79.side_ref
  58.9 1.3 %shard_map.80 = bf16[4,8,160,128]{3,2,1,0:T(8,128)(2,1)} custom-call(bf16[16,120,128]{2,1,0:T(8,128)(2,1)S(1)} %all-to-all-done.got_ref, bf16[8,64,128]{2,1,0:T(8,128)(2,1)S(1)} %shard_map.79.side_ref), custom_call_target="tpu_custom_call" | custom-call | flops 1000000 | bytes 1933312 | tf_op jit(solution)/shard_map/pallas_call | solution.py:24
  60.2 2.9 %collective-permute-done.5 = bf16[128,768]{1,0:T(8,128)(2,1)S(1)} collective-permute-done((bf16[128,768]{1,0:T(8,128)(2,1)S(1)}, bf16[128,768]{1,0:T(8,128)(2,1)S(1)}, u32[]{:S(2)}, u32[]{:S(2)}) %collective-permute-start.5) | collective-permute-done | bytes 196640 | tf_op jit(solution)/shard_map/ppermute | solution.py:267
  63.1 0.1 add_convert_fusion.refs_0_
  63.2 5.4 %all-to-all-start.1 = ((bf16[32,160,128]{2,1,0:T(8,128)(2,1)}), bf16[32,160,128]{2,1,0:T(8,128)(2,1)S(1)}, u32[]{:S(2)}, u32[]{:S(2)}) async-start(bf16[32,160,128]{2,1,0:T(8,128)(2,1)} %bitcast), calls=%async_computation.1 | async-start | bytes 2621440 | tf_op jit(solution)/shard_map/all_to_all | solution.py:282
  68.6 4.8 %collective-permute-start.9 = (bf16[64,1536]{1,0:T(8,128)(2,1)S(1)}, bf16[64,1536]{1,0:T(8,128)(2,1)S(1)}, u32[]{:S(2)}, u32[]{:S(2)}) collective-permute-start(bf16[64,1536]{1,0:T(8,128)(2,1)S(1)} %pad_maximum_fusion.2), channel_id=1, source_target_pairs={{0,2},{1,3},{2,0},{3,1},{4,6},{5,7},{6,4},{7,5},{8,10},{9,11},{10,... | collective-permute-start | bytes 589832 | tf_op jit(solution)/shard_map/ppermute | solution.py:240
  73.4 2.6 %collective-permute-start.8 = (bf16[128,768]{1,0:T(8,128)(2,1)S(1)}, bf16[128,768]{1,0:T(8,128)(2,1)S(1)}, u32[]{:S(2)}, u32[]{:S(2)}) collective-permute-start(bf16[128,768]{1,0:T(8,128)(2,1)S(1)} %add_convert_fusion.refs_0_), channel_id=1, source_target_pairs={{0,120},{8,0},{16,8},{24,16},{32,24},{40,32},{48,40},{56,48},{64,5... | collective-permute-start | bytes 589832 | tf_op jit(solution)/shard_map/ppermute | solution.py:285
  76.0 2.7 %collective-permute-start.7 = (bf16[128,768]{1,0:T(8,128)(2,1)S(1)}, bf16[128,768]{1,0:T(8,128)(2,1)S(1)}, u32[]{:S(2)}, u32[]{:S(2)}) collective-permute-start(bf16[128,768]{1,0:T(8,128)(2,1)S(1)} %add_convert_fusion.refs_0_), channel_id=1, source_target_pairs={{0,8},{8,16},{16,24},{24,32},{32,40},{40,48},{48,56},{56,64},{64,7... | collective-permute-start | bytes 589832 | tf_op jit(solution)/shard_map/ppermute | solution.py:285
  78.7 5.2 %collective-permute-start.6 = (bf16[128,768]{1,0:T(8,128)(2,1)S(1)}, bf16[128,768]{1,0:T(8,128)(2,1)S(1)}, u32[]{:S(2)}, u32[]{:S(2)}) collective-permute-start(bf16[128,768]{1,0:T(8,128)(2,1)S(1)} %add_convert_fusion.refs_0_), channel_id=1, source_target_pairs={{0,16},{8,24},{16,32},{24,40},{32,48},{40,56},{48,64},{56,72},{64,... | collective-permute-start | bytes 589832 | tf_op jit(solution)/shard_map/ppermute | solution.py:285
  83.9 7.2 %collective-permute-done.9.refs_2_ = bf16[64,1536]{1,0:T(8,128)(2,1)S(1)} collective-permute-done((bf16[64,1536]{1,0:T(8,128)(2,1)S(1)}, bf16[64,1536]{1,0:T(8,128)(2,1)S(1)}, u32[]{:S(2)}, u32[]{:S(2)}) %collective-permute-start.9) | collective-permute-done | bytes 196640 | tf_op jit(solution)/shard_map/ppermute | solution.py:240
  91.1 5.4 %collective-permute-done.6.refs_1_ = bf16[128,768]{1,0:T(8,128)(2,1)S(1)} collective-permute-done((bf16[128,768]{1,0:T(8,128)(2,1)S(1)}, bf16[128,768]{1,0:T(8,128)(2,1)S(1)}, u32[]{:S(2)}, u32[]{:S(2)}) %collective-permute-start.6) | collective-permute-done | bytes 196640 | tf_op jit(solution)/shard_map/ppermute | solution.py:285
  96.6 0.5 shard_map.81
  97.0 3.7 %collective-permute-start.10 = (bf16[96,768]{1,0:T(8,128)(2,1)S(1)}, bf16[96,768]{1,0:T(8,128)(2,1)S(1)}, u32[]{:S(2)}, u32[]{:S(2)}) collective-permute-start(bf16[96,768]{1,0:T(8,128)(2,1)S(1)} %get-tuple-element.34), channel_id=1, source_target_pairs={{0,128},{128,0},{256,384},{384,256},{1,129},{129,1},{257,385},{385... | collective-permute-start | bytes 442376 | tf_op jit(solution)/shard_map/ppermute | solution.py:299
  100.8 1.4 %shard_map.82 = (f32[48,1536]{1,0:T(8,128)}, f32[48,1536]{1,0:T(8,128)}) custom-call(bf16[4,8,160,128]{3,2,1,0:T(8,128)(2,1)S(1)} %bitcast.3, bf16[128,1536]{1,0:T(8,128)(2,1)S(1)} %pad_maximum_fusion.refs_0_, bf16[128,1536]{1,0:T(8,128)(2,1)S(1)} %collective-permute-done.1.refs_1_, bf16[64,1536]{1,0:T(8,128)(2,1)S(1)} %collective-permute-done.9.refs_2_, ...), custom_call_target="tpu_custom_call" | custom-call | flops 201326592 | bytes 3276800 | tf_op jit(solution)/shard_map/pallas_call | solution.py:24
  102.2 0.7 convert_add_fusion.1
  (19 shorter events, 0.2 us)
Async XLA Ops:
  0.6 1.0 copy-start.1
  1.6 0.7 copy-start.3
  3.0 21.4 %collective-permute-start = (bf16[64,1536]{1,0:T(8,128)(2,1)S(1)}, bf16[64,1536]{1,0:T(8,128)(2,1)S(1)}, u32[]{:S(2)}, u32[]{:S(2)}) collective-permute-start(bf16[64,1536]{1,0:T(8,128)(2,1)S(1)} %shard_map.77.gy_ref), channel_id=1, source_target_pairs={{0,4},{1,5},{2,6},{3,7},{4,0},{5,1},{6,2},{7,3},{8,12},{9,13},{10,... | collective-permute-start | bytes 589832 | tf_op jit(solution)/shard_map/ppermute | solution.py:250
  9.8 43.8 %all-to-all-start = ((bf16[16,120,128]{2,1,0:T(8,128)(2,1)}), bf16[16,120,128]{2,1,0:T(8,128)(2,1)S(1)}, u32[]{:S(2)}, u32[]{:S(2)}) async-start(bf16[16,120,128]{2,1,0:T(8,128)(2,1)} %shard_map.76), calls=%async_computation | async-start | bytes 983040 | tf_op jit(solution)/shard_map/all_to_all | solution.py:237
  24.5 19.8 %collective-permute-start.3 = (bf16[128,1536]{1,0:T(8,128)(2,1)S(1)}, bf16[128,1536]{1,0:T(8,128)(2,1)S(1)}, u32[]{:S(2)}, u32[]{:S(2)}) collective-permute-start(bf16[128,1536]{1,0:T(8,128)(2,1)S(1)} %pad_maximum_fusion.refs_0_), channel_id=1, source_target_pairs={{0,3},{1,0},{2,1},{3,2},{4,7},{5,4},{6,5},{7,6},{8,11},{9,8},{10,9... | collective-permute-start | bytes 1179656 | tf_op jit(solution)/shard_map/ppermute | solution.py:240
  29.1 15.1 %collective-permute-start.1 = (bf16[128,1536]{1,0:T(8,128)(2,1)S(1)}, bf16[128,1536]{1,0:T(8,128)(2,1)S(1)}, u32[]{:S(2)}, u32[]{:S(2)}) collective-permute-start(bf16[128,1536]{1,0:T(8,128)(2,1)S(1)} %pad_maximum_fusion.refs_0_), channel_id=1, source_target_pairs={{0,1},{1,2},{2,3},{3,0},{4,5},{5,6},{6,7},{7,4},{8,9},{9,10},{10,1... | collective-permute-start | bytes 1179656 | tf_op jit(solution)/shard_map/ppermute | solution.py:240
  31.1 26.8 %copy-start.2 = (bf16[128,384]{1,0:T(8,128)(2,1)S(1)}, bf16[128,384]{1,0:T(8,128)(2,1)}, u32[]{:S(2)}) copy-start(bf16[128,384]{1,0:T(8,128)(2,1)} %x_ref.1) | copy-start | bytes 294916
  31.1 26.8 %copy-start.4 = (s32[32]{0:T(128)S(1)}, s32[32]{0:T(128)}, u32[]{:S(2)}) copy-start(s32[32]{0:T(128)} %picks.5) | copy-start | bytes 388
  31.1 13.1 %collective-permute-start.2 = (bf16[64,1536]{1,0:T(8,128)(2,1)S(1)}, bf16[64,1536]{1,0:T(8,128)(2,1)S(1)}, u32[]{:S(2)}, u32[]{:S(2)}) collective-permute-start(bf16[64,1536]{1,0:T(8,128)(2,1)S(1)} %pad_maximum_fusion.1), channel_id=1, source_target_pairs={{0,2},{1,3},{2,0},{3,1},{4,6},{5,7},{6,4},{7,5},{8,10},{9,11},{10,... | collective-permute-start | bytes 589832 | tf_op jit(solution)/shard_map/ppermute | solution.py:240
  44.3 1.7 %copy-start = (bf16[1536,768]{1,0:T(8,128)(2,1)S(1)}, bf16[1536,768]{1,0:T(8,128)(2,1)}, u32[]{:S(2)}) copy-start(bf16[1536,768]{1,0:T(8,128)(2,1)} %b_ref.1) | copy-start | bytes 7077892
  46.8 6.7 %collective-permute-start.4 = (bf16[128,768]{1,0:T(8,128)(2,1)S(1)}, bf16[128,768]{1,0:T(8,128)(2,1)S(1)}, u32[]{:S(2)}, u32[]{:S(2)}) collective-permute-start(bf16[128,768]{1,0:T(8,128)(2,1)S(1)} %get-tuple-element.22), channel_id=1, source_target_pairs={{0,128},{128,0},{256,384},{384,256},{1,129},{129,1},{257,385},{385... | collective-permute-start | bytes 589832 | tf_op jit(solution)/shard_map/ppermute | solution.py:263
  53.6 9.5 %collective-permute-start.5 = (bf16[128,768]{1,0:T(8,128)(2,1)S(1)}, bf16[128,768]{1,0:T(8,128)(2,1)S(1)}, u32[]{:S(2)}, u32[]{:S(2)}) collective-permute-start(bf16[128,768]{1,0:T(8,128)(2,1)S(1)} %fusion), channel_id=1, source_target_pairs={{0,256},{128,384},{256,0},{384,128},{1,257},{129,385},{257,1},{385... | collective-permute-start | bytes 589832 | tf_op jit(solution)/shard_map/ppermute | solution.py:267
  63.2 33.4 %all-to-all-start.1 = ((bf16[32,160,128]{2,1,0:T(8,128)(2,1)}), bf16[32,160,128]{2,1,0:T(8,128)(2,1)S(1)}, u32[]{:S(2)}, u32[]{:S(2)}) async-start(bf16[32,160,128]{2,1,0:T(8,128)(2,1)} %bitcast), calls=%async_computation.1 | async-start | bytes 2621440 | tf_op jit(solution)/shard_map/all_to_all | solution.py:282
  68.6 22.5 %collective-permute-start.9 = (bf16[64,1536]{1,0:T(8,128)(2,1)S(1)}, bf16[64,1536]{1,0:T(8,128)(2,1)S(1)}, u32[]{:S(2)}, u32[]{:S(2)}) collective-permute-start(bf16[64,1536]{1,0:T(8,128)(2,1)S(1)} %pad_maximum_fusion.2), channel_id=1, source_target_pairs={{0,2},{1,3},{2,0},{3,1},{4,6},{5,7},{6,4},{7,5},{8,10},{9,11},{10,... | collective-permute-start | bytes 589832 | tf_op jit(solution)/shard_map/ppermute | solution.py:240
  73.4 17.7 %collective-permute-start.8 = (bf16[128,768]{1,0:T(8,128)(2,1)S(1)}, bf16[128,768]{1,0:T(8,128)(2,1)S(1)}, u32[]{:S(2)}, u32[]{:S(2)}) collective-permute-start(bf16[128,768]{1,0:T(8,128)(2,1)S(1)} %add_convert_fusion.refs_0_), channel_id=1, source_target_pairs={{0,120},{8,0},{16,8},{24,16},{32,24},{40,32},{48,40},{56,48},{64,5... | collective-permute-start | bytes 589832 | tf_op jit(solution)/shard_map/ppermute | solution.py:285
  76.0 15.1 %collective-permute-start.7 = (bf16[128,768]{1,0:T(8,128)(2,1)S(1)}, bf16[128,768]{1,0:T(8,128)(2,1)S(1)}, u32[]{:S(2)}, u32[]{:S(2)}) collective-permute-start(bf16[128,768]{1,0:T(8,128)(2,1)S(1)} %add_convert_fusion.refs_0_), channel_id=1, source_target_pairs={{0,8},{8,16},{16,24},{24,32},{32,40},{40,48},{48,56},{56,64},{64,7... | collective-permute-start | bytes 589832 | tf_op jit(solution)/shard_map/ppermute | solution.py:285
  78.7 17.9 %collective-permute-start.6 = (bf16[128,768]{1,0:T(8,128)(2,1)S(1)}, bf16[128,768]{1,0:T(8,128)(2,1)S(1)}, u32[]{:S(2)}, u32[]{:S(2)}) collective-permute-start(bf16[128,768]{1,0:T(8,128)(2,1)S(1)} %add_convert_fusion.refs_0_), channel_id=1, source_target_pairs={{0,16},{8,24},{16,32},{24,40},{32,48},{40,56},{48,64},{56,72},{64,... | collective-permute-start | bytes 589832 | tf_op jit(solution)/shard_map/ppermute | solution.py:285
  97.0 5.2 %collective-permute-start.10 = (bf16[96,768]{1,0:T(8,128)(2,1)S(1)}, bf16[96,768]{1,0:T(8,128)(2,1)S(1)}, u32[]{:S(2)}, u32[]{:S(2)}) collective-permute-start(bf16[96,768]{1,0:T(8,128)(2,1)S(1)} %get-tuple-element.34), channel_id=1, source_target_pairs={{0,128},{128,0},{256,384},{384,256},{1,129},{129,1},{257,385},{385... | collective-permute-start | bytes 442376 | tf_op jit(solution)/shard_map/ppermute | solution.py:299

commit v18 on v16

--- a/solution.py
+++ b/solution.py
@@ -116,12 +116,6 @@
         out_ref[c] = block.astype(BF)
 
 
-def rows_of(block, begin, count):
-    step = block.shape[0] // 2
-    begin = begin if step > count else 0
-    return [block[at : at + count, :] for at in (begin, step + begin)]
-
-
 def right_kernel(b_hbm, *refs):
     blocks, keep_ref, give_ref, held, b_ref, sems = refs[:-5], *refs[-5:]
     n_blk, unused, size, width = held.shape
@@ -134,8 +128,7 @@
     ]
     for copy in copies:
         copy.start()
-    rows = [piece for block in blocks for piece in rows_of(block, 0, 2 * size)]
-    rows = jnp.concatenate(rows, axis=0)
+    rows = jnp.concatenate([block[: 4 * size, :] for block in blocks], axis=0)
     term = None
     for p in range(parts):
         copies[p].wait()
@@ -209,7 +202,7 @@
         act_ref[16 * k : 16 * (k + 1), :] = term[LANES - 16 :] * scale
     owner = lax.axis_index("row") // 4
     sides = [got_ref[owner, source_of(k), : 2 * samp, :] for k in range(n_col)]
-    rights = [piece for block in blocks for piece in rows_of(block, samp, samp)]
+    rights = [block[block.shape[0] - 2 * samp :, :] for block in blocks]
     right = jnp.concatenate(rights, axis=0)
     left = jnp.concatenate([side[:samp] for side in sides], axis=0)
     term = lax.dot_general(left, right, FIRST, preferred_element_type=F32)
@@ -260,13 +253,16 @@
         (sample_rows, cotangent),
         [shape((2 * size + samp, feat_grp), BF)],
         2 * 64 * tok * feat_grp,
+        limit=56,
     )[0]
     beside = lax.ppermute(picked, "col", [(i, (i + 4) % n_col) for i in range(n_col)])
     cut = 2 * size
-    pair = jnp.concatenate([picked, beside], axis=0)
-    rows = jnp.concatenate([picked[:cut], beside[:cut]], axis=0)
+    kinds = (picked[:cut], beside[:cut], picked[cut:], beside[cut:])
+    pair = jnp.concatenate(kinds, axis=0)
     near = {k: along_y(pair, k) for k in (1, 3)}
-    pairs = [pair, near[1], along_y(rows, 2), near[3]]
+    far_rows = along_y(near[1][: 2 * cut], 1)
+    far_samples = along_y(near[3][2 * cut :], 3)
+    pairs = [pair, near[1], far_rows, near[3]]
     keep, give = call(
         right_kernel,
         (grad_inverse, *pairs),
@@ -282,15 +278,9 @@
     taken = lax.ppermute(give, "grp", [(i, i ^ 1) for i in range(n_grp)])
     some = keep.astype(F32) + taken.astype(F32)
     give = some.astype(BF)
-    first, give = lax.optimization_barrier((first, give))
+    first, give, far_samples = lax.optimization_barrier((first, give, far_samples))
     taken = lax.ppermute(give, "grp", [(i, i ^ 2) for i in range(n_grp)])
     right = (some + taken.astype(F32)).astype(BF)
-    rights = [right] + [
-        lax.ppermute(right, "row", [(i, (i + j) % n_row) for i in range(n_row)])
-        for j in SHIFTS[1:]
-    ]
-    unused, picked_y, beside_y = lax.optimization_barrier((right, picked[cut:], beside[cut:]))
-    far = along_y(jnp.concatenate([picked_y, beside_y], axis=0), 2)
     side = call(
         side_kernel,
         (sample_rows, tokens_in, picked),
@@ -303,10 +293,13 @@
         [shape((n_grp, n_col, size * spread + strip * n_row // n_grp, LANES), BF)],
         1000000,
     )[0]
+    send, right = lax.optimization_barrier((send, right))
     got = lax.all_to_all(send.reshape((n_grp * n_col,) + send.shape[2:]), ("grp", "col"), 0, 0)
     got = got.reshape(send.shape)
-
-    rights, far = lax.optimization_barrier((rights, far))
+    rights = [right] + [
+        lax.ppermute(right, "row", [(i, (i + j) % n_row) for i in range(n_row)])
+        for j in SHIFTS[1:]
+    ]
     term, give = call(
         final_kernel,
         (got, *rights),
@@ -319,7 +312,7 @@
     got, unused = lax.optimization_barrier((got, give))
     act_cov, grad_cov = call(
         factor_kernel,
-        (got, pair, near[1], far, near[3]),
+        (got, pair, near[1], far_samples, near[3]),
         [shape((tile, feat_grp), F32)] * 2,
         4 * LANES * samp * n_col * feat_grp,
     )

time: 111 us -> 106 us (0.955)
  starting transfers between devices: 65.8 us -> 59 us
  local copies, waits for them, and re-layouts: 0.05 us -> 1.74 us
  waiting for transfers between devices: 32.3 us -> 30.8 us
    ppermute x1, waiting for transfers between devices: 17.2 us -> 2.4 us  [body(): taken = lax.ppermute(give, 'grp', [(i, i ^ 2) for i in range(n_grp)])]
    ppermute x4, waiting for transfers between devices: 6.98 us -> 18.2 us  [along_y(): lax.ppermute(block, 'col', [(i, i - i % 4 + (i + k) % 4) for i in range(n...]
    ppermute x3, waiting for transfers between devices: 3.76 us -> 10.1 us  [body(): lax.ppermute(right, 'row', [(i, (i + j) % n_row) for i in range(n_row)])]
    ppermute x1, waiting for transfers between devices: 4.2 us -> 0.01 us  [body(): lax.ppermute(picked, 'col', [(i, (i + 4) % n_col) for i in range(n_col)])]
    ppermute x4, starting transfers between devices: 14.8 us -> 10.8 us  [along_y(): lax.ppermute(block, 'col', [(i, i - i % 4 + (i + k) % 4) for i in range(n...]
    unnamed x8, local copies, waits for them, and re-layouts: 0.02 us -> 1.68 us
  transfers between devices with their start and end apart: 13 -> 13, of which waited for: 5 -> 6; matrix products, arithmetic and copies ran while one was open for 0% -> 0% of each run, Pallas kernels for 5% -> 9%
where the time goes in v18:
time: 106 us; the launch traced here: 105 us
  starting transfers between devices  59 us (56%)
  waiting for transfers between devices  30.8 us (29%)
  Pallas kernels  11.5 us (11%)
  local copies, waits for them, and re-layouts  1.74 us (2%)
    ppermute x4, waiting for transfers between devices, along_y(): lax.ppermute(block, 'col', [(i, i - i % 4 + (i + k) % 4) for i in range(n...  18.2 us
    all_to_all x1, starting transfers between devices, body(): first = lax.all_to_all(payload, 'row', 0, 0)  14.9 us
    pallas_call x7, Pallas kernels, call(): pl.pallas_call(kernel, out_shape=outs, in_specs=places, out_specs=[VMEM]...  11.5 us
    ppermute x4, starting transfers between devices, along_y(): lax.ppermute(block, 'col', [(i, i - i % 4 + (i + k) % 4) for i in range(n...  10.8 us
    ppermute x3, waiting for transfers between devices, body(): lax.ppermute(right, 'row', [(i, (i + j) % n_row) for i in range(n_row)])  10.1 us
    ppermute x3, starting transfers between devices, body(): lax.ppermute(right, 'row', [(i, (i + j) % n_row) for i in range(n_row)])  9.45 us
    ppermute x2, starting transfers between devices, body(): taken = lax.ppermute(give, 'grp', [(i, i ^ 1) for i in range(n_grp)])  8.46 us
    all_to_all x1, starting transfers between devices, body(): lax.all_to_all(send.reshape((n_grp * n_col,) + send.shape[2:]), ('grp', '...  7.02 us
  transfers between devices with their start and end apart: 13, of which 6 were waited for; matrix products, arithmetic and copies ran while one was open for 0% of the time, Pallas kernels for 9%

profile of v18, /device:TPU:1, one launch (start us, length us, event | category | flops | bytes accessed | tf_op | source)
XLA Modules:
  0.0 104.8 jit_solution(12938233031314719078)
XLA Ops:
  0.6 1.9 %shard_map.77.gy_ref = bf16[64,1536]{1,0:T(8,128)(2,1)} custom-call(s32[32]{0:T(128)} %picks.5, bf16[128,1536]{1,0:T(8,128)(2,1)} %g_ref.1), custom_call_target="tpu_custom_call" | custom-call | flops 25165824 | bytes 589952 | tf_op jit(solution)/shard_map/pallas_call | solution.py:24
  2.5 4.1 %collective-permute-start = (bf16[64,1536]{1,0:T(8,128)(2,1)}, bf16[64,1536]{1,0:T(8,128)(2,1)S(1)}, u32[]{:S(2)}, u32[]{:S(2)}) collective-permute-start(bf16[64,1536]{1,0:T(8,128)(2,1)} %shard_map.77.gy_ref), channel_id=1, source_target_pairs={{0,4},{1,5},{2,6},{3,7},{4,0},{5,1},{6,2},{7,3},{8,12},{9,13},{10,... | collective-permute-start | bytes 589832 | tf_op jit(solution)/shard_map/ppermute | solution.py:258
  6.6 3.6 %shard_map.76 = bf16[16,120,128]{2,1,0:T(8,128)(2,1)} custom-call(s32[32]{0:T(128)} %picks.5, bf16[128,384]{1,0:T(8,128)(2,1)} %x_ref.1, bf16[1536,384]{1,0:T(8,128)(2,1)} %a_hbm.1), custom_call_target="tpu_custom_call" | custom-call | flops 150994944 | bytes 1769600 | tf_op jit(solution)/shard_map/pallas_call | solution.py:24
  10.2 14.9 %all-to-all-start = ((bf16[16,120,128]{2,1,0:T(8,128)(2,1)}), bf16[16,120,128]{2,1,0:T(8,128)(2,1)S(1)}, u32[]{:S(2)}, u32[]{:S(2)}) async-start(bf16[16,120,128]{2,1,0:T(8,128)(2,1)} %shard_map.76), calls=%async_computation | async-start | bytes 983040 | tf_op jit(solution)/shard_map/all_to_all | solution.py:244
  25.2 0.0 collective-permute-done
  25.2 3.2 %collective-permute-start.1 = (bf16[128,1536]{1,0:T(8,128)(2,1)S(1)}, bf16[128,1536]{1,0:T(8,128)(2,1)S(1)}, u32[]{:S(2)}, u32[]{:S(2)}) collective-permute-start(bf16[128,1536]{1,0:T(8,128)(2,1)S(1)} %pad_maximum_fusion.refs_0_), channel_id=1, source_target_pairs={{0,1},{1,2},{2,3},{3,0},{4,5},{5,6},{6,7},{7,4},{8,9},{9,10},{10,1... | collective-permute-start | bytes 1179656 | tf_op jit(solution)/shard_map/ppermute | solution.py:247
  28.4 3.4 %collective-permute-start.3 = (bf16[128,1536]{1,0:T(8,128)(2,1)S(1)}, bf16[128,1536]{1,0:T(8,128)(2,1)S(1)}, u32[]{:S(2)}, u32[]{:S(2)}) collective-permute-start(bf16[128,1536]{1,0:T(8,128)(2,1)S(1)} %pad_maximum_fusion.refs_0_), channel_id=1, source_target_pairs={{0,3},{1,0},{2,1},{3,2},{4,7},{5,4},{6,5},{7,6},{8,11},{9,8},{10,9... | collective-permute-start | bytes 1179656 | tf_op jit(solution)/shard_map/ppermute | solution.py:247
  31.8 6.0 %collective-permute-done.1.refs_1_ = bf16[128,1536]{1,0:T(8,128)(2,1)S(1)} collective-permute-done((bf16[128,1536]{1,0:T(8,128)(2,1)S(1)}, bf16[128,1536]{1,0:T(8,128)(2,1)S(1)}, u32[]{:S(2)}, u32[]{:S(2)}) %collective-permute-start.1) | collective-permute-done | bytes 393248 | tf_op jit(solution)/shard_map/ppermute | solution.py:247
  37.9 2.1 %collective-permute-start.2 = (bf16[64,1536]{1,0:T(8,128)(2,1)S(1)}, bf16[64,1536]{1,0:T(8,128)(2,1)S(1)}, u32[]{:S(2)}, u32[]{:S(2)}) collective-permute-start(bf16[64,1536]{1,0:T(8,128)(2,1)S(1)} %slice.28), channel_id=1, source_target_pairs={{0,1},{1,2},{2,3},{3,0},{4,5},{5,6},{6,7},{7,4},{8,9},{9,10},{10,1... | collective-permute-start | bytes 589832 | tf_op jit(solution)/shard_map/ppermute | solution.py:247
  40.0 6.0 %collective-permute-done.2.refs_2_ = bf16[64,1536]{1,0:T(8,128)(2,1)S(1)} collective-permute-done((bf16[64,1536]{1,0:T(8,128)(2,1)S(1)}, bf16[64,1536]{1,0:T(8,128)(2,1)S(1)}, u32[]{:S(2)}, u32[]{:S(2)}) %collective-permute-start.2) | collective-permute-done | bytes 196640 | tf_op jit(solution)/shard_map/ppermute | solution.py:247
  45.9 1.7 %copy-done = bf16[1536,768]{1,0:T(8,128)(2,1)S(1)} copy-done((bf16[1536,768]{1,0:T(8,128)(2,1)S(1)}, bf16[1536,768]{1,0:T(8,128)(2,1)}, u32[]{:S(2)}) %copy-start) | copy-done | bytes 2359320
  47.6 1.9 %shard_map.78 = (bf16[128,768]{1,0:T(8,128)(2,1)S(1)}, bf16[128,768]{1,0:T(8,128)(2,1)S(1)}) custom-call(bf16[1536,768]{1,0:T(8,128)(2,1)S(1)} %copy-done, bf16[128,1536]{1,0:T(8,128)(2,1)S(1)} %pad_maximum_fusion.refs_0_, bf16[128,1536]{1,0:T(8,128)(2,1)S(1)} %collective-permute-done.1.refs_1_, bf16[64,1536]{1,0:T(8,128)(2,1)S(1)} %collective-permute-done.2.refs_2_, ...), custom_call_target="tpu_custom_call" | custom-call | flops 603979776 | bytes 4128768 | tf_op jit(solution)/shard_map/pallas_call | solution.py:24
  49.5 4.8 %collective-permute-start.4 = (bf16[128,768]{1,0:T(8,128)(2,1)S(1)}, bf16[128,768]{1,0:T(8,128)(2,1)S(1)}, u32[]{:S(2)}, u32[]{:S(2)}) collective-permute-start(bf16[128,768]{1,0:T(8,128)(2,1)S(1)} %get-tuple-element.16), channel_id=1, source_target_pairs={{0,128},{128,0},{256,384},{384,256},{1,129},{129,1},{257,385},{385... | collective-permute-start | bytes 589832 | tf_op jit(solution)/shard_map/ppermute | solution.py:278
  54.4 2.2 %collective-permute-start.5 = (bf16[64,1536]{1,0:T(8,128)(2,1)S(1)}, bf16[64,1536]{1,0:T(8,128)(2,1)S(1)}, u32[]{:S(2)}, u32[]{:S(2)}) collective-permute-start(bf16[64,1536]{1,0:T(8,128)(2,1)S(1)} %slice.29), channel_id=1, source_target_pairs={{0,3},{1,0},{2,1},{3,2},{4,7},{5,4},{6,5},{7,6},{8,11},{9,8},{10,9... | collective-permute-start | bytes 589832 | tf_op jit(solution)/shard_map/ppermute | solution.py:247
  56.6 0.0 collective-permute-done.4
  56.6 6.2 %collective-permute-done.5.refs_2_ = bf16[64,1536]{1,0:T(8,128)(2,1)S(1)} collective-permute-done((bf16[64,1536]{1,0:T(8,128)(2,1)S(1)}, bf16[64,1536]{1,0:T(8,128)(2,1)S(1)}, u32[]{:S(2)}, u32[]{:S(2)}) %collective-permute-start.5) | collective-permute-done | bytes 196640 | tf_op jit(solution)/shard_map/ppermute | solution.py:247
  62.8 4.3 %collective-permute-start.6 = (bf16[128,768]{1,0:T(8,128)(2,1)S(1)}, bf16[128,768]{1,0:T(8,128)(2,1)S(1)}, u32[]{:S(2)}, u32[]{:S(2)}) collective-permute-start(bf16[128,768]{1,0:T(8,128)(2,1)S(1)} %fusion), channel_id=1, source_target_pairs={{0,256},{128,384},{256,0},{384,128},{1,257},{129,385},{257,1},{385... | collective-permute-start | bytes 589832 | tf_op jit(solution)/shard_map/ppermute | solution.py:282
  67.2 1.0 shard_map.79.side_ref
  68.1 1.3 %shard_map.80 = bf16[4,8,160,128]{3,2,1,0:T(8,128)(2,1)} custom-call(bf16[16,120,128]{2,1,0:T(8,128)(2,1)S(1)} %all-to-all-done.got_ref, bf16[8,64,128]{2,1,0:T(8,128)(2,1)S(1)} %shard_map.79.side_ref), custom_call_target="tpu_custom_call" | custom-call | flops 1000000 | bytes 1933312 | tf_op jit(solution)/shard_map/pallas_call | solution.py:24
  69.4 2.4 %collective-permute-done.6 = bf16[128,768]{1,0:T(8,128)(2,1)S(1)} collective-permute-done((bf16[128,768]{1,0:T(8,128)(2,1)S(1)}, bf16[128,768]{1,0:T(8,128)(2,1)S(1)}, u32[]{:S(2)}, u32[]{:S(2)}) %collective-permute-start.6) | collective-permute-done | bytes 196640 | tf_op jit(solution)/shard_map/ppermute | solution.py:282
  71.8 0.1 add_convert_fusion.refs_0_
  71.9 7.0 %all-to-all-start.1 = ((bf16[32,160,128]{2,1,0:T(8,128)(2,1)}), bf16[32,160,128]{2,1,0:T(8,128)(2,1)S(1)}, u32[]{:S(2)}, u32[]{:S(2)}) async-start(bf16[32,160,128]{2,1,0:T(8,128)(2,1)} %bitcast), calls=%async_computation.1 | async-start | bytes 2621440 | tf_op jit(solution)/shard_map/all_to_all | solution.py:297
  78.9 4.5 %collective-permute-start.9 = (bf16[128,768]{1,0:T(8,128)(2,1)S(1)}, bf16[128,768]{1,0:T(8,128)(2,1)S(1)}, u32[]{:S(2)}, u32[]{:S(2)}) collective-permute-start(bf16[128,768]{1,0:T(8,128)(2,1)S(1)} %add_convert_fusion.refs_0_), channel_id=1, source_target_pairs={{0,120},{8,0},{16,8},{24,16},{32,24},{40,32},{48,40},{56,48},{64,5... | collective-permute-start | bytes 589832 | tf_op jit(solution)/shard_map/ppermute | solution.py:300
  83.4 1.9 %collective-permute-start.8 = (bf16[128,768]{1,0:T(8,128)(2,1)S(1)}, bf16[128,768]{1,0:T(8,128)(2,1)S(1)}, u32[]{:S(2)}, u32[]{:S(2)}) collective-permute-start(bf16[128,768]{1,0:T(8,128)(2,1)S(1)} %add_convert_fusion.refs_0_), channel_id=1, source_target_pairs={{0,8},{8,16},{16,24},{24,32},{32,40},{40,48},{48,56},{56,64},{64,7... | collective-permute-start | bytes 589832 | tf_op jit(solution)/shard_map/ppermute | solution.py:300
  85.4 3.0 %collective-permute-start.7 = (bf16[128,768]{1,0:T(8,128)(2,1)S(1)}, bf16[128,768]{1,0:T(8,128)(2,1)S(1)}, u32[]{:S(2)}, u32[]{:S(2)}) collective-permute-start(bf16[128,768]{1,0:T(8,128)(2,1)S(1)} %add_convert_fusion.refs_0_), channel_id=1, source_target_pairs={{0,16},{8,24},{16,32},{24,40},{32,48},{40,56},{48,64},{56,72},{64,... | collective-permute-start | bytes 589832 | tf_op jit(solution)/shard_map/ppermute | solution.py:300
  88.4 0.0 collective-permute-done.9.refs_3_
  88.4 4.4 %collective-permute-done.8.refs_2_ = bf16[128,768]{1,0:T(8,128)(2,1)S(1)} collective-permute-done((bf16[128,768]{1,0:T(8,128)(2,1)S(1)}, bf16[128,768]{1,0:T(8,128)(2,1)S(1)}, u32[]{:S(2)}, u32[]{:S(2)}) %collective-permute-start.8) | collective-permute-done | bytes 196640 | tf_op jit(solution)/shard_map/ppermute | solution.py:300
  92.8 5.8 %collective-permute-done.7.refs_1_ = bf16[128,768]{1,0:T(8,128)(2,1)S(1)} collective-permute-done((bf16[128,768]{1,0:T(8,128)(2,1)S(1)}, bf16[128,768]{1,0:T(8,128)(2,1)S(1)}, u32[]{:S(2)}, u32[]{:S(2)}) %collective-permute-start.7) | collective-permute-done | bytes 196640 | tf_op jit(solution)/shard_map/ppermute | solution.py:300
  98.6 0.5 shard_map.81
  99.0 3.6 %collective-permute-start.10 = (bf16[96,768]{1,0:T(8,128)(2,1)S(1)}, bf16[96,768]{1,0:T(8,128)(2,1)S(1)}, u32[]{:S(2)}, u32[]{:S(2)}) collective-permute-start(bf16[96,768]{1,0:T(8,128)(2,1)S(1)} %get-tuple-element.22), channel_id=1, source_target_pairs={{0,128},{128,0},{256,384},{384,256},{1,129},{129,1},{257,385},{385... | collective-permute-start | bytes 442376 | tf_op jit(solution)/shard_map/ppermute | solution.py:310
  102.7 1.4 %shard_map.82 = (f32[48,1536]{1,0:T(8,128)}, f32[48,1536]{1,0:T(8,128)}) custom-call(bf16[4,8,160,128]{3,2,1,0:T(8,128)(2,1)S(1)} %bitcast.3, bf16[128,1536]{1,0:T(8,128)(2,1)S(1)} %pad_maximum_fusion.refs_0_, bf16[128,1536]{1,0:T(8,128)(2,1)S(1)} %collective-permute-done.1.refs_1_, bf16[64,1536]{1,0:T(8,128)(2,1)S(1)} %collective-permute-done.5.refs_2_, ...), custom_call_target="tpu_custom_call" | custom-call | flops 201326592 | bytes 3276800 | tf_op jit(solution)/shard_map/pallas_call | solution.py:24
  104.1 0.7 convert_add_fusion.1
  (17 shorter events, 0.2 us)
Async XLA Ops:
  2.5 22.6 %copy-start.1 = (bf16[64,1536]{1,0:T(8,128)(2,1)S(1)}, bf16[64,1536]{1,0:T(8,128)(2,1)}, u32[]{:S(2)}) copy-start(bf16[64,1536]{1,0:T(8,128)(2,1)} %shard_map.77.gy_ref) | copy-start | bytes 589828
  2.5 22.6 %collective-permute-start = (bf16[64,1536]{1,0:T(8,128)(2,1)}, bf16[64,1536]{1,0:T(8,128)(2,1)S(1)}, u32[]{:S(2)}, u32[]{:S(2)}) collective-permute-start(bf16[64,1536]{1,0:T(8,128)(2,1)} %shard_map.77.gy_ref), channel_id=1, source_target_pairs={{0,4},{1,5},{2,6},{3,7},{4,0},{5,1},{6,2},{7,3},{8,12},{9,13},{10,... | collective-permute-start | bytes 589832 | tf_op jit(solution)/shard_map/ppermute | solution.py:258
  10.2 52.6 %all-to-all-start = ((bf16[16,120,128]{2,1,0:T(8,128)(2,1)}), bf16[16,120,128]{2,1,0:T(8,128)(2,1)S(1)}, u32[]{:S(2)}, u32[]{:S(2)}) async-start(bf16[16,120,128]{2,1,0:T(8,128)(2,1)} %shard_map.76), calls=%async_computation | async-start | bytes 983040 | tf_op jit(solution)/shard_map/all_to_all | solution.py:244
  25.2 12.6 %collective-permute-start.1 = (bf16[128,1536]{1,0:T(8,128)(2,1)S(1)}, bf16[128,1536]{1,0:T(8,128)(2,1)S(1)}, u32[]{:S(2)}, u32[]{:S(2)}) collective-permute-start(bf16[128,1536]{1,0:T(8,128)(2,1)S(1)} %pad_maximum_fusion.refs_0_), channel_id=1, source_target_pairs={{0,1},{1,2},{2,3},{3,0},{4,5},{5,6},{6,7},{7,4},{8,9},{9,10},{10,1... | collective-permute-start | bytes 1179656 | tf_op jit(solution)/shard_map/ppermute | solution.py:247
  28.4 11.5 %collective-permute-start.3 = (bf16[128,1536]{1,0:T(8,128)(2,1)S(1)}, bf16[128,1536]{1,0:T(8,128)(2,1)S(1)}, u32[]{:S(2)}, u32[]{:S(2)}) collective-permute-start(bf16[128,1536]{1,0:T(8,128)(2,1)S(1)} %pad_maximum_fusion.refs_0_), channel_id=1, source_target_pairs={{0,3},{1,0},{2,1},{3,2},{4,7},{5,4},{6,5},{7,6},{8,11},{9,8},{10,9... | collective-permute-start | bytes 1179656 | tf_op jit(solution)/shard_map/ppermute | solution.py:247
  37.9 29.3 %copy-start.2 = (bf16[128,384]{1,0:T(8,128)(2,1)S(1)}, bf16[128,384]{1,0:T(8,128)(2,1)}, u32[]{:S(2)}) copy-start(bf16[128,384]{1,0:T(8,128)(2,1)} %x_ref.1) | copy-start | bytes 294916
  37.9 29.3 %copy-start.3 = (s32[32]{0:T(128)S(1)}, s32[32]{0:T(128)}, u32[]{:S(2)}) copy-start(s32[32]{0:T(128)} %picks.5) | copy-start | bytes 388
  37.9 8.1 %collective-permute-start.2 = (bf16[64,1536]{1,0:T(8,128)(2,1)S(1)}, bf16[64,1536]{1,0:T(8,128)(2,1)S(1)}, u32[]{:S(2)}, u32[]{:S(2)}) collective-permute-start(bf16[64,1536]{1,0:T(8,128)(2,1)S(1)} %slice.28), channel_id=1, source_target_pairs={{0,1},{1,2},{2,3},{3,0},{4,5},{5,6},{6,7},{7,4},{8,9},{9,10},{10,1... | collective-permute-start | bytes 589832 | tf_op jit(solution)/shard_map/ppermute | solution.py:247
  45.9 1.7 %copy-start = (bf16[1536,768]{1,0:T(8,128)(2,1)S(1)}, bf16[1536,768]{1,0:T(8,128)(2,1)}, u32[]{:S(2)}) copy-start(bf16[1536,768]{1,0:T(8,128)(2,1)} %b_hbm.1) | copy-start | bytes 7077892
  49.5 7.0 %collective-permute-start.4 = (bf16[128,768]{1,0:T(8,128)(2,1)S(1)}, bf16[128,768]{1,0:T(8,128)(2,1)S(1)}, u32[]{:S(2)}, u32[]{:S(2)}) collective-permute-start(bf16[128,768]{1,0:T(8,128)(2,1)S(1)} %get-tuple-element.16), channel_id=1, source_target_pairs={{0,128},{128,0},{256,384},{384,256},{1,129},{129,1},{257,385},{385... | collective-permute-start | bytes 589832 | tf_op jit(solution)/shard_map/ppermute | solution.py:278
  54.4 8.4 %collective-permute-start.5 = (bf16[64,1536]{1,0:T(8,128)(2,1)S(1)}, bf16[64,1536]{1,0:T(8,128)(2,1)S(1)}, u32[]{:S(2)}, u32[]{:S(2)}) collective-permute-start(bf16[64,1536]{1,0:T(8,128)(2,1)S(1)} %slice.29), channel_id=1, source_target_pairs={{0,3},{1,0},{2,1},{3,2},{4,7},{5,4},{6,5},{7,6},{8,11},{9,8},{10,9... | collective-permute-start | bytes 589832 | tf_op jit(solution)/shard_map/ppermute | solution.py:247
  62.8 9.0 %collective-permute-start.6 = (bf16[128,768]{1,0:T(8,128)(2,1)S(1)}, bf16[128,768]{1,0:T(8,128)(2,1)S(1)}, u32[]{:S(2)}, u32[]{:S(2)}) collective-permute-start(bf16[128,768]{1,0:T(8,128)(2,1)S(1)} %fusion), channel_id=1, source_target_pairs={{0,256},{128,384},{256,0},{384,128},{1,257},{129,385},{257,1},{385... | collective-permute-start | bytes 589832 | tf_op jit(solution)/shard_map/ppermute | solution.py:282
  71.9 26.7 %all-to-all-start.1 = ((bf16[32,160,128]{2,1,0:T(8,128)(2,1)}), bf16[32,160,128]{2,1,0:T(8,128)(2,1)S(1)}, u32[]{:S(2)}, u32[]{:S(2)}) async-start(bf16[32,160,128]{2,1,0:T(8,128)(2,1)} %bitcast), calls=%async_computation.1 | async-start | bytes 2621440 | tf_op jit(solution)/shard_map/all_to_all | solution.py:297
  78.9 9.5 %collective-permute-start.9 = (bf16[128,768]{1,0:T(8,128)(2,1)S(1)}, bf16[128,768]{1,0:T(8,128)(2,1)S(1)}, u32[]{:S(2)}, u32[]{:S(2)}) collective-permute-start(bf16[128,768]{1,0:T(8,128)(2,1)S(1)} %add_convert_fusion.refs_0_), channel_id=1, source_target_pairs={{0,120},{8,0},{16,8},{24,16},{32,24},{40,32},{48,40},{56,48},{64,5... | collective-permute-start | bytes 589832 | tf_op jit(solution)/shard_map/ppermute | solution.py:300
  83.4 9.4 %collective-permute-start.8 = (bf16[128,768]{1,0:T(8,128)(2,1)S(1)}, bf16[128,768]{1,0:T(8,128)(2,1)S(1)}, u32[]{:S(2)}, u32[]{:S(2)}) collective-permute-start(bf16[128,768]{1,0:T(8,128)(2,1)S(1)} %add_convert_fusion.refs_0_), channel_id=1, source_target_pairs={{0,8},{8,16},{16,24},{24,32},{32,40},{40,48},{48,56},{56,64},{64,7... | collective-permute-start | bytes 589832 | tf_op jit(solution)/shard_map/ppermute | solution.py:300
  85.4 13.2 %collective-permute-start.7 = (bf16[128,768]{1,0:T(8,128)(2,1)S(1)}, bf16[128,768]{1,0:T(8,128)(2,1)S(1)}, u32[]{:S(2)}, u32[]{:S(2)}) collective-permute-start(bf16[128,768]{1,0:T(8,128)(2,1)S(1)} %add_convert_fusion.refs_0_), channel_id=1, source_target_pairs={{0,16},{8,24},{16,32},{24,40},{32,48},{40,56},{48,64},{56,72},{64,... | collective-permute-start | bytes 589832 | tf_op jit(solution)/shard_map/ppermute | solution.py:300
  99.0 5.0 %collective-permute-start.10 = (bf16[96,768]{1,0:T(8,128)(2,1)S(1)}, bf16[96,768]{1,0:T(8,128)(2,1)S(1)}, u32[]{:S(2)}, u32[]{:S(2)}) collective-permute-start(bf16[96,768]{1,0:T(8,128)(2,1)S(1)} %get-tuple-element.22), channel_id=1, source_target_pairs={{0,128},{128,0},{256,384},{384,256},{1,129},{129,1},{257,385},{385... | collective-permute-start | bytes 442376 | tf_op jit(solution)/shard_map/ppermute | solution.py:310

commit v19 on v18

--- a/solution.py
+++ b/solution.py
@@ -14,6 +14,7 @@
 LAST = (((1,), (1,)), ((), ()))
 SMEM = pl.BlockSpec(memory_space=pltpu.SMEM)
 VMEM = pl.BlockSpec(memory_space=pltpu.VMEM)
+HBM = pl.BlockSpec(memory_space=pltpu.HBM)
 PLANES = 4
 SHIFTS = (0, 2, 1, -1)
 
@@ -238,9 +239,9 @@
             pltpu.VMEM(act_inverse.shape, BF),
             pltpu.SemaphoreType.DMA((5,)),
         ],
-        [SMEM] + [pl.BlockSpec(memory_space=pl.ANY)] * 2,
-        limit=56,
+        [SMEM] + [HBM] * 2,
     )[0]
+    payload, cot = lax.optimization_barrier((payload, cotangent))
     first = lax.all_to_all(payload, "row", 0, 0)
 
     def along_y(block, k):
@@ -250,10 +251,9 @@
 
     picked = call(
         pick_kernel,
-        (sample_rows, cotangent),
+        (sample_rows, cot),
         [shape((2 * size + samp, feat_grp), BF)],
         2 * 64 * tok * feat_grp,
-        limit=56,
     )[0]
     beside = lax.ppermute(picked, "col", [(i, (i + 4) % n_col) for i in range(n_col)])
     cut = 2 * size
@@ -273,12 +273,12 @@
             pltpu.VMEM(grad_inverse.shape, BF),
             pltpu.SemaphoreType.DMA((4,)),
         ],
-        places=[pl.BlockSpec(memory_space=pl.ANY)] + [VMEM] * 4,
+        places=[HBM] + [VMEM] * 4,
     )
     taken = lax.ppermute(give, "grp", [(i, i ^ 1) for i in range(n_grp)])
     some = keep.astype(F32) + taken.astype(F32)
     give = some.astype(BF)
-    first, give, far_samples = lax.optimization_barrier((first, give, far_samples))
+    first, far_samples, unused = lax.optimization_barrier((first, far_samples, give))
     taken = lax.ppermute(give, "grp", [(i, i ^ 2) for i in range(n_grp)])
     right = (some + taken.astype(F32)).astype(BF)
     side = call(

time: 106 us -> 106 us (level)
  Pallas kernels: 11.5 us -> 9.75 us
  waiting for transfers between devices: 30.8 us -> 32.2 us
  starting transfers between devices: 59 us -> 57.8 us
  local copies, waits for them, and re-layouts: 1.74 us -> 2.89 us
    ppermute x1, waiting for transfers between devices: 0.01 us -> 4.2 us  [body(): lax.ppermute(picked, 'col', [(i, (i + 4) % n_col) for i in range(n_col)])]
    ppermute x4, waiting for transfers between devices: 18.2 us -> 15.1 us  [along_y(): lax.ppermute(block, 'col', [(i, i - i % 4 + (i + k) % 4) for i in range(n...]
    pallas_call x7, Pallas kernels: 11.5 us -> 9.75 us  [call(): pl.pallas_call(kernel, out_shape=outs, in_specs=places, out_specs=[VMEM]...]
    all_to_all x1, starting transfers between devices: 7.02 us -> 5.26 us  [body(): lax.all_to_all(send.reshape((n_grp * n_col,) + send.shape[2:]), ('grp', '...]
    unnamed x8 -> x14, local copies, waits for them, and re-layouts: 1.68 us -> 2.83 us
  transfers between devices with their start and end apart: 13 -> 13, of which waited for: 6 -> 8; matrix products, arithmetic and copies ran while one was open for 0% -> 0% of each run, Pallas kernels for 9% -> 5%
where the time goes in v19:
time: 106 us; the launch traced here: 104 us
  starting transfers between devices  57.8 us (55%)
  waiting for transfers between devices  32.2 us (30%)
  Pallas kernels  9.75 us (9%)
  local copies, waits for them, and re-layouts  2.89 us (3%)
    all_to_all x1, starting transfers between devices, body(): first = lax.all_to_all(payload, 'row', 0, 0)  15.8 us
    ppermute x4, waiting for transfers between devices, along_y(): lax.ppermute(block, 'col', [(i, i - i % 4 + (i + k) % 4) for i in range(n...  15.1 us
    ppermute x4, starting transfers between devices, along_y(): lax.ppermute(block, 'col', [(i, i - i % 4 + (i + k) % 4) for i in range(n...  10.8 us
    ppermute x3, waiting for transfers between devices, body(): lax.ppermute(right, 'row', [(i, (i + j) % n_row) for i in range(n_row)])  10.1 us
    pallas_call x7, Pallas kernels, call(): pl.pallas_call(kernel, out_shape=outs, in_specs=places, out_specs=[VMEM]...  9.75 us
    ppermute x3, starting transfers between devices, body(): lax.ppermute(right, 'row', [(i, (i + j) % n_row) for i in range(n_row)])  9.16 us
    ppermute x2, starting transfers between devices, body(): taken = lax.ppermute(give, 'grp', [(i, i ^ 1) for i in range(n_grp)])  9.12 us
    all_to_all x1, starting transfers between devices, body(): lax.all_to_all(send.reshape((n_grp * n_col,) + send.shape[2:]), ('grp', '...  5.26 us
  transfers between devices with their start and end apart: 13, of which 8 were waited for; matrix products, arithmetic and copies ran while one was open for 0% of the time, Pallas kernels for 5%

profile of v19, /device:TPU:1, one launch (start us, length us, event | category | flops | bytes accessed | tf_op | source)
XLA Modules:
  0.0 104.5 jit_solution(14716100339414980673)
XLA Ops:
  0.6 1.3 %copy-done.1 = bf16[1536,384]{1,0:T(8,128)(2,1)S(1)} copy-done((bf16[1536,384]{1,0:T(8,128)(2,1)S(1)}, bf16[1536,384]{1,0:T(8,128)(2,1)}, u32[]{:S(2)}) %copy-start.1) | copy-done | bytes 1179672
  1.9 0.9 copy-done.3
  2.8 0.7 copy-done.5
  3.5 3.0 %shard_map.76 = bf16[16,120,128]{2,1,0:T(8,128)(2,1)} custom-call(s32[32]{0:T(128)S(1)} %copy-done.5, bf16[128,384]{1,0:T(8,128)(2,1)S(1)} %copy-done.3, bf16[1536,384]{1,0:T(8,128)(2,1)S(1)} %copy-done.1), custom_call_target="tpu_custom_call" | custom-call | flops 150994944 | bytes 1769600 | tf_op jit(solution)/shard_map/pallas_call | solution.py:25
  6.4 15.8 %all-to-all-start = ((bf16[16,120,128]{2,1,0:T(8,128)(2,1)}), bf16[16,120,128]{2,1,0:T(8,128)(2,1)S(1)}, u32[]{:S(2)}, u32[]{:S(2)}) async-start(bf16[16,120,128]{2,1,0:T(8,128)(2,1)} %shard_map.76), calls=%async_computation | async-start | bytes 983040 | tf_op jit(solution)/shard_map/all_to_all | solution.py:245
  22.2 0.7 shard_map.77.gy_ref
  23.0 3.1 %collective-permute-start = (bf16[64,1536]{1,0:T(8,128)(2,1)S(1)}, bf16[64,1536]{1,0:T(8,128)(2,1)S(1)}, u32[]{:S(2)}, u32[]{:S(2)}) collective-permute-start(bf16[64,1536]{1,0:T(8,128)(2,1)S(1)} %shard_map.77.gy_ref), channel_id=1, source_target_pairs={{0,4},{1,5},{2,6},{3,7},{4,0},{5,1},{6,2},{7,3},{8,12},{9,13},{10,... | collective-permute-start | bytes 589832 | tf_op jit(solution)/shard_map/ppermute | solution.py:258
  26.1 4.2 %collective-permute-done = bf16[64,1536]{1,0:T(8,128)(2,1)S(1)} collective-permute-done((bf16[64,1536]{1,0:T(8,128)(2,1)S(1)}, bf16[64,1536]{1,0:T(8,128)(2,1)S(1)}, u32[]{:S(2)}, u32[]{:S(2)}) %collective-permute-start) | collective-permute-done | bytes 196640 | tf_op jit(solution)/shard_map/ppermute | solution.py:258
  30.4 3.2 %collective-permute-start.3 = (bf16[128,1536]{1,0:T(8,128)(2,1)S(1)}, bf16[128,1536]{1,0:T(8,128)(2,1)S(1)}, u32[]{:S(2)}, u32[]{:S(2)}) collective-permute-start(bf16[128,1536]{1,0:T(8,128)(2,1)S(1)} %pad_maximum_fusion.refs_0_), channel_id=1, source_target_pairs={{0,1},{1,2},{2,3},{3,0},{4,5},{5,6},{6,7},{7,4},{8,9},{9,10},{10,1... | collective-permute-start | bytes 1179656 | tf_op jit(solution)/shard_map/ppermute | solution.py:248
  33.6 3.3 %collective-permute-start.1 = (bf16[128,1536]{1,0:T(8,128)(2,1)S(1)}, bf16[128,1536]{1,0:T(8,128)(2,1)S(1)}, u32[]{:S(2)}, u32[]{:S(2)}) collective-permute-start(bf16[128,1536]{1,0:T(8,128)(2,1)S(1)} %pad_maximum_fusion.refs_0_), channel_id=1, source_target_pairs={{0,3},{1,0},{2,1},{3,2},{4,7},{5,4},{6,5},{7,6},{8,11},{9,8},{10,9... | collective-permute-start | bytes 1179656 | tf_op jit(solution)/shard_map/ppermute | solution.py:248
  37.0 5.4 %collective-permute-done.3.refs_1_ = bf16[128,1536]{1,0:T(8,128)(2,1)S(1)} collective-permute-done((bf16[128,1536]{1,0:T(8,128)(2,1)S(1)}, bf16[128,1536]{1,0:T(8,128)(2,1)S(1)}, u32[]{:S(2)}, u32[]{:S(2)}) %collective-permute-start.3) | collective-permute-done | bytes 393248 | tf_op jit(solution)/shard_map/ppermute | solution.py:248
  42.4 2.1 %collective-permute-start.4 = (bf16[64,1536]{1,0:T(8,128)(2,1)S(1)}, bf16[64,1536]{1,0:T(8,128)(2,1)S(1)}, u32[]{:S(2)}, u32[]{:S(2)}) collective-permute-start(bf16[64,1536]{1,0:T(8,128)(2,1)S(1)} %slice.29), channel_id=1, source_target_pairs={{0,1},{1,2},{2,3},{3,0},{4,5},{5,6},{6,7},{7,4},{8,9},{9,10},{10,1... | collective-permute-start | bytes 589832 | tf_op jit(solution)/shard_map/ppermute | solution.py:248
  44.4 6.0 %collective-permute-done.4.refs_2_ = bf16[64,1536]{1,0:T(8,128)(2,1)S(1)} collective-permute-done((bf16[64,1536]{1,0:T(8,128)(2,1)S(1)}, bf16[64,1536]{1,0:T(8,128)(2,1)S(1)}, u32[]{:S(2)}, u32[]{:S(2)}) %collective-permute-start.4) | collective-permute-done | bytes 196640 | tf_op jit(solution)/shard_map/ppermute | solution.py:248
  50.4 1.9 %shard_map.78 = (bf16[128,768]{1,0:T(8,128)(2,1)S(1)}, bf16[128,768]{1,0:T(8,128)(2,1)S(1)}) custom-call(bf16[1536,768]{1,0:T(8,128)(2,1)S(1)} %copy-done, bf16[128,1536]{1,0:T(8,128)(2,1)S(1)} %pad_maximum_fusion.refs_0_, bf16[128,1536]{1,0:T(8,128)(2,1)S(1)} %collective-permute-done.3.refs_1_, bf16[64,1536]{1,0:T(8,128)(2,1)S(1)} %collective-permute-done.4.refs_2_, ...), custom_call_target="tpu_custom_call" | custom-call | flops 603979776 | bytes 4128768 | tf_op jit(solution)/shard_map/pallas_call | solution.py:25
  52.3 5.5 %collective-permute-start.5 = (bf16[128,768]{1,0:T(8,128)(2,1)S(1)}, bf16[128,768]{1,0:T(8,128)(2,1)S(1)}, u32[]{:S(2)}, u32[]{:S(2)}) collective-permute-start(bf16[128,768]{1,0:T(8,128)(2,1)S(1)} %get-tuple-element.19), channel_id=1, source_target_pairs={{0,128},{128,0},{256,384},{384,256},{1,129},{129,1},{257,385},{385... | collective-permute-start | bytes 589832 | tf_op jit(solution)/shard_map/ppermute | solution.py:278
  57.8 1.0 %collective-permute-done.5 = bf16[128,768]{1,0:T(8,128)(2,1)S(1)} collective-permute-done((bf16[128,768]{1,0:T(8,128)(2,1)S(1)}, bf16[128,768]{1,0:T(8,128)(2,1)S(1)}, u32[]{:S(2)}, u32[]{:S(2)}) %collective-permute-start.5) | collective-permute-done | bytes 196640 | tf_op jit(solution)/shard_map/ppermute | solution.py:278
  59.0 4.7 %collective-permute-start.6 = (bf16[128,768]{1,0:T(8,128)(2,1)S(1)}, bf16[128,768]{1,0:T(8,128)(2,1)S(1)}, u32[]{:S(2)}, u32[]{:S(2)}) collective-permute-start(bf16[128,768]{1,0:T(8,128)(2,1)S(1)} %fusion), channel_id=1, source_target_pairs={{0,256},{128,384},{256,0},{384,128},{1,257},{129,385},{257,1},{385... | collective-permute-start | bytes 589832 | tf_op jit(solution)/shard_map/ppermute | solution.py:282
  63.6 1.0 shard_map.79.side_ref
  64.6 2.2 %collective-permute-start.2 = (bf16[64,1536]{1,0:T(8,128)(2,1)S(1)}, bf16[64,1536]{1,0:T(8,128)(2,1)S(1)}, u32[]{:S(2)}, u32[]{:S(2)}) collective-permute-start(bf16[64,1536]{1,0:T(8,128)(2,1)S(1)} %slice.28), channel_id=1, source_target_pairs={{0,3},{1,0},{2,1},{3,2},{4,7},{5,4},{6,5},{7,6},{8,11},{9,8},{10,9... | collective-permute-start | bytes 589832 | tf_op jit(solution)/shard_map/ppermute | solution.py:248
  66.8 1.7 %collective-permute-done.6 = bf16[128,768]{1,0:T(8,128)(2,1)S(1)} collective-permute-done((bf16[128,768]{1,0:T(8,128)(2,1)S(1)}, bf16[128,768]{1,0:T(8,128)(2,1)S(1)}, u32[]{:S(2)}, u32[]{:S(2)}) %collective-permute-start.6) | collective-permute-done | bytes 196640 | tf_op jit(solution)/shard_map/ppermute | solution.py:282
  68.6 3.8 %collective-permute-done.2.refs_2_ = bf16[64,1536]{1,0:T(8,128)(2,1)S(1)} collective-permute-done((bf16[64,1536]{1,0:T(8,128)(2,1)S(1)}, bf16[64,1536]{1,0:T(8,128)(2,1)S(1)}, u32[]{:S(2)}, u32[]{:S(2)}) %collective-permute-start.2) | collective-permute-done | bytes 196640 | tf_op jit(solution)/shard_map/ppermute | solution.py:248
  72.3 1.3 %shard_map.80 = bf16[4,8,160,128]{3,2,1,0:T(8,128)(2,1)} custom-call(bf16[16,120,128]{2,1,0:T(8,128)(2,1)S(1)} %all-to-all-done.got_ref, bf16[8,64,128]{2,1,0:T(8,128)(2,1)S(1)} %shard_map.79.side_ref), custom_call_target="tpu_custom_call" | custom-call | flops 1000000 | bytes 1933312 | tf_op jit(solution)/shard_map/pallas_call | solution.py:25
  73.6 5.3 %all-to-all-start.1 = ((bf16[32,160,128]{2,1,0:T(8,128)(2,1)}), bf16[32,160,128]{2,1,0:T(8,128)(2,1)S(1)}, u32[]{:S(2)}, u32[]{:S(2)}) async-start(bf16[32,160,128]{2,1,0:T(8,128)(2,1)} %bitcast), calls=%async_computation.1 | async-start | bytes 2621440 | tf_op jit(solution)/shard_map/all_to_all | solution.py:297
  78.9 4.2 %collective-permute-start.9 = (bf16[128,768]{1,0:T(8,128)(2,1)S(1)}, bf16[128,768]{1,0:T(8,128)(2,1)S(1)}, u32[]{:S(2)}, u32[]{:S(2)}) collective-permute-start(bf16[128,768]{1,0:T(8,128)(2,1)S(1)} %add_convert_fusion.refs_0_), channel_id=1, source_target_pairs={{0,120},{8,0},{16,8},{24,16},{32,24},{40,32},{48,40},{56,48},{64,5... | collective-permute-start | bytes 589832 | tf_op jit(solution)/shard_map/ppermute | solution.py:300
  83.1 1.9 %collective-permute-start.8 = (bf16[128,768]{1,0:T(8,128)(2,1)S(1)}, bf16[128,768]{1,0:T(8,128)(2,1)S(1)}, u32[]{:S(2)}, u32[]{:S(2)}) collective-permute-start(bf16[128,768]{1,0:T(8,128)(2,1)S(1)} %add_convert_fusion.refs_0_), channel_id=1, source_target_pairs={{0,8},{8,16},{16,24},{24,32},{32,40},{40,48},{48,56},{56,64},{64,7... | collective-permute-start | bytes 589832 | tf_op jit(solution)/shard_map/ppermute | solution.py:300
  85.0 3.0 %collective-permute-start.7 = (bf16[128,768]{1,0:T(8,128)(2,1)S(1)}, bf16[128,768]{1,0:T(8,128)(2,1)S(1)}, u32[]{:S(2)}, u32[]{:S(2)}) collective-permute-start(bf16[128,768]{1,0:T(8,128)(2,1)S(1)} %add_convert_fusion.refs_0_), channel_id=1, source_target_pairs={{0,16},{8,24},{16,32},{24,40},{32,48},{40,56},{48,64},{56,72},{64,... | collective-permute-start | bytes 589832 | tf_op jit(solution)/shard_map/ppermute | solution.py:300
  88.1 4.4 %collective-permute-done.8.refs_2_ = bf16[128,768]{1,0:T(8,128)(2,1)S(1)} collective-permute-done((bf16[128,768]{1,0:T(8,128)(2,1)S(1)}, bf16[128,768]{1,0:T(8,128)(2,1)S(1)}, u32[]{:S(2)}, u32[]{:S(2)}) %collective-permute-start.8) | collective-permute-done | bytes 196640 | tf_op jit(solution)/shard_map/ppermute | solution.py:300
  92.4 5.8 %collective-permute-done.7.refs_1_ = bf16[128,768]{1,0:T(8,128)(2,1)S(1)} collective-permute-done((bf16[128,768]{1,0:T(8,128)(2,1)S(1)}, bf16[128,768]{1,0:T(8,128)(2,1)S(1)}, u32[]{:S(2)}, u32[]{:S(2)}) %collective-permute-start.7) | collective-permute-done | bytes 196640 | tf_op jit(solution)/shard_map/ppermute | solution.py:300
  98.2 0.5 shard_map.81
  98.7 3.6 %collective-permute-start.10 = (bf16[96,768]{1,0:T(8,128)(2,1)S(1)}, bf16[96,768]{1,0:T(8,128)(2,1)S(1)}, u32[]{:S(2)}, u32[]{:S(2)}) collective-permute-start(bf16[96,768]{1,0:T(8,128)(2,1)S(1)} %get-tuple-element.24), channel_id=1, source_target_pairs={{0,128},{128,0},{256,384},{384,256},{1,129},{129,1},{257,385},{385... | collective-permute-start | bytes 442376 | tf_op jit(solution)/shard_map/ppermute | solution.py:310
  102.3 1.4 %shard_map.82 = (f32[48,1536]{1,0:T(8,128)}, f32[48,1536]{1,0:T(8,128)}) custom-call(bf16[4,8,160,128]{3,2,1,0:T(8,128)(2,1)S(1)} %bitcast.3, bf16[128,1536]{1,0:T(8,128)(2,1)S(1)} %pad_maximum_fusion.refs_0_, bf16[128,1536]{1,0:T(8,128)(2,1)S(1)} %collective-permute-done.3.refs_1_, bf16[64,1536]{1,0:T(8,128)(2,1)S(1)} %collective-permute-done.2.refs_2_, ...), custom_call_target="tpu_custom_call" | custom-call | flops 201326592 | bytes 3276800 | tf_op jit(solution)/shard_map/pallas_call | solution.py:25
  103.7 0.7 convert_add_fusion.1
  (23 shorter events, 0.3 us)
Async XLA Ops:
  0.6 1.3 %copy-start.1 = (bf16[1536,384]{1,0:T(8,128)(2,1)S(1)}, bf16[1536,384]{1,0:T(8,128)(2,1)}, u32[]{:S(2)}) copy-start(bf16[1536,384]{1,0:T(8,128)(2,1)} %a_hbm.1) | copy-start | bytes 3538948
  1.9 0.9 copy-start.3
  2.8 0.7 copy-start.5
  3.5 18.7 %copy-start.2 = (bf16[128,1536]{1,0:T(8,128)(2,1)S(1)}, bf16[128,1536]{1,0:T(8,128)(2,1)}, u32[]{:S(2)}) copy-start(bf16[128,1536]{1,0:T(8,128)(2,1)} %g_ref) | copy-start | bytes 1179652
  3.5 18.8 %copy-start.6 = (s32[32]{0:T(128)S(1)}, s32[32]{0:T(128)}, u32[]{:S(2)}) copy-start(s32[32]{0:T(128)} %picks.5) | copy-start | bytes 388
  6.4 65.9 %all-to-all-start = ((bf16[16,120,128]{2,1,0:T(8,128)(2,1)}), bf16[16,120,128]{2,1,0:T(8,128)(2,1)S(1)}, u32[]{:S(2)}, u32[]{:S(2)}) async-start(bf16[16,120,128]{2,1,0:T(8,128)(2,1)} %shard_map.76), calls=%async_computation | async-start | bytes 983040 | tf_op jit(solution)/shard_map/all_to_all | solution.py:245
  22.2 28.2 %copy-start = (bf16[1536,768]{1,0:T(8,128)(2,1)S(1)}, bf16[1536,768]{1,0:T(8,128)(2,1)}, u32[]{:S(2)}) copy-start(bf16[1536,768]{1,0:T(8,128)(2,1)} %b_hbm.1) | copy-start | bytes 7077892
  23.0 7.3 %collective-permute-start = (bf16[64,1536]{1,0:T(8,128)(2,1)S(1)}, bf16[64,1536]{1,0:T(8,128)(2,1)S(1)}, u32[]{:S(2)}, u32[]{:S(2)}) collective-permute-start(bf16[64,1536]{1,0:T(8,128)(2,1)S(1)} %shard_map.77.gy_ref), channel_id=1, source_target_pairs={{0,4},{1,5},{2,6},{3,7},{4,0},{5,1},{6,2},{7,3},{8,12},{9,13},{10,... | collective-permute-start | bytes 589832 | tf_op jit(solution)/shard_map/ppermute | solution.py:258
  30.4 12.0 %collective-permute-start.3 = (bf16[128,1536]{1,0:T(8,128)(2,1)S(1)}, bf16[128,1536]{1,0:T(8,128)(2,1)S(1)}, u32[]{:S(2)}, u32[]{:S(2)}) collective-permute-start(bf16[128,1536]{1,0:T(8,128)(2,1)S(1)} %pad_maximum_fusion.refs_0_), channel_id=1, source_target_pairs={{0,1},{1,2},{2,3},{3,0},{4,5},{5,6},{6,7},{7,4},{8,9},{9,10},{10,1... | collective-permute-start | bytes 1179656 | tf_op jit(solution)/shard_map/ppermute | solution.py:248
  33.6 10.8 %collective-permute-start.1 = (bf16[128,1536]{1,0:T(8,128)(2,1)S(1)}, bf16[128,1536]{1,0:T(8,128)(2,1)S(1)}, u32[]{:S(2)}, u32[]{:S(2)}) collective-permute-start(bf16[128,1536]{1,0:T(8,128)(2,1)S(1)} %pad_maximum_fusion.refs_0_), channel_id=1, source_target_pairs={{0,3},{1,0},{2,1},{3,2},{4,7},{5,4},{6,5},{7,6},{8,11},{9,8},{10,9... | collective-permute-start | bytes 1179656 | tf_op jit(solution)/shard_map/ppermute | solution.py:248
  42.4 21.3 %copy-start.4 = (bf16[128,384]{1,0:T(8,128)(2,1)S(1)}, bf16[128,384]{1,0:T(8,128)(2,1)}, u32[]{:S(2)}) copy-start(bf16[128,384]{1,0:T(8,128)(2,1)} %x_ref.1) | copy-start | bytes 294916
  42.4 8.1 %collective-permute-start.4 = (bf16[64,1536]{1,0:T(8,128)(2,1)S(1)}, bf16[64,1536]{1,0:T(8,128)(2,1)S(1)}, u32[]{:S(2)}, u32[]{:S(2)}) collective-permute-start(bf16[64,1536]{1,0:T(8,128)(2,1)S(1)} %slice.29), channel_id=1, source_target_pairs={{0,1},{1,2},{2,3},{3,0},{4,5},{5,6},{6,7},{7,4},{8,9},{9,10},{10,1... | collective-permute-start | bytes 589832 | tf_op jit(solution)/shard_map/ppermute | solution.py:248
  52.3 6.5 %collective-permute-start.5 = (bf16[128,768]{1,0:T(8,128)(2,1)S(1)}, bf16[128,768]{1,0:T(8,128)(2,1)S(1)}, u32[]{:S(2)}, u32[]{:S(2)}) collective-permute-start(bf16[128,768]{1,0:T(8,128)(2,1)S(1)} %get-tuple-element.19), channel_id=1, source_target_pairs={{0,128},{128,0},{256,384},{384,256},{1,129},{129,1},{257,385},{385... | collective-permute-start | bytes 589832 | tf_op jit(solution)/shard_map/ppermute | solution.py:278
  59.0 9.5 %collective-permute-start.6 = (bf16[128,768]{1,0:T(8,128)(2,1)S(1)}, bf16[128,768]{1,0:T(8,128)(2,1)S(1)}, u32[]{:S(2)}, u32[]{:S(2)}) collective-permute-start(bf16[128,768]{1,0:T(8,128)(2,1)S(1)} %fusion), channel_id=1, source_target_pairs={{0,256},{128,384},{256,0},{384,128},{1,257},{129,385},{257,1},{385... | collective-permute-start | bytes 589832 | tf_op jit(solution)/shard_map/ppermute | solution.py:282
  64.6 7.7 %collective-permute-start.2 = (bf16[64,1536]{1,0:T(8,128)(2,1)S(1)}, bf16[64,1536]{1,0:T(8,128)(2,1)S(1)}, u32[]{:S(2)}, u32[]{:S(2)}) collective-permute-start(bf16[64,1536]{1,0:T(8,128)(2,1)S(1)} %slice.28), channel_id=1, source_target_pairs={{0,3},{1,0},{2,1},{3,2},{4,7},{5,4},{6,5},{7,6},{8,11},{9,8},{10,9... | collective-permute-start | bytes 589832 | tf_op jit(solution)/shard_map/ppermute | solution.py:248
  73.6 24.6 %all-to-all-start.1 = ((bf16[32,160,128]{2,1,0:T(8,128)(2,1)}), bf16[32,160,128]{2,1,0:T(8,128)(2,1)S(1)}, u32[]{:S(2)}, u32[]{:S(2)}) async-start(bf16[32,160,128]{2,1,0:T(8,128)(2,1)} %bitcast), calls=%async_computation.1 | async-start | bytes 2621440 | tf_op jit(solution)/shard_map/all_to_all | solution.py:297
  78.9 9.2 %collective-permute-start.9 = (bf16[128,768]{1,0:T(8,128)(2,1)S(1)}, bf16[128,768]{1,0:T(8,128)(2,1)S(1)}, u32[]{:S(2)}, u32[]{:S(2)}) collective-permute-start(bf16[128,768]{1,0:T(8,128)(2,1)S(1)} %add_convert_fusion.refs_0_), channel_id=1, source_target_pairs={{0,120},{8,0},{16,8},{24,16},{32,24},{40,32},{48,40},{56,48},{64,5... | collective-permute-start | bytes 589832 | tf_op jit(solution)/shard_map/ppermute | solution.py:300
  83.1 9.4 %collective-permute-start.8 = (bf16[128,768]{1,0:T(8,128)(2,1)S(1)}, bf16[128,768]{1,0:T(8,128)(2,1)S(1)}, u32[]{:S(2)}, u32[]{:S(2)}) collective-permute-start(bf16[128,768]{1,0:T(8,128)(2,1)S(1)} %add_convert_fusion.refs_0_), channel_id=1, source_target_pairs={{0,8},{8,16},{16,24},{24,32},{32,40},{40,48},{48,56},{56,64},{64,7... | collective-permute-start | bytes 589832 | tf_op jit(solution)/shard_map/ppermute | solution.py:300
  85.0 13.2 %collective-permute-start.7 = (bf16[128,768]{1,0:T(8,128)(2,1)S(1)}, bf16[128,768]{1,0:T(8,128)(2,1)S(1)}, u32[]{:S(2)}, u32[]{:S(2)}) collective-permute-start(bf16[128,768]{1,0:T(8,128)(2,1)S(1)} %add_convert_fusion.refs_0_), channel_id=1, source_target_pairs={{0,16},{8,24},{16,32},{24,40},{32,48},{40,56},{48,64},{56,72},{64,... | collective-permute-start | bytes 589832 | tf_op jit(solution)/shard_map/ppermute | solution.py:300
  98.7 5.1 %collective-permute-start.10 = (bf16[96,768]{1,0:T(8,128)(2,1)S(1)}, bf16[96,768]{1,0:T(8,128)(2,1)S(1)}, u32[]{:S(2)}, u32[]{:S(2)}) collective-permute-start(bf16[96,768]{1,0:T(8,128)(2,1)S(1)} %get-tuple-element.24), channel_id=1, source_target_pairs={{0,128},{128,0},{256,384},{384,256},{1,129},{129,1},{257,385},{385... | collective-permute-start | bytes 442376 | tf_op jit(solution)/shard_map/ppermute | solution.py:310

commit v20 on v16

--- a/solution.py
+++ b/solution.py
@@ -248,6 +248,7 @@
         [SMEM] + [pl.BlockSpec(memory_space=pl.ANY)] * 2,
         limit=56,
     )[0]
+    payload, cot = lax.optimization_barrier((payload, cotangent))
     first = lax.all_to_all(payload, "row", 0, 0)
 
     def along_y(block, k):
@@ -257,7 +258,7 @@
 
     picked = call(
         pick_kernel,
-        (sample_rows, cotangent),
+        (sample_rows, cot),
         [shape((2 * size + samp, feat_grp), BF)],
         2 * 64 * tok * feat_grp,
     )[0]
@@ -285,12 +286,6 @@
     first, give = lax.optimization_barrier((first, give))
     taken = lax.ppermute(give, "grp", [(i, i ^ 2) for i in range(n_grp)])
     right = (some + taken.astype(F32)).astype(BF)
-    rights = [right] + [
-        lax.ppermute(right, "row", [(i, (i + j) % n_row) for i in range(n_row)])
-        for j in SHIFTS[1:]
-    ]
-    unused, picked_y, beside_y = lax.optimization_barrier((right, picked[cut:], beside[cut:]))
-    far = along_y(jnp.concatenate([picked_y, beside_y], axis=0), 2)
     side = call(
         side_kernel,
         (sample_rows, tokens_in, picked),
@@ -303,10 +298,17 @@
         [shape((n_grp, n_col, size * spread + strip * n_row // n_grp, LANES), BF)],
         1000000,
     )[0]
+    send, picked_y, beside_y = lax.optimization_barrier((send, picked[cut:], beside[cut:]))
+    far = along_y(jnp.concatenate([picked_y, beside_y], axis=0), 2)
+    send, right = lax.optimization_barrier((send, right))
     got = lax.all_to_all(send.reshape((n_grp * n_col,) + send.shape[2:]), ("grp", "col"), 0, 0)
     got = got.reshape(send.shape)
-
-    rights, far = lax.optimization_barrier((rights, far))
+    right, far = lax.optimization_barrier((right, far))
+    rights = [right] + [
+        lax.ppermute(right, "row", [(i, (i + j) % n_row) for i in range(n_row)])
+        for j in SHIFTS[1:]
+    ]
+
     term, give = call(
         final_kernel,
         (got, *rights),

time: 111 us -> 122 us (1.099)
  waiting for transfers between devices: 32.3 us -> 45.2 us
  starting transfers between devices: 65.8 us -> 62.9 us
    ppermute x4, waiting for transfers between devices: 6.98 us -> 26.8 us  [along_y(): lax.ppermute(block, 'col', [(i, i - i % 4 + (i + k) % 4) for i in range(n...]
    ppermute x1, waiting for transfers between devices: 17.2 us -> 2.59 us  [body(): taken = lax.ppermute(give, 'grp', [(i, i ^ 2) for i in range(n_grp)])]
    ppermute x3, waiting for transfers between devices: 3.76 us -> 10.5 us  [body(): lax.ppermute(right, 'row', [(i, (i + j) % n_row) for i in range(n_row)])]
    all_to_all x1, starting transfers between devices: 7.94 us -> 5.7 us  [body(): lax.all_to_all(send.reshape((n_grp * n_col,) + send.shape[2:]), ('grp', '...]
    ppermute x3, starting transfers between devices: 10.4 us -> 9.14 us  [body(): lax.ppermute(right, 'row', [(i, (i + j) % n_row) for i in range(n_row)])]
  transfers between devices with their start and end apart: 13 -> 13, of which waited for: 5 -> 7; matrix products, arithmetic and copies ran while one was open for 0% -> 0% of each run, Pallas kernels for 5% -> 5%
where the time goes in v20:
time: 122 us; the launch traced here: 120 us
  starting transfers between devices  62.9 us (52%)
  waiting for transfers between devices  45.2 us (37%)
  Pallas kernels  10.5 us (9%)
    ppermute x4, waiting for transfers between devices, along_y(): lax.ppermute(block, 'col', [(i, i - i % 4 + (i + k) % 4) for i in range(n...  26.8 us
    all_to_all x1, starting transfers between devices, body(): first = lax.all_to_all(payload, 'row', 0, 0)  15.8 us
    ppermute x4, starting transfers between devices, along_y(): lax.ppermute(block, 'col', [(i, i - i % 4 + (i + k) % 4) for i in range(n...  15 us
    pallas_call x7, Pallas kernels, call(): pl.pallas_call(kernel, out_shape=outs, in_specs=places, out_specs=[VMEM]...  10.5 us
    ppermute x3, waiting for transfers between devices, body(): lax.ppermute(right, 'row', [(i, (i + j) % n_row) for i in range(n_row)])  10.5 us
    ppermute x2, starting transfers between devices, body(): taken = lax.ppermute(give, 'grp', [(i, i ^ 1) for i in range(n_grp)])  9.53 us
    ppermute x3, starting transfers between devices, body(): lax.ppermute(right, 'row', [(i, (i + j) % n_row) for i in range(n_row)])  9.14 us
    all_to_all x1, starting transfers between devices, body(): lax.all_to_all(send.reshape((n_grp * n_col,) + send.shape[2:]), ('grp', '...  5.7 us
  transfers between devices with their start and end apart: 13, of which 7 were waited for; matrix products, arithmetic and copies ran while one was open for 0% of the time, Pallas kernels for 5%

profile of v20, /device:TPU:1, one launch (start us, length us, event | category | flops | bytes accessed | tf_op | source)
XLA Modules:
  0.0 120.5 jit_solution(850275841077364488)
XLA Ops:
  0.7 3.7 %shard_map.76 = bf16[16,120,128]{2,1,0:T(8,128)(2,1)} custom-call(s32[32]{0:T(128)} %picks.5, bf16[128,384]{1,0:T(8,128)(2,1)} %x_ref.1, bf16[1536,384]{1,0:T(8,128)(2,1)} %a_hbm.1), custom_call_target="tpu_custom_call" | custom-call | flops 150994944 | bytes 1769600 | tf_op jit(solution)/shard_map/pallas_call | solution.py:24
  4.4 15.8 %all-to-all-start = ((bf16[16,120,128]{2,1,0:T(8,128)(2,1)}), bf16[16,120,128]{2,1,0:T(8,128)(2,1)S(1)}, u32[]{:S(2)}, u32[]{:S(2)}) async-start(bf16[16,120,128]{2,1,0:T(8,128)(2,1)} %shard_map.76), calls=%async_computation | async-start | bytes 983040 | tf_op jit(solution)/shard_map/all_to_all | solution.py:252
  20.2 0.0 copy-start
  20.2 0.7 shard_map.77.gy_ref
  20.9 3.1 %collective-permute-start = (bf16[64,1536]{1,0:T(8,128)(2,1)S(1)}, bf16[64,1536]{1,0:T(8,128)(2,1)S(1)}, u32[]{:S(2)}, u32[]{:S(2)}) collective-permute-start(bf16[64,1536]{1,0:T(8,128)(2,1)S(1)} %shard_map.77.gy_ref), channel_id=1, source_target_pairs={{0,4},{1,5},{2,6},{3,7},{4,0},{5,1},{6,2},{7,3},{8,12},{9,13},{10,... | collective-permute-start | bytes 589832 | tf_op jit(solution)/shard_map/ppermute | solution.py:265
  24.1 4.2 %collective-permute-done = bf16[64,1536]{1,0:T(8,128)(2,1)S(1)} collective-permute-done((bf16[64,1536]{1,0:T(8,128)(2,1)S(1)}, bf16[64,1536]{1,0:T(8,128)(2,1)S(1)}, u32[]{:S(2)}, u32[]{:S(2)}) %collective-permute-start) | collective-permute-done | bytes 196640 | tf_op jit(solution)/shard_map/ppermute | solution.py:265
  28.3 4.6 %collective-permute-start.3 = (bf16[128,1536]{1,0:T(8,128)(2,1)S(1)}, bf16[128,1536]{1,0:T(8,128)(2,1)S(1)}, u32[]{:S(2)}, u32[]{:S(2)}) collective-permute-start(bf16[128,1536]{1,0:T(8,128)(2,1)S(1)} %pad_maximum_fusion.refs_0_), channel_id=1, source_target_pairs={{0,3},{1,0},{2,1},{3,2},{4,7},{5,4},{6,5},{7,6},{8,11},{9,8},{10,9... | collective-permute-start | bytes 1179656 | tf_op jit(solution)/shard_map/ppermute | solution.py:255
  32.9 1.9 %collective-permute-start.1 = (bf16[128,1536]{1,0:T(8,128)(2,1)S(1)}, bf16[128,1536]{1,0:T(8,128)(2,1)S(1)}, u32[]{:S(2)}, u32[]{:S(2)}) collective-permute-start(bf16[128,1536]{1,0:T(8,128)(2,1)S(1)} %pad_maximum_fusion.refs_0_), channel_id=1, source_target_pairs={{0,1},{1,2},{2,3},{3,0},{4,5},{5,6},{6,7},{7,4},{8,9},{9,10},{10,1... | collective-permute-start | bytes 1179656 | tf_op jit(solution)/shard_map/ppermute | solution.py:255
  34.9 0.0 copy-start.2
  34.9 3.7 %collective-permute-start.2 = (bf16[64,1536]{1,0:T(8,128)(2,1)S(1)}, bf16[64,1536]{1,0:T(8,128)(2,1)S(1)}, u32[]{:S(2)}, u32[]{:S(2)}) collective-permute-start(bf16[64,1536]{1,0:T(8,128)(2,1)S(1)} %pad_maximum_fusion.1), channel_id=1, source_target_pairs={{0,2},{1,3},{2,0},{3,1},{4,6},{5,7},{6,4},{7,5},{8,10},{9,11},{10,... | collective-permute-start | bytes 589832 | tf_op jit(solution)/shard_map/ppermute | solution.py:255
  38.6 9.1 %collective-permute-done.2.refs_2_ = bf16[64,1536]{1,0:T(8,128)(2,1)S(1)} collective-permute-done((bf16[64,1536]{1,0:T(8,128)(2,1)S(1)}, bf16[64,1536]{1,0:T(8,128)(2,1)S(1)}, u32[]{:S(2)}, u32[]{:S(2)}) %collective-permute-start.2) | collective-permute-done | bytes 196640 | tf_op jit(solution)/shard_map/ppermute | solution.py:255
  47.7 0.0 collective-permute-done.3.refs_3_
  47.7 1.9 %shard_map.78 = (bf16[128,768]{1,0:T(8,128)(2,1)S(1)}, bf16[128,768]{1,0:T(8,128)(2,1)S(1)}) custom-call(bf16[1536,768]{1,0:T(8,128)(2,1)S(1)} %copy-done, bf16[128,1536]{1,0:T(8,128)(2,1)S(1)} %pad_maximum_fusion.refs_0_, bf16[128,1536]{1,0:T(8,128)(2,1)S(1)} %collective-permute-done.1.refs_1_, bf16[64,1536]{1,0:T(8,128)(2,1)S(1)} %collective-permute-done.2.refs_2_, ...), custom_call_target="tpu_custom_call" | custom-call | flops 603979776 | bytes 4128768 | tf_op jit(solution)/shard_map/pallas_call | solution.py:24
  49.6 6.0 %collective-permute-start.4 = (bf16[128,768]{1,0:T(8,128)(2,1)S(1)}, bf16[128,768]{1,0:T(8,128)(2,1)S(1)}, u32[]{:S(2)}, u32[]{:S(2)}) collective-permute-start(bf16[128,768]{1,0:T(8,128)(2,1)S(1)} %get-tuple-element.24), channel_id=1, source_target_pairs={{0,128},{128,0},{256,384},{384,256},{1,129},{129,1},{257,385},{385... | collective-permute-start | bytes 589832 | tf_op jit(solution)/shard_map/ppermute | solution.py:283
  55.6 1.0 collective-permute-done.4
  56.8 4.6 %collective-permute-start.5 = (bf16[128,768]{1,0:T(8,128)(2,1)S(1)}, bf16[128,768]{1,0:T(8,128)(2,1)S(1)}, u32[]{:S(2)}, u32[]{:S(2)}) collective-permute-start(bf16[128,768]{1,0:T(8,128)(2,1)S(1)} %fusion), channel_id=1, source_target_pairs={{0,256},{128,384},{256,0},{384,128},{1,257},{129,385},{257,1},{385... | collective-permute-start | bytes 589832 | tf_op jit(solution)/shard_map/ppermute | solution.py:287
  61.4 1.0 shard_map.79.side_ref
  62.4 1.3 %shard_map.80 = bf16[4,8,160,128]{3,2,1,0:T(8,128)(2,1)} custom-call(bf16[16,120,128]{2,1,0:T(8,128)(2,1)S(1)} %all-to-all-done.got_ref, bf16[8,64,128]{2,1,0:T(8,128)(2,1)S(1)} %shard_map.79.side_ref), custom_call_target="tpu_custom_call" | custom-call | flops 1000000 | bytes 1933312 | tf_op jit(solution)/shard_map/pallas_call | solution.py:24
  63.7 2.6 %collective-permute-done.5 = bf16[128,768]{1,0:T(8,128)(2,1)S(1)} collective-permute-done((bf16[128,768]{1,0:T(8,128)(2,1)S(1)}, bf16[128,768]{1,0:T(8,128)(2,1)S(1)}, u32[]{:S(2)}, u32[]{:S(2)}) %collective-permute-start.5) | collective-permute-done | bytes 196640 | tf_op jit(solution)/shard_map/ppermute | solution.py:287
  66.3 0.1 add_convert_fusion.refs_0_
  66.3 5.7 %all-to-all-start.1 = ((bf16[32,160,128]{2,1,0:T(8,128)(2,1)}), bf16[32,160,128]{2,1,0:T(8,128)(2,1)S(1)}, u32[]{:S(2)}, u32[]{:S(2)}) async-start(bf16[32,160,128]{2,1,0:T(8,128)(2,1)} %bitcast), calls=%async_computation.1 | async-start | bytes 2621440 | tf_op jit(solution)/shard_map/all_to_all | solution.py:304
  72.1 4.8 %collective-permute-start.6 = (bf16[64,1536]{1,0:T(8,128)(2,1)S(1)}, bf16[64,1536]{1,0:T(8,128)(2,1)S(1)}, u32[]{:S(2)}, u32[]{:S(2)}) collective-permute-start(bf16[64,1536]{1,0:T(8,128)(2,1)S(1)} %pad_maximum_fusion.2), channel_id=1, source_target_pairs={{0,2},{1,3},{2,0},{3,1},{4,6},{5,7},{6,4},{7,5},{8,10},{9,11},{10,... | collective-permute-start | bytes 589832 | tf_op jit(solution)/shard_map/ppermute | solution.py:255
  76.9 17.7 %collective-permute-done.6.refs_2_ = bf16[64,1536]{1,0:T(8,128)(2,1)S(1)} collective-permute-done((bf16[64,1536]{1,0:T(8,128)(2,1)S(1)}, bf16[64,1536]{1,0:T(8,128)(2,1)S(1)}, u32[]{:S(2)}, u32[]{:S(2)}) %collective-permute-start.6) | collective-permute-done | bytes 196640 | tf_op jit(solution)/shard_map/ppermute | solution.py:255
  94.6 4.2 %collective-permute-start.9 = (bf16[128,768]{1,0:T(8,128)(2,1)S(1)}, bf16[128,768]{1,0:T(8,128)(2,1)S(1)}, u32[]{:S(2)}, u32[]{:S(2)}) collective-permute-start(bf16[128,768]{1,0:T(8,128)(2,1)S(1)} %add_convert_fusion.refs_0_), channel_id=1, source_target_pairs={{0,120},{8,0},{16,8},{24,16},{32,24},{40,32},{48,40},{56,48},{64,5... | collective-permute-start | bytes 589832 | tf_op jit(solution)/shard_map/ppermute | solution.py:308
  98.8 1.9 %collective-permute-start.8 = (bf16[128,768]{1,0:T(8,128)(2,1)S(1)}, bf16[128,768]{1,0:T(8,128)(2,1)S(1)}, u32[]{:S(2)}, u32[]{:S(2)}) collective-permute-start(bf16[128,768]{1,0:T(8,128)(2,1)S(1)} %add_convert_fusion.refs_0_), channel_id=1, source_target_pairs={{0,8},{8,16},{16,24},{24,32},{32,40},{40,48},{48,56},{56,64},{64,7... | collective-permute-start | bytes 589832 | tf_op jit(solution)/shard_map/ppermute | solution.py:308
  100.7 3.0 %collective-permute-start.7 = (bf16[128,768]{1,0:T(8,128)(2,1)S(1)}, bf16[128,768]{1,0:T(8,128)(2,1)S(1)}, u32[]{:S(2)}, u32[]{:S(2)}) collective-permute-start(bf16[128,768]{1,0:T(8,128)(2,1)S(1)} %add_convert_fusion.refs_0_), channel_id=1, source_target_pairs={{0,16},{8,24},{16,32},{24,40},{32,48},{40,56},{48,64},{56,72},{64,... | collective-permute-start | bytes 589832 | tf_op jit(solution)/shard_map/ppermute | solution.py:308
  103.8 3.4 %collective-permute-done.8.refs_2_ = bf16[128,768]{1,0:T(8,128)(2,1)S(1)} collective-permute-done((bf16[128,768]{1,0:T(8,128)(2,1)S(1)}, bf16[128,768]{1,0:T(8,128)(2,1)S(1)}, u32[]{:S(2)}, u32[]{:S(2)}) %collective-permute-start.8) | collective-permute-done | bytes 196640 | tf_op jit(solution)/shard_map/ppermute | solution.py:308
  107.2 7.1 %collective-permute-done.7.refs_1_ = bf16[128,768]{1,0:T(8,128)(2,1)S(1)} collective-permute-done((bf16[128,768]{1,0:T(8,128)(2,1)S(1)}, bf16[128,768]{1,0:T(8,128)(2,1)S(1)}, u32[]{:S(2)}, u32[]{:S(2)}) %collective-permute-start.7) | collective-permute-done | bytes 196640 | tf_op jit(solution)/shard_map/ppermute | solution.py:308
  114.3 0.5 shard_map.81
  114.7 3.5 %collective-permute-start.10 = (bf16[96,768]{1,0:T(8,128)(2,1)S(1)}, bf16[96,768]{1,0:T(8,128)(2,1)S(1)}, u32[]{:S(2)}, u32[]{:S(2)}) collective-permute-start(bf16[96,768]{1,0:T(8,128)(2,1)S(1)} %get-tuple-element.34), channel_id=1, source_target_pairs={{0,128},{128,0},{256,384},{384,256},{1,129},{129,1},{257,385},{385... | collective-permute-start | bytes 442376 | tf_op jit(solution)/shard_map/ppermute | solution.py:319
  118.3 1.4 %shard_map.82 = (f32[48,1536]{1,0:T(8,128)}, f32[48,1536]{1,0:T(8,128)}) custom-call(bf16[4,8,160,128]{3,2,1,0:T(8,128)(2,1)S(1)} %bitcast.3, bf16[128,1536]{1,0:T(8,128)(2,1)S(1)} %pad_maximum_fusion.refs_0_, bf16[128,1536]{1,0:T(8,128)(2,1)S(1)} %collective-permute-done.1.refs_1_, bf16[64,1536]{1,0:T(8,128)(2,1)S(1)} %collective-permute-done.6.refs_2_, ...), custom_call_target="tpu_custom_call" | custom-call | flops 201326592 | bytes 3276800 | tf_op jit(solution)/shard_map/pallas_call | solution.py:24
  119.7 0.7 convert_add_fusion.1
  (17 shorter events, 0.2 us)
Async XLA Ops:
  0.6 19.5 %copy-start.3 = (s32[32]{0:T(128)S(1)}, s32[32]{0:T(128)}, u32[]{:S(2)}) copy-start(s32[32]{0:T(128)} %picks.5) | copy-start | bytes 388
  0.6 19.5 %copy-start.1 = (bf16[128,1536]{1,0:T(8,128)(2,1)S(1)}, bf16[128,1536]{1,0:T(8,128)(2,1)}, u32[]{:S(2)}) copy-start(bf16[128,1536]{1,0:T(8,128)(2,1)} %g_ref) | copy-start | bytes 1179652
  4.4 52.4 %all-to-all-start = ((bf16[16,120,128]{2,1,0:T(8,128)(2,1)}), bf16[16,120,128]{2,1,0:T(8,128)(2,1)S(1)}, u32[]{:S(2)}, u32[]{:S(2)}) async-start(bf16[16,120,128]{2,1,0:T(8,128)(2,1)} %shard_map.76), calls=%async_computation | async-start | bytes 983040 | tf_op jit(solution)/shard_map/all_to_all | solution.py:252
  20.2 27.5 %copy-start = (bf16[1536,768]{1,0:T(8,128)(2,1)S(1)}, bf16[1536,768]{1,0:T(8,128)(2,1)}, u32[]{:S(2)}) copy-start(bf16[1536,768]{1,0:T(8,128)(2,1)} %b_hbm.1) | copy-start | bytes 7077892
  20.9 7.3 %collective-permute-start = (bf16[64,1536]{1,0:T(8,128)(2,1)S(1)}, bf16[64,1536]{1,0:T(8,128)(2,1)S(1)}, u32[]{:S(2)}, u32[]{:S(2)}) collective-permute-start(bf16[64,1536]{1,0:T(8,128)(2,1)S(1)} %shard_map.77.gy_ref), channel_id=1, source_target_pairs={{0,4},{1,5},{2,6},{3,7},{4,0},{5,1},{6,2},{7,3},{8,12},{9,13},{10,... | collective-permute-start | bytes 589832 | tf_op jit(solution)/shard_map/ppermute | solution.py:265
  28.3 19.4 %collective-permute-start.3 = (bf16[128,1536]{1,0:T(8,128)(2,1)S(1)}, bf16[128,1536]{1,0:T(8,128)(2,1)S(1)}, u32[]{:S(2)}, u32[]{:S(2)}) collective-permute-start(bf16[128,1536]{1,0:T(8,128)(2,1)S(1)} %pad_maximum_fusion.refs_0_), channel_id=1, source_target_pairs={{0,3},{1,0},{2,1},{3,2},{4,7},{5,4},{6,5},{7,6},{8,11},{9,8},{10,9... | collective-permute-start | bytes 1179656 | tf_op jit(solution)/shard_map/ppermute | solution.py:255
  32.9 14.8 %collective-permute-start.1 = (bf16[128,1536]{1,0:T(8,128)(2,1)S(1)}, bf16[128,1536]{1,0:T(8,128)(2,1)S(1)}, u32[]{:S(2)}, u32[]{:S(2)}) collective-permute-start(bf16[128,1536]{1,0:T(8,128)(2,1)S(1)} %pad_maximum_fusion.refs_0_), channel_id=1, source_target_pairs={{0,1},{1,2},{2,3},{3,0},{4,5},{5,6},{6,7},{7,4},{8,9},{9,10},{10,1... | collective-permute-start | bytes 1179656 | tf_op jit(solution)/shard_map/ppermute | solution.py:255
  34.9 26.5 %copy-start.2 = (bf16[128,384]{1,0:T(8,128)(2,1)S(1)}, bf16[128,384]{1,0:T(8,128)(2,1)}, u32[]{:S(2)}) copy-start(bf16[128,384]{1,0:T(8,128)(2,1)} %x_ref.1) | copy-start | bytes 294916
  34.9 12.8 %collective-permute-start.2 = (bf16[64,1536]{1,0:T(8,128)(2,1)S(1)}, bf16[64,1536]{1,0:T(8,128)(2,1)S(1)}, u32[]{:S(2)}, u32[]{:S(2)}) collective-permute-start(bf16[64,1536]{1,0:T(8,128)(2,1)S(1)} %pad_maximum_fusion.1), channel_id=1, source_target_pairs={{0,2},{1,3},{2,0},{3,1},{4,6},{5,7},{6,4},{7,5},{8,10},{9,11},{10,... | collective-permute-start | bytes 589832 | tf_op jit(solution)/shard_map/ppermute | solution.py:255
  49.6 7.1 %collective-permute-start.4 = (bf16[128,768]{1,0:T(8,128)(2,1)S(1)}, bf16[128,768]{1,0:T(8,128)(2,1)S(1)}, u32[]{:S(2)}, u32[]{:S(2)}) collective-permute-start(bf16[128,768]{1,0:T(8,128)(2,1)S(1)} %get-tuple-element.24), channel_id=1, source_target_pairs={{0,128},{128,0},{256,384},{384,256},{1,129},{129,1},{257,385},{385... | collective-permute-start | bytes 589832 | tf_op jit(solution)/shard_map/ppermute | solution.py:283
  56.8 9.5 %collective-permute-start.5 = (bf16[128,768]{1,0:T(8,128)(2,1)S(1)}, bf16[128,768]{1,0:T(8,128)(2,1)S(1)}, u32[]{:S(2)}, u32[]{:S(2)}) collective-permute-start(bf16[128,768]{1,0:T(8,128)(2,1)S(1)} %fusion), channel_id=1, source_target_pairs={{0,256},{128,384},{256,0},{384,128},{1,257},{129,385},{257,1},{385... | collective-permute-start | bytes 589832 | tf_op jit(solution)/shard_map/ppermute | solution.py:287
  66.3 47.9 %all-to-all-start.1 = ((bf16[32,160,128]{2,1,0:T(8,128)(2,1)}), bf16[32,160,128]{2,1,0:T(8,128)(2,1)S(1)}, u32[]{:S(2)}, u32[]{:S(2)}) async-start(bf16[32,160,128]{2,1,0:T(8,128)(2,1)} %bitcast), calls=%async_computation.1 | async-start | bytes 2621440 | tf_op jit(solution)/shard_map/all_to_all | solution.py:304
  72.1 22.5 %collective-permute-start.6 = (bf16[64,1536]{1,0:T(8,128)(2,1)S(1)}, bf16[64,1536]{1,0:T(8,128)(2,1)S(1)}, u32[]{:S(2)}, u32[]{:S(2)}) collective-permute-start(bf16[64,1536]{1,0:T(8,128)(2,1)S(1)} %pad_maximum_fusion.2), channel_id=1, source_target_pairs={{0,2},{1,3},{2,0},{3,1},{4,6},{5,7},{6,4},{7,5},{8,10},{9,11},{10,... | collective-permute-start | bytes 589832 | tf_op jit(solution)/shard_map/ppermute | solution.py:255
  94.6 9.2 %collective-permute-start.9 = (bf16[128,768]{1,0:T(8,128)(2,1)S(1)}, bf16[128,768]{1,0:T(8,128)(2,1)S(1)}, u32[]{:S(2)}, u32[]{:S(2)}) collective-permute-start(bf16[128,768]{1,0:T(8,128)(2,1)S(1)} %add_convert_fusion.refs_0_), channel_id=1, source_target_pairs={{0,120},{8,0},{16,8},{24,16},{32,24},{40,32},{48,40},{56,48},{64,5... | collective-permute-start | bytes 589832 | tf_op jit(solution)/shard_map/ppermute | solution.py:308
  98.8 8.3 %collective-permute-start.8 = (bf16[128,768]{1,0:T(8,128)(2,1)S(1)}, bf16[128,768]{1,0:T(8,128)(2,1)S(1)}, u32[]{:S(2)}, u32[]{:S(2)}) collective-permute-start(bf16[128,768]{1,0:T(8,128)(2,1)S(1)} %add_convert_fusion.refs_0_), channel_id=1, source_target_pairs={{0,8},{8,16},{16,24},{24,32},{32,40},{40,48},{48,56},{56,64},{64,7... | collective-permute-start | bytes 589832 | tf_op jit(solution)/shard_map/ppermute | solution.py:308
  100.7 13.5 %collective-permute-start.7 = (bf16[128,768]{1,0:T(8,128)(2,1)S(1)}, bf16[128,768]{1,0:T(8,128)(2,1)S(1)}, u32[]{:S(2)}, u32[]{:S(2)}) collective-permute-start(bf16[128,768]{1,0:T(8,128)(2,1)S(1)} %add_convert_fusion.refs_0_), channel_id=1, source_target_pairs={{0,16},{8,24},{16,32},{24,40},{32,48},{40,56},{48,64},{56,72},{64,... | collective-permute-start | bytes 589832 | tf_op jit(solution)/shard_map/ppermute | solution.py:308
  114.7 5.0 %collective-permute-start.10 = (bf16[96,768]{1,0:T(8,128)(2,1)S(1)}, bf16[96,768]{1,0:T(8,128)(2,1)S(1)}, u32[]{:S(2)}, u32[]{:S(2)}) collective-permute-start(bf16[96,768]{1,0:T(8,128)(2,1)S(1)} %get-tuple-element.34), channel_id=1, source_target_pairs={{0,128},{128,0},{256,384},{384,256},{1,129},{129,1},{257,385},{385... | collective-permute-start | bytes 442376 | tf_op jit(solution)/shard_map/ppermute | solution.py:319

commit v21 on v15

--- a/solution.py
+++ b/solution.py
@@ -116,12 +116,6 @@
         out_ref[c] = block.astype(BF)
 
 
-def rows_of(block, begin, count):
-    step = block.shape[0] // 2
-    begin = begin if step > count else 0
-    return [block[at : at + count, :] for at in (begin, step + begin)]
-
-
 def right_kernel(b_hbm, *refs):
     blocks, keep_ref, give_ref, held, b_ref, sems = refs[:-5], *refs[-5:]
     n_blk, unused, size, width = held.shape
@@ -134,8 +128,7 @@
     ]
     for copy in copies:
         copy.start()
-    rows = [piece for block in blocks for piece in rows_of(block, 0, 2 * size)]
-    rows = jnp.concatenate(rows, axis=0)
+    rows = jnp.concatenate([block[: 4 * size, :] for block in blocks], axis=0)
     term = None
     for p in range(parts):
         copies[p].wait()
@@ -209,7 +202,7 @@
         act_ref[16 * k : 16 * (k + 1), :] = term[LANES - 16 :] * scale
     owner = lax.axis_index("row") // 4
     sides = [got_ref[owner, source_of(k), : 2 * samp, :] for k in range(n_col)]
-    rights = [piece for block in blocks for piece in rows_of(block, samp, samp)]
+    rights = [block[block.shape[0] - 2 * samp :, :] for block in blocks]
     right = jnp.concatenate(rights, axis=0)
     left = jnp.concatenate([side[:samp] for side in sides], axis=0)
     term = lax.dot_general(left, right, FIRST, preferred_element_type=F32)
@@ -263,10 +256,12 @@
     )[0]
     beside = lax.ppermute(picked, "col", [(i, (i + 4) % n_col) for i in range(n_col)])
     cut = 2 * size
-    pair = jnp.concatenate([picked, beside], axis=0)
     rows = jnp.concatenate([picked[:cut], beside[:cut]], axis=0)
-    near = {k: along_y(pair, k) for k in (1, 3)}
-    pairs = [pair, near[1], along_y(rows, 2), near[3]]
+    samples = jnp.concatenate([picked[cut:], beside[cut:]], axis=0)
+    pair = jnp.concatenate([rows, samples], axis=0)
+    after = along_y(pair, 3)
+    before = along_y(rows, 1)
+    pairs = [pair, before, along_y(rows, 2), after]
     keep, give = call(
         right_kernel,
         (grad_inverse, *pairs),
@@ -279,9 +274,11 @@
         ],
         places=[pl.BlockSpec(memory_space=pl.ANY)] + [VMEM] * 4,
     )
-    first, unused = lax.optimization_barrier((first, give))
+    before, samples = lax.optimization_barrier((before, samples))
+    nearby = along_y(samples, 1)
     taken = lax.ppermute(give, "grp", [(i, i ^ 1) for i in range(n_grp)])
     right = (keep.astype(F32) + taken.astype(F32)).astype(BF)
+    first, unused = lax.optimization_barrier((first, (right, nearby)))
     rights = [right] + [
         lax.ppermute(right, "row", [(i, (i + j) % n_row) for i in range(n_row)])
         for j in SHIFTS[1:]
@@ -308,13 +305,13 @@
         2 * n_grp * LANES * n_col * spread * size * width,
         [pltpu.VMEM((n_col, spread, size, width), BF)],
     )[0]
-    got, picked, beside, unused = lax.optimization_barrier((got, picked, beside, term))
+    got, beyond, unused = lax.optimization_barrier((got, after[2 * cut :], term))
     term = lax.all_to_all(term, "grp", 0, 0)
-    far = along_y(jnp.concatenate([picked[cut:], beside[cut:]], axis=0), 2)
+    far = along_y(beyond, 3)
     precond = jnp.sum(term.astype(F32), axis=0)
     act_cov, grad_cov = call(
         factor_kernel,
-        (got, pair, near[1], far, near[3]),
+        (got, pair, nearby, far, after),
         [shape((tile, feat_grp), F32)] * 2,
         4 * LANES * samp * n_col * feat_grp,
     )

time: 101 us -> 103 us (1.020)
  local copies, waits for them, and re-layouts: 0.05 us -> 1.71 us
    ppermute x4 -> x5, waiting for transfers between devices: 11.5 us -> 17 us  [along_y(): lax.ppermute(block, 'col', [(i, i - i % 4 + (i + k) % 4) for i in range(n...]
    all_to_all x1, starting transfers between devices: 10.4 us -> 5.72 us  [body(): lax.all_to_all(send.reshape((n_grp * n_col,) + send.shape[2:]), ('grp', '...]
    ppermute x1, waiting for transfers between devices: 4.21 us -> 0.01 us  [body(): lax.ppermute(picked, 'col', [(i, (i + 4) % n_col) for i in range(n_col)])]
    ppermute x4 -> x5, starting transfers between devices: 14.7 us -> 17.1 us  [along_y(): lax.ppermute(block, 'col', [(i, i - i % 4 + (i + k) % 4) for i in range(n...]
    ppermute x1, starting transfers between devices: 2.14 us -> 4.38 us  [body(): taken = lax.ppermute(give, 'grp', [(i, i ^ 1) for i in range(n_grp)])]
    unnamed x10, local copies, waits for them, and re-layouts: 0.02 us -> 1.66 us
    ppermute x1, waiting for transfers between devices: 1.19 us -> 0.01 us  [body(): taken = lax.ppermute(give, 'grp', [(i, i ^ 1) for i in range(n_grp)])]
  transfers between devices with their start and end apart: 12 -> 13, of which waited for: 6 -> 7; matrix products, arithmetic and copies ran while one was open for 0% -> 0% of each run, Pallas kernels for 5% -> 8%
where the time goes in v21:
time: 103 us; the launch traced here: 102 us
  starting transfers between devices  61.8 us (60%)
  waiting for transfers between devices  25.8 us (25%)
  Pallas kernels  11.4 us (11%)
  local copies, waits for them, and re-layouts  1.71 us (2%)
    ppermute x5, starting transfers between devices, along_y(): lax.ppermute(block, 'col', [(i, i - i % 4 + (i + k) % 4) for i in range(n...  17.1 us
    ppermute x5, waiting for transfers between devices, along_y(): lax.ppermute(block, 'col', [(i, i - i % 4 + (i + k) % 4) for i in range(n...  17 us
    all_to_all x1, starting transfers between devices, body(): first = lax.all_to_all(payload, 'row', 0, 0)  15.1 us
    pallas_call x7, Pallas kernels, call(): pl.pallas_call(kernel, out_shape=outs, in_specs=places, out_specs=[VMEM]...  11.4 us
    ppermute x3, starting transfers between devices, body(): lax.ppermute(right, 'row', [(i, (i + j) % n_row) for i in range(n_row)])  10.7 us
    ppermute x3, waiting for transfers between devices, body(): lax.ppermute(right, 'row', [(i, (i + j) % n_row) for i in range(n_row)])  8.6 us
    all_to_all x1, starting transfers between devices, body(): lax.all_to_all(send.reshape((n_grp * n_col,) + send.shape[2:]), ('grp', '...  5.72 us
    all_to_all x1, starting transfers between devices, body(): term = lax.all_to_all(term, 'grp', 0, 0)  4.92 us
  transfers between devices with their start and end apart: 13, of which 7 were waited for; matrix products, arithmetic and copies ran while one was open for 0% of the time, Pallas kernels for 8%

profile of v21, /device:TPU:1, one launch (start us, length us, event | category | flops | bytes accessed | tf_op | source)
XLA Modules:
  0.0 102.4 jit_solution(17434561997538417351)
XLA Ops:
  0.6 1.0 copy-done.1
  1.6 0.7 copy-done.3
  2.3 0.7 shard_map.77.gy_ref
  3.0 4.0 %collective-permute-start = (bf16[64,1536]{1,0:T(8,128)(2,1)S(1)}, bf16[64,1536]{1,0:T(8,128)(2,1)S(1)}, u32[]{:S(2)}, u32[]{:S(2)}) collective-permute-start(bf16[64,1536]{1,0:T(8,128)(2,1)S(1)} %shard_map.77.gy_ref), channel_id=1, source_target_pairs={{0,4},{1,5},{2,6},{3,7},{4,0},{5,1},{6,2},{7,3},{8,12},{9,13},{10,... | collective-permute-start | bytes 589832 | tf_op jit(solution)/shard_map/ppermute | solution.py:257
  7.0 3.6 %shard_map.76 = bf16[16,120,128]{2,1,0:T(8,128)(2,1)} custom-call(s32[32]{0:T(128)} %picks.5, bf16[128,384]{1,0:T(8,128)(2,1)} %x_ref.1, bf16[1536,384]{1,0:T(8,128)(2,1)} %a_hbm.1), custom_call_target="tpu_custom_call" | custom-call | flops 150994944 | bytes 1769600 | tf_op jit(solution)/shard_map/pallas_call | solution.py:24
  10.6 0.0 copy-start.2
  10.6 15.1 %all-to-all-start = ((bf16[16,120,128]{2,1,0:T(8,128)(2,1)}), bf16[16,120,128]{2,1,0:T(8,128)(2,1)S(1)}, u32[]{:S(2)}, u32[]{:S(2)}) async-start(bf16[16,120,128]{2,1,0:T(8,128)(2,1)} %shard_map.76), calls=%async_computation | async-start | bytes 983040 | tf_op jit(solution)/shard_map/all_to_all | solution.py:244
  25.7 0.0 copy-start
  25.8 4.8 %collective-permute-start.3 = (bf16[128,1536]{1,0:T(8,128)(2,1)S(1)}, bf16[128,1536]{1,0:T(8,128)(2,1)S(1)}, u32[]{:S(2)}, u32[]{:S(2)}) collective-permute-start(bf16[128,1536]{1,0:T(8,128)(2,1)S(1)} %pad_maximum_fusion.refs_0_), channel_id=1, source_target_pairs={{0,3},{1,0},{2,1},{3,2},{4,7},{5,4},{6,5},{7,6},{8,11},{9,8},{10,9... | collective-permute-start | bytes 1179656 | tf_op jit(solution)/shard_map/ppermute | solution.py:247
  30.6 1.9 %collective-permute-start.1 = (bf16[64,1536]{1,0:T(8,128)(2,1)S(1)}, bf16[64,1536]{1,0:T(8,128)(2,1)S(1)}, u32[]{:S(2)}, u32[]{:S(2)}) collective-permute-start(bf16[64,1536]{1,0:T(8,128)(2,1)S(1)} %pad_maximum_fusion.1), channel_id=1, source_target_pairs={{0,1},{1,2},{2,3},{3,0},{4,5},{5,6},{6,7},{7,4},{8,9},{9,10},{10,1... | collective-permute-start | bytes 589832 | tf_op jit(solution)/shard_map/ppermute | solution.py:247
  32.5 3.5 %collective-permute-start.2 = (bf16[64,1536]{1,0:T(8,128)(2,1)S(1)}, bf16[64,1536]{1,0:T(8,128)(2,1)S(1)}, u32[]{:S(2)}, u32[]{:S(2)}) collective-permute-start(bf16[64,1536]{1,0:T(8,128)(2,1)S(1)} %pad_maximum_fusion.1), channel_id=1, source_target_pairs={{0,2},{1,3},{2,0},{3,1},{4,6},{5,7},{6,4},{7,5},{8,10},{9,11},{10,... | collective-permute-start | bytes 589832 | tf_op jit(solution)/shard_map/ppermute | solution.py:247
  36.1 1.0 shard_map.79.side_ref
  37.1 1.5 %collective-permute-done.1.refs_1_ = bf16[64,1536]{1,0:T(8,128)(2,1)S(1)} collective-permute-done((bf16[64,1536]{1,0:T(8,128)(2,1)S(1)}, bf16[64,1536]{1,0:T(8,128)(2,1)S(1)}, u32[]{:S(2)}, u32[]{:S(2)}) %collective-permute-start.1) | collective-permute-done | bytes 196640 | tf_op jit(solution)/shard_map/ppermute | solution.py:247
  38.6 4.2 %collective-permute-done.2.refs_2_ = bf16[64,1536]{1,0:T(8,128)(2,1)S(1)} collective-permute-done((bf16[64,1536]{1,0:T(8,128)(2,1)S(1)}, bf16[64,1536]{1,0:T(8,128)(2,1)S(1)}, u32[]{:S(2)}, u32[]{:S(2)}) %collective-permute-start.2) | collective-permute-done | bytes 196640 | tf_op jit(solution)/shard_map/ppermute | solution.py:247
  42.8 1.9 %shard_map.78 = (bf16[128,768]{1,0:T(8,128)(2,1)S(1)}, bf16[128,768]{1,0:T(8,128)(2,1)S(1)}) custom-call(bf16[1536,768]{1,0:T(8,128)(2,1)S(1)} %copy-done, bf16[128,1536]{1,0:T(8,128)(2,1)S(1)} %pad_maximum_fusion.refs_0_, bf16[64,1536]{1,0:T(8,128)(2,1)S(1)} %collective-permute-done.1.refs_1_, bf16[64,1536]{1,0:T(8,128)(2,1)S(1)} %collective-permute-done.2.refs_2_, ...), custom_call_target="tpu_custom_call" | custom-call | flops 603979776 | bytes 3932160 | tf_op jit(solution)/shard_map/pallas_call | solution.py:24
  44.7 4.4 %collective-permute-start.4 = (bf16[128,768]{1,0:T(8,128)(2,1)S(1)}, bf16[128,768]{1,0:T(8,128)(2,1)S(1)}, u32[]{:S(2)}, u32[]{:S(2)}) collective-permute-start(bf16[128,768]{1,0:T(8,128)(2,1)S(1)} %get-tuple-element.12), channel_id=1, source_target_pairs={{0,128},{128,0},{256,384},{384,256},{1,129},{129,1},{257,385},{385... | collective-permute-start | bytes 589832 | tf_op jit(solution)/shard_map/ppermute | solution.py:279
  49.1 2.5 %collective-permute-start.5 = (bf16[64,1536]{1,0:T(8,128)(2,1)S(1)}, bf16[64,1536]{1,0:T(8,128)(2,1)S(1)}, u32[]{:S(2)}, u32[]{:S(2)}) collective-permute-start(bf16[64,1536]{1,0:T(8,128)(2,1)S(1)} %pad_maximum_fusion.2), channel_id=1, source_target_pairs={{0,1},{1,2},{2,3},{3,0},{4,5},{5,6},{6,7},{7,4},{8,9},{9,10},{10,1... | collective-permute-start | bytes 589832 | tf_op jit(solution)/shard_map/ppermute | solution.py:247
  51.7 7.0 %collective-permute-done.5.refs_1_ = bf16[64,1536]{1,0:T(8,128)(2,1)S(1)} collective-permute-done((bf16[64,1536]{1,0:T(8,128)(2,1)S(1)}, bf16[64,1536]{1,0:T(8,128)(2,1)S(1)}, u32[]{:S(2)}, u32[]{:S(2)}) %collective-permute-start.5) | collective-permute-done | bytes 196640 | tf_op jit(solution)/shard_map/ppermute | solution.py:247
  58.7 1.3 %shard_map.80 = bf16[4,8,160,128]{3,2,1,0:T(8,128)(2,1)} custom-call(bf16[16,120,128]{2,1,0:T(8,128)(2,1)S(1)} %all-to-all-done.got_ref, bf16[8,64,128]{2,1,0:T(8,128)(2,1)S(1)} %shard_map.79.side_ref), custom_call_target="tpu_custom_call" | custom-call | flops 1000000 | bytes 1933312 | tf_op jit(solution)/shard_map/pallas_call | solution.py:24
  60.0 5.7 %all-to-all-start.1 = ((bf16[32,160,128]{2,1,0:T(8,128)(2,1)}), bf16[32,160,128]{2,1,0:T(8,128)(2,1)S(1)}, u32[]{:S(2)}, u32[]{:S(2)}) async-start(bf16[32,160,128]{2,1,0:T(8,128)(2,1)} %bitcast), calls=%async_computation.1 | async-start | bytes 2621440 | tf_op jit(solution)/shard_map/all_to_all | solution.py:298
  65.7 4.2 %collective-permute-start.6 = (bf16[128,768]{1,0:T(8,128)(2,1)S(1)}, bf16[128,768]{1,0:T(8,128)(2,1)S(1)}, u32[]{:S(2)}, u32[]{:S(2)}) collective-permute-start(bf16[128,768]{1,0:T(8,128)(2,1)S(1)} %add_convert_fusion.refs_0_), channel_id=1, source_target_pairs={{0,16},{8,24},{16,32},{24,40},{32,48},{40,56},{48,64},{56,72},{64,... | collective-permute-start | bytes 589832 | tf_op jit(solution)/shard_map/ppermute | solution.py:283
  69.9 3.1 %collective-permute-start.7 = (bf16[128,768]{1,0:T(8,128)(2,1)S(1)}, bf16[128,768]{1,0:T(8,128)(2,1)S(1)}, u32[]{:S(2)}, u32[]{:S(2)}) collective-permute-start(bf16[128,768]{1,0:T(8,128)(2,1)S(1)} %add_convert_fusion.refs_0_), channel_id=1, source_target_pairs={{0,8},{8,16},{16,24},{24,32},{32,40},{40,48},{48,56},{56,64},{64,7... | collective-permute-start | bytes 589832 | tf_op jit(solution)/shard_map/ppermute | solution.py:283
  73.0 3.4 %collective-permute-start.8 = (bf16[128,768]{1,0:T(8,128)(2,1)S(1)}, bf16[128,768]{1,0:T(8,128)(2,1)S(1)}, u32[]{:S(2)}, u32[]{:S(2)}) collective-permute-start(bf16[128,768]{1,0:T(8,128)(2,1)S(1)} %add_convert_fusion.refs_0_), channel_id=1, source_target_pairs={{0,120},{8,0},{16,8},{24,16},{32,24},{40,32},{48,40},{56,48},{64,5... | collective-permute-start | bytes 589832 | tf_op jit(solution)/shard_map/ppermute | solution.py:283
  76.4 1.6 %collective-permute-done.6.refs_1_ = bf16[128,768]{1,0:T(8,128)(2,1)S(1)} collective-permute-done((bf16[128,768]{1,0:T(8,128)(2,1)S(1)}, bf16[128,768]{1,0:T(8,128)(2,1)S(1)}, u32[]{:S(2)}, u32[]{:S(2)}) %collective-permute-start.6) | collective-permute-done | bytes 196640 | tf_op jit(solution)/shard_map/ppermute | solution.py:283
  78.1 7.0 %collective-permute-done.7.refs_2_ = bf16[128,768]{1,0:T(8,128)(2,1)S(1)} collective-permute-done((bf16[128,768]{1,0:T(8,128)(2,1)S(1)}, bf16[128,768]{1,0:T(8,128)(2,1)S(1)}, u32[]{:S(2)}, u32[]{:S(2)}) %collective-permute-start.7) | collective-permute-done | bytes 196640 | tf_op jit(solution)/shard_map/ppermute | solution.py:283
  85.0 1.5 %shard_map.81 = bf16[4,96,768]{2,1,0:T(8,128)(2,1)} custom-call(bf16[4,8,160,128]{3,2,1,0:T(8,128)(2,1)S(1)} %bitcast.2, bf16[128,768]{1,0:T(8,128)(2,1)S(1)} %add_convert_fusion.refs_0_, bf16[128,768]{1,0:T(8,128)(2,1)S(1)} %collective-permute-done.6.refs_1_, bf16[128,768]{1,0:T(8,128)(2,1)S(1)} %collective-permute-done.7.refs_2_, ...), custom_call_target="tpu_custom_call" | custom-call | flops 402653184 | bytes 2686976 | tf_op jit(solution)/shard_map/pallas_call | solution.py:24
  86.5 4.9 %all-to-all-start.2 = ((bf16[4,96,768]{2,1,0:T(8,128)(2,1)}), bf16[4,96,768]{2,1,0:T(8,128)(2,1)S(1)}, u32[]{:S(2)}, u32[]{:S(2)}) async-start(bf16[4,96,768]{2,1,0:T(8,128)(2,1)} %shard_map.81), calls=%async_computation.2 | async-start | bytes 1179648 | tf_op jit(solution)/shard_map/all_to_all | solution.py:309
  91.4 4.3 %collective-permute-start.9 = (bf16[64,1536]{1,0:T(8,128)(2,1)S(1)}, bf16[64,1536]{1,0:T(8,128)(2,1)S(1)}, u32[]{:S(2)}, u32[]{:S(2)}) collective-permute-start(bf16[64,1536]{1,0:T(8,128)(2,1)S(1)} %slice.24), channel_id=1, source_target_pairs={{0,3},{1,0},{2,1},{3,2},{4,7},{5,4},{6,5},{7,6},{8,11},{9,8},{10,9... | collective-permute-start | bytes 589832 | tf_op jit(solution)/shard_map/ppermute | solution.py:247
  95.8 4.3 %collective-permute-done.9.refs_2_ = bf16[64,1536]{1,0:T(8,128)(2,1)S(1)} collective-permute-done((bf16[64,1536]{1,0:T(8,128)(2,1)S(1)}, bf16[64,1536]{1,0:T(8,128)(2,1)S(1)}, u32[]{:S(2)}, u32[]{:S(2)}) %collective-permute-start.9) | collective-permute-done | bytes 196640 | tf_op jit(solution)/shard_map/ppermute | solution.py:247
  100.1 1.4 %shard_map.82 = (f32[48,1536]{1,0:T(8,128)}, f32[48,1536]{1,0:T(8,128)}) custom-call(bf16[4,8,160,128]{3,2,1,0:T(8,128)(2,1)S(1)} %bitcast.3, bf16[128,1536]{1,0:T(8,128)(2,1)S(1)} %pad_maximum_fusion.refs_0_, bf16[64,1536]{1,0:T(8,128)(2,1)S(1)} %collective-permute-done.5.refs_1_, bf16[64,1536]{1,0:T(8,128)(2,1)S(1)} %collective-permute-done.9.refs_2_, ...), custom_call_target="tpu_custom_call" | custom-call | flops 201326592 | bytes 3080192 | tf_op jit(solution)/shard_map/pallas_call | solution.py:24
  101.5 0.1 all-to-all-done.2
  101.6 0.8 convert_reduce_fusion
  (19 shorter events, 0.2 us)
Async XLA Ops:
  0.6 1.0 copy-start.1
  1.6 0.7 copy-start.3
  3.0 22.7 %collective-permute-start = (bf16[64,1536]{1,0:T(8,128)(2,1)S(1)}, bf16[64,1536]{1,0:T(8,128)(2,1)S(1)}, u32[]{:S(2)}, u32[]{:S(2)}) collective-permute-start(bf16[64,1536]{1,0:T(8,128)(2,1)S(1)} %shard_map.77.gy_ref), channel_id=1, source_target_pairs={{0,4},{1,5},{2,6},{3,7},{4,0},{5,1},{6,2},{7,3},{8,12},{9,13},{10,... | collective-permute-start | bytes 589832 | tf_op jit(solution)/shard_map/ppermute | solution.py:257
  10.6 25.5 %copy-start.2 = (bf16[128,384]{1,0:T(8,128)(2,1)S(1)}, bf16[128,384]{1,0:T(8,128)(2,1)}, u32[]{:S(2)}) copy-start(bf16[128,384]{1,0:T(8,128)(2,1)} %x_ref.1) | copy-start | bytes 294916
  10.6 25.5 %copy-start.4 = (s32[32]{0:T(128)S(1)}, s32[32]{0:T(128)}, u32[]{:S(2)}) copy-start(s32[32]{0:T(128)} %picks.5) | copy-start | bytes 388
  10.6 48.1 %all-to-all-start = ((bf16[16,120,128]{2,1,0:T(8,128)(2,1)}), bf16[16,120,128]{2,1,0:T(8,128)(2,1)S(1)}, u32[]{:S(2)}, u32[]{:S(2)}) async-start(bf16[16,120,128]{2,1,0:T(8,128)(2,1)} %shard_map.76), calls=%async_computation | async-start | bytes 983040 | tf_op jit(solution)/shard_map/all_to_all | solution.py:244
  25.7 17.1 %copy-start = (bf16[1536,768]{1,0:T(8,128)(2,1)S(1)}, bf16[1536,768]{1,0:T(8,128)(2,1)}, u32[]{:S(2)}) copy-start(bf16[1536,768]{1,0:T(8,128)(2,1)} %b_hbm.1) | copy-start | bytes 7077892
  25.8 17.0 %collective-permute-start.3 = (bf16[128,1536]{1,0:T(8,128)(2,1)S(1)}, bf16[128,1536]{1,0:T(8,128)(2,1)S(1)}, u32[]{:S(2)}, u32[]{:S(2)}) collective-permute-start(bf16[128,1536]{1,0:T(8,128)(2,1)S(1)} %pad_maximum_fusion.refs_0_), channel_id=1, source_target_pairs={{0,3},{1,0},{2,1},{3,2},{4,7},{5,4},{6,5},{7,6},{8,11},{9,8},{10,9... | collective-permute-start | bytes 1179656 | tf_op jit(solution)/shard_map/ppermute | solution.py:247
  30.6 8.0 %collective-permute-start.1 = (bf16[64,1536]{1,0:T(8,128)(2,1)S(1)}, bf16[64,1536]{1,0:T(8,128)(2,1)S(1)}, u32[]{:S(2)}, u32[]{:S(2)}) collective-permute-start(bf16[64,1536]{1,0:T(8,128)(2,1)S(1)} %pad_maximum_fusion.1), channel_id=1, source_target_pairs={{0,1},{1,2},{2,3},{3,0},{4,5},{5,6},{6,7},{7,4},{8,9},{9,10},{10,1... | collective-permute-start | bytes 589832 | tf_op jit(solution)/shard_map/ppermute | solution.py:247
  32.5 10.2 %collective-permute-start.2 = (bf16[64,1536]{1,0:T(8,128)(2,1)S(1)}, bf16[64,1536]{1,0:T(8,128)(2,1)S(1)}, u32[]{:S(2)}, u32[]{:S(2)}) collective-permute-start(bf16[64,1536]{1,0:T(8,128)(2,1)S(1)} %pad_maximum_fusion.1), channel_id=1, source_target_pairs={{0,2},{1,3},{2,0},{3,1},{4,6},{5,7},{6,4},{7,5},{8,10},{9,11},{10,... | collective-permute-start | bytes 589832 | tf_op jit(solution)/shard_map/ppermute | solution.py:247
  44.7 7.0 %collective-permute-start.4 = (bf16[128,768]{1,0:T(8,128)(2,1)S(1)}, bf16[128,768]{1,0:T(8,128)(2,1)S(1)}, u32[]{:S(2)}, u32[]{:S(2)}) collective-permute-start(bf16[128,768]{1,0:T(8,128)(2,1)S(1)} %get-tuple-element.12), channel_id=1, source_target_pairs={{0,128},{128,0},{256,384},{384,256},{1,129},{129,1},{257,385},{385... | collective-permute-start | bytes 589832 | tf_op jit(solution)/shard_map/ppermute | solution.py:279
  49.1 9.6 %collective-permute-start.5 = (bf16[64,1536]{1,0:T(8,128)(2,1)S(1)}, bf16[64,1536]{1,0:T(8,128)(2,1)S(1)}, u32[]{:S(2)}, u32[]{:S(2)}) collective-permute-start(bf16[64,1536]{1,0:T(8,128)(2,1)S(1)} %pad_maximum_fusion.2), channel_id=1, source_target_pairs={{0,1},{1,2},{2,3},{3,0},{4,5},{5,6},{6,7},{7,4},{8,9},{9,10},{10,1... | collective-permute-start | bytes 589832 | tf_op jit(solution)/shard_map/ppermute | solution.py:247
  60.0 25.0 %all-to-all-start.1 = ((bf16[32,160,128]{2,1,0:T(8,128)(2,1)}), bf16[32,160,128]{2,1,0:T(8,128)(2,1)S(1)}, u32[]{:S(2)}, u32[]{:S(2)}) async-start(bf16[32,160,128]{2,1,0:T(8,128)(2,1)} %bitcast), calls=%async_computation.1 | async-start | bytes 2621440 | tf_op jit(solution)/shard_map/all_to_all | solution.py:298
  65.7 12.3 %collective-permute-start.6 = (bf16[128,768]{1,0:T(8,128)(2,1)S(1)}, bf16[128,768]{1,0:T(8,128)(2,1)S(1)}, u32[]{:S(2)}, u32[]{:S(2)}) collective-permute-start(bf16[128,768]{1,0:T(8,128)(2,1)S(1)} %add_convert_fusion.refs_0_), channel_id=1, source_target_pairs={{0,16},{8,24},{16,32},{24,40},{32,48},{40,56},{48,64},{56,72},{64,... | collective-permute-start | bytes 589832 | tf_op jit(solution)/shard_map/ppermute | solution.py:283
  69.9 15.1 %collective-permute-start.7 = (bf16[128,768]{1,0:T(8,128)(2,1)S(1)}, bf16[128,768]{1,0:T(8,128)(2,1)S(1)}, u32[]{:S(2)}, u32[]{:S(2)}) collective-permute-start(bf16[128,768]{1,0:T(8,128)(2,1)S(1)} %add_convert_fusion.refs_0_), channel_id=1, source_target_pairs={{0,8},{8,16},{16,24},{24,32},{32,40},{40,48},{48,56},{56,64},{64,7... | collective-permute-start | bytes 589832 | tf_op jit(solution)/shard_map/ppermute | solution.py:283
  73.0 12.0 %collective-permute-start.8 = (bf16[128,768]{1,0:T(8,128)(2,1)S(1)}, bf16[128,768]{1,0:T(8,128)(2,1)S(1)}, u32[]{:S(2)}, u32[]{:S(2)}) collective-permute-start(bf16[128,768]{1,0:T(8,128)(2,1)S(1)} %add_convert_fusion.refs_0_), channel_id=1, source_target_pairs={{0,120},{8,0},{16,8},{24,16},{32,24},{40,32},{48,40},{56,48},{64,5... | collective-permute-start | bytes 589832 | tf_op jit(solution)/shard_map/ppermute | solution.py:283
  86.5 15.1 %all-to-all-start.2 = ((bf16[4,96,768]{2,1,0:T(8,128)(2,1)}), bf16[4,96,768]{2,1,0:T(8,128)(2,1)S(1)}, u32[]{:S(2)}, u32[]{:S(2)}) async-start(bf16[4,96,768]{2,1,0:T(8,128)(2,1)} %shard_map.81), calls=%async_computation.2 | async-start | bytes 1179648 | tf_op jit(solution)/shard_map/all_to_all | solution.py:309
  91.4 8.6 %collective-permute-start.9 = (bf16[64,1536]{1,0:T(8,128)(2,1)S(1)}, bf16[64,1536]{1,0:T(8,128)(2,1)S(1)}, u32[]{:S(2)}, u32[]{:S(2)}) collective-permute-start(bf16[64,1536]{1,0:T(8,128)(2,1)S(1)} %slice.24), channel_id=1, source_target_pairs={{0,3},{1,0},{2,1},{3,2},{4,7},{5,4},{6,5},{7,6},{8,11},{9,8},{10,9... | collective-permute-start | bytes 589832 | tf_op jit(solution)/shard_map/ppermute | solution.py:247

commit v22 on v18

--- a/solution.py
+++ b/solution.py
@@ -253,16 +253,15 @@
         (sample_rows, cotangent),
         [shape((2 * size + samp, feat_grp), BF)],
         2 * 64 * tok * feat_grp,
-        limit=56,
     )[0]
     beside = lax.ppermute(picked, "col", [(i, (i + 4) % n_col) for i in range(n_col)])
     cut = 2 * size
-    kinds = (picked[:cut], beside[:cut], picked[cut:], beside[cut:])
-    pair = jnp.concatenate(kinds, axis=0)
-    near = {k: along_y(pair, k) for k in (1, 3)}
-    far_rows = along_y(near[1][: 2 * cut], 1)
-    far_samples = along_y(near[3][2 * cut :], 3)
-    pairs = [pair, near[1], far_rows, near[3]]
+    rows = jnp.concatenate([picked[:cut], beside[:cut]], axis=0)
+    samples = jnp.concatenate([picked[cut:], beside[cut:]], axis=0)
+    pair = jnp.concatenate([rows, samples], axis=0)
+    after = along_y(pair, 3)
+    before = along_y(pair, 1)
+    pairs = [pair, before, along_y(rows, 2), after]
     keep, give = call(
         right_kernel,
         (grad_inverse, *pairs),
@@ -278,7 +277,7 @@
     taken = lax.ppermute(give, "grp", [(i, i ^ 1) for i in range(n_grp)])
     some = keep.astype(F32) + taken.astype(F32)
     give = some.astype(BF)
-    first, give, far_samples = lax.optimization_barrier((first, give, far_samples))
+    first, give = lax.optimization_barrier((first, give))
     taken = lax.ppermute(give, "grp", [(i, i ^ 2) for i in range(n_grp)])
     right = (some + taken.astype(F32)).astype(BF)
     side = call(
@@ -300,6 +299,10 @@
         lax.ppermute(right, "row", [(i, (i + j) % n_row) for i in range(n_row)])
         for j in SHIFTS[1:]
     ]
+    unused, beyond = lax.optimization_barrier((rights[1], after[2 * cut :]))
+    far = along_y(beyond, 3)
+
+    rights, far = lax.optimization_barrier((rights, far))
     term, give = call(
         final_kernel,
         (got, *rights),
@@ -312,7 +315,7 @@
     got, unused = lax.optimization_barrier((got, give))
     act_cov, grad_cov = call(
         factor_kernel,
-        (got, pair, near[1], far_samples, near[3]),
+        (got, pair, before, far, after),
         [shape((tile, feat_grp), F32)] * 2,
         4 * LANES * samp * n_col * feat_grp,
     )

time: 106 us -> 101 us (0.953)
  waiting for transfers between devices: 30.8 us -> 19.8 us
  starting transfers between devices: 59 us -> 67.7 us
  local copies, waits for them, and re-layouts: 1.74 us -> 0.06 us
    ppermute x4, waiting for transfers between devices: 18.2 us -> 7.68 us  [along_y(): lax.ppermute(block, 'col', [(i, i - i % 4 + (i + k) % 4) for i in range(n...]
    ppermute x3, waiting for transfers between devices: 10.1 us -> 4.24 us  [body(): lax.ppermute(right, 'row', [(i, (i + j) % n_row) for i in range(n_row)])]
    ppermute x1, waiting for transfers between devices: 0.01 us -> 4.2 us  [body(): lax.ppermute(picked, 'col', [(i, (i + 4) % n_col) for i in range(n_col)])]
    ppermute x4, starting transfers between devices: 10.8 us -> 14.6 us  [along_y(): lax.ppermute(block, 'col', [(i, i - i % 4 + (i + k) % 4) for i in range(n...]
    ppermute x2, starting transfers between devices: 8.46 us -> 10.4 us  [body(): taken = lax.ppermute(give, 'grp', [(i, i ^ 1) for i in range(n_grp)])]
    all_to_all x1, starting transfers between devices: 7.02 us -> 8.78 us  [body(): lax.all_to_all(send.reshape((n_grp * n_col,) + send.shape[2:]), ('grp', '...]
    unnamed x8, local copies, waits for them, and re-layouts: 1.68 us -> 0.02 us
  transfers between devices with their start and end apart: 13 -> 13, of which waited for: 6 -> 7; matrix products, arithmetic and copies ran while one was open for 0% -> 0% of each run, Pallas kernels for 9% -> 6%
where the time goes in v22:
time: 101 us; the launch traced here: 99.8 us
  starting transfers between devices  67.7 us (67%)
  waiting for transfers between devices  19.8 us (20%)
  Pallas kernels  10.5 us (10%)
    all_to_all x1, starting transfers between devices, body(): first = lax.all_to_all(payload, 'row', 0, 0)  15.8 us
    ppermute x4, starting transfers between devices, along_y(): lax.ppermute(block, 'col', [(i, i - i % 4 + (i + k) % 4) for i in range(n...  14.6 us
    pallas_call x7, Pallas kernels, call(): pl.pallas_call(kernel, out_shape=outs, in_specs=places, out_specs=[VMEM]...  10.5 us
    ppermute x2, starting transfers between devices, body(): taken = lax.ppermute(give, 'grp', [(i, i ^ 1) for i in range(n_grp)])  10.4 us
    ppermute x3, starting transfers between devices, body(): lax.ppermute(right, 'row', [(i, (i + j) % n_row) for i in range(n_row)])  10.4 us
    all_to_all x1, starting transfers between devices, body(): lax.all_to_all(send.reshape((n_grp * n_col,) + send.shape[2:]), ('grp', '...  8.78 us
    ppermute x4, waiting for transfers between devices, along_y(): lax.ppermute(block, 'col', [(i, i - i % 4 + (i + k) % 4) for i in range(n...  7.68 us
    ppermute x1, starting transfers between devices, body(): taken = lax.ppermute(give, 'grp', [(i, i ^ 2) for i in range(n_grp)])  4.66 us
  transfers between devices with their start and end apart: 13, of which 7 were waited for; matrix products, arithmetic and copies ran while one was open for 0% of the time, Pallas kernels for 6%

profile of v22, /device:TPU:1, one launch (start us, length us, event | category | flops | bytes accessed | tf_op | source)
XLA Modules:
  0.0 99.8 jit_solution(12930436267554813514)
XLA Ops:
  0.7 3.7 %shard_map.76 = bf16[16,120,128]{2,1,0:T(8,128)(2,1)} custom-call(s32[32]{0:T(128)} %picks.5, bf16[128,384]{1,0:T(8,128)(2,1)} %x_ref.1, bf16[1536,384]{1,0:T(8,128)(2,1)} %a_hbm.1), custom_call_target="tpu_custom_call" | custom-call | flops 150994944 | bytes 1769600 | tf_op jit(solution)/shard_map/pallas_call | solution.py:24
  4.4 15.8 %all-to-all-start = ((bf16[16,120,128]{2,1,0:T(8,128)(2,1)}), bf16[16,120,128]{2,1,0:T(8,128)(2,1)S(1)}, u32[]{:S(2)}, u32[]{:S(2)}) async-start(bf16[16,120,128]{2,1,0:T(8,128)(2,1)} %shard_map.76), calls=%async_computation | async-start | bytes 983040 | tf_op jit(solution)/shard_map/all_to_all | solution.py:244
  20.2 0.0 copy-start
  20.2 0.7 shard_map.77.gy_ref
  20.9 3.1 %collective-permute-start = (bf16[64,1536]{1,0:T(8,128)(2,1)S(1)}, bf16[64,1536]{1,0:T(8,128)(2,1)S(1)}, u32[]{:S(2)}, u32[]{:S(2)}) collective-permute-start(bf16[64,1536]{1,0:T(8,128)(2,1)S(1)} %shard_map.77.gy_ref), channel_id=1, source_target_pairs={{0,4},{1,5},{2,6},{3,7},{4,0},{5,1},{6,2},{7,3},{8,12},{9,13},{10,... | collective-permute-start | bytes 589832 | tf_op jit(solution)/shard_map/ppermute | solution.py:257
  24.1 4.2 %collective-permute-done = bf16[64,1536]{1,0:T(8,128)(2,1)S(1)} collective-permute-done((bf16[64,1536]{1,0:T(8,128)(2,1)S(1)}, bf16[64,1536]{1,0:T(8,128)(2,1)S(1)}, u32[]{:S(2)}, u32[]{:S(2)}) %collective-permute-start) | collective-permute-done | bytes 196640 | tf_op jit(solution)/shard_map/ppermute | solution.py:257
  28.3 3.2 %collective-permute-start.1 = (bf16[128,1536]{1,0:T(8,128)(2,1)S(1)}, bf16[128,1536]{1,0:T(8,128)(2,1)S(1)}, u32[]{:S(2)}, u32[]{:S(2)}) collective-permute-start(bf16[128,1536]{1,0:T(8,128)(2,1)S(1)} %pad_maximum_fusion.refs_0_), channel_id=1, source_target_pairs={{0,1},{1,2},{2,3},{3,0},{4,5},{5,6},{6,7},{7,4},{8,9},{9,10},{10,1... | collective-permute-start | bytes 1179656 | tf_op jit(solution)/shard_map/ppermute | solution.py:247
  31.5 3.3 %collective-permute-start.3 = (bf16[128,1536]{1,0:T(8,128)(2,1)S(1)}, bf16[128,1536]{1,0:T(8,128)(2,1)S(1)}, u32[]{:S(2)}, u32[]{:S(2)}) collective-permute-start(bf16[128,1536]{1,0:T(8,128)(2,1)S(1)} %pad_maximum_fusion.refs_0_), channel_id=1, source_target_pairs={{0,3},{1,0},{2,1},{3,2},{4,7},{5,4},{6,5},{7,6},{8,11},{9,8},{10,9... | collective-permute-start | bytes 1179656 | tf_op jit(solution)/shard_map/ppermute | solution.py:247
  34.9 0.0 copy-start.2
  34.9 3.7 %collective-permute-start.2 = (bf16[64,1536]{1,0:T(8,128)(2,1)S(1)}, bf16[64,1536]{1,0:T(8,128)(2,1)S(1)}, u32[]{:S(2)}, u32[]{:S(2)}) collective-permute-start(bf16[64,1536]{1,0:T(8,128)(2,1)S(1)} %pad_maximum_fusion.1), channel_id=1, source_target_pairs={{0,2},{1,3},{2,0},{3,1},{4,6},{5,7},{6,4},{7,5},{8,10},{9,11},{10,... | collective-permute-start | bytes 589832 | tf_op jit(solution)/shard_map/ppermute | solution.py:247
  38.6 7.0 %collective-permute-done.2.refs_2_ = bf16[64,1536]{1,0:T(8,128)(2,1)S(1)} collective-permute-done((bf16[64,1536]{1,0:T(8,128)(2,1)S(1)}, bf16[64,1536]{1,0:T(8,128)(2,1)S(1)}, u32[]{:S(2)}, u32[]{:S(2)}) %collective-permute-start.2) | collective-permute-done | bytes 196640 | tf_op jit(solution)/shard_map/ppermute | solution.py:247
  45.6 0.0 collective-permute-done.1.refs_1_
  45.6 1.9 %shard_map.78 = (bf16[128,768]{1,0:T(8,128)(2,1)S(1)}, bf16[128,768]{1,0:T(8,128)(2,1)S(1)}) custom-call(bf16[1536,768]{1,0:T(8,128)(2,1)S(1)} %copy-done, bf16[128,1536]{1,0:T(8,128)(2,1)S(1)} %pad_maximum_fusion.refs_0_, bf16[128,1536]{1,0:T(8,128)(2,1)S(1)} %collective-permute-done.1.refs_1_, bf16[64,1536]{1,0:T(8,128)(2,1)S(1)} %collective-permute-done.2.refs_2_, ...), custom_call_target="tpu_custom_call" | custom-call | flops 603979776 | bytes 4128768 | tf_op jit(solution)/shard_map/pallas_call | solution.py:24
  47.6 4.7 %collective-permute-start.4 = (bf16[128,768]{1,0:T(8,128)(2,1)S(1)}, bf16[128,768]{1,0:T(8,128)(2,1)S(1)}, u32[]{:S(2)}, u32[]{:S(2)}) collective-permute-start(bf16[128,768]{1,0:T(8,128)(2,1)S(1)} %get-tuple-element.21), channel_id=1, source_target_pairs={{0,128},{128,0},{256,384},{384,256},{1,129},{129,1},{257,385},{385... | collective-permute-start | bytes 589832 | tf_op jit(solution)/shard_map/ppermute | solution.py:277
  52.3 1.0 %collective-permute-done.4 = bf16[128,768]{1,0:T(8,128)(2,1)S(1)} collective-permute-done((bf16[128,768]{1,0:T(8,128)(2,1)S(1)}, bf16[128,768]{1,0:T(8,128)(2,1)S(1)}, u32[]{:S(2)}, u32[]{:S(2)}) %collective-permute-start.4) | collective-permute-done | bytes 196640 | tf_op jit(solution)/shard_map/ppermute | solution.py:277
  53.4 4.7 %collective-permute-start.5 = (bf16[128,768]{1,0:T(8,128)(2,1)S(1)}, bf16[128,768]{1,0:T(8,128)(2,1)S(1)}, u32[]{:S(2)}, u32[]{:S(2)}) collective-permute-start(bf16[128,768]{1,0:T(8,128)(2,1)S(1)} %fusion), channel_id=1, source_target_pairs={{0,256},{128,384},{256,0},{384,128},{1,257},{129,385},{257,1},{385... | collective-permute-start | bytes 589832 | tf_op jit(solution)/shard_map/ppermute | solution.py:281
  58.1 1.0 shard_map.79.side_ref
  59.0 1.3 %shard_map.80 = bf16[4,8,160,128]{3,2,1,0:T(8,128)(2,1)} custom-call(bf16[16,120,128]{2,1,0:T(8,128)(2,1)S(1)} %all-to-all-done.got_ref, bf16[8,64,128]{2,1,0:T(8,128)(2,1)S(1)} %shard_map.79.side_ref), custom_call_target="tpu_custom_call" | custom-call | flops 1000000 | bytes 1933312 | tf_op jit(solution)/shard_map/pallas_call | solution.py:24
  60.3 2.6 %collective-permute-done.5 = bf16[128,768]{1,0:T(8,128)(2,1)S(1)} collective-permute-done((bf16[128,768]{1,0:T(8,128)(2,1)S(1)}, bf16[128,768]{1,0:T(8,128)(2,1)S(1)}, u32[]{:S(2)}, u32[]{:S(2)}) %collective-permute-start.5) | collective-permute-done | bytes 196640 | tf_op jit(solution)/shard_map/ppermute | solution.py:281
  62.9 0.1 add_convert_fusion.refs_0_
  63.0 8.8 %all-to-all-start.1 = ((bf16[32,160,128]{2,1,0:T(8,128)(2,1)}), bf16[32,160,128]{2,1,0:T(8,128)(2,1)S(1)}, u32[]{:S(2)}, u32[]{:S(2)}) async-start(bf16[32,160,128]{2,1,0:T(8,128)(2,1)} %bitcast), calls=%async_computation.1 | async-start | bytes 2621440 | tf_op jit(solution)/shard_map/all_to_all | solution.py:296
  71.8 3.9 %collective-permute-start.6 = (bf16[128,768]{1,0:T(8,128)(2,1)S(1)}, bf16[128,768]{1,0:T(8,128)(2,1)S(1)}, u32[]{:S(2)}, u32[]{:S(2)}) collective-permute-start(bf16[128,768]{1,0:T(8,128)(2,1)S(1)} %add_convert_fusion.refs_0_), channel_id=1, source_target_pairs={{0,16},{8,24},{16,32},{24,40},{32,48},{40,56},{48,64},{56,72},{64,... | collective-permute-start | bytes 589832 | tf_op jit(solution)/shard_map/ppermute | solution.py:299
  75.7 3.1 %collective-permute-start.7 = (bf16[128,768]{1,0:T(8,128)(2,1)S(1)}, bf16[128,768]{1,0:T(8,128)(2,1)S(1)}, u32[]{:S(2)}, u32[]{:S(2)}) collective-permute-start(bf16[128,768]{1,0:T(8,128)(2,1)S(1)} %add_convert_fusion.refs_0_), channel_id=1, source_target_pairs={{0,8},{8,16},{16,24},{24,32},{32,40},{40,48},{48,56},{56,64},{64,7... | collective-permute-start | bytes 589832 | tf_op jit(solution)/shard_map/ppermute | solution.py:299
  78.8 3.4 %collective-permute-start.8 = (bf16[128,768]{1,0:T(8,128)(2,1)S(1)}, bf16[128,768]{1,0:T(8,128)(2,1)S(1)}, u32[]{:S(2)}, u32[]{:S(2)}) collective-permute-start(bf16[128,768]{1,0:T(8,128)(2,1)S(1)} %add_convert_fusion.refs_0_), channel_id=1, source_target_pairs={{0,120},{8,0},{16,8},{24,16},{32,24},{40,32},{48,40},{56,48},{64,5... | collective-permute-start | bytes 589832 | tf_op jit(solution)/shard_map/ppermute | solution.py:299
  82.2 1.9 %collective-permute-done.6.refs_1_ = bf16[128,768]{1,0:T(8,128)(2,1)S(1)} collective-permute-done((bf16[128,768]{1,0:T(8,128)(2,1)S(1)}, bf16[128,768]{1,0:T(8,128)(2,1)S(1)}, u32[]{:S(2)}, u32[]{:S(2)}) %collective-permute-start.6) | collective-permute-done | bytes 196640 | tf_op jit(solution)/shard_map/ppermute | solution.py:299
  84.1 4.4 %collective-permute-start.9 = (bf16[64,1536]{1,0:T(8,128)(2,1)S(1)}, bf16[64,1536]{1,0:T(8,128)(2,1)S(1)}, u32[]{:S(2)}, u32[]{:S(2)}) collective-permute-start(bf16[64,1536]{1,0:T(8,128)(2,1)S(1)} %slice.24), channel_id=1, source_target_pairs={{0,3},{1,0},{2,1},{3,2},{4,7},{5,4},{6,5},{7,6},{8,11},{9,8},{10,9... | collective-permute-start | bytes 589832 | tf_op jit(solution)/shard_map/ppermute | solution.py:247
  88.4 2.3 %collective-permute-done.7.refs_2_ = bf16[128,768]{1,0:T(8,128)(2,1)S(1)} collective-permute-done((bf16[128,768]{1,0:T(8,128)(2,1)S(1)}, bf16[128,768]{1,0:T(8,128)(2,1)S(1)}, u32[]{:S(2)}, u32[]{:S(2)}) %collective-permute-start.7) | collective-permute-done | bytes 196640 | tf_op jit(solution)/shard_map/ppermute | solution.py:299
  90.8 0.7 collective-permute-done.9.refs_2_
  91.5 0.5 shard_map.81
  91.9 5.7 %collective-permute-start.10 = (bf16[96,768]{1,0:T(8,128)(2,1)S(1)}, bf16[96,768]{1,0:T(8,128)(2,1)S(1)}, u32[]{:S(2)}, u32[]{:S(2)}) collective-permute-start(bf16[96,768]{1,0:T(8,128)(2,1)S(1)} %get-tuple-element.32), channel_id=1, source_target_pairs={{0,128},{128,0},{256,384},{384,256},{1,129},{129,1},{257,385},{385... | collective-permute-start | bytes 442376 | tf_op jit(solution)/shard_map/ppermute | solution.py:313
  97.7 1.4 %shard_map.82 = (f32[48,1536]{1,0:T(8,128)}, f32[48,1536]{1,0:T(8,128)}) custom-call(bf16[4,8,160,128]{3,2,1,0:T(8,128)(2,1)S(1)} %bitcast.3, bf16[128,1536]{1,0:T(8,128)(2,1)S(1)} %pad_maximum_fusion.refs_0_, bf16[128,1536]{1,0:T(8,128)(2,1)S(1)} %collective-permute-done.1.refs_1_, bf16[64,1536]{1,0:T(8,128)(2,1)S(1)} %collective-permute-done.9.refs_2_, ...), custom_call_target="tpu_custom_call" | custom-call | flops 201326592 | bytes 3276800 | tf_op jit(solution)/shard_map/pallas_call | solution.py:24
  99.1 0.7 convert_add_fusion.1
  (17 shorter events, 0.2 us)
Async XLA Ops:
  0.6 19.5 %copy-start.3 = (s32[32]{0:T(128)S(1)}, s32[32]{0:T(128)}, u32[]{:S(2)}) copy-start(s32[32]{0:T(128)} %picks.5) | copy-start | bytes 388
  0.6 19.5 %copy-start.1 = (bf16[128,1536]{1,0:T(8,128)(2,1)S(1)}, bf16[128,1536]{1,0:T(8,128)(2,1)}, u32[]{:S(2)}) copy-start(bf16[128,1536]{1,0:T(8,128)(2,1)} %g_ref.1) | copy-start | bytes 1179652
  4.4 49.0 %all-to-all-start = ((bf16[16,120,128]{2,1,0:T(8,128)(2,1)}), bf16[16,120,128]{2,1,0:T(8,128)(2,1)S(1)}, u32[]{:S(2)}, u32[]{:S(2)}) async-start(bf16[16,120,128]{2,1,0:T(8,128)(2,1)} %shard_map.76), calls=%async_computation | async-start | bytes 983040 | tf_op jit(solution)/shard_map/all_to_all | solution.py:244
  20.2 25.5 %copy-start = (bf16[1536,768]{1,0:T(8,128)(2,1)S(1)}, bf16[1536,768]{1,0:T(8,128)(2,1)}, u32[]{:S(2)}) copy-start(bf16[1536,768]{1,0:T(8,128)(2,1)} %b_hbm.1) | copy-start | bytes 7077892
  20.9 7.3 %collective-permute-start = (bf16[64,1536]{1,0:T(8,128)(2,1)S(1)}, bf16[64,1536]{1,0:T(8,128)(2,1)S(1)}, u32[]{:S(2)}, u32[]{:S(2)}) collective-permute-start(bf16[64,1536]{1,0:T(8,128)(2,1)S(1)} %shard_map.77.gy_ref), channel_id=1, source_target_pairs={{0,4},{1,5},{2,6},{3,7},{4,0},{5,1},{6,2},{7,3},{8,12},{9,13},{10,... | collective-permute-start | bytes 589832 | tf_op jit(solution)/shard_map/ppermute | solution.py:257
  28.3 17.3 %collective-permute-start.1 = (bf16[128,1536]{1,0:T(8,128)(2,1)S(1)}, bf16[128,1536]{1,0:T(8,128)(2,1)S(1)}, u32[]{:S(2)}, u32[]{:S(2)}) collective-permute-start(bf16[128,1536]{1,0:T(8,128)(2,1)S(1)} %pad_maximum_fusion.refs_0_), channel_id=1, source_target_pairs={{0,1},{1,2},{2,3},{3,0},{4,5},{5,6},{6,7},{7,4},{8,9},{9,10},{10,1... | collective-permute-start | bytes 1179656 | tf_op jit(solution)/shard_map/ppermute | solution.py:247
  31.5 14.1 %collective-permute-start.3 = (bf16[128,1536]{1,0:T(8,128)(2,1)S(1)}, bf16[128,1536]{1,0:T(8,128)(2,1)S(1)}, u32[]{:S(2)}, u32[]{:S(2)}) collective-permute-start(bf16[128,1536]{1,0:T(8,128)(2,1)S(1)} %pad_maximum_fusion.refs_0_), channel_id=1, source_target_pairs={{0,3},{1,0},{2,1},{3,2},{4,7},{5,4},{6,5},{7,6},{8,11},{9,8},{10,9... | collective-permute-start | bytes 1179656 | tf_op jit(solution)/shard_map/ppermute | solution.py:247
  34.9 23.1 %copy-start.2 = (bf16[128,384]{1,0:T(8,128)(2,1)S(1)}, bf16[128,384]{1,0:T(8,128)(2,1)}, u32[]{:S(2)}) copy-start(bf16[128,384]{1,0:T(8,128)(2,1)} %x_ref.1) | copy-start | bytes 294916
  34.9 10.7 %collective-permute-start.2 = (bf16[64,1536]{1,0:T(8,128)(2,1)S(1)}, bf16[64,1536]{1,0:T(8,128)(2,1)S(1)}, u32[]{:S(2)}, u32[]{:S(2)}) collective-permute-start(bf16[64,1536]{1,0:T(8,128)(2,1)S(1)} %pad_maximum_fusion.1), channel_id=1, source_target_pairs={{0,2},{1,3},{2,0},{3,1},{4,6},{5,7},{6,4},{7,5},{8,10},{9,11},{10,... | collective-permute-start | bytes 589832 | tf_op jit(solution)/shard_map/ppermute | solution.py:247
  47.6 5.8 %collective-permute-start.4 = (bf16[128,768]{1,0:T(8,128)(2,1)S(1)}, bf16[128,768]{1,0:T(8,128)(2,1)S(1)}, u32[]{:S(2)}, u32[]{:S(2)}) collective-permute-start(bf16[128,768]{1,0:T(8,128)(2,1)S(1)} %get-tuple-element.21), channel_id=1, source_target_pairs={{0,128},{128,0},{256,384},{384,256},{1,129},{129,1},{257,385},{385... | collective-permute-start | bytes 589832 | tf_op jit(solution)/shard_map/ppermute | solution.py:277
  53.4 9.5 %collective-permute-start.5 = (bf16[128,768]{1,0:T(8,128)(2,1)S(1)}, bf16[128,768]{1,0:T(8,128)(2,1)S(1)}, u32[]{:S(2)}, u32[]{:S(2)}) collective-permute-start(bf16[128,768]{1,0:T(8,128)(2,1)S(1)} %fusion), channel_id=1, source_target_pairs={{0,256},{128,384},{256,0},{384,128},{1,257},{129,385},{257,1},{385... | collective-permute-start | bytes 589832 | tf_op jit(solution)/shard_map/ppermute | solution.py:281
  63.0 28.5 %all-to-all-start.1 = ((bf16[32,160,128]{2,1,0:T(8,128)(2,1)}), bf16[32,160,128]{2,1,0:T(8,128)(2,1)S(1)}, u32[]{:S(2)}, u32[]{:S(2)}) async-start(bf16[32,160,128]{2,1,0:T(8,128)(2,1)} %bitcast), calls=%async_computation.1 | async-start | bytes 2621440 | tf_op jit(solution)/shard_map/all_to_all | solution.py:296
  71.8 12.3 %collective-permute-start.6 = (bf16[128,768]{1,0:T(8,128)(2,1)S(1)}, bf16[128,768]{1,0:T(8,128)(2,1)S(1)}, u32[]{:S(2)}, u32[]{:S(2)}) collective-permute-start(bf16[128,768]{1,0:T(8,128)(2,1)S(1)} %add_convert_fusion.refs_0_), channel_id=1, source_target_pairs={{0,16},{8,24},{16,32},{24,40},{32,48},{40,56},{48,64},{56,72},{64,... | collective-permute-start | bytes 589832 | tf_op jit(solution)/shard_map/ppermute | solution.py:299
  75.7 15.1 %collective-permute-start.7 = (bf16[128,768]{1,0:T(8,128)(2,1)S(1)}, bf16[128,768]{1,0:T(8,128)(2,1)S(1)}, u32[]{:S(2)}, u32[]{:S(2)}) collective-permute-start(bf16[128,768]{1,0:T(8,128)(2,1)S(1)} %add_convert_fusion.refs_0_), channel_id=1, source_target_pairs={{0,8},{8,16},{16,24},{24,32},{32,40},{40,48},{48,56},{56,64},{64,7... | collective-permute-start | bytes 589832 | tf_op jit(solution)/shard_map/ppermute | solution.py:299
  78.8 12.0 %collective-permute-start.8 = (bf16[128,768]{1,0:T(8,128)(2,1)S(1)}, bf16[128,768]{1,0:T(8,128)(2,1)S(1)}, u32[]{:S(2)}, u32[]{:S(2)}) collective-permute-start(bf16[128,768]{1,0:T(8,128)(2,1)S(1)} %add_convert_fusion.refs_0_), channel_id=1, source_target_pairs={{0,120},{8,0},{16,8},{24,16},{32,24},{40,32},{48,40},{56,48},{64,5... | collective-permute-start | bytes 589832 | tf_op jit(solution)/shard_map/ppermute | solution.py:299
  84.1 7.4 %collective-permute-start.9 = (bf16[64,1536]{1,0:T(8,128)(2,1)S(1)}, bf16[64,1536]{1,0:T(8,128)(2,1)S(1)}, u32[]{:S(2)}, u32[]{:S(2)}) collective-permute-start(bf16[64,1536]{1,0:T(8,128)(2,1)S(1)} %slice.24), channel_id=1, source_target_pairs={{0,3},{1,0},{2,1},{3,2},{4,7},{5,4},{6,5},{7,6},{8,11},{9,8},{10,9... | collective-permute-start | bytes 589832 | tf_op jit(solution)/shard_map/ppermute | solution.py:247
  91.9 7.2 %collective-permute-start.10 = (bf16[96,768]{1,0:T(8,128)(2,1)S(1)}, bf16[96,768]{1,0:T(8,128)(2,1)S(1)}, u32[]{:S(2)}, u32[]{:S(2)}) collective-permute-start(bf16[96,768]{1,0:T(8,128)(2,1)S(1)} %get-tuple-element.32), channel_id=1, source_target_pairs={{0,128},{128,0},{256,384},{384,256},{1,129},{129,1},{257,385},{385... | collective-permute-start | bytes 442376 | tf_op jit(solution)/shard_map/ppermute | solution.py:313

commit v23 on v22

--- a/solution.py
+++ b/solution.py
@@ -228,9 +228,22 @@
     size = tok // 2 // spread
     shape = jax.ShapeDtypeStruct
 
+    def along_y(block, k):
+        return lax.ppermute(
+            block, "col", [(i, i - i % 4 + (i + k) % 4) for i in range(n_col)]
+        )
+
+    picked = call(
+        pick_kernel,
+        (sample_rows, cotangent),
+        [shape((2 * size + samp, feat_grp), BF)],
+        2 * 64 * tok * feat_grp,
+    )[0]
+    beside = lax.ppermute(picked, "col", [(i, (i + 4) % n_col) for i in range(n_col)])
+    picked, x_in = lax.optimization_barrier((picked, tokens_in))
     payload = call(
         first_kernel,
-        (sample_rows, tokens_in, act_inverse),
+        (sample_rows, x_in, act_inverse),
         [shape((n_row, out_rows + strip, tok), BF)],
         2 * feat_grp * feat_row * tok,
         [
@@ -243,18 +256,6 @@
     )[0]
     first = lax.all_to_all(payload, "row", 0, 0)
 
-    def along_y(block, k):
-        return lax.ppermute(
-            block, "col", [(i, i - i % 4 + (i + k) % 4) for i in range(n_col)]
-        )
-
-    picked = call(
-        pick_kernel,
-        (sample_rows, cotangent),
-        [shape((2 * size + samp, feat_grp), BF)],
-        2 * 64 * tok * feat_grp,
-    )[0]
-    beside = lax.ppermute(picked, "col", [(i, (i + 4) % n_col) for i in range(n_col)])
     cut = 2 * size
     rows = jnp.concatenate([picked[:cut], beside[:cut]], axis=0)
     samples = jnp.concatenate([picked[cut:], beside[cut:]], axis=0)

time: 101 us -> 99.8 us (0.988)
  the two profiles are of different devices: /device:TPU:1 before, /device:TPU:57 now
where the time goes in v23:
time: 99.8 us; the launch traced here: 99 us
  starting transfers between devices  59.1 us (59%)
  waiting for transfers between devices  24.4 us (24%)
  Pallas kernels  10.4 us (10%)
  local copies, waits for them, and re-layouts  3.36 us (3%)
    ppermute x4, waiting for transfers between devices, along_y(): lax.ppermute(block, 'col', [(i, i - i % 4 + (i + k) % 4) for i in range(n...  16 us
    all_to_all x1, starting transfers between devices, body(): first = lax.all_to_all(payload, 'row', 0, 0)  14.7 us
    ppermute x4, starting transfers between devices, along_y(): lax.ppermute(block, 'col', [(i, i - i % 4 + (i + k) % 4) for i in range(n...  10.8 us
    pallas_call x7, Pallas kernels, call(): pl.pallas_call(kernel, out_shape=outs, in_specs=places, out_specs=[VMEM]...  10.4 us
    ppermute x3, starting transfers between devices, body(): lax.ppermute(right, 'row', [(i, (i + j) % n_row) for i in range(n_row)])  10.2 us
    ppermute x2, starting transfers between devices, body(): taken = lax.ppermute(give, 'grp', [(i, i ^ 1) for i in range(n_grp)])  8.19 us
    all_to_all x1, starting transfers between devices, body(): lax.all_to_all(send.reshape((n_grp * n_col,) + send.shape[2:]), ('grp', '...  7.76 us
    ppermute x3, waiting for transfers between devices, body(): lax.ppermute(right, 'row', [(i, (i + j) % n_row) for i in range(n_row)])  4.63 us
  transfers between devices with their start and end apart: 13, of which 5 were waited for; matrix products, arithmetic and copies ran while one was open for 0% of the time, Pallas kernels for 9%

profile of v23, /device:TPU:57, one launch (start us, length us, event | category | flops | bytes accessed | tf_op | source)
XLA Modules:
  0.0 99.0 jit_solution(12889823403094073484)
XLA Ops:
  0.6 1.0 copy-done.1
  1.6 0.7 copy-done.3
  2.3 0.7 shard_map.76.gy_ref
  3.0 3.1 %collective-permute-start = (bf16[64,1536]{1,0:T(8,128)(2,1)S(1)}, bf16[64,1536]{1,0:T(8,128)(2,1)S(1)}, u32[]{:S(2)}, u32[]{:S(2)}) collective-permute-start(bf16[64,1536]{1,0:T(8,128)(2,1)S(1)} %shard_map.76.gy_ref), channel_id=1, source_target_pairs={{0,4},{1,5},{2,6},{3,7},{4,0},{5,1},{6,2},{7,3},{8,12},{9,13},{10,... | collective-permute-start | bytes 589832 | tf_op jit(solution)/shard_map/ppermute | solution.py:242
  6.2 3.6 %shard_map.77 = bf16[16,120,128]{2,1,0:T(8,128)(2,1)} custom-call(s32[32]{0:T(128)} %picks.5, bf16[128,384]{1,0:T(8,128)(2,1)} %x_ref.1, bf16[1536,384]{1,0:T(8,128)(2,1)} %a_hbm.1), custom_call_target="tpu_custom_call" | custom-call | flops 150994944 | bytes 1769600 | tf_op jit(solution)/shard_map/pallas_call | solution.py:24
  9.8 14.7 %all-to-all-start = ((bf16[16,120,128]{2,1,0:T(8,128)(2,1)}), bf16[16,120,128]{2,1,0:T(8,128)(2,1)S(1)}, u32[]{:S(2)}, u32[]{:S(2)}) async-start(bf16[16,120,128]{2,1,0:T(8,128)(2,1)} %shard_map.77), calls=%async_computation | async-start | bytes 983040 | tf_op jit(solution)/shard_map/all_to_all | solution.py:257
  24.5 1.9 %collective-permute-start.1 = (bf16[128,1536]{1,0:T(8,128)(2,1)S(1)}, bf16[128,1536]{1,0:T(8,128)(2,1)S(1)}, u32[]{:S(2)}, u32[]{:S(2)}) collective-permute-start(bf16[128,1536]{1,0:T(8,128)(2,1)S(1)} %pad_maximum_fusion.refs_0_), channel_id=1, source_target_pairs={{0,1},{1,2},{2,3},{3,0},{4,5},{5,6},{6,7},{7,4},{8,9},{9,10},{10,1... | collective-permute-start | bytes 1179656 | tf_op jit(solution)/shard_map/ppermute | solution.py:232
  26.4 3.4 %collective-permute-start.3 = (bf16[128,1536]{1,0:T(8,128)(2,1)S(1)}, bf16[128,1536]{1,0:T(8,128)(2,1)S(1)}, u32[]{:S(2)}, u32[]{:S(2)}) collective-permute-start(bf16[128,1536]{1,0:T(8,128)(2,1)S(1)} %pad_maximum_fusion.refs_0_), channel_id=1, source_target_pairs={{0,3},{1,0},{2,1},{3,2},{4,7},{5,4},{6,5},{7,6},{8,11},{9,8},{10,9... | collective-permute-start | bytes 1179656 | tf_op jit(solution)/shard_map/ppermute | solution.py:232
  29.8 0.0 copy-start.2
  29.8 0.0 copy-start.4
  29.9 3.0 %collective-permute-start.2 = (bf16[64,1536]{1,0:T(8,128)(2,1)S(1)}, bf16[64,1536]{1,0:T(8,128)(2,1)S(1)}, u32[]{:S(2)}, u32[]{:S(2)}) collective-permute-start(bf16[64,1536]{1,0:T(8,128)(2,1)S(1)} %pad_maximum_fusion.1), channel_id=1, source_target_pairs={{0,2},{1,3},{2,0},{3,1},{4,6},{5,7},{6,4},{7,5},{8,10},{9,11},{10,... | collective-permute-start | bytes 589832 | tf_op jit(solution)/shard_map/ppermute | solution.py:232
  32.9 9.4 %collective-permute-done.2.refs_2_ = bf16[64,1536]{1,0:T(8,128)(2,1)S(1)} collective-permute-done((bf16[64,1536]{1,0:T(8,128)(2,1)S(1)}, bf16[64,1536]{1,0:T(8,128)(2,1)S(1)}, u32[]{:S(2)}, u32[]{:S(2)}) %collective-permute-start.2) | collective-permute-done | bytes 196640 | tf_op jit(solution)/shard_map/ppermute | solution.py:232
  42.3 1.7 %copy-done = bf16[1536,768]{1,0:T(8,128)(2,1)S(1)} copy-done((bf16[1536,768]{1,0:T(8,128)(2,1)S(1)}, bf16[1536,768]{1,0:T(8,128)(2,1)}, u32[]{:S(2)}) %copy-start) | copy-done | bytes 2359320
  44.0 1.9 %shard_map.78 = (bf16[128,768]{1,0:T(8,128)(2,1)S(1)}, bf16[128,768]{1,0:T(8,128)(2,1)S(1)}) custom-call(bf16[1536,768]{1,0:T(8,128)(2,1)S(1)} %copy-done, bf16[128,1536]{1,0:T(8,128)(2,1)S(1)} %pad_maximum_fusion.refs_0_, bf16[128,1536]{1,0:T(8,128)(2,1)S(1)} %collective-permute-done.1.refs_1_, bf16[64,1536]{1,0:T(8,128)(2,1)S(1)} %collective-permute-done.2.refs_2_, ...), custom_call_target="tpu_custom_call" | custom-call | flops 603979776 | bytes 4128768 | tf_op jit(solution)/shard_map/pallas_call | solution.py:24
  45.9 4.9 %collective-permute-start.4 = (bf16[128,768]{1,0:T(8,128)(2,1)S(1)}, bf16[128,768]{1,0:T(8,128)(2,1)S(1)}, u32[]{:S(2)}, u32[]{:S(2)}) collective-permute-start(bf16[128,768]{1,0:T(8,128)(2,1)S(1)} %get-tuple-element.25), channel_id=1, source_target_pairs={{0,128},{128,0},{256,384},{384,256},{1,129},{129,1},{257,385},{385... | collective-permute-start | bytes 589832 | tf_op jit(solution)/shard_map/ppermute | solution.py:278
  50.8 1.0 %collective-permute-done.4 = bf16[128,768]{1,0:T(8,128)(2,1)S(1)} collective-permute-done((bf16[128,768]{1,0:T(8,128)(2,1)S(1)}, bf16[128,768]{1,0:T(8,128)(2,1)S(1)}, u32[]{:S(2)}, u32[]{:S(2)}) %collective-permute-start.4) | collective-permute-done | bytes 196640 | tf_op jit(solution)/shard_map/ppermute | solution.py:278
  51.9 4.4 %collective-permute-start.5 = (bf16[128,768]{1,0:T(8,128)(2,1)S(1)}, bf16[128,768]{1,0:T(8,128)(2,1)S(1)}, u32[]{:S(2)}, u32[]{:S(2)}) collective-permute-start(bf16[128,768]{1,0:T(8,128)(2,1)S(1)} %fusion), channel_id=1, source_target_pairs={{0,256},{128,384},{256,0},{384,128},{1,257},{129,385},{257,1},{385... | collective-permute-start | bytes 589832 | tf_op jit(solution)/shard_map/ppermute | solution.py:282
  56.3 1.0 shard_map.79.side_ref
  57.3 1.3 %shard_map.80 = bf16[4,8,160,128]{3,2,1,0:T(8,128)(2,1)} custom-call(bf16[16,120,128]{2,1,0:T(8,128)(2,1)S(1)} %all-to-all-done.got_ref, bf16[8,64,128]{2,1,0:T(8,128)(2,1)S(1)} %shard_map.79.side_ref), custom_call_target="tpu_custom_call" | custom-call | flops 1000000 | bytes 1933312 | tf_op jit(solution)/shard_map/pallas_call | solution.py:24
  58.5 2.8 %collective-permute-done.5 = bf16[128,768]{1,0:T(8,128)(2,1)S(1)} collective-permute-done((bf16[128,768]{1,0:T(8,128)(2,1)S(1)}, bf16[128,768]{1,0:T(8,128)(2,1)S(1)}, u32[]{:S(2)}, u32[]{:S(2)}) %collective-permute-start.5) | collective-permute-done | bytes 196640 | tf_op jit(solution)/shard_map/ppermute | solution.py:282
  61.3 0.1 add_convert_fusion.refs_0_
  61.4 7.8 %all-to-all-start.1 = ((bf16[32,160,128]{2,1,0:T(8,128)(2,1)}), bf16[32,160,128]{2,1,0:T(8,128)(2,1)S(1)}, u32[]{:S(2)}, u32[]{:S(2)}) async-start(bf16[32,160,128]{2,1,0:T(8,128)(2,1)} %bitcast), calls=%async_computation.1 | async-start | bytes 2621440 | tf_op jit(solution)/shard_map/all_to_all | solution.py:297
  69.2 4.0 %collective-permute-start.6 = (bf16[128,768]{1,0:T(8,128)(2,1)S(1)}, bf16[128,768]{1,0:T(8,128)(2,1)S(1)}, u32[]{:S(2)}, u32[]{:S(2)}) collective-permute-start(bf16[128,768]{1,0:T(8,128)(2,1)S(1)} %add_convert_fusion.refs_0_), channel_id=1, source_target_pairs={{0,16},{8,24},{16,32},{24,40},{32,48},{40,56},{48,64},{56,72},{64,... | collective-permute-start | bytes 589832 | tf_op jit(solution)/shard_map/ppermute | solution.py:300
  73.2 4.3 %collective-permute-start.7 = (bf16[128,768]{1,0:T(8,128)(2,1)S(1)}, bf16[128,768]{1,0:T(8,128)(2,1)S(1)}, u32[]{:S(2)}, u32[]{:S(2)}) collective-permute-start(bf16[128,768]{1,0:T(8,128)(2,1)S(1)} %add_convert_fusion.refs_0_), channel_id=1, source_target_pairs={{0,8},{8,16},{16,24},{24,32},{32,40},{40,48},{48,56},{56,64},{64,7... | collective-permute-start | bytes 589832 | tf_op jit(solution)/shard_map/ppermute | solution.py:300
  77.5 1.9 %collective-permute-start.8 = (bf16[128,768]{1,0:T(8,128)(2,1)S(1)}, bf16[128,768]{1,0:T(8,128)(2,1)S(1)}, u32[]{:S(2)}, u32[]{:S(2)}) collective-permute-start(bf16[128,768]{1,0:T(8,128)(2,1)S(1)} %add_convert_fusion.refs_0_), channel_id=1, source_target_pairs={{0,120},{8,0},{16,8},{24,16},{32,24},{40,32},{48,40},{56,48},{64,5... | collective-permute-start | bytes 589832 | tf_op jit(solution)/shard_map/ppermute | solution.py:300
  79.5 4.6 %collective-permute-done.6.refs_1_ = bf16[128,768]{1,0:T(8,128)(2,1)S(1)} collective-permute-done((bf16[128,768]{1,0:T(8,128)(2,1)S(1)}, bf16[128,768]{1,0:T(8,128)(2,1)S(1)}, u32[]{:S(2)}, u32[]{:S(2)}) %collective-permute-start.6) | collective-permute-done | bytes 196640 | tf_op jit(solution)/shard_map/ppermute | solution.py:300
  84.1 2.5 %collective-permute-start.9 = (bf16[64,1536]{1,0:T(8,128)(2,1)S(1)}, bf16[64,1536]{1,0:T(8,128)(2,1)S(1)}, u32[]{:S(2)}, u32[]{:S(2)}) collective-permute-start(bf16[64,1536]{1,0:T(8,128)(2,1)S(1)} %slice.22), channel_id=1, source_target_pairs={{0,3},{1,0},{2,1},{3,2},{4,7},{5,4},{6,5},{7,6},{8,11},{9,8},{10,9... | collective-permute-start | bytes 589832 | tf_op jit(solution)/shard_map/ppermute | solution.py:232
  86.6 6.5 %collective-permute-done.9.refs_2_ = bf16[64,1536]{1,0:T(8,128)(2,1)S(1)} collective-permute-done((bf16[64,1536]{1,0:T(8,128)(2,1)S(1)}, bf16[64,1536]{1,0:T(8,128)(2,1)S(1)}, u32[]{:S(2)}, u32[]{:S(2)}) %collective-permute-start.9) | collective-permute-done | bytes 196640 | tf_op jit(solution)/shard_map/ppermute | solution.py:232
  93.1 0.5 shard_map.81
  93.6 3.3 %collective-permute-start.10 = (bf16[96,768]{1,0:T(8,128)(2,1)S(1)}, bf16[96,768]{1,0:T(8,128)(2,1)S(1)}, u32[]{:S(2)}, u32[]{:S(2)}) collective-permute-start(bf16[96,768]{1,0:T(8,128)(2,1)S(1)} %get-tuple-element.36), channel_id=1, source_target_pairs={{0,128},{128,0},{256,384},{384,256},{1,129},{129,1},{257,385},{385... | collective-permute-start | bytes 442376 | tf_op jit(solution)/shard_map/ppermute | solution.py:314
  96.9 1.4 %shard_map.82 = (f32[48,1536]{1,0:T(8,128)}, f32[48,1536]{1,0:T(8,128)}) custom-call(bf16[4,8,160,128]{3,2,1,0:T(8,128)(2,1)S(1)} %bitcast.3, bf16[128,1536]{1,0:T(8,128)(2,1)S(1)} %pad_maximum_fusion.refs_0_, bf16[128,1536]{1,0:T(8,128)(2,1)S(1)} %collective-permute-done.1.refs_1_, bf16[64,1536]{1,0:T(8,128)(2,1)S(1)} %collective-permute-done.9.refs_2_, ...), custom_call_target="tpu_custom_call" | custom-call | flops 201326592 | bytes 3276800 | tf_op jit(solution)/shard_map/pallas_call | solution.py:24
  98.3 0.7 convert_add_fusion.1
  (19 shorter events, 0.2 us)
Async XLA Ops:
  0.6 1.0 %copy-start.1 = (bf16[128,1536]{1,0:T(8,128)(2,1)S(1)}, bf16[128,1536]{1,0:T(8,128)(2,1)}, u32[]{:S(2)}) copy-start(bf16[128,1536]{1,0:T(8,128)(2,1)} %g_ref.1) | copy-start | bytes 1179652
  1.6 0.7 copy-start.3
  3.0 21.4 %collective-permute-start = (bf16[64,1536]{1,0:T(8,128)(2,1)S(1)}, bf16[64,1536]{1,0:T(8,128)(2,1)S(1)}, u32[]{:S(2)}, u32[]{:S(2)}) collective-permute-start(bf16[64,1536]{1,0:T(8,128)(2,1)S(1)} %shard_map.76.gy_ref), channel_id=1, source_target_pairs={{0,4},{1,5},{2,6},{3,7},{4,0},{5,1},{6,2},{7,3},{8,12},{9,13},{10,... | collective-permute-start | bytes 589832 | tf_op jit(solution)/shard_map/ppermute | solution.py:242
  9.8 42.1 %all-to-all-start = ((bf16[16,120,128]{2,1,0:T(8,128)(2,1)}), bf16[16,120,128]{2,1,0:T(8,128)(2,1)S(1)}, u32[]{:S(2)}, u32[]{:S(2)}) async-start(bf16[16,120,128]{2,1,0:T(8,128)(2,1)} %shard_map.77), calls=%async_computation | async-start | bytes 983040 | tf_op jit(solution)/shard_map/all_to_all | solution.py:257
  24.5 17.8 %collective-permute-start.1 = (bf16[128,1536]{1,0:T(8,128)(2,1)S(1)}, bf16[128,1536]{1,0:T(8,128)(2,1)S(1)}, u32[]{:S(2)}, u32[]{:S(2)}) collective-permute-start(bf16[128,1536]{1,0:T(8,128)(2,1)S(1)} %pad_maximum_fusion.refs_0_), channel_id=1, source_target_pairs={{0,1},{1,2},{2,3},{3,0},{4,5},{5,6},{6,7},{7,4},{8,9},{9,10},{10,1... | collective-permute-start | bytes 1179656 | tf_op jit(solution)/shard_map/ppermute | solution.py:232
  26.4 15.9 %collective-permute-start.3 = (bf16[128,1536]{1,0:T(8,128)(2,1)S(1)}, bf16[128,1536]{1,0:T(8,128)(2,1)S(1)}, u32[]{:S(2)}, u32[]{:S(2)}) collective-permute-start(bf16[128,1536]{1,0:T(8,128)(2,1)S(1)} %pad_maximum_fusion.refs_0_), channel_id=1, source_target_pairs={{0,3},{1,0},{2,1},{3,2},{4,7},{5,4},{6,5},{7,6},{8,11},{9,8},{10,9... | collective-permute-start | bytes 1179656 | tf_op jit(solution)/shard_map/ppermute | solution.py:232
  29.8 26.5 %copy-start.2 = (bf16[128,384]{1,0:T(8,128)(2,1)S(1)}, bf16[128,384]{1,0:T(8,128)(2,1)}, u32[]{:S(2)}) copy-start(bf16[128,384]{1,0:T(8,128)(2,1)} %x_ref.1) | copy-start | bytes 294916
  29.8 26.5 %copy-start.4 = (s32[32]{0:T(128)S(1)}, s32[32]{0:T(128)}, u32[]{:S(2)}) copy-start(s32[32]{0:T(128)} %picks.5) | copy-start | bytes 388
  29.9 12.4 %collective-permute-start.2 = (bf16[64,1536]{1,0:T(8,128)(2,1)S(1)}, bf16[64,1536]{1,0:T(8,128)(2,1)S(1)}, u32[]{:S(2)}, u32[]{:S(2)}) collective-permute-start(bf16[64,1536]{1,0:T(8,128)(2,1)S(1)} %pad_maximum_fusion.1), channel_id=1, source_target_pairs={{0,2},{1,3},{2,0},{3,1},{4,6},{5,7},{6,4},{7,5},{8,10},{9,11},{10,... | collective-permute-start | bytes 589832 | tf_op jit(solution)/shard_map/ppermute | solution.py:232
  42.3 1.7 %copy-start = (bf16[1536,768]{1,0:T(8,128)(2,1)S(1)}, bf16[1536,768]{1,0:T(8,128)(2,1)}, u32[]{:S(2)}) copy-start(bf16[1536,768]{1,0:T(8,128)(2,1)} %b_hbm.1) | copy-start | bytes 7077892
  45.9 5.9 %collective-permute-start.4 = (bf16[128,768]{1,0:T(8,128)(2,1)S(1)}, bf16[128,768]{1,0:T(8,128)(2,1)S(1)}, u32[]{:S(2)}, u32[]{:S(2)}) collective-permute-start(bf16[128,768]{1,0:T(8,128)(2,1)S(1)} %get-tuple-element.25), channel_id=1, source_target_pairs={{0,128},{128,0},{256,384},{384,256},{1,129},{129,1},{257,385},{385... | collective-permute-start | bytes 589832 | tf_op jit(solution)/shard_map/ppermute | solution.py:278
  51.9 9.4 %collective-permute-start.5 = (bf16[128,768]{1,0:T(8,128)(2,1)S(1)}, bf16[128,768]{1,0:T(8,128)(2,1)S(1)}, u32[]{:S(2)}, u32[]{:S(2)}) collective-permute-start(bf16[128,768]{1,0:T(8,128)(2,1)S(1)} %fusion), channel_id=1, source_target_pairs={{0,256},{128,384},{256,0},{384,128},{1,257},{129,385},{257,1},{385... | collective-permute-start | bytes 589832 | tf_op jit(solution)/shard_map/ppermute | solution.py:282
  61.4 31.7 %all-to-all-start.1 = ((bf16[32,160,128]{2,1,0:T(8,128)(2,1)}), bf16[32,160,128]{2,1,0:T(8,128)(2,1)S(1)}, u32[]{:S(2)}, u32[]{:S(2)}) async-start(bf16[32,160,128]{2,1,0:T(8,128)(2,1)} %bitcast), calls=%async_computation.1 | async-start | bytes 2621440 | tf_op jit(solution)/shard_map/all_to_all | solution.py:297
  69.2 14.9 %collective-permute-start.6 = (bf16[128,768]{1,0:T(8,128)(2,1)S(1)}, bf16[128,768]{1,0:T(8,128)(2,1)S(1)}, u32[]{:S(2)}, u32[]{:S(2)}) collective-permute-start(bf16[128,768]{1,0:T(8,128)(2,1)S(1)} %add_convert_fusion.refs_0_), channel_id=1, source_target_pairs={{0,16},{8,24},{16,32},{24,40},{32,48},{40,56},{48,64},{56,72},{64,... | collective-permute-start | bytes 589832 | tf_op jit(solution)/shard_map/ppermute | solution.py:300
  73.2 13.3 %collective-permute-start.7 = (bf16[128,768]{1,0:T(8,128)(2,1)S(1)}, bf16[128,768]{1,0:T(8,128)(2,1)S(1)}, u32[]{:S(2)}, u32[]{:S(2)}) collective-permute-start(bf16[128,768]{1,0:T(8,128)(2,1)S(1)} %add_convert_fusion.refs_0_), channel_id=1, source_target_pairs={{0,8},{8,16},{16,24},{24,32},{32,40},{40,48},{48,56},{56,64},{64,7... | collective-permute-start | bytes 589832 | tf_op jit(solution)/shard_map/ppermute | solution.py:300
  77.5 9.0 %collective-permute-start.8 = (bf16[128,768]{1,0:T(8,128)(2,1)S(1)}, bf16[128,768]{1,0:T(8,128)(2,1)S(1)}, u32[]{:S(2)}, u32[]{:S(2)}) collective-permute-start(bf16[128,768]{1,0:T(8,128)(2,1)S(1)} %add_convert_fusion.refs_0_), channel_id=1, source_target_pairs={{0,120},{8,0},{16,8},{24,16},{32,24},{40,32},{48,40},{56,48},{64,5... | collective-permute-start | bytes 589832 | tf_op jit(solution)/shard_map/ppermute | solution.py:300
  84.1 9.0 %collective-permute-start.9 = (bf16[64,1536]{1,0:T(8,128)(2,1)S(1)}, bf16[64,1536]{1,0:T(8,128)(2,1)S(1)}, u32[]{:S(2)}, u32[]{:S(2)}) collective-permute-start(bf16[64,1536]{1,0:T(8,128)(2,1)S(1)} %slice.22), channel_id=1, source_target_pairs={{0,3},{1,0},{2,1},{3,2},{4,7},{5,4},{6,5},{7,6},{8,11},{9,8},{10,9... | collective-permute-start | bytes 589832 | tf_op jit(solution)/shard_map/ppermute | solution.py:232
  93.6 4.7 %collective-permute-start.10 = (bf16[96,768]{1,0:T(8,128)(2,1)S(1)}, bf16[96,768]{1,0:T(8,128)(2,1)S(1)}, u32[]{:S(2)}, u32[]{:S(2)}) collective-permute-start(bf16[96,768]{1,0:T(8,128)(2,1)S(1)} %get-tuple-element.36), channel_id=1, source_target_pairs={{0,128},{128,0},{256,384},{384,256},{1,129},{129,1},{257,385},{385... | collective-permute-start | bytes 442376 | tf_op jit(solution)/shard_map/ppermute | solution.py:314

commit v24 on v23

--- a/solution.py
+++ b/solution.py
@@ -116,25 +116,11 @@
         out_ref[c] = block.astype(BF)
 
 
-def right_kernel(b_hbm, *refs):
-    blocks, keep_ref, give_ref, held, b_ref, sems = refs[:-5], *refs[-5:]
+def right_kernel(b_ref, *refs):
+    blocks, keep_ref, give_ref, held = refs[:-3], refs[-3], refs[-2], refs[-1]
     n_blk, unused, size, width = held.shape
-    parts = sems.shape[0]
-    step = b_ref.shape[0] // parts
-    spans = [pl.ds(p * step, step) for p in range(parts)]
-    copies = [
-        pltpu.make_async_copy(b_hbm.at[span], b_ref.at[span], sems.at[p])
-        for p, span in enumerate(spans)
-    ]
-    for copy in copies:
-        copy.start()
     rows = jnp.concatenate([block[: 4 * size, :] for block in blocks], axis=0)
-    term = None
-    for p in range(parts):
-        copies[p].wait()
-        left = rows[:, p * step : (p + 1) * step]
-        part = jnp.dot(left, b_ref[spans[p], :], preferred_element_type=F32)
-        term = part if term is None else term + part
+    term = jnp.dot(rows, b_ref[...], preferred_element_type=F32)
     held[...] = term.reshape(held.shape)
     core = lax.axis_index("grp") % 2
     keep_ref[...] = held[:, core].reshape(n_blk * size, width).astype(BF)
@@ -238,6 +224,7 @@
         (sample_rows, cotangent),
         [shape((2 * size + samp, feat_grp), BF)],
         2 * 64 * tok * feat_grp,
+        limit=56,
     )[0]
     beside = lax.ppermute(picked, "col", [(i, (i + 4) % n_col) for i in range(n_col)])
     picked, x_in = lax.optimization_barrier((picked, tokens_in))
@@ -268,17 +255,12 @@
         (grad_inverse, *pairs),
         [shape((n_col * size, width), BF)] * 2,
         4 * n_col * size * feat_grp * width,
-        [
-            pltpu.VMEM((n_col, 2, size, width), F32),
-            pltpu.VMEM(grad_inverse.shape, BF),
-            pltpu.SemaphoreType.DMA((4,)),
-        ],
-        places=[pl.BlockSpec(memory_space=pl.ANY)] + [VMEM] * 4,
+        [pltpu.VMEM((n_col, 2, size, width), F32)],
     )
     taken = lax.ppermute(give, "grp", [(i, i ^ 1) for i in range(n_grp)])
     some = keep.astype(F32) + taken.astype(F32)
     give = some.astype(BF)
-    first, give = lax.optimization_barrier((first, give))
+    first, unused = lax.optimization_barrier((first, give))
     taken = lax.ppermute(give, "grp", [(i, i ^ 2) for i in range(n_grp)])
     right = (some + taken.astype(F32)).astype(BF)
     side = call(

time: 99.8 us -> 99.6 us (level)
  the two profiles are of different devices: /device:TPU:57 before, /device:TPU:1 now
where the time goes in v24:
time: 99.6 us; the launch traced here: 98.2 us
  starting transfers between devices  66.7 us (67%)
  waiting for transfers between devices  17.5 us (18%)
  Pallas kernels  10.5 us (11%)
  local copies, waits for them, and re-layouts  1.73 us (2%)
    all_to_all x1, starting transfers between devices, body(): first = lax.all_to_all(payload, 'row', 0, 0)  14.9 us
    ppermute x4, starting transfers between devices, along_y(): lax.ppermute(block, 'col', [(i, i - i % 4 + (i + k) % 4) for i in range(n...  14.6 us
    ppermute x3, starting transfers between devices, body(): lax.ppermute(right, 'row', [(i, (i + j) % n_row) for i in range(n_row)])  10.7 us
    pallas_call x7, Pallas kernels, call(): pl.pallas_call(kernel, out_shape=outs, in_specs=places, out_specs=[VMEM]...  10.5 us
    ppermute x2, starting transfers between devices, body(): taken = lax.ppermute(give, 'grp', [(i, i ^ 1) for i in range(n_grp)])  9.66 us
    all_to_all x1, starting transfers between devices, body(): lax.all_to_all(send.reshape((n_grp * n_col,) + send.shape[2:]), ('grp', '...  8.48 us
    ppermute x4, waiting for transfers between devices, along_y(): lax.ppermute(block, 'col', [(i, i - i % 4 + (i + k) % 4) for i in range(n...  8.04 us
    ppermute x1, starting transfers between devices, body(): taken = lax.ppermute(give, 'grp', [(i, i ^ 2) for i in range(n_grp)])  4.35 us
  transfers between devices with their start and end apart: 13, of which 6 were waited for; matrix products, arithmetic and copies ran while one was open for 0% of the time, Pallas kernels for 7%

profile of v24, /device:TPU:1, one launch (start us, length us, event | category | flops | bytes accessed | tf_op | source)
XLA Modules:
  0.0 98.2 jit_solution(11195759280280777430)
XLA Ops:
  0.6 1.9 %shard_map.76.gy_ref = bf16[64,1536]{1,0:T(8,128)(2,1)} custom-call(s32[32]{0:T(128)} %picks.5, bf16[128,1536]{1,0:T(8,128)(2,1)} %g_ref.1), custom_call_target="tpu_custom_call" | custom-call | flops 25165824 | bytes 589952 | tf_op jit(solution)/shard_map/pallas_call | solution.py:24
  2.5 4.1 %collective-permute-start = (bf16[64,1536]{1,0:T(8,128)(2,1)}, bf16[64,1536]{1,0:T(8,128)(2,1)S(1)}, u32[]{:S(2)}, u32[]{:S(2)}) collective-permute-start(bf16[64,1536]{1,0:T(8,128)(2,1)} %shard_map.76.gy_ref), channel_id=1, source_target_pairs={{0,4},{1,5},{2,6},{3,7},{4,0},{5,1},{6,2},{7,3},{8,12},{9,13},{10,... | collective-permute-start | bytes 589832 | tf_op jit(solution)/shard_map/ppermute | solution.py:229
  6.6 3.6 %shard_map.77 = bf16[16,120,128]{2,1,0:T(8,128)(2,1)} custom-call(s32[32]{0:T(128)} %picks.5, bf16[128,384]{1,0:T(8,128)(2,1)} %x_ref.1, bf16[1536,384]{1,0:T(8,128)(2,1)} %a_hbm.1), custom_call_target="tpu_custom_call" | custom-call | flops 150994944 | bytes 1769600 | tf_op jit(solution)/shard_map/pallas_call | solution.py:24
  10.2 14.9 %all-to-all-start = ((bf16[16,120,128]{2,1,0:T(8,128)(2,1)}), bf16[16,120,128]{2,1,0:T(8,128)(2,1)S(1)}, u32[]{:S(2)}, u32[]{:S(2)}) async-start(bf16[16,120,128]{2,1,0:T(8,128)(2,1)} %shard_map.77), calls=%async_computation | async-start | bytes 983040 | tf_op jit(solution)/shard_map/all_to_all | solution.py:244
  25.2 0.0 collective-permute-done
  25.2 3.2 %collective-permute-start.1 = (bf16[128,1536]{1,0:T(8,128)(2,1)S(1)}, bf16[128,1536]{1,0:T(8,128)(2,1)S(1)}, u32[]{:S(2)}, u32[]{:S(2)}) collective-permute-start(bf16[128,1536]{1,0:T(8,128)(2,1)S(1)} %pad_maximum_fusion.refs_0_), channel_id=1, source_target_pairs={{0,1},{1,2},{2,3},{3,0},{4,5},{5,6},{6,7},{7,4},{8,9},{9,10},{10,1... | collective-permute-start | bytes 1179656 | tf_op jit(solution)/shard_map/ppermute | solution.py:218
  28.4 3.4 %collective-permute-start.3 = (bf16[128,1536]{1,0:T(8,128)(2,1)S(1)}, bf16[128,1536]{1,0:T(8,128)(2,1)S(1)}, u32[]{:S(2)}, u32[]{:S(2)}) collective-permute-start(bf16[128,1536]{1,0:T(8,128)(2,1)S(1)} %pad_maximum_fusion.refs_0_), channel_id=1, source_target_pairs={{0,3},{1,0},{2,1},{3,2},{4,7},{5,4},{6,5},{7,6},{8,11},{9,8},{10,9... | collective-permute-start | bytes 1179656 | tf_op jit(solution)/shard_map/ppermute | solution.py:218
  31.8 0.0 copy-start.2
  31.8 0.0 copy-start.3
  31.9 3.7 %collective-permute-start.2 = (bf16[64,1536]{1,0:T(8,128)(2,1)S(1)}, bf16[64,1536]{1,0:T(8,128)(2,1)S(1)}, u32[]{:S(2)}, u32[]{:S(2)}) collective-permute-start(bf16[64,1536]{1,0:T(8,128)(2,1)S(1)} %pad_maximum_fusion.1), channel_id=1, source_target_pairs={{0,2},{1,3},{2,0},{3,1},{4,6},{5,7},{6,4},{7,5},{8,10},{9,11},{10,... | collective-permute-start | bytes 589832 | tf_op jit(solution)/shard_map/ppermute | solution.py:218
  35.5 7.6 %collective-permute-done.2.refs_2_ = bf16[64,1536]{1,0:T(8,128)(2,1)S(1)} collective-permute-done((bf16[64,1536]{1,0:T(8,128)(2,1)S(1)}, bf16[64,1536]{1,0:T(8,128)(2,1)S(1)}, u32[]{:S(2)}, u32[]{:S(2)}) %collective-permute-start.2) | collective-permute-done | bytes 196640 | tf_op jit(solution)/shard_map/ppermute | solution.py:218
  43.2 1.7 %copy-done = bf16[1536,768]{1,0:T(8,128)(2,1)S(1)} copy-done((bf16[1536,768]{1,0:T(8,128)(2,1)S(1)}, bf16[1536,768]{1,0:T(8,128)(2,1)}, u32[]{:S(2)}) %copy-start) | copy-done | bytes 2359320
  44.8 0.9 shard_map.78
  45.7 4.1 %collective-permute-start.4 = (bf16[128,768]{1,0:T(8,128)(2,1)S(1)}, bf16[128,768]{1,0:T(8,128)(2,1)S(1)}, u32[]{:S(2)}, u32[]{:S(2)}) collective-permute-start(bf16[128,768]{1,0:T(8,128)(2,1)S(1)} %get-tuple-element.24), channel_id=1, source_target_pairs={{0,128},{128,0},{256,384},{384,256},{1,129},{129,1},{257,385},{385... | collective-permute-start | bytes 589832 | tf_op jit(solution)/shard_map/ppermute | solution.py:260
  49.8 1.0 %collective-permute-done.4 = bf16[128,768]{1,0:T(8,128)(2,1)S(1)} collective-permute-done((bf16[128,768]{1,0:T(8,128)(2,1)S(1)}, bf16[128,768]{1,0:T(8,128)(2,1)S(1)}, u32[]{:S(2)}, u32[]{:S(2)}) %collective-permute-start.4) | collective-permute-done | bytes 196640 | tf_op jit(solution)/shard_map/ppermute | solution.py:260
  50.9 4.3 %collective-permute-start.5 = (bf16[128,768]{1,0:T(8,128)(2,1)S(1)}, bf16[128,768]{1,0:T(8,128)(2,1)S(1)}, u32[]{:S(2)}, u32[]{:S(2)}) collective-permute-start(bf16[128,768]{1,0:T(8,128)(2,1)S(1)} %fusion), channel_id=1, source_target_pairs={{0,256},{128,384},{256,0},{384,128},{1,257},{129,385},{257,1},{385... | collective-permute-start | bytes 589832 | tf_op jit(solution)/shard_map/ppermute | solution.py:264
  55.3 1.0 shard_map.79.side_ref
  56.2 4.2 %collective-permute-done.5 = bf16[128,768]{1,0:T(8,128)(2,1)S(1)} collective-permute-done((bf16[128,768]{1,0:T(8,128)(2,1)S(1)}, bf16[128,768]{1,0:T(8,128)(2,1)S(1)}, u32[]{:S(2)}, u32[]{:S(2)}) %collective-permute-start.5) | collective-permute-done | bytes 196640 | tf_op jit(solution)/shard_map/ppermute | solution.py:264
  60.4 0.1 add_convert_fusion.refs_0_
  60.5 1.3 %shard_map.80 = bf16[4,8,160,128]{3,2,1,0:T(8,128)(2,1)} custom-call(bf16[16,120,128]{2,1,0:T(8,128)(2,1)S(1)} %all-to-all-done.got_ref, bf16[8,64,128]{2,1,0:T(8,128)(2,1)S(1)} %shard_map.79.side_ref), custom_call_target="tpu_custom_call" | custom-call | flops 1000000 | bytes 1933312 | tf_op jit(solution)/shard_map/pallas_call | solution.py:24
  61.8 8.5 %all-to-all-start.1 = ((bf16[32,160,128]{2,1,0:T(8,128)(2,1)}), bf16[32,160,128]{2,1,0:T(8,128)(2,1)S(1)}, u32[]{:S(2)}, u32[]{:S(2)}) async-start(bf16[32,160,128]{2,1,0:T(8,128)(2,1)} %bitcast), calls=%async_computation.1 | async-start | bytes 2621440 | tf_op jit(solution)/shard_map/all_to_all | solution.py:279
  70.3 4.2 %collective-permute-start.6 = (bf16[128,768]{1,0:T(8,128)(2,1)S(1)}, bf16[128,768]{1,0:T(8,128)(2,1)S(1)}, u32[]{:S(2)}, u32[]{:S(2)}) collective-permute-start(bf16[128,768]{1,0:T(8,128)(2,1)S(1)} %add_convert_fusion.refs_0_), channel_id=1, source_target_pairs={{0,16},{8,24},{16,32},{24,40},{32,48},{40,56},{48,64},{56,72},{64,... | collective-permute-start | bytes 589832 | tf_op jit(solution)/shard_map/ppermute | solution.py:282
  74.5 3.1 %collective-permute-start.7 = (bf16[128,768]{1,0:T(8,128)(2,1)S(1)}, bf16[128,768]{1,0:T(8,128)(2,1)S(1)}, u32[]{:S(2)}, u32[]{:S(2)}) collective-permute-start(bf16[128,768]{1,0:T(8,128)(2,1)S(1)} %add_convert_fusion.refs_0_), channel_id=1, source_target_pairs={{0,8},{8,16},{16,24},{24,32},{32,40},{40,48},{48,56},{56,64},{64,7... | collective-permute-start | bytes 589832 | tf_op jit(solution)/shard_map/ppermute | solution.py:282
  77.6 3.4 %collective-permute-start.8 = (bf16[128,768]{1,0:T(8,128)(2,1)S(1)}, bf16[128,768]{1,0:T(8,128)(2,1)S(1)}, u32[]{:S(2)}, u32[]{:S(2)}) collective-permute-start(bf16[128,768]{1,0:T(8,128)(2,1)S(1)} %add_convert_fusion.refs_0_), channel_id=1, source_target_pairs={{0,120},{8,0},{16,8},{24,16},{32,24},{40,32},{48,40},{56,48},{64,5... | collective-permute-start | bytes 589832 | tf_op jit(solution)/shard_map/ppermute | solution.py:282
  81.0 1.6 %collective-permute-done.6.refs_1_ = bf16[128,768]{1,0:T(8,128)(2,1)S(1)} collective-permute-done((bf16[128,768]{1,0:T(8,128)(2,1)S(1)}, bf16[128,768]{1,0:T(8,128)(2,1)S(1)}, u32[]{:S(2)}, u32[]{:S(2)}) %collective-permute-start.6) | collective-permute-done | bytes 196640 | tf_op jit(solution)/shard_map/ppermute | solution.py:282
  82.6 4.3 %collective-permute-start.9 = (bf16[64,1536]{1,0:T(8,128)(2,1)S(1)}, bf16[64,1536]{1,0:T(8,128)(2,1)S(1)}, u32[]{:S(2)}, u32[]{:S(2)}) collective-permute-start(bf16[64,1536]{1,0:T(8,128)(2,1)S(1)} %slice.22), channel_id=1, source_target_pairs={{0,3},{1,0},{2,1},{3,2},{4,7},{5,4},{6,5},{7,6},{8,11},{9,8},{10,9... | collective-permute-start | bytes 589832 | tf_op jit(solution)/shard_map/ppermute | solution.py:218
  86.9 2.6 %collective-permute-done.7.refs_2_ = bf16[128,768]{1,0:T(8,128)(2,1)S(1)} collective-permute-done((bf16[128,768]{1,0:T(8,128)(2,1)S(1)}, bf16[128,768]{1,0:T(8,128)(2,1)S(1)}, u32[]{:S(2)}, u32[]{:S(2)}) %collective-permute-start.7) | collective-permute-done | bytes 196640 | tf_op jit(solution)/shard_map/ppermute | solution.py:282
  89.6 0.4 collective-permute-done.9.refs_2_
  90.0 0.5 shard_map.81
  90.4 5.6 %collective-permute-start.10 = (bf16[96,768]{1,0:T(8,128)(2,1)S(1)}, bf16[96,768]{1,0:T(8,128)(2,1)S(1)}, u32[]{:S(2)}, u32[]{:S(2)}) collective-permute-start(bf16[96,768]{1,0:T(8,128)(2,1)S(1)} %get-tuple-element.34), channel_id=1, source_target_pairs={{0,128},{128,0},{256,384},{384,256},{1,129},{129,1},{257,385},{385... | collective-permute-start | bytes 442376 | tf_op jit(solution)/shard_map/ppermute | solution.py:296
  96.1 1.4 %shard_map.82 = (f32[48,1536]{1,0:T(8,128)}, f32[48,1536]{1,0:T(8,128)}) custom-call(bf16[4,8,160,128]{3,2,1,0:T(8,128)(2,1)S(1)} %bitcast.3, bf16[128,1536]{1,0:T(8,128)(2,1)S(1)} %pad_maximum_fusion.refs_0_, bf16[128,1536]{1,0:T(8,128)(2,1)S(1)} %collective-permute-done.1.refs_1_, bf16[64,1536]{1,0:T(8,128)(2,1)S(1)} %collective-permute-done.9.refs_2_, ...), custom_call_target="tpu_custom_call" | custom-call | flops 201326592 | bytes 3276800 | tf_op jit(solution)/shard_map/pallas_call | solution.py:24
  97.5 0.7 convert_add_fusion.1
  (17 shorter events, 0.2 us)
Async XLA Ops:
  2.5 22.6 %copy-start.1 = (bf16[64,1536]{1,0:T(8,128)(2,1)S(1)}, bf16[64,1536]{1,0:T(8,128)(2,1)}, u32[]{:S(2)}) copy-start(bf16[64,1536]{1,0:T(8,128)(2,1)} %shard_map.76.gy_ref) | copy-start | bytes 589828
  2.5 22.6 %collective-permute-start = (bf16[64,1536]{1,0:T(8,128)(2,1)}, bf16[64,1536]{1,0:T(8,128)(2,1)S(1)}, u32[]{:S(2)}, u32[]{:S(2)}) collective-permute-start(bf16[64,1536]{1,0:T(8,128)(2,1)} %shard_map.76.gy_ref), channel_id=1, source_target_pairs={{0,4},{1,5},{2,6},{3,7},{4,0},{5,1},{6,2},{7,3},{8,12},{9,13},{10,... | collective-permute-start | bytes 589832 | tf_op jit(solution)/shard_map/ppermute | solution.py:229
  10.2 50.3 %all-to-all-start = ((bf16[16,120,128]{2,1,0:T(8,128)(2,1)}), bf16[16,120,128]{2,1,0:T(8,128)(2,1)S(1)}, u32[]{:S(2)}, u32[]{:S(2)}) async-start(bf16[16,120,128]{2,1,0:T(8,128)(2,1)} %shard_map.77), calls=%async_computation | async-start | bytes 983040 | tf_op jit(solution)/shard_map/all_to_all | solution.py:244
  25.2 17.9 %collective-permute-start.1 = (bf16[128,1536]{1,0:T(8,128)(2,1)S(1)}, bf16[128,1536]{1,0:T(8,128)(2,1)S(1)}, u32[]{:S(2)}, u32[]{:S(2)}) collective-permute-start(bf16[128,1536]{1,0:T(8,128)(2,1)S(1)} %pad_maximum_fusion.refs_0_), channel_id=1, source_target_pairs={{0,1},{1,2},{2,3},{3,0},{4,5},{5,6},{6,7},{7,4},{8,9},{9,10},{10,1... | collective-permute-start | bytes 1179656 | tf_op jit(solution)/shard_map/ppermute | solution.py:218
  28.4 14.7 %collective-permute-start.3 = (bf16[128,1536]{1,0:T(8,128)(2,1)S(1)}, bf16[128,1536]{1,0:T(8,128)(2,1)S(1)}, u32[]{:S(2)}, u32[]{:S(2)}) collective-permute-start(bf16[128,1536]{1,0:T(8,128)(2,1)S(1)} %pad_maximum_fusion.refs_0_), channel_id=1, source_target_pairs={{0,3},{1,0},{2,1},{3,2},{4,7},{5,4},{6,5},{7,6},{8,11},{9,8},{10,9... | collective-permute-start | bytes 1179656 | tf_op jit(solution)/shard_map/ppermute | solution.py:218
  31.8 23.4 %copy-start.2 = (bf16[128,384]{1,0:T(8,128)(2,1)S(1)}, bf16[128,384]{1,0:T(8,128)(2,1)}, u32[]{:S(2)}) copy-start(bf16[128,384]{1,0:T(8,128)(2,1)} %x_ref.1) | copy-start | bytes 294916
  31.8 23.4 %copy-start.3 = (s32[32]{0:T(128)S(1)}, s32[32]{0:T(128)}, u32[]{:S(2)}) copy-start(s32[32]{0:T(128)} %picks.5) | copy-start | bytes 388
  31.9 11.3 %collective-permute-start.2 = (bf16[64,1536]{1,0:T(8,128)(2,1)S(1)}, bf16[64,1536]{1,0:T(8,128)(2,1)S(1)}, u32[]{:S(2)}, u32[]{:S(2)}) collective-permute-start(bf16[64,1536]{1,0:T(8,128)(2,1)S(1)} %pad_maximum_fusion.1), channel_id=1, source_target_pairs={{0,2},{1,3},{2,0},{3,1},{4,6},{5,7},{6,4},{7,5},{8,10},{9,11},{10,... | collective-permute-start | bytes 589832 | tf_op jit(solution)/shard_map/ppermute | solution.py:218
  43.2 1.7 %copy-start = (bf16[1536,768]{1,0:T(8,128)(2,1)S(1)}, bf16[1536,768]{1,0:T(8,128)(2,1)}, u32[]{:S(2)}) copy-start(bf16[1536,768]{1,0:T(8,128)(2,1)} %b_ref.1) | copy-start | bytes 7077892
  45.7 5.1 %collective-permute-start.4 = (bf16[128,768]{1,0:T(8,128)(2,1)S(1)}, bf16[128,768]{1,0:T(8,128)(2,1)S(1)}, u32[]{:S(2)}, u32[]{:S(2)}) collective-permute-start(bf16[128,768]{1,0:T(8,128)(2,1)S(1)} %get-tuple-element.24), channel_id=1, source_target_pairs={{0,128},{128,0},{256,384},{384,256},{1,129},{129,1},{257,385},{385... | collective-permute-start | bytes 589832 | tf_op jit(solution)/shard_map/ppermute | solution.py:260
  50.9 9.5 %collective-permute-start.5 = (bf16[128,768]{1,0:T(8,128)(2,1)S(1)}, bf16[128,768]{1,0:T(8,128)(2,1)S(1)}, u32[]{:S(2)}, u32[]{:S(2)}) collective-permute-start(bf16[128,768]{1,0:T(8,128)(2,1)S(1)} %fusion), channel_id=1, source_target_pairs={{0,256},{128,384},{256,0},{384,128},{1,257},{129,385},{257,1},{385... | collective-permute-start | bytes 589832 | tf_op jit(solution)/shard_map/ppermute | solution.py:264
  61.8 28.2 %all-to-all-start.1 = ((bf16[32,160,128]{2,1,0:T(8,128)(2,1)}), bf16[32,160,128]{2,1,0:T(8,128)(2,1)S(1)}, u32[]{:S(2)}, u32[]{:S(2)}) async-start(bf16[32,160,128]{2,1,0:T(8,128)(2,1)} %bitcast), calls=%async_computation.1 | async-start | bytes 2621440 | tf_op jit(solution)/shard_map/all_to_all | solution.py:279
  70.3 12.3 %collective-permute-start.6 = (bf16[128,768]{1,0:T(8,128)(2,1)S(1)}, bf16[128,768]{1,0:T(8,128)(2,1)S(1)}, u32[]{:S(2)}, u32[]{:S(2)}) collective-permute-start(bf16[128,768]{1,0:T(8,128)(2,1)S(1)} %add_convert_fusion.refs_0_), channel_id=1, source_target_pairs={{0,16},{8,24},{16,32},{24,40},{32,48},{40,56},{48,64},{56,72},{64,... | collective-permute-start | bytes 589832 | tf_op jit(solution)/shard_map/ppermute | solution.py:282
  74.5 15.1 %collective-permute-start.7 = (bf16[128,768]{1,0:T(8,128)(2,1)S(1)}, bf16[128,768]{1,0:T(8,128)(2,1)S(1)}, u32[]{:S(2)}, u32[]{:S(2)}) collective-permute-start(bf16[128,768]{1,0:T(8,128)(2,1)S(1)} %add_convert_fusion.refs_0_), channel_id=1, source_target_pairs={{0,8},{8,16},{16,24},{24,32},{32,40},{40,48},{48,56},{56,64},{64,7... | collective-permute-start | bytes 589832 | tf_op jit(solution)/shard_map/ppermute | solution.py:282
  77.6 12.0 %collective-permute-start.8 = (bf16[128,768]{1,0:T(8,128)(2,1)S(1)}, bf16[128,768]{1,0:T(8,128)(2,1)S(1)}, u32[]{:S(2)}, u32[]{:S(2)}) collective-permute-start(bf16[128,768]{1,0:T(8,128)(2,1)S(1)} %add_convert_fusion.refs_0_), channel_id=1, source_target_pairs={{0,120},{8,0},{16,8},{24,16},{32,24},{40,32},{48,40},{56,48},{64,5... | collective-permute-start | bytes 589832 | tf_op jit(solution)/shard_map/ppermute | solution.py:282
  82.6 7.4 %collective-permute-start.9 = (bf16[64,1536]{1,0:T(8,128)(2,1)S(1)}, bf16[64,1536]{1,0:T(8,128)(2,1)S(1)}, u32[]{:S(2)}, u32[]{:S(2)}) collective-permute-start(bf16[64,1536]{1,0:T(8,128)(2,1)S(1)} %slice.22), channel_id=1, source_target_pairs={{0,3},{1,0},{2,1},{3,2},{4,7},{5,4},{6,5},{7,6},{8,11},{9,8},{10,9... | collective-permute-start | bytes 589832 | tf_op jit(solution)/shard_map/ppermute | solution.py:218
  90.4 7.0 %collective-permute-start.10 = (bf16[96,768]{1,0:T(8,128)(2,1)S(1)}, bf16[96,768]{1,0:T(8,128)(2,1)S(1)}, u32[]{:S(2)}, u32[]{:S(2)}) collective-permute-start(bf16[96,768]{1,0:T(8,128)(2,1)S(1)} %get-tuple-element.34), channel_id=1, source_target_pairs={{0,128},{128,0},{256,384},{384,256},{1,129},{129,1},{257,385},{385... | collective-permute-start | bytes 442376 | tf_op jit(solution)/shard_map/ppermute | solution.py:296

commit v25 on v24

--- a/solution.py
+++ b/solution.py
@@ -275,17 +275,14 @@
         [shape((n_grp, n_col, size * spread + strip * n_row // n_grp, LANES), BF)],
         1000000,
     )[0]
-    send, right = lax.optimization_barrier((send, right))
+    far = along_y(after[2 * cut :], 3)
+    send, right, far = lax.optimization_barrier((send, right, far))
     got = lax.all_to_all(send.reshape((n_grp * n_col,) + send.shape[2:]), ("grp", "col"), 0, 0)
     got = got.reshape(send.shape)
     rights = [right] + [
         lax.ppermute(right, "row", [(i, (i + j) % n_row) for i in range(n_row)])
         for j in SHIFTS[1:]
     ]
-    unused, beyond = lax.optimization_barrier((rights[1], after[2 * cut :]))
-    far = along_y(beyond, 3)
-
-    rights, far = lax.optimization_barrier((rights, far))
     term, give = call(
         final_kernel,
         (got, *rights),

time: 99.6 us -> 102 us (1.024)
  waiting for transfers between devices: 17.5 us -> 25.2 us
  starting transfers between devices: 66.7 us -> 59.3 us
  local copies, waits for them, and re-layouts: 1.73 us -> 4.01 us
    ppermute x3, waiting for transfers between devices: 4.22 us -> 10 us  [body(): lax.ppermute(right, 'row', [(i, (i + j) % n_row) for i in range(n_row)])]
    ppermute x4, waiting for transfers between devices: 8.04 us -> 11.9 us  [along_y(): lax.ppermute(block, 'col', [(i, i - i % 4 + (i + k) % 4) for i in range(n...]
    all_to_all x1, starting transfers between devices: 8.48 us -> 5.17 us  [body(): lax.all_to_all(send.reshape((n_grp * n_col,) + send.shape[2:]), ('grp', '...]
    ppermute x4, starting transfers between devices: 14.6 us -> 12.2 us  [along_y(): lax.ppermute(block, 'col', [(i, i - i % 4 + (i + k) % 4) for i in range(n...]
    unnamed x8 -> x16, local copies, waits for them, and re-layouts: 1.68 us -> 3.96 us
    ppermute x1, waiting for transfers between devices: 4.17 us -> 2.22 us  [body(): taken = lax.ppermute(give, 'grp', [(i, i ^ 2) for i in range(n_grp)])]
    ppermute x3, starting transfers between devices: 10.7 us -> 9.45 us  [body(): lax.ppermute(right, 'row', [(i, (i + j) % n_row) for i in range(n_row)])]
  transfers between devices with their start and end apart: 13 -> 13, of which waited for: 6 -> 6; matrix products, arithmetic and copies ran while one was open for 0% -> 0% of each run, Pallas kernels for 7% -> 8%
where the time goes in v25:
time: 102 us; the launch traced here: 101 us
  starting transfers between devices  59.3 us (58%)
  waiting for transfers between devices  25.2 us (25%)
  Pallas kernels  10.5 us (10%)
  local copies, waits for them, and re-layouts  4.01 us (4%)
    all_to_all x1, starting transfers between devices, body(): first = lax.all_to_all(payload, 'row', 0, 0)  14.9 us
    ppermute x4, starting transfers between devices, along_y(): lax.ppermute(block, 'col', [(i, i - i % 4 + (i + k) % 4) for i in range(n...  12.2 us
    ppermute x4, waiting for transfers between devices, along_y(): lax.ppermute(block, 'col', [(i, i - i % 4 + (i + k) % 4) for i in range(n...  11.9 us
    pallas_call x7, Pallas kernels, call(): pl.pallas_call(kernel, out_shape=outs, in_specs=places, out_specs=[VMEM]...  10.5 us
    ppermute x3, waiting for transfers between devices, body(): lax.ppermute(right, 'row', [(i, (i + j) % n_row) for i in range(n_row)])  10 us
    ppermute x3, starting transfers between devices, body(): lax.ppermute(right, 'row', [(i, (i + j) % n_row) for i in range(n_row)])  9.45 us
    ppermute x2, starting transfers between devices, body(): taken = lax.ppermute(give, 'grp', [(i, i ^ 1) for i in range(n_grp)])  9.12 us
    all_to_all x1, starting transfers between devices, body(): lax.all_to_all(send.reshape((n_grp * n_col,) + send.shape[2:]), ('grp', '...  5.17 us
  transfers between devices with their start and end apart: 13, of which 6 were waited for; matrix products, arithmetic and copies ran while one was open for 0% of the time, Pallas kernels for 8%

profile of v25, /device:TPU:1, one launch (start us, length us, event | category | flops | bytes accessed | tf_op | source)
XLA Modules:
  0.0 100.7 jit_solution(1339233729152870924)
XLA Ops:
  0.6 1.9 %shard_map.76.gy_ref = bf16[64,1536]{1,0:T(8,128)(2,1)} custom-call(s32[32]{0:T(128)} %picks.5, bf16[128,1536]{1,0:T(8,128)(2,1)} %g_ref.1), custom_call_target="tpu_custom_call" | custom-call | flops 25165824 | bytes 589952 | tf_op jit(solution)/shard_map/pallas_call | solution.py:24
  2.5 4.1 %collective-permute-start = (bf16[64,1536]{1,0:T(8,128)(2,1)}, bf16[64,1536]{1,0:T(8,128)(2,1)S(1)}, u32[]{:S(2)}, u32[]{:S(2)}) collective-permute-start(bf16[64,1536]{1,0:T(8,128)(2,1)} %shard_map.76.gy_ref), channel_id=1, source_target_pairs={{0,4},{1,5},{2,6},{3,7},{4,0},{5,1},{6,2},{7,3},{8,12},{9,13},{10,... | collective-permute-start | bytes 589832 | tf_op jit(solution)/shard_map/ppermute | solution.py:229
  6.6 3.6 %shard_map.77 = bf16[16,120,128]{2,1,0:T(8,128)(2,1)} custom-call(s32[32]{0:T(128)} %picks.5, bf16[128,384]{1,0:T(8,128)(2,1)} %x_ref.1, bf16[1536,384]{1,0:T(8,128)(2,1)} %a_hbm.1), custom_call_target="tpu_custom_call" | custom-call | flops 150994944 | bytes 1769600 | tf_op jit(solution)/shard_map/pallas_call | solution.py:24
  10.2 14.9 %all-to-all-start = ((bf16[16,120,128]{2,1,0:T(8,128)(2,1)}), bf16[16,120,128]{2,1,0:T(8,128)(2,1)S(1)}, u32[]{:S(2)}, u32[]{:S(2)}) async-start(bf16[16,120,128]{2,1,0:T(8,128)(2,1)} %shard_map.77), calls=%async_computation | async-start | bytes 983040 | tf_op jit(solution)/shard_map/all_to_all | solution.py:244
  25.2 4.6 %collective-permute-start.3 = (bf16[128,1536]{1,0:T(8,128)(2,1)S(1)}, bf16[128,1536]{1,0:T(8,128)(2,1)S(1)}, u32[]{:S(2)}, u32[]{:S(2)}) collective-permute-start(bf16[128,1536]{1,0:T(8,128)(2,1)S(1)} %pad_maximum_fusion.refs_0_), channel_id=1, source_target_pairs={{0,3},{1,0},{2,1},{3,2},{4,7},{5,4},{6,5},{7,6},{8,11},{9,8},{10,9... | collective-permute-start | bytes 1179656 | tf_op jit(solution)/shard_map/ppermute | solution.py:218
  29.9 1.9 %collective-permute-start.1 = (bf16[128,1536]{1,0:T(8,128)(2,1)S(1)}, bf16[128,1536]{1,0:T(8,128)(2,1)S(1)}, u32[]{:S(2)}, u32[]{:S(2)}) collective-permute-start(bf16[128,1536]{1,0:T(8,128)(2,1)S(1)} %pad_maximum_fusion.refs_0_), channel_id=1, source_target_pairs={{0,1},{1,2},{2,3},{3,0},{4,5},{5,6},{6,7},{7,4},{8,9},{9,10},{10,1... | collective-permute-start | bytes 1179656 | tf_op jit(solution)/shard_map/ppermute | solution.py:218
  31.9 3.7 %collective-permute-start.2 = (bf16[64,1536]{1,0:T(8,128)(2,1)S(1)}, bf16[64,1536]{1,0:T(8,128)(2,1)S(1)}, u32[]{:S(2)}, u32[]{:S(2)}) collective-permute-start(bf16[64,1536]{1,0:T(8,128)(2,1)S(1)} %pad_maximum_fusion.1), channel_id=1, source_target_pairs={{0,2},{1,3},{2,0},{3,1},{4,6},{5,7},{6,4},{7,5},{8,10},{9,11},{10,... | collective-permute-start | bytes 589832 | tf_op jit(solution)/shard_map/ppermute | solution.py:218
  35.6 9.7 %collective-permute-done.2.refs_2_ = bf16[64,1536]{1,0:T(8,128)(2,1)S(1)} collective-permute-done((bf16[64,1536]{1,0:T(8,128)(2,1)S(1)}, bf16[64,1536]{1,0:T(8,128)(2,1)S(1)}, u32[]{:S(2)}, u32[]{:S(2)}) %collective-permute-start.2) | collective-permute-done | bytes 196640 | tf_op jit(solution)/shard_map/ppermute | solution.py:218
  45.3 1.7 %copy-done = bf16[1536,768]{1,0:T(8,128)(2,1)S(1)} copy-done((bf16[1536,768]{1,0:T(8,128)(2,1)S(1)}, bf16[1536,768]{1,0:T(8,128)(2,1)}, u32[]{:S(2)}) %copy-start) | copy-done | bytes 2359320
  46.9 0.9 shard_map.78
  47.8 5.4 %collective-permute-start.4 = (bf16[128,768]{1,0:T(8,128)(2,1)S(1)}, bf16[128,768]{1,0:T(8,128)(2,1)S(1)}, u32[]{:S(2)}, u32[]{:S(2)}) collective-permute-start(bf16[128,768]{1,0:T(8,128)(2,1)S(1)} %get-tuple-element.19), channel_id=1, source_target_pairs={{0,128},{128,0},{256,384},{384,256},{1,129},{129,1},{257,385},{385... | collective-permute-start | bytes 589832 | tf_op jit(solution)/shard_map/ppermute | solution.py:260
  53.2 1.0 %collective-permute-done.4 = bf16[128,768]{1,0:T(8,128)(2,1)S(1)} collective-permute-done((bf16[128,768]{1,0:T(8,128)(2,1)S(1)}, bf16[128,768]{1,0:T(8,128)(2,1)S(1)}, u32[]{:S(2)}, u32[]{:S(2)}) %collective-permute-start.4) | collective-permute-done | bytes 196640 | tf_op jit(solution)/shard_map/ppermute | solution.py:260
  54.3 4.3 %collective-permute-start.5 = (bf16[128,768]{1,0:T(8,128)(2,1)S(1)}, bf16[128,768]{1,0:T(8,128)(2,1)S(1)}, u32[]{:S(2)}, u32[]{:S(2)}) collective-permute-start(bf16[128,768]{1,0:T(8,128)(2,1)S(1)} %fusion), channel_id=1, source_target_pairs={{0,256},{128,384},{256,0},{384,128},{1,257},{129,385},{257,1},{385... | collective-permute-start | bytes 589832 | tf_op jit(solution)/shard_map/ppermute | solution.py:264
  58.7 1.0 shard_map.79.side_ref
  59.7 1.9 %collective-permute-start.6 = (bf16[64,1536]{1,0:T(8,128)(2,1)S(1)}, bf16[64,1536]{1,0:T(8,128)(2,1)S(1)}, u32[]{:S(2)}, u32[]{:S(2)}) collective-permute-start(bf16[64,1536]{1,0:T(8,128)(2,1)S(1)} %slice.22), channel_id=1, source_target_pairs={{0,3},{1,0},{2,1},{3,2},{4,7},{5,4},{6,5},{7,6},{8,11},{9,8},{10,9... | collective-permute-start | bytes 589832 | tf_op jit(solution)/shard_map/ppermute | solution.py:218
  61.6 2.2 %collective-permute-done.5 = bf16[128,768]{1,0:T(8,128)(2,1)S(1)} collective-permute-done((bf16[128,768]{1,0:T(8,128)(2,1)S(1)}, bf16[128,768]{1,0:T(8,128)(2,1)S(1)}, u32[]{:S(2)}, u32[]{:S(2)}) %collective-permute-start.5) | collective-permute-done | bytes 196640 | tf_op jit(solution)/shard_map/ppermute | solution.py:264
  63.8 0.1 add_convert_fusion.refs_0_
  63.9 1.3 %shard_map.80 = bf16[4,8,160,128]{3,2,1,0:T(8,128)(2,1)} custom-call(bf16[16,120,128]{2,1,0:T(8,128)(2,1)S(1)} %all-to-all-done.got_ref, bf16[8,64,128]{2,1,0:T(8,128)(2,1)S(1)} %shard_map.79.side_ref), custom_call_target="tpu_custom_call" | custom-call | flops 1000000 | bytes 1933312 | tf_op jit(solution)/shard_map/pallas_call | solution.py:24
  65.2 2.2 %collective-permute-done.6.refs_2_ = bf16[64,1536]{1,0:T(8,128)(2,1)S(1)} collective-permute-done((bf16[64,1536]{1,0:T(8,128)(2,1)S(1)}, bf16[64,1536]{1,0:T(8,128)(2,1)S(1)}, u32[]{:S(2)}, u32[]{:S(2)}) %collective-permute-start.6) | collective-permute-done | bytes 196640 | tf_op jit(solution)/shard_map/ppermute | solution.py:218
  67.4 0.7 copy-done.5
  68.0 5.2 %all-to-all-start.1 = ((bf16[32,160,128]{2,1,0:T(8,128)(2,1)}), bf16[32,160,128]{2,1,0:T(8,128)(2,1)S(1)}, u32[]{:S(2)}, u32[]{:S(2)}) async-start(bf16[32,160,128]{2,1,0:T(8,128)(2,1)} %bitcast), calls=%async_computation.1 | async-start | bytes 2621440 | tf_op jit(solution)/shard_map/all_to_all | solution.py:280
  73.2 4.5 %collective-permute-start.9 = (bf16[128,768]{1,0:T(8,128)(2,1)S(1)}, bf16[128,768]{1,0:T(8,128)(2,1)S(1)}, u32[]{:S(2)}, u32[]{:S(2)}) collective-permute-start(bf16[128,768]{1,0:T(8,128)(2,1)S(1)} %add_convert_fusion.refs_0_), channel_id=1, source_target_pairs={{0,120},{8,0},{16,8},{24,16},{32,24},{40,32},{48,40},{56,48},{64,5... | collective-permute-start | bytes 589832 | tf_op jit(solution)/shard_map/ppermute | solution.py:283
  77.7 1.9 %collective-permute-start.8 = (bf16[128,768]{1,0:T(8,128)(2,1)S(1)}, bf16[128,768]{1,0:T(8,128)(2,1)S(1)}, u32[]{:S(2)}, u32[]{:S(2)}) collective-permute-start(bf16[128,768]{1,0:T(8,128)(2,1)S(1)} %add_convert_fusion.refs_0_), channel_id=1, source_target_pairs={{0,8},{8,16},{16,24},{24,32},{32,40},{40,48},{48,56},{56,64},{64,7... | collective-permute-start | bytes 589832 | tf_op jit(solution)/shard_map/ppermute | solution.py:283
  79.6 3.0 %collective-permute-start.7 = (bf16[128,768]{1,0:T(8,128)(2,1)S(1)}, bf16[128,768]{1,0:T(8,128)(2,1)S(1)}, u32[]{:S(2)}, u32[]{:S(2)}) collective-permute-start(bf16[128,768]{1,0:T(8,128)(2,1)S(1)} %add_convert_fusion.refs_0_), channel_id=1, source_target_pairs={{0,16},{8,24},{16,32},{24,40},{32,48},{40,56},{48,64},{56,72},{64,... | collective-permute-start | bytes 589832 | tf_op jit(solution)/shard_map/ppermute | solution.py:283
  82.7 4.3 %collective-permute-done.8.refs_2_ = bf16[128,768]{1,0:T(8,128)(2,1)S(1)} collective-permute-done((bf16[128,768]{1,0:T(8,128)(2,1)S(1)}, bf16[128,768]{1,0:T(8,128)(2,1)S(1)}, u32[]{:S(2)}, u32[]{:S(2)}) %collective-permute-start.8) | collective-permute-done | bytes 196640 | tf_op jit(solution)/shard_map/ppermute | solution.py:283
  87.0 5.7 %collective-permute-done.7.refs_1_ = bf16[128,768]{1,0:T(8,128)(2,1)S(1)} collective-permute-done((bf16[128,768]{1,0:T(8,128)(2,1)S(1)}, bf16[128,768]{1,0:T(8,128)(2,1)S(1)}, u32[]{:S(2)}, u32[]{:S(2)}) %collective-permute-start.7) | collective-permute-done | bytes 196640 | tf_op jit(solution)/shard_map/ppermute | solution.py:283
  92.7 0.7 copy-done.3
  93.4 0.9 copy-done.4
  94.3 0.5 shard_map.81
  94.8 3.8 %collective-permute-start.10 = (bf16[96,768]{1,0:T(8,128)(2,1)S(1)}, bf16[96,768]{1,0:T(8,128)(2,1)S(1)}, u32[]{:S(2)}, u32[]{:S(2)}) collective-permute-start(bf16[96,768]{1,0:T(8,128)(2,1)S(1)} %get-tuple-element.24), channel_id=1, source_target_pairs={{0,128},{128,0},{256,384},{384,256},{1,129},{129,1},{257,385},{385... | collective-permute-start | bytes 442376 | tf_op jit(solution)/shard_map/ppermute | solution.py:293
  98.6 1.4 %shard_map.82 = (f32[48,1536]{1,0:T(8,128)}, f32[48,1536]{1,0:T(8,128)}) custom-call(bf16[4,8,160,128]{3,2,1,0:T(8,128)(2,1)S(1)} %bitcast.3, bf16[128,1536]{1,0:T(8,128)(2,1)S(1)} %pad_maximum_fusion.refs_0_, bf16[128,1536]{1,0:T(8,128)(2,1)S(1)} %collective-permute-done.1.refs_1_, bf16[64,1536]{1,0:T(8,128)(2,1)S(1)} %copy-done.6, ...), custom_call_target="tpu_custom_call" | custom-call | flops 201326592 | bytes 3276800 | tf_op jit(solution)/shard_map/pallas_call | solution.py:24
  100.0 0.7 convert_add_fusion.1
  (25 shorter events, 0.2 us)
Async XLA Ops:
  2.5 22.6 %copy-start.1 = (bf16[64,1536]{1,0:T(8,128)(2,1)S(1)}, bf16[64,1536]{1,0:T(8,128)(2,1)}, u32[]{:S(2)}) copy-start(bf16[64,1536]{1,0:T(8,128)(2,1)} %shard_map.76.gy_ref) | copy-start | bytes 589828
  2.5 22.6 %collective-permute-start = (bf16[64,1536]{1,0:T(8,128)(2,1)}, bf16[64,1536]{1,0:T(8,128)(2,1)S(1)}, u32[]{:S(2)}, u32[]{:S(2)}) collective-permute-start(bf16[64,1536]{1,0:T(8,128)(2,1)} %shard_map.76.gy_ref), channel_id=1, source_target_pairs={{0,4},{1,5},{2,6},{3,7},{4,0},{5,1},{6,2},{7,3},{8,12},{9,13},{10,... | collective-permute-start | bytes 589832 | tf_op jit(solution)/shard_map/ppermute | solution.py:229
  10.2 53.7 %all-to-all-start = ((bf16[16,120,128]{2,1,0:T(8,128)(2,1)}), bf16[16,120,128]{2,1,0:T(8,128)(2,1)S(1)}, u32[]{:S(2)}, u32[]{:S(2)}) async-start(bf16[16,120,128]{2,1,0:T(8,128)(2,1)} %shard_map.77), calls=%async_computation | async-start | bytes 983040 | tf_op jit(solution)/shard_map/all_to_all | solution.py:244
  25.2 20.0 %collective-permute-start.3 = (bf16[128,1536]{1,0:T(8,128)(2,1)S(1)}, bf16[128,1536]{1,0:T(8,128)(2,1)S(1)}, u32[]{:S(2)}, u32[]{:S(2)}) collective-permute-start(bf16[128,1536]{1,0:T(8,128)(2,1)S(1)} %pad_maximum_fusion.refs_0_), channel_id=1, source_target_pairs={{0,3},{1,0},{2,1},{3,2},{4,7},{5,4},{6,5},{7,6},{8,11},{9,8},{10,9... | collective-permute-start | bytes 1179656 | tf_op jit(solution)/shard_map/ppermute | solution.py:218
  29.9 15.4 %collective-permute-start.1 = (bf16[128,1536]{1,0:T(8,128)(2,1)S(1)}, bf16[128,1536]{1,0:T(8,128)(2,1)S(1)}, u32[]{:S(2)}, u32[]{:S(2)}) collective-permute-start(bf16[128,1536]{1,0:T(8,128)(2,1)S(1)} %pad_maximum_fusion.refs_0_), channel_id=1, source_target_pairs={{0,1},{1,2},{2,3},{3,0},{4,5},{5,6},{6,7},{7,4},{8,9},{9,10},{10,1... | collective-permute-start | bytes 1179656 | tf_op jit(solution)/shard_map/ppermute | solution.py:218
  31.8 26.8 %copy-start.2 = (bf16[128,384]{1,0:T(8,128)(2,1)S(1)}, bf16[128,384]{1,0:T(8,128)(2,1)}, u32[]{:S(2)}) copy-start(bf16[128,384]{1,0:T(8,128)(2,1)} %x_ref.1) | copy-start | bytes 294916
  31.8 26.8 %copy-start.7 = (s32[32]{0:T(128)S(1)}, s32[32]{0:T(128)}, u32[]{:S(2)}) copy-start(s32[32]{0:T(128)} %picks.5) | copy-start | bytes 388
  31.9 13.4 %collective-permute-start.2 = (bf16[64,1536]{1,0:T(8,128)(2,1)S(1)}, bf16[64,1536]{1,0:T(8,128)(2,1)S(1)}, u32[]{:S(2)}, u32[]{:S(2)}) collective-permute-start(bf16[64,1536]{1,0:T(8,128)(2,1)S(1)} %pad_maximum_fusion.1), channel_id=1, source_target_pairs={{0,2},{1,3},{2,0},{3,1},{4,6},{5,7},{6,4},{7,5},{8,10},{9,11},{10,... | collective-permute-start | bytes 589832 | tf_op jit(solution)/shard_map/ppermute | solution.py:218
  45.3 1.7 %copy-start = (bf16[1536,768]{1,0:T(8,128)(2,1)S(1)}, bf16[1536,768]{1,0:T(8,128)(2,1)}, u32[]{:S(2)}) copy-start(bf16[1536,768]{1,0:T(8,128)(2,1)} %b_ref.1) | copy-start | bytes 7077892
  47.8 6.4 %collective-permute-start.4 = (bf16[128,768]{1,0:T(8,128)(2,1)S(1)}, bf16[128,768]{1,0:T(8,128)(2,1)S(1)}, u32[]{:S(2)}, u32[]{:S(2)}) collective-permute-start(bf16[128,768]{1,0:T(8,128)(2,1)S(1)} %get-tuple-element.19), channel_id=1, source_target_pairs={{0,128},{128,0},{256,384},{384,256},{1,129},{129,1},{257,385},{385... | collective-permute-start | bytes 589832 | tf_op jit(solution)/shard_map/ppermute | solution.py:260
  54.3 9.5 %collective-permute-start.5 = (bf16[128,768]{1,0:T(8,128)(2,1)S(1)}, bf16[128,768]{1,0:T(8,128)(2,1)S(1)}, u32[]{:S(2)}, u32[]{:S(2)}) collective-permute-start(bf16[128,768]{1,0:T(8,128)(2,1)S(1)} %fusion), channel_id=1, source_target_pairs={{0,256},{128,384},{256,0},{384,128},{1,257},{129,385},{257,1},{385... | collective-permute-start | bytes 589832 | tf_op jit(solution)/shard_map/ppermute | solution.py:264
  59.7 7.7 %collective-permute-start.6 = (bf16[64,1536]{1,0:T(8,128)(2,1)S(1)}, bf16[64,1536]{1,0:T(8,128)(2,1)S(1)}, u32[]{:S(2)}, u32[]{:S(2)}) collective-permute-start(bf16[64,1536]{1,0:T(8,128)(2,1)S(1)} %slice.22), channel_id=1, source_target_pairs={{0,3},{1,0},{2,1},{3,2},{4,7},{5,4},{6,5},{7,6},{8,11},{9,8},{10,9... | collective-permute-start | bytes 589832 | tf_op jit(solution)/shard_map/ppermute | solution.py:218
  67.4 0.7 copy-start.5
  68.0 25.4 %all-to-all-start.1 = ((bf16[32,160,128]{2,1,0:T(8,128)(2,1)}), bf16[32,160,128]{2,1,0:T(8,128)(2,1)S(1)}, u32[]{:S(2)}, u32[]{:S(2)}) async-start(bf16[32,160,128]{2,1,0:T(8,128)(2,1)} %bitcast), calls=%async_computation.1 | async-start | bytes 2621440 | tf_op jit(solution)/shard_map/all_to_all | solution.py:280
  73.2 9.5 %collective-permute-start.9 = (bf16[128,768]{1,0:T(8,128)(2,1)S(1)}, bf16[128,768]{1,0:T(8,128)(2,1)S(1)}, u32[]{:S(2)}, u32[]{:S(2)}) collective-permute-start(bf16[128,768]{1,0:T(8,128)(2,1)S(1)} %add_convert_fusion.refs_0_), channel_id=1, source_target_pairs={{0,120},{8,0},{16,8},{24,16},{32,24},{40,32},{48,40},{56,48},{64,5... | collective-permute-start | bytes 589832 | tf_op jit(solution)/shard_map/ppermute | solution.py:283
  77.7 9.3 %collective-permute-start.8 = (bf16[128,768]{1,0:T(8,128)(2,1)S(1)}, bf16[128,768]{1,0:T(8,128)(2,1)S(1)}, u32[]{:S(2)}, u32[]{:S(2)}) collective-permute-start(bf16[128,768]{1,0:T(8,128)(2,1)S(1)} %add_convert_fusion.refs_0_), channel_id=1, source_target_pairs={{0,8},{8,16},{16,24},{24,32},{32,40},{40,48},{48,56},{56,64},{64,7... | collective-permute-start | bytes 589832 | tf_op jit(solution)/shard_map/ppermute | solution.py:283
  79.6 13.1 %collective-permute-start.7 = (bf16[128,768]{1,0:T(8,128)(2,1)S(1)}, bf16[128,768]{1,0:T(8,128)(2,1)S(1)}, u32[]{:S(2)}, u32[]{:S(2)}) collective-permute-start(bf16[128,768]{1,0:T(8,128)(2,1)S(1)} %add_convert_fusion.refs_0_), channel_id=1, source_target_pairs={{0,16},{8,24},{16,32},{24,40},{32,48},{40,56},{48,64},{56,72},{64,... | collective-permute-start | bytes 589832 | tf_op jit(solution)/shard_map/ppermute | solution.py:283
  92.7 0.7 copy-start.3
  93.4 0.9 copy-start.4
  94.3 4.2 %copy-start.6 = (bf16[64,1536]{1,0:T(8,128)(2,1)S(1)}, bf16[64,1536]{1,0:T(8,128)(2,1)}, u32[]{:S(2)}) copy-start(bf16[64,1536]{1,0:T(8,128)(2,1)} %copy-done.5) | copy-start | bytes 589828
  94.8 5.2 %collective-permute-start.10 = (bf16[96,768]{1,0:T(8,128)(2,1)S(1)}, bf16[96,768]{1,0:T(8,128)(2,1)S(1)}, u32[]{:S(2)}, u32[]{:S(2)}) collective-permute-start(bf16[96,768]{1,0:T(8,128)(2,1)S(1)} %get-tuple-element.24), channel_id=1, source_target_pairs={{0,128},{128,0},{256,384},{384,256},{1,129},{129,1},{257,385},{385... | collective-permute-start | bytes 442376 | tf_op jit(solution)/shard_map/ppermute | solution.py:293

commit v26 on v24

--- a/solution.py
+++ b/solution.py
@@ -262,7 +262,6 @@
     give = some.astype(BF)
     first, unused = lax.optimization_barrier((first, give))
     taken = lax.ppermute(give, "grp", [(i, i ^ 2) for i in range(n_grp)])
-    right = (some + taken.astype(F32)).astype(BF)
     side = call(
         side_kernel,
         (sample_rows, tokens_in, picked),
@@ -275,6 +274,8 @@
         [shape((n_grp, n_col, size * spread + strip * n_row // n_grp, LANES), BF)],
         1000000,
     )[0]
+    taken, send = lax.optimization_barrier((taken, send))
+    right = (some + taken.astype(F32)).astype(BF)
     send, right = lax.optimization_barrier((send, right))
     got = lax.all_to_all(send.reshape((n_grp * n_col,) + send.shape[2:]), ("grp", "col"), 0, 0)
     got = got.reshape(send.shape)
@@ -282,7 +283,7 @@
         lax.ppermute(right, "row", [(i, (i + j) % n_row) for i in range(n_row)])
         for j in SHIFTS[1:]
     ]
-    unused, beyond = lax.optimization_barrier((rights[1], after[2 * cut :]))
+    unused, beyond = lax.optimization_barrier((right, after[2 * cut :]))
     far = along_y(beyond, 3)
 
     rights, far = lax.optimization_barrier((rights, far))

time: 99.6 us -> 96.2 us (0.966)
  starting transfers between devices: 66.7 us -> 64.2 us
    ppermute x2, starting transfers between devices: 9.66 us -> 7 us  [body(): taken = lax.ppermute(give, 'grp', [(i, i ^ 1) for i in range(n_grp)])]
    ppermute x1, waiting for transfers between devices: 4.17 us -> 2.87 us  [body(): taken = lax.ppermute(give, 'grp', [(i, i ^ 2) for i in range(n_grp)])]
    ppermute x4, waiting for transfers between devices: 8.04 us -> 9.2 us  [along_y(): lax.ppermute(block, 'col', [(i, i - i % 4 + (i + k) % 4) for i in range(n...]
  transfers between devices with their start and end apart: 13 -> 13, of which waited for: 6 -> 5; matrix products, arithmetic and copies ran while one was open for 0% -> 0% of each run, Pallas kernels for 7% -> 9%
where the time goes in v26:
time: 96.2 us; the launch traced here: 95.5 us
  starting transfers between devices  64.2 us (67%)
  waiting for transfers between devices  17.2 us (18%)
  Pallas kernels  10.5 us (11%)
  local copies, waits for them, and re-layouts  1.73 us (2%)
    all_to_all x1, starting transfers between devices, body(): first = lax.all_to_all(payload, 'row', 0, 0)  14.9 us
    ppermute x4, starting transfers between devices, along_y(): lax.ppermute(block, 'col', [(i, i - i % 4 + (i + k) % 4) for i in range(n...  14.7 us
    ppermute x3, starting transfers between devices, body(): lax.ppermute(right, 'row', [(i, (i + j) % n_row) for i in range(n_row)])  10.7 us
    pallas_call x7, Pallas kernels, call(): pl.pallas_call(kernel, out_shape=outs, in_specs=places, out_specs=[VMEM]...  10.5 us
    ppermute x4, waiting for transfers between devices, along_y(): lax.ppermute(block, 'col', [(i, i - i % 4 + (i + k) % 4) for i in range(n...  9.2 us
    all_to_all x1, starting transfers between devices, body(): lax.all_to_all(send.reshape((n_grp * n_col,) + send.shape[2:]), ('grp', '...  8.49 us
    ppermute x2, starting transfers between devices, body(): taken = lax.ppermute(give, 'grp', [(i, i ^ 1) for i in range(n_grp)])  7 us
    ppermute x1, starting transfers between devices, body(): taken = lax.ppermute(give, 'grp', [(i, i ^ 2) for i in range(n_grp)])  4.35 us
  transfers between devices with their start and end apart: 13, of which 5 were waited for; matrix products, arithmetic and copies ran while one was open for 0% of the time, Pallas kernels for 9%

profile of v26, /device:TPU:1, one launch (start us, length us, event | category | flops | bytes accessed | tf_op | source)
XLA Modules:
  0.0 95.5 jit_solution(3473807510161658017)
XLA Ops:
  0.6 1.9 %shard_map.76.gy_ref = bf16[64,1536]{1,0:T(8,128)(2,1)} custom-call(s32[32]{0:T(128)} %picks.5, bf16[128,1536]{1,0:T(8,128)(2,1)} %g_ref.1), custom_call_target="tpu_custom_call" | custom-call | flops 25165824 | bytes 589952 | tf_op jit(solution)/shard_map/pallas_call | solution.py:24
  2.5 4.1 %collective-permute-start = (bf16[64,1536]{1,0:T(8,128)(2,1)}, bf16[64,1536]{1,0:T(8,128)(2,1)S(1)}, u32[]{:S(2)}, u32[]{:S(2)}) collective-permute-start(bf16[64,1536]{1,0:T(8,128)(2,1)} %shard_map.76.gy_ref), channel_id=1, source_target_pairs={{0,4},{1,5},{2,6},{3,7},{4,0},{5,1},{6,2},{7,3},{8,12},{9,13},{10,... | collective-permute-start | bytes 589832 | tf_op jit(solution)/shard_map/ppermute | solution.py:229
  6.6 3.6 %shard_map.78 = bf16[16,120,128]{2,1,0:T(8,128)(2,1)} custom-call(s32[32]{0:T(128)} %picks.5, bf16[128,384]{1,0:T(8,128)(2,1)} %x_ref.1, bf16[1536,384]{1,0:T(8,128)(2,1)} %a_hbm.1), custom_call_target="tpu_custom_call" | custom-call | flops 150994944 | bytes 1769600 | tf_op jit(solution)/shard_map/pallas_call | solution.py:24
  10.2 14.9 %all-to-all-start = ((bf16[16,120,128]{2,1,0:T(8,128)(2,1)}), bf16[16,120,128]{2,1,0:T(8,128)(2,1)S(1)}, u32[]{:S(2)}, u32[]{:S(2)}) async-start(bf16[16,120,128]{2,1,0:T(8,128)(2,1)} %shard_map.78), calls=%async_computation | async-start | bytes 983040 | tf_op jit(solution)/shard_map/all_to_all | solution.py:244
  25.2 0.0 collective-permute-done
  25.2 3.2 %collective-permute-start.1 = (bf16[128,1536]{1,0:T(8,128)(2,1)S(1)}, bf16[128,1536]{1,0:T(8,128)(2,1)S(1)}, u32[]{:S(2)}, u32[]{:S(2)}) collective-permute-start(bf16[128,1536]{1,0:T(8,128)(2,1)S(1)} %pad_maximum_fusion.refs_0_), channel_id=1, source_target_pairs={{0,1},{1,2},{2,3},{3,0},{4,5},{5,6},{6,7},{7,4},{8,9},{9,10},{10,1... | collective-permute-start | bytes 1179656 | tf_op jit(solution)/shard_map/ppermute | solution.py:218
  28.4 3.4 %collective-permute-start.3 = (bf16[128,1536]{1,0:T(8,128)(2,1)S(1)}, bf16[128,1536]{1,0:T(8,128)(2,1)S(1)}, u32[]{:S(2)}, u32[]{:S(2)}) collective-permute-start(bf16[128,1536]{1,0:T(8,128)(2,1)S(1)} %pad_maximum_fusion.refs_0_), channel_id=1, source_target_pairs={{0,3},{1,0},{2,1},{3,2},{4,7},{5,4},{6,5},{7,6},{8,11},{9,8},{10,9... | collective-permute-start | bytes 1179656 | tf_op jit(solution)/shard_map/ppermute | solution.py:218
  31.8 0.0 copy-start.2
  31.8 0.0 copy-start.3
  31.9 3.7 %collective-permute-start.2 = (bf16[64,1536]{1,0:T(8,128)(2,1)S(1)}, bf16[64,1536]{1,0:T(8,128)(2,1)S(1)}, u32[]{:S(2)}, u32[]{:S(2)}) collective-permute-start(bf16[64,1536]{1,0:T(8,128)(2,1)S(1)} %pad_maximum_fusion.1), channel_id=1, source_target_pairs={{0,2},{1,3},{2,0},{3,1},{4,6},{5,7},{6,4},{7,5},{8,10},{9,11},{10,... | collective-permute-start | bytes 589832 | tf_op jit(solution)/shard_map/ppermute | solution.py:218
  35.5 7.6 %collective-permute-done.2.refs_2_ = bf16[64,1536]{1,0:T(8,128)(2,1)S(1)} collective-permute-done((bf16[64,1536]{1,0:T(8,128)(2,1)S(1)}, bf16[64,1536]{1,0:T(8,128)(2,1)S(1)}, u32[]{:S(2)}, u32[]{:S(2)}) %collective-permute-start.2) | collective-permute-done | bytes 196640 | tf_op jit(solution)/shard_map/ppermute | solution.py:218
  43.2 1.7 %copy-done = bf16[1536,768]{1,0:T(8,128)(2,1)S(1)} copy-done((bf16[1536,768]{1,0:T(8,128)(2,1)S(1)}, bf16[1536,768]{1,0:T(8,128)(2,1)}, u32[]{:S(2)}) %copy-start) | copy-done | bytes 2359320
  44.8 0.9 shard_map.77
  45.7 4.1 %collective-permute-start.4 = (bf16[128,768]{1,0:T(8,128)(2,1)S(1)}, bf16[128,768]{1,0:T(8,128)(2,1)S(1)}, u32[]{:S(2)}, u32[]{:S(2)}) collective-permute-start(bf16[128,768]{1,0:T(8,128)(2,1)S(1)} %get-tuple-element.25), channel_id=1, source_target_pairs={{0,128},{128,0},{256,384},{384,256},{1,129},{129,1},{257,385},{385... | collective-permute-start | bytes 589832 | tf_op jit(solution)/shard_map/ppermute | solution.py:260
  49.8 1.0 %collective-permute-done.4 = bf16[128,768]{1,0:T(8,128)(2,1)S(1)} collective-permute-done((bf16[128,768]{1,0:T(8,128)(2,1)S(1)}, bf16[128,768]{1,0:T(8,128)(2,1)S(1)}, u32[]{:S(2)}, u32[]{:S(2)}) %collective-permute-start.4) | collective-permute-done | bytes 196640 | tf_op jit(solution)/shard_map/ppermute | solution.py:260
  50.9 4.3 %collective-permute-start.5 = (bf16[128,768]{1,0:T(8,128)(2,1)S(1)}, bf16[128,768]{1,0:T(8,128)(2,1)S(1)}, u32[]{:S(2)}, u32[]{:S(2)}) collective-permute-start(bf16[128,768]{1,0:T(8,128)(2,1)S(1)} %fusion), channel_id=1, source_target_pairs={{0,256},{128,384},{256,0},{384,128},{1,257},{129,385},{257,1},{385... | collective-permute-start | bytes 589832 | tf_op jit(solution)/shard_map/ppermute | solution.py:264
  55.3 1.0 %shard_map.79.side_ref = bf16[8,64,128]{2,1,0:T(8,128)(2,1)S(1)} custom-call(s32[32]{0:T(128)S(1)} %copy-done.3, bf16[128,384]{1,0:T(8,128)(2,1)S(1)} %copy-done.2, bf16[64,1536]{1,0:T(8,128)(2,1)S(1)} %copy-done.1), custom_call_target="tpu_custom_call" | custom-call | flops 3145728 | bytes 426112 | tf_op jit(solution)/shard_map/pallas_call | solution.py:24
  56.2 0.0 all-to-all-done.got_ref
  56.3 1.3 %shard_map.80 = bf16[4,8,160,128]{3,2,1,0:T(8,128)(2,1)} custom-call(bf16[16,120,128]{2,1,0:T(8,128)(2,1)S(1)} %all-to-all-done.got_ref, bf16[8,64,128]{2,1,0:T(8,128)(2,1)S(1)} %shard_map.79.side_ref), custom_call_target="tpu_custom_call" | custom-call | flops 1000000 | bytes 1933312 | tf_op jit(solution)/shard_map/pallas_call | solution.py:24
  57.5 2.9 %collective-permute-done.5 = bf16[128,768]{1,0:T(8,128)(2,1)S(1)} collective-permute-done((bf16[128,768]{1,0:T(8,128)(2,1)S(1)}, bf16[128,768]{1,0:T(8,128)(2,1)S(1)}, u32[]{:S(2)}, u32[]{:S(2)}) %collective-permute-start.5) | collective-permute-done | bytes 196640 | tf_op jit(solution)/shard_map/ppermute | solution.py:264
  60.4 0.1 add_convert_fusion.refs_0_
  60.5 8.5 %all-to-all-start.1 = ((bf16[32,160,128]{2,1,0:T(8,128)(2,1)}), bf16[32,160,128]{2,1,0:T(8,128)(2,1)S(1)}, u32[]{:S(2)}, u32[]{:S(2)}) async-start(bf16[32,160,128]{2,1,0:T(8,128)(2,1)} %bitcast), calls=%async_computation.1 | async-start | bytes 2621440 | tf_op jit(solution)/shard_map/all_to_all | solution.py:280
  69.0 4.2 %collective-permute-start.6 = (bf16[128,768]{1,0:T(8,128)(2,1)S(1)}, bf16[128,768]{1,0:T(8,128)(2,1)S(1)}, u32[]{:S(2)}, u32[]{:S(2)}) collective-permute-start(bf16[128,768]{1,0:T(8,128)(2,1)S(1)} %add_convert_fusion.refs_0_), channel_id=1, source_target_pairs={{0,16},{8,24},{16,32},{24,40},{32,48},{40,56},{48,64},{56,72},{64,... | collective-permute-start | bytes 589832 | tf_op jit(solution)/shard_map/ppermute | solution.py:283
  73.2 3.1 %collective-permute-start.7 = (bf16[128,768]{1,0:T(8,128)(2,1)S(1)}, bf16[128,768]{1,0:T(8,128)(2,1)S(1)}, u32[]{:S(2)}, u32[]{:S(2)}) collective-permute-start(bf16[128,768]{1,0:T(8,128)(2,1)S(1)} %add_convert_fusion.refs_0_), channel_id=1, source_target_pairs={{0,8},{8,16},{16,24},{24,32},{32,40},{40,48},{48,56},{56,64},{64,7... | collective-permute-start | bytes 589832 | tf_op jit(solution)/shard_map/ppermute | solution.py:283
  76.3 3.4 %collective-permute-start.8 = (bf16[128,768]{1,0:T(8,128)(2,1)S(1)}, bf16[128,768]{1,0:T(8,128)(2,1)S(1)}, u32[]{:S(2)}, u32[]{:S(2)}) collective-permute-start(bf16[128,768]{1,0:T(8,128)(2,1)S(1)} %add_convert_fusion.refs_0_), channel_id=1, source_target_pairs={{0,120},{8,0},{16,8},{24,16},{32,24},{40,32},{48,40},{56,48},{64,5... | collective-permute-start | bytes 589832 | tf_op jit(solution)/shard_map/ppermute | solution.py:283
  79.7 4.5 %collective-permute-start.9 = (bf16[64,1536]{1,0:T(8,128)(2,1)S(1)}, bf16[64,1536]{1,0:T(8,128)(2,1)S(1)}, u32[]{:S(2)}, u32[]{:S(2)}) collective-permute-start(bf16[64,1536]{1,0:T(8,128)(2,1)S(1)} %slice.22), channel_id=1, source_target_pairs={{0,3},{1,0},{2,1},{3,2},{4,7},{5,4},{6,5},{7,6},{8,11},{9,8},{10,9... | collective-permute-start | bytes 589832 | tf_op jit(solution)/shard_map/ppermute | solution.py:218
  84.2 4.1 %collective-permute-done.7.refs_2_ = bf16[128,768]{1,0:T(8,128)(2,1)S(1)} collective-permute-done((bf16[128,768]{1,0:T(8,128)(2,1)S(1)}, bf16[128,768]{1,0:T(8,128)(2,1)S(1)}, u32[]{:S(2)}, u32[]{:S(2)}) %collective-permute-start.7) | collective-permute-done | bytes 196640 | tf_op jit(solution)/shard_map/ppermute | solution.py:283
  88.3 1.6 %collective-permute-done.9.refs_2_ = bf16[64,1536]{1,0:T(8,128)(2,1)S(1)} collective-permute-done((bf16[64,1536]{1,0:T(8,128)(2,1)S(1)}, bf16[64,1536]{1,0:T(8,128)(2,1)S(1)}, u32[]{:S(2)}, u32[]{:S(2)}) %collective-permute-start.9) | collective-permute-done | bytes 196640 | tf_op jit(solution)/shard_map/ppermute | solution.py:218
  89.9 0.5 shard_map.81
  90.3 2.9 %collective-permute-start.10 = (bf16[96,768]{1,0:T(8,128)(2,1)S(1)}, bf16[96,768]{1,0:T(8,128)(2,1)S(1)}, u32[]{:S(2)}, u32[]{:S(2)}) collective-permute-start(bf16[96,768]{1,0:T(8,128)(2,1)S(1)} %get-tuple-element.38), channel_id=1, source_target_pairs={{0,128},{128,0},{256,384},{384,256},{1,129},{129,1},{257,385},{385... | collective-permute-start | bytes 442376 | tf_op jit(solution)/shard_map/ppermute | solution.py:297
  93.3 1.4 %shard_map.82 = (f32[48,1536]{1,0:T(8,128)}, f32[48,1536]{1,0:T(8,128)}) custom-call(bf16[4,8,160,128]{3,2,1,0:T(8,128)(2,1)S(1)} %bitcast.3, bf16[128,1536]{1,0:T(8,128)(2,1)S(1)} %pad_maximum_fusion.refs_0_, bf16[128,1536]{1,0:T(8,128)(2,1)S(1)} %collective-permute-done.1.refs_1_, bf16[64,1536]{1,0:T(8,128)(2,1)S(1)} %collective-permute-done.9.refs_2_, ...), custom_call_target="tpu_custom_call" | custom-call | flops 201326592 | bytes 3276800 | tf_op jit(solution)/shard_map/pallas_call | solution.py:24
  94.7 0.7 convert_add_fusion.1
  (17 shorter events, 0.2 us)
Async XLA Ops:
  2.5 22.6 %copy-start.1 = (bf16[64,1536]{1,0:T(8,128)(2,1)S(1)}, bf16[64,1536]{1,0:T(8,128)(2,1)}, u32[]{:S(2)}) copy-start(bf16[64,1536]{1,0:T(8,128)(2,1)} %shard_map.76.gy_ref) | copy-start | bytes 589828
  2.5 22.6 %collective-permute-start = (bf16[64,1536]{1,0:T(8,128)(2,1)}, bf16[64,1536]{1,0:T(8,128)(2,1)S(1)}, u32[]{:S(2)}, u32[]{:S(2)}) collective-permute-start(bf16[64,1536]{1,0:T(8,128)(2,1)} %shard_map.76.gy_ref), channel_id=1, source_target_pairs={{0,4},{1,5},{2,6},{3,7},{4,0},{5,1},{6,2},{7,3},{8,12},{9,13},{10,... | collective-permute-start | bytes 589832 | tf_op jit(solution)/shard_map/ppermute | solution.py:229
  10.2 46.1 %all-to-all-start = ((bf16[16,120,128]{2,1,0:T(8,128)(2,1)}), bf16[16,120,128]{2,1,0:T(8,128)(2,1)S(1)}, u32[]{:S(2)}, u32[]{:S(2)}) async-start(bf16[16,120,128]{2,1,0:T(8,128)(2,1)} %shard_map.78), calls=%async_computation | async-start | bytes 983040 | tf_op jit(solution)/shard_map/all_to_all | solution.py:244
  25.2 17.9 %collective-permute-start.1 = (bf16[128,1536]{1,0:T(8,128)(2,1)S(1)}, bf16[128,1536]{1,0:T(8,128)(2,1)S(1)}, u32[]{:S(2)}, u32[]{:S(2)}) collective-permute-start(bf16[128,1536]{1,0:T(8,128)(2,1)S(1)} %pad_maximum_fusion.refs_0_), channel_id=1, source_target_pairs={{0,1},{1,2},{2,3},{3,0},{4,5},{5,6},{6,7},{7,4},{8,9},{9,10},{10,1... | collective-permute-start | bytes 1179656 | tf_op jit(solution)/shard_map/ppermute | solution.py:218
  28.4 14.7 %collective-permute-start.3 = (bf16[128,1536]{1,0:T(8,128)(2,1)S(1)}, bf16[128,1536]{1,0:T(8,128)(2,1)S(1)}, u32[]{:S(2)}, u32[]{:S(2)}) collective-permute-start(bf16[128,1536]{1,0:T(8,128)(2,1)S(1)} %pad_maximum_fusion.refs_0_), channel_id=1, source_target_pairs={{0,3},{1,0},{2,1},{3,2},{4,7},{5,4},{6,5},{7,6},{8,11},{9,8},{10,9... | collective-permute-start | bytes 1179656 | tf_op jit(solution)/shard_map/ppermute | solution.py:218
  31.8 23.4 %copy-start.2 = (bf16[128,384]{1,0:T(8,128)(2,1)S(1)}, bf16[128,384]{1,0:T(8,128)(2,1)}, u32[]{:S(2)}) copy-start(bf16[128,384]{1,0:T(8,128)(2,1)} %x_ref.1) | copy-start | bytes 294916
  31.8 23.4 %copy-start.3 = (s32[32]{0:T(128)S(1)}, s32[32]{0:T(128)}, u32[]{:S(2)}) copy-start(s32[32]{0:T(128)} %picks.5) | copy-start | bytes 388
  31.9 11.3 %collective-permute-start.2 = (bf16[64,1536]{1,0:T(8,128)(2,1)S(1)}, bf16[64,1536]{1,0:T(8,128)(2,1)S(1)}, u32[]{:S(2)}, u32[]{:S(2)}) collective-permute-start(bf16[64,1536]{1,0:T(8,128)(2,1)S(1)} %pad_maximum_fusion.1), channel_id=1, source_target_pairs={{0,2},{1,3},{2,0},{3,1},{4,6},{5,7},{6,4},{7,5},{8,10},{9,11},{10,... | collective-permute-start | bytes 589832 | tf_op jit(solution)/shard_map/ppermute | solution.py:218
  43.2 1.7 %copy-start = (bf16[1536,768]{1,0:T(8,128)(2,1)S(1)}, bf16[1536,768]{1,0:T(8,128)(2,1)}, u32[]{:S(2)}) copy-start(bf16[1536,768]{1,0:T(8,128)(2,1)} %b_ref.1) | copy-start | bytes 7077892
  45.7 5.1 %collective-permute-start.4 = (bf16[128,768]{1,0:T(8,128)(2,1)S(1)}, bf16[128,768]{1,0:T(8,128)(2,1)S(1)}, u32[]{:S(2)}, u32[]{:S(2)}) collective-permute-start(bf16[128,768]{1,0:T(8,128)(2,1)S(1)} %get-tuple-element.25), channel_id=1, source_target_pairs={{0,128},{128,0},{256,384},{384,256},{1,129},{129,1},{257,385},{385... | collective-permute-start | bytes 589832 | tf_op jit(solution)/shard_map/ppermute | solution.py:260
  50.9 9.5 %collective-permute-start.5 = (bf16[128,768]{1,0:T(8,128)(2,1)S(1)}, bf16[128,768]{1,0:T(8,128)(2,1)S(1)}, u32[]{:S(2)}, u32[]{:S(2)}) collective-permute-start(bf16[128,768]{1,0:T(8,128)(2,1)S(1)} %fusion), channel_id=1, source_target_pairs={{0,256},{128,384},{256,0},{384,128},{1,257},{129,385},{257,1},{385... | collective-permute-start | bytes 589832 | tf_op jit(solution)/shard_map/ppermute | solution.py:264
  60.5 29.4 %all-to-all-start.1 = ((bf16[32,160,128]{2,1,0:T(8,128)(2,1)}), bf16[32,160,128]{2,1,0:T(8,128)(2,1)S(1)}, u32[]{:S(2)}, u32[]{:S(2)}) async-start(bf16[32,160,128]{2,1,0:T(8,128)(2,1)} %bitcast), calls=%async_computation.1 | async-start | bytes 2621440 | tf_op jit(solution)/shard_map/all_to_all | solution.py:280
  69.0 15.2 %collective-permute-start.6 = (bf16[128,768]{1,0:T(8,128)(2,1)S(1)}, bf16[128,768]{1,0:T(8,128)(2,1)S(1)}, u32[]{:S(2)}, u32[]{:S(2)}) collective-permute-start(bf16[128,768]{1,0:T(8,128)(2,1)S(1)} %add_convert_fusion.refs_0_), channel_id=1, source_target_pairs={{0,16},{8,24},{16,32},{24,40},{32,48},{40,56},{48,64},{56,72},{64,... | collective-permute-start | bytes 589832 | tf_op jit(solution)/shard_map/ppermute | solution.py:283
  73.2 15.1 %collective-permute-start.7 = (bf16[128,768]{1,0:T(8,128)(2,1)S(1)}, bf16[128,768]{1,0:T(8,128)(2,1)S(1)}, u32[]{:S(2)}, u32[]{:S(2)}) collective-permute-start(bf16[128,768]{1,0:T(8,128)(2,1)S(1)} %add_convert_fusion.refs_0_), channel_id=1, source_target_pairs={{0,8},{8,16},{16,24},{24,32},{32,40},{40,48},{48,56},{56,64},{64,7... | collective-permute-start | bytes 589832 | tf_op jit(solution)/shard_map/ppermute | solution.py:283
  76.3 12.0 %collective-permute-start.8 = (bf16[128,768]{1,0:T(8,128)(2,1)S(1)}, bf16[128,768]{1,0:T(8,128)(2,1)S(1)}, u32[]{:S(2)}, u32[]{:S(2)}) collective-permute-start(bf16[128,768]{1,0:T(8,128)(2,1)S(1)} %add_convert_fusion.refs_0_), channel_id=1, source_target_pairs={{0,120},{8,0},{16,8},{24,16},{32,24},{40,32},{48,40},{56,48},{64,5... | collective-permute-start | bytes 589832 | tf_op jit(solution)/shard_map/ppermute | solution.py:283
  79.7 10.2 %collective-permute-start.9 = (bf16[64,1536]{1,0:T(8,128)(2,1)S(1)}, bf16[64,1536]{1,0:T(8,128)(2,1)S(1)}, u32[]{:S(2)}, u32[]{:S(2)}) collective-permute-start(bf16[64,1536]{1,0:T(8,128)(2,1)S(1)} %slice.22), channel_id=1, source_target_pairs={{0,3},{1,0},{2,1},{3,2},{4,7},{5,4},{6,5},{7,6},{8,11},{9,8},{10,9... | collective-permute-start | bytes 589832 | tf_op jit(solution)/shard_map/ppermute | solution.py:218
  90.3 4.4 %collective-permute-start.10 = (bf16[96,768]{1,0:T(8,128)(2,1)S(1)}, bf16[96,768]{1,0:T(8,128)(2,1)S(1)}, u32[]{:S(2)}, u32[]{:S(2)}) collective-permute-start(bf16[96,768]{1,0:T(8,128)(2,1)S(1)} %get-tuple-element.38), channel_id=1, source_target_pairs={{0,128},{128,0},{256,384},{384,256},{1,129},{129,1},{257,385},{385... | collective-permute-start | bytes 442376 | tf_op jit(solution)/shard_map/ppermute | solution.py:297

commit v27 on v26

--- a/solution.py
+++ b/solution.py
@@ -114,6 +114,19 @@
         block = jnp.concatenate([top, low], axis=0)
         block = jnp.concatenate([jnp.zeros((depth, LANES - 32), F32), block], axis=1)
         out_ref[c] = block.astype(BF)
+
+
+def stage_kernel(b_hbm, out_ref, sems):
+    parts = sems.shape[0]
+    step = out_ref.shape[0] // parts
+    copies = []
+    for p in range(parts):
+        span = pl.ds(p * step, step)
+        copies.append(pltpu.make_async_copy(b_hbm.at[span], out_ref.at[span], sems.at[p]))
+    for copy in copies:
+        copy.start()
+    for copy in copies:
+        copy.wait()
 
 
 def right_kernel(b_ref, *refs):
@@ -250,9 +263,21 @@
     after = along_y(pair, 3)
     before = along_y(pair, 1)
     pairs = [pair, before, along_y(rows, 2), after]
+    unused, factor = lax.optimization_barrier((beside, grad_inverse))
+    factor = pl.pallas_call(
+        stage_kernel,
+        out_shape=shape(factor.shape, BF),
+        in_specs=[pl.BlockSpec(memory_space=pl.ANY)],
+        out_specs=pl.BlockSpec(memory_space=pl.ANY),
+        scratch_shapes=[pltpu.SemaphoreType.DMA((4,))],
+        compiler_params=pltpu.CompilerParams(vmem_limit_bytes=1024 * 1024),
+        cost_estimate=pl.CostEstimate(
+            flops=0, bytes_accessed=4 * factor.size, transcendentals=0
+        ),
+    )(factor)
     keep, give = call(
         right_kernel,
-        (grad_inverse, *pairs),
+        (factor, *pairs),
         [shape((n_col * size, width), BF)] * 2,
         4 * n_col * size * feat_grp * width,
         [pltpu.VMEM((n_col, 2, size, width), F32)],

time: 96.2 us -> 94.6 us (0.983)
  waiting for transfers between devices: 17.2 us -> 15.2 us
    ppermute x4, waiting for transfers between devices: 9.2 us -> 7.14 us  [along_y(): lax.ppermute(block, 'col', [(i, i - i % 4 + (i + k) % 4) for i in range(n...]
where the time goes in v27:
time: 94.6 us; the launch traced here: 93.8 us
  starting transfers between devices  64.1 us (68%)
  waiting for transfers between devices  15.2 us (16%)
  Pallas kernels  11 us (12%)
  local copies, waits for them, and re-layouts  1.72 us (2%)
    all_to_all x1, starting transfers between devices, body(): first = lax.all_to_all(payload, 'row', 0, 0)  14.9 us
    ppermute x4, starting transfers between devices, along_y(): lax.ppermute(block, 'col', [(i, i - i % 4 + (i + k) % 4) for i in range(n...  14.6 us
    ppermute x3, starting transfers between devices, body(): lax.ppermute(right, 'row', [(i, (i + j) % n_row) for i in range(n_row)])  10.7 us
    pallas_call x7, Pallas kernels, call(): pl.pallas_call(kernel, out_shape=outs, in_specs=places, out_specs=[VMEM]...  10.5 us
    all_to_all x1, starting transfers between devices, body(): lax.all_to_all(send.reshape((n_grp * n_col,) + send.shape[2:]), ('grp', '...  8.5 us
    ppermute x4, waiting for transfers between devices, along_y(): lax.ppermute(block, 'col', [(i, i - i % 4 + (i + k) % 4) for i in range(n...  7.14 us
    ppermute x2, starting transfers between devices, body(): taken = lax.ppermute(give, 'grp', [(i, i ^ 1) for i in range(n_grp)])  6.99 us
    ppermute x1, starting transfers between devices, body(): taken = lax.ppermute(give, 'grp', [(i, i ^ 2) for i in range(n_grp)])  4.34 us
  transfers between devices with their start and end apart: 13, of which 5 were waited for; matrix products, arithmetic and copies ran while one was open for 0% of the time, Pallas kernels for 9%

profile of v27, /device:TPU:1, one launch (start us, length us, event | category | flops | bytes accessed | tf_op | source)
XLA Modules:
  0.0 93.8 jit_solution(15011105088653936019)
XLA Ops:
  0.6 1.9 %shard_map.76.gy_ref = bf16[64,1536]{1,0:T(8,128)(2,1)} custom-call(s32[32]{0:T(128)} %picks.5, bf16[128,1536]{1,0:T(8,128)(2,1)} %g_ref.1), custom_call_target="tpu_custom_call" | custom-call | flops 25165824 | bytes 589952 | tf_op jit(solution)/shard_map/pallas_call | solution.py:24
  2.5 4.1 %collective-permute-start = (bf16[64,1536]{1,0:T(8,128)(2,1)}, bf16[64,1536]{1,0:T(8,128)(2,1)S(1)}, u32[]{:S(2)}, u32[]{:S(2)}) collective-permute-start(bf16[64,1536]{1,0:T(8,128)(2,1)} %shard_map.76.gy_ref), channel_id=1, source_target_pairs={{0,4},{1,5},{2,6},{3,7},{4,0},{5,1},{6,2},{7,3},{8,12},{9,13},{10,... | collective-permute-start | bytes 589832 | tf_op jit(solution)/shard_map/ppermute | solution.py:242
  6.6 3.6 %shard_map.79 = bf16[16,120,128]{2,1,0:T(8,128)(2,1)} custom-call(s32[32]{0:T(128)} %picks.5, bf16[128,384]{1,0:T(8,128)(2,1)} %x_ref.1, bf16[1536,384]{1,0:T(8,128)(2,1)} %a_hbm.1), custom_call_target="tpu_custom_call" | custom-call | flops 150994944 | bytes 1769600 | tf_op jit(solution)/shard_map/pallas_call | solution.py:24
  10.2 14.9 %all-to-all-start = ((bf16[16,120,128]{2,1,0:T(8,128)(2,1)}), bf16[16,120,128]{2,1,0:T(8,128)(2,1)S(1)}, u32[]{:S(2)}, u32[]{:S(2)}) async-start(bf16[16,120,128]{2,1,0:T(8,128)(2,1)} %shard_map.79), calls=%async_computation | async-start | bytes 983040 | tf_op jit(solution)/shard_map/all_to_all | solution.py:257
  25.2 3.2 %collective-permute-start.1 = (bf16[128,1536]{1,0:T(8,128)(2,1)S(1)}, bf16[128,1536]{1,0:T(8,128)(2,1)S(1)}, u32[]{:S(2)}, u32[]{:S(2)}) collective-permute-start(bf16[128,1536]{1,0:T(8,128)(2,1)S(1)} %pad_maximum_fusion.refs_0_), channel_id=1, source_target_pairs={{0,1},{1,2},{2,3},{3,0},{4,5},{5,6},{6,7},{7,4},{8,9},{9,10},{10,1... | collective-permute-start | bytes 1179656 | tf_op jit(solution)/shard_map/ppermute | solution.py:231
  28.4 3.4 %collective-permute-start.3 = (bf16[128,1536]{1,0:T(8,128)(2,1)S(1)}, bf16[128,1536]{1,0:T(8,128)(2,1)S(1)}, u32[]{:S(2)}, u32[]{:S(2)}) collective-permute-start(bf16[128,1536]{1,0:T(8,128)(2,1)S(1)} %pad_maximum_fusion.refs_0_), channel_id=1, source_target_pairs={{0,3},{1,0},{2,1},{3,2},{4,7},{5,4},{6,5},{7,6},{8,11},{9,8},{10,9... | collective-permute-start | bytes 1179656 | tf_op jit(solution)/shard_map/ppermute | solution.py:231
  31.8 3.5 %collective-permute-start.2 = (bf16[64,1536]{1,0:T(8,128)(2,1)S(1)}, bf16[64,1536]{1,0:T(8,128)(2,1)S(1)}, u32[]{:S(2)}, u32[]{:S(2)}) collective-permute-start(bf16[64,1536]{1,0:T(8,128)(2,1)S(1)} %pad_maximum_fusion.1), channel_id=1, source_target_pairs={{0,2},{1,3},{2,0},{3,1},{4,6},{5,7},{6,4},{7,5},{8,10},{9,11},{10,... | collective-permute-start | bytes 589832 | tf_op jit(solution)/shard_map/ppermute | solution.py:231
  35.4 0.0 copy-start
  35.4 1.7 %copy-done = bf16[1536,768]{1,0:T(8,128)(2,1)S(1)} copy-done((bf16[1536,768]{1,0:T(8,128)(2,1)S(1)}, bf16[1536,768]{1,0:T(8,128)(2,1)}, u32[]{:S(2)}) %copy-start) | copy-done | bytes 2359320
  37.1 0.5 shard_map.77.b_ref
  37.6 0.0 copy-start.2
  37.6 0.0 copy-start.3
  37.6 5.6 %collective-permute-done.2.refs_2_ = bf16[64,1536]{1,0:T(8,128)(2,1)S(1)} collective-permute-done((bf16[64,1536]{1,0:T(8,128)(2,1)S(1)}, bf16[64,1536]{1,0:T(8,128)(2,1)S(1)}, u32[]{:S(2)}, u32[]{:S(2)}) %collective-permute-start.2) | collective-permute-done | bytes 196640 | tf_op jit(solution)/shard_map/ppermute | solution.py:231
  43.2 0.9 shard_map.78
  44.1 4.1 %collective-permute-start.4 = (bf16[128,768]{1,0:T(8,128)(2,1)S(1)}, bf16[128,768]{1,0:T(8,128)(2,1)S(1)}, u32[]{:S(2)}, u32[]{:S(2)}) collective-permute-start(bf16[128,768]{1,0:T(8,128)(2,1)S(1)} %get-tuple-element.27), channel_id=1, source_target_pairs={{0,128},{128,0},{256,384},{384,256},{1,129},{129,1},{257,385},{385... | collective-permute-start | bytes 589832 | tf_op jit(solution)/shard_map/ppermute | solution.py:285
  48.1 1.0 %collective-permute-done.4 = bf16[128,768]{1,0:T(8,128)(2,1)S(1)} collective-permute-done((bf16[128,768]{1,0:T(8,128)(2,1)S(1)}, bf16[128,768]{1,0:T(8,128)(2,1)S(1)}, u32[]{:S(2)}, u32[]{:S(2)}) %collective-permute-start.4) | collective-permute-done | bytes 196640 | tf_op jit(solution)/shard_map/ppermute | solution.py:285
  49.2 4.3 %collective-permute-start.5 = (bf16[128,768]{1,0:T(8,128)(2,1)S(1)}, bf16[128,768]{1,0:T(8,128)(2,1)S(1)}, u32[]{:S(2)}, u32[]{:S(2)}) collective-permute-start(bf16[128,768]{1,0:T(8,128)(2,1)S(1)} %fusion), channel_id=1, source_target_pairs={{0,256},{128,384},{256,0},{384,128},{1,257},{129,385},{257,1},{385... | collective-permute-start | bytes 589832 | tf_op jit(solution)/shard_map/ppermute | solution.py:289
  53.6 1.0 %shard_map.80.side_ref = bf16[8,64,128]{2,1,0:T(8,128)(2,1)S(1)} custom-call(s32[32]{0:T(128)S(1)} %copy-done.3, bf16[128,384]{1,0:T(8,128)(2,1)S(1)} %copy-done.2, bf16[64,1536]{1,0:T(8,128)(2,1)S(1)} %copy-done.1), custom_call_target="tpu_custom_call" | custom-call | flops 3145728 | bytes 426112 | tf_op jit(solution)/shard_map/pallas_call | solution.py:24
  54.6 1.3 %shard_map.81 = bf16[4,8,160,128]{3,2,1,0:T(8,128)(2,1)} custom-call(bf16[16,120,128]{2,1,0:T(8,128)(2,1)S(1)} %all-to-all-done.got_ref, bf16[8,64,128]{2,1,0:T(8,128)(2,1)S(1)} %shard_map.80.side_ref), custom_call_target="tpu_custom_call" | custom-call | flops 1000000 | bytes 1933312 | tf_op jit(solution)/shard_map/pallas_call | solution.py:24
  55.9 2.9 %collective-permute-done.5 = bf16[128,768]{1,0:T(8,128)(2,1)S(1)} collective-permute-done((bf16[128,768]{1,0:T(8,128)(2,1)S(1)}, bf16[128,768]{1,0:T(8,128)(2,1)S(1)}, u32[]{:S(2)}, u32[]{:S(2)}) %collective-permute-start.5) | collective-permute-done | bytes 196640 | tf_op jit(solution)/shard_map/ppermute | solution.py:289
  58.7 0.1 add_convert_fusion.refs_0_
  58.8 8.5 %all-to-all-start.1 = ((bf16[32,160,128]{2,1,0:T(8,128)(2,1)}), bf16[32,160,128]{2,1,0:T(8,128)(2,1)S(1)}, u32[]{:S(2)}, u32[]{:S(2)}) async-start(bf16[32,160,128]{2,1,0:T(8,128)(2,1)} %bitcast), calls=%async_computation.1 | async-start | bytes 2621440 | tf_op jit(solution)/shard_map/all_to_all | solution.py:305
  67.3 4.2 %collective-permute-start.6 = (bf16[128,768]{1,0:T(8,128)(2,1)S(1)}, bf16[128,768]{1,0:T(8,128)(2,1)S(1)}, u32[]{:S(2)}, u32[]{:S(2)}) collective-permute-start(bf16[128,768]{1,0:T(8,128)(2,1)S(1)} %add_convert_fusion.refs_0_), channel_id=1, source_target_pairs={{0,16},{8,24},{16,32},{24,40},{32,48},{40,56},{48,64},{56,72},{64,... | collective-permute-start | bytes 589832 | tf_op jit(solution)/shard_map/ppermute | solution.py:308
  71.5 3.1 %collective-permute-start.7 = (bf16[128,768]{1,0:T(8,128)(2,1)S(1)}, bf16[128,768]{1,0:T(8,128)(2,1)S(1)}, u32[]{:S(2)}, u32[]{:S(2)}) collective-permute-start(bf16[128,768]{1,0:T(8,128)(2,1)S(1)} %add_convert_fusion.refs_0_), channel_id=1, source_target_pairs={{0,8},{8,16},{16,24},{24,32},{32,40},{40,48},{48,56},{56,64},{64,7... | collective-permute-start | bytes 589832 | tf_op jit(solution)/shard_map/ppermute | solution.py:308
  74.6 3.4 %collective-permute-start.8 = (bf16[128,768]{1,0:T(8,128)(2,1)S(1)}, bf16[128,768]{1,0:T(8,128)(2,1)S(1)}, u32[]{:S(2)}, u32[]{:S(2)}) collective-permute-start(bf16[128,768]{1,0:T(8,128)(2,1)S(1)} %add_convert_fusion.refs_0_), channel_id=1, source_target_pairs={{0,120},{8,0},{16,8},{24,16},{32,24},{40,32},{48,40},{56,48},{64,5... | collective-permute-start | bytes 589832 | tf_op jit(solution)/shard_map/ppermute | solution.py:308
  78.0 4.5 %collective-permute-start.9 = (bf16[64,1536]{1,0:T(8,128)(2,1)S(1)}, bf16[64,1536]{1,0:T(8,128)(2,1)S(1)}, u32[]{:S(2)}, u32[]{:S(2)}) collective-permute-start(bf16[64,1536]{1,0:T(8,128)(2,1)S(1)} %slice.22), channel_id=1, source_target_pairs={{0,3},{1,0},{2,1},{3,2},{4,7},{5,4},{6,5},{7,6},{8,11},{9,8},{10,9... | collective-permute-start | bytes 589832 | tf_op jit(solution)/shard_map/ppermute | solution.py:231
  82.6 4.1 %collective-permute-done.7.refs_2_ = bf16[128,768]{1,0:T(8,128)(2,1)S(1)} collective-permute-done((bf16[128,768]{1,0:T(8,128)(2,1)S(1)}, bf16[128,768]{1,0:T(8,128)(2,1)S(1)}, u32[]{:S(2)}, u32[]{:S(2)}) %collective-permute-start.7) | collective-permute-done | bytes 196640 | tf_op jit(solution)/shard_map/ppermute | solution.py:308
  86.6 1.6 %collective-permute-done.9.refs_2_ = bf16[64,1536]{1,0:T(8,128)(2,1)S(1)} collective-permute-done((bf16[64,1536]{1,0:T(8,128)(2,1)S(1)}, bf16[64,1536]{1,0:T(8,128)(2,1)S(1)}, u32[]{:S(2)}, u32[]{:S(2)}) %collective-permute-start.9) | collective-permute-done | bytes 196640 | tf_op jit(solution)/shard_map/ppermute | solution.py:231
  88.2 0.5 shard_map.82
  88.7 2.9 %collective-permute-start.10 = (bf16[96,768]{1,0:T(8,128)(2,1)S(1)}, bf16[96,768]{1,0:T(8,128)(2,1)S(1)}, u32[]{:S(2)}, u32[]{:S(2)}) collective-permute-start(bf16[96,768]{1,0:T(8,128)(2,1)S(1)} %get-tuple-element.40), channel_id=1, source_target_pairs={{0,128},{128,0},{256,384},{384,256},{1,129},{129,1},{257,385},{385... | collective-permute-start | bytes 442376 | tf_op jit(solution)/shard_map/ppermute | solution.py:322
  91.6 1.4 %shard_map.83 = (f32[48,1536]{1,0:T(8,128)}, f32[48,1536]{1,0:T(8,128)}) custom-call(bf16[4,8,160,128]{3,2,1,0:T(8,128)(2,1)S(1)} %bitcast.3, bf16[128,1536]{1,0:T(8,128)(2,1)S(1)} %pad_maximum_fusion.refs_0_, bf16[128,1536]{1,0:T(8,128)(2,1)S(1)} %collective-permute-done.1.refs_1_, bf16[64,1536]{1,0:T(8,128)(2,1)S(1)} %collective-permute-done.9.refs_2_, ...), custom_call_target="tpu_custom_call" | custom-call | flops 201326592 | bytes 3276800 | tf_op jit(solution)/shard_map/pallas_call | solution.py:24
  93.0 0.7 convert_add_fusion.1
  (18 shorter events, 0.2 us)
Async XLA Ops:
  2.5 22.6 %copy-start.1 = (bf16[64,1536]{1,0:T(8,128)(2,1)S(1)}, bf16[64,1536]{1,0:T(8,128)(2,1)}, u32[]{:S(2)}) copy-start(bf16[64,1536]{1,0:T(8,128)(2,1)} %shard_map.76.gy_ref) | copy-start | bytes 589828
  2.5 22.6 %collective-permute-start = (bf16[64,1536]{1,0:T(8,128)(2,1)}, bf16[64,1536]{1,0:T(8,128)(2,1)S(1)}, u32[]{:S(2)}, u32[]{:S(2)}) collective-permute-start(bf16[64,1536]{1,0:T(8,128)(2,1)} %shard_map.76.gy_ref), channel_id=1, source_target_pairs={{0,4},{1,5},{2,6},{3,7},{4,0},{5,1},{6,2},{7,3},{8,12},{9,13},{10,... | collective-permute-start | bytes 589832 | tf_op jit(solution)/shard_map/ppermute | solution.py:242
  10.2 44.4 %all-to-all-start = ((bf16[16,120,128]{2,1,0:T(8,128)(2,1)}), bf16[16,120,128]{2,1,0:T(8,128)(2,1)S(1)}, u32[]{:S(2)}, u32[]{:S(2)}) async-start(bf16[16,120,128]{2,1,0:T(8,128)(2,1)} %shard_map.79), calls=%async_computation | async-start | bytes 983040 | tf_op jit(solution)/shard_map/all_to_all | solution.py:257
  25.2 17.9 %collective-permute-start.1 = (bf16[128,1536]{1,0:T(8,128)(2,1)S(1)}, bf16[128,1536]{1,0:T(8,128)(2,1)S(1)}, u32[]{:S(2)}, u32[]{:S(2)}) collective-permute-start(bf16[128,1536]{1,0:T(8,128)(2,1)S(1)} %pad_maximum_fusion.refs_0_), channel_id=1, source_target_pairs={{0,1},{1,2},{2,3},{3,0},{4,5},{5,6},{6,7},{7,4},{8,9},{9,10},{10,1... | collective-permute-start | bytes 1179656 | tf_op jit(solution)/shard_map/ppermute | solution.py:231
  28.4 14.7 %collective-permute-start.3 = (bf16[128,1536]{1,0:T(8,128)(2,1)S(1)}, bf16[128,1536]{1,0:T(8,128)(2,1)S(1)}, u32[]{:S(2)}, u32[]{:S(2)}) collective-permute-start(bf16[128,1536]{1,0:T(8,128)(2,1)S(1)} %pad_maximum_fusion.refs_0_), channel_id=1, source_target_pairs={{0,3},{1,0},{2,1},{3,2},{4,7},{5,4},{6,5},{7,6},{8,11},{9,8},{10,9... | collective-permute-start | bytes 1179656 | tf_op jit(solution)/shard_map/ppermute | solution.py:231
  31.8 11.3 %collective-permute-start.2 = (bf16[64,1536]{1,0:T(8,128)(2,1)S(1)}, bf16[64,1536]{1,0:T(8,128)(2,1)S(1)}, u32[]{:S(2)}, u32[]{:S(2)}) collective-permute-start(bf16[64,1536]{1,0:T(8,128)(2,1)S(1)} %pad_maximum_fusion.1), channel_id=1, source_target_pairs={{0,2},{1,3},{2,0},{3,1},{4,6},{5,7},{6,4},{7,5},{8,10},{9,11},{10,... | collective-permute-start | bytes 589832 | tf_op jit(solution)/shard_map/ppermute | solution.py:231
  35.4 1.7 %copy-start = (bf16[1536,768]{1,0:T(8,128)(2,1)S(1)}, bf16[1536,768]{1,0:T(8,128)(2,1)}, u32[]{:S(2)}) copy-start(bf16[1536,768]{1,0:T(8,128)(2,1)} %b_hbm) | copy-start | bytes 7077892
  37.6 16.0 %copy-start.2 = (bf16[128,384]{1,0:T(8,128)(2,1)S(1)}, bf16[128,384]{1,0:T(8,128)(2,1)}, u32[]{:S(2)}) copy-start(bf16[128,384]{1,0:T(8,128)(2,1)} %x_ref.1) | copy-start | bytes 294916
  37.6 16.0 %copy-start.3 = (s32[32]{0:T(128)S(1)}, s32[32]{0:T(128)}, u32[]{:S(2)}) copy-start(s32[32]{0:T(128)} %picks.5) | copy-start | bytes 388
  44.1 5.1 %collective-permute-start.4 = (bf16[128,768]{1,0:T(8,128)(2,1)S(1)}, bf16[128,768]{1,0:T(8,128)(2,1)S(1)}, u32[]{:S(2)}, u32[]{:S(2)}) collective-permute-start(bf16[128,768]{1,0:T(8,128)(2,1)S(1)} %get-tuple-element.27), channel_id=1, source_target_pairs={{0,128},{128,0},{256,384},{384,256},{1,129},{129,1},{257,385},{385... | collective-permute-start | bytes 589832 | tf_op jit(solution)/shard_map/ppermute | solution.py:285
  49.2 9.5 %collective-permute-start.5 = (bf16[128,768]{1,0:T(8,128)(2,1)S(1)}, bf16[128,768]{1,0:T(8,128)(2,1)S(1)}, u32[]{:S(2)}, u32[]{:S(2)}) collective-permute-start(bf16[128,768]{1,0:T(8,128)(2,1)S(1)} %fusion), channel_id=1, source_target_pairs={{0,256},{128,384},{256,0},{384,128},{1,257},{129,385},{257,1},{385... | collective-permute-start | bytes 589832 | tf_op jit(solution)/shard_map/ppermute | solution.py:289
  58.8 29.4 %all-to-all-start.1 = ((bf16[32,160,128]{2,1,0:T(8,128)(2,1)}), bf16[32,160,128]{2,1,0:T(8,128)(2,1)S(1)}, u32[]{:S(2)}, u32[]{:S(2)}) async-start(bf16[32,160,128]{2,1,0:T(8,128)(2,1)} %bitcast), calls=%async_computation.1 | async-start | bytes 2621440 | tf_op jit(solution)/shard_map/all_to_all | solution.py:305
  67.3 15.2 %collective-permute-start.6 = (bf16[128,768]{1,0:T(8,128)(2,1)S(1)}, bf16[128,768]{1,0:T(8,128)(2,1)S(1)}, u32[]{:S(2)}, u32[]{:S(2)}) collective-permute-start(bf16[128,768]{1,0:T(8,128)(2,1)S(1)} %add_convert_fusion.refs_0_), channel_id=1, source_target_pairs={{0,16},{8,24},{16,32},{24,40},{32,48},{40,56},{48,64},{56,72},{64,... | collective-permute-start | bytes 589832 | tf_op jit(solution)/shard_map/ppermute | solution.py:308
  71.5 15.1 %collective-permute-start.7 = (bf16[128,768]{1,0:T(8,128)(2,1)S(1)}, bf16[128,768]{1,0:T(8,128)(2,1)S(1)}, u32[]{:S(2)}, u32[]{:S(2)}) collective-permute-start(bf16[128,768]{1,0:T(8,128)(2,1)S(1)} %add_convert_fusion.refs_0_), channel_id=1, source_target_pairs={{0,8},{8,16},{16,24},{24,32},{32,40},{40,48},{48,56},{56,64},{64,7... | collective-permute-start | bytes 589832 | tf_op jit(solution)/shard_map/ppermute | solution.py:308
  74.6 12.0 %collective-permute-start.8 = (bf16[128,768]{1,0:T(8,128)(2,1)S(1)}, bf16[128,768]{1,0:T(8,128)(2,1)S(1)}, u32[]{:S(2)}, u32[]{:S(2)}) collective-permute-start(bf16[128,768]{1,0:T(8,128)(2,1)S(1)} %add_convert_fusion.refs_0_), channel_id=1, source_target_pairs={{0,120},{8,0},{16,8},{24,16},{32,24},{40,32},{48,40},{56,48},{64,5... | collective-permute-start | bytes 589832 | tf_op jit(solution)/shard_map/ppermute | solution.py:308
  78.0 10.2 %collective-permute-start.9 = (bf16[64,1536]{1,0:T(8,128)(2,1)S(1)}, bf16[64,1536]{1,0:T(8,128)(2,1)S(1)}, u32[]{:S(2)}, u32[]{:S(2)}) collective-permute-start(bf16[64,1536]{1,0:T(8,128)(2,1)S(1)} %slice.22), channel_id=1, source_target_pairs={{0,3},{1,0},{2,1},{3,2},{4,7},{5,4},{6,5},{7,6},{8,11},{9,8},{10,9... | collective-permute-start | bytes 589832 | tf_op jit(solution)/shard_map/ppermute | solution.py:231
  88.7 4.4 %collective-permute-start.10 = (bf16[96,768]{1,0:T(8,128)(2,1)S(1)}, bf16[96,768]{1,0:T(8,128)(2,1)S(1)}, u32[]{:S(2)}, u32[]{:S(2)}) collective-permute-start(bf16[96,768]{1,0:T(8,128)(2,1)S(1)} %get-tuple-element.40), channel_id=1, source_target_pairs={{0,128},{128,0},{256,384},{384,256},{1,129},{129,1},{257,385},{385... | collective-permute-start | bytes 442376 | tf_op jit(solution)/shard_map/ppermute | solution.py:322

commit v28 on v27

--- a/solution.py
+++ b/solution.py
@@ -305,7 +305,11 @@
     got = lax.all_to_all(send.reshape((n_grp * n_col,) + send.shape[2:]), ("grp", "col"), 0, 0)
     got = got.reshape(send.shape)
     rights = [right] + [
-        lax.ppermute(right, "row", [(i, (i + j) % n_row) for i in range(n_row)])
+        lax.ppermute(
+            right,
+            "row",
+            [(i, (i + (-j if j == 2 and i % 2 else j)) % n_row) for i in range(n_row)],
+        )
         for j in SHIFTS[1:]
     ]
     unused, beyond = lax.optimization_barrier((right, after[2 * cut :]))

time: 94.6 us -> 94.6 us (level)
    ppermute x3, waiting for transfers between devices: 4.09 us -> 0.85 us  [body(): lax.ppermute(right, 'row', [(i, (i + (-j if j == 2 and i % 2 else j)) % n...]
    ppermute x4, waiting for transfers between devices: 7.14 us -> 10.4 us  [along_y(): lax.ppermute(block, 'col', [(i, i - i % 4 + (i + k) % 4) for i in range(n...]
where the time goes in v28:
time: 94.6 us; the launch traced here: 93.8 us
  starting transfers between devices  64.1 us (68%)
  waiting for transfers between devices  15.1 us (16%)
  Pallas kernels  11 us (12%)
  local copies, waits for them, and re-layouts  1.72 us (2%)
    all_to_all x1, starting transfers between devices, body(): first = lax.all_to_all(payload, 'row', 0, 0)  14.9 us
    ppermute x4, starting transfers between devices, along_y(): lax.ppermute(block, 'col', [(i, i - i % 4 + (i + k) % 4) for i in range(n...  14.6 us
    ppermute x3, starting transfers between devices, body(): lax.ppermute(right, 'row', [(i, (i + (-j if j == 2 and i % 2 else j)) % n...  10.7 us
    pallas_call x7, Pallas kernels, call(): pl.pallas_call(kernel, out_shape=outs, in_specs=places, out_specs=[VMEM]...  10.5 us
    ppermute x4, waiting for transfers between devices, along_y(): lax.ppermute(block, 'col', [(i, i - i % 4 + (i + k) % 4) for i in range(n...  10.4 us
    all_to_all x1, starting transfers between devices, body(): lax.all_to_all(send.reshape((n_grp * n_col,) + send.shape[2:]), ('grp', '...  8.5 us
    ppermute x2, starting transfers between devices, body(): taken = lax.ppermute(give, 'grp', [(i, i ^ 1) for i in range(n_grp)])  6.99 us
    ppermute x1, starting transfers between devices, body(): taken = lax.ppermute(give, 'grp', [(i, i ^ 2) for i in range(n_grp)])  4.34 us
  transfers between devices with their start and end apart: 13, of which 5 were waited for; matrix products, arithmetic and copies ran while one was open for 0% of the time, Pallas kernels for 9%

profile of v28, /device:TPU:1, one launch (start us, length us, event | category | flops | bytes accessed | tf_op | source)
XLA Modules:
  0.0 93.8 jit_solution(17032460400925104724)
XLA Ops:
  0.6 1.9 %shard_map.76.gy_ref = bf16[64,1536]{1,0:T(8,128)(2,1)} custom-call(s32[32]{0:T(128)} %picks.5, bf16[128,1536]{1,0:T(8,128)(2,1)} %g_ref.1), custom_call_target="tpu_custom_call" | custom-call | flops 25165824 | bytes 589952 | tf_op jit(solution)/shard_map/pallas_call | solution.py:24
  2.5 4.1 %collective-permute-start = (bf16[64,1536]{1,0:T(8,128)(2,1)}, bf16[64,1536]{1,0:T(8,128)(2,1)S(1)}, u32[]{:S(2)}, u32[]{:S(2)}) collective-permute-start(bf16[64,1536]{1,0:T(8,128)(2,1)} %shard_map.76.gy_ref), channel_id=1, source_target_pairs={{0,4},{1,5},{2,6},{3,7},{4,0},{5,1},{6,2},{7,3},{8,12},{9,13},{10,... | collective-permute-start | bytes 589832 | tf_op jit(solution)/shard_map/ppermute | solution.py:242
  6.6 3.6 %shard_map.79 = bf16[16,120,128]{2,1,0:T(8,128)(2,1)} custom-call(s32[32]{0:T(128)} %picks.5, bf16[128,384]{1,0:T(8,128)(2,1)} %x_ref.1, bf16[1536,384]{1,0:T(8,128)(2,1)} %a_hbm.1), custom_call_target="tpu_custom_call" | custom-call | flops 150994944 | bytes 1769600 | tf_op jit(solution)/shard_map/pallas_call | solution.py:24
  10.2 14.9 %all-to-all-start = ((bf16[16,120,128]{2,1,0:T(8,128)(2,1)}), bf16[16,120,128]{2,1,0:T(8,128)(2,1)S(1)}, u32[]{:S(2)}, u32[]{:S(2)}) async-start(bf16[16,120,128]{2,1,0:T(8,128)(2,1)} %shard_map.79), calls=%async_computation | async-start | bytes 983040 | tf_op jit(solution)/shard_map/all_to_all | solution.py:257
  25.2 3.2 %collective-permute-start.1 = (bf16[128,1536]{1,0:T(8,128)(2,1)S(1)}, bf16[128,1536]{1,0:T(8,128)(2,1)S(1)}, u32[]{:S(2)}, u32[]{:S(2)}) collective-permute-start(bf16[128,1536]{1,0:T(8,128)(2,1)S(1)} %pad_maximum_fusion.refs_0_), channel_id=1, source_target_pairs={{0,1},{1,2},{2,3},{3,0},{4,5},{5,6},{6,7},{7,4},{8,9},{9,10},{10,1... | collective-permute-start | bytes 1179656 | tf_op jit(solution)/shard_map/ppermute | solution.py:231
  28.4 3.4 %collective-permute-start.3 = (bf16[128,1536]{1,0:T(8,128)(2,1)S(1)}, bf16[128,1536]{1,0:T(8,128)(2,1)S(1)}, u32[]{:S(2)}, u32[]{:S(2)}) collective-permute-start(bf16[128,1536]{1,0:T(8,128)(2,1)S(1)} %pad_maximum_fusion.refs_0_), channel_id=1, source_target_pairs={{0,3},{1,0},{2,1},{3,2},{4,7},{5,4},{6,5},{7,6},{8,11},{9,8},{10,9... | collective-permute-start | bytes 1179656 | tf_op jit(solution)/shard_map/ppermute | solution.py:231
  31.8 3.5 %collective-permute-start.2 = (bf16[64,1536]{1,0:T(8,128)(2,1)S(1)}, bf16[64,1536]{1,0:T(8,128)(2,1)S(1)}, u32[]{:S(2)}, u32[]{:S(2)}) collective-permute-start(bf16[64,1536]{1,0:T(8,128)(2,1)S(1)} %pad_maximum_fusion.1), channel_id=1, source_target_pairs={{0,2},{1,3},{2,0},{3,1},{4,6},{5,7},{6,4},{7,5},{8,10},{9,11},{10,... | collective-permute-start | bytes 589832 | tf_op jit(solution)/shard_map/ppermute | solution.py:231
  35.4 0.0 copy-start
  35.4 1.7 %copy-done = bf16[1536,768]{1,0:T(8,128)(2,1)S(1)} copy-done((bf16[1536,768]{1,0:T(8,128)(2,1)S(1)}, bf16[1536,768]{1,0:T(8,128)(2,1)}, u32[]{:S(2)}) %copy-start) | copy-done | bytes 2359320
  37.1 0.5 shard_map.77.b_ref
  37.6 0.0 copy-start.2
  37.6 0.0 copy-start.3
  37.6 5.6 %collective-permute-done.2.refs_2_ = bf16[64,1536]{1,0:T(8,128)(2,1)S(1)} collective-permute-done((bf16[64,1536]{1,0:T(8,128)(2,1)S(1)}, bf16[64,1536]{1,0:T(8,128)(2,1)S(1)}, u32[]{:S(2)}, u32[]{:S(2)}) %collective-permute-start.2) | collective-permute-done | bytes 196640 | tf_op jit(solution)/shard_map/ppermute | solution.py:231
  43.2 0.9 shard_map.78
  44.1 4.1 %collective-permute-start.4 = (bf16[128,768]{1,0:T(8,128)(2,1)S(1)}, bf16[128,768]{1,0:T(8,128)(2,1)S(1)}, u32[]{:S(2)}, u32[]{:S(2)}) collective-permute-start(bf16[128,768]{1,0:T(8,128)(2,1)S(1)} %get-tuple-element.27), channel_id=1, source_target_pairs={{0,128},{128,0},{256,384},{384,256},{1,129},{129,1},{257,385},{385... | collective-permute-start | bytes 589832 | tf_op jit(solution)/shard_map/ppermute | solution.py:285
  48.1 1.0 %collective-permute-done.4 = bf16[128,768]{1,0:T(8,128)(2,1)S(1)} collective-permute-done((bf16[128,768]{1,0:T(8,128)(2,1)S(1)}, bf16[128,768]{1,0:T(8,128)(2,1)S(1)}, u32[]{:S(2)}, u32[]{:S(2)}) %collective-permute-start.4) | collective-permute-done | bytes 196640 | tf_op jit(solution)/shard_map/ppermute | solution.py:285
  49.2 4.3 %collective-permute-start.5 = (bf16[128,768]{1,0:T(8,128)(2,1)S(1)}, bf16[128,768]{1,0:T(8,128)(2,1)S(1)}, u32[]{:S(2)}, u32[]{:S(2)}) collective-permute-start(bf16[128,768]{1,0:T(8,128)(2,1)S(1)} %fusion), channel_id=1, source_target_pairs={{0,256},{128,384},{256,0},{384,128},{1,257},{129,385},{257,1},{385... | collective-permute-start | bytes 589832 | tf_op jit(solution)/shard_map/ppermute | solution.py:289
  53.6 1.0 %shard_map.80.side_ref = bf16[8,64,128]{2,1,0:T(8,128)(2,1)S(1)} custom-call(s32[32]{0:T(128)S(1)} %copy-done.3, bf16[128,384]{1,0:T(8,128)(2,1)S(1)} %copy-done.2, bf16[64,1536]{1,0:T(8,128)(2,1)S(1)} %copy-done.1), custom_call_target="tpu_custom_call" | custom-call | flops 3145728 | bytes 426112 | tf_op jit(solution)/shard_map/pallas_call | solution.py:24
  54.6 1.3 %shard_map.81 = bf16[4,8,160,128]{3,2,1,0:T(8,128)(2,1)} custom-call(bf16[16,120,128]{2,1,0:T(8,128)(2,1)S(1)} %all-to-all-done.got_ref, bf16[8,64,128]{2,1,0:T(8,128)(2,1)S(1)} %shard_map.80.side_ref), custom_call_target="tpu_custom_call" | custom-call | flops 1000000 | bytes 1933312 | tf_op jit(solution)/shard_map/pallas_call | solution.py:24
  55.9 2.9 %collective-permute-done.5 = bf16[128,768]{1,0:T(8,128)(2,1)S(1)} collective-permute-done((bf16[128,768]{1,0:T(8,128)(2,1)S(1)}, bf16[128,768]{1,0:T(8,128)(2,1)S(1)}, u32[]{:S(2)}, u32[]{:S(2)}) %collective-permute-start.5) | collective-permute-done | bytes 196640 | tf_op jit(solution)/shard_map/ppermute | solution.py:289
  58.7 0.1 add_convert_fusion.refs_0_
  58.8 8.5 %all-to-all-start.1 = ((bf16[32,160,128]{2,1,0:T(8,128)(2,1)}), bf16[32,160,128]{2,1,0:T(8,128)(2,1)S(1)}, u32[]{:S(2)}, u32[]{:S(2)}) async-start(bf16[32,160,128]{2,1,0:T(8,128)(2,1)} %bitcast), calls=%async_computation.1 | async-start | bytes 2621440 | tf_op jit(solution)/shard_map/all_to_all | solution.py:305
  67.3 4.2 %collective-permute-start.6 = (bf16[128,768]{1,0:T(8,128)(2,1)S(1)}, bf16[128,768]{1,0:T(8,128)(2,1)S(1)}, u32[]{:S(2)}, u32[]{:S(2)}) collective-permute-start(bf16[128,768]{1,0:T(8,128)(2,1)S(1)} %add_convert_fusion.refs_0_), channel_id=1, source_target_pairs={{0,16},{8,120},{16,32},{24,8},{32,48},{40,24},{48,64},{56,40},{64,... | collective-permute-start | bytes 589832 | tf_op jit(solution)/shard_map/ppermute | solution.py:308
  71.5 3.4 %collective-permute-start.7 = (bf16[128,768]{1,0:T(8,128)(2,1)S(1)}, bf16[128,768]{1,0:T(8,128)(2,1)S(1)}, u32[]{:S(2)}, u32[]{:S(2)}) collective-permute-start(bf16[128,768]{1,0:T(8,128)(2,1)S(1)} %add_convert_fusion.refs_0_), channel_id=1, source_target_pairs={{0,8},{8,16},{16,24},{24,32},{32,40},{40,48},{48,56},{56,64},{64,7... | collective-permute-start | bytes 589832 | tf_op jit(solution)/shard_map/ppermute | solution.py:308
  74.9 3.1 %collective-permute-start.8 = (bf16[128,768]{1,0:T(8,128)(2,1)S(1)}, bf16[128,768]{1,0:T(8,128)(2,1)S(1)}, u32[]{:S(2)}, u32[]{:S(2)}) collective-permute-start(bf16[128,768]{1,0:T(8,128)(2,1)S(1)} %add_convert_fusion.refs_0_), channel_id=1, source_target_pairs={{0,120},{8,0},{16,8},{24,16},{32,24},{40,32},{48,40},{56,48},{64,5... | collective-permute-start | bytes 589832 | tf_op jit(solution)/shard_map/ppermute | solution.py:308
  78.0 4.5 %collective-permute-start.9 = (bf16[64,1536]{1,0:T(8,128)(2,1)S(1)}, bf16[64,1536]{1,0:T(8,128)(2,1)S(1)}, u32[]{:S(2)}, u32[]{:S(2)}) collective-permute-start(bf16[64,1536]{1,0:T(8,128)(2,1)S(1)} %slice.22), channel_id=1, source_target_pairs={{0,3},{1,0},{2,1},{3,2},{4,7},{5,4},{6,5},{7,6},{8,11},{9,8},{10,9... | collective-permute-start | bytes 589832 | tf_op jit(solution)/shard_map/ppermute | solution.py:231
  82.6 0.8 collective-permute-done.8.refs_3_
  83.4 4.8 %collective-permute-done.9.refs_2_ = bf16[64,1536]{1,0:T(8,128)(2,1)S(1)} collective-permute-done((bf16[64,1536]{1,0:T(8,128)(2,1)S(1)}, bf16[64,1536]{1,0:T(8,128)(2,1)S(1)}, u32[]{:S(2)}, u32[]{:S(2)}) %collective-permute-start.9) | collective-permute-done | bytes 196640 | tf_op jit(solution)/shard_map/ppermute | solution.py:231
  88.2 0.5 shard_map.82
  88.7 2.9 %collective-permute-start.10 = (bf16[96,768]{1,0:T(8,128)(2,1)S(1)}, bf16[96,768]{1,0:T(8,128)(2,1)S(1)}, u32[]{:S(2)}, u32[]{:S(2)}) collective-permute-start(bf16[96,768]{1,0:T(8,128)(2,1)S(1)} %get-tuple-element.40), channel_id=1, source_target_pairs={{0,128},{128,0},{256,384},{384,256},{1,129},{129,1},{257,385},{385... | collective-permute-start | bytes 442376 | tf_op jit(solution)/shard_map/ppermute | solution.py:326
  91.6 1.4 %shard_map.83 = (f32[48,1536]{1,0:T(8,128)}, f32[48,1536]{1,0:T(8,128)}) custom-call(bf16[4,8,160,128]{3,2,1,0:T(8,128)(2,1)S(1)} %bitcast.3, bf16[128,1536]{1,0:T(8,128)(2,1)S(1)} %pad_maximum_fusion.refs_0_, bf16[128,1536]{1,0:T(8,128)(2,1)S(1)} %collective-permute-done.1.refs_1_, bf16[64,1536]{1,0:T(8,128)(2,1)S(1)} %collective-permute-done.9.refs_2_, ...), custom_call_target="tpu_custom_call" | custom-call | flops 201326592 | bytes 3276800 | tf_op jit(solution)/shard_map/pallas_call | solution.py:24
  93.0 0.7 convert_add_fusion.1
  (18 shorter events, 0.2 us)
Async XLA Ops:
  2.5 22.6 %copy-start.1 = (bf16[64,1536]{1,0:T(8,128)(2,1)S(1)}, bf16[64,1536]{1,0:T(8,128)(2,1)}, u32[]{:S(2)}) copy-start(bf16[64,1536]{1,0:T(8,128)(2,1)} %shard_map.76.gy_ref) | copy-start | bytes 589828
  2.5 22.6 %collective-permute-start = (bf16[64,1536]{1,0:T(8,128)(2,1)}, bf16[64,1536]{1,0:T(8,128)(2,1)S(1)}, u32[]{:S(2)}, u32[]{:S(2)}) collective-permute-start(bf16[64,1536]{1,0:T(8,128)(2,1)} %shard_map.76.gy_ref), channel_id=1, source_target_pairs={{0,4},{1,5},{2,6},{3,7},{4,0},{5,1},{6,2},{7,3},{8,12},{9,13},{10,... | collective-permute-start | bytes 589832 | tf_op jit(solution)/shard_map/ppermute | solution.py:242
  10.2 44.4 %all-to-all-start = ((bf16[16,120,128]{2,1,0:T(8,128)(2,1)}), bf16[16,120,128]{2,1,0:T(8,128)(2,1)S(1)}, u32[]{:S(2)}, u32[]{:S(2)}) async-start(bf16[16,120,128]{2,1,0:T(8,128)(2,1)} %shard_map.79), calls=%async_computation | async-start | bytes 983040 | tf_op jit(solution)/shard_map/all_to_all | solution.py:257
  25.2 17.9 %collective-permute-start.1 = (bf16[128,1536]{1,0:T(8,128)(2,1)S(1)}, bf16[128,1536]{1,0:T(8,128)(2,1)S(1)}, u32[]{:S(2)}, u32[]{:S(2)}) collective-permute-start(bf16[128,1536]{1,0:T(8,128)(2,1)S(1)} %pad_maximum_fusion.refs_0_), channel_id=1, source_target_pairs={{0,1},{1,2},{2,3},{3,0},{4,5},{5,6},{6,7},{7,4},{8,9},{9,10},{10,1... | collective-permute-start | bytes 1179656 | tf_op jit(solution)/shard_map/ppermute | solution.py:231
  28.4 14.7 %collective-permute-start.3 = (bf16[128,1536]{1,0:T(8,128)(2,1)S(1)}, bf16[128,1536]{1,0:T(8,128)(2,1)S(1)}, u32[]{:S(2)}, u32[]{:S(2)}) collective-permute-start(bf16[128,1536]{1,0:T(8,128)(2,1)S(1)} %pad_maximum_fusion.refs_0_), channel_id=1, source_target_pairs={{0,3},{1,0},{2,1},{3,2},{4,7},{5,4},{6,5},{7,6},{8,11},{9,8},{10,9... | collective-permute-start | bytes 1179656 | tf_op jit(solution)/shard_map/ppermute | solution.py:231
  31.8 11.3 %collective-permute-start.2 = (bf16[64,1536]{1,0:T(8,128)(2,1)S(1)}, bf16[64,1536]{1,0:T(8,128)(2,1)S(1)}, u32[]{:S(2)}, u32[]{:S(2)}) collective-permute-start(bf16[64,1536]{1,0:T(8,128)(2,1)S(1)} %pad_maximum_fusion.1), channel_id=1, source_target_pairs={{0,2},{1,3},{2,0},{3,1},{4,6},{5,7},{6,4},{7,5},{8,10},{9,11},{10,... | collective-permute-start | bytes 589832 | tf_op jit(solution)/shard_map/ppermute | solution.py:231
  35.4 1.7 %copy-start = (bf16[1536,768]{1,0:T(8,128)(2,1)S(1)}, bf16[1536,768]{1,0:T(8,128)(2,1)}, u32[]{:S(2)}) copy-start(bf16[1536,768]{1,0:T(8,128)(2,1)} %b_hbm) | copy-start | bytes 7077892
  37.6 16.0 %copy-start.2 = (bf16[128,384]{1,0:T(8,128)(2,1)S(1)}, bf16[128,384]{1,0:T(8,128)(2,1)}, u32[]{:S(2)}) copy-start(bf16[128,384]{1,0:T(8,128)(2,1)} %x_ref.1) | copy-start | bytes 294916
  37.6 16.0 %copy-start.3 = (s32[32]{0:T(128)S(1)}, s32[32]{0:T(128)}, u32[]{:S(2)}) copy-start(s32[32]{0:T(128)} %picks.5) | copy-start | bytes 388
  44.1 5.1 %collective-permute-start.4 = (bf16[128,768]{1,0:T(8,128)(2,1)S(1)}, bf16[128,768]{1,0:T(8,128)(2,1)S(1)}, u32[]{:S(2)}, u32[]{:S(2)}) collective-permute-start(bf16[128,768]{1,0:T(8,128)(2,1)S(1)} %get-tuple-element.27), channel_id=1, source_target_pairs={{0,128},{128,0},{256,384},{384,256},{1,129},{129,1},{257,385},{385... | collective-permute-start | bytes 589832 | tf_op jit(solution)/shard_map/ppermute | solution.py:285
  49.2 9.5 %collective-permute-start.5 = (bf16[128,768]{1,0:T(8,128)(2,1)S(1)}, bf16[128,768]{1,0:T(8,128)(2,1)S(1)}, u32[]{:S(2)}, u32[]{:S(2)}) collective-permute-start(bf16[128,768]{1,0:T(8,128)(2,1)S(1)} %fusion), channel_id=1, source_target_pairs={{0,256},{128,384},{256,0},{384,128},{1,257},{129,385},{257,1},{385... | collective-permute-start | bytes 589832 | tf_op jit(solution)/shard_map/ppermute | solution.py:289
  58.8 29.4 %all-to-all-start.1 = ((bf16[32,160,128]{2,1,0:T(8,128)(2,1)}), bf16[32,160,128]{2,1,0:T(8,128)(2,1)S(1)}, u32[]{:S(2)}, u32[]{:S(2)}) async-start(bf16[32,160,128]{2,1,0:T(8,128)(2,1)} %bitcast), calls=%async_computation.1 | async-start | bytes 2621440 | tf_op jit(solution)/shard_map/all_to_all | solution.py:305
  67.3 15.2 %collective-permute-start.6 = (bf16[128,768]{1,0:T(8,128)(2,1)S(1)}, bf16[128,768]{1,0:T(8,128)(2,1)S(1)}, u32[]{:S(2)}, u32[]{:S(2)}) collective-permute-start(bf16[128,768]{1,0:T(8,128)(2,1)S(1)} %add_convert_fusion.refs_0_), channel_id=1, source_target_pairs={{0,16},{8,120},{16,32},{24,8},{32,48},{40,24},{48,64},{56,40},{64,... | collective-permute-start | bytes 589832 | tf_op jit(solution)/shard_map/ppermute | solution.py:308
  71.5 11.0 %collective-permute-start.7 = (bf16[128,768]{1,0:T(8,128)(2,1)S(1)}, bf16[128,768]{1,0:T(8,128)(2,1)S(1)}, u32[]{:S(2)}, u32[]{:S(2)}) collective-permute-start(bf16[128,768]{1,0:T(8,128)(2,1)S(1)} %add_convert_fusion.refs_0_), channel_id=1, source_target_pairs={{0,8},{8,16},{16,24},{24,32},{32,40},{40,48},{48,56},{56,64},{64,7... | collective-permute-start | bytes 589832 | tf_op jit(solution)/shard_map/ppermute | solution.py:308
  74.9 8.5 %collective-permute-start.8 = (bf16[128,768]{1,0:T(8,128)(2,1)S(1)}, bf16[128,768]{1,0:T(8,128)(2,1)S(1)}, u32[]{:S(2)}, u32[]{:S(2)}) collective-permute-start(bf16[128,768]{1,0:T(8,128)(2,1)S(1)} %add_convert_fusion.refs_0_), channel_id=1, source_target_pairs={{0,120},{8,0},{16,8},{24,16},{32,24},{40,32},{48,40},{56,48},{64,5... | collective-permute-start | bytes 589832 | tf_op jit(solution)/shard_map/ppermute | solution.py:308
  78.0 10.2 %collective-permute-start.9 = (bf16[64,1536]{1,0:T(8,128)(2,1)S(1)}, bf16[64,1536]{1,0:T(8,128)(2,1)S(1)}, u32[]{:S(2)}, u32[]{:S(2)}) collective-permute-start(bf16[64,1536]{1,0:T(8,128)(2,1)S(1)} %slice.22), channel_id=1, source_target_pairs={{0,3},{1,0},{2,1},{3,2},{4,7},{5,4},{6,5},{7,6},{8,11},{9,8},{10,9... | collective-permute-start | bytes 589832 | tf_op jit(solution)/shard_map/ppermute | solution.py:231
  88.7 4.4 %collective-permute-start.10 = (bf16[96,768]{1,0:T(8,128)(2,1)S(1)}, bf16[96,768]{1,0:T(8,128)(2,1)S(1)}, u32[]{:S(2)}, u32[]{:S(2)}) collective-permute-start(bf16[96,768]{1,0:T(8,128)(2,1)S(1)} %get-tuple-element.40), channel_id=1, source_target_pairs={{0,128},{128,0},{256,384},{384,256},{1,129},{129,1},{257,385},{385... | collective-permute-start | bytes 442376 | tf_op jit(solution)/shard_map/ppermute | solution.py:326
